TPU v7x, 32 devices: a whole 2x2x4 slice. The times are simulated.
32 devices in a mesh: dp: 4 (over y, core), seq: 8 (over z, x).
Axes of the slice: x: 2, y: 2, z: 4, core: 2. Of those that a mesh axis runs over, the one named last changes fastest.
Arguments:
- query_rows: bfloat16 [512, 8, 2048], P('seq', 'dp'), may hold values from -6 to 6
- key_rows: bfloat16 [512, 8, 2048], P('seq', 'dp'), may hold values from -6 to 6
- value_rows: bfloat16 [512, 8, 2048], P('seq', 'dp'), may hold values from -6 to 6
- region_lengths: int32 [8], P('dp'), may hold values from 64 to 512, as said below
- norm_gain: float32 [2048], replicated, may hold values from 0.1 to 1.9
- conv_weight: bfloat16 [9, 128, 128], replicated, may hold values from -0.1875 to 0.1875
- cotangent: bfloat16 [8, 32, 256, 128], P('dp', 'seq'), may hold values from -6 to 6
Outputs:
- decoded: bfloat16 [8, 32, 256, 128], P('dp', 'seq')
- weight_grad: float32 [9, 128, 128], replicated
Inputs may be any that keep to these rules, and one draw needn't show every extreme that they name: Region r's tokens fill its first region_lengths[r] slots; in every draw some region fills all 512 slots.
All inputs are finite; a program needn't handle non-finite values.
Results may differ from a plain program's by a relative error of at most 0.0063.
Values may be sent and summed in bfloat16 or wider, within the bound.
No kernel may reach another device: no remote copies, remote signals or barrier semaphores. Data moves between devices by JAX's collectives and lax.ppermute only.
A program may use at most 64 MiB of HBM per device.

v0:
```python
import math

import jax
import jax.numpy as jnp
from jax import lax
from jax.sharding import PartitionSpec as P

HEADS = 16
PATCH = 4


def extended(shard, sides, width):
    for axis, dim in sides:
        size, length = (lax.axis_size(axis), shard.shape[dim])
        up = [(i, (i + 1) % size) for i in range(size - 1)]
        down = [(j, i) for i, j in up]
        last = lax.slice_in_dim(shard, length - width, length, axis=dim)
        initial = lax.slice_in_dim(shard, 0, width, axis=dim)
        before = lax.ppermute(last, axis, up)
        after = lax.ppermute(initial, axis, down)
        shard = jnp.concatenate([before, shard, after], axis=dim)
    return shard


def attend(query_mat, key_mat, value_mat, live_rows, key_count):
    total_rows = query_mat.shape[0]
    block_rows = min(512, total_rows)
    scale_factor = 1.0 / math.sqrt(query_mat.shape[1])
    key_valid = jnp.arange(key_mat.shape[0], dtype=jnp.int32) < key_count

    def one_block(number, output):
        start_row = number * block_rows
        query_blk = lax.dynamic_slice_in_dim(query_mat, start_row, block_rows, 0)
        scores = (
            lax.dot_general(
                query_blk, key_mat, (((1,), (1,)), ((), ())), preferred_element_type=jnp.float32
            )
            * scale_factor
        )
        scores = jnp.where(key_valid[None, :], scores, -1e30)
        top_score = jnp.max(scores, axis=1, keepdims=True)
        powers = jnp.exp(scores - top_score)
        totals = jnp.sum(powers, axis=1, keepdims=True)
        mixed = (
            jnp.dot(powers.astype(jnp.bfloat16), value_mat, preferred_element_type=jnp.float32)
            / totals
        )
        return lax.dynamic_update_slice_in_dim(output, mixed.astype(jnp.bfloat16), start_row, 0)

    blocks_live = (live_rows + block_rows - 1) // block_rows
    return lax.fori_loop(0, blocks_live, one_block, jnp.zeros(query_mat.shape, jnp.bfloat16))


def pick_length(lengths_local, which):
    return jnp.sum(
        jnp.where(jnp.arange(lengths_local.shape[0], dtype=jnp.int32) == which, lengths_local, 0)
    )


def body(query_rows, key_rows, value_rows, region_lengths, norm_gain, conv_weight, cotangent):
    local_tokens, group_regions, model_width = query_rows.shape
    head_width = model_width // HEADS
    seq_count = lax.axis_size("seq")
    seq_index = lax.axis_index("seq")
    item_total = group_regions * HEADS
    got_query, got_key, got_value = (
        lax.all_to_all(
            query_rows.reshape(local_tokens, item_total, head_width),
            "seq",
            split_axis=1,
            concat_axis=0,
            tiled=True,
        ),
        lax.all_to_all(
            key_rows.reshape(local_tokens, item_total, head_width),
            "seq",
            split_axis=1,
            concat_axis=0,
            tiled=True,
        ),
        lax.all_to_all(
            value_rows.reshape(local_tokens, item_total, head_width),
            "seq",
            split_axis=1,
            concat_axis=0,
            tiled=True,
        ),
    )
    per_device = item_total // seq_count
    outputs = []
    for offset in range(per_device):
        global_item = seq_index * per_device + offset
        region_len = pick_length(region_lengths, global_item // HEADS)
        outputs.append(
            attend(
                got_query[:, offset],
                got_key[:, offset],
                got_value[:, offset],
                region_len,
                region_len,
            )
        )
    stacked = jnp.stack(outputs, axis=1)
    returned = lax.all_to_all(stacked, "seq", split_axis=0, concat_axis=1, tiled=True)
    attended = returned.reshape(local_tokens, group_regions, model_width)
    values32 = attended.astype(jnp.float32)
    mean_val = jnp.mean(values32, axis=-1, keepdims=True)
    centered = values32 - mean_val
    variance = jnp.mean(centered * centered, axis=-1, keepdims=True)
    normed = centered * lax.rsqrt(variance + 1e-05) * norm_gain
    positions = seq_index * local_tokens + jnp.arange(local_tokens, dtype=jnp.int32)
    token_live = positions[:, None] < region_lengths[None, :]
    normed = jnp.where(token_live[:, :, None], normed, 0.0).astype(jnp.bfloat16)
    channels = model_width // (PATCH * PATCH)
    pix_cols = local_tokens * PATCH
    image = normed.reshape(local_tokens, group_regions, PATCH, PATCH, channels).transpose(
        1, 2, 0, 3, 4
    )
    image = image.reshape(group_regions, PATCH, pix_cols, channels)
    rimmed = extended(image, (("seq", 1),), 1)
    padded = jnp.pad(rimmed, ((0, 0), (0, 0), (1, 1), (0, 0)))
    cot_flat = cotangent.reshape(-1, channels)
    accum = jnp.zeros((group_regions * PATCH * pix_cols, channels), jnp.float32)
    grads = []
    for tap_number in range(9):
        row_shift, col_shift = divmod(tap_number, 3)
        window = padded[
            :, row_shift : row_shift + PATCH, col_shift : col_shift + pix_cols, :
        ].reshape(-1, channels)
        accum = accum + jnp.dot(window, conv_weight[tap_number], preferred_element_type=jnp.float32)
        grads.append(jnp.dot(window.T, cot_flat, preferred_element_type=jnp.float32))
    decoded = accum.reshape(cotangent.shape).astype(jnp.bfloat16)
    local_grad = jnp.stack(grads)
    factor = 1.0 / math.sqrt(PATCH * pix_cols)
    summed = lax.psum(local_grad, ("dp", "seq"))
    return (decoded, summed * factor)


def solution(mesh):
    placed = (
        P("seq", "dp", None),
        P("seq", "dp", None),
        P("seq", "dp", None),
        P("dp"),
        P(),
        P(),
        P("dp", "seq", None, None),
    )
    return jax.shard_map(
        body,
        mesh=mesh,
        in_specs=placed,
        out_specs=(P("dp", "seq", None, None), P()),
        check_vma=False,
    )
```

profile of v0, /device:TPU:0, one launch (start us, length us, event | category | flops | bytes accessed | tf_op | source)
XLA Modules:
  0.0 265.7 jit_solution(14229589120227682625)
XLA Ops:
  7.2 1.4 reshape.117
  8.6 1.0 copy.84
  9.6 7.3 %all-to-all-start = ((bf16[64,32,128]{2,0,1:T(8,128)(2,1)}), bf16[64,32,128]{2,0,1:T(8,128)(2,1)S(1)}, u32[]{:S(2)}, u32[]{:S(2)}) async-start(bf16[64,32,128]{2,0,1:T(8,128)(2,1)} %copy.84), calls=%async_computation | async-start | bytes 1048576 | tf_op jit(solution)/shard_map/all_to_all | solution.py:67
  17.2 1.0 copy.86
  18.2 13.1 %all-to-all-done = bf16[64,32,128]{2,0,1:T(8,128)(2,1)S(1)} async-done(((bf16[64,32,128]{2,0,1:T(8,128)(2,1)}), bf16[64,32,128]{2,0,1:T(8,128)(2,1)S(1)}, u32[]{:S(2)}, u32[]{:S(2)}) %all-to-all-start) | async-done | bytes 524320 | tf_op jit(solution)/shard_map/all_to_all | solution.py:67
  31.4 3.6 %all-to-all-start.1 = ((bf16[64,32,128]{2,0,1:T(8,128)(2,1)}), bf16[64,32,128]{2,0,1:T(8,128)(2,1)S(1)}, u32[]{:S(2)}, u32[]{:S(2)}) async-start(bf16[64,32,128]{2,0,1:T(8,128)(2,1)} %copy.86), calls=%async_computation.1 | async-start | bytes 1048576 | tf_op jit(solution)/shard_map/all_to_all | solution.py:74
  35.4 1.0 copy.88
  36.4 13.3 %all-to-all-done.1 = bf16[64,32,128]{2,0,1:T(8,128)(2,1)S(1)} async-done(((bf16[64,32,128]{2,0,1:T(8,128)(2,1)}), bf16[64,32,128]{2,0,1:T(8,128)(2,1)S(1)}, u32[]{:S(2)}, u32[]{:S(2)}) %all-to-all-start.1) | async-done | bytes 524320 | tf_op jit(solution)/shard_map/all_to_all | solution.py:74
  49.7 3.6 %all-to-all-start.2 = ((bf16[64,32,128]{2,0,1:T(8,128)(2,1)}), bf16[64,32,128]{2,0,1:T(8,128)(2,1)S(1)}, u32[]{:S(2)}, u32[]{:S(2)}) async-start(bf16[64,32,128]{2,0,1:T(8,128)(2,1)} %copy.88), calls=%async_computation.2 | async-start | bytes 1048576 | tf_op jit(solution)/shard_map/all_to_all | solution.py:81
  53.3 0.8 fusion.67
  56.7 1.2 iota_compare_fusion.4
  57.9 1.3 iota_compare_fusion.2
  59.3 8.7 %all-to-all-done.2 = bf16[64,32,128]{2,0,1:T(8,128)(2,1)S(1)} async-done(((bf16[64,32,128]{2,0,1:T(8,128)(2,1)}), bf16[64,32,128]{2,0,1:T(8,128)(2,1)S(1)}, u32[]{:S(2)}, u32[]{:S(2)}) %all-to-all-start.2) | async-done | bytes 524320 | tf_op jit(solution)/shard_map/all_to_all | solution.py:81
  68.5 0.3 fusion.36
  70.3 0.3 fusion.42
  71.5 0.7 broadcast.88.clone
  72.1 0.8 while.51
  72.1 0.8 divide_convert_fusion.11
  72.9 0.7 broadcast.88.clone.1
  73.6 0.8 while.50
  73.6 0.8 divide_convert_fusion.10
  74.4 0.7 broadcast.88.clone.2
  75.1 0.8 while.49
  75.1 0.8 divide_convert_fusion.9
  75.8 0.7 broadcast.88.clone.3
  76.5 0.8 while.48
  76.5 0.8 divide_convert_fusion.8
  77.3 1.0 pad_maximum_fusion.2
  78.3 1.2 copy.90
  79.5 3.6 %all-to-all-start.3 = ((bf16[512,4,128]{2,1,0:T(4,128)(2,1)}), bf16[512,4,128]{2,1,0:T(4,128)(2,1)S(1)}, u32[]{:S(2)}, u32[]{:S(2)}) async-start(bf16[512,4,128]{2,1,0:T(4,128)(2,1)} %copy.90), calls=%async_computation.3 | async-start | bytes 1048576 | tf_op jit(solution)/shard_map/all_to_all | solution.py:104
  83.3 14.5 %all-to-all-done.3 = bf16[512,4,128]{2,1,0:T(4,128)(2,1)S(1)} async-done(((bf16[512,4,128]{2,1,0:T(4,128)(2,1)}), bf16[512,4,128]{2,1,0:T(4,128)(2,1)S(1)}, u32[]{:S(2)}, u32[]{:S(2)}) %all-to-all-start.3) | async-done | bytes 524320 | tf_op jit(solution)/shard_map/all_to_all | solution.py:104
  97.8 1.0 bitcast_reduce_fusion
  98.8 7.4 %fusion.21 = f32[64,8]{0,1:T(8,128)S(1)} fusion(bf16[8,64,4,128]{3,2,1,0:T(4,128)(2,1)S(1)} %bitcast.217, f32[64,8]{0,1:T(8,128)S(1)} %bitcast.250), kind=kLoop, calls=%fused_computation.50 | loop fusion | flops 1048064 | bytes 528384 | tf_op jit(solution)/shard_map/reduce_sum | solution.py:109
  106.3 0.6 select_convert_fusion
  107.2 3.4 %collective-permute-start = (bf16[2,1,256,128]{2,3,1,0:T(8,128)(2,1)S(1)}, bf16[2,1,256,128]{2,3,1,0:T(8,128)(2,1)S(1)}, u32[]{:S(2)}, u32[]{:S(2)}) collective-permute-start(bf16[2,1,256,128]{2,3,1,0:T(8,128)(2,1)S(1)} %get-tuple-element.378), channel_id=1, source_target_pairs={{0,1},{1,2},{2,3},{3,4},{4,5},{5,6},{6,7},{8,9},{9,10},{10,11},{11... | collective-permute-start | bytes 393224 | tf_op jit(solution)/shard_map/ppermute | solution.py:19
  110.6 1.5 collective-permute-start.1
  112.1 2.4 collective-permute-done
  114.5 3.0 %collective-permute-done.1 = bf16[2,1,256,128]{2,3,1,0:T(8,128)(2,1)S(1)} collective-permute-done((bf16[2,1,256,128]{2,3,1,0:T(8,128)(2,1)S(1)}, bf16[2,1,256,128]{2,3,1,0:T(8,128)(2,1)S(1)}, u32[]{:S(2)}, u32[]{:S(2)}) %collective-permute-start.1) | collective-permute-done | bytes 131104 | tf_op jit(solution)/shard_map/ppermute | solution.py:20
  117.5 1.0 copy.102
  118.5 1.0 copy.96
  119.5 0.6 fusion.10
  120.2 1.8 fusion.79
  122.0 0.9 fusion.19
  122.9 0.9 fusion.12
  123.8 1.0 fusion.18
  124.8 0.9 fusion.17
  125.7 1.0 fusion.16
  126.7 1.0 fusion.15
  127.7 0.9 fusion.14
  128.6 0.9 fusion.11
  129.6 1.0 fusion.13
  130.6 2.1 copy.100
  132.7 2.0 copy.99
  134.7 1.0 copy.98
  135.7 1.0 copy.97
  137.3 0.5 copy-done.3
  138.1 0.8 copy-done.7
  139.1 0.8 copy-done.6
  140.4 0.8 copy-done.5
  141.5 0.8 copy-done.4
  142.5 0.8 copy-done.2
  143.8 1.1 fusion
  144.9 112.0 %all-reduce.3.cloned.1.call-done = f32[9,128,128]{2,1,0:T(8,128)} async-done(((f32[9,128,128]{2,1,0:T(8,128)}), f32[9,128,128]{2,1,0:T(8,128)}) %all-reduce.3.cloned.1.call-update) | async-done | bytes 589840 | tf_op jit(solution)/shard_map/psum | solution.py:135
  257.0 1.9 broadcast_multiply_fusion
  (64 shorter events, 6.9 us)
Async XLA Ops:
  7.2 114.8 %copy-start = (bf16[2,4,256,128]{3,2,1,0:T(8,128)(2,1)S(1)}, bf16[2,4,256,128]{3,2,1,0:T(8,128)(2,1)}, u32[]{:S(2)}) copy-start(bf16[2,4,256,128]{3,2,1,0:T(8,128)(2,1)} %param.21) | copy-start | bytes 1572868
  8.6 8.3 %copy-start.8 = (bf16[64,2,2048]{2,1,0:T(2,128)(2,1)S(1)}, bf16[64,2,2048]{2,1,0:T(2,128)(2,1)}, u32[]{:S(2)}) copy-start(bf16[64,2,2048]{2,1,0:T(2,128)(2,1)} %param.16) | copy-start | bytes 1572868
  9.6 21.7 %all-to-all-start = ((bf16[64,32,128]{2,0,1:T(8,128)(2,1)}), bf16[64,32,128]{2,0,1:T(8,128)(2,1)S(1)}, u32[]{:S(2)}, u32[]{:S(2)}) async-start(bf16[64,32,128]{2,0,1:T(8,128)(2,1)} %copy.84), calls=%async_computation | async-start | bytes 1048576 | tf_op jit(solution)/shard_map/all_to_all | solution.py:67
  17.2 17.8 %copy-start.9 = (bf16[64,2,2048]{2,1,0:T(2,128)(2,1)S(1)}, bf16[64,2,2048]{2,1,0:T(2,128)(2,1)}, u32[]{:S(2)}) copy-start(bf16[64,2,2048]{2,1,0:T(2,128)(2,1)} %param.17) | copy-start | bytes 1572868
  31.4 18.3 %all-to-all-start.1 = ((bf16[64,32,128]{2,0,1:T(8,128)(2,1)}), bf16[64,32,128]{2,0,1:T(8,128)(2,1)S(1)}, u32[]{:S(2)}, u32[]{:S(2)}) async-start(bf16[64,32,128]{2,0,1:T(8,128)(2,1)} %copy.86), calls=%async_computation.1 | async-start | bytes 1048576 | tf_op jit(solution)/shard_map/all_to_all | solution.py:74
  35.3 18.0 %copy-start.15 = (s32[2]{0:T(128)S(1)}, s32[2]{0:T(128)}, u32[]{:S(2)}) copy-start(s32[2]{0:T(128)} %param.18) | copy-start | bytes 28
  49.7 18.3 %all-to-all-start.2 = ((bf16[64,32,128]{2,0,1:T(8,128)(2,1)}), bf16[64,32,128]{2,0,1:T(8,128)(2,1)S(1)}, u32[]{:S(2)}, u32[]{:S(2)}) async-start(bf16[64,32,128]{2,0,1:T(8,128)(2,1)} %copy.88), calls=%async_computation.2 | async-start | bytes 1048576 | tf_op jit(solution)/shard_map/all_to_all | solution.py:81
  75.8 1.5 copy-start.10
  75.8 1.5 copy-start.11
  75.8 1.5 copy-start.12
  79.5 18.3 %all-to-all-start.3 = ((bf16[512,4,128]{2,1,0:T(4,128)(2,1)}), bf16[512,4,128]{2,1,0:T(4,128)(2,1)S(1)}, u32[]{:S(2)}, u32[]{:S(2)}) async-start(bf16[512,4,128]{2,1,0:T(4,128)(2,1)} %copy.90), calls=%async_computation.3 | async-start | bytes 1048576 | tf_op jit(solution)/shard_map/all_to_all | solution.py:104
  83.1 173.8 %all-reduce.3.cloned.1.call-start = ((), (), s32[]{:S(2)}) async-start(), calls=%async_computation.4 | async-start | bytes 1179648 | tf_op jit(solution)/shard_map/psum | solution.py:135
  98.8 7.5 %copy-start.14 = (f32[2048]{0:T(1024)S(1)}, f32[2048]{0:T(1024)}, u32[]{:S(2)}) copy-start(f32[2048]{0:T(1024)} %param.19) | copy-start | bytes 24580
  107.2 7.3 %collective-permute-start = (bf16[2,1,256,128]{2,3,1,0:T(8,128)(2,1)S(1)}, bf16[2,1,256,128]{2,3,1,0:T(8,128)(2,1)S(1)}, u32[]{:S(2)}, u32[]{:S(2)}) collective-permute-start(bf16[2,1,256,128]{2,3,1,0:T(8,128)(2,1)S(1)} %get-tuple-element.378), channel_id=1, source_target_pairs={{0,1},{1,2},{2,3},{3,4},{4,5},{5,6},{6,7},{8,9},{9,10},{10,11},{11... | collective-permute-start | bytes 393224 | tf_op jit(solution)/shard_map/ppermute | solution.py:19
  110.6 6.9 %collective-permute-start.1 = (bf16[2,1,256,128]{2,3,1,0:T(8,128)(2,1)S(1)}, bf16[2,1,256,128]{2,3,1,0:T(8,128)(2,1)S(1)}, u32[]{:S(2)}, u32[]{:S(2)}) collective-permute-start(bf16[2,1,256,128]{2,3,1,0:T(8,128)(2,1)S(1)} %get-tuple-element.379), channel_id=1, source_target_pairs={{1,0},{2,1},{3,2},{4,3},{5,4},{6,5},{7,6},{9,8},{10,9},{11,10},{12... | collective-permute-start | bytes 393224 | tf_op jit(solution)/shard_map/ppermute | solution.py:20
  130.6 4.1 %copy-start.1 = (bf16[2,4,256,128]{2,3,1,0:T(8,128)(2,1)S(1)}, bf16[2,4,256,128]{2,3,1,0:T(8,128)(2,1)}, u32[]{:S(2)}) copy-start(bf16[2,4,256,128]{2,3,1,0:T(8,128)(2,1)} %get-tuple-element.373) | copy-start | bytes 1572868
  135.7 1.3 copy-start.13
  136.7 1.0 copy-start.3
  137.8 1.0 copy-start.7
  138.8 1.0 copy-start.6
  140.1 1.0 copy-start.5
  141.2 1.0 copy-start.4
  142.2 1.0 copy-start.2
Sparse Core Ops, SparseCore 0:
  130.7 126.2 all-reduce.2
where the time goes:
time: 267 us; the launch traced here: 266 us
  waiting for transfers between devices  167 us (63%)
  local copies, waits for them, and re-layouts  24.2 us (9%)
  starting transfers between devices  23 us (9%)
  other arithmetic  20 us (7%)
  between operations  17 us (6%)
  matrix products  14.5 us (5%)
    psum x1, waiting for transfers between devices, body(): summed = lax.psum(local_grad, ('dp', 'seq'))  112 us
    all_to_all x1, waiting for transfers between devices, body(): lax.all_to_all(stacked, 'seq', split_axis=0, concat_axis=1, tiled=True)  14.5 us
    all_to_all x1, waiting for transfers between devices, body(): lax.all_to_all(key_rows.reshape(local_tokens, item_total, head_width), 's...  13.3 us
    all_to_all x1, waiting for transfers between devices, body(): lax.all_to_all(query_rows.reshape(local_tokens, item_total, head_width),...  13.1 us
    slice x9, local copies, waits for them, and re-layouts, body(): padded[:, row_shift:row_shift + PATCH, col_shift:col_shift + pix_cols, :]  10.5 us
    all_to_all x1, waiting for transfers between devices, body(): lax.all_to_all(value_rows.reshape(local_tokens, item_total, head_width),...  8.66 us
    dot_general x9, matrix products, body(): jnp.dot(window.T, cot_flat, preferred_element_type=jnp.float32)  8.55 us
    reduce_sum x2, other arithmetic, body(): variance = jnp.mean(centered * centered, axis=-1, keepdims=True)  7.4 us
  transfers between devices with their start and end apart: 7, of which 7 were waited for; matrix products, arithmetic and copies ran while one was open for 6% of the time, Pallas kernels for 0%

commit v1 on v0

v1 whole, which is shorter than its diff:
```python
import functools
import math

import jax
import jax.numpy as jnp
from jax import lax
from jax.experimental import pallas as pl
from jax.experimental.pallas import tpu as pltpu
from jax.sharding import PartitionSpec as P

HEADS = 16
PATCH = 4
RIM = 8
VMEM_LIMIT = 48 * 1024 * 1024

VMEM = functools.partial(pl.BlockSpec, memory_space=pltpu.VMEM)
SMEM = functools.partial(pl.BlockSpec, memory_space=pltpu.SMEM)


def call(kernel, name, out_shape, in_specs, scratch=(), flops=0, moved=0, exps=0):
    many = isinstance(out_shape, (list, tuple))
    return pl.pallas_call(
        kernel,
        out_shape=out_shape,
        in_specs=in_specs,
        out_specs=[VMEM() for _ in out_shape] if many else VMEM(),
        scratch_shapes=list(scratch),
        compiler_params=pltpu.CompilerParams(vmem_limit_bytes=VMEM_LIMIT),
        cost_estimate=pl.CostEstimate(flops=flops, bytes_accessed=moved, transcendentals=exps),
        name=name,
    )


def pack_kernel(regions, heads, per_device, *refs):
    sources, out_ref = refs[:-1], refs[-1]
    width = sources[0].shape[2] // heads
    for which, ref in enumerate(sources):
        for head in range(heads):
            block = ref[:, :, head * width : (head + 1) * width].astype(jnp.float32)
            for region in range(regions):
                item = head * regions + region
                out_ref[item // per_device, which, item % per_device] = block[:, region, :].astype(
                    jnp.bfloat16
                )


def attend_kernel(block_rows, lengths_ref, packed_ref, out_ref):
    sources, _, per_device, tokens, width = packed_ref.shape
    capacity = sources * tokens
    blocks = capacity // block_rows
    per_block = block_rows // tokens
    factor = math.log2(math.e) / math.sqrt(width)
    columns = lax.broadcasted_iota(jnp.int32, (1, capacity), 1)
    for item in range(per_device):
        length = lengths_ref[item]
        key_valid = columns < length
        for block in range(blocks):
            rows = slice(block * per_block, (block + 1) * per_block)

            @pl.when(block * block_rows < length)
            def _(item=item, rows=rows, key_valid=key_valid):
                query = packed_ref[rows, 0, item].reshape(block_rows, width)
                keys = packed_ref[:, 1, item].reshape(capacity, width)
                values = packed_ref[:, 2, item].reshape(capacity, width)
                scores = lax.dot_general(
                    query, keys, (((1,), (1,)), ((), ())), preferred_element_type=jnp.float32
                )
                scores = jnp.where(key_valid, scores * factor, -1e30)
                powers = jnp.exp2(scores - jnp.max(scores, axis=1, keepdims=True))
                totals = jnp.sum(powers, axis=1, keepdims=True)
                mixed = jnp.dot(
                    powers.astype(jnp.bfloat16), values, preferred_element_type=jnp.float32
                )
                mixed = (mixed / totals).astype(jnp.bfloat16)
                out_ref[rows, item] = mixed.reshape(per_block, tokens, width)

            @pl.when(block * block_rows >= length)
            def _(item=item, rows=rows):
                out_ref[rows, item] = jnp.zeros((per_block, tokens, width), jnp.bfloat16)


def three_windows(padded, columns):
    return jnp.concatenate(
        [padded[RIM - 1 + shift : RIM - 1 + shift + columns].astype(jnp.bfloat16) for shift in range(3)],
        axis=1,
    )


def norm_kernel(
    chunk_rows,
    lengths_ref,
    base_ref,
    attended_ref,
    gain_ref,
    cot_ref,
    cot_before_ref,
    cot_after_ref,
    image_ref,
    first_ref,
    last_ref,
    grad_ref,
    pixels,
    windows,
    cots,
    grads,
):
    heads, regions, tokens, width = attended_ref.shape
    columns = tokens * PATCH
    features = heads * width
    position = base_ref[0] + lax.broadcasted_iota(jnp.int32, (tokens, 1), 0)
    pixels[:, :, :RIM, :] = jnp.zeros((regions, PATCH, RIM, width), jnp.float32)
    pixels[:, :, RIM + columns :, :] = jnp.zeros((regions, PATCH, RIM, width), jnp.float32)
    for region in range(regions):
        total = jnp.zeros((tokens, width), jnp.float32)
        for head in range(heads):
            total = total + attended_ref[head, region].astype(jnp.float32)
        mean = jnp.sum(total, axis=1, keepdims=True) * (1.0 / features)
        total = jnp.zeros((tokens, width), jnp.float32)
        for head in range(heads):
            centered = attended_ref[head, region].astype(jnp.float32) - mean
            total = total + centered * centered
        variance = jnp.sum(total, axis=1, keepdims=True) * (1.0 / features)
        spread = lax.rsqrt(variance + 1e-05)
        live = position < lengths_ref[region]
        for head in range(heads):
            centered = attended_ref[head, region].astype(jnp.float32) - mean
            normed = jnp.where(live, centered * spread * gain_ref[head : head + 1, :], 0.0)
            row, column = divmod(head, PATCH)
            pixels[region, row, pl.ds(RIM + column, tokens, stride=PATCH), :] = normed
        for row in range(PATCH):
            window = three_windows(pixels[region, row], columns)
            middle = window[:, width : 2 * width]
            image_ref[region, row] = middle
            if row == 0:
                first_ref[region] = middle
            if row == PATCH - 1:
                last_ref[region] = middle
            start = (region * PATCH + row) * columns
            windows[start : start + columns, :] = window
            below = cot_ref[region, row + 1] if row < PATCH - 1 else cot_after_ref[region]
            above = cot_ref[region, row - 1] if row > 0 else cot_before_ref[region]
            cots[start : start + columns, :] = jnp.concatenate(
                [below, cot_ref[region, row], above], axis=1
            )
    product = lax.dot_general(
        windows[...], cots[...], (((0,), (0,)), ((), ())), preferred_element_type=jnp.float32
    )
    for down in range(3):
        for across in range(3):
            tap = 3 * down + across
            grads[tap * width : (tap + 1) * width, :] = product[
                across * width : (across + 1) * width, down * width : (down + 1) * width
            ]
    filled = 9 * width
    if filled < grads.shape[0]:
        grads[filled:, :] = jnp.zeros((grads.shape[0] - filled, width), jnp.float32)
    for chunk in range(grad_ref.shape[0]):
        grad_ref[chunk] = grads[chunk * chunk_rows : (chunk + 1) * chunk_rows, :].astype(jnp.bfloat16)


def decode_kernel(image_ref, before_ref, after_ref, weight_ref, out_ref, padded):
    regions, rows, columns, width = image_ref.shape
    padded[:RIM, :] = jnp.zeros((RIM, width), jnp.float32)
    padded[RIM + columns :, :] = jnp.zeros((RIM, width), jnp.float32)
    for region in range(regions):
        strips = []
        for row in range(-1, rows + 1):
            if row < 0:
                source = before_ref[region]
            elif row == rows:
                source = after_ref[region]
            else:
                source = image_ref[region, row]
            padded[RIM : RIM + columns, :] = source.astype(jnp.float32)
            strips.append(three_windows(padded[...], columns))
            if len(strips) == 3:
                total = jnp.dot(strips[0], weight_ref[0], preferred_element_type=jnp.float32)
                for down in (1, 2):
                    total = total + jnp.dot(
                        strips[down], weight_ref[down], preferred_element_type=jnp.float32
                    )
                out_ref[region, row - 1] = total.astype(jnp.bfloat16)
                strips.pop(0)


def sum_kernel(factor, parts_ref, out_ref):
    total = parts_ref[0].astype(jnp.float32)
    for part in range(1, parts_ref.shape[0]):
        total = total + parts_ref[part].astype(jnp.float32)
    total = (total * factor).astype(jnp.bfloat16)
    for part in range(out_ref.shape[0]):
        out_ref[part] = total


def spread_kernel(parts_ref, out_ref):
    rows = parts_ref.shape[1]
    for part in range(parts_ref.shape[0]):
        start = part * rows
        kept = min(rows, out_ref.shape[0] - start)
        if kept > 0:
            out_ref[start : start + kept, :] = parts_ref[part, :kept, :].astype(jnp.float32)


def swap(parts, axes):
    return lax.all_to_all(parts, axes, split_axis=0, concat_axis=0, tiled=True)


def body(query_rows, key_rows, value_rows, region_lengths, norm_gain, conv_weight, cotangent):
    tokens, regions, model_width = query_rows.shape
    width = model_width // HEADS
    seq_count = lax.axis_size("seq")
    seq_index = lax.axis_index("seq")
    everyone = lax.axis_size("dp") * seq_count
    columns = tokens * PATCH
    capacity = seq_count * tokens
    per_device = regions * HEADS // seq_count
    up = [(i, i + 1) for i in range(seq_count - 1)]
    down = [(j, i) for i, j in up]
    local_bytes = 2 * query_rows.size

    packed = call(
        functools.partial(pack_kernel, regions, HEADS, per_device),
        "pack",
        jax.ShapeDtypeStruct((seq_count, 3, per_device, tokens, width), jnp.bfloat16),
        [VMEM()] * 3,
        moved=6 * local_bytes,
    )(query_rows, key_rows, value_rows)
    packed = swap(packed, "seq")

    cot_before = lax.ppermute(cotangent[:, PATCH - 1], "seq", up)
    cot_after = lax.ppermute(cotangent[:, 0], "seq", down)

    items = seq_index * per_device + jnp.arange(per_device, dtype=jnp.int32)
    item_lengths = jnp.sum(
        jnp.where(
            (items % regions)[:, None] == jnp.arange(regions, dtype=jnp.int32)[None, :],
            region_lengths[None, :],
            0,
        ),
        axis=1,
    )
    block_rows = min(256, capacity)
    mixed = call(
        functools.partial(attend_kernel, block_rows),
        "attend",
        jax.ShapeDtypeStruct((seq_count, per_device, tokens, width), jnp.bfloat16),
        [SMEM(), VMEM()],
        flops=4 * per_device * capacity * capacity * width,
        moved=4 * local_bytes,
        exps=per_device * capacity * capacity,
    )(item_lengths, packed)
    attended = swap(mixed, "seq").reshape(HEADS, regions, tokens, width)

    chunk_rows = -(-9 * width // everyone)
    pixel_rows = regions * PATCH * columns
    conv_flops = 18 * pixel_rows * width * width
    row_shape = jax.ShapeDtypeStruct((regions, columns, width), jnp.bfloat16)
    image, first, last, grad_parts = call(
        functools.partial(norm_kernel, chunk_rows),
        "norm_and_gradient",
        [
            jax.ShapeDtypeStruct((regions, PATCH, columns, width), jnp.bfloat16),
            row_shape,
            row_shape,
            jax.ShapeDtypeStruct((everyone, chunk_rows, width), jnp.bfloat16),
        ],
        [SMEM(), SMEM()] + [VMEM()] * 5,
        scratch=[
            pltpu.VMEM((regions, PATCH, columns + 2 * RIM, width), jnp.float32),
            pltpu.VMEM((pixel_rows, 3 * width), jnp.bfloat16),
            pltpu.VMEM((pixel_rows, 3 * width), jnp.bfloat16),
            pltpu.VMEM((everyone * chunk_rows, width), jnp.float32),
        ],
        flops=conv_flops,
        moved=4 * local_bytes,
    )(
        region_lengths,
        (seq_index * tokens).reshape(1),
        attended,
        norm_gain.reshape(HEADS, width),
        cotangent,
        cot_before,
        cot_after,
    )
    grad_parts = swap(grad_parts, ("dp", "seq"))
    before = lax.ppermute(last, "seq", up)
    after = lax.ppermute(first, "seq", down)
    sums = call(
        functools.partial(sum_kernel, 1.0 / math.sqrt(PATCH * columns)),
        "sum_parts",
        jax.ShapeDtypeStruct(grad_parts.shape, jnp.bfloat16),
        [VMEM()],
        moved=4 * grad_parts.size,
    )(grad_parts)
    sums = swap(sums, ("dp", "seq"))
    decoded = call(
        decode_kernel,
        "decode",
        jax.ShapeDtypeStruct(cotangent.shape, jnp.bfloat16),
        [VMEM()] * 4,
        scratch=[pltpu.VMEM((columns + 2 * RIM, width), jnp.float32)],
        flops=conv_flops,
        moved=2 * local_bytes,
    )(image, before, after, conv_weight.reshape(3, 3 * width, width))
    weight_grad = call(
        spread_kernel,
        "spread_sums",
        jax.ShapeDtypeStruct((9 * width, width), jnp.float32),
        [VMEM()],
        moved=6 * grad_parts.size,
    )(sums)
    return (decoded, weight_grad.reshape(conv_weight.shape))


def solution(mesh):
    placed = (
        P("seq", "dp", None),
        P("seq", "dp", None),
        P("seq", "dp", None),
        P("dp"),
        P(),
        P(),
        P("dp", "seq", None, None),
    )
    return jax.shard_map(
        body,
        mesh=mesh,
        in_specs=placed,
        out_specs=(P("dp", "seq", None, None), P()),
        check_vma=False,
    )
```

time: 267 us -> 114 us (0.43)
  waiting for transfers between devices: 167 us -> 53.1 us
  local copies, waits for them, and re-layouts: 24.2 us -> 3.15 us
  other arithmetic: 20 us -> 0.1 us
  between operations: 17 us -> 0.72 us
  blocking collectives: 0 us -> 16.2 us
  Pallas kernels: 0 us -> 15.3 us
  matrix products: 14.5 us -> 0 us
    psum x1 -> x0, waiting for transfers between devices: 112 us -> none  [body(): summed = lax.psum(local_grad, ('dp', 'seq'))]
    all_to_all x0 -> x1, blocking collectives: none -> 16.2 us  [swap(): return lax.all_to_all(parts, axes, split_axis=0, concat_axis=0, tiled=True)]
    pallas_call x0 -> x6, Pallas kernels: none -> 15.3 us  [the longest x1 5.01 us: body(): call(functools.partial(attend_kernel, block_rows), 'attend', jax.ShapeDty...]
    dot_general x26 -> x0, matrix products: 14.5 us -> none  [the longest x9 8.55 us: body(): jnp.dot(window.T, cot_flat, preferred_element_type=jnp.float32)]
    slice x10 -> x0, local copies, waits for them, and re-layouts: 10.5 us -> none  [the longest x9 10.5 us: body(): padded[:, row_shift:row_shift + PATCH, col_shift:col_shift + pix_cols, :]]
    reduce_sum x9 -> x1, other arithmetic: 9.93 us -> 0.09 us  [body(): jnp.sum(jnp.where((items % regions)[:, None] == jnp.arange(regions, dtype...]
    all_to_all x4 -> x3, waiting for transfers between devices: 49.6 us -> 41.1 us  [swap(): return lax.all_to_all(parts, axes, split_axis=0, concat_axis=0, tiled=True)]
    ppermute x2 -> x4, waiting for transfers between devices: 5.38 us -> 12 us  [the longest x1 4.43 us: body(): cot_before = lax.ppermute(cotangent[:, PATCH - 1], 'seq', up)]
  transfers between devices with their start and end apart: 7 -> 7, of which waited for: 7 -> 6; matrix products, arithmetic and copies ran while one was open for 6% -> 0% of each run, Pallas kernels for 0% -> 2%
where the time goes in v1:
time: 114 us; the launch traced here: 112 us
  waiting for transfers between devices  53.1 us (47%)
  starting transfers between devices  23.7 us (21%)
  blocking collectives  16.2 us (14%)
  Pallas kernels  15.3 us (13%)
  local copies, waits for them, and re-layouts  3.15 us (3%)
    all_to_all x3, waiting for transfers between devices, swap(): return lax.all_to_all(parts, axes, split_axis=0, concat_axis=0, tiled=True)  41.1 us
    all_to_all x1, blocking collectives, swap(): return lax.all_to_all(parts, axes, split_axis=0, concat_axis=0, tiled=True)  16.2 us
    all_to_all x3, starting transfers between devices, swap(): return lax.all_to_all(parts, axes, split_axis=0, concat_axis=0, tiled=True)  13.6 us
    pallas_call x1, Pallas kernels, body(): call(functools.partial(attend_kernel, block_rows), 'attend', jax.ShapeDty...  5.01 us
    ppermute x1, waiting for transfers between devices, body(): cot_before = lax.ppermute(cotangent[:, PATCH - 1], 'seq', up)  4.43 us
    ppermute x1, starting transfers between devices, body(): cot_before = lax.ppermute(cotangent[:, PATCH - 1], 'seq', up)  3.92 us
    pallas_call x1, Pallas kernels, body(): call(functools.partial(pack_kernel, regions, HEADS, per_device), 'pack',...  3.56 us
    ppermute x1, starting transfers between devices, body(): before = lax.ppermute(last, 'seq', up)  3.55 us
  transfers between devices with their start and end apart: 7, of which 6 were waited for; matrix products, arithmetic and copies ran while one was open for 0% of the time, Pallas kernels for 2%

profile of v1, /device:TPU:0, one launch (start us, length us, event | category | flops | bytes accessed | tf_op | source)
XLA Modules:
  0.0 112.2 jit_solution(17509880905919736509)
XLA Ops:
  0.6 0.0 copy-start
  0.6 1.0 copy-done
  1.7 0.0 copy-start.1
  1.7 1.0 copy-done.1
  2.7 0.0 copy-start.2
  2.7 1.0 copy-done.2
  3.8 3.6 %pack.1 = bf16[8,3,4,64,128]{4,3,2,1,0:T(8,128)(2,1)} custom-call(bf16[64,2,2048]{2,1,0:T(2,128)(2,1)S(1)} %copy-done, bf16[64,2,2048]{2,1,0:T(2,128)(2,1)S(1)} %copy-done.1, bf16[64,2,2048]{2,1,0:T(2,128)(2,1)S(1)} %copy-done.2), custom_call_target="tpu_custom_call" | custom-call | bytes 3145728 | tf_op jit(solution)/shard_map/pack/pallas_call | solution.py:221
  7.3 0.0 copy-start.6
  7.3 7.4 %all-to-all-start = ((bf16[8,3,4,64,128]{4,3,2,1,0:T(8,128)(2,1)}), bf16[8,3,4,64,128]{4,3,2,1,0:T(8,128)(2,1)S(1)}, u32[]{:S(2)}, u32[]{:S(2)}) async-start(bf16[8,3,4,64,128]{4,3,2,1,0:T(8,128)(2,1)} %pack.1), calls=%async_computation | async-start | bytes 3145728 | tf_op jit(solution)/shard_map/all_to_all | solution.py:205
  14.7 0.0 copy-done.6
  14.7 0.1 fusion.lengths_ref
  14.8 0.0 copy-start.3
  14.8 0.0 copy-start.5
  14.8 36.9 %all-to-all-done.packed_ref = bf16[8,3,4,64,128]{4,3,2,1,0:T(8,128)(2,1)S(1)} async-done(((bf16[8,3,4,64,128]{4,3,2,1,0:T(8,128)(2,1)}), bf16[8,3,4,64,128]{4,3,2,1,0:T(8,128)(2,1)S(1)}, u32[]{:S(2)}, u32[]{:S(2)}) %all-to-all-start) | async-done | bytes 1572896 | tf_op jit(solution)/shard_map/all_to_all | solution.py:205
  51.7 5.0 %attend.1 = bf16[8,4,64,128]{3,2,1,0:T(8,128)(2,1)} custom-call(s32[4]{0:T(128)S(1)} %fusion.lengths_ref, bf16[8,3,4,64,128]{4,3,2,1,0:T(8,128)(2,1)S(1)} %all-to-all-done.packed_ref), custom_call_target="tpu_custom_call" | custom-call | flops 536870912 | bytes 2097152 | tf_op jit(solution)/shard_map/attend/pallas_call | solution.py:243
  56.7 3.7 %all-to-all-start.1 = ((bf16[8,4,64,128]{3,2,1,0:T(8,128)(2,1)}), bf16[8,4,64,128]{3,2,1,0:T(8,128)(2,1)S(1)}, u32[]{:S(2)}, u32[]{:S(2)}) async-start(bf16[8,4,64,128]{3,2,1,0:T(8,128)(2,1)} %attend.1), calls=%async_computation.1 | async-start | bytes 1048576 | tf_op jit(solution)/shard_map/all_to_all | solution.py:205
  60.4 0.0 copy-done.3
  60.4 3.9 %collective-permute-start = (bf16[2,256,128]{2,1,0:T(8,128)(2,1)S(1)}, bf16[2,256,128]{2,1,0:T(8,128)(2,1)S(1)}, u32[]{:S(2)}, u32[]{:S(2)}) collective-permute-start(bf16[2,256,128]{2,1,0:T(8,128)(2,1)S(1)} %get-tuple-element.11), channel_id=1, source_target_pairs={{0,1},{1,2},{2,3},{3,4},{4,5},{5,6},{6,7},{8,9},{9,10},{10,11},{11... | collective-permute-start | bytes 393224 | tf_op jit(solution)/shard_map/ppermute | solution.py:230
  64.3 1.3 %collective-permute-start.1 = (bf16[2,256,128]{2,1,0:T(8,128)(2,1)S(1)}, bf16[2,256,128]{2,1,0:T(8,128)(2,1)S(1)}, u32[]{:S(2)}, u32[]{:S(2)}) collective-permute-start(bf16[2,256,128]{2,1,0:T(8,128)(2,1)S(1)} %get-tuple-element.10), channel_id=1, source_target_pairs={{1,0},{2,1},{3,2},{4,3},{5,4},{6,5},{7,6},{9,8},{10,9},{11,10},{12... | collective-permute-start | bytes 393224 | tf_op jit(solution)/shard_map/ppermute | solution.py:231
  65.7 4.4 %collective-permute-done.cot_before_ref = bf16[2,256,128]{2,1,0:T(8,128)(2,1)S(1)} collective-permute-done((bf16[2,256,128]{2,1,0:T(8,128)(2,1)S(1)}, bf16[2,256,128]{2,1,0:T(8,128)(2,1)S(1)}, u32[]{:S(2)}, u32[]{:S(2)}) %collective-permute-start) | collective-permute-done | bytes 131104 | tf_op jit(solution)/shard_map/ppermute | solution.py:230
  70.1 1.3 %collective-permute-done.1.cot_after_ref = bf16[2,256,128]{2,1,0:T(8,128)(2,1)S(1)} collective-permute-done((bf16[2,256,128]{2,1,0:T(8,128)(2,1)S(1)}, bf16[2,256,128]{2,1,0:T(8,128)(2,1)S(1)}, u32[]{:S(2)}, u32[]{:S(2)}) %collective-permute-start.1) | collective-permute-done | bytes 131104 | tf_op jit(solution)/shard_map/ppermute | solution.py:231
  71.4 4.2 %all-to-all-done.1 = bf16[8,4,64,128]{3,2,1,0:T(8,128)(2,1)S(1)} async-done(((bf16[8,4,64,128]{3,2,1,0:T(8,128)(2,1)}), bf16[8,4,64,128]{3,2,1,0:T(8,128)(2,1)S(1)}, u32[]{:S(2)}, u32[]{:S(2)}) %all-to-all-start.1) | async-done | bytes 524320 | tf_op jit(solution)/shard_map/all_to_all | solution.py:205
  75.6 0.0 copy-done.5
  75.6 0.0 copy-start.4
  75.6 2.9 %norm_and_gradient.1 = (bf16[2,4,256,128]{3,2,1,0:T(8,128)(2,1)S(1)}, bf16[2,256,128]{2,1,0:T(8,128)(2,1)S(1)}, bf16[2,256,128]{2,1,0:T(8,128)(2,1)S(1)}, bf16[32,36,128]{2,1,0:T(8,128)(2,1)S(1)}) custom-call(s32[2]{0:T(128)S(1)} %copy-done.6, s32[1]{0:T(128)} %bitcast.base_ref, bf16[16,2,64,128]{3,2,1,0:T(8,128)(2,1)S(1)} %bitcast.13, ...), custom_call_target="tpu_custom_call" | custom-call | flops 603979776 | bytes 2097152 | tf_op jit(solution)/shard_map/norm_and_gradient/pallas_call | solution.py:258
  78.5 16.2 %all_to_all.20.parts_ref = bf16[32,36,128]{2,1,0:T(8,128)(2,1)S(1)} all-to-all(bf16[32,36,128]{2,1,0:T(8,128)(2,1)S(1)} %get-tuple-element.9), channel_id=1, replica_groups=mesh['dp'=4,'seq'=8] {'dp','seq'}, dimensions={0} | all-to-all | bytes 589824 | tf_op jit(solution)/shard_map/all_to_all | solution.py:205
  94.7 0.8 sum_parts.1
  95.5 2.6 %all-to-all-start.3 = ((bf16[32,36,128]{2,1,0:T(8,128)(2,1)}), bf16[32,36,128]{2,1,0:T(8,128)(2,1)S(1)}, u32[]{:S(2)}, u32[]{:S(2)}) async-start(bf16[32,36,128]{2,1,0:T(8,128)(2,1)} %sum_parts.1), calls=%async_computation.3 | async-start | bytes 655360 | tf_op jit(solution)/shard_map/all_to_all | solution.py:205
  98.1 3.5 %collective-permute-start.2 = (bf16[2,256,128]{2,1,0:T(8,128)(2,1)S(1)}, bf16[2,256,128]{2,1,0:T(8,128)(2,1)S(1)}, u32[]{:S(2)}, u32[]{:S(2)}) collective-permute-start(bf16[2,256,128]{2,1,0:T(8,128)(2,1)S(1)} %get-tuple-element.7), channel_id=1, source_target_pairs={{0,1},{1,2},{2,3},{3,4},{4,5},{5,6},{6,7},{8,9},{9,10},{10,11},{11... | collective-permute-start | bytes 393224 | tf_op jit(solution)/shard_map/ppermute | solution.py:286
  101.6 1.3 %collective-permute-start.3 = (bf16[2,256,128]{2,1,0:T(8,128)(2,1)S(1)}, bf16[2,256,128]{2,1,0:T(8,128)(2,1)S(1)}, u32[]{:S(2)}, u32[]{:S(2)}) collective-permute-start(bf16[2,256,128]{2,1,0:T(8,128)(2,1)S(1)} %get-tuple-element.8), channel_id=1, source_target_pairs={{1,0},{2,1},{3,2},{4,3},{5,4},{6,5},{7,6},{9,8},{10,9},{11,10},{12... | collective-permute-start | bytes 393224 | tf_op jit(solution)/shard_map/ppermute | solution.py:287
  102.9 2.7 %collective-permute-done.2.before_ref = bf16[2,256,128]{2,1,0:T(8,128)(2,1)S(1)} collective-permute-done((bf16[2,256,128]{2,1,0:T(8,128)(2,1)S(1)}, bf16[2,256,128]{2,1,0:T(8,128)(2,1)S(1)}, u32[]{:S(2)}, u32[]{:S(2)}) %collective-permute-start.2) | collective-permute-done | bytes 131104 | tf_op jit(solution)/shard_map/ppermute | solution.py:286
  105.6 3.5 %collective-permute-done.3.after_ref = bf16[2,256,128]{2,1,0:T(8,128)(2,1)S(1)} collective-permute-done((bf16[2,256,128]{2,1,0:T(8,128)(2,1)S(1)}, bf16[2,256,128]{2,1,0:T(8,128)(2,1)S(1)}, u32[]{:S(2)}, u32[]{:S(2)}) %collective-permute-start.3) | collective-permute-done | bytes 131104 | tf_op jit(solution)/shard_map/ppermute | solution.py:287
  109.2 0.0 copy-done.4
  109.2 2.2 %decode.1 = bf16[2,4,256,128]{3,2,1,0:T(8,128)(2,1)} custom-call(bf16[2,4,256,128]{3,2,1,0:T(8,128)(2,1)S(1)} %get-tuple-element.6.image_ref, bf16[2,256,128]{2,1,0:T(8,128)(2,1)S(1)} %collective-permute-done.2.before_ref, bf16[2,256,128]{2,1,0:T(8,128)(2,1)S(1)} %collective-permute-done.3.after_ref, bf16[3,384,128]{2,1,0:T(8,128)(2,1)S(1)} %bitcast.14), custom_call_target="tpu_custom_call" | custom-call | flops 603979776 | bytes 1048576 | tf_op jit(solution)/shard_map/decode/pallas_call | solution.py:296
  111.4 0.0 all-to-all-done.3.parts_ref
  111.4 0.9 spread_sums.1
  (2 shorter events, 0.0 us)
Async XLA Ops:
  0.6 1.0 copy-start
  1.7 1.0 copy-start.1
  2.7 1.0 copy-start.2
  7.3 7.4 %copy-start.6 = (s32[2]{0:T(128)S(1)}, s32[2]{0:T(128)}, u32[]{:S(2)}) copy-start(s32[2]{0:T(128)} %lengths_ref.1) | copy-start | bytes 28
  7.3 44.4 %all-to-all-start = ((bf16[8,3,4,64,128]{4,3,2,1,0:T(8,128)(2,1)}), bf16[8,3,4,64,128]{4,3,2,1,0:T(8,128)(2,1)S(1)}, u32[]{:S(2)}, u32[]{:S(2)}) async-start(bf16[8,3,4,64,128]{4,3,2,1,0:T(8,128)(2,1)} %pack.1), calls=%async_computation | async-start | bytes 3145728 | tf_op jit(solution)/shard_map/all_to_all | solution.py:205
  14.8 45.6 %copy-start.3 = (bf16[2,4,256,128]{3,2,1,0:T(8,128)(2,1)S(1)}, bf16[2,4,256,128]{3,2,1,0:T(8,128)(2,1)}, u32[]{:S(2)}) copy-start(bf16[2,4,256,128]{3,2,1,0:T(8,128)(2,1)} %cot_ref.1) | copy-start | bytes 1572868
  14.8 60.8 %copy-start.5 = (f32[2048]{0:T(1024)S(1)}, f32[2048]{0:T(1024)}, u32[]{:S(2)}) copy-start(f32[2048]{0:T(1024)} %param.11) | copy-start | bytes 24580
  56.7 18.9 %all-to-all-start.1 = ((bf16[8,4,64,128]{3,2,1,0:T(8,128)(2,1)}), bf16[8,4,64,128]{3,2,1,0:T(8,128)(2,1)S(1)}, u32[]{:S(2)}, u32[]{:S(2)}) async-start(bf16[8,4,64,128]{3,2,1,0:T(8,128)(2,1)} %attend.1), calls=%async_computation.1 | async-start | bytes 1048576 | tf_op jit(solution)/shard_map/all_to_all | solution.py:205
  60.4 9.7 %collective-permute-start = (bf16[2,256,128]{2,1,0:T(8,128)(2,1)S(1)}, bf16[2,256,128]{2,1,0:T(8,128)(2,1)S(1)}, u32[]{:S(2)}, u32[]{:S(2)}) collective-permute-start(bf16[2,256,128]{2,1,0:T(8,128)(2,1)S(1)} %get-tuple-element.11), channel_id=1, source_target_pairs={{0,1},{1,2},{2,3},{3,4},{4,5},{5,6},{6,7},{8,9},{9,10},{10,11},{11... | collective-permute-start | bytes 393224 | tf_op jit(solution)/shard_map/ppermute | solution.py:230
  64.3 7.0 %collective-permute-start.1 = (bf16[2,256,128]{2,1,0:T(8,128)(2,1)S(1)}, bf16[2,256,128]{2,1,0:T(8,128)(2,1)S(1)}, u32[]{:S(2)}, u32[]{:S(2)}) collective-permute-start(bf16[2,256,128]{2,1,0:T(8,128)(2,1)S(1)} %get-tuple-element.10), channel_id=1, source_target_pairs={{1,0},{2,1},{3,2},{4,3},{5,4},{6,5},{7,6},{9,8},{10,9},{11,10},{12... | collective-permute-start | bytes 393224 | tf_op jit(solution)/shard_map/ppermute | solution.py:231
  75.6 33.6 %copy-start.4 = (bf16[9,128,128]{2,1,0:T(8,128)(2,1)S(1)}, bf16[9,128,128]{2,1,0:T(8,128)(2,1)}, u32[]{:S(2)}) copy-start(bf16[9,128,128]{2,1,0:T(8,128)(2,1)} %param.12) | copy-start | bytes 884740
  95.5 15.9 %all-to-all-start.3 = ((bf16[32,36,128]{2,1,0:T(8,128)(2,1)}), bf16[32,36,128]{2,1,0:T(8,128)(2,1)S(1)}, u32[]{:S(2)}, u32[]{:S(2)}) async-start(bf16[32,36,128]{2,1,0:T(8,128)(2,1)} %sum_parts.1), calls=%async_computation.3 | async-start | bytes 655360 | tf_op jit(solution)/shard_map/all_to_all | solution.py:205
  98.1 7.6 %collective-permute-start.2 = (bf16[2,256,128]{2,1,0:T(8,128)(2,1)S(1)}, bf16[2,256,128]{2,1,0:T(8,128)(2,1)S(1)}, u32[]{:S(2)}, u32[]{:S(2)}) collective-permute-start(bf16[2,256,128]{2,1,0:T(8,128)(2,1)S(1)} %get-tuple-element.7), channel_id=1, source_target_pairs={{0,1},{1,2},{2,3},{3,4},{4,5},{5,6},{6,7},{8,9},{9,10},{10,11},{11... | collective-permute-start | bytes 393224 | tf_op jit(solution)/shard_map/ppermute | solution.py:286
  101.6 7.5 %collective-permute-start.3 = (bf16[2,256,128]{2,1,0:T(8,128)(2,1)S(1)}, bf16[2,256,128]{2,1,0:T(8,128)(2,1)S(1)}, u32[]{:S(2)}, u32[]{:S(2)}) collective-permute-start(bf16[2,256,128]{2,1,0:T(8,128)(2,1)S(1)} %get-tuple-element.8), channel_id=1, source_target_pairs={{1,0},{2,1},{3,2},{4,3},{5,4},{6,5},{7,6},{9,8},{10,9},{11,10},{12... | collective-permute-start | bytes 393224 | tf_op jit(solution)/shard_map/ppermute | solution.py:287

commit v2 on v1

--- a/solution.py
+++ b/solution.py
@@ -12,71 +12,98 @@
 PATCH = 4
 RIM = 8
 VMEM_LIMIT = 48 * 1024 * 1024
+VMEM_WHOLE = 60 * 1024 * 1024
 
 VMEM = functools.partial(pl.BlockSpec, memory_space=pltpu.VMEM)
+HBM = functools.partial(pl.BlockSpec, memory_space=pltpu.HBM)
+ANY = functools.partial(pl.BlockSpec, memory_space=pl.ANY)
 SMEM = functools.partial(pl.BlockSpec, memory_space=pltpu.SMEM)
 
 
-def call(kernel, name, out_shape, in_specs, scratch=(), flops=0, moved=0, exps=0):
+def call(kernel, name, out_shape, in_specs, out_specs=None, scratch=(), flops=0, moved=0, exps=0, grant=VMEM_LIMIT):
     many = isinstance(out_shape, (list, tuple))
     return pl.pallas_call(
         kernel,
         out_shape=out_shape,
         in_specs=in_specs,
-        out_specs=[VMEM() for _ in out_shape] if many else VMEM(),
+        out_specs=out_specs or ([VMEM() for _ in out_shape] if many else VMEM()),
         scratch_shapes=list(scratch),
-        compiler_params=pltpu.CompilerParams(vmem_limit_bytes=VMEM_LIMIT),
+        compiler_params=pltpu.CompilerParams(vmem_limit_bytes=grant),
         cost_estimate=pl.CostEstimate(flops=flops, bytes_accessed=moved, transcendentals=exps),
         name=name,
     )
 
 
-def pack_kernel(regions, heads, per_device, *refs):
-    sources, out_ref = refs[:-1], refs[-1]
-    width = sources[0].shape[2] // heads
-    for which, ref in enumerate(sources):
+def pack_kernel(
+    regions, heads, per_device, query_ref, key_ref, value_ref, cot_ref, out_ref, first_ref, last_ref, held, ready, sems
+):
+    width = held.shape[3] // heads
+    copies = [
+        pltpu.make_async_copy(ref, held.at[which], sems.at[which])
+        for which, ref in enumerate((query_ref, key_ref, value_ref))
+    ]
+    rows = cot_ref.shape[1]
+    edges = [
+        pltpu.make_async_copy(cot_ref.at[:, 0], first_ref, sems.at[3]),
+        pltpu.make_async_copy(cot_ref.at[:, rows - 1], last_ref, sems.at[4]),
+    ]
+    for copy in copies + edges:
+        copy.start()
+    for which, copy in enumerate(copies):
+        copy.wait()
         for head in range(heads):
-            block = ref[:, :, head * width : (head + 1) * width].astype(jnp.float32)
+            block = held[which, :, :, head * width : (head + 1) * width].astype(jnp.float32)
             for region in range(regions):
                 item = head * regions + region
-                out_ref[item // per_device, which, item % per_device] = block[:, region, :].astype(
+                ready[item // per_device, which, item % per_device] = block[:, region, :].astype(
                     jnp.bfloat16
                 )
-
-
-def attend_kernel(block_rows, lengths_ref, packed_ref, out_ref):
+        store = pltpu.make_async_copy(ready.at[:, which], out_ref.at[:, which], sems.at[5 + which])
+        store.start()
+        edges.append(store)
+    for copy in edges:
+        copy.wait()
+
+
+def attend_kernel(block_rows, group, lengths_ref, packed_ref, before_ref, after_ref, out_ref):
+    del before_ref, after_ref
     sources, _, per_device, tokens, width = packed_ref.shape
     capacity = sources * tokens
-    blocks = capacity // block_rows
     per_block = block_rows // tokens
     factor = math.log2(math.e) / math.sqrt(width)
-    columns = lax.broadcasted_iota(jnp.int32, (1, capacity), 1)
-    for item in range(per_device):
-        length = lengths_ref[item]
-        key_valid = columns < length
-        for block in range(blocks):
+    slots = lax.broadcasted_iota(jnp.int32, (capacity, block_rows), 0)
+    for lead in range(group):
+        length = lengths_ref[lead]
+        items = range(lead, per_device, group)
+        for block in range(capacity // block_rows):
             rows = slice(block * per_block, (block + 1) * per_block)
 
             @pl.when(block * block_rows < length)
-            def _(item=item, rows=rows, key_valid=key_valid):
-                query = packed_ref[rows, 0, item].reshape(block_rows, width)
-                keys = packed_ref[:, 1, item].reshape(capacity, width)
-                values = packed_ref[:, 2, item].reshape(capacity, width)
-                scores = lax.dot_general(
-                    query, keys, (((1,), (1,)), ((), ())), preferred_element_type=jnp.float32
-                )
-                scores = jnp.where(key_valid, scores * factor, -1e30)
-                powers = jnp.exp2(scores - jnp.max(scores, axis=1, keepdims=True))
-                totals = jnp.sum(powers, axis=1, keepdims=True)
-                mixed = jnp.dot(
-                    powers.astype(jnp.bfloat16), values, preferred_element_type=jnp.float32
-                )
-                mixed = (mixed / totals).astype(jnp.bfloat16)
-                out_ref[rows, item] = mixed.reshape(per_block, tokens, width)
+            def _(items=items, rows=rows, length=length):
+                key_valid = slots < length
+                for item in items:
+                    query = packed_ref[rows, 0, item].reshape(block_rows, width)
+                    keys = packed_ref[:, 1, item].reshape(capacity, width)
+                    values = packed_ref[:, 2, item].reshape(capacity, width)
+                    scores = lax.dot_general(
+                        keys, query, (((1,), (1,)), ((), ())), preferred_element_type=jnp.float32
+                    )
+                    scores = jnp.where(key_valid, scores * factor, -1e30)
+                    powers = jnp.exp2(scores - jnp.max(scores, axis=0, keepdims=True))
+                    totals = jnp.sum(powers, axis=0, keepdims=True)
+                    mixed = lax.dot_general(
+                        values,
+                        powers.astype(jnp.bfloat16),
+                        (((0,), (0,)), ((), ())),
+                        preferred_element_type=jnp.float32,
+                    )
+                    mixed = (mixed / totals).T.astype(jnp.bfloat16)
+                    out_ref[rows, item] = mixed.reshape(per_block, tokens, width)
 
             @pl.when(block * block_rows >= length)
-            def _(item=item, rows=rows):
-                out_ref[rows, item] = jnp.zeros((per_block, tokens, width), jnp.bfloat16)
+            def _(items=items, rows=rows):
+                for item in items:
+                    out_ref[rows, item] = jnp.zeros((per_block, tokens, width), jnp.bfloat16)
 
 
 def three_windows(padded, columns):
@@ -183,7 +210,8 @@
                 strips.pop(0)
 
 
-def sum_kernel(factor, parts_ref, out_ref):
+def sum_kernel(factor, parts_ref, before_ref, after_ref, out_ref):
+    del before_ref, after_ref
     total = parts_ref[0].astype(jnp.float32)
     for part in range(1, parts_ref.shape[0]):
         total = total + parts_ref[part].astype(jnp.float32)
@@ -218,17 +246,28 @@
     down = [(j, i) for i, j in up]
     local_bytes = 2 * query_rows.size
 
-    packed = call(
+    edge_shape = jax.ShapeDtypeStruct((regions, columns, width), jnp.bfloat16)
+    packed, cot_first, cot_last = call(
         functools.partial(pack_kernel, regions, HEADS, per_device),
         "pack",
-        jax.ShapeDtypeStruct((seq_count, 3, per_device, tokens, width), jnp.bfloat16),
-        [VMEM()] * 3,
+        [
+            jax.ShapeDtypeStruct((seq_count, 3, per_device, tokens, width), jnp.bfloat16),
+            edge_shape,
+            edge_shape,
+        ],
+        [HBM()] * 4,
+        out_specs=[HBM()] * 3,
+        scratch=[
+            pltpu.VMEM((3,) + query_rows.shape, jnp.bfloat16),
+            pltpu.VMEM((seq_count, 3, per_device, tokens, width), jnp.bfloat16),
+            pltpu.SemaphoreType.DMA((8,)),
+        ],
         moved=6 * local_bytes,
-    )(query_rows, key_rows, value_rows)
+        grant=VMEM_WHOLE,
+    )(query_rows, key_rows, value_rows, cotangent)
     packed = swap(packed, "seq")
-
-    cot_before = lax.ppermute(cotangent[:, PATCH - 1], "seq", up)
-    cot_after = lax.ppermute(cotangent[:, 0], "seq", down)
+    cot_before = lax.ppermute(cot_last, "seq", up)
+    cot_after = lax.ppermute(cot_first, "seq", down)
 
     items = seq_index * per_device + jnp.arange(per_device, dtype=jnp.int32)
     item_lengths = jnp.sum(
@@ -240,28 +279,28 @@
         axis=1,
     )
     block_rows = min(256, capacity)
+    group = regions if per_device % regions == 0 else per_device
     mixed = call(
-        functools.partial(attend_kernel, block_rows),
+        functools.partial(attend_kernel, block_rows, group),
         "attend",
         jax.ShapeDtypeStruct((seq_count, per_device, tokens, width), jnp.bfloat16),
-        [SMEM(), VMEM()],
+        [SMEM(), VMEM(), ANY(), ANY()],
         flops=4 * per_device * capacity * capacity * width,
         moved=4 * local_bytes,
         exps=per_device * capacity * capacity,
-    )(item_lengths, packed)
+    )(item_lengths, packed, cot_before, cot_after)
     attended = swap(mixed, "seq").reshape(HEADS, regions, tokens, width)
 
     chunk_rows = -(-9 * width // everyone)
     pixel_rows = regions * PATCH * columns
     conv_flops = 18 * pixel_rows * width * width
-    row_shape = jax.ShapeDtypeStruct((regions, columns, width), jnp.bfloat16)
     image, first, last, grad_parts = call(
         functools.partial(norm_kernel, chunk_rows),
         "norm_and_gradient",
         [
             jax.ShapeDtypeStruct((regions, PATCH, columns, width), jnp.bfloat16),
-            row_shape,
-            row_shape,
+            edge_shape,
+            edge_shape,
             jax.ShapeDtypeStruct((everyone, chunk_rows, width), jnp.bfloat16),
         ],
         [SMEM(), SMEM()] + [VMEM()] * 5,
@@ -289,9 +328,9 @@
         functools.partial(sum_kernel, 1.0 / math.sqrt(PATCH * columns)),
         "sum_parts",
         jax.ShapeDtypeStruct(grad_parts.shape, jnp.bfloat16),
-        [VMEM()],
+        [VMEM(), ANY(), ANY()],
         moved=4 * grad_parts.size,
-    )(grad_parts)
+    )(grad_parts, before, after)
     sums = swap(sums, ("dp", "seq"))
     decoded = call(
         decode_kernel,

time: 114 us -> 118 us (1.035)
  blocking collectives: 16.2 us -> 0 us
  waiting for transfers between devices: 53.1 us -> 64.8 us
  starting transfers between devices: 23.7 us -> 30.3 us
  Pallas kernels: 15.3 us -> 21.2 us
  local copies, waits for them, and re-layouts: 3.15 us -> 0.03 us
    all_to_all x1 -> x0, blocking collectives: 16.2 us -> none  [swap(): return lax.all_to_all(parts, axes, split_axis=0, concat_axis=0, tiled=True)]
    ppermute x2, waiting for transfers between devices: 5.72 us -> 12.6 us  [the longest x1 12.6 us: body(): cot_before = lax.ppermute(cot_last, 'seq', up)]
    all_to_all x3 -> x4, starting transfers between devices: 13.6 us -> 20.1 us  [swap(): return lax.all_to_all(parts, axes, split_axis=0, concat_axis=0, tiled=True)]
    pallas_call x1, Pallas kernels: 3.56 us -> 9.12 us  [body(): call(functools.partial(pack_kernel, regions, HEADS, per_device), 'pack',...]
    all_to_all x3 -> x4, waiting for transfers between devices: 41.1 us -> 45.9 us  [swap(): return lax.all_to_all(parts, axes, split_axis=0, concat_axis=0, tiled=True)]
    unnamed x14 -> x12, local copies, waits for them, and re-layouts: 3.13 us -> 0.03 us
  transfers between devices with their start and end apart: 7 -> 8, of which waited for: 6 -> 7; matrix products, arithmetic and copies ran while one was open for 0% -> 0% of each run, Pallas kernels for 2% -> 2%
where the time goes in v2:
time: 118 us; the launch traced here: 117 us
  waiting for transfers between devices  64.8 us (55%)
  starting transfers between devices  30.3 us (26%)
  Pallas kernels  21.2 us (18%)
    all_to_all x4, waiting for transfers between devices, swap(): return lax.all_to_all(parts, axes, split_axis=0, concat_axis=0, tiled=True)  45.9 us
    all_to_all x4, starting transfers between devices, swap(): return lax.all_to_all(parts, axes, split_axis=0, concat_axis=0, tiled=True)  20.1 us
    ppermute x1, waiting for transfers between devices, body(): cot_before = lax.ppermute(cot_last, 'seq', up)  12.6 us
    pallas_call x1, Pallas kernels, body(): call(functools.partial(pack_kernel, regions, HEADS, per_device), 'pack',...  9.12 us
    pallas_call x1, Pallas kernels, body(): call(functools.partial(attend_kernel, block_rows, group), 'attend', jax.S...  4.54 us
    ppermute x1, starting transfers between devices, body(): cot_before = lax.ppermute(cot_last, 'seq', up)  3.92 us
    pallas_call x1, Pallas kernels, body(): call(functools.partial(norm_kernel, chunk_rows), 'norm_and_gradient', [ja...  3.68 us
    ppermute x1, starting transfers between devices, body(): before = lax.ppermute(last, 'seq', up)  3.67 us
  transfers between devices with their start and end apart: 8, of which 7 were waited for; matrix products, arithmetic and copies ran while one was open for 0% of the time, Pallas kernels for 2%

profile of v2, /device:TPU:0, one launch (start us, length us, event | category | flops | bytes accessed | tf_op | source)
XLA Modules:
  0.0 117.1 jit_solution(204525206156141771)
XLA Ops:
  0.6 9.1 %pack.1 = (bf16[8,3,4,64,128]{4,3,2,1,0:T(8,128)(2,1)}, bf16[2,256,128]{2,1,0:T(8,128)(2,1)}, bf16[2,256,128]{2,1,0:T(8,128)(2,1)}) custom-call(bf16[64,2,2048]{2,1,0:T(2,128)(2,1)} %query_ref.1, bf16[64,2,2048]{2,1,0:T(2,128)(2,1)} %key_ref.1, bf16[64,2,2048]{2,1,0:T(2,128)(2,1)} %value_ref.1, bf16[2,4,256,128]{3,2,1,0:T(8,128)(2,1)} %cot_ref.3), custom_call_target="tpu_custom_call" | custom-call | bytes 3145728 | tf_op jit(solution)/shard_map/pack/pallas_call | solution.py:250
  9.8 0.0 copy-start.5
  9.8 0.0 copy-start.4
  9.8 0.0 copy-start.3
  9.8 7.4 %all-to-all-start = ((bf16[8,3,4,64,128]{4,3,2,1,0:T(8,128)(2,1)}), bf16[8,3,4,64,128]{4,3,2,1,0:T(8,128)(2,1)S(1)}, u32[]{:S(2)}, u32[]{:S(2)}) async-start(bf16[8,3,4,64,128]{4,3,2,1,0:T(8,128)(2,1)} %get-tuple-element.9), calls=%async_computation | async-start | bytes 3145728 | tf_op jit(solution)/shard_map/all_to_all | solution.py:233
  17.2 0.0 copy-done.5
  17.2 3.9 %collective-permute-start = (bf16[2,256,128]{2,1,0:T(8,128)(2,1)S(1)}, bf16[2,256,128]{2,1,0:T(8,128)(2,1)S(1)}, u32[]{:S(2)}, u32[]{:S(2)}) collective-permute-start(bf16[2,256,128]{2,1,0:T(8,128)(2,1)S(1)} %copy-done.5), channel_id=1, source_target_pairs={{0,1},{1,2},{2,3},{3,4},{4,5},{5,6},{6,7},{8,9},{9,10},{10,11},{11... | collective-permute-start | bytes 393224 | tf_op jit(solution)/shard_map/ppermute | solution.py:269
  21.1 0.0 copy-done.4
  21.1 1.3 %collective-permute-start.1 = (bf16[2,256,128]{2,1,0:T(8,128)(2,1)S(1)}, bf16[2,256,128]{2,1,0:T(8,128)(2,1)S(1)}, u32[]{:S(2)}, u32[]{:S(2)}) collective-permute-start(bf16[2,256,128]{2,1,0:T(8,128)(2,1)S(1)} %copy-done.4), channel_id=1, source_target_pairs={{1,0},{2,1},{3,2},{4,3},{5,4},{6,5},{7,6},{9,8},{10,9},{11,10},{12... | collective-permute-start | bytes 393224 | tf_op jit(solution)/shard_map/ppermute | solution.py:270
  22.5 0.0 copy-done.3
  22.5 0.1 fusion.lengths_ref
  22.6 0.0 copy-start
  22.6 0.0 copy-start.2
  22.6 12.6 %collective-permute-done.before_ref.cot_before_ref = bf16[2,256,128]{2,1,0:T(8,128)(2,1)S(1)} collective-permute-done((bf16[2,256,128]{2,1,0:T(8,128)(2,1)S(1)}, bf16[2,256,128]{2,1,0:T(8,128)(2,1)S(1)}, u32[]{:S(2)}, u32[]{:S(2)}) %collective-permute-start) | collective-permute-done | bytes 131104 | tf_op jit(solution)/shard_map/ppermute | solution.py:269
  35.1 0.0 collective-permute-done.1.after_ref.cot_after_ref
  35.1 20.5 %all-to-all-done.packed_ref = bf16[8,3,4,64,128]{4,3,2,1,0:T(8,128)(2,1)S(1)} async-done(((bf16[8,3,4,64,128]{4,3,2,1,0:T(8,128)(2,1)}), bf16[8,3,4,64,128]{4,3,2,1,0:T(8,128)(2,1)S(1)}, u32[]{:S(2)}, u32[]{:S(2)}) %all-to-all-start) | async-done | bytes 1572896 | tf_op jit(solution)/shard_map/all_to_all | solution.py:233
  55.6 4.5 %attend.1 = bf16[8,4,64,128]{3,2,1,0:T(8,128)(2,1)} custom-call(s32[4]{0:T(128)S(1)} %fusion.lengths_ref, bf16[8,3,4,64,128]{4,3,2,1,0:T(8,128)(2,1)S(1)} %all-to-all-done.packed_ref, bf16[2,256,128]{2,1,0:T(8,128)(2,1)S(1)} %collective-permute-done.before_ref.cot_before_ref, bf16[2,256,128]{2,1,0:T(8,128)(2,1)S(1)} %collective-permute-done.1.after_ref.cot_after_ref), custom_call_target="tpu_custom_call" | custom-call | flops 536870912 | bytes 2097152 | tf_op jit(solution)/shard_map/attend/pallas_call | solution.py:283
  60.1 4.2 %all-to-all-start.1 = ((bf16[8,4,64,128]{3,2,1,0:T(8,128)(2,1)}), bf16[8,4,64,128]{3,2,1,0:T(8,128)(2,1)S(1)}, u32[]{:S(2)}, u32[]{:S(2)}) async-start(bf16[8,4,64,128]{3,2,1,0:T(8,128)(2,1)} %attend.1), calls=%async_computation.1 | async-start | bytes 1048576 | tf_op jit(solution)/shard_map/all_to_all | solution.py:233
  64.3 14.7 %all-to-all-done.1 = bf16[8,4,64,128]{3,2,1,0:T(8,128)(2,1)S(1)} async-done(((bf16[8,4,64,128]{3,2,1,0:T(8,128)(2,1)}), bf16[8,4,64,128]{3,2,1,0:T(8,128)(2,1)S(1)}, u32[]{:S(2)}, u32[]{:S(2)}) %all-to-all-start.1) | async-done | bytes 524320 | tf_op jit(solution)/shard_map/all_to_all | solution.py:233
  79.0 0.0 copy-done
  79.0 0.0 copy-done.2
  79.0 3.7 %norm_and_gradient.1 = (bf16[2,4,256,128]{3,2,1,0:T(8,128)(2,1)S(1)}, bf16[2,256,128]{2,1,0:T(8,128)(2,1)S(1)}, bf16[2,256,128]{2,1,0:T(8,128)(2,1)S(1)}, bf16[32,36,128]{2,1,0:T(8,128)(2,1)}) custom-call(s32[2]{0:T(128)S(1)} %copy-done.3, s32[1]{0:T(128)} %bitcast.base_ref, bf16[16,2,64,128]{3,2,1,0:T(8,128)(2,1)S(1)} %bitcast.5, f32[16,128]{1,0:T(8,128)S(1)} %bitcast.7, ...), custom_call_target="tpu_custom_call" | custom-call | flops 603979776 | bytes 2097152 | tf_op jit(solution)/shard_map/norm_and_gradient/pallas_call | solution.py:297
  82.7 0.0 copy-start.1
  82.7 2.7 %all-to-all-start.2 = ((bf16[32,36,128]{2,1,0:T(8,128)(2,1)}), bf16[32,36,128]{2,1,0:T(8,128)(2,1)S(1)}, u32[]{:S(2)}, u32[]{:S(2)}) async-start(bf16[32,36,128]{2,1,0:T(8,128)(2,1)} %get-tuple-element.15), calls=%async_computation.2 | async-start | bytes 655360 | tf_op jit(solution)/shard_map/all_to_all | solution.py:233
  85.4 3.7 %collective-permute-start.2 = (bf16[2,256,128]{2,1,0:T(8,128)(2,1)S(1)}, bf16[2,256,128]{2,1,0:T(8,128)(2,1)S(1)}, u32[]{:S(2)}, u32[]{:S(2)}) collective-permute-start(bf16[2,256,128]{2,1,0:T(8,128)(2,1)S(1)} %get-tuple-element.13), channel_id=1, source_target_pairs={{0,1},{1,2},{2,3},{3,4},{4,5},{5,6},{6,7},{8,9},{9,10},{10,11},{11... | collective-permute-start | bytes 393224 | tf_op jit(solution)/shard_map/ppermute | solution.py:325
  89.1 1.3 %collective-permute-start.3 = (bf16[2,256,128]{2,1,0:T(8,128)(2,1)S(1)}, bf16[2,256,128]{2,1,0:T(8,128)(2,1)S(1)}, u32[]{:S(2)}, u32[]{:S(2)}) collective-permute-start(bf16[2,256,128]{2,1,0:T(8,128)(2,1)S(1)} %get-tuple-element.14), channel_id=1, source_target_pairs={{1,0},{2,1},{3,2},{4,3},{5,4},{6,5},{7,6},{9,8},{10,9},{11,10},{12... | collective-permute-start | bytes 393224 | tf_op jit(solution)/shard_map/ppermute | solution.py:326
  90.4 2.7 %collective-permute-done.2.before_ref = bf16[2,256,128]{2,1,0:T(8,128)(2,1)S(1)} collective-permute-done((bf16[2,256,128]{2,1,0:T(8,128)(2,1)S(1)}, bf16[2,256,128]{2,1,0:T(8,128)(2,1)S(1)}, u32[]{:S(2)}, u32[]{:S(2)}) %collective-permute-start.2) | collective-permute-done | bytes 131104 | tf_op jit(solution)/shard_map/ppermute | solution.py:325
  93.0 3.6 %collective-permute-done.3.after_ref = bf16[2,256,128]{2,1,0:T(8,128)(2,1)S(1)} collective-permute-done((bf16[2,256,128]{2,1,0:T(8,128)(2,1)S(1)}, bf16[2,256,128]{2,1,0:T(8,128)(2,1)S(1)}, u32[]{:S(2)}, u32[]{:S(2)}) %collective-permute-start.3) | collective-permute-done | bytes 131104 | tf_op jit(solution)/shard_map/ppermute | solution.py:326
  96.7 0.9 all-to-all-done.2.parts_ref
  97.5 0.8 sum_parts.1
  98.3 5.8 %all-to-all-start.3 = ((bf16[32,36,128]{2,1,0:T(8,128)(2,1)}), bf16[32,36,128]{2,1,0:T(8,128)(2,1)S(1)}, u32[]{:S(2)}, u32[]{:S(2)}) async-start(bf16[32,36,128]{2,1,0:T(8,128)(2,1)} %sum_parts.1), calls=%async_computation.3 | async-start | bytes 655360 | tf_op jit(solution)/shard_map/all_to_all | solution.py:233
  104.1 0.0 copy-done.1
  104.2 2.2 %decode.1 = bf16[2,4,256,128]{3,2,1,0:T(8,128)(2,1)} custom-call(bf16[2,4,256,128]{3,2,1,0:T(8,128)(2,1)S(1)} %get-tuple-element.12.image_ref, bf16[2,256,128]{2,1,0:T(8,128)(2,1)S(1)} %collective-permute-done.2.before_ref, bf16[2,256,128]{2,1,0:T(8,128)(2,1)S(1)} %collective-permute-done.3.after_ref, bf16[3,384,128]{2,1,0:T(8,128)(2,1)S(1)} %bitcast.6), custom_call_target="tpu_custom_call" | custom-call | flops 603979776 | bytes 1048576 | tf_op jit(solution)/shard_map/decode/pallas_call | solution.py:335
  106.4 9.9 %all-to-all-done.3.parts_ref = bf16[32,36,128]{2,1,0:T(8,128)(2,1)S(1)} async-done(((bf16[32,36,128]{2,1,0:T(8,128)(2,1)}), bf16[32,36,128]{2,1,0:T(8,128)(2,1)S(1)}, u32[]{:S(2)}, u32[]{:S(2)}) %all-to-all-start.3) | async-done | bytes 294944 | tf_op jit(solution)/shard_map/all_to_all | solution.py:233
  116.3 0.9 spread_sums.1
  (1 shorter events, 0.0 us)
Async XLA Ops:
  9.8 7.4 %copy-start.5 = (bf16[2,256,128]{2,1,0:T(8,128)(2,1)S(1)}, bf16[2,256,128]{2,1,0:T(8,128)(2,1)}, u32[]{:S(2)}) copy-start(bf16[2,256,128]{2,1,0:T(8,128)(2,1)} %get-tuple-element.10) | copy-start | bytes 393220
  9.8 11.4 %copy-start.4 = (bf16[2,256,128]{2,1,0:T(8,128)(2,1)S(1)}, bf16[2,256,128]{2,1,0:T(8,128)(2,1)}, u32[]{:S(2)}) copy-start(bf16[2,256,128]{2,1,0:T(8,128)(2,1)} %get-tuple-element.11) | copy-start | bytes 393220
  9.8 12.7 %copy-start.3 = (s32[2]{0:T(128)S(1)}, s32[2]{0:T(128)}, u32[]{:S(2)}) copy-start(s32[2]{0:T(128)} %lengths_ref.1) | copy-start | bytes 28
  9.8 45.8 %all-to-all-start = ((bf16[8,3,4,64,128]{4,3,2,1,0:T(8,128)(2,1)}), bf16[8,3,4,64,128]{4,3,2,1,0:T(8,128)(2,1)S(1)}, u32[]{:S(2)}, u32[]{:S(2)}) async-start(bf16[8,3,4,64,128]{4,3,2,1,0:T(8,128)(2,1)} %get-tuple-element.9), calls=%async_computation | async-start | bytes 3145728 | tf_op jit(solution)/shard_map/all_to_all | solution.py:233
  17.2 17.9 %collective-permute-start = (bf16[2,256,128]{2,1,0:T(8,128)(2,1)S(1)}, bf16[2,256,128]{2,1,0:T(8,128)(2,1)S(1)}, u32[]{:S(2)}, u32[]{:S(2)}) collective-permute-start(bf16[2,256,128]{2,1,0:T(8,128)(2,1)S(1)} %copy-done.5), channel_id=1, source_target_pairs={{0,1},{1,2},{2,3},{3,4},{4,5},{5,6},{6,7},{8,9},{9,10},{10,11},{11... | collective-permute-start | bytes 393224 | tf_op jit(solution)/shard_map/ppermute | solution.py:269
  21.1 14.0 %collective-permute-start.1 = (bf16[2,256,128]{2,1,0:T(8,128)(2,1)S(1)}, bf16[2,256,128]{2,1,0:T(8,128)(2,1)S(1)}, u32[]{:S(2)}, u32[]{:S(2)}) collective-permute-start(bf16[2,256,128]{2,1,0:T(8,128)(2,1)S(1)} %copy-done.4), channel_id=1, source_target_pairs={{1,0},{2,1},{3,2},{4,3},{5,4},{6,5},{7,6},{9,8},{10,9},{11,10},{12... | collective-permute-start | bytes 393224 | tf_op jit(solution)/shard_map/ppermute | solution.py:270
  22.6 56.4 %copy-start = (bf16[2,4,256,128]{3,2,1,0:T(8,128)(2,1)S(1)}, bf16[2,4,256,128]{3,2,1,0:T(8,128)(2,1)}, u32[]{:S(2)}) copy-start(bf16[2,4,256,128]{3,2,1,0:T(8,128)(2,1)} %cot_ref.3) | copy-start | bytes 1572868
  22.6 56.4 %copy-start.2 = (f32[2048]{0:T(1024)S(1)}, f32[2048]{0:T(1024)}, u32[]{:S(2)}) copy-start(f32[2048]{0:T(1024)} %param.11) | copy-start | bytes 24580
  60.1 18.8 %all-to-all-start.1 = ((bf16[8,4,64,128]{3,2,1,0:T(8,128)(2,1)}), bf16[8,4,64,128]{3,2,1,0:T(8,128)(2,1)S(1)}, u32[]{:S(2)}, u32[]{:S(2)}) async-start(bf16[8,4,64,128]{3,2,1,0:T(8,128)(2,1)} %attend.1), calls=%async_computation.1 | async-start | bytes 1048576 | tf_op jit(solution)/shard_map/all_to_all | solution.py:233
  82.7 21.5 %copy-start.1 = (bf16[9,128,128]{2,1,0:T(8,128)(2,1)S(1)}, bf16[9,128,128]{2,1,0:T(8,128)(2,1)}, u32[]{:S(2)}) copy-start(bf16[9,128,128]{2,1,0:T(8,128)(2,1)} %param.12) | copy-start | bytes 884740
  82.7 14.9 %all-to-all-start.2 = ((bf16[32,36,128]{2,1,0:T(8,128)(2,1)}), bf16[32,36,128]{2,1,0:T(8,128)(2,1)S(1)}, u32[]{:S(2)}, u32[]{:S(2)}) async-start(bf16[32,36,128]{2,1,0:T(8,128)(2,1)} %get-tuple-element.15), calls=%async_computation.2 | async-start | bytes 655360 | tf_op jit(solution)/shard_map/all_to_all | solution.py:233
  85.4 7.6 %collective-permute-start.2 = (bf16[2,256,128]{2,1,0:T(8,128)(2,1)S(1)}, bf16[2,256,128]{2,1,0:T(8,128)(2,1)S(1)}, u32[]{:S(2)}, u32[]{:S(2)}) collective-permute-start(bf16[2,256,128]{2,1,0:T(8,128)(2,1)S(1)} %get-tuple-element.13), channel_id=1, source_target_pairs={{0,1},{1,2},{2,3},{3,4},{4,5},{5,6},{6,7},{8,9},{9,10},{10,11},{11... | collective-permute-start | bytes 393224 | tf_op jit(solution)/shard_map/ppermute | solution.py:325
  89.1 7.6 %collective-permute-start.3 = (bf16[2,256,128]{2,1,0:T(8,128)(2,1)S(1)}, bf16[2,256,128]{2,1,0:T(8,128)(2,1)S(1)}, u32[]{:S(2)}, u32[]{:S(2)}) collective-permute-start(bf16[2,256,128]{2,1,0:T(8,128)(2,1)S(1)} %get-tuple-element.14), channel_id=1, source_target_pairs={{1,0},{2,1},{3,2},{4,3},{5,4},{6,5},{7,6},{9,8},{10,9},{11,10},{12... | collective-permute-start | bytes 393224 | tf_op jit(solution)/shard_map/ppermute | solution.py:326
  98.3 17.9 %all-to-all-start.3 = ((bf16[32,36,128]{2,1,0:T(8,128)(2,1)}), bf16[32,36,128]{2,1,0:T(8,128)(2,1)S(1)}, u32[]{:S(2)}, u32[]{:S(2)}) async-start(bf16[32,36,128]{2,1,0:T(8,128)(2,1)} %sum_parts.1), calls=%async_computation.3 | async-start | bytes 655360 | tf_op jit(solution)/shard_map/all_to_all | solution.py:233

commit v3 on v2

--- a/solution.py
+++ b/solution.py
@@ -35,22 +35,34 @@
 
 
 def pack_kernel(
-    regions, heads, per_device, query_ref, key_ref, value_ref, cot_ref, out_ref, first_ref, last_ref, held, ready, sems
+    regions,
+    heads,
+    per_device,
+    query_ref,
+    key_ref,
+    value_ref,
+    cot_ref,
+    out_ref,
+    first_ref,
+    last_ref,
+    held,
+    ready,
+    edges,
+    sems,
 ):
     width = held.shape[3] // heads
-    copies = [
+    rows = cot_ref.shape[1]
+    loads = [
         pltpu.make_async_copy(ref, held.at[which], sems.at[which])
         for which, ref in enumerate((query_ref, key_ref, value_ref))
     ]
-    rows = cot_ref.shape[1]
-    edges = [
-        pltpu.make_async_copy(cot_ref.at[:, 0], first_ref, sems.at[3]),
-        pltpu.make_async_copy(cot_ref.at[:, rows - 1], last_ref, sems.at[4]),
-    ]
-    for copy in copies + edges:
-        copy.start()
-    for which, copy in enumerate(copies):
-        copy.wait()
+    loads.append(pltpu.make_async_copy(cot_ref.at[:, 0], edges.at[0], sems.at[3]))
+    loads.append(pltpu.make_async_copy(cot_ref.at[:, rows - 1], edges.at[1], sems.at[4]))
+    for load in loads:
+        load.start()
+    stores = []
+    for which in range(3):
+        loads[which].wait()
         for head in range(heads):
             block = held[which, :, :, head * width : (head + 1) * width].astype(jnp.float32)
             for region in range(regions):
@@ -58,52 +70,96 @@
                 ready[item // per_device, which, item % per_device] = block[:, region, :].astype(
                     jnp.bfloat16
                 )
-        store = pltpu.make_async_copy(ready.at[:, which], out_ref.at[:, which], sems.at[5 + which])
-        store.start()
-        edges.append(store)
-    for copy in edges:
-        copy.wait()
-
-
-def attend_kernel(block_rows, group, lengths_ref, packed_ref, before_ref, after_ref, out_ref):
+        stores.append(
+            pltpu.make_async_copy(ready.at[:, which], out_ref.at[:, which], sems.at[5 + which])
+        )
+        stores[-1].start()
+        if which == 0:
+            for edge, ref in enumerate((first_ref, last_ref)):
+                loads[3 + edge].wait()
+                stores.append(pltpu.make_async_copy(edges.at[edge], ref, sems.at[8 + edge]))
+                stores[-1].start()
+    for store in stores:
+        store.wait()
+
+
+def attend_kernel(
+    block_rows, group, lengths_ref, packed_ref, before_ref, after_ref, out_ref, mixed_ref, sems
+):
     del before_ref, after_ref
     sources, _, per_device, tokens, width = packed_ref.shape
     capacity = sources * tokens
     per_block = block_rows // tokens
+    blocks = capacity // block_rows
     factor = math.log2(math.e) / math.sqrt(width)
-    slots = lax.broadcasted_iota(jnp.int32, (capacity, block_rows), 0)
+    slots = lax.broadcasted_iota(jnp.int32, (1, capacity), 1)
+
+    def rows_of(block):
+        return slice(block * per_block, (block + 1) * per_block)
+
+    def clear(item, block):
+        mixed_ref[rows_of(block), item] = jnp.zeros((per_block, tokens, width), jnp.bfloat16)
+
+    def score(item, block):
+        query = packed_ref[rows_of(block), 0, item].reshape(block_rows, width)
+        keys = packed_ref[:, 1, item].reshape(capacity, width)
+        return lax.dot_general(
+            query, keys, (((1,), (1,)), ((), ())), preferred_element_type=jnp.float32
+        )
+
+    def finish(item, block, scores, key_valid):
+        values = packed_ref[:, 2, item].reshape(capacity, width)
+        scores = jnp.where(key_valid, scores * factor, -1e30)
+        powers = jnp.exp2(scores - jnp.max(scores, axis=1, keepdims=True))
+        totals = jnp.sum(powers, axis=1, keepdims=True)
+        mixed = jnp.dot(powers.astype(jnp.bfloat16), values, preferred_element_type=jnp.float32)
+        mixed = (mixed / totals).astype(jnp.bfloat16)
+        mixed_ref[rows_of(block), item] = mixed.reshape(per_block, tokens, width)
+
+    def attend(tasks, length):
+        key_valid = slots < length
+        waiting = None
+        for item, block in tasks:
+            scores = score(item, block)
+            if waiting is not None:
+                finish(*waiting, key_valid)
+            waiting = (item, block, scores)
+        finish(*waiting, key_valid)
+
+    stores = []
     for lead in range(group):
         length = lengths_ref[lead]
-        items = range(lead, per_device, group)
-        for block in range(capacity // block_rows):
-            rows = slice(block * per_block, (block + 1) * per_block)
-
-            @pl.when(block * block_rows < length)
-            def _(items=items, rows=rows, length=length):
-                key_valid = slots < length
-                for item in items:
-                    query = packed_ref[rows, 0, item].reshape(block_rows, width)
-                    keys = packed_ref[:, 1, item].reshape(capacity, width)
-                    values = packed_ref[:, 2, item].reshape(capacity, width)
-                    scores = lax.dot_general(
-                        keys, query, (((1,), (1,)), ((), ())), preferred_element_type=jnp.float32
-                    )
-                    scores = jnp.where(key_valid, scores * factor, -1e30)
-                    powers = jnp.exp2(scores - jnp.max(scores, axis=0, keepdims=True))
-                    totals = jnp.sum(powers, axis=0, keepdims=True)
-                    mixed = lax.dot_general(
-                        values,
-                        powers.astype(jnp.bfloat16),
-                        (((0,), (0,)), ((), ())),
-                        preferred_element_type=jnp.float32,
-                    )
-                    mixed = (mixed / totals).T.astype(jnp.bfloat16)
-                    out_ref[rows, item] = mixed.reshape(per_block, tokens, width)
-
-            @pl.when(block * block_rows >= length)
-            def _(items=items, rows=rows):
-                for item in items:
-                    out_ref[rows, item] = jnp.zeros((per_block, tokens, width), jnp.bfloat16)
+        items = list(range(lead, per_device, group))
+        for block in range(0, blocks, 2):
+            pair = list(range(block, min(block + 2, blocks)))
+            start = block * block_rows
+
+            @pl.when(length > start + block_rows)
+            def _(items=items, pair=pair, length=length):
+                attend([(item, one) for one in pair for item in items], length)
+
+            @pl.when((length > start) & (length <= start + block_rows))
+            def _(items=items, pair=pair, length=length):
+                attend([(item, pair[0]) for item in items], length)
+                for one in pair[1:]:
+                    for item in items:
+                        clear(item, one)
+
+            @pl.when(length <= start)
+            def _(items=items, pair=pair):
+                for one in pair:
+                    for item in items:
+                        clear(item, one)
+
+            rows = slice(pair[0] * per_block, (pair[-1] + 1) * per_block)
+            for item in items:
+                store = pltpu.make_async_copy(
+                    mixed_ref.at[rows, item], out_ref.at[rows, item], sems.at[len(stores)]
+                )
+                store.start()
+                stores.append(store)
+    for store in stores:
+        store.wait()
 
 
 def three_windows(padded, columns):
@@ -210,12 +266,14 @@
                 strips.pop(0)
 
 
-def sum_kernel(factor, parts_ref, before_ref, after_ref, out_ref):
-    del before_ref, after_ref
+def sum_kernel(factor, parts_ref, *refs):
+    out_ref = refs[-1]
     total = parts_ref[0].astype(jnp.float32)
     for part in range(1, parts_ref.shape[0]):
         total = total + parts_ref[part].astype(jnp.float32)
-    total = (total * factor).astype(jnp.bfloat16)
+    if factor is not None:
+        total = total * factor
+    total = total.astype(jnp.bfloat16)
     for part in range(out_ref.shape[0]):
         out_ref[part] = total
 
@@ -229,8 +287,22 @@
             out_ref[start : start + kept, :] = parts_ref[part, :kept, :].astype(jnp.float32)
 
 
-def swap(parts, axes):
-    return lax.all_to_all(parts, axes, split_axis=0, concat_axis=0, tiled=True)
+def swap(parts, axes, groups=None):
+    return lax.all_to_all(
+        parts, axes, split_axis=0, concat_axis=0, axis_index_groups=groups, tiled=True
+    )
+
+
+def planes_and_columns(outer, seq_count):
+    inner = 1
+    while seq_count % (2 * inner) == 0 and (2 * inner) ** 2 <= seq_count:
+        inner *= 2
+    planes = [
+        [o * seq_count + start + i for o in range(outer) for i in range(inner)]
+        for start in range(0, seq_count, inner)
+    ]
+    columns = [list(column) for column in zip(*planes)]
+    return planes, columns
 
 
 def body(query_rows, key_rows, value_rows, region_lengths, norm_gain, conv_weight, cotangent):
@@ -238,7 +310,7 @@
     width = model_width // HEADS
     seq_count = lax.axis_size("seq")
     seq_index = lax.axis_index("seq")
-    everyone = lax.axis_size("dp") * seq_count
+    planes, lines = planes_and_columns(lax.axis_size("dp"), seq_count)
     columns = tokens * PATCH
     capacity = seq_count * tokens
     per_device = regions * HEADS // seq_count
@@ -260,7 +332,8 @@
         scratch=[
             pltpu.VMEM((3,) + query_rows.shape, jnp.bfloat16),
             pltpu.VMEM((seq_count, 3, per_device, tokens, width), jnp.bfloat16),
-            pltpu.SemaphoreType.DMA((8,)),
+            pltpu.VMEM((2,) + edge_shape.shape, jnp.bfloat16),
+            pltpu.SemaphoreType.DMA((10,)),
         ],
         moved=6 * local_bytes,
         grant=VMEM_WHOLE,
@@ -285,13 +358,18 @@
         "attend",
         jax.ShapeDtypeStruct((seq_count, per_device, tokens, width), jnp.bfloat16),
         [SMEM(), VMEM(), ANY(), ANY()],
+        out_specs=HBM(),
+        scratch=[
+            pltpu.VMEM((seq_count, per_device, tokens, width), jnp.bfloat16),
+            pltpu.SemaphoreType.DMA((per_device * -(-capacity // block_rows),)),
+        ],
         flops=4 * per_device * capacity * capacity * width,
         moved=4 * local_bytes,
         exps=per_device * capacity * capacity,
     )(item_lengths, packed, cot_before, cot_after)
     attended = swap(mixed, "seq").reshape(HEADS, regions, tokens, width)
 
-    chunk_rows = -(-9 * width // everyone)
+    chunk_rows = -(-9 * width // len(lines))
     pixel_rows = regions * PATCH * columns
     conv_flops = 18 * pixel_rows * width * width
     image, first, last, grad_parts = call(
@@ -301,14 +379,14 @@
             jax.ShapeDtypeStruct((regions, PATCH, columns, width), jnp.bfloat16),
             edge_shape,
             edge_shape,
-            jax.ShapeDtypeStruct((everyone, chunk_rows, width), jnp.bfloat16),
+            jax.ShapeDtypeStruct((len(lines), chunk_rows, width), jnp.bfloat16),
         ],
         [SMEM(), SMEM()] + [VMEM()] * 5,
         scratch=[
             pltpu.VMEM((regions, PATCH, columns + 2 * RIM, width), jnp.float32),
             pltpu.VMEM((pixel_rows, 3 * width), jnp.bfloat16),
             pltpu.VMEM((pixel_rows, 3 * width), jnp.bfloat16),
-            pltpu.VMEM((everyone * chunk_rows, width), jnp.float32),
+            pltpu.VMEM((len(lines) * chunk_rows, width), jnp.float32),
         ],
         flops=conv_flops,
         moved=4 * local_bytes,
@@ -321,17 +399,25 @@
         cot_before,
         cot_after,
     )
-    grad_parts = swap(grad_parts, ("dp", "seq"))
+    grad_parts = swap(grad_parts, ("dp", "seq"), planes)
     before = lax.ppermute(last, "seq", up)
     after = lax.ppermute(first, "seq", down)
+    plane_sums = call(
+        functools.partial(sum_kernel, None),
+        "sum_plane",
+        jax.ShapeDtypeStruct((len(planes), chunk_rows, width), jnp.bfloat16),
+        [VMEM()],
+        moved=4 * grad_parts.size,
+    )(grad_parts)
+    plane_sums = swap(plane_sums, ("dp", "seq"), lines)
     sums = call(
         functools.partial(sum_kernel, 1.0 / math.sqrt(PATCH * columns)),
-        "sum_parts",
+        "sum_planes",
         jax.ShapeDtypeStruct(grad_parts.shape, jnp.bfloat16),
         [VMEM(), ANY(), ANY()],
         moved=4 * grad_parts.size,
-    )(grad_parts, before, after)
-    sums = swap(sums, ("dp", "seq"))
+    )(plane_sums, before, after)
+    sums = swap(sums, ("dp", "seq"), planes)
     decoded = call(
         decode_kernel,
         "decode",

time: 118 us -> 114 us (0.966)
  blocking collectives: 0 us -> 11.2 us
  Pallas kernels: 21.2 us -> 14.2 us
  waiting for transfers between devices: 64.8 us -> 58.9 us
  starting transfers between devices: 30.3 us -> 27.9 us
    all_to_all x0 -> x1, blocking collectives: none -> 11.2 us  [swap(): lax.all_to_all(parts, axes, split_axis=0, concat_axis=0, axis_index_group...]
    all_to_all x4, waiting for transfers between devices: 45.9 us -> 39.7 us  [swap(): lax.all_to_all(parts, axes, split_axis=0, concat_axis=0, axis_index_group...]
    pallas_call x1, Pallas kernels: 9.12 us -> 3.92 us  [body(): call(functools.partial(pack_kernel, regions, HEADS, per_device), 'pack',...]
    pallas_call x1, Pallas kernels: 4.54 us -> 2.82 us  [body(): call(functools.partial(attend_kernel, block_rows, group), 'attend', jax.S...]
    ppermute x1, waiting for transfers between devices: 3.63 us -> 4.97 us  [body(): after = lax.ppermute(first, 'seq', down)]
    all_to_all x4, starting transfers between devices: 20.1 us -> 18.8 us  [swap(): lax.all_to_all(parts, axes, split_axis=0, concat_axis=0, axis_index_group...]
  transfers between devices with their start and end apart: 8 -> 8, of which waited for: 7 -> 6; matrix products, arithmetic and copies ran while one was open for 0% -> 0% of each run, Pallas kernels for 2% -> 2%
where the time goes in v3:
time: 114 us; the launch traced here: 113 us
  waiting for transfers between devices  58.9 us (52%)
  starting transfers between devices  27.9 us (24%)
  Pallas kernels  14.2 us (12%)
  blocking collectives  11.2 us (10%)
    all_to_all x4, waiting for transfers between devices, swap(): lax.all_to_all(parts, axes, split_axis=0, concat_axis=0, axis_index_group...  39.7 us
    all_to_all x4, starting transfers between devices, swap(): lax.all_to_all(parts, axes, split_axis=0, concat_axis=0, axis_index_group...  18.8 us
    ppermute x1, waiting for transfers between devices, body(): cot_before = lax.ppermute(cot_last, 'seq', up)  12.6 us
    all_to_all x1, blocking collectives, swap(): lax.all_to_all(parts, axes, split_axis=0, concat_axis=0, axis_index_group...  11.2 us
    ppermute x1, waiting for transfers between devices, body(): after = lax.ppermute(first, 'seq', down)  4.97 us
    pallas_call x1, Pallas kernels, body(): call(functools.partial(pack_kernel, regions, HEADS, per_device), 'pack',...  3.92 us
    ppermute x1, starting transfers between devices, body(): cot_before = lax.ppermute(cot_last, 'seq', up)  3.92 us
    pallas_call x1, Pallas kernels, body(): call(functools.partial(norm_kernel, chunk_rows), 'norm_and_gradient', [ja...  2.89 us
  transfers between devices with their start and end apart: 8, of which 6 were waited for; matrix products, arithmetic and copies ran while one was open for 0% of the time, Pallas kernels for 2%

profile of v3, /device:TPU:0, one launch (start us, length us, event | category | flops | bytes accessed | tf_op | source)
XLA Modules:
  0.0 113.1 jit_solution(6685198226805771107)
XLA Ops:
  0.6 3.9 %pack.1 = (bf16[8,3,4,64,128]{4,3,2,1,0:T(8,128)(2,1)}, bf16[2,256,128]{2,1,0:T(8,128)(2,1)}, bf16[2,256,128]{2,1,0:T(8,128)(2,1)}) custom-call(bf16[64,2,2048]{2,1,0:T(2,128)(2,1)} %query_ref.1, bf16[64,2,2048]{2,1,0:T(2,128)(2,1)} %key_ref.1, bf16[64,2,2048]{2,1,0:T(2,128)(2,1)} %value_ref.1, bf16[2,4,256,128]{3,2,1,0:T(8,128)(2,1)} %cot_ref.3), custom_call_target="tpu_custom_call" | custom-call | bytes 3145728 | tf_op jit(solution)/shard_map/pack/pallas_call | solution.py:322
  4.6 0.0 copy-start.5
  4.6 0.0 copy-start.4
  4.6 0.0 copy-start.3
  4.6 7.4 %all-to-all-start = ((bf16[8,3,4,64,128]{4,3,2,1,0:T(8,128)(2,1)}), bf16[8,3,4,64,128]{4,3,2,1,0:T(8,128)(2,1)S(1)}, u32[]{:S(2)}, u32[]{:S(2)}) async-start(bf16[8,3,4,64,128]{4,3,2,1,0:T(8,128)(2,1)} %get-tuple-element.9), calls=%async_computation | async-start | bytes 3145728 | tf_op jit(solution)/shard_map/all_to_all | solution.py:291
  12.0 0.0 copy-done.5
  12.0 3.9 %collective-permute-start = (bf16[2,256,128]{2,1,0:T(8,128)(2,1)S(1)}, bf16[2,256,128]{2,1,0:T(8,128)(2,1)S(1)}, u32[]{:S(2)}, u32[]{:S(2)}) collective-permute-start(bf16[2,256,128]{2,1,0:T(8,128)(2,1)S(1)} %copy-done.5), channel_id=1, source_target_pairs={{0,1},{1,2},{2,3},{3,4},{4,5},{5,6},{6,7},{8,9},{9,10},{10,11},{11... | collective-permute-start | bytes 393224 | tf_op jit(solution)/shard_map/ppermute | solution.py:342
  15.9 0.0 copy-done.4
  15.9 1.3 %collective-permute-start.1 = (bf16[2,256,128]{2,1,0:T(8,128)(2,1)S(1)}, bf16[2,256,128]{2,1,0:T(8,128)(2,1)S(1)}, u32[]{:S(2)}, u32[]{:S(2)}) collective-permute-start(bf16[2,256,128]{2,1,0:T(8,128)(2,1)S(1)} %copy-done.4), channel_id=1, source_target_pairs={{1,0},{2,1},{3,2},{4,3},{5,4},{6,5},{7,6},{9,8},{10,9},{11,10},{12... | collective-permute-start | bytes 393224 | tf_op jit(solution)/shard_map/ppermute | solution.py:343
  17.3 0.0 copy-done.3
  17.3 0.1 fusion.lengths_ref
  17.3 0.0 copy-start
  17.3 0.0 copy-start.2
  17.4 12.6 %collective-permute-done.before_ref.cot_before_ref = bf16[2,256,128]{2,1,0:T(8,128)(2,1)S(1)} collective-permute-done((bf16[2,256,128]{2,1,0:T(8,128)(2,1)S(1)}, bf16[2,256,128]{2,1,0:T(8,128)(2,1)S(1)}, u32[]{:S(2)}, u32[]{:S(2)}) %collective-permute-start) | collective-permute-done | bytes 131104 | tf_op jit(solution)/shard_map/ppermute | solution.py:342
  29.9 0.0 collective-permute-done.1.after_ref.cot_after_ref
  29.9 20.5 %all-to-all-done.packed_ref = bf16[8,3,4,64,128]{4,3,2,1,0:T(8,128)(2,1)S(1)} async-done(((bf16[8,3,4,64,128]{4,3,2,1,0:T(8,128)(2,1)}), bf16[8,3,4,64,128]{4,3,2,1,0:T(8,128)(2,1)S(1)}, u32[]{:S(2)}, u32[]{:S(2)}) %all-to-all-start) | async-done | bytes 1572896 | tf_op jit(solution)/shard_map/all_to_all | solution.py:291
  50.4 2.8 %attend.1 = bf16[8,4,64,128]{3,2,1,0:T(8,128)(2,1)} custom-call(s32[4]{0:T(128)S(1)} %fusion.lengths_ref, bf16[8,3,4,64,128]{4,3,2,1,0:T(8,128)(2,1)S(1)} %all-to-all-done.packed_ref, bf16[2,256,128]{2,1,0:T(8,128)(2,1)S(1)} %collective-permute-done.before_ref.cot_before_ref, bf16[2,256,128]{2,1,0:T(8,128)(2,1)S(1)} %collective-permute-done.1.after_ref.cot_after_ref), custom_call_target="tpu_custom_call" | custom-call | flops 536870912 | bytes 2097152 | tf_op jit(solution)/shard_map/attend/pallas_call | solution.py:356
  53.2 4.2 %all-to-all-start.1 = ((bf16[8,4,64,128]{3,2,1,0:T(8,128)(2,1)}), bf16[8,4,64,128]{3,2,1,0:T(8,128)(2,1)S(1)}, u32[]{:S(2)}, u32[]{:S(2)}) async-start(bf16[8,4,64,128]{3,2,1,0:T(8,128)(2,1)} %attend.1), calls=%async_computation.1 | async-start | bytes 1048576 | tf_op jit(solution)/shard_map/all_to_all | solution.py:291
  57.4 14.7 %all-to-all-done.1 = bf16[8,4,64,128]{3,2,1,0:T(8,128)(2,1)S(1)} async-done(((bf16[8,4,64,128]{3,2,1,0:T(8,128)(2,1)}), bf16[8,4,64,128]{3,2,1,0:T(8,128)(2,1)S(1)}, u32[]{:S(2)}, u32[]{:S(2)}) %all-to-all-start.1) | async-done | bytes 524320 | tf_op jit(solution)/shard_map/all_to_all | solution.py:291
  72.1 0.0 copy-done
  72.1 0.0 copy-done.2
  72.1 2.9 %norm_and_gradient.1 = (bf16[2,4,256,128]{3,2,1,0:T(8,128)(2,1)S(1)}, bf16[2,256,128]{2,1,0:T(8,128)(2,1)S(1)}, bf16[2,256,128]{2,1,0:T(8,128)(2,1)S(1)}, bf16[8,144,128]{2,1,0:T(8,128)(2,1)S(1)}) custom-call(s32[2]{0:T(128)S(1)} %copy-done.3, s32[1]{0:T(128)} %bitcast.base_ref, bf16[16,2,64,128]{3,2,1,0:T(8,128)(2,1)S(1)} %bitcast.5, ...), custom_call_target="tpu_custom_call" | custom-call | flops 603979776 | bytes 2097152 | tf_op jit(solution)/shard_map/norm_and_gradient/pallas_call | solution.py:375
  75.0 0.0 copy-start.1
  75.0 11.2 %all_to_all.25.parts_ref = bf16[8,144,128]{2,1,0:T(8,128)(2,1)S(1)} all-to-all(bf16[8,144,128]{2,1,0:T(8,128)(2,1)S(1)} %get-tuple-element.15), channel_id=1, replica_groups={{0,1,8,9,16,17,24,25},{2,3,10,11,18,19,26,27},{4,5,12,13,20,21,28,29},{..., dimensions={0} | all-to-all | bytes 589824 | tf_op jit(solution)/shard_map/all_to_all | solution.py:291
  86.2 0.7 sum_plane.1
  86.9 3.3 %all-to-all-start.3 = ((bf16[4,144,128]{2,1,0:T(8,128)(2,1)}), bf16[4,144,128]{2,1,0:T(8,128)(2,1)S(1)}, u32[]{:S(2)}, u32[]{:S(2)}) async-start(bf16[4,144,128]{2,1,0:T(8,128)(2,1)} %sum_plane.1), calls=%async_computation.3 | async-start | bytes 294912 | tf_op jit(solution)/shard_map/all_to_all | solution.py:291
  90.3 2.6 %collective-permute-start.2 = (bf16[2,256,128]{2,1,0:T(8,128)(2,1)S(1)}, bf16[2,256,128]{2,1,0:T(8,128)(2,1)S(1)}, u32[]{:S(2)}, u32[]{:S(2)}) collective-permute-start(bf16[2,256,128]{2,1,0:T(8,128)(2,1)S(1)} %get-tuple-element.13), channel_id=1, source_target_pairs={{0,1},{1,2},{2,3},{3,4},{4,5},{5,6},{6,7},{8,9},{9,10},{10,11},{11... | collective-permute-start | bytes 393224 | tf_op jit(solution)/shard_map/ppermute | solution.py:403
  92.8 1.3 %collective-permute-start.3 = (bf16[2,256,128]{2,1,0:T(8,128)(2,1)S(1)}, bf16[2,256,128]{2,1,0:T(8,128)(2,1)S(1)}, u32[]{:S(2)}, u32[]{:S(2)}) collective-permute-start(bf16[2,256,128]{2,1,0:T(8,128)(2,1)S(1)} %get-tuple-element.14), channel_id=1, source_target_pairs={{1,0},{2,1},{3,2},{4,3},{5,4},{6,5},{7,6},{9,8},{10,9},{11,10},{12... | collective-permute-start | bytes 393224 | tf_op jit(solution)/shard_map/ppermute | solution.py:404
  94.1 1.6 %collective-permute-done.2.before_ref.refs_0_ = bf16[2,256,128]{2,1,0:T(8,128)(2,1)S(1)} collective-permute-done((bf16[2,256,128]{2,1,0:T(8,128)(2,1)S(1)}, bf16[2,256,128]{2,1,0:T(8,128)(2,1)S(1)}, u32[]{:S(2)}, u32[]{:S(2)}) %collective-permute-start.2) | collective-permute-done | bytes 131104 | tf_op jit(solution)/shard_map/ppermute | solution.py:403
  95.8 5.0 %collective-permute-done.3.after_ref.refs_1_ = bf16[2,256,128]{2,1,0:T(8,128)(2,1)S(1)} collective-permute-done((bf16[2,256,128]{2,1,0:T(8,128)(2,1)S(1)}, bf16[2,256,128]{2,1,0:T(8,128)(2,1)S(1)}, u32[]{:S(2)}, u32[]{:S(2)}) %collective-permute-start.3) | collective-permute-done | bytes 131104 | tf_op jit(solution)/shard_map/ppermute | solution.py:404
  100.7 0.0 all-to-all-done.3.parts_ref
  100.7 0.7 sum_planes.1
  101.5 3.9 %all-to-all-start.4 = ((bf16[8,144,128]{2,1,0:T(8,128)(2,1)}), bf16[8,144,128]{2,1,0:T(8,128)(2,1)S(1)}, u32[]{:S(2)}, u32[]{:S(2)}) async-start(bf16[8,144,128]{2,1,0:T(8,128)(2,1)} %sum_planes.1), calls=%async_computation.4 | async-start | bytes 589824 | tf_op jit(solution)/shard_map/all_to_all | solution.py:291
  105.4 0.0 copy-done.1
  105.4 2.2 %decode.1 = bf16[2,4,256,128]{3,2,1,0:T(8,128)(2,1)} custom-call(bf16[2,4,256,128]{3,2,1,0:T(8,128)(2,1)S(1)} %get-tuple-element.12.image_ref, bf16[2,256,128]{2,1,0:T(8,128)(2,1)S(1)} %collective-permute-done.2.before_ref.refs_0_, bf16[2,256,128]{2,1,0:T(8,128)(2,1)S(1)} %collective-permute-done.3.after_ref.refs_1_, bf16[3,384,128]{2,1,0:T(8,128)(2,1)S(1)} %bitcast.6), custom_call_target="tpu_custom_call" | custom-call | flops 603979776 | bytes 1048576 | tf_op jit(solution)/shard_map/decode/pallas_call | solution.py:421
  107.6 4.6 %all-to-all-done.4.parts_ref = bf16[8,144,128]{2,1,0:T(8,128)(2,1)S(1)} async-done(((bf16[8,144,128]{2,1,0:T(8,128)(2,1)}), bf16[8,144,128]{2,1,0:T(8,128)(2,1)S(1)}, u32[]{:S(2)}, u32[]{:S(2)}) %all-to-all-start.4) | async-done | bytes 294944 | tf_op jit(solution)/shard_map/all_to_all | solution.py:291
  112.2 0.9 spread_sums.1
  (1 shorter events, 0.0 us)
Async XLA Ops:
  4.6 7.4 %copy-start.5 = (bf16[2,256,128]{2,1,0:T(8,128)(2,1)S(1)}, bf16[2,256,128]{2,1,0:T(8,128)(2,1)}, u32[]{:S(2)}) copy-start(bf16[2,256,128]{2,1,0:T(8,128)(2,1)} %get-tuple-element.10) | copy-start | bytes 393220
  4.6 11.4 %copy-start.4 = (bf16[2,256,128]{2,1,0:T(8,128)(2,1)S(1)}, bf16[2,256,128]{2,1,0:T(8,128)(2,1)}, u32[]{:S(2)}) copy-start(bf16[2,256,128]{2,1,0:T(8,128)(2,1)} %get-tuple-element.11) | copy-start | bytes 393220
  4.6 12.7 %copy-start.3 = (s32[2]{0:T(128)S(1)}, s32[2]{0:T(128)}, u32[]{:S(2)}) copy-start(s32[2]{0:T(128)} %lengths_ref.1) | copy-start | bytes 28
  4.6 45.8 %all-to-all-start = ((bf16[8,3,4,64,128]{4,3,2,1,0:T(8,128)(2,1)}), bf16[8,3,4,64,128]{4,3,2,1,0:T(8,128)(2,1)S(1)}, u32[]{:S(2)}, u32[]{:S(2)}) async-start(bf16[8,3,4,64,128]{4,3,2,1,0:T(8,128)(2,1)} %get-tuple-element.9), calls=%async_computation | async-start | bytes 3145728 | tf_op jit(solution)/shard_map/all_to_all | solution.py:291
  12.0 17.9 %collective-permute-start = (bf16[2,256,128]{2,1,0:T(8,128)(2,1)S(1)}, bf16[2,256,128]{2,1,0:T(8,128)(2,1)S(1)}, u32[]{:S(2)}, u32[]{:S(2)}) collective-permute-start(bf16[2,256,128]{2,1,0:T(8,128)(2,1)S(1)} %copy-done.5), channel_id=1, source_target_pairs={{0,1},{1,2},{2,3},{3,4},{4,5},{5,6},{6,7},{8,9},{9,10},{10,11},{11... | collective-permute-start | bytes 393224 | tf_op jit(solution)/shard_map/ppermute | solution.py:342
  15.9 14.0 %collective-permute-start.1 = (bf16[2,256,128]{2,1,0:T(8,128)(2,1)S(1)}, bf16[2,256,128]{2,1,0:T(8,128)(2,1)S(1)}, u32[]{:S(2)}, u32[]{:S(2)}) collective-permute-start(bf16[2,256,128]{2,1,0:T(8,128)(2,1)S(1)} %copy-done.4), channel_id=1, source_target_pairs={{1,0},{2,1},{3,2},{4,3},{5,4},{6,5},{7,6},{9,8},{10,9},{11,10},{12... | collective-permute-start | bytes 393224 | tf_op jit(solution)/shard_map/ppermute | solution.py:343
  17.3 54.7 %copy-start = (bf16[2,4,256,128]{3,2,1,0:T(8,128)(2,1)S(1)}, bf16[2,4,256,128]{3,2,1,0:T(8,128)(2,1)}, u32[]{:S(2)}) copy-start(bf16[2,4,256,128]{3,2,1,0:T(8,128)(2,1)} %cot_ref.3) | copy-start | bytes 1572868
  17.3 54.7 %copy-start.2 = (f32[2048]{0:T(1024)S(1)}, f32[2048]{0:T(1024)}, u32[]{:S(2)}) copy-start(f32[2048]{0:T(1024)} %param.11) | copy-start | bytes 24580
  53.2 18.8 %all-to-all-start.1 = ((bf16[8,4,64,128]{3,2,1,0:T(8,128)(2,1)}), bf16[8,4,64,128]{3,2,1,0:T(8,128)(2,1)S(1)}, u32[]{:S(2)}, u32[]{:S(2)}) async-start(bf16[8,4,64,128]{3,2,1,0:T(8,128)(2,1)} %attend.1), calls=%async_computation.1 | async-start | bytes 1048576 | tf_op jit(solution)/shard_map/all_to_all | solution.py:291
  75.0 30.4 %copy-start.1 = (bf16[9,128,128]{2,1,0:T(8,128)(2,1)S(1)}, bf16[9,128,128]{2,1,0:T(8,128)(2,1)}, u32[]{:S(2)}) copy-start(bf16[9,128,128]{2,1,0:T(8,128)(2,1)} %param.12) | copy-start | bytes 884740
  86.9 13.8 %all-to-all-start.3 = ((bf16[4,144,128]{2,1,0:T(8,128)(2,1)}), bf16[4,144,128]{2,1,0:T(8,128)(2,1)S(1)}, u32[]{:S(2)}, u32[]{:S(2)}) async-start(bf16[4,144,128]{2,1,0:T(8,128)(2,1)} %sum_plane.1), calls=%async_computation.3 | async-start | bytes 294912 | tf_op jit(solution)/shard_map/all_to_all | solution.py:291
  90.3 5.5 %collective-permute-start.2 = (bf16[2,256,128]{2,1,0:T(8,128)(2,1)S(1)}, bf16[2,256,128]{2,1,0:T(8,128)(2,1)S(1)}, u32[]{:S(2)}, u32[]{:S(2)}) collective-permute-start(bf16[2,256,128]{2,1,0:T(8,128)(2,1)S(1)} %get-tuple-element.13), channel_id=1, source_target_pairs={{0,1},{1,2},{2,3},{3,4},{4,5},{5,6},{6,7},{8,9},{9,10},{10,11},{11... | collective-permute-start | bytes 393224 | tf_op jit(solution)/shard_map/ppermute | solution.py:403
  92.8 7.9 %collective-permute-start.3 = (bf16[2,256,128]{2,1,0:T(8,128)(2,1)S(1)}, bf16[2,256,128]{2,1,0:T(8,128)(2,1)S(1)}, u32[]{:S(2)}, u32[]{:S(2)}) collective-permute-start(bf16[2,256,128]{2,1,0:T(8,128)(2,1)S(1)} %get-tuple-element.14), channel_id=1, source_target_pairs={{1,0},{2,1},{3,2},{4,3},{5,4},{6,5},{7,6},{9,8},{10,9},{11,10},{12... | collective-permute-start | bytes 393224 | tf_op jit(solution)/shard_map/ppermute | solution.py:404
  101.5 10.7 %all-to-all-start.4 = ((bf16[8,144,128]{2,1,0:T(8,128)(2,1)}), bf16[8,144,128]{2,1,0:T(8,128)(2,1)S(1)}, u32[]{:S(2)}, u32[]{:S(2)}) async-start(bf16[8,144,128]{2,1,0:T(8,128)(2,1)} %sum_planes.1), calls=%async_computation.4 | async-start | bytes 589824 | tf_op jit(solution)/shard_map/all_to_all | solution.py:291

commit v4 on v3

--- a/solution.py
+++ b/solution.py
@@ -38,18 +38,16 @@
     regions,
     heads,
     per_device,
+    index_ref,
     query_ref,
     key_ref,
     value_ref,
     cot_ref,
-    out_ref,
-    first_ref,
-    last_ref,
-    held,
-    ready,
-    edges,
-    sems,
+    *refs,
 ):
+    held, ready, edges, sems = refs[-4:]
+    first_ref, last_ref = refs[-6:-4]
+    out_refs = refs[:-6]
     width = held.shape[3] // heads
     rows = cot_ref.shape[1]
     loads = [
@@ -67,26 +65,36 @@
             block = held[which, :, :, head * width : (head + 1) * width].astype(jnp.float32)
             for region in range(regions):
                 item = head * regions + region
-                ready[item // per_device, which, item % per_device] = block[:, region, :].astype(
-                    jnp.bfloat16
+                slot = lax.bitwise_xor(index_ref[0], item // per_device)
+                ready[slot, which, item % per_device] = block[:, region, :].astype(jnp.bfloat16)
+        for number, ref in enumerate(out_refs):
+            stores.append(
+                pltpu.make_async_copy(
+                    ready.at[number, which], ref.at[which], sems.at[7 + 3 * number + which]
                 )
-        stores.append(
-            pltpu.make_async_copy(ready.at[:, which], out_ref.at[:, which], sems.at[5 + which])
-        )
-        stores[-1].start()
+            )
+            stores[-1].start()
         if which == 0:
             for edge, ref in enumerate((first_ref, last_ref)):
                 loads[3 + edge].wait()
-                stores.append(pltpu.make_async_copy(edges.at[edge], ref, sems.at[8 + edge]))
+                stores.append(pltpu.make_async_copy(edges.at[edge], ref, sems.at[5 + edge]))
                 stores[-1].start()
     for store in stores:
         store.wait()
 
 
-def attend_kernel(
-    block_rows, group, lengths_ref, packed_ref, before_ref, after_ref, out_ref, mixed_ref, sems
-):
-    del before_ref, after_ref
+def attend_kernel(block_rows, group, index_ref, lengths_ref, *refs):
+    out_ref, packed_ref, mixed_ref, load_sems, sems = refs[-5:]
+    loads = [
+        pltpu.make_async_copy(
+            ref, packed_ref.at[lax.bitwise_xor(index_ref[0], number)], load_sems.at[number]
+        )
+        for number, ref in enumerate(refs[:-5])
+    ]
+    for load in loads:
+        load.start()
+    for load in loads:
+        load.wait()
     sources, _, per_device, tokens, width = packed_ref.shape
     capacity = sources * tokens
     per_block = block_rows // tokens
@@ -271,9 +279,7 @@
     total = parts_ref[0].astype(jnp.float32)
     for part in range(1, parts_ref.shape[0]):
         total = total + parts_ref[part].astype(jnp.float32)
-    if factor is not None:
-        total = total * factor
-    total = total.astype(jnp.bfloat16)
+    total = (total * factor).astype(jnp.bfloat16)
     for part in range(out_ref.shape[0]):
         out_ref[part] = total
 
@@ -287,22 +293,8 @@
             out_ref[start : start + kept, :] = parts_ref[part, :kept, :].astype(jnp.float32)
 
 
-def swap(parts, axes, groups=None):
-    return lax.all_to_all(
-        parts, axes, split_axis=0, concat_axis=0, axis_index_groups=groups, tiled=True
-    )
-
-
-def planes_and_columns(outer, seq_count):
-    inner = 1
-    while seq_count % (2 * inner) == 0 and (2 * inner) ** 2 <= seq_count:
-        inner *= 2
-    planes = [
-        [o * seq_count + start + i for o in range(outer) for i in range(inner)]
-        for start in range(0, seq_count, inner)
-    ]
-    columns = [list(column) for column in zip(*planes)]
-    return planes, columns
+def swap(parts, axes):
+    return lax.all_to_all(parts, axes, split_axis=0, concat_axis=0, tiled=True)
 
 
 def body(query_rows, key_rows, value_rows, region_lengths, norm_gain, conv_weight, cotangent):
@@ -310,7 +302,7 @@
     width = model_width // HEADS
     seq_count = lax.axis_size("seq")
     seq_index = lax.axis_index("seq")
-    planes, lines = planes_and_columns(lax.axis_size("dp"), seq_count)
+    everyone = lax.axis_size("dp") * seq_count
     columns = tokens * PATCH
     capacity = seq_count * tokens
     per_device = regions * HEADS // seq_count
@@ -319,26 +311,27 @@
     local_bytes = 2 * query_rows.size
 
     edge_shape = jax.ShapeDtypeStruct((regions, columns, width), jnp.bfloat16)
-    packed, cot_first, cot_last = call(
+    chunk_shape = jax.ShapeDtypeStruct((3, per_device, tokens, width), jnp.bfloat16)
+    index = seq_index.reshape(1)
+    *packed, cot_first, cot_last = call(
         functools.partial(pack_kernel, regions, HEADS, per_device),
         "pack",
-        [
-            jax.ShapeDtypeStruct((seq_count, 3, per_device, tokens, width), jnp.bfloat16),
-            edge_shape,
-            edge_shape,
-        ],
-        [HBM()] * 4,
-        out_specs=[HBM()] * 3,
+        [chunk_shape] * seq_count + [edge_shape] * 2,
+        [SMEM()] + [HBM()] * 4,
+        out_specs=[HBM()] * (seq_count + 2),
         scratch=[
             pltpu.VMEM((3,) + query_rows.shape, jnp.bfloat16),
-            pltpu.VMEM((seq_count, 3, per_device, tokens, width), jnp.bfloat16),
+            pltpu.VMEM((seq_count,) + chunk_shape.shape, jnp.bfloat16),
             pltpu.VMEM((2,) + edge_shape.shape, jnp.bfloat16),
-            pltpu.SemaphoreType.DMA((10,)),
+            pltpu.SemaphoreType.DMA((7 + 3 * seq_count,)),
         ],
         moved=6 * local_bytes,
         grant=VMEM_WHOLE,
-    )(query_rows, key_rows, value_rows, cotangent)
-    packed = swap(packed, "seq")
+    )(index, query_rows, key_rows, value_rows, cotangent)
+    half = seq_count // 2
+    for distance in list(range(half, seq_count)) + list(range(1, half)):
+        pairs = [(i, i ^ distance) for i in range(seq_count)]
+        packed[distance] = lax.ppermute(packed[distance], "seq", pairs)
     cot_before = lax.ppermute(cot_last, "seq", up)
     cot_after = lax.ppermute(cot_first, "seq", down)
 
@@ -357,19 +350,21 @@
         functools.partial(attend_kernel, block_rows, group),
         "attend",
         jax.ShapeDtypeStruct((seq_count, per_device, tokens, width), jnp.bfloat16),
-        [SMEM(), VMEM(), ANY(), ANY()],
+        [SMEM(), SMEM()] + [ANY()] * seq_count,
         out_specs=HBM(),
         scratch=[
+            pltpu.VMEM((seq_count,) + chunk_shape.shape, jnp.bfloat16),
             pltpu.VMEM((seq_count, per_device, tokens, width), jnp.bfloat16),
+            pltpu.SemaphoreType.DMA((seq_count,)),
             pltpu.SemaphoreType.DMA((per_device * -(-capacity // block_rows),)),
         ],
         flops=4 * per_device * capacity * capacity * width,
         moved=4 * local_bytes,
         exps=per_device * capacity * capacity,
-    )(item_lengths, packed, cot_before, cot_after)
+    )(index, item_lengths, *packed)
     attended = swap(mixed, "seq").reshape(HEADS, regions, tokens, width)
 
-    chunk_rows = -(-9 * width // len(lines))
+    chunk_rows = -(-9 * width // everyone)
     pixel_rows = regions * PATCH * columns
     conv_flops = 18 * pixel_rows * width * width
     image, first, last, grad_parts = call(
@@ -379,14 +374,14 @@
             jax.ShapeDtypeStruct((regions, PATCH, columns, width), jnp.bfloat16),
             edge_shape,
             edge_shape,
-            jax.ShapeDtypeStruct((len(lines), chunk_rows, width), jnp.bfloat16),
+            jax.ShapeDtypeStruct((everyone, chunk_rows, width), jnp.bfloat16),
         ],
         [SMEM(), SMEM()] + [VMEM()] * 5,
         scratch=[
             pltpu.VMEM((regions, PATCH, columns + 2 * RIM, width), jnp.float32),
             pltpu.VMEM((pixel_rows, 3 * width), jnp.bfloat16),
             pltpu.VMEM((pixel_rows, 3 * width), jnp.bfloat16),
-            pltpu.VMEM((len(lines) * chunk_rows, width), jnp.float32),
+            pltpu.VMEM((everyone * chunk_rows, width), jnp.float32),
         ],
         flops=conv_flops,
         moved=4 * local_bytes,
@@ -399,25 +394,17 @@
         cot_before,
         cot_after,
     )
-    grad_parts = swap(grad_parts, ("dp", "seq"), planes)
+    grad_parts = swap(grad_parts, ("dp", "seq"))
     before = lax.ppermute(last, "seq", up)
     after = lax.ppermute(first, "seq", down)
-    plane_sums = call(
-        functools.partial(sum_kernel, None),
-        "sum_plane",
-        jax.ShapeDtypeStruct((len(planes), chunk_rows, width), jnp.bfloat16),
-        [VMEM()],
-        moved=4 * grad_parts.size,
-    )(grad_parts)
-    plane_sums = swap(plane_sums, ("dp", "seq"), lines)
     sums = call(
         functools.partial(sum_kernel, 1.0 / math.sqrt(PATCH * columns)),
-        "sum_planes",
+        "sum_parts",
         jax.ShapeDtypeStruct(grad_parts.shape, jnp.bfloat16),
         [VMEM(), ANY(), ANY()],
         moved=4 * grad_parts.size,
-    )(plane_sums, before, after)
-    sums = swap(sums, ("dp", "seq"), planes)
+    )(grad_parts, before, after)
+    sums = swap(sums, ("dp", "seq"))
     decoded = call(
         decode_kernel,
         "decode",

time: 114 us -> 111 us (0.974)
  starting transfers between devices: 27.9 us -> 44.8 us
  waiting for transfers between devices: 58.9 us -> 47.5 us
  blocking collectives: 11.2 us -> 0 us
  Pallas kernels: 14.2 us -> 16.9 us
    all_to_all x4 -> x3, waiting for transfers between devices: 39.7 us -> 12.8 us  [swap(): return lax.all_to_all(parts, axes, split_axis=0, concat_axis=0, tiled=True)]
    ppermute x0 -> x7, waiting for transfers between devices: none -> 22.5 us  [body(): packed[distance] = lax.ppermute(packed[distance], 'seq', pairs)]
    ppermute x0 -> x7, starting transfers between devices: none -> 13.3 us  [body(): packed[distance] = lax.ppermute(packed[distance], 'seq', pairs)]
    all_to_all x1 -> x0, blocking collectives: 11.2 us -> none  [swap(): lax.all_to_all(parts, axes, split_axis=0, concat_axis=0, axis_index_group...]
    ppermute x1, waiting for transfers between devices: 12.6 us -> 3.66 us  [body(): cot_before = lax.ppermute(cot_last, 'seq', up)]
    ppermute x1, waiting for transfers between devices: 0.01 us -> 2.67 us  [body(): cot_after = lax.ppermute(cot_first, 'seq', down)]
    pallas_call x1, Pallas kernels: 2.82 us -> 5.3 us  [body(): call(functools.partial(attend_kernel, block_rows, group), 'attend', jax.S...]
    ppermute x1, starting transfers between devices: 2.56 us -> 4.55 us  [body(): before = lax.ppermute(last, 'seq', up)]
  transfers between devices with their start and end apart: 8 -> 14, of which waited for: 6 -> 10; matrix products, arithmetic and copies ran while one was open for 0% -> 0% of each run, Pallas kernels for 2% -> 2%
where the time goes in v4:
time: 111 us
  waiting for transfers between devices  47.5 us (43%)
  starting transfers between devices  44.8 us (40%)
  Pallas kernels  16.9 us (15%)
    ppermute x7, waiting for transfers between devices, body(): packed[distance] = lax.ppermute(packed[distance], 'seq', pairs)  22.5 us
    all_to_all x3, starting transfers between devices, swap(): return lax.all_to_all(parts, axes, split_axis=0, concat_axis=0, tiled=True)  20.3 us
    ppermute x7, starting transfers between devices, body(): packed[distance] = lax.ppermute(packed[distance], 'seq', pairs)  13.3 us
    all_to_all x3, waiting for transfers between devices, swap(): return lax.all_to_all(parts, axes, split_axis=0, concat_axis=0, tiled=True)  12.8 us
    pallas_call x1, Pallas kernels, body(): call(functools.partial(attend_kernel, block_rows, group), 'attend', jax.S...  5.3 us
    ppermute x1, starting transfers between devices, body(): before = lax.ppermute(last, 'seq', up)  4.55 us
    pallas_call x1, Pallas kernels, body(): call(functools.partial(pack_kernel, regions, HEADS, per_device), 'pack',...  4.07 us
    ppermute x1, starting transfers between devices, body(): cot_before = lax.ppermute(cot_last, 'seq', up)  4.05 us
  transfers between devices with their start and end apart: 14, of which 10 were waited for; matrix products, arithmetic and copies ran while one was open for 0% of the time, Pallas kernels for 2%

profile of v4, /device:TPU:0, one launch (start us, length us, event | category | flops | bytes accessed | tf_op | source)
XLA Modules:
  0.0 111.0 jit_solution(12818867022092373262)
XLA Ops:
  0.6 4.1 %pack.1 = (bf16[3,4,64,128]{3,2,1,0:T(8,128)(2,1)}, bf16[3,4,64,128]{3,2,1,0:T(8,128)(2,1)}, bf16[3,4,64,128]{3,2,1,0:T(8,128)(2,1)}, bf16[3,4,64,128]{3,2,1,0:T...) custom-call(s32[1]{0:T(128)} %bitcast.1.index_ref, ...), custom_call_target="tpu_custom_call" | custom-call | bytes 3145728 | tf_op jit(solution)/shard_map/pack/pallas_call | solution.py:316
  4.7 3.0 %collective-permute-start = (bf16[3,4,64,128]{3,2,1,0:T(8,128)(2,1)}, bf16[3,4,64,128]{3,2,1,0:T(8,128)(2,1)S(1)}, u32[]{:S(2)}, u32[]{:S(2)}) collective-permute-start(bf16[3,4,64,128]{3,2,1,0:T(8,128)(2,1)} %get-tuple-element.17), channel_id=1, source_target_pairs={{0,1},{1,0},{2,3},{3,2},{4,5},{5,4},{6,7},{7,6},{8,9},{9,8},{10,11... | collective-permute-start | bytes 589832 | tf_op jit(solution)/shard_map/ppermute | solution.py:334
  7.7 1.6 %collective-permute-start.1 = (bf16[3,4,64,128]{3,2,1,0:T(8,128)(2,1)}, bf16[3,4,64,128]{3,2,1,0:T(8,128)(2,1)S(1)}, u32[]{:S(2)}, u32[]{:S(2)}) collective-permute-start(bf16[3,4,64,128]{3,2,1,0:T(8,128)(2,1)} %get-tuple-element.18), channel_id=1, source_target_pairs={{0,2},{1,3},{2,0},{3,1},{4,6},{5,7},{6,4},{7,5},{8,10},{9,11},{10,... | collective-permute-start | bytes 589832 | tf_op jit(solution)/shard_map/ppermute | solution.py:334
  9.3 0.0 collective-permute-start.2
  9.3 3.0 %collective-permute-start.3 = (bf16[3,4,64,128]{3,2,1,0:T(8,128)(2,1)}, bf16[3,4,64,128]{3,2,1,0:T(8,128)(2,1)S(1)}, u32[]{:S(2)}, u32[]{:S(2)}) collective-permute-start(bf16[3,4,64,128]{3,2,1,0:T(8,128)(2,1)} %get-tuple-element.20), channel_id=1, source_target_pairs={{0,4},{1,5},{2,6},{3,7},{4,0},{5,1},{6,2},{7,3},{8,12},{9,13},{10,... | collective-permute-start | bytes 589832 | tf_op jit(solution)/shard_map/ppermute | solution.py:334
  12.3 1.3 %collective-permute-start.4 = (bf16[3,4,64,128]{3,2,1,0:T(8,128)(2,1)}, bf16[3,4,64,128]{3,2,1,0:T(8,128)(2,1)S(1)}, u32[]{:S(2)}, u32[]{:S(2)}) collective-permute-start(bf16[3,4,64,128]{3,2,1,0:T(8,128)(2,1)} %get-tuple-element.21), channel_id=1, source_target_pairs={{0,5},{1,4},{2,7},{3,6},{4,1},{5,0},{6,3},{7,2},{8,13},{9,12},{10,... | collective-permute-start | bytes 589832 | tf_op jit(solution)/shard_map/ppermute | solution.py:334
  13.6 0.0 collective-permute-done.refs_1_
  13.6 3.6 %collective-permute-start.5 = (bf16[3,4,64,128]{3,2,1,0:T(8,128)(2,1)}, bf16[3,4,64,128]{3,2,1,0:T(8,128)(2,1)S(1)}, u32[]{:S(2)}, u32[]{:S(2)}) collective-permute-start(bf16[3,4,64,128]{3,2,1,0:T(8,128)(2,1)} %get-tuple-element.22), channel_id=1, source_target_pairs={{0,6},{1,7},{2,4},{3,5},{4,2},{5,3},{6,0},{7,1},{8,14},{9,15},{10,... | collective-permute-start | bytes 589832 | tf_op jit(solution)/shard_map/ppermute | solution.py:334
  17.2 6.2 %collective-permute-done.1.refs_2_ = bf16[3,4,64,128]{3,2,1,0:T(8,128)(2,1)S(1)} collective-permute-done((bf16[3,4,64,128]{3,2,1,0:T(8,128)(2,1)}, bf16[3,4,64,128]{3,2,1,0:T(8,128)(2,1)S(1)}, u32[]{:S(2)}, u32[]{:S(2)}) %collective-permute-start.1) | collective-permute-done | bytes 196640 | tf_op jit(solution)/shard_map/ppermute | solution.py:334
  23.4 0.0 copy-start.4
  23.4 0.9 collective-permute-start.6
  24.3 0.0 copy-done.4
  24.3 0.1 fusion.lengths_ref
  24.4 0.7 collective-permute-done.2.refs_3_
  25.1 0.0 collective-permute-done.3.refs_4_
  25.1 15.5 %collective-permute-done.4.refs_5_ = bf16[3,4,64,128]{3,2,1,0:T(8,128)(2,1)S(1)} collective-permute-done((bf16[3,4,64,128]{3,2,1,0:T(8,128)(2,1)}, bf16[3,4,64,128]{3,2,1,0:T(8,128)(2,1)S(1)}, u32[]{:S(2)}, u32[]{:S(2)}) %collective-permute-start.4) | collective-permute-done | bytes 196640 | tf_op jit(solution)/shard_map/ppermute | solution.py:334
  40.6 0.0 collective-permute-done.5.refs_6_
  40.6 0.0 collective-permute-done.6.refs_7_
  40.6 0.0 copy-start.1
  40.7 0.9 copy-done.1
  41.6 5.3 %attend.1 = bf16[8,4,64,128]{3,2,1,0:T(8,128)(2,1)} custom-call(s32[1]{0:T(128)} %bitcast.1.index_ref, s32[4]{0:T(128)S(1)} %fusion.lengths_ref, bf16[3,4,64,128]{3,2,1,0:T(8,128)(2,1)S(1)} %copy-done.1, bf16[3,4,64,128]{3,2,1,0:T(8,128)(2,1)S(1)} %collective-permute-done.refs_1_, bf16[3,4,64,128]{3,2,1,0:T(8,128)(2,1)S(1)} %collective-permute-done.1.refs_2_, ...), custom_call_target="tpu_custom_call" | custom-call | flops 536870912 | bytes 2097152 | tf_op jit(solution)/shard_map/attend/pallas_call | solution.py:349
  46.9 0.0 copy-start.6
  46.9 0.0 copy-start.5
  46.9 0.0 copy-start
  46.9 10.6 %all-to-all-start = ((bf16[8,4,64,128]{3,2,1,0:T(8,128)(2,1)}), bf16[8,4,64,128]{3,2,1,0:T(8,128)(2,1)S(1)}, u32[]{:S(2)}, u32[]{:S(2)}) async-start(bf16[8,4,64,128]{3,2,1,0:T(8,128)(2,1)} %attend.1), calls=%async_computation | async-start | bytes 1048576 | tf_op jit(solution)/shard_map/all_to_all | solution.py:297
  57.5 0.0 copy-start.3
  57.5 0.0 copy-done.6
  57.5 4.0 %collective-permute-start.7 = (bf16[2,256,128]{2,1,0:T(8,128)(2,1)S(1)}, bf16[2,256,128]{2,1,0:T(8,128)(2,1)S(1)}, u32[]{:S(2)}, u32[]{:S(2)}) collective-permute-start(bf16[2,256,128]{2,1,0:T(8,128)(2,1)S(1)} %copy-done.6), channel_id=1, source_target_pairs={{0,1},{1,2},{2,3},{3,4},{4,5},{5,6},{6,7},{8,9},{9,10},{10,11},{11... | collective-permute-start | bytes 393224 | tf_op jit(solution)/shard_map/ppermute | solution.py:335
  61.6 0.0 copy-done.5
  61.6 1.3 %collective-permute-start.8 = (bf16[2,256,128]{2,1,0:T(8,128)(2,1)S(1)}, bf16[2,256,128]{2,1,0:T(8,128)(2,1)S(1)}, u32[]{:S(2)}, u32[]{:S(2)}) collective-permute-start(bf16[2,256,128]{2,1,0:T(8,128)(2,1)S(1)} %copy-done.5), channel_id=1, source_target_pairs={{1,0},{2,1},{3,2},{4,3},{5,4},{6,5},{7,6},{9,8},{10,9},{11,10},{12... | collective-permute-start | bytes 393224 | tf_op jit(solution)/shard_map/ppermute | solution.py:336
  62.9 3.7 %collective-permute-done.7.cot_before_ref = bf16[2,256,128]{2,1,0:T(8,128)(2,1)S(1)} collective-permute-done((bf16[2,256,128]{2,1,0:T(8,128)(2,1)S(1)}, bf16[2,256,128]{2,1,0:T(8,128)(2,1)S(1)}, u32[]{:S(2)}, u32[]{:S(2)}) %collective-permute-start.7) | collective-permute-done | bytes 131104 | tf_op jit(solution)/shard_map/ppermute | solution.py:335
  66.5 2.7 %collective-permute-done.8.cot_after_ref = bf16[2,256,128]{2,1,0:T(8,128)(2,1)S(1)} collective-permute-done((bf16[2,256,128]{2,1,0:T(8,128)(2,1)S(1)}, bf16[2,256,128]{2,1,0:T(8,128)(2,1)S(1)}, u32[]{:S(2)}, u32[]{:S(2)}) %collective-permute-start.8) | collective-permute-done | bytes 131104 | tf_op jit(solution)/shard_map/ppermute | solution.py:336
  69.2 2.5 %all-to-all-done = bf16[8,4,64,128]{3,2,1,0:T(8,128)(2,1)S(1)} async-done(((bf16[8,4,64,128]{3,2,1,0:T(8,128)(2,1)}), bf16[8,4,64,128]{3,2,1,0:T(8,128)(2,1)S(1)}, u32[]{:S(2)}, u32[]{:S(2)}) %all-to-all-start) | async-done | bytes 524320 | tf_op jit(solution)/shard_map/all_to_all | solution.py:297
  71.7 0.0 copy-done
  71.7 0.0 copy-done.3
  71.7 3.6 %norm_and_gradient.1 = (bf16[2,4,256,128]{3,2,1,0:T(8,128)(2,1)S(1)}, bf16[2,256,128]{2,1,0:T(8,128)(2,1)S(1)}, bf16[2,256,128]{2,1,0:T(8,128)(2,1)S(1)}, bf16[32,36,128]{2,1,0:T(8,128)(2,1)}) custom-call(s32[2]{0:T(128)S(1)} %copy-done.4, s32[1]{0:T(128)} %bitcast.base_ref, bf16[16,2,64,128]{3,2,1,0:T(8,128)(2,1)S(1)} %bitcast.6, f32[16,128]{1,0:T(8,128)S(1)} %bitcast.8, ...), custom_call_target="tpu_custom_call" | custom-call | flops 603979776 | bytes 2097152 | tf_op jit(solution)/shard_map/norm_and_gradient/pallas_call | solution.py:370
  75.4 4.2 %all-to-all-start.1 = ((bf16[32,36,128]{2,1,0:T(8,128)(2,1)}), bf16[32,36,128]{2,1,0:T(8,128)(2,1)S(1)}, u32[]{:S(2)}, u32[]{:S(2)}) async-start(bf16[32,36,128]{2,1,0:T(8,128)(2,1)} %get-tuple-element.29), calls=%async_computation.1 | async-start | bytes 655360 | tf_op jit(solution)/shard_map/all_to_all | solution.py:297
  79.6 1.3 %collective-permute-start.10 = (bf16[2,256,128]{2,1,0:T(8,128)(2,1)S(1)}, bf16[2,256,128]{2,1,0:T(8,128)(2,1)S(1)}, u32[]{:S(2)}, u32[]{:S(2)}) collective-permute-start(bf16[2,256,128]{2,1,0:T(8,128)(2,1)S(1)} %get-tuple-element.28), channel_id=1, source_target_pairs={{1,0},{2,1},{3,2},{4,3},{5,4},{6,5},{7,6},{9,8},{10,9},{11,10},{12... | collective-permute-start | bytes 393224 | tf_op jit(solution)/shard_map/ppermute | solution.py:399
  80.9 4.6 %collective-permute-start.9 = (bf16[2,256,128]{2,1,0:T(8,128)(2,1)S(1)}, bf16[2,256,128]{2,1,0:T(8,128)(2,1)S(1)}, u32[]{:S(2)}, u32[]{:S(2)}) collective-permute-start(bf16[2,256,128]{2,1,0:T(8,128)(2,1)S(1)} %get-tuple-element.27), channel_id=1, source_target_pairs={{0,1},{1,2},{2,3},{3,4},{4,5},{5,6},{6,7},{8,9},{9,10},{10,11},{11... | collective-permute-start | bytes 393224 | tf_op jit(solution)/shard_map/ppermute | solution.py:398
  85.4 3.7 %collective-permute-done.10.after_ref.refs_1_ = bf16[2,256,128]{2,1,0:T(8,128)(2,1)S(1)} collective-permute-done((bf16[2,256,128]{2,1,0:T(8,128)(2,1)S(1)}, bf16[2,256,128]{2,1,0:T(8,128)(2,1)S(1)}, u32[]{:S(2)}, u32[]{:S(2)}) %collective-permute-start.10) | collective-permute-done | bytes 131104 | tf_op jit(solution)/shard_map/ppermute | solution.py:399
  89.1 2.2 %collective-permute-done.9.before_ref.refs_0_ = bf16[2,256,128]{2,1,0:T(8,128)(2,1)S(1)} collective-permute-done((bf16[2,256,128]{2,1,0:T(8,128)(2,1)S(1)}, bf16[2,256,128]{2,1,0:T(8,128)(2,1)S(1)}, u32[]{:S(2)}, u32[]{:S(2)}) %collective-permute-start.9) | collective-permute-done | bytes 131104 | tf_op jit(solution)/shard_map/ppermute | solution.py:398
  91.4 0.3 all-to-all-done.1.parts_ref
  91.7 0.8 sum_parts.1
  92.5 0.0 copy-start.2
  92.5 5.5 %all-to-all-start.2 = ((bf16[32,36,128]{2,1,0:T(8,128)(2,1)}), bf16[32,36,128]{2,1,0:T(8,128)(2,1)S(1)}, u32[]{:S(2)}, u32[]{:S(2)}) async-start(bf16[32,36,128]{2,1,0:T(8,128)(2,1)} %sum_parts.1), calls=%async_computation.2 | async-start | bytes 655360 | tf_op jit(solution)/shard_map/all_to_all | solution.py:297
  98.0 0.0 copy-done.2
  98.1 2.2 %decode.1 = bf16[2,4,256,128]{3,2,1,0:T(8,128)(2,1)} custom-call(bf16[2,4,256,128]{3,2,1,0:T(8,128)(2,1)S(1)} %get-tuple-element.26.image_ref, bf16[2,256,128]{2,1,0:T(8,128)(2,1)S(1)} %collective-permute-done.9.before_ref.refs_0_, bf16[2,256,128]{2,1,0:T(8,128)(2,1)S(1)} %collective-permute-done.10.after_ref.refs_1_, bf16[3,384,128]{2,1,0:T(8,128)(2,1)S(1)} %bitcast.7), custom_call_target="tpu_custom_call" | custom-call | flops 603979776 | bytes 1048576 | tf_op jit(solution)/shard_map/decode/pallas_call | solution.py:408
  100.3 9.9 %all-to-all-done.2.parts_ref = bf16[32,36,128]{2,1,0:T(8,128)(2,1)S(1)} async-done(((bf16[32,36,128]{2,1,0:T(8,128)(2,1)}), bf16[32,36,128]{2,1,0:T(8,128)(2,1)S(1)}, u32[]{:S(2)}, u32[]{:S(2)}) %all-to-all-start.2) | async-done | bytes 294944 | tf_op jit(solution)/shard_map/all_to_all | solution.py:297
  110.2 0.9 spread_sums.1
  (1 shorter events, 0.0 us)
Async XLA Ops:
  4.7 8.9 %collective-permute-start = (bf16[3,4,64,128]{3,2,1,0:T(8,128)(2,1)}, bf16[3,4,64,128]{3,2,1,0:T(8,128)(2,1)S(1)}, u32[]{:S(2)}, u32[]{:S(2)}) collective-permute-start(bf16[3,4,64,128]{3,2,1,0:T(8,128)(2,1)} %get-tuple-element.17), channel_id=1, source_target_pairs={{0,1},{1,0},{2,3},{3,2},{4,5},{5,4},{6,7},{7,6},{8,9},{9,8},{10,11... | collective-permute-start | bytes 589832 | tf_op jit(solution)/shard_map/ppermute | solution.py:334
  7.7 15.7 %collective-permute-start.1 = (bf16[3,4,64,128]{3,2,1,0:T(8,128)(2,1)}, bf16[3,4,64,128]{3,2,1,0:T(8,128)(2,1)S(1)}, u32[]{:S(2)}, u32[]{:S(2)}) collective-permute-start(bf16[3,4,64,128]{3,2,1,0:T(8,128)(2,1)} %get-tuple-element.18), channel_id=1, source_target_pairs={{0,2},{1,3},{2,0},{3,1},{4,6},{5,7},{6,4},{7,5},{8,10},{9,11},{10,... | collective-permute-start | bytes 589832 | tf_op jit(solution)/shard_map/ppermute | solution.py:334
  9.3 15.8 %collective-permute-start.2 = (bf16[3,4,64,128]{3,2,1,0:T(8,128)(2,1)}, bf16[3,4,64,128]{3,2,1,0:T(8,128)(2,1)S(1)}, u32[]{:S(2)}, u32[]{:S(2)}) collective-permute-start(bf16[3,4,64,128]{3,2,1,0:T(8,128)(2,1)} %get-tuple-element.19), channel_id=1, source_target_pairs={{0,3},{1,2},{2,1},{3,0},{4,7},{5,6},{6,5},{7,4},{8,11},{9,10},{10,... | collective-permute-start | bytes 589832 | tf_op jit(solution)/shard_map/ppermute | solution.py:334
  9.3 15.8 %collective-permute-start.3 = (bf16[3,4,64,128]{3,2,1,0:T(8,128)(2,1)}, bf16[3,4,64,128]{3,2,1,0:T(8,128)(2,1)S(1)}, u32[]{:S(2)}, u32[]{:S(2)}) collective-permute-start(bf16[3,4,64,128]{3,2,1,0:T(8,128)(2,1)} %get-tuple-element.20), channel_id=1, source_target_pairs={{0,4},{1,5},{2,6},{3,7},{4,0},{5,1},{6,2},{7,3},{8,12},{9,13},{10,... | collective-permute-start | bytes 589832 | tf_op jit(solution)/shard_map/ppermute | solution.py:334
  12.3 28.3 %collective-permute-start.4 = (bf16[3,4,64,128]{3,2,1,0:T(8,128)(2,1)}, bf16[3,4,64,128]{3,2,1,0:T(8,128)(2,1)S(1)}, u32[]{:S(2)}, u32[]{:S(2)}) collective-permute-start(bf16[3,4,64,128]{3,2,1,0:T(8,128)(2,1)} %get-tuple-element.21), channel_id=1, source_target_pairs={{0,5},{1,4},{2,7},{3,6},{4,1},{5,0},{6,3},{7,2},{8,13},{9,12},{10,... | collective-permute-start | bytes 589832 | tf_op jit(solution)/shard_map/ppermute | solution.py:334
  13.6 27.1 %collective-permute-start.5 = (bf16[3,4,64,128]{3,2,1,0:T(8,128)(2,1)}, bf16[3,4,64,128]{3,2,1,0:T(8,128)(2,1)S(1)}, u32[]{:S(2)}, u32[]{:S(2)}) collective-permute-start(bf16[3,4,64,128]{3,2,1,0:T(8,128)(2,1)} %get-tuple-element.22), channel_id=1, source_target_pairs={{0,6},{1,7},{2,4},{3,5},{4,2},{5,3},{6,0},{7,1},{8,14},{9,15},{10,... | collective-permute-start | bytes 589832 | tf_op jit(solution)/shard_map/ppermute | solution.py:334
  23.4 0.9 copy-start.4
  23.4 17.2 %collective-permute-start.6 = (bf16[3,4,64,128]{3,2,1,0:T(8,128)(2,1)}, bf16[3,4,64,128]{3,2,1,0:T(8,128)(2,1)S(1)}, u32[]{:S(2)}, u32[]{:S(2)}) collective-permute-start(bf16[3,4,64,128]{3,2,1,0:T(8,128)(2,1)} %get-tuple-element.23), channel_id=1, source_target_pairs={{0,7},{1,6},{2,5},{3,4},{4,3},{5,2},{6,1},{7,0},{8,15},{9,14},{10,... | collective-permute-start | bytes 589832 | tf_op jit(solution)/shard_map/ppermute | solution.py:334
  40.6 0.9 copy-start.1
  46.9 10.6 %copy-start.6 = (bf16[2,256,128]{2,1,0:T(8,128)(2,1)S(1)}, bf16[2,256,128]{2,1,0:T(8,128)(2,1)}, u32[]{:S(2)}) copy-start(bf16[2,256,128]{2,1,0:T(8,128)(2,1)} %get-tuple-element.24) | copy-start | bytes 393220
  46.9 14.7 %copy-start.5 = (bf16[2,256,128]{2,1,0:T(8,128)(2,1)S(1)}, bf16[2,256,128]{2,1,0:T(8,128)(2,1)}, u32[]{:S(2)}) copy-start(bf16[2,256,128]{2,1,0:T(8,128)(2,1)} %get-tuple-element.25) | copy-start | bytes 393220
  46.9 24.8 %copy-start = (bf16[2,4,256,128]{3,2,1,0:T(8,128)(2,1)S(1)}, bf16[2,4,256,128]{3,2,1,0:T(8,128)(2,1)}, u32[]{:S(2)}) copy-start(bf16[2,4,256,128]{3,2,1,0:T(8,128)(2,1)} %cot_ref.3) | copy-start | bytes 1572868
  46.9 24.8 %all-to-all-start = ((bf16[8,4,64,128]{3,2,1,0:T(8,128)(2,1)}), bf16[8,4,64,128]{3,2,1,0:T(8,128)(2,1)S(1)}, u32[]{:S(2)}, u32[]{:S(2)}) async-start(bf16[8,4,64,128]{3,2,1,0:T(8,128)(2,1)} %attend.1), calls=%async_computation | async-start | bytes 1048576 | tf_op jit(solution)/shard_map/all_to_all | solution.py:297
  57.5 14.2 %copy-start.3 = (f32[2048]{0:T(1024)S(1)}, f32[2048]{0:T(1024)}, u32[]{:S(2)}) copy-start(f32[2048]{0:T(1024)} %param.11) | copy-start | bytes 24580
  57.5 9.0 %collective-permute-start.7 = (bf16[2,256,128]{2,1,0:T(8,128)(2,1)S(1)}, bf16[2,256,128]{2,1,0:T(8,128)(2,1)S(1)}, u32[]{:S(2)}, u32[]{:S(2)}) collective-permute-start(bf16[2,256,128]{2,1,0:T(8,128)(2,1)S(1)} %copy-done.6), channel_id=1, source_target_pairs={{0,1},{1,2},{2,3},{3,4},{4,5},{5,6},{6,7},{8,9},{9,10},{10,11},{11... | collective-permute-start | bytes 393224 | tf_op jit(solution)/shard_map/ppermute | solution.py:335
  61.6 7.6 %collective-permute-start.8 = (bf16[2,256,128]{2,1,0:T(8,128)(2,1)S(1)}, bf16[2,256,128]{2,1,0:T(8,128)(2,1)S(1)}, u32[]{:S(2)}, u32[]{:S(2)}) collective-permute-start(bf16[2,256,128]{2,1,0:T(8,128)(2,1)S(1)} %copy-done.5), channel_id=1, source_target_pairs={{1,0},{2,1},{3,2},{4,3},{5,4},{6,5},{7,6},{9,8},{10,9},{11,10},{12... | collective-permute-start | bytes 393224 | tf_op jit(solution)/shard_map/ppermute | solution.py:336
  75.4 16.4 %all-to-all-start.1 = ((bf16[32,36,128]{2,1,0:T(8,128)(2,1)}), bf16[32,36,128]{2,1,0:T(8,128)(2,1)S(1)}, u32[]{:S(2)}, u32[]{:S(2)}) async-start(bf16[32,36,128]{2,1,0:T(8,128)(2,1)} %get-tuple-element.29), calls=%async_computation.1 | async-start | bytes 655360 | tf_op jit(solution)/shard_map/all_to_all | solution.py:297
  79.6 9.6 %collective-permute-start.10 = (bf16[2,256,128]{2,1,0:T(8,128)(2,1)S(1)}, bf16[2,256,128]{2,1,0:T(8,128)(2,1)S(1)}, u32[]{:S(2)}, u32[]{:S(2)}) collective-permute-start(bf16[2,256,128]{2,1,0:T(8,128)(2,1)S(1)} %get-tuple-element.28), channel_id=1, source_target_pairs={{1,0},{2,1},{3,2},{4,3},{5,4},{6,5},{7,6},{9,8},{10,9},{11,10},{12... | collective-permute-start | bytes 393224 | tf_op jit(solution)/shard_map/ppermute | solution.py:399
  80.9 10.5 %collective-permute-start.9 = (bf16[2,256,128]{2,1,0:T(8,128)(2,1)S(1)}, bf16[2,256,128]{2,1,0:T(8,128)(2,1)S(1)}, u32[]{:S(2)}, u32[]{:S(2)}) collective-permute-start(bf16[2,256,128]{2,1,0:T(8,128)(2,1)S(1)} %get-tuple-element.27), channel_id=1, source_target_pairs={{0,1},{1,2},{2,3},{3,4},{4,5},{5,6},{6,7},{8,9},{9,10},{10,11},{11... | collective-permute-start | bytes 393224 | tf_op jit(solution)/shard_map/ppermute | solution.py:398
  92.5 5.5 %copy-start.2 = (bf16[9,128,128]{2,1,0:T(8,128)(2,1)S(1)}, bf16[9,128,128]{2,1,0:T(8,128)(2,1)}, u32[]{:S(2)}) copy-start(bf16[9,128,128]{2,1,0:T(8,128)(2,1)} %param.12) | copy-start | bytes 884740
  92.5 17.7 %all-to-all-start.2 = ((bf16[32,36,128]{2,1,0:T(8,128)(2,1)}), bf16[32,36,128]{2,1,0:T(8,128)(2,1)S(1)}, u32[]{:S(2)}, u32[]{:S(2)}) async-start(bf16[32,36,128]{2,1,0:T(8,128)(2,1)} %sum_parts.1), calls=%async_computation.2 | async-start | bytes 655360 | tf_op jit(solution)/shard_map/all_to_all | solution.py:297

commit v5 on v4

v5 whole, which is shorter than its diff:
```python
import functools
import math

import jax
import jax.numpy as jnp
from jax import lax
from jax.experimental import pallas as pl
from jax.experimental.pallas import tpu as pltpu
from jax.sharding import PartitionSpec as P

HEADS = 16
PATCH = 4
RIM = 8
VMEM_LIMIT = 48 * 1024 * 1024
VMEM_WHOLE = 60 * 1024 * 1024

VMEM = functools.partial(pl.BlockSpec, memory_space=pltpu.VMEM)
HBM = functools.partial(pl.BlockSpec, memory_space=pltpu.HBM)
ANY = functools.partial(pl.BlockSpec, memory_space=pl.ANY)
SMEM = functools.partial(pl.BlockSpec, memory_space=pltpu.SMEM)


def call(kernel, name, out_shape, in_specs, out_specs=None, scratch=(), flops=0, moved=0, exps=0, grant=VMEM_LIMIT):
    many = isinstance(out_shape, (list, tuple))
    return pl.pallas_call(
        kernel,
        out_shape=out_shape,
        in_specs=in_specs,
        out_specs=out_specs or ([VMEM() for _ in out_shape] if many else VMEM()),
        scratch_shapes=list(scratch),
        compiler_params=pltpu.CompilerParams(vmem_limit_bytes=grant),
        cost_estimate=pl.CostEstimate(flops=flops, bytes_accessed=moved, transcendentals=exps),
        name=name,
    )


def pack_kernel(
    regions,
    heads,
    per_device,
    index_ref,
    query_ref,
    key_ref,
    value_ref,
    cot_ref,
    *refs,
):
    held, ready, edges, sems = refs[-4:]
    edge_refs = refs[-6:-4]
    out_refs = refs[:-6]
    width = held.shape[3] // heads
    rows = cot_ref.shape[1]
    loads = [
        pltpu.make_async_copy(ref, held.at[which], sems.at[which])
        for which, ref in enumerate((query_ref, key_ref, value_ref))
    ]
    odd = lax.rem(index_ref[0], 2)
    for edge, row in enumerate(((1 - odd) * (rows - 1), odd * (rows - 1))):
        loads.append(pltpu.make_async_copy(cot_ref.at[:, row], edges.at[edge], sems.at[3 + edge]))
    for load in loads:
        load.start()
    stores = []
    for which in range(3):
        loads[which].wait()
        for head in range(heads):
            block = held[which, :, :, head * width : (head + 1) * width].astype(jnp.float32)
            for region in range(regions):
                item = head * regions + region
                slot = lax.bitwise_xor(index_ref[0], item // per_device)
                ready[slot, which, item % per_device] = block[:, region, :].astype(jnp.bfloat16)
        for number, ref in enumerate(out_refs):
            stores.append(
                pltpu.make_async_copy(
                    ready.at[number, which], ref.at[which], sems.at[7 + 3 * number + which]
                )
            )
            stores[-1].start()
        if which == 0:
            for edge, ref in enumerate(edge_refs):
                loads[3 + edge].wait()
                stores.append(pltpu.make_async_copy(edges.at[edge], ref, sems.at[5 + edge]))
                stores[-1].start()
    for store in stores:
        store.wait()


def attend_kernel(block_rows, group, order, index_ref, lengths_ref, *refs):
    out_ref, mixed_ref, sems = refs[-3:]
    chunks = dict(zip(order, refs[:-3]))
    index = index_ref[0]
    sources = len(chunks)
    _, per_device, tokens, width = chunks[0].shape
    capacity = sources * tokens
    per_block = block_rows // tokens
    blocks = capacity // block_rows
    factor = math.log2(math.e) / math.sqrt(width)
    columns = lax.broadcasted_iota(jnp.int32, (1, capacity), 1)
    slots = columns
    for distance in range(sources):
        here = (columns >= distance * tokens) & (columns < (distance + 1) * tokens)
        moved = (lax.bitwise_xor(index, distance) - distance) * tokens
        slots = jnp.where(here, columns + moved, slots)

    def rows_of(which, item, distances):
        return jnp.concatenate([chunks[distance][which, item] for distance in distances], axis=0)

    def distances_of(block):
        return range(block * per_block, (block + 1) * per_block)

    def start_of(block, span):
        return lax.bitwise_xor(lax.div(index, span), block) * span

    def clear(item, block):
        for distance in distances_of(block):
            mixed_ref[lax.bitwise_xor(index, distance), item] = jnp.zeros(
                (tokens, width), jnp.bfloat16
            )

    def score(item, block):
        return lax.dot_general(
            rows_of(0, item, distances_of(block)),
            rows_of(1, item, range(sources)),
            (((1,), (1,)), ((), ())),
            preferred_element_type=jnp.float32,
        )

    def finish(item, block, scores, key_valid):
        scores = jnp.where(key_valid, scores * factor, -1e30)
        powers = jnp.exp2(scores - jnp.max(scores, axis=1, keepdims=True))
        totals = jnp.sum(powers, axis=1, keepdims=True)
        mixed = jnp.dot(
            powers.astype(jnp.bfloat16),
            rows_of(2, item, range(sources)),
            preferred_element_type=jnp.float32,
        )
        mixed = (mixed / totals).astype(jnp.bfloat16)
        for number, distance in enumerate(distances_of(block)):
            mixed_ref[lax.bitwise_xor(index, distance), item] = mixed[
                number * tokens : (number + 1) * tokens
            ]

    def attend(items, live, dead, length):
        key_valid = slots < length
        waiting = None
        for block in live:
            for item in items:
                scores = score(item, block)
                if waiting is not None:
                    finish(*waiting, key_valid)
                waiting = (item, block, scores)
        if waiting is not None:
            finish(*waiting, key_valid)
        for block in dead:
            for item in items:
                clear(item, block)

    stores = []
    for lead in range(group):
        length = lengths_ref[lead]
        items = list(range(lead, per_device, group))
        for block in range(0, blocks, 2):
            pair = list(range(block, min(block + 2, blocks)))
            alive = [length > start_of(one, per_block) * tokens for one in pair]
            for case in range(2 ** len(pair)):
                live = [one for bit, one in enumerate(pair) if case >> bit & 1]
                dead = [one for one in pair if one not in live]
                chosen = None
                for bit in range(len(pair)):
                    test = alive[bit] if case >> bit & 1 else jnp.logical_not(alive[bit])
                    chosen = test if chosen is None else chosen & test

                @pl.when(chosen)
                def _(items=items, live=live, dead=dead, length=length):
                    attend(items, live, dead, length)

            span = per_block * len(pair)
            rows = pl.ds(start_of(block // len(pair), span), span)
            for item in items:
                store = pltpu.make_async_copy(
                    mixed_ref.at[rows, item], out_ref.at[rows, item], sems.at[len(stores)]
                )
                store.start()
                stores.append(store)
    for store in stores:
        store.wait()


def three_windows(padded, columns):
    return jnp.concatenate(
        [padded[RIM - 1 + shift : RIM - 1 + shift + columns].astype(jnp.bfloat16) for shift in range(3)],
        axis=1,
    )


def around(odd, near, far):
    return jnp.where(odd == 1, near, far), jnp.where(odd == 1, far, near)


def norm_kernel(
    chunk_rows,
    lengths_ref,
    index_ref,
    attended_ref,
    gain_ref,
    cot_ref,
    cot_near_ref,
    cot_far_ref,
    image_ref,
    near_ref,
    far_ref,
    grad_ref,
    pixels,
    windows,
    cots,
    grads,
):
    heads, regions, tokens, width = attended_ref.shape
    columns = tokens * PATCH
    features = heads * width
    odd = lax.rem(index_ref[0], 2)
    position = index_ref[0] * tokens + lax.broadcasted_iota(jnp.int32, (tokens, 1), 0)
    pixels[:, :, :RIM, :] = jnp.zeros((regions, PATCH, RIM, width), jnp.float32)
    pixels[:, :, RIM + columns :, :] = jnp.zeros((regions, PATCH, RIM, width), jnp.float32)
    for region in range(regions):
        total = jnp.zeros((tokens, width), jnp.float32)
        for head in range(heads):
            total = total + attended_ref[head, region].astype(jnp.float32)
        mean = jnp.sum(total, axis=1, keepdims=True) * (1.0 / features)
        total = jnp.zeros((tokens, width), jnp.float32)
        for head in range(heads):
            centered = attended_ref[head, region].astype(jnp.float32) - mean
            total = total + centered * centered
        variance = jnp.sum(total, axis=1, keepdims=True) * (1.0 / features)
        spread = lax.rsqrt(variance + 1e-05)
        live = position < lengths_ref[region]
        for head in range(heads):
            centered = attended_ref[head, region].astype(jnp.float32) - mean
            normed = jnp.where(live, centered * spread * gain_ref[head : head + 1, :], 0.0)
            row, column = divmod(head, PATCH)
            pixels[region, row, pl.ds(RIM + column, tokens, stride=PATCH), :] = normed
        cot_before, cot_after = around(odd, cot_near_ref[region], cot_far_ref[region])
        for row in range(PATCH):
            window = three_windows(pixels[region, row], columns)
            middle = window[:, width : 2 * width]
            image_ref[region, row] = middle
            start = (region * PATCH + row) * columns
            windows[start : start + columns, :] = window
            below = cot_ref[region, row + 1] if row < PATCH - 1 else cot_after
            above = cot_ref[region, row - 1] if row > 0 else cot_before
            cots[start : start + columns, :] = jnp.concatenate(
                [below, cot_ref[region, row], above], axis=1
            )
        near_ref[region] = image_ref[region, (1 - odd) * (PATCH - 1)]
        far_ref[region] = image_ref[region, odd * (PATCH - 1)]
    product = lax.dot_general(
        windows[...], cots[...], (((0,), (0,)), ((), ())), preferred_element_type=jnp.float32
    )
    for down in range(3):
        for across in range(3):
            tap = 3 * down + across
            grads[tap * width : (tap + 1) * width, :] = product[
                across * width : (across + 1) * width, down * width : (down + 1) * width
            ]
    filled = 9 * width
    if filled < grads.shape[0]:
        grads[filled:, :] = jnp.zeros((grads.shape[0] - filled, width), jnp.float32)
    for chunk in range(grad_ref.shape[0]):
        grad_ref[chunk] = grads[chunk * chunk_rows : (chunk + 1) * chunk_rows, :].astype(jnp.bfloat16)


def decode_kernel(index_ref, image_ref, near_ref, far_ref, weight_ref, out_ref, padded):
    regions, rows, columns, width = image_ref.shape
    padded[:RIM, :] = jnp.zeros((RIM, width), jnp.float32)
    padded[RIM + columns :, :] = jnp.zeros((RIM, width), jnp.float32)
    for region in range(regions):
        strips = []
        before, after = around(lax.rem(index_ref[0], 2), near_ref[region], far_ref[region])
        for row in range(-1, rows + 1):
            if row < 0:
                source = before
            elif row == rows:
                source = after
            else:
                source = image_ref[region, row]
            padded[RIM : RIM + columns, :] = source.astype(jnp.float32)
            strips.append(three_windows(padded[...], columns))
            if len(strips) == 3:
                total = jnp.dot(strips[0], weight_ref[0], preferred_element_type=jnp.float32)
                for down in (1, 2):
                    total = total + jnp.dot(
                        strips[down], weight_ref[down], preferred_element_type=jnp.float32
                    )
                out_ref[region, row - 1] = total.astype(jnp.bfloat16)
                strips.pop(0)


def sum_kernel(count, factor, *refs):
    out_ref = refs[-1]
    if count == 1:
        parts = [refs[0].at[part] for part in range(refs[0].shape[0])]
    else:
        parts = refs[:count]
    totals = [part[...].astype(jnp.float32) for part in parts]
    while len(totals) > 1:
        paired = [one + other for one, other in zip(totals[::2], totals[1::2])]
        totals = paired + totals[2 * len(paired) :]
    total = totals[0]
    if factor is not None:
        total = total * factor
    total = total.astype(jnp.bfloat16)
    if out_ref.ndim == 2:
        out_ref[...] = total
    else:
        for part in range(out_ref.shape[0]):
            out_ref[part] = total


def spread_kernel(parts_ref, out_ref):
    rows = parts_ref.shape[1]
    for part in range(parts_ref.shape[0]):
        start = part * rows
        kept = min(rows, out_ref.shape[0] - start)
        if kept > 0:
            out_ref[start : start + kept, :] = parts_ref[part, :kept, :].astype(jnp.float32)


def swap(parts, axes, groups=None):
    return lax.all_to_all(
        parts, axes, split_axis=0, concat_axis=0, axis_index_groups=groups, tiled=True
    )


def trade(values, distance):
    pairs = [(i, i ^ distance) for i in range(lax.axis_size("seq"))]
    return lax.ppermute(values, "seq", pairs)


def planes_of(outer, seq_count):
    inner = 1
    while seq_count % (2 * inner) == 0 and (2 * inner) ** 2 <= seq_count:
        inner *= 2
    planes = [
        [o * seq_count + start + i for o in range(outer) for i in range(inner)]
        for start in range(0, seq_count, inner)
    ]
    return inner, planes


def body(query_rows, key_rows, value_rows, region_lengths, norm_gain, conv_weight, cotangent):
    tokens, regions, model_width = query_rows.shape
    width = model_width // HEADS
    seq_count = lax.axis_size("seq")
    seq_index = lax.axis_index("seq")
    inner, planes = planes_of(lax.axis_size("dp"), seq_count)
    plane_size = len(planes[0])
    columns = tokens * PATCH
    capacity = seq_count * tokens
    per_device = regions * HEADS // seq_count
    far_pairs = [(i, i + 1) for i in range(1, seq_count - 1, 2)]
    far_pairs = far_pairs + [(j, i) for i, j in far_pairs]
    local_bytes = 2 * query_rows.size

    edge_shape = jax.ShapeDtypeStruct((regions, columns, width), jnp.bfloat16)
    chunk_shape = jax.ShapeDtypeStruct((3, per_device, tokens, width), jnp.bfloat16)
    index = seq_index.reshape(1)
    *packed, cot_near, cot_far = call(
        functools.partial(pack_kernel, regions, HEADS, per_device),
        "pack",
        [chunk_shape] * seq_count + [edge_shape] * 2,
        [SMEM()] + [HBM()] * 4,
        out_specs=[HBM()] * (seq_count + 2),
        scratch=[
            pltpu.VMEM((3,) + query_rows.shape, jnp.bfloat16),
            pltpu.VMEM((seq_count,) + chunk_shape.shape, jnp.bfloat16),
            pltpu.VMEM((2,) + edge_shape.shape, jnp.bfloat16),
            pltpu.SemaphoreType.DMA((7 + 3 * seq_count,)),
        ],
        moved=6 * local_bytes,
        grant=VMEM_WHOLE,
    )(index, query_rows, key_rows, value_rows, cotangent)
    half = seq_count // 2
    order = list(range(half, seq_count)) + list(range(1, half)) + [0]
    for distance in order[:-1]:
        packed[distance] = trade(packed[distance], distance)
    cot_near = trade(cot_near, 1)
    cot_far = lax.ppermute(cot_far, "seq", far_pairs)

    items = seq_index * per_device + jnp.arange(per_device, dtype=jnp.int32)
    item_lengths = jnp.sum(
        jnp.where(
            (items % regions)[:, None] == jnp.arange(regions, dtype=jnp.int32)[None, :],
            region_lengths[None, :],
            0,
        ),
        axis=1,
    )
    block_rows = min(256, capacity)
    group = regions if per_device % regions == 0 else per_device
    mixed = call(
        functools.partial(attend_kernel, block_rows, group, order),
        "attend",
        jax.ShapeDtypeStruct((seq_count, per_device, tokens, width), jnp.bfloat16),
        [SMEM(), SMEM()] + [VMEM()] * seq_count,
        out_specs=HBM(),
        scratch=[
            pltpu.VMEM((seq_count, per_device, tokens, width), jnp.bfloat16),
            pltpu.SemaphoreType.DMA((per_device * -(-capacity // block_rows),)),
        ],
        flops=4 * per_device * capacity * capacity * width,
        moved=4 * local_bytes,
        exps=per_device * capacity * capacity,
    )(index, item_lengths, *[packed[distance] for distance in order])
    attended = swap(mixed, "seq").reshape(HEADS, regions, tokens, width)

    chunk_rows = -(-9 * width // plane_size)
    pixel_rows = regions * PATCH * columns
    conv_flops = 18 * pixel_rows * width * width
    image, near, far, grad_parts = call(
        functools.partial(norm_kernel, chunk_rows),
        "norm_and_gradient",
        [
            jax.ShapeDtypeStruct((regions, PATCH, columns, width), jnp.bfloat16),
            edge_shape,
            edge_shape,
            jax.ShapeDtypeStruct((plane_size, chunk_rows, width), jnp.bfloat16),
        ],
        [SMEM(), SMEM()] + [VMEM()] * 5,
        scratch=[
            pltpu.VMEM((regions, PATCH, columns + 2 * RIM, width), jnp.float32),
            pltpu.VMEM((pixel_rows, 3 * width), jnp.bfloat16),
            pltpu.VMEM((pixel_rows, 3 * width), jnp.bfloat16),
            pltpu.VMEM((plane_size * chunk_rows, width), jnp.float32),
        ],
        flops=conv_flops,
        moved=4 * local_bytes,
    )(
        region_lengths,
        index,
        attended,
        norm_gain.reshape(HEADS, width),
        cotangent,
        cot_near,
        cot_far,
    )
    grad_parts = swap(grad_parts, ("dp", "seq"), planes)
    near = trade(near, 1)
    far = lax.ppermute(far, "seq", far_pairs)
    plane_sum = call(
        functools.partial(sum_kernel, 1, None),
        "sum_plane",
        jax.ShapeDtypeStruct((chunk_rows, width), jnp.bfloat16),
        [VMEM()],
        moved=2 * grad_parts.size,
    )(grad_parts)
    plane_sums = [plane_sum] + [trade(plane_sum, inner * step) for step in range(1, len(planes))]
    sums = call(
        functools.partial(sum_kernel, len(planes), 1.0 / math.sqrt(PATCH * columns)),
        "sum_planes",
        jax.ShapeDtypeStruct(grad_parts.shape, jnp.bfloat16),
        [VMEM()] * len(planes) + [ANY(), ANY()],
        moved=4 * grad_parts.size,
    )(*plane_sums, near, far)
    sums = swap(sums, ("dp", "seq"), planes)
    decoded = call(
        decode_kernel,
        "decode",
        jax.ShapeDtypeStruct(cotangent.shape, jnp.bfloat16),
        [SMEM()] + [VMEM()] * 4,
        scratch=[pltpu.VMEM((columns + 2 * RIM, width), jnp.float32)],
        flops=conv_flops,
        moved=2 * local_bytes,
    )(index, image, near, far, conv_weight.reshape(3, 3 * width, width))
    weight_grad = call(
        spread_kernel,
        "spread_sums",
        jax.ShapeDtypeStruct((9 * width, width), jnp.float32),
        [VMEM()],
        moved=6 * grad_parts.size,
    )(sums)
    return (decoded, weight_grad.reshape(conv_weight.shape))


def solution(mesh):
    placed = (
        P("seq", "dp", None),
        P("seq", "dp", None),
        P("seq", "dp", None),
        P("dp"),
        P(),
        P(),
        P("dp", "seq", None, None),
    )
    return jax.shard_map(
        body,
        mesh=mesh,
        in_specs=placed,
        out_specs=(P("dp", "seq", None, None), P()),
        check_vma=False,
    )
```

time: 111 us -> 106 us (0.955)
  starting transfers between devices: 44.8 us -> 35 us
  waiting for transfers between devices: 47.5 us -> 53.9 us
  Pallas kernels: 16.9 us -> 14.1 us
    all_to_all x3, starting transfers between devices: 20.3 us -> 14.4 us  [swap(): lax.all_to_all(parts, axes, split_axis=0, concat_axis=0, axis_index_group...]
    ppermute x11 -> x14, waiting for transfers between devices: 34.7 us -> 39.6 us  [the longest x12 39.6 us: trade(): return lax.ppermute(values, 'seq', pairs)]
    ppermute x11 -> x14, starting transfers between devices: 24.5 us -> 20.6 us  [the longest x12 19.3 us: trade(): return lax.ppermute(values, 'seq', pairs)]
    pallas_call x2 -> x3, Pallas kernels: 6.1 us -> 3.28 us  [the longest x1 2.5 us: body(): call(functools.partial(attend_kernel, block_rows, group, order), 'attend'...]
    all_to_all x3, waiting for transfers between devices: 12.8 us -> 14.3 us  [swap(): lax.all_to_all(parts, axes, split_axis=0, concat_axis=0, axis_index_group...]
  transfers between devices with their start and end apart: 14 -> 17, of which waited for: 10 -> 11; matrix products, arithmetic and copies ran while one was open for 0% -> 0% of each run, Pallas kernels for 2% -> 2%
where the time goes in v5:
time: 106 us; the launch traced here: 105 us
  waiting for transfers between devices  53.9 us (51%)
  starting transfers between devices  35 us (33%)
  Pallas kernels  14.1 us (13%)
  local copies, waits for them, and re-layouts  1.59 us (2%)
    ppermute x12, waiting for transfers between devices, trade(): return lax.ppermute(values, 'seq', pairs)  39.6 us
    ppermute x12, starting transfers between devices, trade(): return lax.ppermute(values, 'seq', pairs)  19.3 us
    all_to_all x3, starting transfers between devices, swap(): lax.all_to_all(parts, axes, split_axis=0, concat_axis=0, axis_index_group...  14.4 us
    all_to_all x3, waiting for transfers between devices, swap(): lax.all_to_all(parts, axes, split_axis=0, concat_axis=0, axis_index_group...  14.3 us
    pallas_call x1, Pallas kernels, body(): call(functools.partial(pack_kernel, regions, HEADS, per_device), 'pack',...  4.08 us
    pallas_call x1, Pallas kernels, body(): call(functools.partial(norm_kernel, chunk_rows), 'norm_and_gradient', [ja...  3.65 us
    pallas_call x1, Pallas kernels, body(): call(functools.partial(attend_kernel, block_rows, group, order), 'attend'...  2.5 us
    pallas_call x1, Pallas kernels, body(): call(decode_kernel, 'decode', jax.ShapeDtypeStruct(cotangent.shape, jnp.b...  2.23 us
  transfers between devices with their start and end apart: 17, of which 11 were waited for; matrix products, arithmetic and copies ran while one was open for 0% of the time, Pallas kernels for 2%

profile of v5, /device:TPU:0, one launch (start us, length us, event | category | flops | bytes accessed | tf_op | source)
XLA Modules:
  0.0 105.4 jit_solution(13361934272976130044)
XLA Ops:
  0.6 4.1 %pack.1 = (bf16[3,4,64,128]{3,2,1,0:T(8,128)(2,1)}, bf16[3,4,64,128]{3,2,1,0:T(8,128)(2,1)}, bf16[3,4,64,128]{3,2,1,0:T(8,128)(2,1)}, bf16[3,4,64,128]{3,2,1,0:T...) custom-call(s32[1]{0:T(128)} %bitcast.index_ref, ...), custom_call_target="tpu_custom_call" | custom-call | bytes 3145728 | tf_op jit(solution)/shard_map/pack/pallas_call | solution.py:366
  4.7 4.1 %collective-permute-start = (bf16[3,4,64,128]{3,2,1,0:T(8,128)(2,1)}, bf16[3,4,64,128]{3,2,1,0:T(8,128)(2,1)S(1)}, u32[]{:S(2)}, u32[]{:S(2)}) collective-permute-start(bf16[3,4,64,128]{3,2,1,0:T(8,128)(2,1)} %get-tuple-element.16), channel_id=1, source_target_pairs={{0,4},{1,5},{2,6},{3,7},{4,0},{5,1},{6,2},{7,3},{8,12},{9,13},{10,... | collective-permute-start | bytes 589832 | tf_op jit(solution)/shard_map/ppermute | solution.py:335
  8.8 1.3 %collective-permute-start.1 = (bf16[3,4,64,128]{3,2,1,0:T(8,128)(2,1)}, bf16[3,4,64,128]{3,2,1,0:T(8,128)(2,1)S(1)}, u32[]{:S(2)}, u32[]{:S(2)}) collective-permute-start(bf16[3,4,64,128]{3,2,1,0:T(8,128)(2,1)} %get-tuple-element.17), channel_id=1, source_target_pairs={{0,5},{1,4},{2,7},{3,6},{4,1},{5,0},{6,3},{7,2},{8,13},{9,12},{10,... | collective-permute-start | bytes 589832 | tf_op jit(solution)/shard_map/ppermute | solution.py:335
  10.1 3.6 %collective-permute-start.2 = (bf16[3,4,64,128]{3,2,1,0:T(8,128)(2,1)}, bf16[3,4,64,128]{3,2,1,0:T(8,128)(2,1)S(1)}, u32[]{:S(2)}, u32[]{:S(2)}) collective-permute-start(bf16[3,4,64,128]{3,2,1,0:T(8,128)(2,1)} %get-tuple-element.18), channel_id=1, source_target_pairs={{0,6},{1,7},{2,4},{3,5},{4,2},{5,3},{6,0},{7,1},{8,14},{9,15},{10,... | collective-permute-start | bytes 589832 | tf_op jit(solution)/shard_map/ppermute | solution.py:335
  13.7 0.0 collective-permute-start.3
  13.7 1.7 %collective-permute-start.4 = (bf16[3,4,64,128]{3,2,1,0:T(8,128)(2,1)}, bf16[3,4,64,128]{3,2,1,0:T(8,128)(2,1)S(1)}, u32[]{:S(2)}, u32[]{:S(2)}) collective-permute-start(bf16[3,4,64,128]{3,2,1,0:T(8,128)(2,1)} %get-tuple-element.20), channel_id=1, source_target_pairs={{0,1},{1,0},{2,3},{3,2},{4,5},{5,4},{6,7},{7,6},{8,9},{9,8},{10,11... | collective-permute-start | bytes 589832 | tf_op jit(solution)/shard_map/ppermute | solution.py:335
  15.4 16.2 %collective-permute-done.refs_0_ = bf16[3,4,64,128]{3,2,1,0:T(8,128)(2,1)S(1)} collective-permute-done((bf16[3,4,64,128]{3,2,1,0:T(8,128)(2,1)}, bf16[3,4,64,128]{3,2,1,0:T(8,128)(2,1)S(1)}, u32[]{:S(2)}, u32[]{:S(2)}) %collective-permute-start) | collective-permute-done | bytes 196640 | tf_op jit(solution)/shard_map/ppermute | solution.py:335
  31.6 0.1 collective-permute-start.5
  31.7 5.4 %collective-permute-done.1.refs_1_ = bf16[3,4,64,128]{3,2,1,0:T(8,128)(2,1)S(1)} collective-permute-done((bf16[3,4,64,128]{3,2,1,0:T(8,128)(2,1)}, bf16[3,4,64,128]{3,2,1,0:T(8,128)(2,1)S(1)}, u32[]{:S(2)}, u32[]{:S(2)}) %collective-permute-start.1) | collective-permute-done | bytes 196640 | tf_op jit(solution)/shard_map/ppermute | solution.py:335
  37.1 0.0 copy-start.4
  37.1 0.0 collective-permute-start.6
  37.1 0.6 copy-done.4
  37.8 0.1 fusion.lengths_ref
  37.8 0.0 collective-permute-done.2.refs_2_
  37.8 0.0 collective-permute-done.3.refs_3_
  37.9 0.0 collective-permute-done.4.refs_4_
  37.9 2.0 %collective-permute-done.5.refs_5_ = bf16[3,4,64,128]{3,2,1,0:T(8,128)(2,1)S(1)} collective-permute-done((bf16[3,4,64,128]{3,2,1,0:T(8,128)(2,1)}, bf16[3,4,64,128]{3,2,1,0:T(8,128)(2,1)S(1)}, u32[]{:S(2)}, u32[]{:S(2)}) %collective-permute-start.5) | collective-permute-done | bytes 196640 | tf_op jit(solution)/shard_map/ppermute | solution.py:335
  39.9 4.5 %collective-permute-done.6.refs_6_ = bf16[3,4,64,128]{3,2,1,0:T(8,128)(2,1)S(1)} collective-permute-done((bf16[3,4,64,128]{3,2,1,0:T(8,128)(2,1)}, bf16[3,4,64,128]{3,2,1,0:T(8,128)(2,1)S(1)}, u32[]{:S(2)}, u32[]{:S(2)}) %collective-permute-start.6) | collective-permute-done | bytes 196640 | tf_op jit(solution)/shard_map/ppermute | solution.py:335
  44.4 0.0 copy-start.1
  44.4 0.9 copy-done.1
  45.3 2.5 %attend.1 = bf16[8,4,64,128]{3,2,1,0:T(8,128)(2,1)} custom-call(s32[1]{0:T(128)} %bitcast.index_ref, s32[4]{0:T(128)S(1)} %fusion.lengths_ref, bf16[3,4,64,128]{3,2,1,0:T(8,128)(2,1)S(1)} %collective-permute-done.refs_0_, bf16[3,4,64,128]{3,2,1,0:T(8,128)(2,1)S(1)} %collective-permute-done.1.refs_1_, ...), custom_call_target="tpu_custom_call" | custom-call | flops 536870912 | bytes 2097152 | tf_op jit(solution)/shard_map/attend/pallas_call | solution.py:399
  47.8 0.0 copy-start.6
  47.8 0.0 copy-start.5
  47.9 0.0 copy-start
  47.9 0.0 copy-start.3
  47.9 7.5 %all-to-all-start = ((bf16[8,4,64,128]{3,2,1,0:T(8,128)(2,1)}), bf16[8,4,64,128]{3,2,1,0:T(8,128)(2,1)S(1)}, u32[]{:S(2)}, u32[]{:S(2)}) async-start(bf16[8,4,64,128]{3,2,1,0:T(8,128)(2,1)} %attend.1), calls=%async_computation | async-start | bytes 1048576 | tf_op jit(solution)/shard_map/all_to_all | solution.py:328
  55.3 0.0 copy-done.6
  55.3 2.0 %collective-permute-start.7 = (bf16[2,256,128]{2,1,0:T(8,128)(2,1)S(1)}, bf16[2,256,128]{2,1,0:T(8,128)(2,1)S(1)}, u32[]{:S(2)}, u32[]{:S(2)}) collective-permute-start(bf16[2,256,128]{2,1,0:T(8,128)(2,1)S(1)} %copy-done.6), channel_id=1, source_target_pairs={{0,1},{1,0},{2,3},{3,2},{4,5},{5,4},{6,7},{7,6},{8,9},{9,8},{10,11... | collective-permute-start | bytes 393224 | tf_op jit(solution)/shard_map/ppermute | solution.py:335
  57.4 0.0 copy-done.5
  57.4 0.7 collective-permute-start.8
  58.0 7.4 %collective-permute-done.7.cot_near_ref = bf16[2,256,128]{2,1,0:T(8,128)(2,1)S(1)} collective-permute-done((bf16[2,256,128]{2,1,0:T(8,128)(2,1)S(1)}, bf16[2,256,128]{2,1,0:T(8,128)(2,1)S(1)}, u32[]{:S(2)}, u32[]{:S(2)}) %collective-permute-start.7) | collective-permute-done | bytes 131104 | tf_op jit(solution)/shard_map/ppermute | solution.py:335
  65.5 0.0 collective-permute-done.8.cot_far_ref
  65.5 5.6 %all-to-all-done = bf16[8,4,64,128]{3,2,1,0:T(8,128)(2,1)S(1)} async-done(((bf16[8,4,64,128]{3,2,1,0:T(8,128)(2,1)}), bf16[8,4,64,128]{3,2,1,0:T(8,128)(2,1)S(1)}, u32[]{:S(2)}, u32[]{:S(2)}) %all-to-all-start) | async-done | bytes 524320 | tf_op jit(solution)/shard_map/all_to_all | solution.py:328
  71.1 0.0 copy-done
  71.1 0.0 copy-done.3
  71.1 3.7 %norm_and_gradient.1 = (bf16[2,4,256,128]{3,2,1,0:T(8,128)(2,1)S(1)}, bf16[2,256,128]{2,1,0:T(8,128)(2,1)S(1)}, bf16[2,256,128]{2,1,0:T(8,128)(2,1)S(1)}, bf16[8,144,128]{2,1,0:T(8,128)(2,1)}) custom-call(s32[2]{0:T(128)S(1)} %copy-done.4, s32[1]{0:T(128)} %bitcast.index_ref, bf16[16,2,64,128]{3,2,1,0:T(8,128)(2,1)S(1)} %bitcast.5, f32[16,128]{1,0:T(8,128)S(1)} %bitcast.7, ...), custom_call_target="tpu_custom_call" | custom-call | flops 603979776 | bytes 2097152 | tf_op jit(solution)/shard_map/norm_and_gradient/pallas_call | solution.py:418
  74.8 3.4 %all-to-all-start.1 = ((bf16[8,144,128]{2,1,0:T(8,128)(2,1)}), bf16[8,144,128]{2,1,0:T(8,128)(2,1)S(1)}, u32[]{:S(2)}, u32[]{:S(2)}) async-start(bf16[8,144,128]{2,1,0:T(8,128)(2,1)} %get-tuple-element.29), calls=%async_computation.1 | async-start | bytes 589824 | tf_op jit(solution)/shard_map/all_to_all | solution.py:328
  78.2 1.9 %collective-permute-start.9 = (bf16[2,256,128]{2,1,0:T(8,128)(2,1)S(1)}, bf16[2,256,128]{2,1,0:T(8,128)(2,1)S(1)}, u32[]{:S(2)}, u32[]{:S(2)}) collective-permute-start(bf16[2,256,128]{2,1,0:T(8,128)(2,1)S(1)} %get-tuple-element.27), channel_id=1, source_target_pairs={{0,1},{1,0},{2,3},{3,2},{4,5},{5,4},{6,7},{7,6},{8,9},{9,8},{10,11... | collective-permute-start | bytes 393224 | tf_op jit(solution)/shard_map/ppermute | solution.py:335
  80.1 0.7 collective-permute-start.10
  80.8 4.1 %all-to-all-done.1.refs_0_ = bf16[8,144,128]{2,1,0:T(8,128)(2,1)S(1)} async-done(((bf16[8,144,128]{2,1,0:T(8,128)(2,1)}), bf16[8,144,128]{2,1,0:T(8,128)(2,1)S(1)}, u32[]{:S(2)}, u32[]{:S(2)}) %all-to-all-start.1) | async-done | bytes 294944 | tf_op jit(solution)/shard_map/all_to_all | solution.py:328
  85.0 1.3 %collective-permute-start.13 = (bf16[144,128]{1,0:T(8,128)(2,1)S(1)}, bf16[144,128]{1,0:T(8,128)(2,1)S(1)}, u32[]{:S(2)}, u32[]{:S(2)}) collective-permute-start(bf16[144,128]{1,0:T(8,128)(2,1)S(1)} %sum_plane.1.refs_0_), channel_id=1, source_target_pairs={{0,6},{1,7},{2,4},{3,5},{4,2},{5,3},{6,0},{7,1},{8,14},{9,15},{10,... | collective-permute-start | bytes 110600 | tf_op jit(solution)/shard_map/ppermute | solution.py:335
  86.3 3.3 %collective-permute-start.12 = (bf16[144,128]{1,0:T(8,128)(2,1)S(1)}, bf16[144,128]{1,0:T(8,128)(2,1)S(1)}, u32[]{:S(2)}, u32[]{:S(2)}) collective-permute-start(bf16[144,128]{1,0:T(8,128)(2,1)S(1)} %sum_plane.1.refs_0_), channel_id=1, source_target_pairs={{0,4},{1,5},{2,6},{3,7},{4,0},{5,1},{6,2},{7,3},{8,12},{9,13},{10,... | collective-permute-start | bytes 110600 | tf_op jit(solution)/shard_map/ppermute | solution.py:335
  89.6 0.0 collective-permute-start.11
  89.6 0.0 collective-permute-done.9.near_ref.refs_4_
  89.6 0.0 collective-permute-done.10.far_ref.refs_5_
  89.6 1.3 %collective-permute-done.13.refs_3_ = bf16[144,128]{1,0:T(8,128)(2,1)S(1)} collective-permute-done((bf16[144,128]{1,0:T(8,128)(2,1)S(1)}, bf16[144,128]{1,0:T(8,128)(2,1)S(1)}, u32[]{:S(2)}, u32[]{:S(2)}) %collective-permute-start.13) | collective-permute-done | bytes 36896 | tf_op jit(solution)/shard_map/ppermute | solution.py:335
  90.9 1.8 %collective-permute-done.12.refs_2_ = bf16[144,128]{1,0:T(8,128)(2,1)S(1)} collective-permute-done((bf16[144,128]{1,0:T(8,128)(2,1)S(1)}, bf16[144,128]{1,0:T(8,128)(2,1)S(1)}, u32[]{:S(2)}, u32[]{:S(2)}) %collective-permute-start.12) | collective-permute-done | bytes 36896 | tf_op jit(solution)/shard_map/ppermute | solution.py:335
  92.7 0.9 collective-permute-done.11.refs_1_
  93.5 0.7 sum_planes.1
  94.3 0.0 copy-start.2
  94.3 3.6 %all-to-all-start.2 = ((bf16[8,144,128]{2,1,0:T(8,128)(2,1)}), bf16[8,144,128]{2,1,0:T(8,128)(2,1)S(1)}, u32[]{:S(2)}, u32[]{:S(2)}) async-start(bf16[8,144,128]{2,1,0:T(8,128)(2,1)} %sum_planes.1), calls=%async_computation.2 | async-start | bytes 589824 | tf_op jit(solution)/shard_map/all_to_all | solution.py:328
  97.9 0.0 copy-done.2
  97.9 2.2 %decode.1 = bf16[2,4,256,128]{3,2,1,0:T(8,128)(2,1)} custom-call(s32[1]{0:T(128)} %bitcast.index_ref, bf16[2,4,256,128]{3,2,1,0:T(8,128)(2,1)S(1)} %get-tuple-element.26.image_ref, bf16[2,256,128]{2,1,0:T(8,128)(2,1)S(1)} %collective-permute-done.9.near_ref.refs_4_, bf16[2,256,128]{2,1,0:T(8,128)(2,1)S(1)} %collective-permute-done.10.far_ref.refs_5_, ...), custom_call_target="tpu_custom_call" | custom-call | flops 603979776 | bytes 1048576 | tf_op jit(solution)/shard_map/decode/pallas_call | solution.py:464
  100.1 4.5 %all-to-all-done.2.parts_ref = bf16[8,144,128]{2,1,0:T(8,128)(2,1)S(1)} async-done(((bf16[8,144,128]{2,1,0:T(8,128)(2,1)}), bf16[8,144,128]{2,1,0:T(8,128)(2,1)S(1)}, u32[]{:S(2)}, u32[]{:S(2)}) %all-to-all-start.2) | async-done | bytes 294944 | tf_op jit(solution)/shard_map/all_to_all | solution.py:328
  104.6 0.9 spread_sums.1
  (2 shorter events, 0.1 us)
Async XLA Ops:
  4.7 26.9 %collective-permute-start = (bf16[3,4,64,128]{3,2,1,0:T(8,128)(2,1)}, bf16[3,4,64,128]{3,2,1,0:T(8,128)(2,1)S(1)}, u32[]{:S(2)}, u32[]{:S(2)}) collective-permute-start(bf16[3,4,64,128]{3,2,1,0:T(8,128)(2,1)} %get-tuple-element.16), channel_id=1, source_target_pairs={{0,4},{1,5},{2,6},{3,7},{4,0},{5,1},{6,2},{7,3},{8,12},{9,13},{10,... | collective-permute-start | bytes 589832 | tf_op jit(solution)/shard_map/ppermute | solution.py:335
  8.8 28.3 %collective-permute-start.1 = (bf16[3,4,64,128]{3,2,1,0:T(8,128)(2,1)}, bf16[3,4,64,128]{3,2,1,0:T(8,128)(2,1)S(1)}, u32[]{:S(2)}, u32[]{:S(2)}) collective-permute-start(bf16[3,4,64,128]{3,2,1,0:T(8,128)(2,1)} %get-tuple-element.17), channel_id=1, source_target_pairs={{0,5},{1,4},{2,7},{3,6},{4,1},{5,0},{6,3},{7,2},{8,13},{9,12},{10,... | collective-permute-start | bytes 589832 | tf_op jit(solution)/shard_map/ppermute | solution.py:335
  10.1 27.8 %collective-permute-start.2 = (bf16[3,4,64,128]{3,2,1,0:T(8,128)(2,1)}, bf16[3,4,64,128]{3,2,1,0:T(8,128)(2,1)S(1)}, u32[]{:S(2)}, u32[]{:S(2)}) collective-permute-start(bf16[3,4,64,128]{3,2,1,0:T(8,128)(2,1)} %get-tuple-element.18), channel_id=1, source_target_pairs={{0,6},{1,7},{2,4},{3,5},{4,2},{5,3},{6,0},{7,1},{8,14},{9,15},{10,... | collective-permute-start | bytes 589832 | tf_op jit(solution)/shard_map/ppermute | solution.py:335
  13.7 24.2 %collective-permute-start.3 = (bf16[3,4,64,128]{3,2,1,0:T(8,128)(2,1)}, bf16[3,4,64,128]{3,2,1,0:T(8,128)(2,1)S(1)}, u32[]{:S(2)}, u32[]{:S(2)}) collective-permute-start(bf16[3,4,64,128]{3,2,1,0:T(8,128)(2,1)} %get-tuple-element.19), channel_id=1, source_target_pairs={{0,7},{1,6},{2,5},{3,4},{4,3},{5,2},{6,1},{7,0},{8,15},{9,14},{10,... | collective-permute-start | bytes 589832 | tf_op jit(solution)/shard_map/ppermute | solution.py:335
  13.7 24.2 %collective-permute-start.4 = (bf16[3,4,64,128]{3,2,1,0:T(8,128)(2,1)}, bf16[3,4,64,128]{3,2,1,0:T(8,128)(2,1)S(1)}, u32[]{:S(2)}, u32[]{:S(2)}) collective-permute-start(bf16[3,4,64,128]{3,2,1,0:T(8,128)(2,1)} %get-tuple-element.20), channel_id=1, source_target_pairs={{0,1},{1,0},{2,3},{3,2},{4,5},{5,4},{6,7},{7,6},{8,9},{9,8},{10,11... | collective-permute-start | bytes 589832 | tf_op jit(solution)/shard_map/ppermute | solution.py:335
  31.6 8.3 %collective-permute-start.5 = (bf16[3,4,64,128]{3,2,1,0:T(8,128)(2,1)}, bf16[3,4,64,128]{3,2,1,0:T(8,128)(2,1)S(1)}, u32[]{:S(2)}, u32[]{:S(2)}) collective-permute-start(bf16[3,4,64,128]{3,2,1,0:T(8,128)(2,1)} %get-tuple-element.21), channel_id=1, source_target_pairs={{0,2},{1,3},{2,0},{3,1},{4,6},{5,7},{6,4},{7,5},{8,10},{9,11},{10,... | collective-permute-start | bytes 589832 | tf_op jit(solution)/shard_map/ppermute | solution.py:335
  37.1 0.7 copy-start.4
  37.1 7.3 %collective-permute-start.6 = (bf16[3,4,64,128]{3,2,1,0:T(8,128)(2,1)}, bf16[3,4,64,128]{3,2,1,0:T(8,128)(2,1)S(1)}, u32[]{:S(2)}, u32[]{:S(2)}) collective-permute-start(bf16[3,4,64,128]{3,2,1,0:T(8,128)(2,1)} %get-tuple-element.22), channel_id=1, source_target_pairs={{0,3},{1,2},{2,1},{3,0},{4,7},{5,6},{6,5},{7,4},{8,11},{9,10},{10,... | collective-permute-start | bytes 589832 | tf_op jit(solution)/shard_map/ppermute | solution.py:335
  44.4 0.9 copy-start.1
  47.8 7.5 %copy-start.6 = (bf16[2,256,128]{2,1,0:T(8,128)(2,1)S(1)}, bf16[2,256,128]{2,1,0:T(8,128)(2,1)}, u32[]{:S(2)}) copy-start(bf16[2,256,128]{2,1,0:T(8,128)(2,1)} %get-tuple-element.24) | copy-start | bytes 393220
  47.8 9.5 %copy-start.5 = (bf16[2,256,128]{2,1,0:T(8,128)(2,1)S(1)}, bf16[2,256,128]{2,1,0:T(8,128)(2,1)}, u32[]{:S(2)}) copy-start(bf16[2,256,128]{2,1,0:T(8,128)(2,1)} %get-tuple-element.25) | copy-start | bytes 393220
  47.9 23.3 %copy-start = (bf16[2,4,256,128]{3,2,1,0:T(8,128)(2,1)S(1)}, bf16[2,4,256,128]{3,2,1,0:T(8,128)(2,1)}, u32[]{:S(2)}) copy-start(bf16[2,4,256,128]{3,2,1,0:T(8,128)(2,1)} %cot_ref.3) | copy-start | bytes 1572868
  47.9 23.3 %copy-start.3 = (f32[2048]{0:T(1024)S(1)}, f32[2048]{0:T(1024)}, u32[]{:S(2)}) copy-start(f32[2048]{0:T(1024)} %param.11) | copy-start | bytes 24580
  47.9 23.2 %all-to-all-start = ((bf16[8,4,64,128]{3,2,1,0:T(8,128)(2,1)}), bf16[8,4,64,128]{3,2,1,0:T(8,128)(2,1)S(1)}, u32[]{:S(2)}, u32[]{:S(2)}) async-start(bf16[8,4,64,128]{3,2,1,0:T(8,128)(2,1)} %attend.1), calls=%async_computation | async-start | bytes 1048576 | tf_op jit(solution)/shard_map/all_to_all | solution.py:328
  55.3 10.1 %collective-permute-start.7 = (bf16[2,256,128]{2,1,0:T(8,128)(2,1)S(1)}, bf16[2,256,128]{2,1,0:T(8,128)(2,1)S(1)}, u32[]{:S(2)}, u32[]{:S(2)}) collective-permute-start(bf16[2,256,128]{2,1,0:T(8,128)(2,1)S(1)} %copy-done.6), channel_id=1, source_target_pairs={{0,1},{1,0},{2,3},{3,2},{4,5},{5,4},{6,7},{7,6},{8,9},{9,8},{10,11... | collective-permute-start | bytes 393224 | tf_op jit(solution)/shard_map/ppermute | solution.py:335
  57.4 8.1 %collective-permute-start.8 = (bf16[2,256,128]{2,1,0:T(8,128)(2,1)S(1)}, bf16[2,256,128]{2,1,0:T(8,128)(2,1)S(1)}, u32[]{:S(2)}, u32[]{:S(2)}) collective-permute-start(bf16[2,256,128]{2,1,0:T(8,128)(2,1)S(1)} %copy-done.5), channel_id=1, source_target_pairs={{1,2},{3,4},{5,6},{2,1},{4,3},{6,5},{9,10},{11,12},{13,14},{10,9},... | collective-permute-start | bytes 393224 | tf_op jit(solution)/shard_map/ppermute | solution.py:386
  74.8 10.2 %all-to-all-start.1 = ((bf16[8,144,128]{2,1,0:T(8,128)(2,1)}), bf16[8,144,128]{2,1,0:T(8,128)(2,1)S(1)}, u32[]{:S(2)}, u32[]{:S(2)}) async-start(bf16[8,144,128]{2,1,0:T(8,128)(2,1)} %get-tuple-element.29), calls=%async_computation.1 | async-start | bytes 589824 | tf_op jit(solution)/shard_map/all_to_all | solution.py:328
  78.2 11.4 %collective-permute-start.9 = (bf16[2,256,128]{2,1,0:T(8,128)(2,1)S(1)}, bf16[2,256,128]{2,1,0:T(8,128)(2,1)S(1)}, u32[]{:S(2)}, u32[]{:S(2)}) collective-permute-start(bf16[2,256,128]{2,1,0:T(8,128)(2,1)S(1)} %get-tuple-element.27), channel_id=1, source_target_pairs={{0,1},{1,0},{2,3},{3,2},{4,5},{5,4},{6,7},{7,6},{8,9},{9,8},{10,11... | collective-permute-start | bytes 393224 | tf_op jit(solution)/shard_map/ppermute | solution.py:335
  80.1 9.5 %collective-permute-start.10 = (bf16[2,256,128]{2,1,0:T(8,128)(2,1)S(1)}, bf16[2,256,128]{2,1,0:T(8,128)(2,1)S(1)}, u32[]{:S(2)}, u32[]{:S(2)}) collective-permute-start(bf16[2,256,128]{2,1,0:T(8,128)(2,1)S(1)} %get-tuple-element.28), channel_id=1, source_target_pairs={{1,2},{3,4},{5,6},{2,1},{4,3},{6,5},{9,10},{11,12},{13,14},{10,9},... | collective-permute-start | bytes 393224 | tf_op jit(solution)/shard_map/ppermute | solution.py:447
  85.0 5.9 %collective-permute-start.13 = (bf16[144,128]{1,0:T(8,128)(2,1)S(1)}, bf16[144,128]{1,0:T(8,128)(2,1)S(1)}, u32[]{:S(2)}, u32[]{:S(2)}) collective-permute-start(bf16[144,128]{1,0:T(8,128)(2,1)S(1)} %sum_plane.1.refs_0_), channel_id=1, source_target_pairs={{0,6},{1,7},{2,4},{3,5},{4,2},{5,3},{6,0},{7,1},{8,14},{9,15},{10,... | collective-permute-start | bytes 110600 | tf_op jit(solution)/shard_map/ppermute | solution.py:335
  86.3 6.4 %collective-permute-start.12 = (bf16[144,128]{1,0:T(8,128)(2,1)S(1)}, bf16[144,128]{1,0:T(8,128)(2,1)S(1)}, u32[]{:S(2)}, u32[]{:S(2)}) collective-permute-start(bf16[144,128]{1,0:T(8,128)(2,1)S(1)} %sum_plane.1.refs_0_), channel_id=1, source_target_pairs={{0,4},{1,5},{2,6},{3,7},{4,0},{5,1},{6,2},{7,3},{8,12},{9,13},{10,... | collective-permute-start | bytes 110600 | tf_op jit(solution)/shard_map/ppermute | solution.py:335
  89.6 4.0 %collective-permute-start.11 = (bf16[144,128]{1,0:T(8,128)(2,1)S(1)}, bf16[144,128]{1,0:T(8,128)(2,1)S(1)}, u32[]{:S(2)}, u32[]{:S(2)}) collective-permute-start(bf16[144,128]{1,0:T(8,128)(2,1)S(1)} %sum_plane.1.refs_0_), channel_id=1, source_target_pairs={{0,2},{1,3},{2,0},{3,1},{4,6},{5,7},{6,4},{7,5},{8,10},{9,11},{10,... | collective-permute-start | bytes 110600 | tf_op jit(solution)/shard_map/ppermute | solution.py:335
  94.3 3.6 %copy-start.2 = (bf16[9,128,128]{2,1,0:T(8,128)(2,1)S(1)}, bf16[9,128,128]{2,1,0:T(8,128)(2,1)}, u32[]{:S(2)}) copy-start(bf16[9,128,128]{2,1,0:T(8,128)(2,1)} %param.12) | copy-start | bytes 884740
  94.3 10.3 %all-to-all-start.2 = ((bf16[8,144,128]{2,1,0:T(8,128)(2,1)}), bf16[8,144,128]{2,1,0:T(8,128)(2,1)S(1)}, u32[]{:S(2)}, u32[]{:S(2)}) async-start(bf16[8,144,128]{2,1,0:T(8,128)(2,1)} %sum_planes.1), calls=%async_computation.2 | async-start | bytes 589824 | tf_op jit(solution)/shard_map/all_to_all | solution.py:328

commit v6 on v5

--- a/solution.py
+++ b/solution.py
@@ -34,21 +34,35 @@
     )
 
 
+def unpack_items(held, which, regions, per_device, owner):
+    width = held.shape[3] // HEADS
+    aligned = per_device % regions == 0
+    items = []
+    for place in range(per_device):
+        if aligned and place % regions:
+            region = place % regions
+        else:
+            item = owner * per_device + place
+            head = lax.div(item, regions)
+            region = 0 if aligned else lax.rem(item, regions)
+            start = pl.multiple_of(head * width, width)
+            block = held[which, :, :, pl.ds(start, width)].astype(jnp.float32)
+        value = block[:, 0, :]
+        for other in range(1, regions):
+            if aligned:
+                value = block[:, other, :] if region == other else value
+            else:
+                value = jnp.where(region == other, block[:, other, :], value)
+        items.append(value.astype(jnp.bfloat16))
+    return items
+
+
 def pack_kernel(
-    regions,
-    heads,
-    per_device,
-    index_ref,
-    query_ref,
-    key_ref,
-    value_ref,
-    cot_ref,
-    *refs,
+    regions, per_device, index_ref, query_ref, key_ref, value_ref, cot_ref, *refs
 ):
     held, ready, edges, sems = refs[-4:]
     edge_refs = refs[-6:-4]
     out_refs = refs[:-6]
-    width = held.shape[3] // heads
     rows = cot_ref.shape[1]
     loads = [
         pltpu.make_async_copy(ref, held.at[which], sems.at[which])
@@ -62,13 +76,10 @@
     stores = []
     for which in range(3):
         loads[which].wait()
-        for head in range(heads):
-            block = held[which, :, :, head * width : (head + 1) * width].astype(jnp.float32)
-            for region in range(regions):
-                item = head * regions + region
-                slot = lax.bitwise_xor(index_ref[0], item // per_device)
-                ready[slot, which, item % per_device] = block[:, region, :].astype(jnp.bfloat16)
         for number, ref in enumerate(out_refs):
+            owner = lax.bitwise_xor(index_ref[0], number + 1)
+            for place, value in enumerate(unpack_items(held, which, regions, per_device, owner)):
+                ready[number, which, place] = value
             stores.append(
                 pltpu.make_async_copy(
                     ready.at[number, which], ref.at[which], sems.at[7 + 3 * number + which]
@@ -84,9 +95,37 @@
         store.wait()
 
 
+def own_kernel(regions, per_device, index_ref, query_ref, key_ref, value_ref, out_ref, held, sems):
+    tokens, width = out_ref.shape[2:]
+    span = max(1, per_device // regions) * width
+    index = index_ref[0]
+    start = lax.div(index * per_device, regions) * width
+    loads = []
+    for which, ref in enumerate((query_ref, key_ref, value_ref)):
+        columns = pl.ds(pl.multiple_of(start, width), span)
+        loads.append(
+            pltpu.make_async_copy(ref.at[:, :, columns], held.at[which], sems.at[which])
+        )
+        loads[-1].start()
+    for which, load in enumerate(loads):
+        load.wait()
+        for head in range(span // width):
+            block = held[which, :, :, head * width : (head + 1) * width].astype(jnp.float32)
+            if per_device % regions:
+                value = block[:, 0, :]
+                for other in range(1, regions):
+                    value = jnp.where(lax.rem(index, regions) == other, block[:, other, :], value)
+                out_ref[which, head] = value.astype(jnp.bfloat16)
+            else:
+                for region in range(regions):
+                    out_ref[which, head * regions + region] = block[:, region, :].astype(
+                        jnp.bfloat16
+                    )
+
+
 def attend_kernel(block_rows, group, order, index_ref, lengths_ref, *refs):
-    out_ref, mixed_ref, sems = refs[-3:]
-    chunks = dict(zip(order, refs[:-3]))
+    chunks = dict(zip(order, refs))
+    out_refs = refs[len(order) :]
     index = index_ref[0]
     sources = len(chunks)
     _, per_device, tokens, width = chunks[0].shape
@@ -112,9 +151,7 @@
 
     def clear(item, block):
         for distance in distances_of(block):
-            mixed_ref[lax.bitwise_xor(index, distance), item] = jnp.zeros(
-                (tokens, width), jnp.bfloat16
-            )
+            out_refs[distance][item] = jnp.zeros((tokens, width), jnp.bfloat16)
 
     def score(item, block):
         return lax.dot_general(
@@ -135,9 +172,7 @@
         )
         mixed = (mixed / totals).astype(jnp.bfloat16)
         for number, distance in enumerate(distances_of(block)):
-            mixed_ref[lax.bitwise_xor(index, distance), item] = mixed[
-                number * tokens : (number + 1) * tokens
-            ]
+            out_refs[distance][item] = mixed[number * tokens : (number + 1) * tokens]
 
     def attend(items, live, dead, length):
         key_valid = slots < length
@@ -154,7 +189,6 @@
             for item in items:
                 clear(item, block)
 
-    stores = []
     for lead in range(group):
         length = lengths_ref[lead]
         items = list(range(lead, per_device, group))
@@ -173,17 +207,6 @@
                 def _(items=items, live=live, dead=dead, length=length):
                     attend(items, live, dead, length)
 
-            span = per_block * len(pair)
-            rows = pl.ds(start_of(block // len(pair), span), span)
-            for item in items:
-                store = pltpu.make_async_copy(
-                    mixed_ref.at[rows, item], out_ref.at[rows, item], sems.at[len(stores)]
-                )
-                store.start()
-                stores.append(store)
-    for store in stores:
-        store.wait()
-
 
 def three_windows(padded, columns):
     return jnp.concatenate(
@@ -200,21 +223,23 @@
     chunk_rows,
     lengths_ref,
     index_ref,
-    attended_ref,
     gain_ref,
     cot_ref,
     cot_near_ref,
     cot_far_ref,
-    image_ref,
-    near_ref,
-    far_ref,
-    grad_ref,
-    pixels,
-    windows,
-    cots,
-    grads,
+    *refs,
 ):
-    heads, regions, tokens, width = attended_ref.shape
+    image_ref, near_ref, far_ref, grad_ref, attended, pixels, windows, cots, grads = refs[-9:]
+    for distance, ref in enumerate(refs[:-9]):
+        attended[lax.bitwise_xor(index_ref[0], distance)] = ref[...]
+    heads = gain_ref.shape[0]
+    regions = image_ref.shape[0]
+    _, per_device, tokens, width = attended.shape
+
+    def load(head, region):
+        owner, place = divmod(head * regions + region, per_device)
+        return attended[owner, place].astype(jnp.float32)
+
     columns = tokens * PATCH
     features = heads * width
     odd = lax.rem(index_ref[0], 2)
@@ -224,17 +249,17 @@
     for region in range(regions):
         total = jnp.zeros((tokens, width), jnp.float32)
         for head in range(heads):
-            total = total + attended_ref[head, region].astype(jnp.float32)
+            total = total + load(head, region)
         mean = jnp.sum(total, axis=1, keepdims=True) * (1.0 / features)
         total = jnp.zeros((tokens, width), jnp.float32)
         for head in range(heads):
-            centered = attended_ref[head, region].astype(jnp.float32) - mean
+            centered = load(head, region) - mean
             total = total + centered * centered
         variance = jnp.sum(total, axis=1, keepdims=True) * (1.0 / features)
         spread = lax.rsqrt(variance + 1e-05)
         live = position < lengths_ref[region]
         for head in range(heads):
-            centered = attended_ref[head, region].astype(jnp.float32) - mean
+            centered = load(head, region) - mean
             normed = jnp.where(live, centered * spread * gain_ref[head : head + 1, :], 0.0)
             row, column = divmod(head, PATCH)
             pixels[region, row, pl.ds(RIM + column, tokens, stride=PATCH), :] = normed
@@ -252,9 +277,14 @@
             )
         near_ref[region] = image_ref[region, (1 - odd) * (PATCH - 1)]
         far_ref[region] = image_ref[region, odd * (PATCH - 1)]
-    product = lax.dot_general(
-        windows[...], cots[...], (((0,), (0,)), ((), ())), preferred_element_type=jnp.float32
-    )
+        part = slice(region * PATCH * columns, (region + 1) * PATCH * columns)
+        term = lax.dot_general(
+            windows[part, :],
+            cots[part, :],
+            (((0,), (0,)), ((), ())),
+            preferred_element_type=jnp.float32,
+        )
+        product = term if region == 0 else product + term
     for down in range(3):
         for across in range(3):
             tap = 3 * down + across
@@ -363,25 +393,34 @@
     edge_shape = jax.ShapeDtypeStruct((regions, columns, width), jnp.bfloat16)
     chunk_shape = jax.ShapeDtypeStruct((3, per_device, tokens, width), jnp.bfloat16)
     index = seq_index.reshape(1)
-    *packed, cot_near, cot_far = call(
-        functools.partial(pack_kernel, regions, HEADS, per_device),
+    *leaving, cot_near, cot_far = call(
+        functools.partial(pack_kernel, regions, per_device),
         "pack",
-        [chunk_shape] * seq_count + [edge_shape] * 2,
+        [chunk_shape] * (seq_count - 1) + [edge_shape] * 2,
         [SMEM()] + [HBM()] * 4,
-        out_specs=[HBM()] * (seq_count + 2),
+        out_specs=[HBM()] * (seq_count + 1),
         scratch=[
             pltpu.VMEM((3,) + query_rows.shape, jnp.bfloat16),
-            pltpu.VMEM((seq_count,) + chunk_shape.shape, jnp.bfloat16),
+            pltpu.VMEM((seq_count - 1,) + chunk_shape.shape, jnp.bfloat16),
             pltpu.VMEM((2,) + edge_shape.shape, jnp.bfloat16),
-            pltpu.SemaphoreType.DMA((7 + 3 * seq_count,)),
+            pltpu.SemaphoreType.DMA((7 + 3 * (seq_count - 1),)),
         ],
         moved=6 * local_bytes,
         grant=VMEM_WHOLE,
     )(index, query_rows, key_rows, value_rows, cotangent)
-    half = seq_count // 2
-    order = list(range(half, seq_count)) + list(range(1, half)) + [0]
-    for distance in order[:-1]:
-        packed[distance] = trade(packed[distance], distance)
+    order = list(range(1, seq_count)) + [0]
+    packed = [trade(chunk, distance) for distance, chunk in zip(order, leaving)]
+    own = call(
+        functools.partial(own_kernel, regions, per_device),
+        "own_chunk",
+        chunk_shape,
+        [SMEM()] + [HBM()] * 3,
+        scratch=[
+            pltpu.VMEM((3, tokens, regions, max(1, per_device // regions) * width), jnp.bfloat16),
+            pltpu.SemaphoreType.DMA((3,)),
+        ],
+        moved=12 * chunk_shape.size,
+    )(index, query_rows, key_rows, value_rows)
     cot_near = trade(cot_near, 1)
     cot_far = lax.ppermute(cot_far, "seq", far_pairs)
 
@@ -399,18 +438,13 @@
     mixed = call(
         functools.partial(attend_kernel, block_rows, group, order),
         "attend",
-        jax.ShapeDtypeStruct((seq_count, per_device, tokens, width), jnp.bfloat16),
+        [jax.ShapeDtypeStruct((per_device, tokens, width), jnp.bfloat16)] * seq_count,
         [SMEM(), SMEM()] + [VMEM()] * seq_count,
-        out_specs=HBM(),
-        scratch=[
-            pltpu.VMEM((seq_count, per_device, tokens, width), jnp.bfloat16),
-            pltpu.SemaphoreType.DMA((per_device * -(-capacity // block_rows),)),
-        ],
         flops=4 * per_device * capacity * capacity * width,
         moved=4 * local_bytes,
         exps=per_device * capacity * capacity,
-    )(index, item_lengths, *[packed[distance] for distance in order])
-    attended = swap(mixed, "seq").reshape(HEADS, regions, tokens, width)
+    )(index, item_lengths, *packed, own)
+    attended = [mixed[0]] + [trade(mixed[distance], distance) for distance in order[:-1]]
 
     chunk_rows = -(-9 * width // plane_size)
     pixel_rows = regions * PATCH * columns
@@ -424,8 +458,9 @@
             edge_shape,
             jax.ShapeDtypeStruct((plane_size, chunk_rows, width), jnp.bfloat16),
         ],
-        [SMEM(), SMEM()] + [VMEM()] * 5,
+        [SMEM(), SMEM()] + [VMEM()] * (4 + seq_count),
         scratch=[
+            pltpu.VMEM((seq_count,) + mixed[0].shape, jnp.bfloat16),
             pltpu.VMEM((regions, PATCH, columns + 2 * RIM, width), jnp.float32),
             pltpu.VMEM((pixel_rows, 3 * width), jnp.bfloat16),
             pltpu.VMEM((pixel_rows, 3 * width), jnp.bfloat16),
@@ -436,11 +471,11 @@
     )(
         region_lengths,
         index,
-        attended,
         norm_gain.reshape(HEADS, width),
         cotangent,
         cot_near,
         cot_far,
+        *attended,
     )
     grad_parts = swap(grad_parts, ("dp", "seq"), planes)
     near = trade(near, 1)

time: 106 us -> 99.5 us (0.939)
  waiting for transfers between devices: 53.9 us -> 34.8 us
  starting transfers between devices: 35 us -> 49.7 us
  local copies, waits for them, and re-layouts: 1.59 us -> 0.03 us
    ppermute x12 -> x19, starting transfers between devices: 19.3 us -> 41.2 us  [trade(): return lax.ppermute(values, 'seq', pairs)]
    ppermute x12 -> x19, waiting for transfers between devices: 39.6 us -> 26.2 us  [trade(): return lax.ppermute(values, 'seq', pairs)]
    all_to_all x3 -> x2, starting transfers between devices: 14.4 us -> 7.14 us  [swap(): lax.all_to_all(parts, axes, split_axis=0, concat_axis=0, axis_index_group...]
    all_to_all x3 -> x2, waiting for transfers between devices: 14.3 us -> 8.63 us  [swap(): lax.all_to_all(parts, axes, split_axis=0, concat_axis=0, axis_index_group...]
    unnamed x14, local copies, waits for them, and re-layouts: 1.59 us -> 0.03 us
    pallas_call x1 -> x2, Pallas kernels: 4.08 us -> 4.21 us  [the longest x1 3.81 us: body(): call(functools.partial(pack_kernel, regions, per_device), 'pack', [chunk_...]
  transfers between devices with their start and end apart: 17 -> 23, of which waited for: 11 -> 11; matrix products, arithmetic and copies ran while one was open for 0% -> 0% of each run, Pallas kernels for 2% -> 5%
where the time goes in v6:
time: 99.5 us; the launch traced here: 99.2 us
  starting transfers between devices  49.7 us (50%)
  waiting for transfers between devices  34.8 us (35%)
  Pallas kernels  13.8 us (14%)
    ppermute x19, starting transfers between devices, trade(): return lax.ppermute(values, 'seq', pairs)  41.2 us
    ppermute x19, waiting for transfers between devices, trade(): return lax.ppermute(values, 'seq', pairs)  26.2 us
    all_to_all x2, waiting for transfers between devices, swap(): lax.all_to_all(parts, axes, split_axis=0, concat_axis=0, axis_index_group...  8.63 us
    all_to_all x2, starting transfers between devices, swap(): lax.all_to_all(parts, axes, split_axis=0, concat_axis=0, axis_index_group...  7.14 us
    pallas_call x1, Pallas kernels, body(): call(functools.partial(pack_kernel, regions, per_device), 'pack', [chunk_...  3.81 us
    pallas_call x1, Pallas kernels, body(): call(functools.partial(norm_kernel, chunk_rows), 'norm_and_gradient', [ja...  3.67 us
    pallas_call x1, Pallas kernels, body(): call(decode_kernel, 'decode', jax.ShapeDtypeStruct(cotangent.shape, jnp.b...  2.21 us
    pallas_call x1, Pallas kernels, body(): call(functools.partial(attend_kernel, block_rows, group, order), 'attend'...  2.08 us
  transfers between devices with their start and end apart: 23, of which 11 were waited for; matrix products, arithmetic and copies ran while one was open for 0% of the time, Pallas kernels for 5%

profile of v6, /device:TPU:0, one launch (start us, length us, event | category | flops | bytes accessed | tf_op | source)
XLA Modules:
  0.0 99.2 jit_solution(10528262849642065767)
XLA Ops:
  0.6 0.0 copy-start
  0.6 0.0 copy-start.1
  0.7 0.0 copy-start.2
  0.7 3.8 %pack.1 = (bf16[3,4,64,128]{3,2,1,0:T(8,128)(2,1)}, bf16[3,4,64,128]{3,2,1,0:T(8,128)(2,1)}, bf16[3,4,64,128]{3,2,1,0:T(8,128)(2,1)}, bf16[3,4,64,128]{3,2,1,0:T...) custom-call(s32[1]{0:T(128)} %bitcast.index_ref, ...), custom_call_target="tpu_custom_call" | custom-call | bytes 3145728 | tf_op jit(solution)/shard_map/pack/pallas_call | solution.py:396
  4.5 3.0 %collective-permute-start.2 = (bf16[3,4,64,128]{3,2,1,0:T(8,128)(2,1)}, bf16[3,4,64,128]{3,2,1,0:T(8,128)(2,1)S(1)}, u32[]{:S(2)}, u32[]{:S(2)}) collective-permute-start(bf16[3,4,64,128]{3,2,1,0:T(8,128)(2,1)} %get-tuple-element.25), channel_id=1, source_target_pairs={{0,1},{1,0},{2,3},{3,2},{4,5},{5,4},{6,7},{7,6},{8,9},{9,8},{10,11... | collective-permute-start | bytes 589832 | tf_op jit(solution)/shard_map/ppermute | solution.py:365
  7.5 1.6 %collective-permute-start.3 = (bf16[3,4,64,128]{3,2,1,0:T(8,128)(2,1)}, bf16[3,4,64,128]{3,2,1,0:T(8,128)(2,1)S(1)}, u32[]{:S(2)}, u32[]{:S(2)}) collective-permute-start(bf16[3,4,64,128]{3,2,1,0:T(8,128)(2,1)} %get-tuple-element.26), channel_id=1, source_target_pairs={{0,2},{1,3},{2,0},{3,1},{4,6},{5,7},{6,4},{7,5},{8,10},{9,11},{10,... | collective-permute-start | bytes 589832 | tf_op jit(solution)/shard_map/ppermute | solution.py:365
  9.1 0.0 collective-permute-start.4
  9.1 3.0 %collective-permute-start.5 = (bf16[3,4,64,128]{3,2,1,0:T(8,128)(2,1)}, bf16[3,4,64,128]{3,2,1,0:T(8,128)(2,1)S(1)}, u32[]{:S(2)}, u32[]{:S(2)}) collective-permute-start(bf16[3,4,64,128]{3,2,1,0:T(8,128)(2,1)} %get-tuple-element.28), channel_id=1, source_target_pairs={{0,4},{1,5},{2,6},{3,7},{4,0},{5,1},{6,2},{7,3},{8,12},{9,13},{10,... | collective-permute-start | bytes 589832 | tf_op jit(solution)/shard_map/ppermute | solution.py:365
  12.1 1.3 %collective-permute-start.6 = (bf16[3,4,64,128]{3,2,1,0:T(8,128)(2,1)}, bf16[3,4,64,128]{3,2,1,0:T(8,128)(2,1)S(1)}, u32[]{:S(2)}, u32[]{:S(2)}) collective-permute-start(bf16[3,4,64,128]{3,2,1,0:T(8,128)(2,1)} %get-tuple-element.29), channel_id=1, source_target_pairs={{0,5},{1,4},{2,7},{3,6},{4,1},{5,0},{6,3},{7,2},{8,13},{9,12},{10,... | collective-permute-start | bytes 589832 | tf_op jit(solution)/shard_map/ppermute | solution.py:365
  13.3 0.0 collective-permute-done.2.refs_0_
  13.3 3.6 %collective-permute-start.7 = (bf16[3,4,64,128]{3,2,1,0:T(8,128)(2,1)}, bf16[3,4,64,128]{3,2,1,0:T(8,128)(2,1)S(1)}, u32[]{:S(2)}, u32[]{:S(2)}) collective-permute-start(bf16[3,4,64,128]{3,2,1,0:T(8,128)(2,1)} %get-tuple-element.30), channel_id=1, source_target_pairs={{0,6},{1,7},{2,4},{3,5},{4,2},{5,3},{6,0},{7,1},{8,14},{9,15},{10,... | collective-permute-start | bytes 589832 | tf_op jit(solution)/shard_map/ppermute | solution.py:365
  16.9 6.2 %collective-permute-done.3.refs_1_ = bf16[3,4,64,128]{3,2,1,0:T(8,128)(2,1)S(1)} collective-permute-done((bf16[3,4,64,128]{3,2,1,0:T(8,128)(2,1)}, bf16[3,4,64,128]{3,2,1,0:T(8,128)(2,1)S(1)}, u32[]{:S(2)}, u32[]{:S(2)}) %collective-permute-start.3) | collective-permute-done | bytes 196640 | tf_op jit(solution)/shard_map/ppermute | solution.py:365
  23.2 0.9 collective-permute-start.8
  24.1 0.8 collective-permute-done.4.refs_2_
  24.9 2.5 %collective-permute-start = (bf16[2,256,128]{2,1,0:T(8,128)(2,1)}, bf16[2,256,128]{2,1,0:T(8,128)(2,1)S(1)}, u32[]{:S(2)}, u32[]{:S(2)}) collective-permute-start(bf16[2,256,128]{2,1,0:T(8,128)(2,1)} %get-tuple-element.23), channel_id=1, source_target_pairs={{0,1},{1,0},{2,3},{3,2},{4,5},{5,4},{6,7},{7,6},{8,9},{9,8},{10,11... | collective-permute-start | bytes 393224 | tf_op jit(solution)/shard_map/ppermute | solution.py:365
  27.4 0.0 collective-permute-done.5.refs_3_
  27.4 0.7 collective-permute-start.1
  28.1 0.0 copy-done.6
  28.1 0.1 fusion.lengths_ref
  28.2 0.0 copy-done.1
  28.2 0.0 copy-done.2
  28.2 0.4 own_chunk.1.refs_7_
  28.6 0.0 copy-start.3
  28.6 11.8 %collective-permute-done.6.refs_4_ = bf16[3,4,64,128]{3,2,1,0:T(8,128)(2,1)S(1)} collective-permute-done((bf16[3,4,64,128]{3,2,1,0:T(8,128)(2,1)}, bf16[3,4,64,128]{3,2,1,0:T(8,128)(2,1)S(1)}, u32[]{:S(2)}, u32[]{:S(2)}) %collective-permute-start.6) | collective-permute-done | bytes 196640 | tf_op jit(solution)/shard_map/ppermute | solution.py:365
  40.4 0.0 collective-permute-done.7.refs_5_
  40.4 0.0 collective-permute-done.8.refs_6_
  40.4 2.1 %attend.1 = (bf16[4,64,128]{2,1,0:T(8,128)(2,1)S(1)}, bf16[4,64,128]{2,1,0:T(8,128)(2,1)S(1)}, bf16[4,64,128]{2,1,0:T(8,128)(2,1)S(1)}, bf16[4,64,128]{2,1,0:T(8...) custom-call(s32[1]{0:T(128)} %bitcast.index_ref, ...), custom_call_target="tpu_custom_call" | custom-call | flops 536870912 | bytes 2097152 | tf_op jit(solution)/shard_map/attend/pallas_call | solution.py:438
  42.5 0.0 copy-start.5
  42.5 0.1 collective-permute-start.9
  42.6 9.3 %collective-permute-start.10 = (bf16[4,64,128]{2,1,0:T(8,128)(2,1)S(1)}, bf16[4,64,128]{2,1,0:T(8,128)(2,1)S(1)}, u32[]{:S(2)}, u32[]{:S(2)}) collective-permute-start(bf16[4,64,128]{2,1,0:T(8,128)(2,1)S(1)} %get-tuple-element.34), channel_id=1, source_target_pairs={{0,2},{1,3},{2,0},{3,1},{4,6},{5,7},{6,4},{7,5},{8,10},{9,11},{10,... | collective-permute-start | bytes 196616 | tf_op jit(solution)/shard_map/ppermute | solution.py:365
  51.9 0.0 collective-permute-start.11
  51.9 0.0 collective-permute-done.cot_near_ref
  51.9 4.7 %collective-permute-start.12 = (bf16[4,64,128]{2,1,0:T(8,128)(2,1)S(1)}, bf16[4,64,128]{2,1,0:T(8,128)(2,1)S(1)}, u32[]{:S(2)}, u32[]{:S(2)}) collective-permute-start(bf16[4,64,128]{2,1,0:T(8,128)(2,1)S(1)} %get-tuple-element.36), channel_id=1, source_target_pairs={{0,4},{1,5},{2,6},{3,7},{4,0},{5,1},{6,2},{7,3},{8,12},{9,13},{10,... | collective-permute-start | bytes 196616 | tf_op jit(solution)/shard_map/ppermute | solution.py:365
  56.7 0.0 collective-permute-done.1.cot_far_ref
  56.7 0.0 collective-permute-start.13
  56.7 0.0 collective-permute-done.9.refs_1_
  56.7 2.4 %collective-permute-start.14 = (bf16[4,64,128]{2,1,0:T(8,128)(2,1)S(1)}, bf16[4,64,128]{2,1,0:T(8,128)(2,1)S(1)}, u32[]{:S(2)}, u32[]{:S(2)}) collective-permute-start(bf16[4,64,128]{2,1,0:T(8,128)(2,1)S(1)} %get-tuple-element.38), channel_id=1, source_target_pairs={{0,6},{1,7},{2,4},{3,5},{4,2},{5,3},{6,0},{7,1},{8,14},{9,15},{10,... | collective-permute-start | bytes 196616 | tf_op jit(solution)/shard_map/ppermute | solution.py:365
  59.0 0.0 collective-permute-done.10.refs_2_
  59.0 2.4 %collective-permute-start.15 = (bf16[4,64,128]{2,1,0:T(8,128)(2,1)S(1)}, bf16[4,64,128]{2,1,0:T(8,128)(2,1)S(1)}, u32[]{:S(2)}, u32[]{:S(2)}) collective-permute-start(bf16[4,64,128]{2,1,0:T(8,128)(2,1)S(1)} %get-tuple-element.39), channel_id=1, source_target_pairs={{0,7},{1,6},{2,5},{3,4},{4,3},{5,2},{6,1},{7,0},{8,15},{9,14},{10,... | collective-permute-start | bytes 196616 | tf_op jit(solution)/shard_map/ppermute | solution.py:365
  61.5 0.0 collective-permute-done.11.refs_3_
  61.5 0.4 collective-permute-done.12.refs_4_
  61.9 2.5 %collective-permute-done.13.refs_5_ = bf16[4,64,128]{2,1,0:T(8,128)(2,1)S(1)} collective-permute-done((bf16[4,64,128]{2,1,0:T(8,128)(2,1)S(1)}, bf16[4,64,128]{2,1,0:T(8,128)(2,1)S(1)}, u32[]{:S(2)}, u32[]{:S(2)}) %collective-permute-start.13) | collective-permute-done | bytes 65568 | tf_op jit(solution)/shard_map/ppermute | solution.py:365
  64.4 0.0 collective-permute-done.14.refs_6_
  64.4 1.7 %collective-permute-done.15.refs_7_ = bf16[4,64,128]{2,1,0:T(8,128)(2,1)S(1)} collective-permute-done((bf16[4,64,128]{2,1,0:T(8,128)(2,1)S(1)}, bf16[4,64,128]{2,1,0:T(8,128)(2,1)S(1)}, u32[]{:S(2)}, u32[]{:S(2)}) %collective-permute-start.15) | collective-permute-done | bytes 65568 | tf_op jit(solution)/shard_map/ppermute | solution.py:365
  66.1 0.0 copy-done.5
  66.1 3.7 %norm_and_gradient.1 = (bf16[2,4,256,128]{3,2,1,0:T(8,128)(2,1)S(1)}, bf16[2,256,128]{2,1,0:T(8,128)(2,1)S(1)}, bf16[2,256,128]{2,1,0:T(8,128)(2,1)S(1)}, bf16[8,144,128]{2,1,0:T(8,128)(2,1)}) custom-call(s32[2]{0:T(128)S(1)} %copy-done.6, s32[1]{0:T(128)} %bitcast.index_ref, f32[16,128]{1,0:T(8,128)S(1)} %bitcast.5, bf16[2,4,256,128]{3,2,1,0:T(8,128)(2,1)S(1)} %copy-done.3, ...), custom_call_target="tpu_custom_call" | custom-call | flops 603979776 | bytes 2097152 | tf_op jit(solution)/shard_map/norm_and_gradient/pallas_call | solution.py:452
  69.8 3.6 %all-to-all-start = ((bf16[8,144,128]{2,1,0:T(8,128)(2,1)}), bf16[8,144,128]{2,1,0:T(8,128)(2,1)S(1)}, u32[]{:S(2)}, u32[]{:S(2)}) async-start(bf16[8,144,128]{2,1,0:T(8,128)(2,1)} %get-tuple-element.43), calls=%async_computation | async-start | bytes 589824 | tf_op jit(solution)/shard_map/all_to_all | solution.py:358
  73.4 2.0 %collective-permute-start.16 = (bf16[2,256,128]{2,1,0:T(8,128)(2,1)S(1)}, bf16[2,256,128]{2,1,0:T(8,128)(2,1)S(1)}, u32[]{:S(2)}, u32[]{:S(2)}) collective-permute-start(bf16[2,256,128]{2,1,0:T(8,128)(2,1)S(1)} %get-tuple-element.41), channel_id=1, source_target_pairs={{0,1},{1,0},{2,3},{3,2},{4,5},{5,4},{6,7},{7,6},{8,9},{9,8},{10,11... | collective-permute-start | bytes 393224 | tf_op jit(solution)/shard_map/ppermute | solution.py:365
  75.4 0.7 collective-permute-start.17
  76.1 4.1 %all-to-all-done.refs_0_ = bf16[8,144,128]{2,1,0:T(8,128)(2,1)S(1)} async-done(((bf16[8,144,128]{2,1,0:T(8,128)(2,1)}), bf16[8,144,128]{2,1,0:T(8,128)(2,1)S(1)}, u32[]{:S(2)}, u32[]{:S(2)}) %all-to-all-start) | async-done | bytes 294944 | tf_op jit(solution)/shard_map/all_to_all | solution.py:358
  80.2 1.7 %collective-permute-start.20 = (bf16[144,128]{1,0:T(8,128)(2,1)S(1)}, bf16[144,128]{1,0:T(8,128)(2,1)S(1)}, u32[]{:S(2)}, u32[]{:S(2)}) collective-permute-start(bf16[144,128]{1,0:T(8,128)(2,1)S(1)} %sum_plane.1.refs_0_), channel_id=1, source_target_pairs={{0,6},{1,7},{2,4},{3,5},{4,2},{5,3},{6,0},{7,1},{8,14},{9,15},{10,... | collective-permute-start | bytes 110600 | tf_op jit(solution)/shard_map/ppermute | solution.py:365
  81.9 0.6 collective-permute-start.19
  82.6 2.1 %collective-permute-start.18 = (bf16[144,128]{1,0:T(8,128)(2,1)S(1)}, bf16[144,128]{1,0:T(8,128)(2,1)S(1)}, u32[]{:S(2)}, u32[]{:S(2)}) collective-permute-start(bf16[144,128]{1,0:T(8,128)(2,1)S(1)} %sum_plane.1.refs_0_), channel_id=1, source_target_pairs={{0,2},{1,3},{2,0},{3,1},{4,6},{5,7},{6,4},{7,5},{8,10},{9,11},{10,... | collective-permute-start | bytes 110600 | tf_op jit(solution)/shard_map/ppermute | solution.py:365
  84.7 0.0 collective-permute-done.16.near_ref.refs_4_
  84.7 0.0 collective-permute-done.17.far_ref.refs_5_
  84.7 1.4 %collective-permute-done.20.refs_3_ = bf16[144,128]{1,0:T(8,128)(2,1)S(1)} collective-permute-done((bf16[144,128]{1,0:T(8,128)(2,1)S(1)}, bf16[144,128]{1,0:T(8,128)(2,1)S(1)}, u32[]{:S(2)}, u32[]{:S(2)}) %collective-permute-start.20) | collective-permute-done | bytes 36896 | tf_op jit(solution)/shard_map/ppermute | solution.py:365
  86.1 1.1 %collective-permute-done.19.refs_2_ = bf16[144,128]{1,0:T(8,128)(2,1)S(1)} collective-permute-done((bf16[144,128]{1,0:T(8,128)(2,1)S(1)}, bf16[144,128]{1,0:T(8,128)(2,1)S(1)}, u32[]{:S(2)}, u32[]{:S(2)}) %collective-permute-start.19) | collective-permute-done | bytes 36896 | tf_op jit(solution)/shard_map/ppermute | solution.py:365
  87.2 0.1 collective-permute-done.18.refs_1_
  87.3 0.7 sum_planes.1
  88.0 3.6 %all-to-all-start.1 = ((bf16[8,144,128]{2,1,0:T(8,128)(2,1)}), bf16[8,144,128]{2,1,0:T(8,128)(2,1)S(1)}, u32[]{:S(2)}, u32[]{:S(2)}) async-start(bf16[8,144,128]{2,1,0:T(8,128)(2,1)} %sum_planes.1), calls=%async_computation.1 | async-start | bytes 589824 | tf_op jit(solution)/shard_map/all_to_all | solution.py:358
  91.6 0.0 copy-done.4
  91.6 2.2 %decode.1 = bf16[2,4,256,128]{3,2,1,0:T(8,128)(2,1)} custom-call(s32[1]{0:T(128)} %bitcast.index_ref, bf16[2,4,256,128]{3,2,1,0:T(8,128)(2,1)S(1)} %get-tuple-element.40.image_ref, bf16[2,256,128]{2,1,0:T(8,128)(2,1)S(1)} %collective-permute-done.16.near_ref.refs_4_, bf16[2,256,128]{2,1,0:T(8,128)(2,1)S(1)} %collective-permute-done.17.far_ref.refs_5_, ...), custom_call_target="tpu_custom_call" | custom-call | flops 603979776 | bytes 1048576 | tf_op jit(solution)/shard_map/decode/pallas_call | solution.py:499
  93.8 4.5 %all-to-all-done.1.parts_ref = bf16[8,144,128]{2,1,0:T(8,128)(2,1)S(1)} async-done(((bf16[8,144,128]{2,1,0:T(8,128)(2,1)}), bf16[8,144,128]{2,1,0:T(8,128)(2,1)S(1)}, u32[]{:S(2)}, u32[]{:S(2)}) %all-to-all-start.1) | async-done | bytes 294944 | tf_op jit(solution)/shard_map/all_to_all | solution.py:358
  98.3 0.9 spread_sums.1
  (6 shorter events, 0.1 us)
Async XLA Ops:
  0.6 27.5 %copy-start = (bf16[64,2,2048]{2,1,0:T(2,128)(2,1)S(1)}, bf16[64,2,2048]{2,1,0:T(2,128)(2,1)}, u32[]{:S(2)}) copy-start(bf16[64,2,2048]{2,1,0:T(2,128)(2,1)} %query_ref.3) | copy-start | bytes 1572868
  0.6 27.5 %copy-start.1 = (bf16[64,2,2048]{2,1,0:T(2,128)(2,1)S(1)}, bf16[64,2,2048]{2,1,0:T(2,128)(2,1)}, u32[]{:S(2)}) copy-start(bf16[64,2,2048]{2,1,0:T(2,128)(2,1)} %key_ref.3) | copy-start | bytes 1572868
  0.7 27.5 %copy-start.2 = (bf16[64,2,2048]{2,1,0:T(2,128)(2,1)S(1)}, bf16[64,2,2048]{2,1,0:T(2,128)(2,1)}, u32[]{:S(2)}) copy-start(bf16[64,2,2048]{2,1,0:T(2,128)(2,1)} %value_ref.3) | copy-start | bytes 1572868
  4.5 8.9 %collective-permute-start.2 = (bf16[3,4,64,128]{3,2,1,0:T(8,128)(2,1)}, bf16[3,4,64,128]{3,2,1,0:T(8,128)(2,1)S(1)}, u32[]{:S(2)}, u32[]{:S(2)}) collective-permute-start(bf16[3,4,64,128]{3,2,1,0:T(8,128)(2,1)} %get-tuple-element.25), channel_id=1, source_target_pairs={{0,1},{1,0},{2,3},{3,2},{4,5},{5,4},{6,7},{7,6},{8,9},{9,8},{10,11... | collective-permute-start | bytes 589832 | tf_op jit(solution)/shard_map/ppermute | solution.py:365
  7.5 15.7 %collective-permute-start.3 = (bf16[3,4,64,128]{3,2,1,0:T(8,128)(2,1)}, bf16[3,4,64,128]{3,2,1,0:T(8,128)(2,1)S(1)}, u32[]{:S(2)}, u32[]{:S(2)}) collective-permute-start(bf16[3,4,64,128]{3,2,1,0:T(8,128)(2,1)} %get-tuple-element.26), channel_id=1, source_target_pairs={{0,2},{1,3},{2,0},{3,1},{4,6},{5,7},{6,4},{7,5},{8,10},{9,11},{10,... | collective-permute-start | bytes 589832 | tf_op jit(solution)/shard_map/ppermute | solution.py:365
  9.1 15.8 %collective-permute-start.4 = (bf16[3,4,64,128]{3,2,1,0:T(8,128)(2,1)}, bf16[3,4,64,128]{3,2,1,0:T(8,128)(2,1)S(1)}, u32[]{:S(2)}, u32[]{:S(2)}) collective-permute-start(bf16[3,4,64,128]{3,2,1,0:T(8,128)(2,1)} %get-tuple-element.27), channel_id=1, source_target_pairs={{0,3},{1,2},{2,1},{3,0},{4,7},{5,6},{6,5},{7,4},{8,11},{9,10},{10,... | collective-permute-start | bytes 589832 | tf_op jit(solution)/shard_map/ppermute | solution.py:365
  9.1 18.3 %collective-permute-start.5 = (bf16[3,4,64,128]{3,2,1,0:T(8,128)(2,1)}, bf16[3,4,64,128]{3,2,1,0:T(8,128)(2,1)S(1)}, u32[]{:S(2)}, u32[]{:S(2)}) collective-permute-start(bf16[3,4,64,128]{3,2,1,0:T(8,128)(2,1)} %get-tuple-element.28), channel_id=1, source_target_pairs={{0,4},{1,5},{2,6},{3,7},{4,0},{5,1},{6,2},{7,3},{8,12},{9,13},{10,... | collective-permute-start | bytes 589832 | tf_op jit(solution)/shard_map/ppermute | solution.py:365
  12.1 28.3 %collective-permute-start.6 = (bf16[3,4,64,128]{3,2,1,0:T(8,128)(2,1)}, bf16[3,4,64,128]{3,2,1,0:T(8,128)(2,1)S(1)}, u32[]{:S(2)}, u32[]{:S(2)}) collective-permute-start(bf16[3,4,64,128]{3,2,1,0:T(8,128)(2,1)} %get-tuple-element.29), channel_id=1, source_target_pairs={{0,5},{1,4},{2,7},{3,6},{4,1},{5,0},{6,3},{7,2},{8,13},{9,12},{10,... | collective-permute-start | bytes 589832 | tf_op jit(solution)/shard_map/ppermute | solution.py:365
  13.3 27.1 %collective-permute-start.7 = (bf16[3,4,64,128]{3,2,1,0:T(8,128)(2,1)}, bf16[3,4,64,128]{3,2,1,0:T(8,128)(2,1)S(1)}, u32[]{:S(2)}, u32[]{:S(2)}) collective-permute-start(bf16[3,4,64,128]{3,2,1,0:T(8,128)(2,1)} %get-tuple-element.30), channel_id=1, source_target_pairs={{0,6},{1,7},{2,4},{3,5},{4,2},{5,3},{6,0},{7,1},{8,14},{9,15},{10,... | collective-permute-start | bytes 589832 | tf_op jit(solution)/shard_map/ppermute | solution.py:365
  23.2 17.2 %collective-permute-start.8 = (bf16[3,4,64,128]{3,2,1,0:T(8,128)(2,1)}, bf16[3,4,64,128]{3,2,1,0:T(8,128)(2,1)S(1)}, u32[]{:S(2)}, u32[]{:S(2)}) collective-permute-start(bf16[3,4,64,128]{3,2,1,0:T(8,128)(2,1)} %get-tuple-element.31), channel_id=1, source_target_pairs={{0,7},{1,6},{2,5},{3,4},{4,3},{5,2},{6,1},{7,0},{8,15},{9,14},{10,... | collective-permute-start | bytes 589832 | tf_op jit(solution)/shard_map/ppermute | solution.py:365
  24.9 3.1 %copy-start.6 = (s32[2]{0:T(128)S(1)}, s32[2]{0:T(128)}, u32[]{:S(2)}) copy-start(s32[2]{0:T(128)} %lengths_ref.1) | copy-start | bytes 28
  24.9 27.0 %collective-permute-start = (bf16[2,256,128]{2,1,0:T(8,128)(2,1)}, bf16[2,256,128]{2,1,0:T(8,128)(2,1)S(1)}, u32[]{:S(2)}, u32[]{:S(2)}) collective-permute-start(bf16[2,256,128]{2,1,0:T(8,128)(2,1)} %get-tuple-element.23), channel_id=1, source_target_pairs={{0,1},{1,0},{2,3},{3,2},{4,5},{5,4},{6,7},{7,6},{8,9},{9,8},{10,11... | collective-permute-start | bytes 393224 | tf_op jit(solution)/shard_map/ppermute | solution.py:365
  27.4 29.3 %collective-permute-start.1 = (bf16[2,256,128]{2,1,0:T(8,128)(2,1)}, bf16[2,256,128]{2,1,0:T(8,128)(2,1)S(1)}, u32[]{:S(2)}, u32[]{:S(2)}) collective-permute-start(bf16[2,256,128]{2,1,0:T(8,128)(2,1)} %get-tuple-element.24), channel_id=1, source_target_pairs={{1,2},{3,4},{5,6},{2,1},{4,3},{6,5},{9,10},{11,12},{13,14},{10,9},... | collective-permute-start | bytes 393224 | tf_op jit(solution)/shard_map/ppermute | solution.py:425
  28.6 37.5 %copy-start.3 = (bf16[2,4,256,128]{3,2,1,0:T(8,128)(2,1)S(1)}, bf16[2,4,256,128]{3,2,1,0:T(8,128)(2,1)}, u32[]{:S(2)}) copy-start(bf16[2,4,256,128]{3,2,1,0:T(8,128)(2,1)} %cot_ref.3) | copy-start | bytes 1572868
  42.5 23.6 %copy-start.5 = (f32[2048]{0:T(1024)S(1)}, f32[2048]{0:T(1024)}, u32[]{:S(2)}) copy-start(f32[2048]{0:T(1024)} %param.11) | copy-start | bytes 24580
  42.5 14.2 %collective-permute-start.9 = (bf16[4,64,128]{2,1,0:T(8,128)(2,1)S(1)}, bf16[4,64,128]{2,1,0:T(8,128)(2,1)S(1)}, u32[]{:S(2)}, u32[]{:S(2)}) collective-permute-start(bf16[4,64,128]{2,1,0:T(8,128)(2,1)S(1)} %get-tuple-element.33), channel_id=1, source_target_pairs={{0,1},{1,0},{2,3},{3,2},{4,5},{5,4},{6,7},{7,6},{8,9},{9,8},{10,11... | collective-permute-start | bytes 196616 | tf_op jit(solution)/shard_map/ppermute | solution.py:365
  42.6 16.5 %collective-permute-start.10 = (bf16[4,64,128]{2,1,0:T(8,128)(2,1)S(1)}, bf16[4,64,128]{2,1,0:T(8,128)(2,1)S(1)}, u32[]{:S(2)}, u32[]{:S(2)}) collective-permute-start(bf16[4,64,128]{2,1,0:T(8,128)(2,1)S(1)} %get-tuple-element.34), channel_id=1, source_target_pairs={{0,2},{1,3},{2,0},{3,1},{4,6},{5,7},{6,4},{7,5},{8,10},{9,11},{10,... | collective-permute-start | bytes 196616 | tf_op jit(solution)/shard_map/ppermute | solution.py:365
  51.9 9.5 %collective-permute-start.11 = (bf16[4,64,128]{2,1,0:T(8,128)(2,1)S(1)}, bf16[4,64,128]{2,1,0:T(8,128)(2,1)S(1)}, u32[]{:S(2)}, u32[]{:S(2)}) collective-permute-start(bf16[4,64,128]{2,1,0:T(8,128)(2,1)S(1)} %get-tuple-element.35), channel_id=1, source_target_pairs={{0,3},{1,2},{2,1},{3,0},{4,7},{5,6},{6,5},{7,4},{8,11},{9,10},{10,... | collective-permute-start | bytes 196616 | tf_op jit(solution)/shard_map/ppermute | solution.py:365
  51.9 9.9 %collective-permute-start.12 = (bf16[4,64,128]{2,1,0:T(8,128)(2,1)S(1)}, bf16[4,64,128]{2,1,0:T(8,128)(2,1)S(1)}, u32[]{:S(2)}, u32[]{:S(2)}) collective-permute-start(bf16[4,64,128]{2,1,0:T(8,128)(2,1)S(1)} %get-tuple-element.36), channel_id=1, source_target_pairs={{0,4},{1,5},{2,6},{3,7},{4,0},{5,1},{6,2},{7,3},{8,12},{9,13},{10,... | collective-permute-start | bytes 196616 | tf_op jit(solution)/shard_map/ppermute | solution.py:365
  56.7 7.7 %collective-permute-start.13 = (bf16[4,64,128]{2,1,0:T(8,128)(2,1)S(1)}, bf16[4,64,128]{2,1,0:T(8,128)(2,1)S(1)}, u32[]{:S(2)}, u32[]{:S(2)}) collective-permute-start(bf16[4,64,128]{2,1,0:T(8,128)(2,1)S(1)} %get-tuple-element.37), channel_id=1, source_target_pairs={{0,5},{1,4},{2,7},{3,6},{4,1},{5,0},{6,3},{7,2},{8,13},{9,12},{10,... | collective-permute-start | bytes 196616 | tf_op jit(solution)/shard_map/ppermute | solution.py:365
  56.7 7.7 %collective-permute-start.14 = (bf16[4,64,128]{2,1,0:T(8,128)(2,1)S(1)}, bf16[4,64,128]{2,1,0:T(8,128)(2,1)S(1)}, u32[]{:S(2)}, u32[]{:S(2)}) collective-permute-start(bf16[4,64,128]{2,1,0:T(8,128)(2,1)S(1)} %get-tuple-element.38), channel_id=1, source_target_pairs={{0,6},{1,7},{2,4},{3,5},{4,2},{5,3},{6,0},{7,1},{8,14},{9,15},{10,... | collective-permute-start | bytes 196616 | tf_op jit(solution)/shard_map/ppermute | solution.py:365
  59.0 7.1 %collective-permute-start.15 = (bf16[4,64,128]{2,1,0:T(8,128)(2,1)S(1)}, bf16[4,64,128]{2,1,0:T(8,128)(2,1)S(1)}, u32[]{:S(2)}, u32[]{:S(2)}) collective-permute-start(bf16[4,64,128]{2,1,0:T(8,128)(2,1)S(1)} %get-tuple-element.39), channel_id=1, source_target_pairs={{0,7},{1,6},{2,5},{3,4},{4,3},{5,2},{6,1},{7,0},{8,15},{9,14},{10,... | collective-permute-start | bytes 196616 | tf_op jit(solution)/shard_map/ppermute | solution.py:365
  69.8 10.4 %all-to-all-start = ((bf16[8,144,128]{2,1,0:T(8,128)(2,1)}), bf16[8,144,128]{2,1,0:T(8,128)(2,1)S(1)}, u32[]{:S(2)}, u32[]{:S(2)}) async-start(bf16[8,144,128]{2,1,0:T(8,128)(2,1)} %get-tuple-element.43), calls=%async_computation | async-start | bytes 589824 | tf_op jit(solution)/shard_map/all_to_all | solution.py:358
  73.4 11.3 %collective-permute-start.16 = (bf16[2,256,128]{2,1,0:T(8,128)(2,1)S(1)}, bf16[2,256,128]{2,1,0:T(8,128)(2,1)S(1)}, u32[]{:S(2)}, u32[]{:S(2)}) collective-permute-start(bf16[2,256,128]{2,1,0:T(8,128)(2,1)S(1)} %get-tuple-element.41), channel_id=1, source_target_pairs={{0,1},{1,0},{2,3},{3,2},{4,5},{5,4},{6,7},{7,6},{8,9},{9,8},{10,11... | collective-permute-start | bytes 393224 | tf_op jit(solution)/shard_map/ppermute | solution.py:365
  75.4 9.3 %collective-permute-start.17 = (bf16[2,256,128]{2,1,0:T(8,128)(2,1)S(1)}, bf16[2,256,128]{2,1,0:T(8,128)(2,1)S(1)}, u32[]{:S(2)}, u32[]{:S(2)}) collective-permute-start(bf16[2,256,128]{2,1,0:T(8,128)(2,1)S(1)} %get-tuple-element.42), channel_id=1, source_target_pairs={{1,2},{3,4},{5,6},{2,1},{4,3},{6,5},{9,10},{11,12},{13,14},{10,9},... | collective-permute-start | bytes 393224 | tf_op jit(solution)/shard_map/ppermute | solution.py:482
  80.2 5.9 %collective-permute-start.20 = (bf16[144,128]{1,0:T(8,128)(2,1)S(1)}, bf16[144,128]{1,0:T(8,128)(2,1)S(1)}, u32[]{:S(2)}, u32[]{:S(2)}) collective-permute-start(bf16[144,128]{1,0:T(8,128)(2,1)S(1)} %sum_plane.1.refs_0_), channel_id=1, source_target_pairs={{0,6},{1,7},{2,4},{3,5},{4,2},{5,3},{6,0},{7,1},{8,14},{9,15},{10,... | collective-permute-start | bytes 110600 | tf_op jit(solution)/shard_map/ppermute | solution.py:365
  81.9 5.3 %collective-permute-start.19 = (bf16[144,128]{1,0:T(8,128)(2,1)S(1)}, bf16[144,128]{1,0:T(8,128)(2,1)S(1)}, u32[]{:S(2)}, u32[]{:S(2)}) collective-permute-start(bf16[144,128]{1,0:T(8,128)(2,1)S(1)} %sum_plane.1.refs_0_), channel_id=1, source_target_pairs={{0,4},{1,5},{2,6},{3,7},{4,0},{5,1},{6,2},{7,3},{8,12},{9,13},{10,... | collective-permute-start | bytes 110600 | tf_op jit(solution)/shard_map/ppermute | solution.py:365
  82.6 4.7 %collective-permute-start.18 = (bf16[144,128]{1,0:T(8,128)(2,1)S(1)}, bf16[144,128]{1,0:T(8,128)(2,1)S(1)}, u32[]{:S(2)}, u32[]{:S(2)}) collective-permute-start(bf16[144,128]{1,0:T(8,128)(2,1)S(1)} %sum_plane.1.refs_0_), channel_id=1, source_target_pairs={{0,2},{1,3},{2,0},{3,1},{4,6},{5,7},{6,4},{7,5},{8,10},{9,11},{10,... | collective-permute-start | bytes 110600 | tf_op jit(solution)/shard_map/ppermute | solution.py:365
  88.0 3.6 %copy-start.4 = (bf16[9,128,128]{2,1,0:T(8,128)(2,1)S(1)}, bf16[9,128,128]{2,1,0:T(8,128)(2,1)}, u32[]{:S(2)}) copy-start(bf16[9,128,128]{2,1,0:T(8,128)(2,1)} %param.12) | copy-start | bytes 884740
  88.0 10.3 %all-to-all-start.1 = ((bf16[8,144,128]{2,1,0:T(8,128)(2,1)}), bf16[8,144,128]{2,1,0:T(8,128)(2,1)S(1)}, u32[]{:S(2)}, u32[]{:S(2)}) async-start(bf16[8,144,128]{2,1,0:T(8,128)(2,1)} %sum_planes.1), calls=%async_computation.1 | async-start | bytes 589824 | tf_op jit(solution)/shard_map/all_to_all | solution.py:358

commit v7 on v6

--- a/solution.py
+++ b/solution.py
@@ -219,18 +219,27 @@
     return jnp.where(odd == 1, near, far), jnp.where(odd == 1, far, near)
 
 
-def norm_kernel(
-    chunk_rows,
-    lengths_ref,
-    index_ref,
-    gain_ref,
-    cot_ref,
-    cot_near_ref,
-    cot_far_ref,
-    *refs,
-):
-    image_ref, near_ref, far_ref, grad_ref, attended, pixels, windows, cots, grads = refs[-9:]
-    for distance, ref in enumerate(refs[:-9]):
+def turn_kernel(index_ref, cot_ref, near_ref, far_ref, out_ref):
+    regions, rows, columns, width = cot_ref.shape
+    for region in range(regions):
+        before, after = around(lax.rem(index_ref[0], 2), near_ref[region], far_ref[region])
+        for row in range(-1, rows + 1):
+            value = before if row < 0 else after if row == rows else cot_ref[region, row]
+            turned = value.T
+            for down in range(3):
+                image_row = row - 1 + down
+                if 0 <= image_row < rows:
+                    start = (region * rows + image_row) * columns
+                    out_ref[down * width : (down + 1) * width, start : start + columns] = turned
+
+
+def norm_kernel(chunk_rows, lengths_ref, index_ref, gain_ref, turned_ref, *refs):
+    attended, pixels, windows, grads = refs[-4:]
+    sources = attended.shape[0]
+    chunks = refs[:sources]
+    image_ref, near_ref, far_ref = refs[sources : sources + 3]
+    grad_refs = refs[sources + 3 : -4]
+    for distance, ref in enumerate(chunks):
         attended[lax.bitwise_xor(index_ref[0], distance)] = ref[...]
     heads = gain_ref.shape[0]
     regions = image_ref.shape[0]
@@ -263,39 +272,29 @@
             normed = jnp.where(live, centered * spread * gain_ref[head : head + 1, :], 0.0)
             row, column = divmod(head, PATCH)
             pixels[region, row, pl.ds(RIM + column, tokens, stride=PATCH), :] = normed
-        cot_before, cot_after = around(odd, cot_near_ref[region], cot_far_ref[region])
         for row in range(PATCH):
             window = three_windows(pixels[region, row], columns)
-            middle = window[:, width : 2 * width]
-            image_ref[region, row] = middle
+            image_ref[region, row] = window[:, width : 2 * width]
             start = (region * PATCH + row) * columns
             windows[start : start + columns, :] = window
-            below = cot_ref[region, row + 1] if row < PATCH - 1 else cot_after
-            above = cot_ref[region, row - 1] if row > 0 else cot_before
-            cots[start : start + columns, :] = jnp.concatenate(
-                [below, cot_ref[region, row], above], axis=1
-            )
         near_ref[region] = image_ref[region, (1 - odd) * (PATCH - 1)]
         far_ref[region] = image_ref[region, odd * (PATCH - 1)]
         part = slice(region * PATCH * columns, (region + 1) * PATCH * columns)
-        term = lax.dot_general(
-            windows[part, :],
-            cots[part, :],
-            (((0,), (0,)), ((), ())),
-            preferred_element_type=jnp.float32,
-        )
+        term = jnp.dot(turned_ref[:, part], windows[part, :], preferred_element_type=jnp.float32)
         product = term if region == 0 else product + term
     for down in range(3):
         for across in range(3):
             tap = 3 * down + across
             grads[tap * width : (tap + 1) * width, :] = product[
-                across * width : (across + 1) * width, down * width : (down + 1) * width
-            ]
+                down * width : (down + 1) * width, across * width : (across + 1) * width
+            ].T
     filled = 9 * width
     if filled < grads.shape[0]:
         grads[filled:, :] = jnp.zeros((grads.shape[0] - filled, width), jnp.float32)
-    for chunk in range(grad_ref.shape[0]):
-        grad_ref[chunk] = grads[chunk * chunk_rows : (chunk + 1) * chunk_rows, :].astype(jnp.bfloat16)
+    for distance, ref in enumerate(grad_refs):
+        start = lax.bitwise_xor(index_ref[1], distance) * chunk_rows
+        rows = pl.ds(pl.multiple_of(start, chunk_rows), chunk_rows)
+        ref[...] = grads[rows, :].astype(jnp.bfloat16)
 
 
 def decode_kernel(index_ref, image_ref, near_ref, far_ref, weight_ref, out_ref, padded):
@@ -326,38 +325,20 @@
 
 def sum_kernel(count, factor, *refs):
     out_ref = refs[-1]
-    if count == 1:
-        parts = [refs[0].at[part] for part in range(refs[0].shape[0])]
-    else:
-        parts = refs[:count]
-    totals = [part[...].astype(jnp.float32) for part in parts]
+    totals = [ref[...].astype(jnp.float32) for ref in refs[:count]]
     while len(totals) > 1:
         paired = [one + other for one, other in zip(totals[::2], totals[1::2])]
         totals = paired + totals[2 * len(paired) :]
-    total = totals[0]
-    if factor is not None:
-        total = total * factor
-    total = total.astype(jnp.bfloat16)
-    if out_ref.ndim == 2:
-        out_ref[...] = total
-    else:
-        for part in range(out_ref.shape[0]):
-            out_ref[part] = total
-
-
-def spread_kernel(parts_ref, out_ref):
-    rows = parts_ref.shape[1]
-    for part in range(parts_ref.shape[0]):
-        start = part * rows
-        kept = min(rows, out_ref.shape[0] - start)
-        if kept > 0:
-            out_ref[start : start + kept, :] = parts_ref[part, :kept, :].astype(jnp.float32)
-
-
-def swap(parts, axes, groups=None):
-    return lax.all_to_all(
-        parts, axes, split_axis=0, concat_axis=0, axis_index_groups=groups, tiled=True
-    )
+    out_ref[...] = (totals[0] * factor).astype(jnp.bfloat16)
+
+
+def spread_kernel(index_ref, *refs):
+    out_ref = refs[-1]
+    chunk_rows = refs[0].shape[0]
+    for distance, ref in enumerate(refs[:-1]):
+        start = lax.bitwise_xor(index_ref[1], distance) * chunk_rows
+        rows = pl.ds(pl.multiple_of(start, chunk_rows), chunk_rows)
+        out_ref[rows, :] = ref[...].astype(jnp.float32)
 
 
 def trade(values, distance):
@@ -365,15 +346,21 @@
     return lax.ppermute(values, "seq", pairs)
 
 
-def planes_of(outer, seq_count):
+def inner_size(seq_count):
     inner = 1
     while seq_count % (2 * inner) == 0 and (2 * inner) ** 2 <= seq_count:
         inner *= 2
-    planes = [
-        [o * seq_count + start + i for o in range(outer) for i in range(inner)]
-        for start in range(0, seq_count, inner)
-    ]
-    return inner, planes
+    return inner
+
+
+def trade_in_plane(values, distance, inner):
+    seq_count = lax.axis_size("seq")
+    pairs = []
+    for outer in range(lax.axis_size("dp")):
+        for seq in range(seq_count):
+            partner, lane = divmod((outer * inner + seq % inner) ^ distance, inner)
+            pairs.append((outer * seq_count + seq, partner * seq_count + seq - seq % inner + lane))
+    return lax.ppermute(values, ("dp", "seq"), pairs)
 
 
 def body(query_rows, key_rows, value_rows, region_lengths, norm_gain, conv_weight, cotangent):
@@ -381,8 +368,9 @@
     width = model_width // HEADS
     seq_count = lax.axis_size("seq")
     seq_index = lax.axis_index("seq")
-    inner, planes = planes_of(lax.axis_size("dp"), seq_count)
-    plane_size = len(planes[0])
+    inner = inner_size(seq_count)
+    plane_size = lax.axis_size("dp") * inner
+    plane_index = lax.axis_index("dp") * inner + lax.rem(seq_index, inner)
     columns = tokens * PATCH
     capacity = seq_count * tokens
     per_device = regions * HEADS // seq_count
@@ -392,7 +380,7 @@
 
     edge_shape = jax.ShapeDtypeStruct((regions, columns, width), jnp.bfloat16)
     chunk_shape = jax.ShapeDtypeStruct((3, per_device, tokens, width), jnp.bfloat16)
-    index = seq_index.reshape(1)
+    index = jnp.stack([seq_index, plane_index]).astype(jnp.int32)
     *leaving, cot_near, cot_far = call(
         functools.partial(pack_kernel, regions, per_device),
         "pack",
@@ -446,56 +434,55 @@
     )(index, item_lengths, *packed, own)
     attended = [mixed[0]] + [trade(mixed[distance], distance) for distance in order[:-1]]
 
-    chunk_rows = -(-9 * width // plane_size)
+    turned = call(
+        turn_kernel,
+        "turn_cotangent",
+        jax.ShapeDtypeStruct((3 * width, cotangent.size // width), jnp.bfloat16),
+        [SMEM()] + [VMEM()] * 3,
+        moved=8 * cotangent.size,
+    )(index, cotangent, cot_near, cot_far)
+    chunk_rows = -(-9 * width // (16 * plane_size)) * 16
     pixel_rows = regions * PATCH * columns
     conv_flops = 18 * pixel_rows * width * width
-    image, near, far, grad_parts = call(
+    part_shape = jax.ShapeDtypeStruct((chunk_rows, width), jnp.bfloat16)
+    image, near, far, *parts = call(
         functools.partial(norm_kernel, chunk_rows),
         "norm_and_gradient",
-        [
-            jax.ShapeDtypeStruct((regions, PATCH, columns, width), jnp.bfloat16),
-            edge_shape,
-            edge_shape,
-            jax.ShapeDtypeStruct((plane_size, chunk_rows, width), jnp.bfloat16),
-        ],
-        [SMEM(), SMEM()] + [VMEM()] * (4 + seq_count),
+        [jax.ShapeDtypeStruct((regions, PATCH, columns, width), jnp.bfloat16)]
+        + [edge_shape] * 2
+        + [part_shape] * plane_size,
+        [SMEM(), SMEM()] + [VMEM()] * (2 + seq_count),
         scratch=[
             pltpu.VMEM((seq_count,) + mixed[0].shape, jnp.bfloat16),
             pltpu.VMEM((regions, PATCH, columns + 2 * RIM, width), jnp.float32),
-            pltpu.VMEM((pixel_rows, 3 * width), jnp.bfloat16),
             pltpu.VMEM((pixel_rows, 3 * width), jnp.bfloat16),
             pltpu.VMEM((plane_size * chunk_rows, width), jnp.float32),
         ],
         flops=conv_flops,
         moved=4 * local_bytes,
-    )(
-        region_lengths,
-        index,
-        norm_gain.reshape(HEADS, width),
-        cotangent,
-        cot_near,
-        cot_far,
-        *attended,
-    )
-    grad_parts = swap(grad_parts, ("dp", "seq"), planes)
+    )(region_lengths, index, norm_gain.reshape(HEADS, width), turned, *attended)
+    distances = range(1, plane_size)
+    parts[1:] = [trade_in_plane(parts[distance], distance, inner) for distance in distances]
     near = trade(near, 1)
     far = lax.ppermute(far, "seq", far_pairs)
     plane_sum = call(
-        functools.partial(sum_kernel, 1, None),
+        functools.partial(sum_kernel, plane_size, 1.0),
         "sum_plane",
-        jax.ShapeDtypeStruct((chunk_rows, width), jnp.bfloat16),
-        [VMEM()],
-        moved=2 * grad_parts.size,
-    )(grad_parts)
-    plane_sums = [plane_sum] + [trade(plane_sum, inner * step) for step in range(1, len(planes))]
-    sums = call(
-        functools.partial(sum_kernel, len(planes), 1.0 / math.sqrt(PATCH * columns)),
+        part_shape,
+        [VMEM()] * plane_size,
+        moved=4 * plane_size * chunk_rows * width,
+    )(*parts)
+    plane_sums = [plane_sum] + [
+        trade(plane_sum, distance) for distance in range(inner, seq_count, inner)
+    ]
+    total = call(
+        functools.partial(sum_kernel, len(plane_sums), 1.0 / math.sqrt(PATCH * columns)),
         "sum_planes",
-        jax.ShapeDtypeStruct(grad_parts.shape, jnp.bfloat16),
-        [VMEM()] * len(planes) + [ANY(), ANY()],
-        moved=4 * grad_parts.size,
+        part_shape,
+        [VMEM()] * len(plane_sums) + [ANY(), ANY()],
+        moved=4 * len(plane_sums) * chunk_rows * width,
     )(*plane_sums, near, far)
-    sums = swap(sums, ("dp", "seq"), planes)
+    totals = [total] + [trade_in_plane(total, distance, inner) for distance in distances]
     decoded = call(
         decode_kernel,
         "decode",
@@ -508,11 +495,11 @@
     weight_grad = call(
         spread_kernel,
         "spread_sums",
-        jax.ShapeDtypeStruct((9 * width, width), jnp.float32),
-        [VMEM()],
-        moved=6 * grad_parts.size,
-    )(sums)
-    return (decoded, weight_grad.reshape(conv_weight.shape))
+        jax.ShapeDtypeStruct((plane_size * chunk_rows, width), jnp.float32),
+        [SMEM()] + [VMEM()] * plane_size,
+        moved=6 * plane_size * chunk_rows * width,
+    )(index, *totals)
+    return (decoded, weight_grad[: 9 * width].reshape(conv_weight.shape))
 
 
 def solution(mesh):

time: 99.5 us -> 105 us (1.055)
  starting transfers between devices: 49.7 us -> 57.3 us
  waiting for transfers between devices: 34.8 us -> 29.9 us
  Pallas kernels: 13.8 us -> 15.6 us
    ppermute x0 -> x14, starting transfers between devices: none -> 15.9 us  [trade_in_plane(): return lax.ppermute(values, ('dp', 'seq'), pairs)]
    all_to_all x2 -> x0, waiting for transfers between devices: 8.63 us -> none  [swap(): lax.all_to_all(parts, axes, split_axis=0, concat_axis=0, axis_index_group...]
    all_to_all x2 -> x0, starting transfers between devices: 7.14 us -> none  [swap(): lax.all_to_all(parts, axes, split_axis=0, concat_axis=0, axis_index_group...]
    ppermute x0 -> x14, waiting for transfers between devices: none -> 4.18 us  [trade_in_plane(): return lax.ppermute(values, ('dp', 'seq'), pairs)]
    ppermute x19, starting transfers between devices: 41.2 us -> 39.9 us  [trade(): return lax.ppermute(values, 'seq', pairs)]
    pallas_call x3 -> x4, Pallas kernels: 1.64 us -> 2.27 us  [the longest x1 1.4 us: body(): call(spread_kernel, 'spread_sums', jax.ShapeDtypeStruct((plane_size * chu...]
  transfers between devices with their start and end apart: 23 -> 35, of which waited for: 11 -> 13; matrix products, arithmetic and copies ran while one was open for 0% -> 0% of each run, Pallas kernels for 5% -> 6%
where the time goes in v7:
time: 105 us; the launch traced here: 104 us
  starting transfers between devices  57.3 us (55%)
  waiting for transfers between devices  29.9 us (28%)
  Pallas kernels  15.6 us (15%)
    ppermute x19, starting transfers between devices, trade(): return lax.ppermute(values, 'seq', pairs)  39.9 us
    ppermute x19, waiting for transfers between devices, trade(): return lax.ppermute(values, 'seq', pairs)  25.7 us
    ppermute x14, starting transfers between devices, trade_in_plane(): return lax.ppermute(values, ('dp', 'seq'), pairs)  15.9 us
    pallas_call x1, Pallas kernels, body(): call(functools.partial(pack_kernel, regions, per_device), 'pack', [chunk_...  4.47 us
    ppermute x14, waiting for transfers between devices, trade_in_plane(): return lax.ppermute(values, ('dp', 'seq'), pairs)  4.18 us
    pallas_call x1, Pallas kernels, body(): call(functools.partial(norm_kernel, chunk_rows), 'norm_and_gradient', [ja...  3.03 us
    pallas_call x1, Pallas kernels, body(): call(decode_kernel, 'decode', jax.ShapeDtypeStruct(cotangent.shape, jnp.b...  2.76 us
  transfers between devices with their start and end apart: 35, of which 13 were waited for; matrix products, arithmetic and copies ran while one was open for 0% of the time, Pallas kernels for 6%

profile of v7, /device:TPU:0, one launch (start us, length us, event | category | flops | bytes accessed | tf_op | source)
XLA Modules:
  0.0 104.4 jit_solution(1935522111308788018)
XLA Ops:
  0.6 0.0 copy-start.3
  0.6 0.0 copy-start.2
  0.7 0.0 copy-start.1
  0.7 0.6 pad_add_fusion.index_ref
  1.3 4.5 %pack.1 = (bf16[3,4,64,128]{3,2,1,0:T(8,128)(2,1)}, bf16[3,4,64,128]{3,2,1,0:T(8,128)(2,1)}, bf16[3,4,64,128]{3,2,1,0:T(8,128)(2,1)}, bf16[3,4,64,128]{3,2,1,0:T...) custom-call(s32[2]{0:T(128)} %pad_add_fusion.index_ref, ...), custom_call_target="tpu_custom_call" | custom-call | bytes 3145728 | tf_op jit(solution)/shard_map/pack/pallas_call | solution.py:384
  5.8 3.0 %collective-permute-start.2 = (bf16[3,4,64,128]{3,2,1,0:T(8,128)(2,1)}, bf16[3,4,64,128]{3,2,1,0:T(8,128)(2,1)S(1)}, u32[]{:S(2)}, u32[]{:S(2)}) collective-permute-start(bf16[3,4,64,128]{3,2,1,0:T(8,128)(2,1)} %get-tuple-element.32), channel_id=1, source_target_pairs={{0,1},{1,0},{2,3},{3,2},{4,5},{5,4},{6,7},{7,6},{8,9},{9,8},{10,11... | collective-permute-start | bytes 589832 | tf_op jit(solution)/shard_map/ppermute | solution.py:346
  8.8 1.6 %collective-permute-start.3 = (bf16[3,4,64,128]{3,2,1,0:T(8,128)(2,1)}, bf16[3,4,64,128]{3,2,1,0:T(8,128)(2,1)S(1)}, u32[]{:S(2)}, u32[]{:S(2)}) collective-permute-start(bf16[3,4,64,128]{3,2,1,0:T(8,128)(2,1)} %get-tuple-element.33), channel_id=1, source_target_pairs={{0,2},{1,3},{2,0},{3,1},{4,6},{5,7},{6,4},{7,5},{8,10},{9,11},{10,... | collective-permute-start | bytes 589832 | tf_op jit(solution)/shard_map/ppermute | solution.py:346
  10.4 3.0 %collective-permute-start.5 = (bf16[3,4,64,128]{3,2,1,0:T(8,128)(2,1)}, bf16[3,4,64,128]{3,2,1,0:T(8,128)(2,1)S(1)}, u32[]{:S(2)}, u32[]{:S(2)}) collective-permute-start(bf16[3,4,64,128]{3,2,1,0:T(8,128)(2,1)} %get-tuple-element.35), channel_id=1, source_target_pairs={{0,4},{1,5},{2,6},{3,7},{4,0},{5,1},{6,2},{7,3},{8,12},{9,13},{10,... | collective-permute-start | bytes 589832 | tf_op jit(solution)/shard_map/ppermute | solution.py:346
  13.4 1.3 %collective-permute-start.6 = (bf16[3,4,64,128]{3,2,1,0:T(8,128)(2,1)}, bf16[3,4,64,128]{3,2,1,0:T(8,128)(2,1)S(1)}, u32[]{:S(2)}, u32[]{:S(2)}) collective-permute-start(bf16[3,4,64,128]{3,2,1,0:T(8,128)(2,1)} %get-tuple-element.36), channel_id=1, source_target_pairs={{0,5},{1,4},{2,7},{3,6},{4,1},{5,0},{6,3},{7,2},{8,13},{9,12},{10,... | collective-permute-start | bytes 589832 | tf_op jit(solution)/shard_map/ppermute | solution.py:346
  14.6 3.6 %collective-permute-start.7 = (bf16[3,4,64,128]{3,2,1,0:T(8,128)(2,1)}, bf16[3,4,64,128]{3,2,1,0:T(8,128)(2,1)S(1)}, u32[]{:S(2)}, u32[]{:S(2)}) collective-permute-start(bf16[3,4,64,128]{3,2,1,0:T(8,128)(2,1)} %get-tuple-element.37), channel_id=1, source_target_pairs={{0,6},{1,7},{2,4},{3,5},{4,2},{5,3},{6,0},{7,1},{8,14},{9,15},{10,... | collective-permute-start | bytes 589832 | tf_op jit(solution)/shard_map/ppermute | solution.py:346
  18.2 6.2 %collective-permute-done.3.refs_1_ = bf16[3,4,64,128]{3,2,1,0:T(8,128)(2,1)S(1)} collective-permute-done((bf16[3,4,64,128]{3,2,1,0:T(8,128)(2,1)}, bf16[3,4,64,128]{3,2,1,0:T(8,128)(2,1)S(1)}, u32[]{:S(2)}, u32[]{:S(2)}) %collective-permute-start.3) | collective-permute-done | bytes 196640 | tf_op jit(solution)/shard_map/ppermute | solution.py:346
  24.5 0.9 collective-permute-start.8
  25.4 0.8 collective-permute-done.4.refs_2_
  26.2 2.5 %collective-permute-start = (bf16[2,256,128]{2,1,0:T(8,128)(2,1)}, bf16[2,256,128]{2,1,0:T(8,128)(2,1)S(1)}, u32[]{:S(2)}, u32[]{:S(2)}) collective-permute-start(bf16[2,256,128]{2,1,0:T(8,128)(2,1)} %get-tuple-element.30), channel_id=1, source_target_pairs={{0,1},{1,0},{2,3},{3,2},{4,5},{5,4},{6,7},{7,6},{8,9},{9,8},{10,11... | collective-permute-start | bytes 393224 | tf_op jit(solution)/shard_map/ppermute | solution.py:346
  28.7 0.0 collective-permute-done.5.refs_3_
  28.7 0.7 collective-permute-start.1
  29.3 0.1 fusion.lengths_ref
  29.5 0.0 copy-start
  29.5 0.9 own_chunk.1.refs_7_
  30.4 11.3 %collective-permute-done.6.refs_4_ = bf16[3,4,64,128]{3,2,1,0:T(8,128)(2,1)S(1)} collective-permute-done((bf16[3,4,64,128]{3,2,1,0:T(8,128)(2,1)}, bf16[3,4,64,128]{3,2,1,0:T(8,128)(2,1)S(1)}, u32[]{:S(2)}, u32[]{:S(2)}) %collective-permute-start.6) | collective-permute-done | bytes 196640 | tf_op jit(solution)/shard_map/ppermute | solution.py:346
  41.7 2.1 %attend.1 = (bf16[4,64,128]{2,1,0:T(8,128)(2,1)S(1)}, bf16[4,64,128]{2,1,0:T(8,128)(2,1)S(1)}, bf16[4,64,128]{2,1,0:T(8,128)(2,1)S(1)}, bf16[4,64,128]{2,1,0:T(8...) custom-call(s32[2]{0:T(128)S(1)} %copy-done.4, ...), custom_call_target="tpu_custom_call" | custom-call | flops 536870912 | bytes 2097152 | tf_op jit(solution)/shard_map/attend/pallas_call | solution.py:426
  43.8 0.0 copy-start.6
  43.8 0.1 collective-permute-start.9
  43.9 9.3 %collective-permute-start.10 = (bf16[4,64,128]{2,1,0:T(8,128)(2,1)S(1)}, bf16[4,64,128]{2,1,0:T(8,128)(2,1)S(1)}, u32[]{:S(2)}, u32[]{:S(2)}) collective-permute-start(bf16[4,64,128]{2,1,0:T(8,128)(2,1)S(1)} %get-tuple-element.41), channel_id=1, source_target_pairs={{0,2},{1,3},{2,0},{3,1},{4,6},{5,7},{6,4},{7,5},{8,10},{9,11},{10,... | collective-permute-start | bytes 196616 | tf_op jit(solution)/shard_map/ppermute | solution.py:346
  53.2 0.0 collective-permute-done.near_ref
  53.2 4.7 %collective-permute-start.12 = (bf16[4,64,128]{2,1,0:T(8,128)(2,1)S(1)}, bf16[4,64,128]{2,1,0:T(8,128)(2,1)S(1)}, u32[]{:S(2)}, u32[]{:S(2)}) collective-permute-start(bf16[4,64,128]{2,1,0:T(8,128)(2,1)S(1)} %get-tuple-element.43), channel_id=1, source_target_pairs={{0,4},{1,5},{2,6},{3,7},{4,0},{5,1},{6,2},{7,3},{8,12},{9,13},{10,... | collective-permute-start | bytes 196616 | tf_op jit(solution)/shard_map/ppermute | solution.py:346
  58.0 2.4 %collective-permute-start.14 = (bf16[4,64,128]{2,1,0:T(8,128)(2,1)S(1)}, bf16[4,64,128]{2,1,0:T(8,128)(2,1)S(1)}, u32[]{:S(2)}, u32[]{:S(2)}) collective-permute-start(bf16[4,64,128]{2,1,0:T(8,128)(2,1)S(1)} %get-tuple-element.45), channel_id=1, source_target_pairs={{0,6},{1,7},{2,4},{3,5},{4,2},{5,3},{6,0},{7,1},{8,14},{9,15},{10,... | collective-permute-start | bytes 196616 | tf_op jit(solution)/shard_map/ppermute | solution.py:346
  60.3 0.0 collective-permute-done.10.refs_2_
  60.3 2.4 %collective-permute-start.15 = (bf16[4,64,128]{2,1,0:T(8,128)(2,1)S(1)}, bf16[4,64,128]{2,1,0:T(8,128)(2,1)S(1)}, u32[]{:S(2)}, u32[]{:S(2)}) collective-permute-start(bf16[4,64,128]{2,1,0:T(8,128)(2,1)S(1)} %get-tuple-element.46), channel_id=1, source_target_pairs={{0,7},{1,6},{2,5},{3,4},{4,3},{5,2},{6,1},{7,0},{8,15},{9,14},{10,... | collective-permute-start | bytes 196616 | tf_op jit(solution)/shard_map/ppermute | solution.py:346
  62.8 0.8 turn_cotangent.1.turned_ref
  63.6 0.0 copy-start.5
  63.6 0.0 collective-permute-done.11.refs_3_
  63.6 1.8 %collective-permute-done.13.refs_5_ = bf16[4,64,128]{2,1,0:T(8,128)(2,1)S(1)} collective-permute-done((bf16[4,64,128]{2,1,0:T(8,128)(2,1)S(1)}, bf16[4,64,128]{2,1,0:T(8,128)(2,1)S(1)}, u32[]{:S(2)}, u32[]{:S(2)}) %collective-permute-start.13) | collective-permute-done | bytes 65568 | tf_op jit(solution)/shard_map/ppermute | solution.py:346
  65.4 0.0 collective-permute-done.14.refs_6_
  65.4 2.0 %collective-permute-done.15.refs_7_ = bf16[4,64,128]{2,1,0:T(8,128)(2,1)S(1)} collective-permute-done((bf16[4,64,128]{2,1,0:T(8,128)(2,1)S(1)}, bf16[4,64,128]{2,1,0:T(8,128)(2,1)S(1)}, u32[]{:S(2)}, u32[]{:S(2)}) %collective-permute-start.15) | collective-permute-done | bytes 65568 | tf_op jit(solution)/shard_map/ppermute | solution.py:346
  67.4 3.0 %norm_and_gradient.1 = (bf16[2,4,256,128]{3,2,1,0:T(8,128)(2,1)S(1)}, bf16[2,256,128]{2,1,0:T(8,128)(2,1)S(1)}, bf16[2,256,128]{2,1,0:T(8,128)(2,1)S(1)}, bf16[1...) custom-call(s32[2]{0:T(128)S(1)} %copy-done.7, ...), custom_call_target="tpu_custom_call" | custom-call | flops 603979776 | bytes 2097152 | tf_op jit(solution)/shard_map/norm_and_gradient/pallas_call | solution.py:448
  70.4 1.4 %collective-permute-start.18 = (bf16[144,128]{1,0:T(8,128)(2,1)S(1)}, bf16[144,128]{1,0:T(8,128)(2,1)S(1)}, u32[]{:S(2)}, u32[]{:S(2)}) collective-permute-start(bf16[144,128]{1,0:T(8,128)(2,1)S(1)} %get-tuple-element.51), channel_id=1, source_target_pairs={{0,1},{1,0},{2,3},{3,2},{4,5},{5,4},{6,7},{7,6},{8,9},{9,8},{10,11... | collective-permute-start | bytes 110600 | tf_op jit(solution)/shard_map/ppermute | solution.py:363
  71.9 0.7 collective-permute-start.16
  72.5 0.8 collective-permute-start.17
  73.4 0.1 collective-permute-start.19
  73.5 3.5 %collective-permute-start.20 = (bf16[144,128]{1,0:T(8,128)(2,1)S(1)}, bf16[144,128]{1,0:T(8,128)(2,1)S(1)}, u32[]{:S(2)}, u32[]{:S(2)}) collective-permute-start(bf16[144,128]{1,0:T(8,128)(2,1)S(1)} %get-tuple-element.53), channel_id=1, source_target_pairs={{0,9},{1,8},{2,11},{3,10},{4,13},{5,12},{6,15},{7,14},{8,1},{9,0},... | collective-permute-start | bytes 110600 | tf_op jit(solution)/shard_map/ppermute | solution.py:363
  76.9 1.5 %collective-permute-start.21 = (bf16[144,128]{1,0:T(8,128)(2,1)S(1)}, bf16[144,128]{1,0:T(8,128)(2,1)S(1)}, u32[]{:S(2)}, u32[]{:S(2)}) collective-permute-start(bf16[144,128]{1,0:T(8,128)(2,1)S(1)} %get-tuple-element.54), channel_id=1, source_target_pairs={{0,16},{1,17},{2,18},{3,19},{4,20},{5,21},{6,22},{7,23},{8,24},{9,... | collective-permute-start | bytes 110600 | tf_op jit(solution)/shard_map/ppermute | solution.py:363
  78.5 0.5 collective-permute-start.22
  79.0 0.8 collective-permute-done.20.refs_3_
  79.8 0.2 collective-permute-start.23
  79.9 1.0 collective-permute-done.21.refs_4_
  80.9 1.9 %collective-permute-start.24 = (bf16[144,128]{1,0:T(8,128)(2,1)S(1)}, bf16[144,128]{1,0:T(8,128)(2,1)S(1)}, u32[]{:S(2)}, u32[]{:S(2)}) collective-permute-start(bf16[144,128]{1,0:T(8,128)(2,1)S(1)} %get-tuple-element.57), channel_id=1, source_target_pairs={{0,25},{1,24},{2,27},{3,26},{4,29},{5,28},{6,31},{7,30},{8,17},{9,... | collective-permute-start | bytes 110600 | tf_op jit(solution)/shard_map/ppermute | solution.py:363
  82.8 0.6 collective-permute-done.22.refs_5_
  83.4 0.4 collective-permute-done.23.refs_6_
  83.9 1.3 %collective-permute-done.24.refs_7_ = bf16[144,128]{1,0:T(8,128)(2,1)S(1)} collective-permute-done((bf16[144,128]{1,0:T(8,128)(2,1)S(1)}, bf16[144,128]{1,0:T(8,128)(2,1)S(1)}, u32[]{:S(2)}, u32[]{:S(2)}) %collective-permute-start.24) | collective-permute-done | bytes 36896 | tf_op jit(solution)/shard_map/ppermute | solution.py:363
  85.2 2.8 %collective-permute-start.27 = (bf16[144,128]{1,0:T(8,128)(2,1)S(1)}, bf16[144,128]{1,0:T(8,128)(2,1)S(1)}, u32[]{:S(2)}, u32[]{:S(2)}) collective-permute-start(bf16[144,128]{1,0:T(8,128)(2,1)S(1)} %sum_plane.1.refs_0_), channel_id=1, source_target_pairs={{0,6},{1,7},{2,4},{3,5},{4,2},{5,3},{6,0},{7,1},{8,14},{9,15},{10,... | collective-permute-start | bytes 110600 | tf_op jit(solution)/shard_map/ppermute | solution.py:346
  88.1 0.8 collective-permute-start.26
  88.9 0.8 collective-permute-start.25
  89.7 1.6 %collective-permute-done.27.refs_3_ = bf16[144,128]{1,0:T(8,128)(2,1)S(1)} collective-permute-done((bf16[144,128]{1,0:T(8,128)(2,1)S(1)}, bf16[144,128]{1,0:T(8,128)(2,1)S(1)}, u32[]{:S(2)}, u32[]{:S(2)}) %collective-permute-start.27) | collective-permute-done | bytes 36896 | tf_op jit(solution)/shard_map/ppermute | solution.py:346
  91.3 1.7 %collective-permute-done.26.refs_2_ = bf16[144,128]{1,0:T(8,128)(2,1)S(1)} collective-permute-done((bf16[144,128]{1,0:T(8,128)(2,1)S(1)}, bf16[144,128]{1,0:T(8,128)(2,1)S(1)}, u32[]{:S(2)}, u32[]{:S(2)}) %collective-permute-start.26) | collective-permute-done | bytes 36896 | tf_op jit(solution)/shard_map/ppermute | solution.py:346
  93.0 0.2 collective-permute-done.25.refs_1_
  93.3 0.2 collective-permute-start.34
  93.5 1.9 %collective-permute-start.33 = (bf16[144,128]{1,0:T(8,128)(2,1)S(1)}, bf16[144,128]{1,0:T(8,128)(2,1)S(1)}, u32[]{:S(2)}, u32[]{:S(2)}) collective-permute-start(bf16[144,128]{1,0:T(8,128)(2,1)S(1)} %sum_planes.1.refs_0_), channel_id=1, source_target_pairs={{0,24},{1,25},{2,26},{3,27},{4,28},{5,29},{6,30},{7,31},{8,16},{9,... | collective-permute-start | bytes 110600 | tf_op jit(solution)/shard_map/ppermute | solution.py:363
  95.4 1.2 %collective-permute-start.32 = (bf16[144,128]{1,0:T(8,128)(2,1)S(1)}, bf16[144,128]{1,0:T(8,128)(2,1)S(1)}, u32[]{:S(2)}, u32[]{:S(2)}) collective-permute-start(bf16[144,128]{1,0:T(8,128)(2,1)S(1)} %sum_planes.1.refs_0_), channel_id=1, source_target_pairs={{0,17},{1,16},{2,19},{3,18},{4,21},{5,20},{6,23},{7,22},{8,25},{9,... | collective-permute-start | bytes 110600 | tf_op jit(solution)/shard_map/ppermute | solution.py:363
  96.6 1.4 %collective-permute-start.31 = (bf16[144,128]{1,0:T(8,128)(2,1)S(1)}, bf16[144,128]{1,0:T(8,128)(2,1)S(1)}, u32[]{:S(2)}, u32[]{:S(2)}) collective-permute-start(bf16[144,128]{1,0:T(8,128)(2,1)S(1)} %sum_planes.1.refs_0_), channel_id=1, source_target_pairs={{0,16},{1,17},{2,18},{3,19},{4,20},{5,21},{6,22},{7,23},{8,24},{9,... | collective-permute-start | bytes 110600 | tf_op jit(solution)/shard_map/ppermute | solution.py:363
  98.0 1.0 collective-permute-start.29
  99.0 1.2 %collective-permute-start.28 = (bf16[144,128]{1,0:T(8,128)(2,1)S(1)}, bf16[144,128]{1,0:T(8,128)(2,1)S(1)}, u32[]{:S(2)}, u32[]{:S(2)}) collective-permute-start(bf16[144,128]{1,0:T(8,128)(2,1)S(1)} %sum_planes.1.refs_0_), channel_id=1, source_target_pairs={{0,1},{1,0},{2,3},{3,2},{4,5},{5,4},{6,7},{7,6},{8,9},{9,8},{10,11... | collective-permute-start | bytes 110600 | tf_op jit(solution)/shard_map/ppermute | solution.py:363
  100.2 2.8 %decode.1 = bf16[2,4,256,128]{3,2,1,0:T(8,128)(2,1)} custom-call(s32[2]{0:T(128)S(1)} %copy-done.4, bf16[2,4,256,128]{3,2,1,0:T(8,128)(2,1)S(1)} %get-tuple-element.47.image_ref, bf16[2,256,128]{2,1,0:T(8,128)(2,1)S(1)} %collective-permute-done.16.near_ref.refs_4_, bf16[2,256,128]{2,1,0:T(8,128)(2,1)S(1)} %collective-permute-done.17.far_ref.refs_5_, ...), custom_call_target="tpu_custom_call" | custom-call | flops 603979776 | bytes 1048576 | tf_op jit(solution)/shard_map/decode/pallas_call | solution.py:486
  103.0 1.4 %spread_sums.1 = f32[1152,128]{1,0:T(8,128)} custom-call(s32[2]{0:T(128)S(1)} %copy-done.4, bf16[144,128]{1,0:T(8,128)(2,1)S(1)} %sum_planes.1.refs_0_, bf16[144,128]{1,0:T(8,128)(2,1)S(1)} %collective-permute-done.28.refs_1_, bf16[144,128]{1,0:T(8,128)(2,1)S(1)} %collective-permute-done.29.refs_2_, bf16[144,128]{1,0:T(8,128)(2,1)S(1)} %collective-permute-done.30.refs_3_, ...), custom_call_target="tpu_custom_call" | custom-call | bytes 884736 | tf_op jit(solution)/shard_map/spread_sums/pallas_call | solution.py:495
  (34 shorter events, 0.2 us)
Async XLA Ops:
  0.6 28.8 %copy-start.3 = (bf16[64,2,2048]{2,1,0:T(2,128)(2,1)S(1)}, bf16[64,2,2048]{2,1,0:T(2,128)(2,1)}, u32[]{:S(2)}) copy-start(bf16[64,2,2048]{2,1,0:T(2,128)(2,1)} %value_ref.3) | copy-start | bytes 1572868
  0.6 28.8 %copy-start.2 = (bf16[64,2,2048]{2,1,0:T(2,128)(2,1)S(1)}, bf16[64,2,2048]{2,1,0:T(2,128)(2,1)}, u32[]{:S(2)}) copy-start(bf16[64,2,2048]{2,1,0:T(2,128)(2,1)} %key_ref.3) | copy-start | bytes 1572868
  0.7 28.8 %copy-start.1 = (bf16[64,2,2048]{2,1,0:T(2,128)(2,1)S(1)}, bf16[64,2,2048]{2,1,0:T(2,128)(2,1)}, u32[]{:S(2)}) copy-start(bf16[64,2,2048]{2,1,0:T(2,128)(2,1)} %query_ref.3) | copy-start | bytes 1572868
  0.7 28.7 %copy-start.7 = (s32[2]{0:T(128)S(1)}, s32[2]{0:T(128)}, u32[]{:S(2)}) copy-start(s32[2]{0:T(128)} %lengths_ref.1) | copy-start | bytes 28
  1.3 28.2 %copy-start.4 = (s32[2]{0:T(128)S(1)}, s32[2]{0:T(128)}, u32[]{:S(2)}) copy-start(s32[2]{0:T(128)} %pad_add_fusion.index_ref) | copy-start | bytes 28
  5.8 8.9 %collective-permute-start.2 = (bf16[3,4,64,128]{3,2,1,0:T(8,128)(2,1)}, bf16[3,4,64,128]{3,2,1,0:T(8,128)(2,1)S(1)}, u32[]{:S(2)}, u32[]{:S(2)}) collective-permute-start(bf16[3,4,64,128]{3,2,1,0:T(8,128)(2,1)} %get-tuple-element.32), channel_id=1, source_target_pairs={{0,1},{1,0},{2,3},{3,2},{4,5},{5,4},{6,7},{7,6},{8,9},{9,8},{10,11... | collective-permute-start | bytes 589832 | tf_op jit(solution)/shard_map/ppermute | solution.py:346
  8.8 15.7 %collective-permute-start.3 = (bf16[3,4,64,128]{3,2,1,0:T(8,128)(2,1)}, bf16[3,4,64,128]{3,2,1,0:T(8,128)(2,1)S(1)}, u32[]{:S(2)}, u32[]{:S(2)}) collective-permute-start(bf16[3,4,64,128]{3,2,1,0:T(8,128)(2,1)} %get-tuple-element.33), channel_id=1, source_target_pairs={{0,2},{1,3},{2,0},{3,1},{4,6},{5,7},{6,4},{7,5},{8,10},{9,11},{10,... | collective-permute-start | bytes 589832 | tf_op jit(solution)/shard_map/ppermute | solution.py:346
  10.4 15.8 %collective-permute-start.4 = (bf16[3,4,64,128]{3,2,1,0:T(8,128)(2,1)}, bf16[3,4,64,128]{3,2,1,0:T(8,128)(2,1)S(1)}, u32[]{:S(2)}, u32[]{:S(2)}) collective-permute-start(bf16[3,4,64,128]{3,2,1,0:T(8,128)(2,1)} %get-tuple-element.34), channel_id=1, source_target_pairs={{0,3},{1,2},{2,1},{3,0},{4,7},{5,6},{6,5},{7,4},{8,11},{9,10},{10,... | collective-permute-start | bytes 589832 | tf_op jit(solution)/shard_map/ppermute | solution.py:346
  10.4 18.3 %collective-permute-start.5 = (bf16[3,4,64,128]{3,2,1,0:T(8,128)(2,1)}, bf16[3,4,64,128]{3,2,1,0:T(8,128)(2,1)S(1)}, u32[]{:S(2)}, u32[]{:S(2)}) collective-permute-start(bf16[3,4,64,128]{3,2,1,0:T(8,128)(2,1)} %get-tuple-element.35), channel_id=1, source_target_pairs={{0,4},{1,5},{2,6},{3,7},{4,0},{5,1},{6,2},{7,3},{8,12},{9,13},{10,... | collective-permute-start | bytes 589832 | tf_op jit(solution)/shard_map/ppermute | solution.py:346
  13.4 28.3 %collective-permute-start.6 = (bf16[3,4,64,128]{3,2,1,0:T(8,128)(2,1)}, bf16[3,4,64,128]{3,2,1,0:T(8,128)(2,1)S(1)}, u32[]{:S(2)}, u32[]{:S(2)}) collective-permute-start(bf16[3,4,64,128]{3,2,1,0:T(8,128)(2,1)} %get-tuple-element.36), channel_id=1, source_target_pairs={{0,5},{1,4},{2,7},{3,6},{4,1},{5,0},{6,3},{7,2},{8,13},{9,12},{10,... | collective-permute-start | bytes 589832 | tf_op jit(solution)/shard_map/ppermute | solution.py:346
  14.6 27.1 %collective-permute-start.7 = (bf16[3,4,64,128]{3,2,1,0:T(8,128)(2,1)}, bf16[3,4,64,128]{3,2,1,0:T(8,128)(2,1)S(1)}, u32[]{:S(2)}, u32[]{:S(2)}) collective-permute-start(bf16[3,4,64,128]{3,2,1,0:T(8,128)(2,1)} %get-tuple-element.37), channel_id=1, source_target_pairs={{0,6},{1,7},{2,4},{3,5},{4,2},{5,3},{6,0},{7,1},{8,14},{9,15},{10,... | collective-permute-start | bytes 589832 | tf_op jit(solution)/shard_map/ppermute | solution.py:346
  24.5 17.2 %collective-permute-start.8 = (bf16[3,4,64,128]{3,2,1,0:T(8,128)(2,1)}, bf16[3,4,64,128]{3,2,1,0:T(8,128)(2,1)S(1)}, u32[]{:S(2)}, u32[]{:S(2)}) collective-permute-start(bf16[3,4,64,128]{3,2,1,0:T(8,128)(2,1)} %get-tuple-element.38), channel_id=1, source_target_pairs={{0,7},{1,6},{2,5},{3,4},{4,3},{5,2},{6,1},{7,0},{8,15},{9,14},{10,... | collective-permute-start | bytes 589832 | tf_op jit(solution)/shard_map/ppermute | solution.py:346
  26.2 27.0 %collective-permute-start = (bf16[2,256,128]{2,1,0:T(8,128)(2,1)}, bf16[2,256,128]{2,1,0:T(8,128)(2,1)S(1)}, u32[]{:S(2)}, u32[]{:S(2)}) collective-permute-start(bf16[2,256,128]{2,1,0:T(8,128)(2,1)} %get-tuple-element.30), channel_id=1, source_target_pairs={{0,1},{1,0},{2,3},{3,2},{4,5},{5,4},{6,7},{7,6},{8,9},{9,8},{10,11... | collective-permute-start | bytes 393224 | tf_op jit(solution)/shard_map/ppermute | solution.py:346
  28.7 29.3 %collective-permute-start.1 = (bf16[2,256,128]{2,1,0:T(8,128)(2,1)}, bf16[2,256,128]{2,1,0:T(8,128)(2,1)S(1)}, u32[]{:S(2)}, u32[]{:S(2)}) collective-permute-start(bf16[2,256,128]{2,1,0:T(8,128)(2,1)} %get-tuple-element.31), channel_id=1, source_target_pairs={{1,2},{3,4},{5,6},{2,1},{4,3},{6,5},{9,10},{11,12},{13,14},{10,9},... | collective-permute-start | bytes 393224 | tf_op jit(solution)/shard_map/ppermute | solution.py:413
  29.5 33.3 %copy-start = (bf16[2,4,256,128]{3,2,1,0:T(8,128)(2,1)S(1)}, bf16[2,4,256,128]{3,2,1,0:T(8,128)(2,1)}, u32[]{:S(2)}) copy-start(bf16[2,4,256,128]{3,2,1,0:T(8,128)(2,1)} %cot_ref.3) | copy-start | bytes 1572868
  43.8 23.6 %copy-start.6 = (f32[2048]{0:T(1024)S(1)}, f32[2048]{0:T(1024)}, u32[]{:S(2)}) copy-start(f32[2048]{0:T(1024)} %param.11) | copy-start | bytes 24580
  43.8 14.2 %collective-permute-start.9 = (bf16[4,64,128]{2,1,0:T(8,128)(2,1)S(1)}, bf16[4,64,128]{2,1,0:T(8,128)(2,1)S(1)}, u32[]{:S(2)}, u32[]{:S(2)}) collective-permute-start(bf16[4,64,128]{2,1,0:T(8,128)(2,1)S(1)} %get-tuple-element.40), channel_id=1, source_target_pairs={{0,1},{1,0},{2,3},{3,2},{4,5},{5,4},{6,7},{7,6},{8,9},{9,8},{10,11... | collective-permute-start | bytes 196616 | tf_op jit(solution)/shard_map/ppermute | solution.py:346
  43.9 16.4 %collective-permute-start.10 = (bf16[4,64,128]{2,1,0:T(8,128)(2,1)S(1)}, bf16[4,64,128]{2,1,0:T(8,128)(2,1)S(1)}, u32[]{:S(2)}, u32[]{:S(2)}) collective-permute-start(bf16[4,64,128]{2,1,0:T(8,128)(2,1)S(1)} %get-tuple-element.41), channel_id=1, source_target_pairs={{0,2},{1,3},{2,0},{3,1},{4,6},{5,7},{6,4},{7,5},{8,10},{9,11},{10,... | collective-permute-start | bytes 196616 | tf_op jit(solution)/shard_map/ppermute | solution.py:346
  53.2 10.4 %collective-permute-start.11 = (bf16[4,64,128]{2,1,0:T(8,128)(2,1)S(1)}, bf16[4,64,128]{2,1,0:T(8,128)(2,1)S(1)}, u32[]{:S(2)}, u32[]{:S(2)}) collective-permute-start(bf16[4,64,128]{2,1,0:T(8,128)(2,1)S(1)} %get-tuple-element.42), channel_id=1, source_target_pairs={{0,3},{1,2},{2,1},{3,0},{4,7},{5,6},{6,5},{7,4},{8,11},{9,10},{10,... | collective-permute-start | bytes 196616 | tf_op jit(solution)/shard_map/ppermute | solution.py:346
  53.2 10.4 %collective-permute-start.12 = (bf16[4,64,128]{2,1,0:T(8,128)(2,1)S(1)}, bf16[4,64,128]{2,1,0:T(8,128)(2,1)S(1)}, u32[]{:S(2)}, u32[]{:S(2)}) collective-permute-start(bf16[4,64,128]{2,1,0:T(8,128)(2,1)S(1)} %get-tuple-element.43), channel_id=1, source_target_pairs={{0,4},{1,5},{2,6},{3,7},{4,0},{5,1},{6,2},{7,3},{8,12},{9,13},{10,... | collective-permute-start | bytes 196616 | tf_op jit(solution)/shard_map/ppermute | solution.py:346
  58.0 7.4 %collective-permute-start.13 = (bf16[4,64,128]{2,1,0:T(8,128)(2,1)S(1)}, bf16[4,64,128]{2,1,0:T(8,128)(2,1)S(1)}, u32[]{:S(2)}, u32[]{:S(2)}) collective-permute-start(bf16[4,64,128]{2,1,0:T(8,128)(2,1)S(1)} %get-tuple-element.44), channel_id=1, source_target_pairs={{0,5},{1,4},{2,7},{3,6},{4,1},{5,0},{6,3},{7,2},{8,13},{9,12},{10,... | collective-permute-start | bytes 196616 | tf_op jit(solution)/shard_map/ppermute | solution.py:346
  58.0 7.4 %collective-permute-start.14 = (bf16[4,64,128]{2,1,0:T(8,128)(2,1)S(1)}, bf16[4,64,128]{2,1,0:T(8,128)(2,1)S(1)}, u32[]{:S(2)}, u32[]{:S(2)}) collective-permute-start(bf16[4,64,128]{2,1,0:T(8,128)(2,1)S(1)} %get-tuple-element.45), channel_id=1, source_target_pairs={{0,6},{1,7},{2,4},{3,5},{4,2},{5,3},{6,0},{7,1},{8,14},{9,15},{10,... | collective-permute-start | bytes 196616 | tf_op jit(solution)/shard_map/ppermute | solution.py:346
  60.3 7.1 %collective-permute-start.15 = (bf16[4,64,128]{2,1,0:T(8,128)(2,1)S(1)}, bf16[4,64,128]{2,1,0:T(8,128)(2,1)S(1)}, u32[]{:S(2)}, u32[]{:S(2)}) collective-permute-start(bf16[4,64,128]{2,1,0:T(8,128)(2,1)S(1)} %get-tuple-element.46), channel_id=1, source_target_pairs={{0,7},{1,6},{2,5},{3,4},{4,3},{5,2},{6,1},{7,0},{8,15},{9,14},{10,... | collective-permute-start | bytes 196616 | tf_op jit(solution)/shard_map/ppermute | solution.py:346
  63.6 36.6 %copy-start.5 = (bf16[9,128,128]{2,1,0:T(8,128)(2,1)S(1)}, bf16[9,128,128]{2,1,0:T(8,128)(2,1)}, u32[]{:S(2)}) copy-start(bf16[9,128,128]{2,1,0:T(8,128)(2,1)} %param.12) | copy-start | bytes 884740
  70.4 6.5 %collective-permute-start.18 = (bf16[144,128]{1,0:T(8,128)(2,1)S(1)}, bf16[144,128]{1,0:T(8,128)(2,1)S(1)}, u32[]{:S(2)}, u32[]{:S(2)}) collective-permute-start(bf16[144,128]{1,0:T(8,128)(2,1)S(1)} %get-tuple-element.51), channel_id=1, source_target_pairs={{0,1},{1,0},{2,3},{3,2},{4,5},{5,4},{6,7},{7,6},{8,9},{9,8},{10,11... | collective-permute-start | bytes 110600 | tf_op jit(solution)/shard_map/ppermute | solution.py:363
  71.9 21.4 %collective-permute-start.16 = (bf16[2,256,128]{2,1,0:T(8,128)(2,1)S(1)}, bf16[2,256,128]{2,1,0:T(8,128)(2,1)S(1)}, u32[]{:S(2)}, u32[]{:S(2)}) collective-permute-start(bf16[2,256,128]{2,1,0:T(8,128)(2,1)S(1)} %get-tuple-element.48), channel_id=1, source_target_pairs={{0,1},{1,0},{2,3},{3,2},{4,5},{5,4},{6,7},{7,6},{8,9},{9,8},{10,11... | collective-permute-start | bytes 393224 | tf_op jit(solution)/shard_map/ppermute | solution.py:346
  72.5 20.7 %collective-permute-start.17 = (bf16[2,256,128]{2,1,0:T(8,128)(2,1)S(1)}, bf16[2,256,128]{2,1,0:T(8,128)(2,1)S(1)}, u32[]{:S(2)}, u32[]{:S(2)}) collective-permute-start(bf16[2,256,128]{2,1,0:T(8,128)(2,1)S(1)} %get-tuple-element.49), channel_id=1, source_target_pairs={{1,2},{3,4},{5,6},{2,1},{4,3},{6,5},{9,10},{11,12},{13,14},{10,9},... | collective-permute-start | bytes 393224 | tf_op jit(solution)/shard_map/ppermute | solution.py:467
  73.4 5.1 %collective-permute-start.19 = (bf16[144,128]{1,0:T(8,128)(2,1)S(1)}, bf16[144,128]{1,0:T(8,128)(2,1)S(1)}, u32[]{:S(2)}, u32[]{:S(2)}) collective-permute-start(bf16[144,128]{1,0:T(8,128)(2,1)S(1)} %get-tuple-element.52), channel_id=1, source_target_pairs={{0,8},{1,9},{2,10},{3,11},{4,12},{5,13},{6,14},{7,15},{8,0},{9,1},... | collective-permute-start | bytes 110600 | tf_op jit(solution)/shard_map/ppermute | solution.py:363
  73.5 6.3 %collective-permute-start.20 = (bf16[144,128]{1,0:T(8,128)(2,1)S(1)}, bf16[144,128]{1,0:T(8,128)(2,1)S(1)}, u32[]{:S(2)}, u32[]{:S(2)}) collective-permute-start(bf16[144,128]{1,0:T(8,128)(2,1)S(1)} %get-tuple-element.53), channel_id=1, source_target_pairs={{0,9},{1,8},{2,11},{3,10},{4,13},{5,12},{6,15},{7,14},{8,1},{9,0},... | collective-permute-start | bytes 110600 | tf_op jit(solution)/shard_map/ppermute | solution.py:363
  76.9 4.0 %collective-permute-start.21 = (bf16[144,128]{1,0:T(8,128)(2,1)S(1)}, bf16[144,128]{1,0:T(8,128)(2,1)S(1)}, u32[]{:S(2)}, u32[]{:S(2)}) collective-permute-start(bf16[144,128]{1,0:T(8,128)(2,1)S(1)} %get-tuple-element.54), channel_id=1, source_target_pairs={{0,16},{1,17},{2,18},{3,19},{4,20},{5,21},{6,22},{7,23},{8,24},{9,... | collective-permute-start | bytes 110600 | tf_op jit(solution)/shard_map/ppermute | solution.py:363
  78.5 5.0 %collective-permute-start.22 = (bf16[144,128]{1,0:T(8,128)(2,1)S(1)}, bf16[144,128]{1,0:T(8,128)(2,1)S(1)}, u32[]{:S(2)}, u32[]{:S(2)}) collective-permute-start(bf16[144,128]{1,0:T(8,128)(2,1)S(1)} %get-tuple-element.55), channel_id=1, source_target_pairs={{0,17},{1,16},{2,19},{3,18},{4,21},{5,20},{6,23},{7,22},{8,25},{9,... | collective-permute-start | bytes 110600 | tf_op jit(solution)/shard_map/ppermute | solution.py:363
  79.8 4.1 %collective-permute-start.23 = (bf16[144,128]{1,0:T(8,128)(2,1)S(1)}, bf16[144,128]{1,0:T(8,128)(2,1)S(1)}, u32[]{:S(2)}, u32[]{:S(2)}) collective-permute-start(bf16[144,128]{1,0:T(8,128)(2,1)S(1)} %get-tuple-element.56), channel_id=1, source_target_pairs={{0,24},{1,25},{2,26},{3,27},{4,28},{5,29},{6,30},{7,31},{8,16},{9,... | collective-permute-start | bytes 110600 | tf_op jit(solution)/shard_map/ppermute | solution.py:363
  80.9 4.3 %collective-permute-start.24 = (bf16[144,128]{1,0:T(8,128)(2,1)S(1)}, bf16[144,128]{1,0:T(8,128)(2,1)S(1)}, u32[]{:S(2)}, u32[]{:S(2)}) collective-permute-start(bf16[144,128]{1,0:T(8,128)(2,1)S(1)} %get-tuple-element.57), channel_id=1, source_target_pairs={{0,25},{1,24},{2,27},{3,26},{4,29},{5,28},{6,31},{7,30},{8,17},{9,... | collective-permute-start | bytes 110600 | tf_op jit(solution)/shard_map/ppermute | solution.py:363
  85.2 6.1 %collective-permute-start.27 = (bf16[144,128]{1,0:T(8,128)(2,1)S(1)}, bf16[144,128]{1,0:T(8,128)(2,1)S(1)}, u32[]{:S(2)}, u32[]{:S(2)}) collective-permute-start(bf16[144,128]{1,0:T(8,128)(2,1)S(1)} %sum_plane.1.refs_0_), channel_id=1, source_target_pairs={{0,6},{1,7},{2,4},{3,5},{4,2},{5,3},{6,0},{7,1},{8,14},{9,15},{10,... | collective-permute-start | bytes 110600 | tf_op jit(solution)/shard_map/ppermute | solution.py:346
  88.1 5.0 %collective-permute-start.26 = (bf16[144,128]{1,0:T(8,128)(2,1)S(1)}, bf16[144,128]{1,0:T(8,128)(2,1)S(1)}, u32[]{:S(2)}, u32[]{:S(2)}) collective-permute-start(bf16[144,128]{1,0:T(8,128)(2,1)S(1)} %sum_plane.1.refs_0_), channel_id=1, source_target_pairs={{0,4},{1,5},{2,6},{3,7},{4,0},{5,1},{6,2},{7,3},{8,12},{9,13},{10,... | collective-permute-start | bytes 110600 | tf_op jit(solution)/shard_map/ppermute | solution.py:346
  88.9 4.4 %collective-permute-start.25 = (bf16[144,128]{1,0:T(8,128)(2,1)S(1)}, bf16[144,128]{1,0:T(8,128)(2,1)S(1)}, u32[]{:S(2)}, u32[]{:S(2)}) collective-permute-start(bf16[144,128]{1,0:T(8,128)(2,1)S(1)} %sum_plane.1.refs_0_), channel_id=1, source_target_pairs={{0,2},{1,3},{2,0},{3,1},{4,6},{5,7},{6,4},{7,5},{8,10},{9,11},{10,... | collective-permute-start | bytes 110600 | tf_op jit(solution)/shard_map/ppermute | solution.py:346
  93.3 4.7 %collective-permute-start.34 = (bf16[144,128]{1,0:T(8,128)(2,1)S(1)}, bf16[144,128]{1,0:T(8,128)(2,1)S(1)}, u32[]{:S(2)}, u32[]{:S(2)}) collective-permute-start(bf16[144,128]{1,0:T(8,128)(2,1)S(1)} %sum_planes.1.refs_0_), channel_id=1, source_target_pairs={{0,25},{1,24},{2,27},{3,26},{4,29},{5,28},{6,31},{7,30},{8,17},{9,... | collective-permute-start | bytes 110600 | tf_op jit(solution)/shard_map/ppermute | solution.py:363
  93.5 5.5 %collective-permute-start.33 = (bf16[144,128]{1,0:T(8,128)(2,1)S(1)}, bf16[144,128]{1,0:T(8,128)(2,1)S(1)}, u32[]{:S(2)}, u32[]{:S(2)}) collective-permute-start(bf16[144,128]{1,0:T(8,128)(2,1)S(1)} %sum_planes.1.refs_0_), channel_id=1, source_target_pairs={{0,24},{1,25},{2,26},{3,27},{4,28},{5,29},{6,30},{7,31},{8,16},{9,... | collective-permute-start | bytes 110600 | tf_op jit(solution)/shard_map/ppermute | solution.py:363
  95.4 7.6 %collective-permute-start.32 = (bf16[144,128]{1,0:T(8,128)(2,1)S(1)}, bf16[144,128]{1,0:T(8,128)(2,1)S(1)}, u32[]{:S(2)}, u32[]{:S(2)}) collective-permute-start(bf16[144,128]{1,0:T(8,128)(2,1)S(1)} %sum_planes.1.refs_0_), channel_id=1, source_target_pairs={{0,17},{1,16},{2,19},{3,18},{4,21},{5,20},{6,23},{7,22},{8,25},{9,... | collective-permute-start | bytes 110600 | tf_op jit(solution)/shard_map/ppermute | solution.py:363
  96.6 6.3 %collective-permute-start.31 = (bf16[144,128]{1,0:T(8,128)(2,1)S(1)}, bf16[144,128]{1,0:T(8,128)(2,1)S(1)}, u32[]{:S(2)}, u32[]{:S(2)}) collective-permute-start(bf16[144,128]{1,0:T(8,128)(2,1)S(1)} %sum_planes.1.refs_0_), channel_id=1, source_target_pairs={{0,16},{1,17},{2,18},{3,19},{4,20},{5,21},{6,22},{7,23},{8,24},{9,... | collective-permute-start | bytes 110600 | tf_op jit(solution)/shard_map/ppermute | solution.py:363
  98.0 4.9 %collective-permute-start.30 = (bf16[144,128]{1,0:T(8,128)(2,1)S(1)}, bf16[144,128]{1,0:T(8,128)(2,1)S(1)}, u32[]{:S(2)}, u32[]{:S(2)}) collective-permute-start(bf16[144,128]{1,0:T(8,128)(2,1)S(1)} %sum_planes.1.refs_0_), channel_id=1, source_target_pairs={{0,9},{1,8},{2,11},{3,10},{4,13},{5,12},{6,15},{7,14},{8,1},{9,0},... | collective-permute-start | bytes 110600 | tf_op jit(solution)/shard_map/ppermute | solution.py:363
  98.0 4.9 %collective-permute-start.29 = (bf16[144,128]{1,0:T(8,128)(2,1)S(1)}, bf16[144,128]{1,0:T(8,128)(2,1)S(1)}, u32[]{:S(2)}, u32[]{:S(2)}) collective-permute-start(bf16[144,128]{1,0:T(8,128)(2,1)S(1)} %sum_planes.1.refs_0_), channel_id=1, source_target_pairs={{0,8},{1,9},{2,10},{3,11},{4,12},{5,13},{6,14},{7,15},{8,0},{9,1},... | collective-permute-start | bytes 110600 | tf_op jit(solution)/shard_map/ppermute | solution.py:363
  99.0 4.0 %collective-permute-start.28 = (bf16[144,128]{1,0:T(8,128)(2,1)S(1)}, bf16[144,128]{1,0:T(8,128)(2,1)S(1)}, u32[]{:S(2)}, u32[]{:S(2)}) collective-permute-start(bf16[144,128]{1,0:T(8,128)(2,1)S(1)} %sum_planes.1.refs_0_), channel_id=1, source_target_pairs={{0,1},{1,0},{2,3},{3,2},{4,5},{5,4},{6,7},{7,6},{8,9},{9,8},{10,11... | collective-permute-start | bytes 110600 | tf_op jit(solution)/shard_map/ppermute | solution.py:363

commit v8 on v7

--- a/solution.py
+++ b/solution.py
@@ -234,12 +234,8 @@
 
 
 def norm_kernel(chunk_rows, lengths_ref, index_ref, gain_ref, turned_ref, *refs):
-    attended, pixels, windows, grads = refs[-4:]
-    sources = attended.shape[0]
-    chunks = refs[:sources]
-    image_ref, near_ref, far_ref = refs[sources : sources + 3]
-    grad_refs = refs[sources + 3 : -4]
-    for distance, ref in enumerate(chunks):
+    image_ref, near_ref, far_ref, grad_ref, attended, pixels, windows, grads = refs[-8:]
+    for distance, ref in enumerate(refs[:-8]):
         attended[lax.bitwise_xor(index_ref[0], distance)] = ref[...]
     heads = gain_ref.shape[0]
     regions = image_ref.shape[0]
@@ -291,13 +287,12 @@
     filled = 9 * width
     if filled < grads.shape[0]:
         grads[filled:, :] = jnp.zeros((grads.shape[0] - filled, width), jnp.float32)
-    for distance, ref in enumerate(grad_refs):
-        start = lax.bitwise_xor(index_ref[1], distance) * chunk_rows
-        rows = pl.ds(pl.multiple_of(start, chunk_rows), chunk_rows)
-        ref[...] = grads[rows, :].astype(jnp.bfloat16)
-
-
-def decode_kernel(index_ref, image_ref, near_ref, far_ref, weight_ref, out_ref, padded):
+    for chunk in range(grad_ref.shape[0]):
+        grad_ref[chunk] = grads[chunk * chunk_rows : (chunk + 1) * chunk_rows, :].astype(jnp.bfloat16)
+
+
+def decode_kernel(index_ref, image_ref, near_ref, far_ref, weight_ref, out_ref, done_ref, padded):
+    done_ref[...] = jnp.zeros(done_ref.shape, jnp.float32)
     regions, rows, columns, width = image_ref.shape
     padded[:RIM, :] = jnp.zeros((RIM, width), jnp.float32)
     padded[RIM + columns :, :] = jnp.zeros((RIM, width), jnp.float32)
@@ -326,17 +321,19 @@
 def sum_kernel(count, factor, *refs):
     out_ref = refs[-1]
     totals = [ref[...].astype(jnp.float32) for ref in refs[:count]]
+    if count == 1:
+        totals = [totals[0][part] for part in range(totals[0].shape[0])]
     while len(totals) > 1:
         paired = [one + other for one, other in zip(totals[::2], totals[1::2])]
         totals = paired + totals[2 * len(paired) :]
     out_ref[...] = (totals[0] * factor).astype(jnp.bfloat16)
 
 
-def spread_kernel(index_ref, *refs):
+def spread_kernel(plane_ref, *refs):
     out_ref = refs[-1]
     chunk_rows = refs[0].shape[0]
     for distance, ref in enumerate(refs[:-1]):
-        start = lax.bitwise_xor(index_ref[1], distance) * chunk_rows
+        start = lax.bitwise_xor(plane_ref[0], distance) * chunk_rows
         rows = pl.ds(pl.multiple_of(start, chunk_rows), chunk_rows)
         out_ref[rows, :] = ref[...].astype(jnp.float32)
 
@@ -351,6 +348,14 @@
     while seq_count % (2 * inner) == 0 and (2 * inner) ** 2 <= seq_count:
         inner *= 2
     return inner
+
+
+def planes_of(inner):
+    outer, seq_count = (lax.axis_size("dp"), lax.axis_size("seq"))
+    return [
+        [o * seq_count + start + lane for o in range(outer) for lane in range(inner)]
+        for start in range(0, seq_count, inner)
+    ]
 
 
 def trade_in_plane(values, distance, inner):
@@ -370,7 +375,7 @@
     seq_index = lax.axis_index("seq")
     inner = inner_size(seq_count)
     plane_size = lax.axis_size("dp") * inner
-    plane_index = lax.axis_index("dp") * inner + lax.rem(seq_index, inner)
+    plane_index = lax.axis_index("dp") * inner + lax.bitwise_and(seq_index, inner - 1)
     columns = tokens * PATCH
     capacity = seq_count * tokens
     per_device = regions * HEADS // seq_count
@@ -380,7 +385,7 @@
 
     edge_shape = jax.ShapeDtypeStruct((regions, columns, width), jnp.bfloat16)
     chunk_shape = jax.ShapeDtypeStruct((3, per_device, tokens, width), jnp.bfloat16)
-    index = jnp.stack([seq_index, plane_index]).astype(jnp.int32)
+    index = seq_index.reshape(1)
     *leaving, cot_near, cot_far = call(
         functools.partial(pack_kernel, regions, per_device),
         "pack",
@@ -445,12 +450,12 @@
     pixel_rows = regions * PATCH * columns
     conv_flops = 18 * pixel_rows * width * width
     part_shape = jax.ShapeDtypeStruct((chunk_rows, width), jnp.bfloat16)
-    image, near, far, *parts = call(
+    image, near, far, parts = call(
         functools.partial(norm_kernel, chunk_rows),
         "norm_and_gradient",
         [jax.ShapeDtypeStruct((regions, PATCH, columns, width), jnp.bfloat16)]
         + [edge_shape] * 2
-        + [part_shape] * plane_size,
+        + [jax.ShapeDtypeStruct((plane_size, chunk_rows, width), jnp.bfloat16)],
         [SMEM(), SMEM()] + [VMEM()] * (2 + seq_count),
         scratch=[
             pltpu.VMEM((seq_count,) + mixed[0].shape, jnp.bfloat16),
@@ -461,44 +466,48 @@
         flops=conv_flops,
         moved=4 * local_bytes,
     )(region_lengths, index, norm_gain.reshape(HEADS, width), turned, *attended)
-    distances = range(1, plane_size)
-    parts[1:] = [trade_in_plane(parts[distance], distance, inner) for distance in distances]
+    parts = lax.all_to_all(
+        parts, ("dp", "seq"), 0, 0, axis_index_groups=planes_of(inner), tiled=True
+    )
     near = trade(near, 1)
     far = lax.ppermute(far, "seq", far_pairs)
     plane_sum = call(
-        functools.partial(sum_kernel, plane_size, 1.0),
+        functools.partial(sum_kernel, 1, 1.0),
         "sum_plane",
         part_shape,
-        [VMEM()] * plane_size,
-        moved=4 * plane_size * chunk_rows * width,
-    )(*parts)
+        [VMEM()],
+        moved=4 * parts.size,
+    )(parts)
     plane_sums = [plane_sum] + [
         trade(plane_sum, distance) for distance in range(inner, seq_count, inner)
     ]
-    total = call(
-        functools.partial(sum_kernel, len(plane_sums), 1.0 / math.sqrt(PATCH * columns)),
-        "sum_planes",
-        part_shape,
-        [VMEM()] * len(plane_sums) + [ANY(), ANY()],
-        moved=4 * len(plane_sums) * chunk_rows * width,
-    )(*plane_sums, near, far)
-    totals = [total] + [trade_in_plane(total, distance, inner) for distance in distances]
-    decoded = call(
+    decoded, done = call(
         decode_kernel,
         "decode",
-        jax.ShapeDtypeStruct(cotangent.shape, jnp.bfloat16),
+        [
+            jax.ShapeDtypeStruct(cotangent.shape, jnp.bfloat16),
+            jax.ShapeDtypeStruct((8, width), jnp.float32),
+        ],
         [SMEM()] + [VMEM()] * 4,
         scratch=[pltpu.VMEM((columns + 2 * RIM, width), jnp.float32)],
         flops=conv_flops,
         moved=2 * local_bytes,
     )(index, image, near, far, conv_weight.reshape(3, 3 * width, width))
+    total = call(
+        functools.partial(sum_kernel, len(plane_sums), 1.0 / math.sqrt(PATCH * columns)),
+        "sum_planes",
+        part_shape,
+        [VMEM()] * len(plane_sums) + [ANY()],
+        moved=4 * len(plane_sums) * chunk_rows * width,
+    )(*plane_sums, done)
+    totals = [total] + [trade_in_plane(total, distance, inner) for distance in range(1, plane_size)]
     weight_grad = call(
         spread_kernel,
         "spread_sums",
         jax.ShapeDtypeStruct((plane_size * chunk_rows, width), jnp.float32),
         [SMEM()] + [VMEM()] * plane_size,
         moved=6 * plane_size * chunk_rows * width,
-    )(index, *totals)
+    )(plane_index.reshape(1), *totals)
     return (decoded, weight_grad[: 9 * width].reshape(conv_weight.shape))
 
 

time: 105 us -> 98 us (0.933)
  starting transfers between devices: 57.3 us -> 52.9 us
  Pallas kernels: 15.6 us -> 13.3 us
    ppermute x14 -> x7, starting transfers between devices: 15.9 us -> 6.88 us  [trade_in_plane(): return lax.ppermute(values, ('dp', 'seq'), pairs)]
    all_to_all x0 -> x1, waiting for transfers between devices: none -> 3.97 us  [body(): lax.all_to_all(parts, ('dp', 'seq'), 0, 0, axis_index_groups=planes_of(in...]
    all_to_all x0 -> x1, starting transfers between devices: none -> 3.42 us  [body(): lax.all_to_all(parts, ('dp', 'seq'), 0, 0, axis_index_groups=planes_of(in...]
    ppermute x19, waiting for transfers between devices: 25.7 us -> 23.8 us  [trade(): return lax.ppermute(values, 'seq', pairs)]
    ppermute x14 -> x7, waiting for transfers between devices: 4.18 us -> 2.69 us  [trade_in_plane(): return lax.ppermute(values, ('dp', 'seq'), pairs)]
    ppermute x19, starting transfers between devices: 39.9 us -> 41.1 us  [trade(): return lax.ppermute(values, 'seq', pairs)]
  transfers between devices with their start and end apart: 35 -> 29, of which waited for: 13 -> 12; matrix products, arithmetic and copies ran while one was open for 0% -> 0% of each run, Pallas kernels for 6% -> 5%
where the time goes in v8:
time: 98 us; the launch traced here: 97.7 us
  starting transfers between devices  52.9 us (54%)
  waiting for transfers between devices  30.5 us (31%)
  Pallas kernels  13.3 us (14%)
    ppermute x19, starting transfers between devices, trade(): return lax.ppermute(values, 'seq', pairs)  41.1 us
    ppermute x19, waiting for transfers between devices, trade(): return lax.ppermute(values, 'seq', pairs)  23.8 us
    ppermute x7, starting transfers between devices, trade_in_plane(): return lax.ppermute(values, ('dp', 'seq'), pairs)  6.88 us
    all_to_all x1, waiting for transfers between devices, body(): lax.all_to_all(parts, ('dp', 'seq'), 0, 0, axis_index_groups=planes_of(in...  3.97 us
    pallas_call x1, Pallas kernels, body(): call(functools.partial(pack_kernel, regions, per_device), 'pack', [chunk_...  3.81 us
    pallas_call x1, Pallas kernels, body(): call(functools.partial(norm_kernel, chunk_rows), 'norm_and_gradient', [ja...  3.65 us
    all_to_all x1, starting transfers between devices, body(): lax.all_to_all(parts, ('dp', 'seq'), 0, 0, axis_index_groups=planes_of(in...  3.42 us
    ppermute x7, waiting for transfers between devices, trade_in_plane(): return lax.ppermute(values, ('dp', 'seq'), pairs)  2.69 us
  transfers between devices with their start and end apart: 29, of which 12 were waited for; matrix products, arithmetic and copies ran while one was open for 0% of the time, Pallas kernels for 5%

profile of v8, /device:TPU:0, one launch (start us, length us, event | category | flops | bytes accessed | tf_op | source)
XLA Modules:
  0.0 97.7 jit_solution(5972138986669846569)
XLA Ops:
  0.7 3.8 %pack.1 = (bf16[3,4,64,128]{3,2,1,0:T(8,128)(2,1)}, bf16[3,4,64,128]{3,2,1,0:T(8,128)(2,1)}, bf16[3,4,64,128]{3,2,1,0:T(8,128)(2,1)}, bf16[3,4,64,128]{3,2,1,0:T...) custom-call(s32[1]{0:T(128)} %bitcast.index_ref, ...), custom_call_target="tpu_custom_call" | custom-call | bytes 3145728 | tf_op jit(solution)/shard_map/pack/pallas_call | solution.py:389
  4.5 3.0 %collective-permute-start.2 = (bf16[3,4,64,128]{3,2,1,0:T(8,128)(2,1)}, bf16[3,4,64,128]{3,2,1,0:T(8,128)(2,1)S(1)}, u32[]{:S(2)}, u32[]{:S(2)}) collective-permute-start(bf16[3,4,64,128]{3,2,1,0:T(8,128)(2,1)} %get-tuple-element.27), channel_id=1, source_target_pairs={{0,1},{1,0},{2,3},{3,2},{4,5},{5,4},{6,7},{7,6},{8,9},{9,8},{10,11... | collective-permute-start | bytes 589832 | tf_op jit(solution)/shard_map/ppermute | solution.py:343
  7.5 1.6 %collective-permute-start.3 = (bf16[3,4,64,128]{3,2,1,0:T(8,128)(2,1)}, bf16[3,4,64,128]{3,2,1,0:T(8,128)(2,1)S(1)}, u32[]{:S(2)}, u32[]{:S(2)}) collective-permute-start(bf16[3,4,64,128]{3,2,1,0:T(8,128)(2,1)} %get-tuple-element.28), channel_id=1, source_target_pairs={{0,2},{1,3},{2,0},{3,1},{4,6},{5,7},{6,4},{7,5},{8,10},{9,11},{10,... | collective-permute-start | bytes 589832 | tf_op jit(solution)/shard_map/ppermute | solution.py:343
  9.1 0.0 collective-permute-start.4
  9.1 3.0 %collective-permute-start.5 = (bf16[3,4,64,128]{3,2,1,0:T(8,128)(2,1)}, bf16[3,4,64,128]{3,2,1,0:T(8,128)(2,1)S(1)}, u32[]{:S(2)}, u32[]{:S(2)}) collective-permute-start(bf16[3,4,64,128]{3,2,1,0:T(8,128)(2,1)} %get-tuple-element.30), channel_id=1, source_target_pairs={{0,4},{1,5},{2,6},{3,7},{4,0},{5,1},{6,2},{7,3},{8,12},{9,13},{10,... | collective-permute-start | bytes 589832 | tf_op jit(solution)/shard_map/ppermute | solution.py:343
  12.1 1.3 %collective-permute-start.6 = (bf16[3,4,64,128]{3,2,1,0:T(8,128)(2,1)}, bf16[3,4,64,128]{3,2,1,0:T(8,128)(2,1)S(1)}, u32[]{:S(2)}, u32[]{:S(2)}) collective-permute-start(bf16[3,4,64,128]{3,2,1,0:T(8,128)(2,1)} %get-tuple-element.31), channel_id=1, source_target_pairs={{0,5},{1,4},{2,7},{3,6},{4,1},{5,0},{6,3},{7,2},{8,13},{9,12},{10,... | collective-permute-start | bytes 589832 | tf_op jit(solution)/shard_map/ppermute | solution.py:343
  13.3 0.0 collective-permute-done.2.refs_0_
  13.3 3.6 %collective-permute-start.7 = (bf16[3,4,64,128]{3,2,1,0:T(8,128)(2,1)}, bf16[3,4,64,128]{3,2,1,0:T(8,128)(2,1)S(1)}, u32[]{:S(2)}, u32[]{:S(2)}) collective-permute-start(bf16[3,4,64,128]{3,2,1,0:T(8,128)(2,1)} %get-tuple-element.32), channel_id=1, source_target_pairs={{0,6},{1,7},{2,4},{3,5},{4,2},{5,3},{6,0},{7,1},{8,14},{9,15},{10,... | collective-permute-start | bytes 589832 | tf_op jit(solution)/shard_map/ppermute | solution.py:343
  16.9 6.2 %collective-permute-done.3.refs_1_ = bf16[3,4,64,128]{3,2,1,0:T(8,128)(2,1)S(1)} collective-permute-done((bf16[3,4,64,128]{3,2,1,0:T(8,128)(2,1)}, bf16[3,4,64,128]{3,2,1,0:T(8,128)(2,1)S(1)}, u32[]{:S(2)}, u32[]{:S(2)}) %collective-permute-start.3) | collective-permute-done | bytes 196640 | tf_op jit(solution)/shard_map/ppermute | solution.py:343
  23.2 0.9 collective-permute-start.8
  24.1 0.8 collective-permute-done.4.refs_2_
  24.9 2.5 %collective-permute-start = (bf16[2,256,128]{2,1,0:T(8,128)(2,1)}, bf16[2,256,128]{2,1,0:T(8,128)(2,1)S(1)}, u32[]{:S(2)}, u32[]{:S(2)}) collective-permute-start(bf16[2,256,128]{2,1,0:T(8,128)(2,1)} %get-tuple-element.25), channel_id=1, source_target_pairs={{0,1},{1,0},{2,3},{3,2},{4,5},{5,4},{6,7},{7,6},{8,9},{9,8},{10,11... | collective-permute-start | bytes 393224 | tf_op jit(solution)/shard_map/ppermute | solution.py:343
  27.4 0.0 collective-permute-done.5.refs_3_
  27.4 0.7 collective-permute-start.1
  28.1 0.1 fusion.lengths_ref
  28.2 0.0 copy-start
  28.2 0.4 own_chunk.1.refs_7_
  28.6 11.8 %collective-permute-done.6.refs_4_ = bf16[3,4,64,128]{3,2,1,0:T(8,128)(2,1)S(1)} collective-permute-done((bf16[3,4,64,128]{3,2,1,0:T(8,128)(2,1)}, bf16[3,4,64,128]{3,2,1,0:T(8,128)(2,1)S(1)}, u32[]{:S(2)}, u32[]{:S(2)}) %collective-permute-start.6) | collective-permute-done | bytes 196640 | tf_op jit(solution)/shard_map/ppermute | solution.py:343
  40.4 0.0 collective-permute-done.7.refs_5_
  40.4 0.0 collective-permute-done.8.refs_6_
  40.4 2.1 %attend.1 = (bf16[4,64,128]{2,1,0:T(8,128)(2,1)S(1)}, bf16[4,64,128]{2,1,0:T(8,128)(2,1)S(1)}, bf16[4,64,128]{2,1,0:T(8,128)(2,1)S(1)}, bf16[4,64,128]{2,1,0:T(8...) custom-call(s32[1]{0:T(128)} %bitcast.index_ref, ...), custom_call_target="tpu_custom_call" | custom-call | flops 536870912 | bytes 2097152 | tf_op jit(solution)/shard_map/attend/pallas_call | solution.py:431
  42.5 0.0 copy-start.5
  42.5 0.1 collective-permute-start.9
  42.6 9.3 %collective-permute-start.10 = (bf16[4,64,128]{2,1,0:T(8,128)(2,1)S(1)}, bf16[4,64,128]{2,1,0:T(8,128)(2,1)S(1)}, u32[]{:S(2)}, u32[]{:S(2)}) collective-permute-start(bf16[4,64,128]{2,1,0:T(8,128)(2,1)S(1)} %get-tuple-element.36), channel_id=1, source_target_pairs={{0,2},{1,3},{2,0},{3,1},{4,6},{5,7},{6,4},{7,5},{8,10},{9,11},{10,... | collective-permute-start | bytes 196616 | tf_op jit(solution)/shard_map/ppermute | solution.py:343
  51.9 0.0 collective-permute-start.11
  51.9 0.0 collective-permute-done.near_ref
  51.9 4.7 %collective-permute-start.12 = (bf16[4,64,128]{2,1,0:T(8,128)(2,1)S(1)}, bf16[4,64,128]{2,1,0:T(8,128)(2,1)S(1)}, u32[]{:S(2)}, u32[]{:S(2)}) collective-permute-start(bf16[4,64,128]{2,1,0:T(8,128)(2,1)S(1)} %get-tuple-element.38), channel_id=1, source_target_pairs={{0,4},{1,5},{2,6},{3,7},{4,0},{5,1},{6,2},{7,3},{8,12},{9,13},{10,... | collective-permute-start | bytes 196616 | tf_op jit(solution)/shard_map/ppermute | solution.py:343
  56.7 0.0 collective-permute-done.1.far_ref
  56.7 0.0 collective-permute-start.13
  56.7 0.0 collective-permute-done.9.refs_1_
  56.7 2.4 %collective-permute-start.14 = (bf16[4,64,128]{2,1,0:T(8,128)(2,1)S(1)}, bf16[4,64,128]{2,1,0:T(8,128)(2,1)S(1)}, u32[]{:S(2)}, u32[]{:S(2)}) collective-permute-start(bf16[4,64,128]{2,1,0:T(8,128)(2,1)S(1)} %get-tuple-element.40), channel_id=1, source_target_pairs={{0,6},{1,7},{2,4},{3,5},{4,2},{5,3},{6,0},{7,1},{8,14},{9,15},{10,... | collective-permute-start | bytes 196616 | tf_op jit(solution)/shard_map/ppermute | solution.py:343
  59.0 0.0 collective-permute-done.10.refs_2_
  59.0 2.4 %collective-permute-start.15 = (bf16[4,64,128]{2,1,0:T(8,128)(2,1)S(1)}, bf16[4,64,128]{2,1,0:T(8,128)(2,1)S(1)}, u32[]{:S(2)}, u32[]{:S(2)}) collective-permute-start(bf16[4,64,128]{2,1,0:T(8,128)(2,1)S(1)} %get-tuple-element.41), channel_id=1, source_target_pairs={{0,7},{1,6},{2,5},{3,4},{4,3},{5,2},{6,1},{7,0},{8,15},{9,14},{10,... | collective-permute-start | bytes 196616 | tf_op jit(solution)/shard_map/ppermute | solution.py:343
  61.5 0.3 turn_cotangent.1.turned_ref
  61.7 0.0 collective-permute-done.11.refs_3_
  61.8 0.1 collective-permute-done.12.refs_4_
  61.9 2.5 %collective-permute-done.13.refs_5_ = bf16[4,64,128]{2,1,0:T(8,128)(2,1)S(1)} collective-permute-done((bf16[4,64,128]{2,1,0:T(8,128)(2,1)S(1)}, bf16[4,64,128]{2,1,0:T(8,128)(2,1)S(1)}, u32[]{:S(2)}, u32[]{:S(2)}) %collective-permute-start.13) | collective-permute-done | bytes 65568 | tf_op jit(solution)/shard_map/ppermute | solution.py:343
  64.4 0.0 collective-permute-done.14.refs_6_
  64.4 1.7 %collective-permute-done.15.refs_7_ = bf16[4,64,128]{2,1,0:T(8,128)(2,1)S(1)} collective-permute-done((bf16[4,64,128]{2,1,0:T(8,128)(2,1)S(1)}, bf16[4,64,128]{2,1,0:T(8,128)(2,1)S(1)}, u32[]{:S(2)}, u32[]{:S(2)}) %collective-permute-start.15) | collective-permute-done | bytes 65568 | tf_op jit(solution)/shard_map/ppermute | solution.py:343
  66.1 3.6 %norm_and_gradient.1 = (bf16[2,4,256,128]{3,2,1,0:T(8,128)(2,1)S(1)}, bf16[2,256,128]{2,1,0:T(8,128)(2,1)S(1)}, bf16[2,256,128]{2,1,0:T(8,128)(2,1)S(1)}, bf16[8,144,128]{2,1,0:T(8,128)(2,1)}) custom-call(s32[2]{0:T(128)S(1)} %copy-done.6, s32[1]{0:T(128)} %bitcast.index_ref, f32[16,128]{1,0:T(8,128)S(1)} %bitcast.6, ...), custom_call_target="tpu_custom_call" | custom-call | flops 603979776 | bytes 2097152 | tf_op jit(solution)/shard_map/norm_and_gradient/pallas_call | solution.py:453
  69.8 3.4 %all-to-all-start = ((bf16[8,144,128]{2,1,0:T(8,128)(2,1)}), bf16[8,144,128]{2,1,0:T(8,128)(2,1)S(1)}, u32[]{:S(2)}, u32[]{:S(2)}) async-start(bf16[8,144,128]{2,1,0:T(8,128)(2,1)} %get-tuple-element.46), calls=%async_computation | async-start | bytes 589824 | tf_op jit(solution)/shard_map/all_to_all | solution.py:469
  73.2 1.9 %collective-permute-start.16 = (bf16[2,256,128]{2,1,0:T(8,128)(2,1)S(1)}, bf16[2,256,128]{2,1,0:T(8,128)(2,1)S(1)}, u32[]{:S(2)}, u32[]{:S(2)}) collective-permute-start(bf16[2,256,128]{2,1,0:T(8,128)(2,1)S(1)} %get-tuple-element.43), channel_id=1, source_target_pairs={{0,1},{1,0},{2,3},{3,2},{4,5},{5,4},{6,7},{7,6},{8,9},{9,8},{10,11... | collective-permute-start | bytes 393224 | tf_op jit(solution)/shard_map/ppermute | solution.py:343
  75.1 0.8 collective-permute-start.17
  76.0 4.0 %all-to-all-done.refs_0_ = bf16[8,144,128]{2,1,0:T(8,128)(2,1)S(1)} async-done(((bf16[8,144,128]{2,1,0:T(8,128)(2,1)}), bf16[8,144,128]{2,1,0:T(8,128)(2,1)S(1)}, u32[]{:S(2)}, u32[]{:S(2)}) %all-to-all-start) | async-done | bytes 294944 | tf_op jit(solution)/shard_map/all_to_all | solution.py:469
  80.0 1.6 %collective-permute-start.20 = (bf16[144,128]{1,0:T(8,128)(2,1)S(1)}, bf16[144,128]{1,0:T(8,128)(2,1)S(1)}, u32[]{:S(2)}, u32[]{:S(2)}) collective-permute-start(bf16[144,128]{1,0:T(8,128)(2,1)S(1)} %sum_plane.1.refs_0_), channel_id=1, source_target_pairs={{0,6},{1,7},{2,4},{3,5},{4,2},{5,3},{6,0},{7,1},{8,14},{9,15},{10,... | collective-permute-start | bytes 110600 | tf_op jit(solution)/shard_map/ppermute | solution.py:343
  81.6 1.0 %collective-permute-start.19 = (bf16[144,128]{1,0:T(8,128)(2,1)S(1)}, bf16[144,128]{1,0:T(8,128)(2,1)S(1)}, u32[]{:S(2)}, u32[]{:S(2)}) collective-permute-start(bf16[144,128]{1,0:T(8,128)(2,1)S(1)} %sum_plane.1.refs_0_), channel_id=1, source_target_pairs={{0,4},{1,5},{2,6},{3,7},{4,0},{5,1},{6,2},{7,3},{8,12},{9,13},{10,... | collective-permute-start | bytes 110600 | tf_op jit(solution)/shard_map/ppermute | solution.py:343
  82.6 1.9 %collective-permute-start.18 = (bf16[144,128]{1,0:T(8,128)(2,1)S(1)}, bf16[144,128]{1,0:T(8,128)(2,1)S(1)}, u32[]{:S(2)}, u32[]{:S(2)}) collective-permute-start(bf16[144,128]{1,0:T(8,128)(2,1)S(1)} %sum_plane.1.refs_0_), channel_id=1, source_target_pairs={{0,2},{1,3},{2,0},{3,1},{4,6},{5,7},{6,4},{7,5},{8,10},{9,11},{10,... | collective-permute-start | bytes 110600 | tf_op jit(solution)/shard_map/ppermute | solution.py:343
  84.4 0.0 collective-permute-done.16.near_ref
  84.4 0.0 collective-permute-done.17.far_ref
  84.4 2.2 %decode.1 = (bf16[2,4,256,128]{3,2,1,0:T(8,128)(2,1)}, f32[8,128]{1,0:T(8,128)S(1)}) custom-call(s32[1]{0:T(128)} %bitcast.index_ref, bf16[2,4,256,128]{3,2,1,0:T(8,128)(2,1)S(1)} %get-tuple-element.42.image_ref, bf16[2,256,128]{2,1,0:T(8,128)(2,1)S(1)} %collective-permute-done.16.near_ref, bf16[2,256,128]{2,1,0:T(8,128)(2,1)S(1)} %collective-permute-done.17.far_ref, ...), custom_call_target="tpu_custom_call" | custom-call | flops 603979776 | bytes 1048576 | tf_op jit(solution)/shard_map/decode/pallas_call | solution.py:484
  86.7 0.0 collective-permute-done.20.refs_3_
  86.7 0.3 collective-permute-done.19.refs_2_
  87.0 0.2 collective-permute-done.18.refs_1_
  87.2 0.9 collective-permute-start.27
  88.2 1.1 %collective-permute-start.26 = (bf16[144,128]{1,0:T(8,128)(2,1)S(1)}, bf16[144,128]{1,0:T(8,128)(2,1)S(1)}, u32[]{:S(2)}, u32[]{:S(2)}) collective-permute-start(bf16[144,128]{1,0:T(8,128)(2,1)S(1)} %sum_planes.1.refs_0_), channel_id=1, source_target_pairs={{0,24},{1,25},{2,26},{3,27},{4,28},{5,29},{6,30},{7,31},{8,16},{9,... | collective-permute-start | bytes 110600 | tf_op jit(solution)/shard_map/ppermute | solution.py:368
  89.2 1.7 %collective-permute-start.25 = (bf16[144,128]{1,0:T(8,128)(2,1)S(1)}, bf16[144,128]{1,0:T(8,128)(2,1)S(1)}, u32[]{:S(2)}, u32[]{:S(2)}) collective-permute-start(bf16[144,128]{1,0:T(8,128)(2,1)S(1)} %sum_planes.1.refs_0_), channel_id=1, source_target_pairs={{0,17},{1,16},{2,19},{3,18},{4,21},{5,20},{6,23},{7,22},{8,25},{9,... | collective-permute-start | bytes 110600 | tf_op jit(solution)/shard_map/ppermute | solution.py:368
  90.9 1.1 %collective-permute-start.24 = (bf16[144,128]{1,0:T(8,128)(2,1)S(1)}, bf16[144,128]{1,0:T(8,128)(2,1)S(1)}, u32[]{:S(2)}, u32[]{:S(2)}) collective-permute-start(bf16[144,128]{1,0:T(8,128)(2,1)S(1)} %sum_planes.1.refs_0_), channel_id=1, source_target_pairs={{0,16},{1,17},{2,18},{3,19},{4,20},{5,21},{6,22},{7,23},{8,24},{9,... | collective-permute-start | bytes 110600 | tf_op jit(solution)/shard_map/ppermute | solution.py:368
  92.0 0.9 collective-permute-start.22
  92.8 1.3 %collective-permute-start.21 = (bf16[144,128]{1,0:T(8,128)(2,1)S(1)}, bf16[144,128]{1,0:T(8,128)(2,1)S(1)}, u32[]{:S(2)}, u32[]{:S(2)}) collective-permute-start(bf16[144,128]{1,0:T(8,128)(2,1)S(1)} %sum_planes.1.refs_0_), channel_id=1, source_target_pairs={{0,1},{1,0},{2,3},{3,2},{4,5},{5,4},{6,7},{7,6},{8,9},{9,8},{10,11... | collective-permute-start | bytes 110600 | tf_op jit(solution)/shard_map/ppermute | solution.py:368
  94.1 0.7 collective-permute-done.24.refs_4_
  94.8 0.5 collective-permute-done.23.refs_3_
  95.3 0.0 collective-permute-done.22.refs_2_
  95.4 1.4 %collective-permute-done.21.refs_1_ = bf16[144,128]{1,0:T(8,128)(2,1)S(1)} collective-permute-done((bf16[144,128]{1,0:T(8,128)(2,1)S(1)}, bf16[144,128]{1,0:T(8,128)(2,1)S(1)}, u32[]{:S(2)}, u32[]{:S(2)}) %collective-permute-start.21) | collective-permute-done | bytes 36896 | tf_op jit(solution)/shard_map/ppermute | solution.py:368
  96.8 0.9 spread_sums.1
  (19 shorter events, 0.1 us)
Async XLA Ops:
  0.6 27.5 %copy-start.3 = (bf16[64,2,2048]{2,1,0:T(2,128)(2,1)S(1)}, bf16[64,2,2048]{2,1,0:T(2,128)(2,1)}, u32[]{:S(2)}) copy-start(bf16[64,2,2048]{2,1,0:T(2,128)(2,1)} %value_ref.3) | copy-start | bytes 1572868
  0.6 27.5 %copy-start.2 = (bf16[64,2,2048]{2,1,0:T(2,128)(2,1)S(1)}, bf16[64,2,2048]{2,1,0:T(2,128)(2,1)}, u32[]{:S(2)}) copy-start(bf16[64,2,2048]{2,1,0:T(2,128)(2,1)} %key_ref.3) | copy-start | bytes 1572868
  0.7 27.5 %copy-start.1 = (bf16[64,2,2048]{2,1,0:T(2,128)(2,1)S(1)}, bf16[64,2,2048]{2,1,0:T(2,128)(2,1)}, u32[]{:S(2)}) copy-start(bf16[64,2,2048]{2,1,0:T(2,128)(2,1)} %query_ref.3) | copy-start | bytes 1572868
  0.7 27.4 %copy-start.6 = (s32[2]{0:T(128)S(1)}, s32[2]{0:T(128)}, u32[]{:S(2)}) copy-start(s32[2]{0:T(128)} %lengths_ref.1) | copy-start | bytes 28
  4.5 8.9 %collective-permute-start.2 = (bf16[3,4,64,128]{3,2,1,0:T(8,128)(2,1)}, bf16[3,4,64,128]{3,2,1,0:T(8,128)(2,1)S(1)}, u32[]{:S(2)}, u32[]{:S(2)}) collective-permute-start(bf16[3,4,64,128]{3,2,1,0:T(8,128)(2,1)} %get-tuple-element.27), channel_id=1, source_target_pairs={{0,1},{1,0},{2,3},{3,2},{4,5},{5,4},{6,7},{7,6},{8,9},{9,8},{10,11... | collective-permute-start | bytes 589832 | tf_op jit(solution)/shard_map/ppermute | solution.py:343
  7.5 15.7 %collective-permute-start.3 = (bf16[3,4,64,128]{3,2,1,0:T(8,128)(2,1)}, bf16[3,4,64,128]{3,2,1,0:T(8,128)(2,1)S(1)}, u32[]{:S(2)}, u32[]{:S(2)}) collective-permute-start(bf16[3,4,64,128]{3,2,1,0:T(8,128)(2,1)} %get-tuple-element.28), channel_id=1, source_target_pairs={{0,2},{1,3},{2,0},{3,1},{4,6},{5,7},{6,4},{7,5},{8,10},{9,11},{10,... | collective-permute-start | bytes 589832 | tf_op jit(solution)/shard_map/ppermute | solution.py:343
  9.1 15.8 %collective-permute-start.4 = (bf16[3,4,64,128]{3,2,1,0:T(8,128)(2,1)}, bf16[3,4,64,128]{3,2,1,0:T(8,128)(2,1)S(1)}, u32[]{:S(2)}, u32[]{:S(2)}) collective-permute-start(bf16[3,4,64,128]{3,2,1,0:T(8,128)(2,1)} %get-tuple-element.29), channel_id=1, source_target_pairs={{0,3},{1,2},{2,1},{3,0},{4,7},{5,6},{6,5},{7,4},{8,11},{9,10},{10,... | collective-permute-start | bytes 589832 | tf_op jit(solution)/shard_map/ppermute | solution.py:343
  9.1 18.3 %collective-permute-start.5 = (bf16[3,4,64,128]{3,2,1,0:T(8,128)(2,1)}, bf16[3,4,64,128]{3,2,1,0:T(8,128)(2,1)S(1)}, u32[]{:S(2)}, u32[]{:S(2)}) collective-permute-start(bf16[3,4,64,128]{3,2,1,0:T(8,128)(2,1)} %get-tuple-element.30), channel_id=1, source_target_pairs={{0,4},{1,5},{2,6},{3,7},{4,0},{5,1},{6,2},{7,3},{8,12},{9,13},{10,... | collective-permute-start | bytes 589832 | tf_op jit(solution)/shard_map/ppermute | solution.py:343
  12.1 28.3 %collective-permute-start.6 = (bf16[3,4,64,128]{3,2,1,0:T(8,128)(2,1)}, bf16[3,4,64,128]{3,2,1,0:T(8,128)(2,1)S(1)}, u32[]{:S(2)}, u32[]{:S(2)}) collective-permute-start(bf16[3,4,64,128]{3,2,1,0:T(8,128)(2,1)} %get-tuple-element.31), channel_id=1, source_target_pairs={{0,5},{1,4},{2,7},{3,6},{4,1},{5,0},{6,3},{7,2},{8,13},{9,12},{10,... | collective-permute-start | bytes 589832 | tf_op jit(solution)/shard_map/ppermute | solution.py:343
  13.3 27.1 %collective-permute-start.7 = (bf16[3,4,64,128]{3,2,1,0:T(8,128)(2,1)}, bf16[3,4,64,128]{3,2,1,0:T(8,128)(2,1)S(1)}, u32[]{:S(2)}, u32[]{:S(2)}) collective-permute-start(bf16[3,4,64,128]{3,2,1,0:T(8,128)(2,1)} %get-tuple-element.32), channel_id=1, source_target_pairs={{0,6},{1,7},{2,4},{3,5},{4,2},{5,3},{6,0},{7,1},{8,14},{9,15},{10,... | collective-permute-start | bytes 589832 | tf_op jit(solution)/shard_map/ppermute | solution.py:343
  23.2 17.2 %collective-permute-start.8 = (bf16[3,4,64,128]{3,2,1,0:T(8,128)(2,1)}, bf16[3,4,64,128]{3,2,1,0:T(8,128)(2,1)S(1)}, u32[]{:S(2)}, u32[]{:S(2)}) collective-permute-start(bf16[3,4,64,128]{3,2,1,0:T(8,128)(2,1)} %get-tuple-element.33), channel_id=1, source_target_pairs={{0,7},{1,6},{2,5},{3,4},{4,3},{5,2},{6,1},{7,0},{8,15},{9,14},{10,... | collective-permute-start | bytes 589832 | tf_op jit(solution)/shard_map/ppermute | solution.py:343
  24.9 27.0 %collective-permute-start = (bf16[2,256,128]{2,1,0:T(8,128)(2,1)}, bf16[2,256,128]{2,1,0:T(8,128)(2,1)S(1)}, u32[]{:S(2)}, u32[]{:S(2)}) collective-permute-start(bf16[2,256,128]{2,1,0:T(8,128)(2,1)} %get-tuple-element.25), channel_id=1, source_target_pairs={{0,1},{1,0},{2,3},{3,2},{4,5},{5,4},{6,7},{7,6},{8,9},{9,8},{10,11... | collective-permute-start | bytes 393224 | tf_op jit(solution)/shard_map/ppermute | solution.py:343
  27.4 29.3 %collective-permute-start.1 = (bf16[2,256,128]{2,1,0:T(8,128)(2,1)}, bf16[2,256,128]{2,1,0:T(8,128)(2,1)S(1)}, u32[]{:S(2)}, u32[]{:S(2)}) collective-permute-start(bf16[2,256,128]{2,1,0:T(8,128)(2,1)} %get-tuple-element.26), channel_id=1, source_target_pairs={{1,2},{3,4},{5,6},{2,1},{4,3},{6,5},{9,10},{11,12},{13,14},{10,9},... | collective-permute-start | bytes 393224 | tf_op jit(solution)/shard_map/ppermute | solution.py:418
  28.2 33.3 %copy-start = (bf16[2,4,256,128]{3,2,1,0:T(8,128)(2,1)S(1)}, bf16[2,4,256,128]{3,2,1,0:T(8,128)(2,1)}, u32[]{:S(2)}) copy-start(bf16[2,4,256,128]{3,2,1,0:T(8,128)(2,1)} %cot_ref.3) | copy-start | bytes 1572868
  42.5 23.6 %copy-start.5 = (f32[2048]{0:T(1024)S(1)}, f32[2048]{0:T(1024)}, u32[]{:S(2)}) copy-start(f32[2048]{0:T(1024)} %param.11) | copy-start | bytes 24580
  42.5 14.2 %collective-permute-start.9 = (bf16[4,64,128]{2,1,0:T(8,128)(2,1)S(1)}, bf16[4,64,128]{2,1,0:T(8,128)(2,1)S(1)}, u32[]{:S(2)}, u32[]{:S(2)}) collective-permute-start(bf16[4,64,128]{2,1,0:T(8,128)(2,1)S(1)} %get-tuple-element.35), channel_id=1, source_target_pairs={{0,1},{1,0},{2,3},{3,2},{4,5},{5,4},{6,7},{7,6},{8,9},{9,8},{10,11... | collective-permute-start | bytes 196616 | tf_op jit(solution)/shard_map/ppermute | solution.py:343
  42.6 16.4 %collective-permute-start.10 = (bf16[4,64,128]{2,1,0:T(8,128)(2,1)S(1)}, bf16[4,64,128]{2,1,0:T(8,128)(2,1)S(1)}, u32[]{:S(2)}, u32[]{:S(2)}) collective-permute-start(bf16[4,64,128]{2,1,0:T(8,128)(2,1)S(1)} %get-tuple-element.36), channel_id=1, source_target_pairs={{0,2},{1,3},{2,0},{3,1},{4,6},{5,7},{6,4},{7,5},{8,10},{9,11},{10,... | collective-permute-start | bytes 196616 | tf_op jit(solution)/shard_map/ppermute | solution.py:343
  51.9 9.8 %collective-permute-start.11 = (bf16[4,64,128]{2,1,0:T(8,128)(2,1)S(1)}, bf16[4,64,128]{2,1,0:T(8,128)(2,1)S(1)}, u32[]{:S(2)}, u32[]{:S(2)}) collective-permute-start(bf16[4,64,128]{2,1,0:T(8,128)(2,1)S(1)} %get-tuple-element.37), channel_id=1, source_target_pairs={{0,3},{1,2},{2,1},{3,0},{4,7},{5,6},{6,5},{7,4},{8,11},{9,10},{10,... | collective-permute-start | bytes 196616 | tf_op jit(solution)/shard_map/ppermute | solution.py:343
  51.9 9.9 %collective-permute-start.12 = (bf16[4,64,128]{2,1,0:T(8,128)(2,1)S(1)}, bf16[4,64,128]{2,1,0:T(8,128)(2,1)S(1)}, u32[]{:S(2)}, u32[]{:S(2)}) collective-permute-start(bf16[4,64,128]{2,1,0:T(8,128)(2,1)S(1)} %get-tuple-element.38), channel_id=1, source_target_pairs={{0,4},{1,5},{2,6},{3,7},{4,0},{5,1},{6,2},{7,3},{8,12},{9,13},{10,... | collective-permute-start | bytes 196616 | tf_op jit(solution)/shard_map/ppermute | solution.py:343
  56.7 7.7 %collective-permute-start.13 = (bf16[4,64,128]{2,1,0:T(8,128)(2,1)S(1)}, bf16[4,64,128]{2,1,0:T(8,128)(2,1)S(1)}, u32[]{:S(2)}, u32[]{:S(2)}) collective-permute-start(bf16[4,64,128]{2,1,0:T(8,128)(2,1)S(1)} %get-tuple-element.39), channel_id=1, source_target_pairs={{0,5},{1,4},{2,7},{3,6},{4,1},{5,0},{6,3},{7,2},{8,13},{9,12},{10,... | collective-permute-start | bytes 196616 | tf_op jit(solution)/shard_map/ppermute | solution.py:343
  56.7 7.7 %collective-permute-start.14 = (bf16[4,64,128]{2,1,0:T(8,128)(2,1)S(1)}, bf16[4,64,128]{2,1,0:T(8,128)(2,1)S(1)}, u32[]{:S(2)}, u32[]{:S(2)}) collective-permute-start(bf16[4,64,128]{2,1,0:T(8,128)(2,1)S(1)} %get-tuple-element.40), channel_id=1, source_target_pairs={{0,6},{1,7},{2,4},{3,5},{4,2},{5,3},{6,0},{7,1},{8,14},{9,15},{10,... | collective-permute-start | bytes 196616 | tf_op jit(solution)/shard_map/ppermute | solution.py:343
  59.0 7.1 %collective-permute-start.15 = (bf16[4,64,128]{2,1,0:T(8,128)(2,1)S(1)}, bf16[4,64,128]{2,1,0:T(8,128)(2,1)S(1)}, u32[]{:S(2)}, u32[]{:S(2)}) collective-permute-start(bf16[4,64,128]{2,1,0:T(8,128)(2,1)S(1)} %get-tuple-element.41), channel_id=1, source_target_pairs={{0,7},{1,6},{2,5},{3,4},{4,3},{5,2},{6,1},{7,0},{8,15},{9,14},{10,... | collective-permute-start | bytes 196616 | tf_op jit(solution)/shard_map/ppermute | solution.py:343
  66.1 18.3 %copy-start.4 = (bf16[9,128,128]{2,1,0:T(8,128)(2,1)S(1)}, bf16[9,128,128]{2,1,0:T(8,128)(2,1)}, u32[]{:S(2)}) copy-start(bf16[9,128,128]{2,1,0:T(8,128)(2,1)} %param.12) | copy-start | bytes 884740
  69.8 10.2 %all-to-all-start = ((bf16[8,144,128]{2,1,0:T(8,128)(2,1)}), bf16[8,144,128]{2,1,0:T(8,128)(2,1)S(1)}, u32[]{:S(2)}, u32[]{:S(2)}) async-start(bf16[8,144,128]{2,1,0:T(8,128)(2,1)} %get-tuple-element.46), calls=%async_computation | async-start | bytes 589824 | tf_op jit(solution)/shard_map/all_to_all | solution.py:469
  73.2 11.2 %collective-permute-start.16 = (bf16[2,256,128]{2,1,0:T(8,128)(2,1)S(1)}, bf16[2,256,128]{2,1,0:T(8,128)(2,1)S(1)}, u32[]{:S(2)}, u32[]{:S(2)}) collective-permute-start(bf16[2,256,128]{2,1,0:T(8,128)(2,1)S(1)} %get-tuple-element.43), channel_id=1, source_target_pairs={{0,1},{1,0},{2,3},{3,2},{4,5},{5,4},{6,7},{7,6},{8,9},{9,8},{10,11... | collective-permute-start | bytes 393224 | tf_op jit(solution)/shard_map/ppermute | solution.py:343
  75.1 9.3 %collective-permute-start.17 = (bf16[2,256,128]{2,1,0:T(8,128)(2,1)S(1)}, bf16[2,256,128]{2,1,0:T(8,128)(2,1)S(1)}, u32[]{:S(2)}, u32[]{:S(2)}) collective-permute-start(bf16[2,256,128]{2,1,0:T(8,128)(2,1)S(1)} %get-tuple-element.44), channel_id=1, source_target_pairs={{1,2},{3,4},{5,6},{2,1},{4,3},{6,5},{9,10},{11,12},{13,14},{10,9},... | collective-permute-start | bytes 393224 | tf_op jit(solution)/shard_map/ppermute | solution.py:473
  80.0 6.7 %collective-permute-start.20 = (bf16[144,128]{1,0:T(8,128)(2,1)S(1)}, bf16[144,128]{1,0:T(8,128)(2,1)S(1)}, u32[]{:S(2)}, u32[]{:S(2)}) collective-permute-start(bf16[144,128]{1,0:T(8,128)(2,1)S(1)} %sum_plane.1.refs_0_), channel_id=1, source_target_pairs={{0,6},{1,7},{2,4},{3,5},{4,2},{5,3},{6,0},{7,1},{8,14},{9,15},{10,... | collective-permute-start | bytes 110600 | tf_op jit(solution)/shard_map/ppermute | solution.py:343
  81.6 5.4 %collective-permute-start.19 = (bf16[144,128]{1,0:T(8,128)(2,1)S(1)}, bf16[144,128]{1,0:T(8,128)(2,1)S(1)}, u32[]{:S(2)}, u32[]{:S(2)}) collective-permute-start(bf16[144,128]{1,0:T(8,128)(2,1)S(1)} %sum_plane.1.refs_0_), channel_id=1, source_target_pairs={{0,4},{1,5},{2,6},{3,7},{4,0},{5,1},{6,2},{7,3},{8,12},{9,13},{10,... | collective-permute-start | bytes 110600 | tf_op jit(solution)/shard_map/ppermute | solution.py:343
  82.6 4.6 %collective-permute-start.18 = (bf16[144,128]{1,0:T(8,128)(2,1)S(1)}, bf16[144,128]{1,0:T(8,128)(2,1)S(1)}, u32[]{:S(2)}, u32[]{:S(2)}) collective-permute-start(bf16[144,128]{1,0:T(8,128)(2,1)S(1)} %sum_plane.1.refs_0_), channel_id=1, source_target_pairs={{0,2},{1,3},{2,0},{3,1},{4,6},{5,7},{6,4},{7,5},{8,10},{9,11},{10,... | collective-permute-start | bytes 110600 | tf_op jit(solution)/shard_map/ppermute | solution.py:343
  87.2 4.7 %collective-permute-start.27 = (bf16[144,128]{1,0:T(8,128)(2,1)S(1)}, bf16[144,128]{1,0:T(8,128)(2,1)S(1)}, u32[]{:S(2)}, u32[]{:S(2)}) collective-permute-start(bf16[144,128]{1,0:T(8,128)(2,1)S(1)} %sum_planes.1.refs_0_), channel_id=1, source_target_pairs={{0,25},{1,24},{2,27},{3,26},{4,29},{5,28},{6,31},{7,30},{8,17},{9,... | collective-permute-start | bytes 110600 | tf_op jit(solution)/shard_map/ppermute | solution.py:368
  88.2 4.7 %collective-permute-start.26 = (bf16[144,128]{1,0:T(8,128)(2,1)S(1)}, bf16[144,128]{1,0:T(8,128)(2,1)S(1)}, u32[]{:S(2)}, u32[]{:S(2)}) collective-permute-start(bf16[144,128]{1,0:T(8,128)(2,1)S(1)} %sum_planes.1.refs_0_), channel_id=1, source_target_pairs={{0,24},{1,25},{2,26},{3,27},{4,28},{5,29},{6,30},{7,31},{8,16},{9,... | collective-permute-start | bytes 110600 | tf_op jit(solution)/shard_map/ppermute | solution.py:368
  89.2 4.9 %collective-permute-start.25 = (bf16[144,128]{1,0:T(8,128)(2,1)S(1)}, bf16[144,128]{1,0:T(8,128)(2,1)S(1)}, u32[]{:S(2)}, u32[]{:S(2)}) collective-permute-start(bf16[144,128]{1,0:T(8,128)(2,1)S(1)} %sum_planes.1.refs_0_), channel_id=1, source_target_pairs={{0,17},{1,16},{2,19},{3,18},{4,21},{5,20},{6,23},{7,22},{8,25},{9,... | collective-permute-start | bytes 110600 | tf_op jit(solution)/shard_map/ppermute | solution.py:368
  90.9 4.0 %collective-permute-start.24 = (bf16[144,128]{1,0:T(8,128)(2,1)S(1)}, bf16[144,128]{1,0:T(8,128)(2,1)S(1)}, u32[]{:S(2)}, u32[]{:S(2)}) collective-permute-start(bf16[144,128]{1,0:T(8,128)(2,1)S(1)} %sum_planes.1.refs_0_), channel_id=1, source_target_pairs={{0,16},{1,17},{2,18},{3,19},{4,20},{5,21},{6,22},{7,23},{8,24},{9,... | collective-permute-start | bytes 110600 | tf_op jit(solution)/shard_map/ppermute | solution.py:368
  92.0 3.4 %collective-permute-start.23 = (bf16[144,128]{1,0:T(8,128)(2,1)S(1)}, bf16[144,128]{1,0:T(8,128)(2,1)S(1)}, u32[]{:S(2)}, u32[]{:S(2)}) collective-permute-start(bf16[144,128]{1,0:T(8,128)(2,1)S(1)} %sum_planes.1.refs_0_), channel_id=1, source_target_pairs={{0,9},{1,8},{2,11},{3,10},{4,13},{5,12},{6,15},{7,14},{8,1},{9,0},... | collective-permute-start | bytes 110600 | tf_op jit(solution)/shard_map/ppermute | solution.py:368
  92.0 3.4 %collective-permute-start.22 = (bf16[144,128]{1,0:T(8,128)(2,1)S(1)}, bf16[144,128]{1,0:T(8,128)(2,1)S(1)}, u32[]{:S(2)}, u32[]{:S(2)}) collective-permute-start(bf16[144,128]{1,0:T(8,128)(2,1)S(1)} %sum_planes.1.refs_0_), channel_id=1, source_target_pairs={{0,8},{1,9},{2,10},{3,11},{4,12},{5,13},{6,14},{7,15},{8,0},{9,1},... | collective-permute-start | bytes 110600 | tf_op jit(solution)/shard_map/ppermute | solution.py:368
  92.8 4.0 %collective-permute-start.21 = (bf16[144,128]{1,0:T(8,128)(2,1)S(1)}, bf16[144,128]{1,0:T(8,128)(2,1)S(1)}, u32[]{:S(2)}, u32[]{:S(2)}) collective-permute-start(bf16[144,128]{1,0:T(8,128)(2,1)S(1)} %sum_planes.1.refs_0_), channel_id=1, source_target_pairs={{0,1},{1,0},{2,3},{3,2},{4,5},{5,4},{6,7},{7,6},{8,9},{9,8},{10,11... | collective-permute-start | bytes 110600 | tf_op jit(solution)/shard_map/ppermute | solution.py:368

commit v9 on v7

--- a/solution.py
+++ b/solution.py
@@ -215,6 +215,10 @@
     )
 
 
+def rows_at(place, rows):
+    return pl.ds(pl.multiple_of(place * rows, rows), rows)
+
+
 def around(odd, near, far):
     return jnp.where(odd == 1, near, far), jnp.where(odd == 1, far, near)
 
@@ -233,13 +237,12 @@
                     out_ref[down * width : (down + 1) * width, start : start + columns] = turned
 
 
-def norm_kernel(chunk_rows, lengths_ref, index_ref, gain_ref, turned_ref, *refs):
+def norm_kernel(lengths_ref, index_ref, quad_ref, gain_ref, turned_ref, *refs):
     attended, pixels, windows, grads = refs[-4:]
     sources = attended.shape[0]
-    chunks = refs[:sources]
     image_ref, near_ref, far_ref = refs[sources : sources + 3]
     grad_refs = refs[sources + 3 : -4]
-    for distance, ref in enumerate(chunks):
+    for distance, ref in enumerate(refs[:sources]):
         attended[lax.bitwise_xor(index_ref[0], distance)] = ref[...]
     heads = gain_ref.shape[0]
     regions = image_ref.shape[0]
@@ -292,8 +295,7 @@
     if filled < grads.shape[0]:
         grads[filled:, :] = jnp.zeros((grads.shape[0] - filled, width), jnp.float32)
     for distance, ref in enumerate(grad_refs):
-        start = lax.bitwise_xor(index_ref[1], distance) * chunk_rows
-        rows = pl.ds(pl.multiple_of(start, chunk_rows), chunk_rows)
+        rows = rows_at(lax.bitwise_xor(quad_ref[0], distance), ref.shape[0])
         ref[...] = grads[rows, :].astype(jnp.bfloat16)
 
 
@@ -323,21 +325,38 @@
                 strips.pop(0)
 
 
+def add_pairs(terms):
+    while len(terms) > 1:
+        paired = [one + other for one, other in zip(terms[::2], terms[1::2])]
+        terms = paired + terms[2 * len(paired) :]
+    return terms[0]
+
+
+def sum_chips_kernel(core_ref, near_ref, far_ref, *refs):
+    keep_ref, send_ref, near_out_ref, far_out_ref, total = refs[-5:]
+    total[...] = add_pairs([ref[...].astype(jnp.float32) for ref in refs[:-5]])
+    half = keep_ref.shape[0]
+    keep_ref[...] = total[rows_at(core_ref[0], half), :]
+    send_ref[...] = total[rows_at(1 - core_ref[0], half), :]
+    near_out_ref[...] = near_ref[...]
+    far_out_ref[...] = far_ref[...]
+
+
 def sum_kernel(count, factor, *refs):
+    total = add_pairs([ref[...].astype(jnp.float32) for ref in refs[:count]])
+    refs[-1][...] = (total * factor).astype(jnp.bfloat16)
+
+
+def join_kernel(core_ref, own_ref, other_ref, out_ref):
+    half = own_ref.shape[0]
+    out_ref[rows_at(core_ref[0], half), :] = own_ref[...]
+    out_ref[rows_at(1 - core_ref[0], half), :] = other_ref[...]
+
+
+def spread_kernel(quad_ref, *refs):
     out_ref = refs[-1]
-    totals = [ref[...].astype(jnp.float32) for ref in refs[:count]]
-    while len(totals) > 1:
-        paired = [one + other for one, other in zip(totals[::2], totals[1::2])]
-        totals = paired + totals[2 * len(paired) :]
-    out_ref[...] = (totals[0] * factor).astype(jnp.bfloat16)
-
-
-def spread_kernel(index_ref, *refs):
-    out_ref = refs[-1]
-    chunk_rows = refs[0].shape[0]
     for distance, ref in enumerate(refs[:-1]):
-        start = lax.bitwise_xor(index_ref[1], distance) * chunk_rows
-        rows = pl.ds(pl.multiple_of(start, chunk_rows), chunk_rows)
+        rows = rows_at(lax.bitwise_xor(quad_ref[0], distance), ref.shape[0])
         out_ref[rows, :] = ref[...].astype(jnp.float32)
 
 
@@ -353,14 +372,19 @@
     return inner
 
 
-def trade_in_plane(values, distance, inner):
+def trade_chips(values, distance, inner):
     seq_count = lax.axis_size("seq")
     pairs = []
     for outer in range(lax.axis_size("dp")):
         for seq in range(seq_count):
-            partner, lane = divmod((outer * inner + seq % inner) ^ distance, inner)
-            pairs.append((outer * seq_count + seq, partner * seq_count + seq - seq % inner + lane))
+            chip, lane = divmod((outer // 2 * inner + seq % inner) ^ distance, inner)
+            partner = (2 * chip + outer % 2) * seq_count + seq - seq % inner + lane
+            pairs.append((outer * seq_count + seq, partner))
     return lax.ppermute(values, ("dp", "seq"), pairs)
+
+
+def trade_cores(values):
+    return lax.ppermute(values, "dp", [(i, i ^ 1) for i in range(lax.axis_size("dp"))])
 
 
 def body(query_rows, key_rows, value_rows, region_lengths, norm_gain, conv_weight, cotangent):
@@ -369,8 +393,11 @@
     seq_count = lax.axis_size("seq")
     seq_index = lax.axis_index("seq")
     inner = inner_size(seq_count)
-    plane_size = lax.axis_size("dp") * inner
-    plane_index = lax.axis_index("dp") * inner + lax.rem(seq_index, inner)
+    quad_size = lax.axis_size("dp") // 2 * inner
+    dp_index = lax.axis_index("dp")
+    lane = lax.bitwise_and(seq_index, inner - 1)
+    quad = (lax.shift_right_logical(dp_index, 1) * inner + lane).reshape(1)
+    core = lax.bitwise_and(dp_index, 1).reshape(1)
     columns = tokens * PATCH
     capacity = seq_count * tokens
     per_device = regions * HEADS // seq_count
@@ -380,7 +407,7 @@
 
     edge_shape = jax.ShapeDtypeStruct((regions, columns, width), jnp.bfloat16)
     chunk_shape = jax.ShapeDtypeStruct((3, per_device, tokens, width), jnp.bfloat16)
-    index = jnp.stack([seq_index, plane_index]).astype(jnp.int32)
+    index = seq_index.reshape(1)
     *leaving, cot_near, cot_far = call(
         functools.partial(pack_kernel, regions, per_device),
         "pack",
@@ -441,48 +468,64 @@
         [SMEM()] + [VMEM()] * 3,
         moved=8 * cotangent.size,
     )(index, cotangent, cot_near, cot_far)
-    chunk_rows = -(-9 * width // (16 * plane_size)) * 16
+    chunk_rows = -(-9 * width // (32 * quad_size)) * 32
     pixel_rows = regions * PATCH * columns
     conv_flops = 18 * pixel_rows * width * width
-    part_shape = jax.ShapeDtypeStruct((chunk_rows, width), jnp.bfloat16)
+    chunk_moved = 8 * quad_size * chunk_rows * width
     image, near, far, *parts = call(
-        functools.partial(norm_kernel, chunk_rows),
+        norm_kernel,
         "norm_and_gradient",
         [jax.ShapeDtypeStruct((regions, PATCH, columns, width), jnp.bfloat16)]
         + [edge_shape] * 2
-        + [part_shape] * plane_size,
-        [SMEM(), SMEM()] + [VMEM()] * (2 + seq_count),
+        + [jax.ShapeDtypeStruct((chunk_rows, width), jnp.bfloat16)] * quad_size,
+        [SMEM()] * 3 + [VMEM()] * (2 + seq_count),
         scratch=[
             pltpu.VMEM((seq_count,) + mixed[0].shape, jnp.bfloat16),
             pltpu.VMEM((regions, PATCH, columns + 2 * RIM, width), jnp.float32),
             pltpu.VMEM((pixel_rows, 3 * width), jnp.bfloat16),
-            pltpu.VMEM((plane_size * chunk_rows, width), jnp.float32),
+            pltpu.VMEM((quad_size * chunk_rows, width), jnp.float32),
         ],
         flops=conv_flops,
         moved=4 * local_bytes,
-    )(region_lengths, index, norm_gain.reshape(HEADS, width), turned, *attended)
-    distances = range(1, plane_size)
-    parts[1:] = [trade_in_plane(parts[distance], distance, inner) for distance in distances]
+    )(region_lengths, index, quad, norm_gain.reshape(HEADS, width), turned, *attended)
+    distances = range(1, quad_size)
+    parts[1:] = [trade_chips(parts[distance], distance, inner) for distance in distances]
+    half_shape = (chunk_rows // 2, width)
+    keep, send, near, far = call(
+        sum_chips_kernel,
+        "sum_chips",
+        [jax.ShapeDtypeStruct(half_shape, jnp.float32)] * 2 + [edge_shape] * 2,
+        [SMEM()] + [VMEM()] * (2 + quad_size),
+        scratch=[pltpu.VMEM((chunk_rows, width), jnp.float32)],
+        moved=chunk_moved,
+    )(core, near, far, *parts)
+    plane_sum = call(
+        functools.partial(sum_kernel, 2, 1.0),
+        "sum_cores",
+        jax.ShapeDtypeStruct(half_shape, jnp.bfloat16),
+        [VMEM()] * 2,
+        moved=chunk_moved // quad_size,
+    )(keep, trade_cores(send))
     near = trade(near, 1)
     far = lax.ppermute(far, "seq", far_pairs)
-    plane_sum = call(
-        functools.partial(sum_kernel, plane_size, 1.0),
-        "sum_plane",
-        part_shape,
-        [VMEM()] * plane_size,
-        moved=4 * plane_size * chunk_rows * width,
-    )(*parts)
     plane_sums = [plane_sum] + [
         trade(plane_sum, distance) for distance in range(inner, seq_count, inner)
     ]
     total = call(
         functools.partial(sum_kernel, len(plane_sums), 1.0 / math.sqrt(PATCH * columns)),
         "sum_planes",
-        part_shape,
-        [VMEM()] * len(plane_sums) + [ANY(), ANY()],
-        moved=4 * len(plane_sums) * chunk_rows * width,
+        jax.ShapeDtypeStruct(half_shape, jnp.bfloat16),
+        [VMEM()] * len(plane_sums) + [ANY()] * 2,
+        moved=chunk_moved // quad_size,
     )(*plane_sums, near, far)
-    totals = [total] + [trade_in_plane(total, distance, inner) for distance in distances]
+    joined = call(
+        join_kernel,
+        "join_cores",
+        jax.ShapeDtypeStruct((chunk_rows, width), jnp.bfloat16),
+        [SMEM()] + [VMEM()] * 2,
+        moved=chunk_moved // quad_size,
+    )(core, total, trade_cores(total))
+    totals = [joined] + [trade_chips(joined, distance, inner) for distance in distances]
     decoded = call(
         decode_kernel,
         "decode",
@@ -495,10 +538,10 @@
     weight_grad = call(
         spread_kernel,
         "spread_sums",
-        jax.ShapeDtypeStruct((plane_size * chunk_rows, width), jnp.float32),
-        [SMEM()] + [VMEM()] * plane_size,
-        moved=6 * plane_size * chunk_rows * width,
-    )(index, *totals)
+        jax.ShapeDtypeStruct((quad_size * chunk_rows, width), jnp.float32),
+        [SMEM()] + [VMEM()] * quad_size,
+        moved=chunk_moved,
+    )(quad, *totals)
     return (decoded, weight_grad[: 9 * width].reshape(conv_weight.shape))
 
 

time: 105 us -> 99.2 us (0.945)
  starting transfers between devices: 57.3 us -> 49.6 us
  waiting for transfers between devices: 29.9 us -> 35 us
  Pallas kernels: 15.6 us -> 13.2 us
    ppermute x14 -> x8, starting transfers between devices: 15.9 us -> 7.25 us  [the longest x6 7.11 us: trade_chips(): return lax.ppermute(values, ('dp', 'seq'), pairs)]
    ppermute x14 -> x8, waiting for transfers between devices: 4.18 us -> 7.76 us  [the longest x6 5.3 us: trade_chips(): return lax.ppermute(values, ('dp', 'seq'), pairs)]
    ppermute x19, waiting for transfers between devices: 25.7 us -> 27.2 us  [trade(): return lax.ppermute(values, 'seq', pairs)]
    ppermute x19, starting transfers between devices: 39.9 us -> 41.1 us  [trade(): return lax.ppermute(values, 'seq', pairs)]
    pallas_call x3 -> x5, Pallas kernels: 4.48 us -> 4.01 us  [the longest x1 3.06 us: body(): call(norm_kernel, 'norm_and_gradient', [jax.ShapeDtypeStruct((regions, PA...]
  transfers between devices with their start and end apart: 35 -> 29, of which waited for: 13 -> 15; matrix products, arithmetic and copies ran while one was open for 0% -> 0% of each run, Pallas kernels for 6% -> 5%
where the time goes in v9:
time: 99.2 us; the launch traced here: 98.8 us
  starting transfers between devices  49.6 us (50%)
  waiting for transfers between devices  35 us (35%)
  Pallas kernels  13.2 us (13%)
    ppermute x19, starting transfers between devices, trade(): return lax.ppermute(values, 'seq', pairs)  41.1 us
    ppermute x19, waiting for transfers between devices, trade(): return lax.ppermute(values, 'seq', pairs)  27.2 us
    ppermute x6, starting transfers between devices, trade_chips(): return lax.ppermute(values, ('dp', 'seq'), pairs)  7.11 us
    ppermute x6, waiting for transfers between devices, trade_chips(): return lax.ppermute(values, ('dp', 'seq'), pairs)  5.3 us
    pallas_call x1, Pallas kernels, body(): call(functools.partial(pack_kernel, regions, per_device), 'pack', [chunk_...  3.81 us
    pallas_call x1, Pallas kernels, body(): call(norm_kernel, 'norm_and_gradient', [jax.ShapeDtypeStruct((regions, PA...  3.06 us
    pallas_call x1, Pallas kernels, body(): call(functools.partial(attend_kernel, block_rows, group, order), 'attend'...  2.48 us
    ppermute x2, waiting for transfers between devices, trade_cores(): lax.ppermute(values, 'dp', [(i, i ^ 1) for i in range(lax.axis_size('dp'))])  2.45 us
  transfers between devices with their start and end apart: 29, of which 15 were waited for; matrix products, arithmetic and copies ran while one was open for 0% of the time, Pallas kernels for 5%

profile of v9, /device:TPU:0, one launch (start us, length us, event | category | flops | bytes accessed | tf_op | source)
XLA Modules:
  0.0 98.8 jit_solution(12254332371647742091)
XLA Ops:
  0.7 3.8 %pack.1 = (bf16[3,4,64,128]{3,2,1,0:T(8,128)(2,1)}, bf16[3,4,64,128]{3,2,1,0:T(8,128)(2,1)}, bf16[3,4,64,128]{3,2,1,0:T(8,128)(2,1)}, bf16[3,4,64,128]{3,2,1,0:T...) custom-call(s32[1]{0:T(128)} %bitcast.index_ref, ...), custom_call_target="tpu_custom_call" | custom-call | bytes 3145728 | tf_op jit(solution)/shard_map/pack/pallas_call | solution.py:411
  4.5 3.0 %collective-permute-start.2 = (bf16[3,4,64,128]{3,2,1,0:T(8,128)(2,1)}, bf16[3,4,64,128]{3,2,1,0:T(8,128)(2,1)S(1)}, u32[]{:S(2)}, u32[]{:S(2)}) collective-permute-start(bf16[3,4,64,128]{3,2,1,0:T(8,128)(2,1)} %get-tuple-element.32), channel_id=1, source_target_pairs={{0,1},{1,0},{2,3},{3,2},{4,5},{5,4},{6,7},{7,6},{8,9},{9,8},{10,11... | collective-permute-start | bytes 589832 | tf_op jit(solution)/shard_map/ppermute | solution.py:365
  7.5 1.6 %collective-permute-start.3 = (bf16[3,4,64,128]{3,2,1,0:T(8,128)(2,1)}, bf16[3,4,64,128]{3,2,1,0:T(8,128)(2,1)S(1)}, u32[]{:S(2)}, u32[]{:S(2)}) collective-permute-start(bf16[3,4,64,128]{3,2,1,0:T(8,128)(2,1)} %get-tuple-element.33), channel_id=1, source_target_pairs={{0,2},{1,3},{2,0},{3,1},{4,6},{5,7},{6,4},{7,5},{8,10},{9,11},{10,... | collective-permute-start | bytes 589832 | tf_op jit(solution)/shard_map/ppermute | solution.py:365
  9.1 0.0 collective-permute-start.4
  9.1 3.0 %collective-permute-start.5 = (bf16[3,4,64,128]{3,2,1,0:T(8,128)(2,1)}, bf16[3,4,64,128]{3,2,1,0:T(8,128)(2,1)S(1)}, u32[]{:S(2)}, u32[]{:S(2)}) collective-permute-start(bf16[3,4,64,128]{3,2,1,0:T(8,128)(2,1)} %get-tuple-element.35), channel_id=1, source_target_pairs={{0,4},{1,5},{2,6},{3,7},{4,0},{5,1},{6,2},{7,3},{8,12},{9,13},{10,... | collective-permute-start | bytes 589832 | tf_op jit(solution)/shard_map/ppermute | solution.py:365
  12.1 1.3 %collective-permute-start.6 = (bf16[3,4,64,128]{3,2,1,0:T(8,128)(2,1)}, bf16[3,4,64,128]{3,2,1,0:T(8,128)(2,1)S(1)}, u32[]{:S(2)}, u32[]{:S(2)}) collective-permute-start(bf16[3,4,64,128]{3,2,1,0:T(8,128)(2,1)} %get-tuple-element.36), channel_id=1, source_target_pairs={{0,5},{1,4},{2,7},{3,6},{4,1},{5,0},{6,3},{7,2},{8,13},{9,12},{10,... | collective-permute-start | bytes 589832 | tf_op jit(solution)/shard_map/ppermute | solution.py:365
  13.3 3.6 %collective-permute-start.7 = (bf16[3,4,64,128]{3,2,1,0:T(8,128)(2,1)}, bf16[3,4,64,128]{3,2,1,0:T(8,128)(2,1)S(1)}, u32[]{:S(2)}, u32[]{:S(2)}) collective-permute-start(bf16[3,4,64,128]{3,2,1,0:T(8,128)(2,1)} %get-tuple-element.37), channel_id=1, source_target_pairs={{0,6},{1,7},{2,4},{3,5},{4,2},{5,3},{6,0},{7,1},{8,14},{9,15},{10,... | collective-permute-start | bytes 589832 | tf_op jit(solution)/shard_map/ppermute | solution.py:365
  16.9 6.2 %collective-permute-done.3.refs_1_ = bf16[3,4,64,128]{3,2,1,0:T(8,128)(2,1)S(1)} collective-permute-done((bf16[3,4,64,128]{3,2,1,0:T(8,128)(2,1)}, bf16[3,4,64,128]{3,2,1,0:T(8,128)(2,1)S(1)}, u32[]{:S(2)}, u32[]{:S(2)}) %collective-permute-start.3) | collective-permute-done | bytes 196640 | tf_op jit(solution)/shard_map/ppermute | solution.py:365
  23.2 0.9 collective-permute-start.8
  24.1 0.8 collective-permute-done.4.refs_2_
  24.9 2.5 %collective-permute-start = (bf16[2,256,128]{2,1,0:T(8,128)(2,1)}, bf16[2,256,128]{2,1,0:T(8,128)(2,1)S(1)}, u32[]{:S(2)}, u32[]{:S(2)}) collective-permute-start(bf16[2,256,128]{2,1,0:T(8,128)(2,1)} %get-tuple-element.30), channel_id=1, source_target_pairs={{0,1},{1,0},{2,3},{3,2},{4,5},{5,4},{6,7},{7,6},{8,9},{9,8},{10,11... | collective-permute-start | bytes 393224 | tf_op jit(solution)/shard_map/ppermute | solution.py:365
  27.4 0.7 collective-permute-start.1
  28.1 0.1 fusion.lengths_ref
  28.2 0.0 copy-start
  28.2 0.4 own_chunk.1.refs_7_
  28.6 11.8 %collective-permute-done.6.refs_4_ = bf16[3,4,64,128]{3,2,1,0:T(8,128)(2,1)S(1)} collective-permute-done((bf16[3,4,64,128]{3,2,1,0:T(8,128)(2,1)}, bf16[3,4,64,128]{3,2,1,0:T(8,128)(2,1)S(1)}, u32[]{:S(2)}, u32[]{:S(2)}) %collective-permute-start.6) | collective-permute-done | bytes 196640 | tf_op jit(solution)/shard_map/ppermute | solution.py:365
  40.4 0.0 collective-permute-done.7.refs_5_
  40.4 0.0 collective-permute-done.8.refs_6_
  40.4 2.5 %attend.1 = (bf16[4,64,128]{2,1,0:T(8,128)(2,1)S(1)}, bf16[4,64,128]{2,1,0:T(8,128)(2,1)S(1)}, bf16[4,64,128]{2,1,0:T(8,128)(2,1)S(1)}, bf16[4,64,128]{2,1,0:T(8...) custom-call(s32[1]{0:T(128)} %bitcast.index_ref, ...), custom_call_target="tpu_custom_call" | custom-call | flops 536870912 | bytes 2097152 | tf_op jit(solution)/shard_map/attend/pallas_call | solution.py:453
  42.9 0.0 copy-start.5
  42.9 0.1 collective-permute-start.9
  43.0 9.3 %collective-permute-start.10 = (bf16[4,64,128]{2,1,0:T(8,128)(2,1)S(1)}, bf16[4,64,128]{2,1,0:T(8,128)(2,1)S(1)}, u32[]{:S(2)}, u32[]{:S(2)}) collective-permute-start(bf16[4,64,128]{2,1,0:T(8,128)(2,1)S(1)} %get-tuple-element.41), channel_id=1, source_target_pairs={{0,2},{1,3},{2,0},{3,1},{4,6},{5,7},{6,4},{7,5},{8,10},{9,11},{10,... | collective-permute-start | bytes 196616 | tf_op jit(solution)/shard_map/ppermute | solution.py:365
  52.3 0.0 collective-permute-start.11
  52.3 0.0 collective-permute-done.near_ref
  52.3 4.7 %collective-permute-start.12 = (bf16[4,64,128]{2,1,0:T(8,128)(2,1)S(1)}, bf16[4,64,128]{2,1,0:T(8,128)(2,1)S(1)}, u32[]{:S(2)}, u32[]{:S(2)}) collective-permute-start(bf16[4,64,128]{2,1,0:T(8,128)(2,1)S(1)} %get-tuple-element.43), channel_id=1, source_target_pairs={{0,4},{1,5},{2,6},{3,7},{4,0},{5,1},{6,2},{7,3},{8,12},{9,13},{10,... | collective-permute-start | bytes 196616 | tf_op jit(solution)/shard_map/ppermute | solution.py:365
  57.1 0.0 collective-permute-done.1.far_ref
  57.1 0.0 collective-permute-start.13
  57.1 0.0 collective-permute-done.9.refs_1_
  57.1 2.4 %collective-permute-start.14 = (bf16[4,64,128]{2,1,0:T(8,128)(2,1)S(1)}, bf16[4,64,128]{2,1,0:T(8,128)(2,1)S(1)}, u32[]{:S(2)}, u32[]{:S(2)}) collective-permute-start(bf16[4,64,128]{2,1,0:T(8,128)(2,1)S(1)} %get-tuple-element.45), channel_id=1, source_target_pairs={{0,6},{1,7},{2,4},{3,5},{4,2},{5,3},{6,0},{7,1},{8,14},{9,15},{10,... | collective-permute-start | bytes 196616 | tf_op jit(solution)/shard_map/ppermute | solution.py:365
  59.4 2.4 %collective-permute-start.15 = (bf16[4,64,128]{2,1,0:T(8,128)(2,1)S(1)}, bf16[4,64,128]{2,1,0:T(8,128)(2,1)S(1)}, u32[]{:S(2)}, u32[]{:S(2)}) collective-permute-start(bf16[4,64,128]{2,1,0:T(8,128)(2,1)S(1)} %get-tuple-element.46), channel_id=1, source_target_pairs={{0,7},{1,6},{2,5},{3,4},{4,3},{5,2},{6,1},{7,0},{8,15},{9,14},{10,... | collective-permute-start | bytes 196616 | tf_op jit(solution)/shard_map/ppermute | solution.py:365
  61.9 0.3 turn_cotangent.1.turned_ref
  62.1 0.0 collective-permute-done.11.refs_3_
  62.2 0.0 collective-permute-done.12.refs_4_
  62.2 2.3 %collective-permute-done.13.refs_5_ = bf16[4,64,128]{2,1,0:T(8,128)(2,1)S(1)} collective-permute-done((bf16[4,64,128]{2,1,0:T(8,128)(2,1)S(1)}, bf16[4,64,128]{2,1,0:T(8,128)(2,1)S(1)}, u32[]{:S(2)}, u32[]{:S(2)}) %collective-permute-start.13) | collective-permute-done | bytes 65568 | tf_op jit(solution)/shard_map/ppermute | solution.py:365
  64.5 0.0 collective-permute-done.14.refs_6_
  64.5 2.0 %collective-permute-done.15.refs_7_ = bf16[4,64,128]{2,1,0:T(8,128)(2,1)S(1)} collective-permute-done((bf16[4,64,128]{2,1,0:T(8,128)(2,1)S(1)}, bf16[4,64,128]{2,1,0:T(8,128)(2,1)S(1)}, u32[]{:S(2)}, u32[]{:S(2)}) %collective-permute-start.15) | collective-permute-done | bytes 65568 | tf_op jit(solution)/shard_map/ppermute | solution.py:365
  66.5 3.1 %norm_and_gradient.1 = (bf16[2,4,256,128]{3,2,1,0:T(8,128)(2,1)S(1)}, bf16[2,256,128]{2,1,0:T(8,128)(2,1)S(1)}, bf16[2,256,128]{2,1,0:T(8,128)(2,1)S(1)}, bf16[2...) custom-call(s32[2]{0:T(128)S(1)} %copy-done.6, ...), custom_call_target="tpu_custom_call" | custom-call | flops 603979776 | bytes 2097152 | tf_op jit(solution)/shard_map/norm_and_gradient/pallas_call | solution.py:475
  69.6 1.4 %collective-permute-start.16 = (bf16[288,128]{1,0:T(8,128)(2,1)S(1)}, bf16[288,128]{1,0:T(8,128)(2,1)S(1)}, u32[]{:S(2)}, u32[]{:S(2)}) collective-permute-start(bf16[288,128]{1,0:T(8,128)(2,1)S(1)} %get-tuple-element.51), channel_id=1, source_target_pairs={{0,1},{1,0},{2,3},{3,2},{4,5},{5,4},{6,7},{7,6},{8,9},{9,8},{10,11... | collective-permute-start | bytes 221192 | tf_op jit(solution)/shard_map/ppermute | solution.py:383
  71.0 1.6 %collective-permute-start.17 = (bf16[288,128]{1,0:T(8,128)(2,1)S(1)}, bf16[288,128]{1,0:T(8,128)(2,1)S(1)}, u32[]{:S(2)}, u32[]{:S(2)}) collective-permute-start(bf16[288,128]{1,0:T(8,128)(2,1)S(1)} %get-tuple-element.52), channel_id=1, source_target_pairs={{0,16},{1,17},{2,18},{3,19},{4,20},{5,21},{6,22},{7,23},{8,24},{9,... | collective-permute-start | bytes 221192 | tf_op jit(solution)/shard_map/ppermute | solution.py:383
  72.6 0.6 collective-permute-start.18
  73.1 1.5 %collective-permute-done.16.refs_1_ = bf16[288,128]{1,0:T(8,128)(2,1)S(1)} collective-permute-done((bf16[288,128]{1,0:T(8,128)(2,1)S(1)}, bf16[288,128]{1,0:T(8,128)(2,1)S(1)}, u32[]{:S(2)}, u32[]{:S(2)}) %collective-permute-start.16) | collective-permute-done | bytes 73760 | tf_op jit(solution)/shard_map/ppermute | solution.py:383
  74.6 0.7 collective-permute-done.17.refs_2_
  75.3 2.5 %collective-permute-done.18.refs_3_ = bf16[288,128]{1,0:T(8,128)(2,1)S(1)} collective-permute-done((bf16[288,128]{1,0:T(8,128)(2,1)S(1)}, bf16[288,128]{1,0:T(8,128)(2,1)S(1)}, u32[]{:S(2)}, u32[]{:S(2)}) %collective-permute-start.18) | collective-permute-done | bytes 73760 | tf_op jit(solution)/shard_map/ppermute | solution.py:383
  77.8 0.1 sum_chips.1
  77.9 0.6 collective-permute-start.19
  78.5 0.7 collective-permute-start.20
  79.2 0.1 collective-permute-start.21
  79.2 1.3 %collective-permute-done.21.refs_1_ = f32[144,128]{1,0:T(8,128)S(1)} collective-permute-done((f32[144,128]{1,0:T(8,128)S(1)}, f32[144,128]{1,0:T(8,128)S(1)}, u32[]{:S(2)}, u32[]{:S(2)}) %collective-permute-start.21) | collective-permute-done | bytes 73760 | tf_op jit(solution)/shard_map/ppermute | solution.py:387
  80.5 3.9 %collective-permute-start.24 = (bf16[144,128]{1,0:T(8,128)(2,1)S(1)}, bf16[144,128]{1,0:T(8,128)(2,1)S(1)}, u32[]{:S(2)}, u32[]{:S(2)}) collective-permute-start(bf16[144,128]{1,0:T(8,128)(2,1)S(1)} %sum_cores.1.refs_0_), channel_id=1, source_target_pairs={{0,6},{1,7},{2,4},{3,5},{4,2},{5,3},{6,0},{7,1},{8,14},{9,15},{10,... | collective-permute-start | bytes 110600 | tf_op jit(solution)/shard_map/ppermute | solution.py:365
  84.4 1.8 %collective-permute-start.23 = (bf16[144,128]{1,0:T(8,128)(2,1)S(1)}, bf16[144,128]{1,0:T(8,128)(2,1)S(1)}, u32[]{:S(2)}, u32[]{:S(2)}) collective-permute-start(bf16[144,128]{1,0:T(8,128)(2,1)S(1)} %sum_cores.1.refs_0_), channel_id=1, source_target_pairs={{0,4},{1,5},{2,6},{3,7},{4,0},{5,1},{6,2},{7,3},{8,12},{9,13},{10,... | collective-permute-start | bytes 110600 | tf_op jit(solution)/shard_map/ppermute | solution.py:365
  86.2 0.4 collective-permute-done.24.refs_3_
  86.7 3.0 %collective-permute-done.23.refs_2_ = bf16[144,128]{1,0:T(8,128)(2,1)S(1)} collective-permute-done((bf16[144,128]{1,0:T(8,128)(2,1)S(1)}, bf16[144,128]{1,0:T(8,128)(2,1)S(1)}, u32[]{:S(2)}, u32[]{:S(2)}) %collective-permute-start.23) | collective-permute-done | bytes 36896 | tf_op jit(solution)/shard_map/ppermute | solution.py:365
  89.7 0.5 collective-permute-done.22.refs_1_
  90.2 0.0 collective-permute-done.19.near_ref.refs_4_
  90.2 0.0 collective-permute-done.20.far_ref.refs_5_
  90.2 0.1 collective-permute-start.25
  90.3 1.2 %collective-permute-done.25.other_ref = bf16[144,128]{1,0:T(8,128)(2,1)S(1)} collective-permute-done((bf16[144,128]{1,0:T(8,128)(2,1)S(1)}, bf16[144,128]{1,0:T(8,128)(2,1)S(1)}, u32[]{:S(2)}, u32[]{:S(2)}) %collective-permute-start.25) | collective-permute-done | bytes 36896 | tf_op jit(solution)/shard_map/ppermute | solution.py:387
  91.5 0.7 collective-permute-start.28
  92.3 1.1 %collective-permute-start.27 = (bf16[288,128]{1,0:T(8,128)(2,1)S(1)}, bf16[288,128]{1,0:T(8,128)(2,1)S(1)}, u32[]{:S(2)}, u32[]{:S(2)}) collective-permute-start(bf16[288,128]{1,0:T(8,128)(2,1)S(1)} %join_cores.1.refs_0_), channel_id=1, source_target_pairs={{0,16},{1,17},{2,18},{3,19},{4,20},{5,21},{6,22},{7,23},{8,24},{9,... | collective-permute-start | bytes 221192 | tf_op jit(solution)/shard_map/ppermute | solution.py:383
  93.4 1.7 %collective-permute-start.26 = (bf16[288,128]{1,0:T(8,128)(2,1)S(1)}, bf16[288,128]{1,0:T(8,128)(2,1)S(1)}, u32[]{:S(2)}, u32[]{:S(2)}) collective-permute-start(bf16[288,128]{1,0:T(8,128)(2,1)S(1)} %join_cores.1.refs_0_), channel_id=1, source_target_pairs={{0,1},{1,0},{2,3},{3,2},{4,5},{5,4},{6,7},{7,6},{8,9},{9,8},{10,11... | collective-permute-start | bytes 221192 | tf_op jit(solution)/shard_map/ppermute | solution.py:383
  95.1 2.2 %decode.1 = bf16[2,4,256,128]{3,2,1,0:T(8,128)(2,1)} custom-call(s32[1]{0:T(128)} %bitcast.index_ref, bf16[2,4,256,128]{3,2,1,0:T(8,128)(2,1)S(1)} %get-tuple-element.47.image_ref, bf16[2,256,128]{2,1,0:T(8,128)(2,1)S(1)} %collective-permute-done.19.near_ref.refs_4_, bf16[2,256,128]{2,1,0:T(8,128)(2,1)S(1)} %collective-permute-done.20.far_ref.refs_5_, ...), custom_call_target="tpu_custom_call" | custom-call | flops 603979776 | bytes 1048576 | tf_op jit(solution)/shard_map/decode/pallas_call | solution.py:529
  97.3 0.3 collective-permute-done.28.refs_3_
  97.6 0.3 collective-permute-done.27.refs_2_
  97.9 0.9 spread_sums.1
  (21 shorter events, 0.1 us)
Async XLA Ops:
  0.6 27.5 %copy-start.3 = (bf16[64,2,2048]{2,1,0:T(2,128)(2,1)S(1)}, bf16[64,2,2048]{2,1,0:T(2,128)(2,1)}, u32[]{:S(2)}) copy-start(bf16[64,2,2048]{2,1,0:T(2,128)(2,1)} %value_ref.3) | copy-start | bytes 1572868
  0.6 27.5 %copy-start.2 = (bf16[64,2,2048]{2,1,0:T(2,128)(2,1)S(1)}, bf16[64,2,2048]{2,1,0:T(2,128)(2,1)}, u32[]{:S(2)}) copy-start(bf16[64,2,2048]{2,1,0:T(2,128)(2,1)} %key_ref.3) | copy-start | bytes 1572868
  0.7 27.5 %copy-start.1 = (bf16[64,2,2048]{2,1,0:T(2,128)(2,1)S(1)}, bf16[64,2,2048]{2,1,0:T(2,128)(2,1)}, u32[]{:S(2)}) copy-start(bf16[64,2,2048]{2,1,0:T(2,128)(2,1)} %query_ref.3) | copy-start | bytes 1572868
  0.7 27.4 %copy-start.6 = (s32[2]{0:T(128)S(1)}, s32[2]{0:T(128)}, u32[]{:S(2)}) copy-start(s32[2]{0:T(128)} %lengths_ref.1) | copy-start | bytes 28
  4.5 8.9 %collective-permute-start.2 = (bf16[3,4,64,128]{3,2,1,0:T(8,128)(2,1)}, bf16[3,4,64,128]{3,2,1,0:T(8,128)(2,1)S(1)}, u32[]{:S(2)}, u32[]{:S(2)}) collective-permute-start(bf16[3,4,64,128]{3,2,1,0:T(8,128)(2,1)} %get-tuple-element.32), channel_id=1, source_target_pairs={{0,1},{1,0},{2,3},{3,2},{4,5},{5,4},{6,7},{7,6},{8,9},{9,8},{10,11... | collective-permute-start | bytes 589832 | tf_op jit(solution)/shard_map/ppermute | solution.py:365
  7.5 15.7 %collective-permute-start.3 = (bf16[3,4,64,128]{3,2,1,0:T(8,128)(2,1)}, bf16[3,4,64,128]{3,2,1,0:T(8,128)(2,1)S(1)}, u32[]{:S(2)}, u32[]{:S(2)}) collective-permute-start(bf16[3,4,64,128]{3,2,1,0:T(8,128)(2,1)} %get-tuple-element.33), channel_id=1, source_target_pairs={{0,2},{1,3},{2,0},{3,1},{4,6},{5,7},{6,4},{7,5},{8,10},{9,11},{10,... | collective-permute-start | bytes 589832 | tf_op jit(solution)/shard_map/ppermute | solution.py:365
  9.1 15.8 %collective-permute-start.4 = (bf16[3,4,64,128]{3,2,1,0:T(8,128)(2,1)}, bf16[3,4,64,128]{3,2,1,0:T(8,128)(2,1)S(1)}, u32[]{:S(2)}, u32[]{:S(2)}) collective-permute-start(bf16[3,4,64,128]{3,2,1,0:T(8,128)(2,1)} %get-tuple-element.34), channel_id=1, source_target_pairs={{0,3},{1,2},{2,1},{3,0},{4,7},{5,6},{6,5},{7,4},{8,11},{9,10},{10,... | collective-permute-start | bytes 589832 | tf_op jit(solution)/shard_map/ppermute | solution.py:365
  9.1 18.3 %collective-permute-start.5 = (bf16[3,4,64,128]{3,2,1,0:T(8,128)(2,1)}, bf16[3,4,64,128]{3,2,1,0:T(8,128)(2,1)S(1)}, u32[]{:S(2)}, u32[]{:S(2)}) collective-permute-start(bf16[3,4,64,128]{3,2,1,0:T(8,128)(2,1)} %get-tuple-element.35), channel_id=1, source_target_pairs={{0,4},{1,5},{2,6},{3,7},{4,0},{5,1},{6,2},{7,3},{8,12},{9,13},{10,... | collective-permute-start | bytes 589832 | tf_op jit(solution)/shard_map/ppermute | solution.py:365
  12.1 28.3 %collective-permute-start.6 = (bf16[3,4,64,128]{3,2,1,0:T(8,128)(2,1)}, bf16[3,4,64,128]{3,2,1,0:T(8,128)(2,1)S(1)}, u32[]{:S(2)}, u32[]{:S(2)}) collective-permute-start(bf16[3,4,64,128]{3,2,1,0:T(8,128)(2,1)} %get-tuple-element.36), channel_id=1, source_target_pairs={{0,5},{1,4},{2,7},{3,6},{4,1},{5,0},{6,3},{7,2},{8,13},{9,12},{10,... | collective-permute-start | bytes 589832 | tf_op jit(solution)/shard_map/ppermute | solution.py:365
  13.3 27.1 %collective-permute-start.7 = (bf16[3,4,64,128]{3,2,1,0:T(8,128)(2,1)}, bf16[3,4,64,128]{3,2,1,0:T(8,128)(2,1)S(1)}, u32[]{:S(2)}, u32[]{:S(2)}) collective-permute-start(bf16[3,4,64,128]{3,2,1,0:T(8,128)(2,1)} %get-tuple-element.37), channel_id=1, source_target_pairs={{0,6},{1,7},{2,4},{3,5},{4,2},{5,3},{6,0},{7,1},{8,14},{9,15},{10,... | collective-permute-start | bytes 589832 | tf_op jit(solution)/shard_map/ppermute | solution.py:365
  23.2 17.2 %collective-permute-start.8 = (bf16[3,4,64,128]{3,2,1,0:T(8,128)(2,1)}, bf16[3,4,64,128]{3,2,1,0:T(8,128)(2,1)S(1)}, u32[]{:S(2)}, u32[]{:S(2)}) collective-permute-start(bf16[3,4,64,128]{3,2,1,0:T(8,128)(2,1)} %get-tuple-element.38), channel_id=1, source_target_pairs={{0,7},{1,6},{2,5},{3,4},{4,3},{5,2},{6,1},{7,0},{8,15},{9,14},{10,... | collective-permute-start | bytes 589832 | tf_op jit(solution)/shard_map/ppermute | solution.py:365
  24.9 27.4 %collective-permute-start = (bf16[2,256,128]{2,1,0:T(8,128)(2,1)}, bf16[2,256,128]{2,1,0:T(8,128)(2,1)S(1)}, u32[]{:S(2)}, u32[]{:S(2)}) collective-permute-start(bf16[2,256,128]{2,1,0:T(8,128)(2,1)} %get-tuple-element.30), channel_id=1, source_target_pairs={{0,1},{1,0},{2,3},{3,2},{4,5},{5,4},{6,7},{7,6},{8,9},{9,8},{10,11... | collective-permute-start | bytes 393224 | tf_op jit(solution)/shard_map/ppermute | solution.py:365
  27.4 29.7 %collective-permute-start.1 = (bf16[2,256,128]{2,1,0:T(8,128)(2,1)}, bf16[2,256,128]{2,1,0:T(8,128)(2,1)S(1)}, u32[]{:S(2)}, u32[]{:S(2)}) collective-permute-start(bf16[2,256,128]{2,1,0:T(8,128)(2,1)} %get-tuple-element.31), channel_id=1, source_target_pairs={{1,2},{3,4},{5,6},{2,1},{4,3},{6,5},{9,10},{11,12},{13,14},{10,9},... | collective-permute-start | bytes 393224 | tf_op jit(solution)/shard_map/ppermute | solution.py:440
  28.2 33.7 %copy-start = (bf16[2,4,256,128]{3,2,1,0:T(8,128)(2,1)S(1)}, bf16[2,4,256,128]{3,2,1,0:T(8,128)(2,1)}, u32[]{:S(2)}) copy-start(bf16[2,4,256,128]{3,2,1,0:T(8,128)(2,1)} %cot_ref.3) | copy-start | bytes 1572868
  42.9 23.6 %copy-start.5 = (f32[2048]{0:T(1024)S(1)}, f32[2048]{0:T(1024)}, u32[]{:S(2)}) copy-start(f32[2048]{0:T(1024)} %param.11) | copy-start | bytes 24580
  42.9 14.2 %collective-permute-start.9 = (bf16[4,64,128]{2,1,0:T(8,128)(2,1)S(1)}, bf16[4,64,128]{2,1,0:T(8,128)(2,1)S(1)}, u32[]{:S(2)}, u32[]{:S(2)}) collective-permute-start(bf16[4,64,128]{2,1,0:T(8,128)(2,1)S(1)} %get-tuple-element.40), channel_id=1, source_target_pairs={{0,1},{1,0},{2,3},{3,2},{4,5},{5,4},{6,7},{7,6},{8,9},{9,8},{10,11... | collective-permute-start | bytes 196616 | tf_op jit(solution)/shard_map/ppermute | solution.py:365
  43.0 16.4 %collective-permute-start.10 = (bf16[4,64,128]{2,1,0:T(8,128)(2,1)S(1)}, bf16[4,64,128]{2,1,0:T(8,128)(2,1)S(1)}, u32[]{:S(2)}, u32[]{:S(2)}) collective-permute-start(bf16[4,64,128]{2,1,0:T(8,128)(2,1)S(1)} %get-tuple-element.41), channel_id=1, source_target_pairs={{0,2},{1,3},{2,0},{3,1},{4,6},{5,7},{6,4},{7,5},{8,10},{9,11},{10,... | collective-permute-start | bytes 196616 | tf_op jit(solution)/shard_map/ppermute | solution.py:365
  52.3 9.8 %collective-permute-start.11 = (bf16[4,64,128]{2,1,0:T(8,128)(2,1)S(1)}, bf16[4,64,128]{2,1,0:T(8,128)(2,1)S(1)}, u32[]{:S(2)}, u32[]{:S(2)}) collective-permute-start(bf16[4,64,128]{2,1,0:T(8,128)(2,1)S(1)} %get-tuple-element.42), channel_id=1, source_target_pairs={{0,3},{1,2},{2,1},{3,0},{4,7},{5,6},{6,5},{7,4},{8,11},{9,10},{10,... | collective-permute-start | bytes 196616 | tf_op jit(solution)/shard_map/ppermute | solution.py:365
  52.3 9.9 %collective-permute-start.12 = (bf16[4,64,128]{2,1,0:T(8,128)(2,1)S(1)}, bf16[4,64,128]{2,1,0:T(8,128)(2,1)S(1)}, u32[]{:S(2)}, u32[]{:S(2)}) collective-permute-start(bf16[4,64,128]{2,1,0:T(8,128)(2,1)S(1)} %get-tuple-element.43), channel_id=1, source_target_pairs={{0,4},{1,5},{2,6},{3,7},{4,0},{5,1},{6,2},{7,3},{8,12},{9,13},{10,... | collective-permute-start | bytes 196616 | tf_op jit(solution)/shard_map/ppermute | solution.py:365
  57.1 7.4 %collective-permute-start.13 = (bf16[4,64,128]{2,1,0:T(8,128)(2,1)S(1)}, bf16[4,64,128]{2,1,0:T(8,128)(2,1)S(1)}, u32[]{:S(2)}, u32[]{:S(2)}) collective-permute-start(bf16[4,64,128]{2,1,0:T(8,128)(2,1)S(1)} %get-tuple-element.44), channel_id=1, source_target_pairs={{0,5},{1,4},{2,7},{3,6},{4,1},{5,0},{6,3},{7,2},{8,13},{9,12},{10,... | collective-permute-start | bytes 196616 | tf_op jit(solution)/shard_map/ppermute | solution.py:365
  57.1 7.4 %collective-permute-start.14 = (bf16[4,64,128]{2,1,0:T(8,128)(2,1)S(1)}, bf16[4,64,128]{2,1,0:T(8,128)(2,1)S(1)}, u32[]{:S(2)}, u32[]{:S(2)}) collective-permute-start(bf16[4,64,128]{2,1,0:T(8,128)(2,1)S(1)} %get-tuple-element.45), channel_id=1, source_target_pairs={{0,6},{1,7},{2,4},{3,5},{4,2},{5,3},{6,0},{7,1},{8,14},{9,15},{10,... | collective-permute-start | bytes 196616 | tf_op jit(solution)/shard_map/ppermute | solution.py:365
  59.4 7.1 %collective-permute-start.15 = (bf16[4,64,128]{2,1,0:T(8,128)(2,1)S(1)}, bf16[4,64,128]{2,1,0:T(8,128)(2,1)S(1)}, u32[]{:S(2)}, u32[]{:S(2)}) collective-permute-start(bf16[4,64,128]{2,1,0:T(8,128)(2,1)S(1)} %get-tuple-element.46), channel_id=1, source_target_pairs={{0,7},{1,6},{2,5},{3,4},{4,3},{5,2},{6,1},{7,0},{8,15},{9,14},{10,... | collective-permute-start | bytes 196616 | tf_op jit(solution)/shard_map/ppermute | solution.py:365
  66.5 28.6 %copy-start.4 = (bf16[9,128,128]{2,1,0:T(8,128)(2,1)S(1)}, bf16[9,128,128]{2,1,0:T(8,128)(2,1)}, u32[]{:S(2)}) copy-start(bf16[9,128,128]{2,1,0:T(8,128)(2,1)} %param.12) | copy-start | bytes 884740
  69.6 5.1 %collective-permute-start.16 = (bf16[288,128]{1,0:T(8,128)(2,1)S(1)}, bf16[288,128]{1,0:T(8,128)(2,1)S(1)}, u32[]{:S(2)}, u32[]{:S(2)}) collective-permute-start(bf16[288,128]{1,0:T(8,128)(2,1)S(1)} %get-tuple-element.51), channel_id=1, source_target_pairs={{0,1},{1,0},{2,3},{3,2},{4,5},{5,4},{6,7},{7,6},{8,9},{9,8},{10,11... | collective-permute-start | bytes 221192 | tf_op jit(solution)/shard_map/ppermute | solution.py:383
  71.0 4.4 %collective-permute-start.17 = (bf16[288,128]{1,0:T(8,128)(2,1)S(1)}, bf16[288,128]{1,0:T(8,128)(2,1)S(1)}, u32[]{:S(2)}, u32[]{:S(2)}) collective-permute-start(bf16[288,128]{1,0:T(8,128)(2,1)S(1)} %get-tuple-element.52), channel_id=1, source_target_pairs={{0,16},{1,17},{2,18},{3,19},{4,20},{5,21},{6,22},{7,23},{8,24},{9,... | collective-permute-start | bytes 221192 | tf_op jit(solution)/shard_map/ppermute | solution.py:383
  72.6 5.3 %collective-permute-start.18 = (bf16[288,128]{1,0:T(8,128)(2,1)S(1)}, bf16[288,128]{1,0:T(8,128)(2,1)S(1)}, u32[]{:S(2)}, u32[]{:S(2)}) collective-permute-start(bf16[288,128]{1,0:T(8,128)(2,1)S(1)} %get-tuple-element.53), channel_id=1, source_target_pairs={{0,17},{1,16},{2,19},{3,18},{4,21},{5,20},{6,23},{7,22},{8,25},{9,... | collective-permute-start | bytes 221192 | tf_op jit(solution)/shard_map/ppermute | solution.py:383
  77.9 12.3 %collective-permute-start.19 = (bf16[2,256,128]{2,1,0:T(8,128)(2,1)S(1)}, bf16[2,256,128]{2,1,0:T(8,128)(2,1)S(1)}, u32[]{:S(2)}, u32[]{:S(2)}) collective-permute-start(bf16[2,256,128]{2,1,0:T(8,128)(2,1)S(1)} %get-tuple-element.54), channel_id=1, source_target_pairs={{0,1},{1,0},{2,3},{3,2},{4,5},{5,4},{6,7},{7,6},{8,9},{9,8},{10,11... | collective-permute-start | bytes 393224 | tf_op jit(solution)/shard_map/ppermute | solution.py:365
  78.5 11.7 %collective-permute-start.20 = (bf16[2,256,128]{2,1,0:T(8,128)(2,1)S(1)}, bf16[2,256,128]{2,1,0:T(8,128)(2,1)S(1)}, u32[]{:S(2)}, u32[]{:S(2)}) collective-permute-start(bf16[2,256,128]{2,1,0:T(8,128)(2,1)S(1)} %get-tuple-element.55), channel_id=1, source_target_pairs={{1,2},{3,4},{5,6},{2,1},{4,3},{6,5},{9,10},{11,12},{13,14},{10,9},... | collective-permute-start | bytes 393224 | tf_op jit(solution)/shard_map/ppermute | solution.py:510
  79.2 1.3 %collective-permute-start.21 = (f32[144,128]{1,0:T(8,128)S(1)}, f32[144,128]{1,0:T(8,128)S(1)}, u32[]{:S(2)}, u32[]{:S(2)}) collective-permute-start(f32[144,128]{1,0:T(8,128)S(1)} %get-tuple-element.57), channel_id=1, source_target_pairs={{0,8},{8,0},{16,24},{24,16},{1,9},{9,1},{17,25},{25,17},{2,10},{10... | collective-permute-start | bytes 221192 | tf_op jit(solution)/shard_map/ppermute | solution.py:387
  80.5 6.2 %collective-permute-start.24 = (bf16[144,128]{1,0:T(8,128)(2,1)S(1)}, bf16[144,128]{1,0:T(8,128)(2,1)S(1)}, u32[]{:S(2)}, u32[]{:S(2)}) collective-permute-start(bf16[144,128]{1,0:T(8,128)(2,1)S(1)} %sum_cores.1.refs_0_), channel_id=1, source_target_pairs={{0,6},{1,7},{2,4},{3,5},{4,2},{5,3},{6,0},{7,1},{8,14},{9,15},{10,... | collective-permute-start | bytes 110600 | tf_op jit(solution)/shard_map/ppermute | solution.py:365
  84.4 5.3 %collective-permute-start.23 = (bf16[144,128]{1,0:T(8,128)(2,1)S(1)}, bf16[144,128]{1,0:T(8,128)(2,1)S(1)}, u32[]{:S(2)}, u32[]{:S(2)}) collective-permute-start(bf16[144,128]{1,0:T(8,128)(2,1)S(1)} %sum_cores.1.refs_0_), channel_id=1, source_target_pairs={{0,4},{1,5},{2,6},{3,7},{4,0},{5,1},{6,2},{7,3},{8,12},{9,13},{10,... | collective-permute-start | bytes 110600 | tf_op jit(solution)/shard_map/ppermute | solution.py:365
  86.2 4.0 %collective-permute-start.22 = (bf16[144,128]{1,0:T(8,128)(2,1)S(1)}, bf16[144,128]{1,0:T(8,128)(2,1)S(1)}, u32[]{:S(2)}, u32[]{:S(2)}) collective-permute-start(bf16[144,128]{1,0:T(8,128)(2,1)S(1)} %sum_cores.1.refs_0_), channel_id=1, source_target_pairs={{0,2},{1,3},{2,0},{3,1},{4,6},{5,7},{6,4},{7,5},{8,10},{9,11},{10,... | collective-permute-start | bytes 110600 | tf_op jit(solution)/shard_map/ppermute | solution.py:365
  90.2 1.3 %collective-permute-start.25 = (bf16[144,128]{1,0:T(8,128)(2,1)S(1)}, bf16[144,128]{1,0:T(8,128)(2,1)S(1)}, u32[]{:S(2)}, u32[]{:S(2)}) collective-permute-start(bf16[144,128]{1,0:T(8,128)(2,1)S(1)} %sum_planes.1.own_ref), channel_id=1, source_target_pairs={{0,8},{8,0},{16,24},{24,16},{1,9},{9,1},{17,25},{25,17},{2,10},{10... | collective-permute-start | bytes 110600 | tf_op jit(solution)/shard_map/ppermute | solution.py:387
  91.5 6.1 %collective-permute-start.28 = (bf16[288,128]{1,0:T(8,128)(2,1)S(1)}, bf16[288,128]{1,0:T(8,128)(2,1)S(1)}, u32[]{:S(2)}, u32[]{:S(2)}) collective-permute-start(bf16[288,128]{1,0:T(8,128)(2,1)S(1)} %join_cores.1.refs_0_), channel_id=1, source_target_pairs={{0,17},{1,16},{2,19},{3,18},{4,21},{5,20},{6,23},{7,22},{8,25},{9,... | collective-permute-start | bytes 221192 | tf_op jit(solution)/shard_map/ppermute | solution.py:383
  92.3 5.6 %collective-permute-start.27 = (bf16[288,128]{1,0:T(8,128)(2,1)S(1)}, bf16[288,128]{1,0:T(8,128)(2,1)S(1)}, u32[]{:S(2)}, u32[]{:S(2)}) collective-permute-start(bf16[288,128]{1,0:T(8,128)(2,1)S(1)} %join_cores.1.refs_0_), channel_id=1, source_target_pairs={{0,16},{1,17},{2,18},{3,19},{4,20},{5,21},{6,22},{7,23},{8,24},{9,... | collective-permute-start | bytes 221192 | tf_op jit(solution)/shard_map/ppermute | solution.py:383
  93.4 4.5 %collective-permute-start.26 = (bf16[288,128]{1,0:T(8,128)(2,1)S(1)}, bf16[288,128]{1,0:T(8,128)(2,1)S(1)}, u32[]{:S(2)}, u32[]{:S(2)}) collective-permute-start(bf16[288,128]{1,0:T(8,128)(2,1)S(1)} %join_cores.1.refs_0_), channel_id=1, source_target_pairs={{0,1},{1,0},{2,3},{3,2},{4,5},{5,4},{6,7},{7,6},{8,9},{9,8},{10,11... | collective-permute-start | bytes 221192 | tf_op jit(solution)/shard_map/ppermute | solution.py:383

commit v10 on v9

--- a/solution.py
+++ b/solution.py
@@ -332,14 +332,27 @@
     return terms[0]
 
 
-def sum_chips_kernel(core_ref, near_ref, far_ref, *refs):
-    keep_ref, send_ref, near_out_ref, far_out_ref, total = refs[-5:]
-    total[...] = add_pairs([ref[...].astype(jnp.float32) for ref in refs[:-5]])
+def hold_kernel(value_ref, after_ref, out_ref):
+    del after_ref
+    out_ref[...] = value_ref[...]
+
+
+def hold(value, after):
+    return call(
+        hold_kernel,
+        "hold",
+        jax.ShapeDtypeStruct(value.shape, value.dtype),
+        [VMEM(), ANY()],
+        moved=4 * value.size,
+    )(value, after)
+
+
+def sum_chips_kernel(core_ref, *refs):
+    keep_ref, send_ref, total = refs[-3:]
+    total[...] = add_pairs([ref[...].astype(jnp.float32) for ref in refs[:-3]])
     half = keep_ref.shape[0]
     keep_ref[...] = total[rows_at(core_ref[0], half), :]
     send_ref[...] = total[rows_at(1 - core_ref[0], half), :]
-    near_out_ref[...] = near_ref[...]
-    far_out_ref[...] = far_ref[...]
 
 
 def sum_kernel(count, factor, *refs):
@@ -347,7 +360,8 @@
     refs[-1][...] = (total * factor).astype(jnp.bfloat16)
 
 
-def join_kernel(core_ref, own_ref, other_ref, out_ref):
+def join_kernel(core_ref, own_ref, other_ref, after_ref, out_ref):
+    del after_ref
     half = own_ref.shape[0]
     out_ref[rows_at(core_ref[0], half), :] = own_ref[...]
     out_ref[rows_at(1 - core_ref[0], half), :] = other_ref[...]
@@ -491,14 +505,15 @@
     distances = range(1, quad_size)
     parts[1:] = [trade_chips(parts[distance], distance, inner) for distance in distances]
     half_shape = (chunk_rows // 2, width)
-    keep, send, near, far = call(
+    near = trade(hold(near, parts[1]), 1)
+    keep, send = call(
         sum_chips_kernel,
         "sum_chips",
-        [jax.ShapeDtypeStruct(half_shape, jnp.float32)] * 2 + [edge_shape] * 2,
-        [SMEM()] + [VMEM()] * (2 + quad_size),
+        [jax.ShapeDtypeStruct(half_shape, jnp.float32)] * 2,
+        [SMEM()] + [VMEM()] * quad_size,
         scratch=[pltpu.VMEM((chunk_rows, width), jnp.float32)],
         moved=chunk_moved,
-    )(core, near, far, *parts)
+    )(core, *parts)
     plane_sum = call(
         functools.partial(sum_kernel, 2, 1.0),
         "sum_cores",
@@ -506,25 +521,24 @@
         [VMEM()] * 2,
         moved=chunk_moved // quad_size,
     )(keep, trade_cores(send))
-    near = trade(near, 1)
-    far = lax.ppermute(far, "seq", far_pairs)
     plane_sums = [plane_sum] + [
         trade(plane_sum, distance) for distance in range(inner, seq_count, inner)
     ]
+    far = lax.ppermute(hold(far, plane_sums[-1]), "seq", far_pairs)
     total = call(
         functools.partial(sum_kernel, len(plane_sums), 1.0 / math.sqrt(PATCH * columns)),
         "sum_planes",
         jax.ShapeDtypeStruct(half_shape, jnp.bfloat16),
-        [VMEM()] * len(plane_sums) + [ANY()] * 2,
+        [VMEM()] * len(plane_sums) + [ANY()],
         moved=chunk_moved // quad_size,
-    )(*plane_sums, near, far)
+    )(*plane_sums, near)
     joined = call(
         join_kernel,
         "join_cores",
         jax.ShapeDtypeStruct((chunk_rows, width), jnp.bfloat16),
-        [SMEM()] + [VMEM()] * 2,
+        [SMEM()] + [VMEM()] * 2 + [ANY()],
         moved=chunk_moved // quad_size,
-    )(core, total, trade_cores(total))
+    )(core, total, trade_cores(total), far)
     totals = [joined] + [trade_chips(joined, distance, inner) for distance in distances]
     decoded = call(
         decode_kernel,

time: 99.2 us -> 103 us (1.038)
  waiting for transfers between devices: 35 us -> 38.7 us
    ppermute x19, waiting for transfers between devices: 27.2 us -> 31.1 us  [trade(): return lax.ppermute(values, 'seq', pairs)]
where the time goes in v10:
time: 103 us; the launch traced here: 102 us
  starting transfers between devices  49.5 us (48%)
  waiting for transfers between devices  38.7 us (38%)
  Pallas kernels  13.2 us (13%)
    ppermute x19, starting transfers between devices, trade(): return lax.ppermute(values, 'seq', pairs)  40.9 us
    ppermute x19, waiting for transfers between devices, trade(): return lax.ppermute(values, 'seq', pairs)  31.1 us
    ppermute x6, starting transfers between devices, trade_chips(): return lax.ppermute(values, ('dp', 'seq'), pairs)  7.11 us
    ppermute x6, waiting for transfers between devices, trade_chips(): return lax.ppermute(values, ('dp', 'seq'), pairs)  5.82 us
    pallas_call x1, Pallas kernels, body(): call(functools.partial(pack_kernel, regions, per_device), 'pack', [chunk_...  3.81 us
    pallas_call x1, Pallas kernels, body(): call(norm_kernel, 'norm_and_gradient', [jax.ShapeDtypeStruct((regions, PA...  3.05 us
    pallas_call x1, Pallas kernels, body(): call(functools.partial(attend_kernel, block_rows, group, order), 'attend'...  2.48 us
    pallas_call x1, Pallas kernels, body(): call(decode_kernel, 'decode', jax.ShapeDtypeStruct(cotangent.shape, jnp.b...  2.22 us
  transfers between devices with their start and end apart: 29, of which 15 were waited for; matrix products, arithmetic and copies ran while one was open for 0% of the time, Pallas kernels for 5%

profile of v10, /device:TPU:0, one launch (start us, length us, event | category | flops | bytes accessed | tf_op | source)
XLA Modules:
  0.0 102.3 jit_solution(17297158738494350195)
XLA Ops:
  0.7 3.8 %pack.1 = (bf16[3,4,64,128]{3,2,1,0:T(8,128)(2,1)}, bf16[3,4,64,128]{3,2,1,0:T(8,128)(2,1)}, bf16[3,4,64,128]{3,2,1,0:T(8,128)(2,1)}, bf16[3,4,64,128]{3,2,1,0:T...) custom-call(s32[1]{0:T(128)} %bitcast.index_ref, ...), custom_call_target="tpu_custom_call" | custom-call | bytes 3145728 | tf_op jit(solution)/shard_map/pack/pallas_call | solution.py:425
  4.5 3.0 %collective-permute-start.2 = (bf16[3,4,64,128]{3,2,1,0:T(8,128)(2,1)}, bf16[3,4,64,128]{3,2,1,0:T(8,128)(2,1)S(1)}, u32[]{:S(2)}, u32[]{:S(2)}) collective-permute-start(bf16[3,4,64,128]{3,2,1,0:T(8,128)(2,1)} %get-tuple-element.30), channel_id=1, source_target_pairs={{0,1},{1,0},{2,3},{3,2},{4,5},{5,4},{6,7},{7,6},{8,9},{9,8},{10,11... | collective-permute-start | bytes 589832 | tf_op jit(solution)/shard_map/ppermute | solution.py:379
  7.5 1.6 %collective-permute-start.3 = (bf16[3,4,64,128]{3,2,1,0:T(8,128)(2,1)}, bf16[3,4,64,128]{3,2,1,0:T(8,128)(2,1)S(1)}, u32[]{:S(2)}, u32[]{:S(2)}) collective-permute-start(bf16[3,4,64,128]{3,2,1,0:T(8,128)(2,1)} %get-tuple-element.31), channel_id=1, source_target_pairs={{0,2},{1,3},{2,0},{3,1},{4,6},{5,7},{6,4},{7,5},{8,10},{9,11},{10,... | collective-permute-start | bytes 589832 | tf_op jit(solution)/shard_map/ppermute | solution.py:379
  9.1 0.0 collective-permute-start.4
  9.1 3.0 %collective-permute-start.5 = (bf16[3,4,64,128]{3,2,1,0:T(8,128)(2,1)}, bf16[3,4,64,128]{3,2,1,0:T(8,128)(2,1)S(1)}, u32[]{:S(2)}, u32[]{:S(2)}) collective-permute-start(bf16[3,4,64,128]{3,2,1,0:T(8,128)(2,1)} %get-tuple-element.33), channel_id=1, source_target_pairs={{0,4},{1,5},{2,6},{3,7},{4,0},{5,1},{6,2},{7,3},{8,12},{9,13},{10,... | collective-permute-start | bytes 589832 | tf_op jit(solution)/shard_map/ppermute | solution.py:379
  12.1 1.3 %collective-permute-start.6 = (bf16[3,4,64,128]{3,2,1,0:T(8,128)(2,1)}, bf16[3,4,64,128]{3,2,1,0:T(8,128)(2,1)S(1)}, u32[]{:S(2)}, u32[]{:S(2)}) collective-permute-start(bf16[3,4,64,128]{3,2,1,0:T(8,128)(2,1)} %get-tuple-element.34), channel_id=1, source_target_pairs={{0,5},{1,4},{2,7},{3,6},{4,1},{5,0},{6,3},{7,2},{8,13},{9,12},{10,... | collective-permute-start | bytes 589832 | tf_op jit(solution)/shard_map/ppermute | solution.py:379
  13.3 3.6 %collective-permute-start.7 = (bf16[3,4,64,128]{3,2,1,0:T(8,128)(2,1)}, bf16[3,4,64,128]{3,2,1,0:T(8,128)(2,1)S(1)}, u32[]{:S(2)}, u32[]{:S(2)}) collective-permute-start(bf16[3,4,64,128]{3,2,1,0:T(8,128)(2,1)} %get-tuple-element.35), channel_id=1, source_target_pairs={{0,6},{1,7},{2,4},{3,5},{4,2},{5,3},{6,0},{7,1},{8,14},{9,15},{10,... | collective-permute-start | bytes 589832 | tf_op jit(solution)/shard_map/ppermute | solution.py:379
  16.9 6.2 %collective-permute-done.3.refs_1_ = bf16[3,4,64,128]{3,2,1,0:T(8,128)(2,1)S(1)} collective-permute-done((bf16[3,4,64,128]{3,2,1,0:T(8,128)(2,1)}, bf16[3,4,64,128]{3,2,1,0:T(8,128)(2,1)S(1)}, u32[]{:S(2)}, u32[]{:S(2)}) %collective-permute-start.3) | collective-permute-done | bytes 196640 | tf_op jit(solution)/shard_map/ppermute | solution.py:379
  23.2 0.9 collective-permute-start.8
  24.1 0.8 collective-permute-done.4.refs_2_
  24.9 2.5 %collective-permute-start = (bf16[2,256,128]{2,1,0:T(8,128)(2,1)}, bf16[2,256,128]{2,1,0:T(8,128)(2,1)S(1)}, u32[]{:S(2)}, u32[]{:S(2)}) collective-permute-start(bf16[2,256,128]{2,1,0:T(8,128)(2,1)} %get-tuple-element.28), channel_id=1, source_target_pairs={{0,1},{1,0},{2,3},{3,2},{4,5},{5,4},{6,7},{7,6},{8,9},{9,8},{10,11... | collective-permute-start | bytes 393224 | tf_op jit(solution)/shard_map/ppermute | solution.py:379
  27.4 0.0 collective-permute-done.5.refs_3_
  27.4 0.7 collective-permute-start.1
  28.1 0.1 fusion.lengths_ref
  28.2 0.0 copy-start
  28.2 0.4 own_chunk.1.refs_7_
  28.6 11.8 %collective-permute-done.6.refs_4_ = bf16[3,4,64,128]{3,2,1,0:T(8,128)(2,1)S(1)} collective-permute-done((bf16[3,4,64,128]{3,2,1,0:T(8,128)(2,1)}, bf16[3,4,64,128]{3,2,1,0:T(8,128)(2,1)S(1)}, u32[]{:S(2)}, u32[]{:S(2)}) %collective-permute-start.6) | collective-permute-done | bytes 196640 | tf_op jit(solution)/shard_map/ppermute | solution.py:379
  40.4 0.0 collective-permute-done.7.refs_5_
  40.4 0.0 collective-permute-done.8.refs_6_
  40.4 2.5 %attend.1 = (bf16[4,64,128]{2,1,0:T(8,128)(2,1)S(1)}, bf16[4,64,128]{2,1,0:T(8,128)(2,1)S(1)}, bf16[4,64,128]{2,1,0:T(8,128)(2,1)S(1)}, bf16[4,64,128]{2,1,0:T(8...) custom-call(s32[1]{0:T(128)} %bitcast.index_ref, ...), custom_call_target="tpu_custom_call" | custom-call | flops 536870912 | bytes 2097152 | tf_op jit(solution)/shard_map/attend/pallas_call | solution.py:467
  42.9 0.0 copy-start.5
  42.9 0.1 collective-permute-start.9
  43.0 9.3 %collective-permute-start.10 = (bf16[4,64,128]{2,1,0:T(8,128)(2,1)S(1)}, bf16[4,64,128]{2,1,0:T(8,128)(2,1)S(1)}, u32[]{:S(2)}, u32[]{:S(2)}) collective-permute-start(bf16[4,64,128]{2,1,0:T(8,128)(2,1)S(1)} %get-tuple-element.39), channel_id=1, source_target_pairs={{0,2},{1,3},{2,0},{3,1},{4,6},{5,7},{6,4},{7,5},{8,10},{9,11},{10,... | collective-permute-start | bytes 196616 | tf_op jit(solution)/shard_map/ppermute | solution.py:379
  52.3 4.7 %collective-permute-start.12 = (bf16[4,64,128]{2,1,0:T(8,128)(2,1)S(1)}, bf16[4,64,128]{2,1,0:T(8,128)(2,1)S(1)}, u32[]{:S(2)}, u32[]{:S(2)}) collective-permute-start(bf16[4,64,128]{2,1,0:T(8,128)(2,1)S(1)} %get-tuple-element.41), channel_id=1, source_target_pairs={{0,4},{1,5},{2,6},{3,7},{4,0},{5,1},{6,2},{7,3},{8,12},{9,13},{10,... | collective-permute-start | bytes 196616 | tf_op jit(solution)/shard_map/ppermute | solution.py:379
  57.1 0.0 collective-permute-done.1.far_ref
  57.1 0.0 collective-permute-start.13
  57.1 2.4 %collective-permute-start.14 = (bf16[4,64,128]{2,1,0:T(8,128)(2,1)S(1)}, bf16[4,64,128]{2,1,0:T(8,128)(2,1)S(1)}, u32[]{:S(2)}, u32[]{:S(2)}) collective-permute-start(bf16[4,64,128]{2,1,0:T(8,128)(2,1)S(1)} %get-tuple-element.43), channel_id=1, source_target_pairs={{0,6},{1,7},{2,4},{3,5},{4,2},{5,3},{6,0},{7,1},{8,14},{9,15},{10,... | collective-permute-start | bytes 196616 | tf_op jit(solution)/shard_map/ppermute | solution.py:379
  59.4 2.4 %collective-permute-start.15 = (bf16[4,64,128]{2,1,0:T(8,128)(2,1)S(1)}, bf16[4,64,128]{2,1,0:T(8,128)(2,1)S(1)}, u32[]{:S(2)}, u32[]{:S(2)}) collective-permute-start(bf16[4,64,128]{2,1,0:T(8,128)(2,1)S(1)} %get-tuple-element.44), channel_id=1, source_target_pairs={{0,7},{1,6},{2,5},{3,4},{4,3},{5,2},{6,1},{7,0},{8,15},{9,14},{10,... | collective-permute-start | bytes 196616 | tf_op jit(solution)/shard_map/ppermute | solution.py:379
  61.9 0.3 turn_cotangent.1.turned_ref
  62.1 0.0 collective-permute-done.11.refs_3_
  62.2 0.0 collective-permute-done.12.refs_4_
  62.2 1.1 %collective-permute-done.13.refs_5_ = bf16[4,64,128]{2,1,0:T(8,128)(2,1)S(1)} collective-permute-done((bf16[4,64,128]{2,1,0:T(8,128)(2,1)S(1)}, bf16[4,64,128]{2,1,0:T(8,128)(2,1)S(1)}, u32[]{:S(2)}, u32[]{:S(2)}) %collective-permute-start.13) | collective-permute-done | bytes 65568 | tf_op jit(solution)/shard_map/ppermute | solution.py:379
  63.3 0.0 collective-permute-done.14.refs_6_
  63.3 3.1 %collective-permute-done.15.refs_7_ = bf16[4,64,128]{2,1,0:T(8,128)(2,1)S(1)} collective-permute-done((bf16[4,64,128]{2,1,0:T(8,128)(2,1)S(1)}, bf16[4,64,128]{2,1,0:T(8,128)(2,1)S(1)}, u32[]{:S(2)}, u32[]{:S(2)}) %collective-permute-start.15) | collective-permute-done | bytes 65568 | tf_op jit(solution)/shard_map/ppermute | solution.py:379
  66.4 3.1 %norm_and_gradient.1 = (bf16[2,4,256,128]{3,2,1,0:T(8,128)(2,1)S(1)}, bf16[2,256,128]{2,1,0:T(8,128)(2,1)S(1)}, bf16[2,256,128]{2,1,0:T(8,128)(2,1)S(1)}, bf16[2...) custom-call(s32[2]{0:T(128)S(1)} %copy-done.6, ...), custom_call_target="tpu_custom_call" | custom-call | flops 603979776 | bytes 2097152 | tf_op jit(solution)/shard_map/norm_and_gradient/pallas_call | solution.py:489
  69.5 1.6 %collective-permute-start.16 = (bf16[288,128]{1,0:T(8,128)(2,1)S(1)}, bf16[288,128]{1,0:T(8,128)(2,1)S(1)}, u32[]{:S(2)}, u32[]{:S(2)}) collective-permute-start(bf16[288,128]{1,0:T(8,128)(2,1)S(1)} %get-tuple-element.47), channel_id=1, source_target_pairs={{0,1},{1,0},{2,3},{3,2},{4,5},{5,4},{6,7},{7,6},{8,9},{9,8},{10,11... | collective-permute-start | bytes 221192 | tf_op jit(solution)/shard_map/ppermute | solution.py:397
  71.1 1.1 %collective-permute-start.18 = (bf16[288,128]{1,0:T(8,128)(2,1)S(1)}, bf16[288,128]{1,0:T(8,128)(2,1)S(1)}, u32[]{:S(2)}, u32[]{:S(2)}) collective-permute-start(bf16[288,128]{1,0:T(8,128)(2,1)S(1)} %get-tuple-element.50), channel_id=1, source_target_pairs={{0,16},{1,17},{2,18},{3,19},{4,20},{5,21},{6,22},{7,23},{8,24},{9,... | collective-permute-start | bytes 221192 | tf_op jit(solution)/shard_map/ppermute | solution.py:397
  72.1 0.9 collective-permute-start.19
  73.0 0.9 collective-permute-done.16.after_ref.refs_1_
  73.9 1.5 %collective-permute-done.18.refs_2_ = bf16[288,128]{1,0:T(8,128)(2,1)S(1)} collective-permute-done((bf16[288,128]{1,0:T(8,128)(2,1)S(1)}, bf16[288,128]{1,0:T(8,128)(2,1)S(1)}, u32[]{:S(2)}, u32[]{:S(2)}) %collective-permute-start.18) | collective-permute-done | bytes 73760 | tf_op jit(solution)/shard_map/ppermute | solution.py:397
  75.4 2.0 %collective-permute-done.19.refs_3_ = bf16[288,128]{1,0:T(8,128)(2,1)S(1)} collective-permute-done((bf16[288,128]{1,0:T(8,128)(2,1)S(1)}, bf16[288,128]{1,0:T(8,128)(2,1)S(1)}, u32[]{:S(2)}, u32[]{:S(2)}) %collective-permute-start.19) | collective-permute-done | bytes 73760 | tf_op jit(solution)/shard_map/ppermute | solution.py:397
  77.4 0.1 sum_chips.1
  77.4 0.1 collective-permute-start.20
  77.5 0.7 collective-permute-start.17
  78.3 0.5 collective-permute-done.20.refs_1_
  78.8 1.7 %collective-permute-start.21 = (bf16[144,128]{1,0:T(8,128)(2,1)S(1)}, bf16[144,128]{1,0:T(8,128)(2,1)S(1)}, u32[]{:S(2)}, u32[]{:S(2)}) collective-permute-start(bf16[144,128]{1,0:T(8,128)(2,1)S(1)} %sum_cores.1.refs_0_), channel_id=1, source_target_pairs={{0,6},{1,7},{2,4},{3,5},{4,2},{5,3},{6,0},{7,1},{8,14},{9,15},{10,... | collective-permute-start | bytes 110600 | tf_op jit(solution)/shard_map/ppermute | solution.py:379
  80.5 4.1 %collective-permute-done.21.after_ref.refs_3_ = bf16[144,128]{1,0:T(8,128)(2,1)S(1)} collective-permute-done((bf16[144,128]{1,0:T(8,128)(2,1)S(1)}, bf16[144,128]{1,0:T(8,128)(2,1)S(1)}, u32[]{:S(2)}, u32[]{:S(2)}) %collective-permute-start.21) | collective-permute-done | bytes 36896 | tf_op jit(solution)/shard_map/ppermute | solution.py:379
  84.6 0.7 collective-permute-start.22
  85.3 2.1 %collective-permute-start.24 = (bf16[144,128]{1,0:T(8,128)(2,1)S(1)}, bf16[144,128]{1,0:T(8,128)(2,1)S(1)}, u32[]{:S(2)}, u32[]{:S(2)}) collective-permute-start(bf16[144,128]{1,0:T(8,128)(2,1)S(1)} %sum_cores.1.refs_0_), channel_id=1, source_target_pairs={{0,4},{1,5},{2,6},{3,7},{4,0},{5,1},{6,2},{7,3},{8,12},{9,13},{10,... | collective-permute-start | bytes 110600 | tf_op jit(solution)/shard_map/ppermute | solution.py:379
  87.4 1.6 %collective-permute-start.23 = (bf16[144,128]{1,0:T(8,128)(2,1)S(1)}, bf16[144,128]{1,0:T(8,128)(2,1)S(1)}, u32[]{:S(2)}, u32[]{:S(2)}) collective-permute-start(bf16[144,128]{1,0:T(8,128)(2,1)S(1)} %sum_cores.1.refs_0_), channel_id=1, source_target_pairs={{0,2},{1,3},{2,0},{3,1},{4,6},{5,7},{6,4},{7,5},{8,10},{9,11},{10,... | collective-permute-start | bytes 110600 | tf_op jit(solution)/shard_map/ppermute | solution.py:379
  89.0 2.0 %collective-permute-done.24.refs_2_ = bf16[144,128]{1,0:T(8,128)(2,1)S(1)} collective-permute-done((bf16[144,128]{1,0:T(8,128)(2,1)S(1)}, bf16[144,128]{1,0:T(8,128)(2,1)S(1)}, u32[]{:S(2)}, u32[]{:S(2)}) %collective-permute-start.24) | collective-permute-done | bytes 36896 | tf_op jit(solution)/shard_map/ppermute | solution.py:379
  91.0 1.9 %collective-permute-done.23.refs_1_ = bf16[144,128]{1,0:T(8,128)(2,1)S(1)} collective-permute-done((bf16[144,128]{1,0:T(8,128)(2,1)S(1)}, bf16[144,128]{1,0:T(8,128)(2,1)S(1)}, u32[]{:S(2)}, u32[]{:S(2)}) %collective-permute-start.23) | collective-permute-done | bytes 36896 | tf_op jit(solution)/shard_map/ppermute | solution.py:379
  92.9 0.0 collective-permute-done.17.near_ref.refs_4_
  92.9 0.1 collective-permute-start.25
  93.0 1.2 %collective-permute-done.25.other_ref = bf16[144,128]{1,0:T(8,128)(2,1)S(1)} collective-permute-done((bf16[144,128]{1,0:T(8,128)(2,1)S(1)}, bf16[144,128]{1,0:T(8,128)(2,1)S(1)}, u32[]{:S(2)}, u32[]{:S(2)}) %collective-permute-start.25) | collective-permute-done | bytes 36896 | tf_op jit(solution)/shard_map/ppermute | solution.py:401
  94.2 0.0 collective-permute-done.22.far_ref.after_ref
  94.2 1.8 %collective-permute-start.28 = (bf16[288,128]{1,0:T(8,128)(2,1)S(1)}, bf16[288,128]{1,0:T(8,128)(2,1)S(1)}, u32[]{:S(2)}, u32[]{:S(2)}) collective-permute-start(bf16[288,128]{1,0:T(8,128)(2,1)S(1)} %join_cores.1.refs_0_), channel_id=1, source_target_pairs={{0,17},{1,16},{2,19},{3,18},{4,21},{5,20},{6,23},{7,22},{8,25},{9,... | collective-permute-start | bytes 221192 | tf_op jit(solution)/shard_map/ppermute | solution.py:397
  96.0 1.1 %collective-permute-start.27 = (bf16[288,128]{1,0:T(8,128)(2,1)S(1)}, bf16[288,128]{1,0:T(8,128)(2,1)S(1)}, u32[]{:S(2)}, u32[]{:S(2)}) collective-permute-start(bf16[288,128]{1,0:T(8,128)(2,1)S(1)} %join_cores.1.refs_0_), channel_id=1, source_target_pairs={{0,16},{1,17},{2,18},{3,19},{4,20},{5,21},{6,22},{7,23},{8,24},{9,... | collective-permute-start | bytes 221192 | tf_op jit(solution)/shard_map/ppermute | solution.py:397
  97.1 0.7 collective-permute-start.26
  97.7 2.2 %decode.1 = bf16[2,4,256,128]{3,2,1,0:T(8,128)(2,1)} custom-call(s32[1]{0:T(128)} %bitcast.index_ref, bf16[2,4,256,128]{3,2,1,0:T(8,128)(2,1)S(1)} %get-tuple-element.45.image_ref, bf16[2,256,128]{2,1,0:T(8,128)(2,1)S(1)} %collective-permute-done.17.near_ref.refs_4_, bf16[2,256,128]{2,1,0:T(8,128)(2,1)S(1)} %collective-permute-done.22.far_ref.after_ref, ...), custom_call_target="tpu_custom_call" | custom-call | flops 603979776 | bytes 1048576 | tf_op jit(solution)/shard_map/decode/pallas_call | solution.py:543
  100.0 0.0 collective-permute-done.28.refs_3_
  100.0 1.1 %collective-permute-done.27.refs_2_ = bf16[288,128]{1,0:T(8,128)(2,1)S(1)} collective-permute-done((bf16[288,128]{1,0:T(8,128)(2,1)S(1)}, bf16[288,128]{1,0:T(8,128)(2,1)S(1)}, u32[]{:S(2)}, u32[]{:S(2)}) %collective-permute-start.27) | collective-permute-done | bytes 73760 | tf_op jit(solution)/shard_map/ppermute | solution.py:397
  101.1 0.4 collective-permute-done.26.refs_1_
  101.4 0.9 spread_sums.1
  (23 shorter events, 0.1 us)
Async XLA Ops:
  0.6 27.5 %copy-start.3 = (bf16[64,2,2048]{2,1,0:T(2,128)(2,1)S(1)}, bf16[64,2,2048]{2,1,0:T(2,128)(2,1)}, u32[]{:S(2)}) copy-start(bf16[64,2,2048]{2,1,0:T(2,128)(2,1)} %value_ref.3) | copy-start | bytes 1572868
  0.6 27.5 %copy-start.2 = (bf16[64,2,2048]{2,1,0:T(2,128)(2,1)S(1)}, bf16[64,2,2048]{2,1,0:T(2,128)(2,1)}, u32[]{:S(2)}) copy-start(bf16[64,2,2048]{2,1,0:T(2,128)(2,1)} %key_ref.3) | copy-start | bytes 1572868
  0.7 27.5 %copy-start.1 = (bf16[64,2,2048]{2,1,0:T(2,128)(2,1)S(1)}, bf16[64,2,2048]{2,1,0:T(2,128)(2,1)}, u32[]{:S(2)}) copy-start(bf16[64,2,2048]{2,1,0:T(2,128)(2,1)} %query_ref.3) | copy-start | bytes 1572868
  0.7 27.4 %copy-start.6 = (s32[2]{0:T(128)S(1)}, s32[2]{0:T(128)}, u32[]{:S(2)}) copy-start(s32[2]{0:T(128)} %lengths_ref.1) | copy-start | bytes 28
  4.5 8.9 %collective-permute-start.2 = (bf16[3,4,64,128]{3,2,1,0:T(8,128)(2,1)}, bf16[3,4,64,128]{3,2,1,0:T(8,128)(2,1)S(1)}, u32[]{:S(2)}, u32[]{:S(2)}) collective-permute-start(bf16[3,4,64,128]{3,2,1,0:T(8,128)(2,1)} %get-tuple-element.30), channel_id=1, source_target_pairs={{0,1},{1,0},{2,3},{3,2},{4,5},{5,4},{6,7},{7,6},{8,9},{9,8},{10,11... | collective-permute-start | bytes 589832 | tf_op jit(solution)/shard_map/ppermute | solution.py:379
  7.5 15.7 %collective-permute-start.3 = (bf16[3,4,64,128]{3,2,1,0:T(8,128)(2,1)}, bf16[3,4,64,128]{3,2,1,0:T(8,128)(2,1)S(1)}, u32[]{:S(2)}, u32[]{:S(2)}) collective-permute-start(bf16[3,4,64,128]{3,2,1,0:T(8,128)(2,1)} %get-tuple-element.31), channel_id=1, source_target_pairs={{0,2},{1,3},{2,0},{3,1},{4,6},{5,7},{6,4},{7,5},{8,10},{9,11},{10,... | collective-permute-start | bytes 589832 | tf_op jit(solution)/shard_map/ppermute | solution.py:379
  9.1 15.8 %collective-permute-start.4 = (bf16[3,4,64,128]{3,2,1,0:T(8,128)(2,1)}, bf16[3,4,64,128]{3,2,1,0:T(8,128)(2,1)S(1)}, u32[]{:S(2)}, u32[]{:S(2)}) collective-permute-start(bf16[3,4,64,128]{3,2,1,0:T(8,128)(2,1)} %get-tuple-element.32), channel_id=1, source_target_pairs={{0,3},{1,2},{2,1},{3,0},{4,7},{5,6},{6,5},{7,4},{8,11},{9,10},{10,... | collective-permute-start | bytes 589832 | tf_op jit(solution)/shard_map/ppermute | solution.py:379
  9.1 18.3 %collective-permute-start.5 = (bf16[3,4,64,128]{3,2,1,0:T(8,128)(2,1)}, bf16[3,4,64,128]{3,2,1,0:T(8,128)(2,1)S(1)}, u32[]{:S(2)}, u32[]{:S(2)}) collective-permute-start(bf16[3,4,64,128]{3,2,1,0:T(8,128)(2,1)} %get-tuple-element.33), channel_id=1, source_target_pairs={{0,4},{1,5},{2,6},{3,7},{4,0},{5,1},{6,2},{7,3},{8,12},{9,13},{10,... | collective-permute-start | bytes 589832 | tf_op jit(solution)/shard_map/ppermute | solution.py:379
  12.1 28.3 %collective-permute-start.6 = (bf16[3,4,64,128]{3,2,1,0:T(8,128)(2,1)}, bf16[3,4,64,128]{3,2,1,0:T(8,128)(2,1)S(1)}, u32[]{:S(2)}, u32[]{:S(2)}) collective-permute-start(bf16[3,4,64,128]{3,2,1,0:T(8,128)(2,1)} %get-tuple-element.34), channel_id=1, source_target_pairs={{0,5},{1,4},{2,7},{3,6},{4,1},{5,0},{6,3},{7,2},{8,13},{9,12},{10,... | collective-permute-start | bytes 589832 | tf_op jit(solution)/shard_map/ppermute | solution.py:379
  13.3 27.1 %collective-permute-start.7 = (bf16[3,4,64,128]{3,2,1,0:T(8,128)(2,1)}, bf16[3,4,64,128]{3,2,1,0:T(8,128)(2,1)S(1)}, u32[]{:S(2)}, u32[]{:S(2)}) collective-permute-start(bf16[3,4,64,128]{3,2,1,0:T(8,128)(2,1)} %get-tuple-element.35), channel_id=1, source_target_pairs={{0,6},{1,7},{2,4},{3,5},{4,2},{5,3},{6,0},{7,1},{8,14},{9,15},{10,... | collective-permute-start | bytes 589832 | tf_op jit(solution)/shard_map/ppermute | solution.py:379
  23.2 17.2 %collective-permute-start.8 = (bf16[3,4,64,128]{3,2,1,0:T(8,128)(2,1)}, bf16[3,4,64,128]{3,2,1,0:T(8,128)(2,1)S(1)}, u32[]{:S(2)}, u32[]{:S(2)}) collective-permute-start(bf16[3,4,64,128]{3,2,1,0:T(8,128)(2,1)} %get-tuple-element.36), channel_id=1, source_target_pairs={{0,7},{1,6},{2,5},{3,4},{4,3},{5,2},{6,1},{7,0},{8,15},{9,14},{10,... | collective-permute-start | bytes 589832 | tf_op jit(solution)/shard_map/ppermute | solution.py:379
  24.9 27.4 %collective-permute-start = (bf16[2,256,128]{2,1,0:T(8,128)(2,1)}, bf16[2,256,128]{2,1,0:T(8,128)(2,1)S(1)}, u32[]{:S(2)}, u32[]{:S(2)}) collective-permute-start(bf16[2,256,128]{2,1,0:T(8,128)(2,1)} %get-tuple-element.28), channel_id=1, source_target_pairs={{0,1},{1,0},{2,3},{3,2},{4,5},{5,4},{6,7},{7,6},{8,9},{9,8},{10,11... | collective-permute-start | bytes 393224 | tf_op jit(solution)/shard_map/ppermute | solution.py:379
  27.4 29.7 %collective-permute-start.1 = (bf16[2,256,128]{2,1,0:T(8,128)(2,1)}, bf16[2,256,128]{2,1,0:T(8,128)(2,1)S(1)}, u32[]{:S(2)}, u32[]{:S(2)}) collective-permute-start(bf16[2,256,128]{2,1,0:T(8,128)(2,1)} %get-tuple-element.29), channel_id=1, source_target_pairs={{1,2},{3,4},{5,6},{2,1},{4,3},{6,5},{9,10},{11,12},{13,14},{10,9},... | collective-permute-start | bytes 393224 | tf_op jit(solution)/shard_map/ppermute | solution.py:454
  28.2 33.7 %copy-start = (bf16[2,4,256,128]{3,2,1,0:T(8,128)(2,1)S(1)}, bf16[2,4,256,128]{3,2,1,0:T(8,128)(2,1)}, u32[]{:S(2)}) copy-start(bf16[2,4,256,128]{3,2,1,0:T(8,128)(2,1)} %cot_ref.3) | copy-start | bytes 1572868
  42.9 23.5 %copy-start.5 = (f32[2048]{0:T(1024)S(1)}, f32[2048]{0:T(1024)}, u32[]{:S(2)}) copy-start(f32[2048]{0:T(1024)} %param.11) | copy-start | bytes 24580
  42.9 14.2 %collective-permute-start.9 = (bf16[4,64,128]{2,1,0:T(8,128)(2,1)S(1)}, bf16[4,64,128]{2,1,0:T(8,128)(2,1)S(1)}, u32[]{:S(2)}, u32[]{:S(2)}) collective-permute-start(bf16[4,64,128]{2,1,0:T(8,128)(2,1)S(1)} %get-tuple-element.38), channel_id=1, source_target_pairs={{0,1},{1,0},{2,3},{3,2},{4,5},{5,4},{6,7},{7,6},{8,9},{9,8},{10,11... | collective-permute-start | bytes 196616 | tf_op jit(solution)/shard_map/ppermute | solution.py:379
  43.0 16.4 %collective-permute-start.10 = (bf16[4,64,128]{2,1,0:T(8,128)(2,1)S(1)}, bf16[4,64,128]{2,1,0:T(8,128)(2,1)S(1)}, u32[]{:S(2)}, u32[]{:S(2)}) collective-permute-start(bf16[4,64,128]{2,1,0:T(8,128)(2,1)S(1)} %get-tuple-element.39), channel_id=1, source_target_pairs={{0,2},{1,3},{2,0},{3,1},{4,6},{5,7},{6,4},{7,5},{8,10},{9,11},{10,... | collective-permute-start | bytes 196616 | tf_op jit(solution)/shard_map/ppermute | solution.py:379
  52.3 9.8 %collective-permute-start.11 = (bf16[4,64,128]{2,1,0:T(8,128)(2,1)S(1)}, bf16[4,64,128]{2,1,0:T(8,128)(2,1)S(1)}, u32[]{:S(2)}, u32[]{:S(2)}) collective-permute-start(bf16[4,64,128]{2,1,0:T(8,128)(2,1)S(1)} %get-tuple-element.40), channel_id=1, source_target_pairs={{0,3},{1,2},{2,1},{3,0},{4,7},{5,6},{6,5},{7,4},{8,11},{9,10},{10,... | collective-permute-start | bytes 196616 | tf_op jit(solution)/shard_map/ppermute | solution.py:379
  52.3 9.8 %collective-permute-start.12 = (bf16[4,64,128]{2,1,0:T(8,128)(2,1)S(1)}, bf16[4,64,128]{2,1,0:T(8,128)(2,1)S(1)}, u32[]{:S(2)}, u32[]{:S(2)}) collective-permute-start(bf16[4,64,128]{2,1,0:T(8,128)(2,1)S(1)} %get-tuple-element.41), channel_id=1, source_target_pairs={{0,4},{1,5},{2,6},{3,7},{4,0},{5,1},{6,2},{7,3},{8,12},{9,13},{10,... | collective-permute-start | bytes 196616 | tf_op jit(solution)/shard_map/ppermute | solution.py:379
  57.1 6.2 %collective-permute-start.13 = (bf16[4,64,128]{2,1,0:T(8,128)(2,1)S(1)}, bf16[4,64,128]{2,1,0:T(8,128)(2,1)S(1)}, u32[]{:S(2)}, u32[]{:S(2)}) collective-permute-start(bf16[4,64,128]{2,1,0:T(8,128)(2,1)S(1)} %get-tuple-element.42), channel_id=1, source_target_pairs={{0,5},{1,4},{2,7},{3,6},{4,1},{5,0},{6,3},{7,2},{8,13},{9,12},{10,... | collective-permute-start | bytes 196616 | tf_op jit(solution)/shard_map/ppermute | solution.py:379
  57.1 6.2 %collective-permute-start.14 = (bf16[4,64,128]{2,1,0:T(8,128)(2,1)S(1)}, bf16[4,64,128]{2,1,0:T(8,128)(2,1)S(1)}, u32[]{:S(2)}, u32[]{:S(2)}) collective-permute-start(bf16[4,64,128]{2,1,0:T(8,128)(2,1)S(1)} %get-tuple-element.43), channel_id=1, source_target_pairs={{0,6},{1,7},{2,4},{3,5},{4,2},{5,3},{6,0},{7,1},{8,14},{9,15},{10,... | collective-permute-start | bytes 196616 | tf_op jit(solution)/shard_map/ppermute | solution.py:379
  59.4 7.0 %collective-permute-start.15 = (bf16[4,64,128]{2,1,0:T(8,128)(2,1)S(1)}, bf16[4,64,128]{2,1,0:T(8,128)(2,1)S(1)}, u32[]{:S(2)}, u32[]{:S(2)}) collective-permute-start(bf16[4,64,128]{2,1,0:T(8,128)(2,1)S(1)} %get-tuple-element.44), channel_id=1, source_target_pairs={{0,7},{1,6},{2,5},{3,4},{4,3},{5,2},{6,1},{7,0},{8,15},{9,14},{10,... | collective-permute-start | bytes 196616 | tf_op jit(solution)/shard_map/ppermute | solution.py:379
  66.4 31.3 %copy-start.4 = (bf16[9,128,128]{2,1,0:T(8,128)(2,1)S(1)}, bf16[9,128,128]{2,1,0:T(8,128)(2,1)}, u32[]{:S(2)}) copy-start(bf16[9,128,128]{2,1,0:T(8,128)(2,1)} %param.12) | copy-start | bytes 884740
  69.5 4.4 %collective-permute-start.16 = (bf16[288,128]{1,0:T(8,128)(2,1)S(1)}, bf16[288,128]{1,0:T(8,128)(2,1)S(1)}, u32[]{:S(2)}, u32[]{:S(2)}) collective-permute-start(bf16[288,128]{1,0:T(8,128)(2,1)S(1)} %get-tuple-element.47), channel_id=1, source_target_pairs={{0,1},{1,0},{2,3},{3,2},{4,5},{5,4},{6,7},{7,6},{8,9},{9,8},{10,11... | collective-permute-start | bytes 221192 | tf_op jit(solution)/shard_map/ppermute | solution.py:397
  71.1 4.4 %collective-permute-start.18 = (bf16[288,128]{1,0:T(8,128)(2,1)S(1)}, bf16[288,128]{1,0:T(8,128)(2,1)S(1)}, u32[]{:S(2)}, u32[]{:S(2)}) collective-permute-start(bf16[288,128]{1,0:T(8,128)(2,1)S(1)} %get-tuple-element.50), channel_id=1, source_target_pairs={{0,16},{1,17},{2,18},{3,19},{4,20},{5,21},{6,22},{7,23},{8,24},{9,... | collective-permute-start | bytes 221192 | tf_op jit(solution)/shard_map/ppermute | solution.py:397
  72.1 5.3 %collective-permute-start.19 = (bf16[288,128]{1,0:T(8,128)(2,1)S(1)}, bf16[288,128]{1,0:T(8,128)(2,1)S(1)}, u32[]{:S(2)}, u32[]{:S(2)}) collective-permute-start(bf16[288,128]{1,0:T(8,128)(2,1)S(1)} %get-tuple-element.51), channel_id=1, source_target_pairs={{0,17},{1,16},{2,19},{3,18},{4,21},{5,20},{6,23},{7,22},{8,25},{9,... | collective-permute-start | bytes 221192 | tf_op jit(solution)/shard_map/ppermute | solution.py:397
  77.4 1.3 %collective-permute-start.20 = (f32[144,128]{1,0:T(8,128)S(1)}, f32[144,128]{1,0:T(8,128)S(1)}, u32[]{:S(2)}, u32[]{:S(2)}) collective-permute-start(f32[144,128]{1,0:T(8,128)S(1)} %get-tuple-element.53), channel_id=1, source_target_pairs={{0,8},{8,0},{16,24},{24,16},{1,9},{9,1},{17,25},{25,17},{2,10},{10... | collective-permute-start | bytes 221192 | tf_op jit(solution)/shard_map/ppermute | solution.py:401
  77.5 15.3 %collective-permute-start.17 = (bf16[2,256,128]{2,1,0:T(8,128)(2,1)S(1)}, bf16[2,256,128]{2,1,0:T(8,128)(2,1)S(1)}, u32[]{:S(2)}, u32[]{:S(2)}) collective-permute-start(bf16[2,256,128]{2,1,0:T(8,128)(2,1)S(1)} %hold.2), channel_id=1, source_target_pairs={{0,1},{1,0},{2,3},{3,2},{4,5},{5,4},{6,7},{7,6},{8,9},{9,8},{10,11... | collective-permute-start | bytes 393224 | tf_op jit(solution)/shard_map/ppermute | solution.py:379
  78.8 5.8 %collective-permute-start.21 = (bf16[144,128]{1,0:T(8,128)(2,1)S(1)}, bf16[144,128]{1,0:T(8,128)(2,1)S(1)}, u32[]{:S(2)}, u32[]{:S(2)}) collective-permute-start(bf16[144,128]{1,0:T(8,128)(2,1)S(1)} %sum_cores.1.refs_0_), channel_id=1, source_target_pairs={{0,6},{1,7},{2,4},{3,5},{4,2},{5,3},{6,0},{7,1},{8,14},{9,15},{10,... | collective-permute-start | bytes 110600 | tf_op jit(solution)/shard_map/ppermute | solution.py:379
  84.6 9.5 %collective-permute-start.22 = (bf16[2,256,128]{2,1,0:T(8,128)(2,1)S(1)}, bf16[2,256,128]{2,1,0:T(8,128)(2,1)S(1)}, u32[]{:S(2)}, u32[]{:S(2)}) collective-permute-start(bf16[2,256,128]{2,1,0:T(8,128)(2,1)S(1)} %hold.3), channel_id=1, source_target_pairs={{1,2},{3,4},{5,6},{2,1},{4,3},{6,5},{9,10},{11,12},{13,14},{10,9},... | collective-permute-start | bytes 393224 | tf_op jit(solution)/shard_map/ppermute | solution.py:527
  85.3 5.7 %collective-permute-start.24 = (bf16[144,128]{1,0:T(8,128)(2,1)S(1)}, bf16[144,128]{1,0:T(8,128)(2,1)S(1)}, u32[]{:S(2)}, u32[]{:S(2)}) collective-permute-start(bf16[144,128]{1,0:T(8,128)(2,1)S(1)} %sum_cores.1.refs_0_), channel_id=1, source_target_pairs={{0,4},{1,5},{2,6},{3,7},{4,0},{5,1},{6,2},{7,3},{8,12},{9,13},{10,... | collective-permute-start | bytes 110600 | tf_op jit(solution)/shard_map/ppermute | solution.py:379
  87.4 5.4 %collective-permute-start.23 = (bf16[144,128]{1,0:T(8,128)(2,1)S(1)}, bf16[144,128]{1,0:T(8,128)(2,1)S(1)}, u32[]{:S(2)}, u32[]{:S(2)}) collective-permute-start(bf16[144,128]{1,0:T(8,128)(2,1)S(1)} %sum_cores.1.refs_0_), channel_id=1, source_target_pairs={{0,2},{1,3},{2,0},{3,1},{4,6},{5,7},{6,4},{7,5},{8,10},{9,11},{10,... | collective-permute-start | bytes 110600 | tf_op jit(solution)/shard_map/ppermute | solution.py:379
  92.9 1.3 %collective-permute-start.25 = (bf16[144,128]{1,0:T(8,128)(2,1)S(1)}, bf16[144,128]{1,0:T(8,128)(2,1)S(1)}, u32[]{:S(2)}, u32[]{:S(2)}) collective-permute-start(bf16[144,128]{1,0:T(8,128)(2,1)S(1)} %sum_planes.1.own_ref), channel_id=1, source_target_pairs={{0,8},{8,0},{16,24},{24,16},{1,9},{9,1},{17,25},{25,17},{2,10},{10... | collective-permute-start | bytes 110600 | tf_op jit(solution)/shard_map/ppermute | solution.py:401
  94.2 5.8 %collective-permute-start.28 = (bf16[288,128]{1,0:T(8,128)(2,1)S(1)}, bf16[288,128]{1,0:T(8,128)(2,1)S(1)}, u32[]{:S(2)}, u32[]{:S(2)}) collective-permute-start(bf16[288,128]{1,0:T(8,128)(2,1)S(1)} %join_cores.1.refs_0_), channel_id=1, source_target_pairs={{0,17},{1,16},{2,19},{3,18},{4,21},{5,20},{6,23},{7,22},{8,25},{9,... | collective-permute-start | bytes 221192 | tf_op jit(solution)/shard_map/ppermute | solution.py:397
  96.0 5.1 %collective-permute-start.27 = (bf16[288,128]{1,0:T(8,128)(2,1)S(1)}, bf16[288,128]{1,0:T(8,128)(2,1)S(1)}, u32[]{:S(2)}, u32[]{:S(2)}) collective-permute-start(bf16[288,128]{1,0:T(8,128)(2,1)S(1)} %join_cores.1.refs_0_), channel_id=1, source_target_pairs={{0,16},{1,17},{2,18},{3,19},{4,20},{5,21},{6,22},{7,23},{8,24},{9,... | collective-permute-start | bytes 221192 | tf_op jit(solution)/shard_map/ppermute | solution.py:397
  97.1 4.4 %collective-permute-start.26 = (bf16[288,128]{1,0:T(8,128)(2,1)S(1)}, bf16[288,128]{1,0:T(8,128)(2,1)S(1)}, u32[]{:S(2)}, u32[]{:S(2)}) collective-permute-start(bf16[288,128]{1,0:T(8,128)(2,1)S(1)} %join_cores.1.refs_0_), channel_id=1, source_target_pairs={{0,1},{1,0},{2,3},{3,2},{4,5},{5,4},{6,7},{7,6},{8,9},{9,8},{10,11... | collective-permute-start | bytes 221192 | tf_op jit(solution)/shard_map/ppermute | solution.py:397

commit v11 on v8

--- a/solution.py
+++ b/solution.py
@@ -215,6 +215,10 @@
     )
 
 
+def rows_at(place, rows):
+    return pl.ds(pl.multiple_of(place * rows, rows), rows)
+
+
 def around(odd, near, far):
     return jnp.where(odd == 1, near, far), jnp.where(odd == 1, far, near)
 
@@ -233,9 +237,9 @@
                     out_ref[down * width : (down + 1) * width, start : start + columns] = turned
 
 
-def norm_kernel(chunk_rows, lengths_ref, index_ref, gain_ref, turned_ref, *refs):
-    image_ref, near_ref, far_ref, grad_ref, attended, pixels, windows, grads = refs[-8:]
-    for distance, ref in enumerate(refs[:-8]):
+def norm_kernel(lengths_ref, index_ref, core_ref, gain_ref, turned_ref, *refs):
+    image_ref, near_ref, far_ref, keep_ref, send_ref, attended, pixels, windows, grads = refs[-9:]
+    for distance, ref in enumerate(refs[:-9]):
         attended[lax.bitwise_xor(index_ref[0], distance)] = ref[...]
     heads = gain_ref.shape[0]
     regions = image_ref.shape[0]
@@ -287,8 +291,9 @@
     filled = 9 * width
     if filled < grads.shape[0]:
         grads[filled:, :] = jnp.zeros((grads.shape[0] - filled, width), jnp.float32)
-    for chunk in range(grad_ref.shape[0]):
-        grad_ref[chunk] = grads[chunk * chunk_rows : (chunk + 1) * chunk_rows, :].astype(jnp.bfloat16)
+    half = keep_ref.shape[0]
+    keep_ref[...] = grads[rows_at(core_ref[0], half), :]
+    send_ref[...] = grads[rows_at(1 - core_ref[0], half), :]
 
 
 def decode_kernel(index_ref, image_ref, near_ref, far_ref, weight_ref, out_ref, done_ref, padded):
@@ -318,24 +323,36 @@
                 strips.pop(0)
 
 
+def add_pairs(terms):
+    while len(terms) > 1:
+        paired = [one + other for one, other in zip(terms[::2], terms[1::2])]
+        terms = paired + terms[2 * len(paired) :]
+    return terms[0]
+
+
+def sum_cores_kernel(quad_ref, keep_ref, other_ref, *refs):
+    total = refs[-1]
+    total[...] = keep_ref[...] + other_ref[...]
+    for distance, ref in enumerate(refs[:-1]):
+        rows = rows_at(lax.bitwise_xor(quad_ref[0], distance), ref.shape[0])
+        ref[...] = total[rows, :].astype(jnp.bfloat16)
+
+
 def sum_kernel(count, factor, *refs):
-    out_ref = refs[-1]
-    totals = [ref[...].astype(jnp.float32) for ref in refs[:count]]
-    if count == 1:
-        totals = [totals[0][part] for part in range(totals[0].shape[0])]
-    while len(totals) > 1:
-        paired = [one + other for one, other in zip(totals[::2], totals[1::2])]
-        totals = paired + totals[2 * len(paired) :]
-    out_ref[...] = (totals[0] * factor).astype(jnp.bfloat16)
-
-
-def spread_kernel(plane_ref, *refs):
-    out_ref = refs[-1]
-    chunk_rows = refs[0].shape[0]
+    total = add_pairs([ref[...].astype(jnp.float32) for ref in refs[:count]])
+    refs[-1][...] = (total * factor).astype(jnp.bfloat16)
+
+
+def join_kernel(quad_ref, *refs):
     for distance, ref in enumerate(refs[:-1]):
-        start = lax.bitwise_xor(plane_ref[0], distance) * chunk_rows
-        rows = pl.ds(pl.multiple_of(start, chunk_rows), chunk_rows)
-        out_ref[rows, :] = ref[...].astype(jnp.float32)
+        rows = rows_at(lax.bitwise_xor(quad_ref[0], distance), ref.shape[0])
+        refs[-1][rows, :] = ref[...]
+
+
+def spread_kernel(core_ref, own_ref, other_ref, out_ref):
+    half = own_ref.shape[0]
+    out_ref[rows_at(core_ref[0], half), :] = own_ref[...].astype(jnp.float32)
+    out_ref[rows_at(1 - core_ref[0], half), :] = other_ref[...].astype(jnp.float32)
 
 
 def trade(values, distance):
@@ -350,22 +367,19 @@
     return inner
 
 
-def planes_of(inner):
-    outer, seq_count = (lax.axis_size("dp"), lax.axis_size("seq"))
-    return [
-        [o * seq_count + start + lane for o in range(outer) for lane in range(inner)]
-        for start in range(0, seq_count, inner)
-    ]
-
-
-def trade_in_plane(values, distance, inner):
+def trade_chips(values, distance, inner):
     seq_count = lax.axis_size("seq")
     pairs = []
     for outer in range(lax.axis_size("dp")):
         for seq in range(seq_count):
-            partner, lane = divmod((outer * inner + seq % inner) ^ distance, inner)
-            pairs.append((outer * seq_count + seq, partner * seq_count + seq - seq % inner + lane))
+            chip, lane = divmod((outer // 2 * inner + seq % inner) ^ distance, inner)
+            partner = (2 * chip + outer % 2) * seq_count + seq - seq % inner + lane
+            pairs.append((outer * seq_count + seq, partner))
     return lax.ppermute(values, ("dp", "seq"), pairs)
+
+
+def trade_cores(values):
+    return lax.ppermute(values, "dp", [(i, i ^ 1) for i in range(lax.axis_size("dp"))])
 
 
 def body(query_rows, key_rows, value_rows, region_lengths, norm_gain, conv_weight, cotangent):
@@ -374,8 +388,11 @@
     seq_count = lax.axis_size("seq")
     seq_index = lax.axis_index("seq")
     inner = inner_size(seq_count)
-    plane_size = lax.axis_size("dp") * inner
-    plane_index = lax.axis_index("dp") * inner + lax.bitwise_and(seq_index, inner - 1)
+    quad_size = lax.axis_size("dp") // 2 * inner
+    dp_index = lax.axis_index("dp")
+    lane = lax.bitwise_and(seq_index, inner - 1)
+    quad = (lax.shift_right_logical(dp_index, 1) * inner + lane).reshape(1)
+    core = lax.bitwise_and(dp_index, 1).reshape(1)
     columns = tokens * PATCH
     capacity = seq_count * tokens
     per_device = regions * HEADS // seq_count
@@ -446,38 +463,46 @@
         [SMEM()] + [VMEM()] * 3,
         moved=8 * cotangent.size,
     )(index, cotangent, cot_near, cot_far)
-    chunk_rows = -(-9 * width // (16 * plane_size)) * 16
+    chunk_rows = -(-9 * width // (32 * quad_size)) * 16
+    half_rows = quad_size * chunk_rows
     pixel_rows = regions * PATCH * columns
     conv_flops = 18 * pixel_rows * width * width
-    part_shape = jax.ShapeDtypeStruct((chunk_rows, width), jnp.bfloat16)
-    image, near, far, parts = call(
-        functools.partial(norm_kernel, chunk_rows),
+    chunk_moved = 8 * chunk_rows * width
+    image, near, far, keep, send = call(
+        norm_kernel,
         "norm_and_gradient",
         [jax.ShapeDtypeStruct((regions, PATCH, columns, width), jnp.bfloat16)]
         + [edge_shape] * 2
-        + [jax.ShapeDtypeStruct((plane_size, chunk_rows, width), jnp.bfloat16)],
-        [SMEM(), SMEM()] + [VMEM()] * (2 + seq_count),
+        + [jax.ShapeDtypeStruct((half_rows, width), jnp.float32)] * 2,
+        [SMEM()] * 3 + [VMEM()] * (2 + seq_count),
         scratch=[
             pltpu.VMEM((seq_count,) + mixed[0].shape, jnp.bfloat16),
             pltpu.VMEM((regions, PATCH, columns + 2 * RIM, width), jnp.float32),
             pltpu.VMEM((pixel_rows, 3 * width), jnp.bfloat16),
-            pltpu.VMEM((plane_size * chunk_rows, width), jnp.float32),
+            pltpu.VMEM((2 * half_rows, width), jnp.float32),
         ],
         flops=conv_flops,
         moved=4 * local_bytes,
-    )(region_lengths, index, norm_gain.reshape(HEADS, width), turned, *attended)
-    parts = lax.all_to_all(
-        parts, ("dp", "seq"), 0, 0, axis_index_groups=planes_of(inner), tiled=True
-    )
+    )(region_lengths, index, core, norm_gain.reshape(HEADS, width), turned, *attended)
+    chunk_shape = jax.ShapeDtypeStruct((chunk_rows, width), jnp.bfloat16)
+    parts = call(
+        sum_cores_kernel,
+        "sum_cores",
+        [chunk_shape] * quad_size,
+        [SMEM()] + [VMEM()] * 2,
+        scratch=[pltpu.VMEM((half_rows, width), jnp.float32)],
+        moved=quad_size * chunk_moved,
+    )(quad, keep, trade_cores(send))
     near = trade(near, 1)
     far = lax.ppermute(far, "seq", far_pairs)
+    distances = range(1, quad_size)
     plane_sum = call(
-        functools.partial(sum_kernel, 1, 1.0),
-        "sum_plane",
-        part_shape,
-        [VMEM()],
-        moved=4 * parts.size,
-    )(parts)
+        functools.partial(sum_kernel, quad_size, 1.0),
+        "sum_chips",
+        chunk_shape,
+        [VMEM()] * quad_size,
+        moved=chunk_moved,
+    )(parts[0], *[trade_chips(parts[distance], distance, inner) for distance in distances])
     plane_sums = [plane_sum] + [
         trade(plane_sum, distance) for distance in range(inner, seq_count, inner)
     ]
@@ -496,18 +521,24 @@
     total = call(
         functools.partial(sum_kernel, len(plane_sums), 1.0 / math.sqrt(PATCH * columns)),
         "sum_planes",
-        part_shape,
+        chunk_shape,
         [VMEM()] * len(plane_sums) + [ANY()],
-        moved=4 * len(plane_sums) * chunk_rows * width,
+        moved=chunk_moved,
     )(*plane_sums, done)
-    totals = [total] + [trade_in_plane(total, distance, inner) for distance in range(1, plane_size)]
+    joined = call(
+        join_kernel,
+        "join_chips",
+        jax.ShapeDtypeStruct((half_rows, width), jnp.bfloat16),
+        [SMEM()] + [VMEM()] * quad_size,
+        moved=quad_size * chunk_moved,
+    )(quad, total, *[trade_chips(total, distance, inner) for distance in distances])
     weight_grad = call(
         spread_kernel,
         "spread_sums",
-        jax.ShapeDtypeStruct((plane_size * chunk_rows, width), jnp.float32),
-        [SMEM()] + [VMEM()] * plane_size,
-        moved=6 * plane_size * chunk_rows * width,
-    )(plane_index.reshape(1), *totals)
+        jax.ShapeDtypeStruct((2 * half_rows, width), jnp.float32),
+        [SMEM()] + [VMEM()] * 2,
+        moved=2 * quad_size * chunk_moved,
+    )(core, joined, trade_cores(joined))
     return (decoded, weight_grad[: 9 * width].reshape(conv_weight.shape))
 
 

time: 98 us -> 97.3 us (level)
  starting transfers between devices: 52.9 us -> 49.4 us
  waiting for transfers between devices: 30.5 us -> 33.6 us
    ppermute x7 -> x8, waiting for transfers between devices: 2.69 us -> 9.17 us  [the longest x6 7.81 us: trade_chips(): return lax.ppermute(values, ('dp', 'seq'), pairs)]
    all_to_all x1 -> x0, waiting for transfers between devices: 3.97 us -> none  [body(): lax.all_to_all(parts, ('dp', 'seq'), 0, 0, axis_index_groups=planes_of(in...]
    all_to_all x1 -> x0, starting transfers between devices: 3.42 us -> none  [body(): lax.all_to_all(parts, ('dp', 'seq'), 0, 0, axis_index_groups=planes_of(in...]
    pallas_call x3 -> x5, Pallas kernels: 4.54 us -> 4.01 us  [the longest x1 3.07 us: body(): call(norm_kernel, 'norm_and_gradient', [jax.ShapeDtypeStruct((regions, PA...]
    ppermute x7 -> x8, starting transfers between devices: 6.88 us -> 7.35 us  [the longest x6 7.2 us: trade_chips(): return lax.ppermute(values, ('dp', 'seq'), pairs)]
where the time goes in v11:
time: 97.3 us; the launch traced here: 96.8 us
  starting transfers between devices  49.4 us (51%)
  waiting for transfers between devices  33.6 us (35%)
  Pallas kernels  12.8 us (13%)
    ppermute x19, starting transfers between devices, trade(): return lax.ppermute(values, 'seq', pairs)  40.6 us
    ppermute x19, waiting for transfers between devices, trade(): return lax.ppermute(values, 'seq', pairs)  24.4 us
    ppermute x6, waiting for transfers between devices, trade_chips(): return lax.ppermute(values, ('dp', 'seq'), pairs)  7.81 us
    ppermute x6, starting transfers between devices, trade_chips(): return lax.ppermute(values, ('dp', 'seq'), pairs)  7.2 us
    pallas_call x1, Pallas kernels, body(): call(functools.partial(pack_kernel, regions, per_device), 'pack', [chunk_...  3.81 us
    pallas_call x1, Pallas kernels, body(): call(norm_kernel, 'norm_and_gradient', [jax.ShapeDtypeStruct((regions, PA...  3.07 us
    pallas_call x1, Pallas kernels, body(): call(decode_kernel, 'decode', [jax.ShapeDtypeStruct(cotangent.shape, jnp....  2.23 us
    pallas_call x1, Pallas kernels, body(): call(functools.partial(attend_kernel, block_rows, group, order), 'attend'...  2.08 us
  transfers between devices with their start and end apart: 29, of which 12 were waited for; matrix products, arithmetic and copies ran while one was open for 0% of the time, Pallas kernels for 5%

profile of v11, /device:TPU:0, one launch (start us, length us, event | category | flops | bytes accessed | tf_op | source)
XLA Modules:
  0.0 96.8 jit_solution(8792584191523773327)
XLA Ops:
  0.7 3.8 %pack.1 = (bf16[3,4,64,128]{3,2,1,0:T(8,128)(2,1)}, bf16[3,4,64,128]{3,2,1,0:T(8,128)(2,1)}, bf16[3,4,64,128]{3,2,1,0:T(8,128)(2,1)}, bf16[3,4,64,128]{3,2,1,0:T...) custom-call(s32[1]{0:T(128)} %bitcast.index_ref, ...), custom_call_target="tpu_custom_call" | custom-call | bytes 3145728 | tf_op jit(solution)/shard_map/pack/pallas_call | solution.py:406
  4.5 3.0 %collective-permute-start.2 = (bf16[3,4,64,128]{3,2,1,0:T(8,128)(2,1)}, bf16[3,4,64,128]{3,2,1,0:T(8,128)(2,1)S(1)}, u32[]{:S(2)}, u32[]{:S(2)}) collective-permute-start(bf16[3,4,64,128]{3,2,1,0:T(8,128)(2,1)} %get-tuple-element.32), channel_id=1, source_target_pairs={{0,1},{1,0},{2,3},{3,2},{4,5},{5,4},{6,7},{7,6},{8,9},{9,8},{10,11... | collective-permute-start | bytes 589832 | tf_op jit(solution)/shard_map/ppermute | solution.py:360
  7.5 1.6 %collective-permute-start.3 = (bf16[3,4,64,128]{3,2,1,0:T(8,128)(2,1)}, bf16[3,4,64,128]{3,2,1,0:T(8,128)(2,1)S(1)}, u32[]{:S(2)}, u32[]{:S(2)}) collective-permute-start(bf16[3,4,64,128]{3,2,1,0:T(8,128)(2,1)} %get-tuple-element.33), channel_id=1, source_target_pairs={{0,2},{1,3},{2,0},{3,1},{4,6},{5,7},{6,4},{7,5},{8,10},{9,11},{10,... | collective-permute-start | bytes 589832 | tf_op jit(solution)/shard_map/ppermute | solution.py:360
  9.1 0.0 collective-permute-start.4
  9.1 3.0 %collective-permute-start.5 = (bf16[3,4,64,128]{3,2,1,0:T(8,128)(2,1)}, bf16[3,4,64,128]{3,2,1,0:T(8,128)(2,1)S(1)}, u32[]{:S(2)}, u32[]{:S(2)}) collective-permute-start(bf16[3,4,64,128]{3,2,1,0:T(8,128)(2,1)} %get-tuple-element.35), channel_id=1, source_target_pairs={{0,4},{1,5},{2,6},{3,7},{4,0},{5,1},{6,2},{7,3},{8,12},{9,13},{10,... | collective-permute-start | bytes 589832 | tf_op jit(solution)/shard_map/ppermute | solution.py:360
  12.1 1.3 %collective-permute-start.6 = (bf16[3,4,64,128]{3,2,1,0:T(8,128)(2,1)}, bf16[3,4,64,128]{3,2,1,0:T(8,128)(2,1)S(1)}, u32[]{:S(2)}, u32[]{:S(2)}) collective-permute-start(bf16[3,4,64,128]{3,2,1,0:T(8,128)(2,1)} %get-tuple-element.36), channel_id=1, source_target_pairs={{0,5},{1,4},{2,7},{3,6},{4,1},{5,0},{6,3},{7,2},{8,13},{9,12},{10,... | collective-permute-start | bytes 589832 | tf_op jit(solution)/shard_map/ppermute | solution.py:360
  13.3 3.6 %collective-permute-start.7 = (bf16[3,4,64,128]{3,2,1,0:T(8,128)(2,1)}, bf16[3,4,64,128]{3,2,1,0:T(8,128)(2,1)S(1)}, u32[]{:S(2)}, u32[]{:S(2)}) collective-permute-start(bf16[3,4,64,128]{3,2,1,0:T(8,128)(2,1)} %get-tuple-element.37), channel_id=1, source_target_pairs={{0,6},{1,7},{2,4},{3,5},{4,2},{5,3},{6,0},{7,1},{8,14},{9,15},{10,... | collective-permute-start | bytes 589832 | tf_op jit(solution)/shard_map/ppermute | solution.py:360
  16.9 6.2 %collective-permute-done.3.refs_1_ = bf16[3,4,64,128]{3,2,1,0:T(8,128)(2,1)S(1)} collective-permute-done((bf16[3,4,64,128]{3,2,1,0:T(8,128)(2,1)}, bf16[3,4,64,128]{3,2,1,0:T(8,128)(2,1)S(1)}, u32[]{:S(2)}, u32[]{:S(2)}) %collective-permute-start.3) | collective-permute-done | bytes 196640 | tf_op jit(solution)/shard_map/ppermute | solution.py:360
  23.2 0.9 collective-permute-start.8
  24.1 0.8 collective-permute-done.4.refs_2_
  24.9 2.5 %collective-permute-start = (bf16[2,256,128]{2,1,0:T(8,128)(2,1)}, bf16[2,256,128]{2,1,0:T(8,128)(2,1)S(1)}, u32[]{:S(2)}, u32[]{:S(2)}) collective-permute-start(bf16[2,256,128]{2,1,0:T(8,128)(2,1)} %get-tuple-element.30), channel_id=1, source_target_pairs={{0,1},{1,0},{2,3},{3,2},{4,5},{5,4},{6,7},{7,6},{8,9},{9,8},{10,11... | collective-permute-start | bytes 393224 | tf_op jit(solution)/shard_map/ppermute | solution.py:360
  27.4 0.7 collective-permute-start.1
  28.1 0.1 fusion.lengths_ref
  28.2 0.0 copy-start
  28.2 0.4 own_chunk.1.refs_7_
  28.6 11.8 %collective-permute-done.6.refs_4_ = bf16[3,4,64,128]{3,2,1,0:T(8,128)(2,1)S(1)} collective-permute-done((bf16[3,4,64,128]{3,2,1,0:T(8,128)(2,1)}, bf16[3,4,64,128]{3,2,1,0:T(8,128)(2,1)S(1)}, u32[]{:S(2)}, u32[]{:S(2)}) %collective-permute-start.6) | collective-permute-done | bytes 196640 | tf_op jit(solution)/shard_map/ppermute | solution.py:360
  40.4 0.0 collective-permute-done.7.refs_5_
  40.4 0.0 collective-permute-done.8.refs_6_
  40.4 2.1 %attend.1 = (bf16[4,64,128]{2,1,0:T(8,128)(2,1)S(1)}, bf16[4,64,128]{2,1,0:T(8,128)(2,1)S(1)}, bf16[4,64,128]{2,1,0:T(8,128)(2,1)S(1)}, bf16[4,64,128]{2,1,0:T(8...) custom-call(s32[1]{0:T(128)} %bitcast.index_ref, ...), custom_call_target="tpu_custom_call" | custom-call | flops 536870912 | bytes 2097152 | tf_op jit(solution)/shard_map/attend/pallas_call | solution.py:448
  42.5 0.0 copy-start.5
  42.5 0.1 collective-permute-start.9
  42.6 9.3 %collective-permute-start.10 = (bf16[4,64,128]{2,1,0:T(8,128)(2,1)S(1)}, bf16[4,64,128]{2,1,0:T(8,128)(2,1)S(1)}, u32[]{:S(2)}, u32[]{:S(2)}) collective-permute-start(bf16[4,64,128]{2,1,0:T(8,128)(2,1)S(1)} %get-tuple-element.41), channel_id=1, source_target_pairs={{0,2},{1,3},{2,0},{3,1},{4,6},{5,7},{6,4},{7,5},{8,10},{9,11},{10,... | collective-permute-start | bytes 196616 | tf_op jit(solution)/shard_map/ppermute | solution.py:360
  51.9 0.0 collective-permute-start.11
  51.9 0.0 collective-permute-done.near_ref
  51.9 4.7 %collective-permute-start.12 = (bf16[4,64,128]{2,1,0:T(8,128)(2,1)S(1)}, bf16[4,64,128]{2,1,0:T(8,128)(2,1)S(1)}, u32[]{:S(2)}, u32[]{:S(2)}) collective-permute-start(bf16[4,64,128]{2,1,0:T(8,128)(2,1)S(1)} %get-tuple-element.43), channel_id=1, source_target_pairs={{0,4},{1,5},{2,6},{3,7},{4,0},{5,1},{6,2},{7,3},{8,12},{9,13},{10,... | collective-permute-start | bytes 196616 | tf_op jit(solution)/shard_map/ppermute | solution.py:360
  56.7 0.0 collective-permute-done.1.far_ref
  56.7 0.0 collective-permute-start.13
  56.7 0.0 collective-permute-done.9.refs_1_
  56.7 2.4 %collective-permute-start.14 = (bf16[4,64,128]{2,1,0:T(8,128)(2,1)S(1)}, bf16[4,64,128]{2,1,0:T(8,128)(2,1)S(1)}, u32[]{:S(2)}, u32[]{:S(2)}) collective-permute-start(bf16[4,64,128]{2,1,0:T(8,128)(2,1)S(1)} %get-tuple-element.45), channel_id=1, source_target_pairs={{0,6},{1,7},{2,4},{3,5},{4,2},{5,3},{6,0},{7,1},{8,14},{9,15},{10,... | collective-permute-start | bytes 196616 | tf_op jit(solution)/shard_map/ppermute | solution.py:360
  59.0 2.4 %collective-permute-start.15 = (bf16[4,64,128]{2,1,0:T(8,128)(2,1)S(1)}, bf16[4,64,128]{2,1,0:T(8,128)(2,1)S(1)}, u32[]{:S(2)}, u32[]{:S(2)}) collective-permute-start(bf16[4,64,128]{2,1,0:T(8,128)(2,1)S(1)} %get-tuple-element.46), channel_id=1, source_target_pairs={{0,7},{1,6},{2,5},{3,4},{4,3},{5,2},{6,1},{7,0},{8,15},{9,14},{10,... | collective-permute-start | bytes 196616 | tf_op jit(solution)/shard_map/ppermute | solution.py:360
  61.5 0.3 turn_cotangent.1.turned_ref
  61.7 0.0 copy-start.4
  61.8 0.0 collective-permute-done.11.refs_3_
  61.8 0.0 collective-permute-done.12.refs_4_
  61.8 2.3 %collective-permute-done.13.refs_5_ = bf16[4,64,128]{2,1,0:T(8,128)(2,1)S(1)} collective-permute-done((bf16[4,64,128]{2,1,0:T(8,128)(2,1)S(1)}, bf16[4,64,128]{2,1,0:T(8,128)(2,1)S(1)}, u32[]{:S(2)}, u32[]{:S(2)}) %collective-permute-start.13) | collective-permute-done | bytes 65568 | tf_op jit(solution)/shard_map/ppermute | solution.py:360
  64.1 0.0 collective-permute-done.14.refs_6_
  64.1 2.0 %collective-permute-done.15.refs_7_ = bf16[4,64,128]{2,1,0:T(8,128)(2,1)S(1)} collective-permute-done((bf16[4,64,128]{2,1,0:T(8,128)(2,1)S(1)}, bf16[4,64,128]{2,1,0:T(8,128)(2,1)S(1)}, u32[]{:S(2)}, u32[]{:S(2)}) %collective-permute-start.15) | collective-permute-done | bytes 65568 | tf_op jit(solution)/shard_map/ppermute | solution.py:360
  66.1 3.1 %norm_and_gradient.1 = (bf16[2,4,256,128]{3,2,1,0:T(8,128)(2,1)S(1)}, bf16[2,256,128]{2,1,0:T(8,128)(2,1)S(1)}, bf16[2,256,128]{2,1,0:T(8,128)(2,1)S(1)}, f32[576,128]{1,0:T(8,128)S(1)}, f32[576,128]{1,0:T(8,128)S(1)}) custom-call(s32[2]{0:T(128)S(1)} %copy-done.6, s32[1]{0:T(128)} %bitcast.index_ref, s32[1]{0:T(128)} %bitcast.1.core_ref, ...), custom_call_target="tpu_custom_call" | custom-call | flops 603979776 | bytes 2097152 | tf_op jit(solution)/shard_map/norm_and_gradient/pallas_call | solution.py:471
  69.2 0.1 collective-permute-start.18
  69.3 1.4 %collective-permute-start.16 = (bf16[2,256,128]{2,1,0:T(8,128)(2,1)S(1)}, bf16[2,256,128]{2,1,0:T(8,128)(2,1)S(1)}, u32[]{:S(2)}, u32[]{:S(2)}) collective-permute-start(bf16[2,256,128]{2,1,0:T(8,128)(2,1)S(1)} %get-tuple-element.48), channel_id=1, source_target_pairs={{0,1},{1,0},{2,3},{3,2},{4,5},{5,4},{6,7},{7,6},{8,9},{9,8},{10,11... | collective-permute-start | bytes 393224 | tf_op jit(solution)/shard_map/ppermute | solution.py:360
  70.7 0.8 collective-permute-start.17
  71.5 0.0 collective-permute-done.18.other_ref
  71.6 2.1 %collective-permute-start.19 = (bf16[144,128]{1,0:T(8,128)(2,1)S(1)}, bf16[144,128]{1,0:T(8,128)(2,1)S(1)}, u32[]{:S(2)}, u32[]{:S(2)}) collective-permute-start(bf16[144,128]{1,0:T(8,128)(2,1)S(1)} %get-tuple-element.54), channel_id=1, source_target_pairs={{0,1},{1,0},{2,3},{3,2},{4,5},{5,4},{6,7},{7,6},{8,9},{9,8},{10,11... | collective-permute-start | bytes 110600 | tf_op jit(solution)/shard_map/ppermute | solution.py:378
  73.7 1.5 %collective-permute-start.20 = (bf16[144,128]{1,0:T(8,128)(2,1)S(1)}, bf16[144,128]{1,0:T(8,128)(2,1)S(1)}, u32[]{:S(2)}, u32[]{:S(2)}) collective-permute-start(bf16[144,128]{1,0:T(8,128)(2,1)S(1)} %get-tuple-element.55), channel_id=1, source_target_pairs={{0,16},{1,17},{2,18},{3,19},{4,20},{5,21},{6,22},{7,23},{8,24},{9,... | collective-permute-start | bytes 110600 | tf_op jit(solution)/shard_map/ppermute | solution.py:378
  75.2 0.0 collective-permute-start.21
  75.3 2.6 %collective-permute-done.19.refs_1_ = bf16[144,128]{1,0:T(8,128)(2,1)S(1)} collective-permute-done((bf16[144,128]{1,0:T(8,128)(2,1)S(1)}, bf16[144,128]{1,0:T(8,128)(2,1)S(1)}, u32[]{:S(2)}, u32[]{:S(2)}) %collective-permute-start.19) | collective-permute-done | bytes 36896 | tf_op jit(solution)/shard_map/ppermute | solution.py:378
  77.9 0.0 collective-permute-done.20.refs_2_
  77.9 2.2 %collective-permute-done.21.refs_3_ = bf16[144,128]{1,0:T(8,128)(2,1)S(1)} collective-permute-done((bf16[144,128]{1,0:T(8,128)(2,1)S(1)}, bf16[144,128]{1,0:T(8,128)(2,1)S(1)}, u32[]{:S(2)}, u32[]{:S(2)}) %collective-permute-start.21) | collective-permute-done | bytes 36896 | tf_op jit(solution)/shard_map/ppermute | solution.py:378
  80.1 2.8 %collective-permute-start.24 = (bf16[144,128]{1,0:T(8,128)(2,1)S(1)}, bf16[144,128]{1,0:T(8,128)(2,1)S(1)}, u32[]{:S(2)}, u32[]{:S(2)}) collective-permute-start(bf16[144,128]{1,0:T(8,128)(2,1)S(1)} %sum_chips.1.refs_0_), channel_id=1, source_target_pairs={{0,6},{1,7},{2,4},{3,5},{4,2},{5,3},{6,0},{7,1},{8,14},{9,15},{10,... | collective-permute-start | bytes 110600 | tf_op jit(solution)/shard_map/ppermute | solution.py:360
  82.9 0.5 collective-permute-start.23
  83.4 1.1 %collective-permute-start.22 = (bf16[144,128]{1,0:T(8,128)(2,1)S(1)}, bf16[144,128]{1,0:T(8,128)(2,1)S(1)}, u32[]{:S(2)}, u32[]{:S(2)}) collective-permute-start(bf16[144,128]{1,0:T(8,128)(2,1)S(1)} %sum_chips.1.refs_0_), channel_id=1, source_target_pairs={{0,2},{1,3},{2,0},{3,1},{4,6},{5,7},{6,4},{7,5},{8,10},{9,11},{10,... | collective-permute-start | bytes 110600 | tf_op jit(solution)/shard_map/ppermute | solution.py:360
  84.6 0.0 collective-permute-done.16.near_ref
  84.6 0.0 collective-permute-done.17.far_ref
  84.6 2.2 %decode.1 = (bf16[2,4,256,128]{3,2,1,0:T(8,128)(2,1)}, f32[8,128]{1,0:T(8,128)S(1)}) custom-call(s32[1]{0:T(128)} %bitcast.index_ref, bf16[2,4,256,128]{3,2,1,0:T(8,128)(2,1)S(1)} %get-tuple-element.47.image_ref, bf16[2,256,128]{2,1,0:T(8,128)(2,1)S(1)} %collective-permute-done.16.near_ref, bf16[2,256,128]{2,1,0:T(8,128)(2,1)S(1)} %collective-permute-done.17.far_ref, ...), custom_call_target="tpu_custom_call" | custom-call | flops 603979776 | bytes 1048576 | tf_op jit(solution)/shard_map/decode/pallas_call | solution.py:509
  86.8 1.1 %collective-permute-done.23.refs_2_ = bf16[144,128]{1,0:T(8,128)(2,1)S(1)} collective-permute-done((bf16[144,128]{1,0:T(8,128)(2,1)S(1)}, bf16[144,128]{1,0:T(8,128)(2,1)S(1)}, u32[]{:S(2)}, u32[]{:S(2)}) %collective-permute-start.23) | collective-permute-done | bytes 36896 | tf_op jit(solution)/shard_map/ppermute | solution.py:360
  88.0 1.4 %collective-permute-start.27 = (bf16[144,128]{1,0:T(8,128)(2,1)S(1)}, bf16[144,128]{1,0:T(8,128)(2,1)S(1)}, u32[]{:S(2)}, u32[]{:S(2)}) collective-permute-start(bf16[144,128]{1,0:T(8,128)(2,1)S(1)} %sum_planes.1.refs_0_), channel_id=1, source_target_pairs={{0,17},{1,16},{2,19},{3,18},{4,21},{5,20},{6,23},{7,22},{8,25},{9,... | collective-permute-start | bytes 110600 | tf_op jit(solution)/shard_map/ppermute | solution.py:378
  89.3 1.2 %collective-permute-start.26 = (bf16[144,128]{1,0:T(8,128)(2,1)S(1)}, bf16[144,128]{1,0:T(8,128)(2,1)S(1)}, u32[]{:S(2)}, u32[]{:S(2)}) collective-permute-start(bf16[144,128]{1,0:T(8,128)(2,1)S(1)} %sum_planes.1.refs_0_), channel_id=1, source_target_pairs={{0,16},{1,17},{2,18},{3,19},{4,20},{5,21},{6,22},{7,23},{8,24},{9,... | collective-permute-start | bytes 110600 | tf_op jit(solution)/shard_map/ppermute | solution.py:378
  90.5 1.0 %collective-permute-start.25 = (bf16[144,128]{1,0:T(8,128)(2,1)S(1)}, bf16[144,128]{1,0:T(8,128)(2,1)S(1)}, u32[]{:S(2)}, u32[]{:S(2)}) collective-permute-start(bf16[144,128]{1,0:T(8,128)(2,1)S(1)} %sum_planes.1.refs_0_), channel_id=1, source_target_pairs={{0,1},{1,0},{2,3},{3,2},{4,5},{5,4},{6,7},{7,6},{8,9},{9,8},{10,11... | collective-permute-start | bytes 110600 | tf_op jit(solution)/shard_map/ppermute | solution.py:378
  91.5 1.4 %collective-permute-done.27.refs_3_ = bf16[144,128]{1,0:T(8,128)(2,1)S(1)} collective-permute-done((bf16[144,128]{1,0:T(8,128)(2,1)S(1)}, bf16[144,128]{1,0:T(8,128)(2,1)S(1)}, u32[]{:S(2)}, u32[]{:S(2)}) %collective-permute-start.27) | collective-permute-done | bytes 36896 | tf_op jit(solution)/shard_map/ppermute | solution.py:378
  92.9 0.4 collective-permute-done.26.refs_2_
  93.3 1.2 %collective-permute-done.25.refs_1_ = bf16[144,128]{1,0:T(8,128)(2,1)S(1)} collective-permute-done((bf16[144,128]{1,0:T(8,128)(2,1)S(1)}, bf16[144,128]{1,0:T(8,128)(2,1)S(1)}, u32[]{:S(2)}, u32[]{:S(2)}) %collective-permute-start.25) | collective-permute-done | bytes 36896 | tf_op jit(solution)/shard_map/ppermute | solution.py:378
  94.5 0.1 collective-permute-start.28
  94.6 1.4 %collective-permute-done.28.other_ref = bf16[576,128]{1,0:T(8,128)(2,1)S(1)} collective-permute-done((bf16[576,128]{1,0:T(8,128)(2,1)S(1)}, bf16[576,128]{1,0:T(8,128)(2,1)S(1)}, u32[]{:S(2)}, u32[]{:S(2)}) %collective-permute-start.28) | collective-permute-done | bytes 147488 | tf_op jit(solution)/shard_map/ppermute | solution.py:382
  96.0 0.9 spread_sums.1
  (21 shorter events, 0.2 us)
Async XLA Ops:
  0.6 27.5 %copy-start.3 = (bf16[64,2,2048]{2,1,0:T(2,128)(2,1)S(1)}, bf16[64,2,2048]{2,1,0:T(2,128)(2,1)}, u32[]{:S(2)}) copy-start(bf16[64,2,2048]{2,1,0:T(2,128)(2,1)} %value_ref.3) | copy-start | bytes 1572868
  0.6 27.5 %copy-start.2 = (bf16[64,2,2048]{2,1,0:T(2,128)(2,1)S(1)}, bf16[64,2,2048]{2,1,0:T(2,128)(2,1)}, u32[]{:S(2)}) copy-start(bf16[64,2,2048]{2,1,0:T(2,128)(2,1)} %key_ref.3) | copy-start | bytes 1572868
  0.7 27.5 %copy-start.1 = (bf16[64,2,2048]{2,1,0:T(2,128)(2,1)S(1)}, bf16[64,2,2048]{2,1,0:T(2,128)(2,1)}, u32[]{:S(2)}) copy-start(bf16[64,2,2048]{2,1,0:T(2,128)(2,1)} %query_ref.3) | copy-start | bytes 1572868
  0.7 27.4 %copy-start.6 = (s32[2]{0:T(128)S(1)}, s32[2]{0:T(128)}, u32[]{:S(2)}) copy-start(s32[2]{0:T(128)} %lengths_ref.1) | copy-start | bytes 28
  4.5 8.9 %collective-permute-start.2 = (bf16[3,4,64,128]{3,2,1,0:T(8,128)(2,1)}, bf16[3,4,64,128]{3,2,1,0:T(8,128)(2,1)S(1)}, u32[]{:S(2)}, u32[]{:S(2)}) collective-permute-start(bf16[3,4,64,128]{3,2,1,0:T(8,128)(2,1)} %get-tuple-element.32), channel_id=1, source_target_pairs={{0,1},{1,0},{2,3},{3,2},{4,5},{5,4},{6,7},{7,6},{8,9},{9,8},{10,11... | collective-permute-start | bytes 589832 | tf_op jit(solution)/shard_map/ppermute | solution.py:360
  7.5 15.7 %collective-permute-start.3 = (bf16[3,4,64,128]{3,2,1,0:T(8,128)(2,1)}, bf16[3,4,64,128]{3,2,1,0:T(8,128)(2,1)S(1)}, u32[]{:S(2)}, u32[]{:S(2)}) collective-permute-start(bf16[3,4,64,128]{3,2,1,0:T(8,128)(2,1)} %get-tuple-element.33), channel_id=1, source_target_pairs={{0,2},{1,3},{2,0},{3,1},{4,6},{5,7},{6,4},{7,5},{8,10},{9,11},{10,... | collective-permute-start | bytes 589832 | tf_op jit(solution)/shard_map/ppermute | solution.py:360
  9.1 15.8 %collective-permute-start.4 = (bf16[3,4,64,128]{3,2,1,0:T(8,128)(2,1)}, bf16[3,4,64,128]{3,2,1,0:T(8,128)(2,1)S(1)}, u32[]{:S(2)}, u32[]{:S(2)}) collective-permute-start(bf16[3,4,64,128]{3,2,1,0:T(8,128)(2,1)} %get-tuple-element.34), channel_id=1, source_target_pairs={{0,3},{1,2},{2,1},{3,0},{4,7},{5,6},{6,5},{7,4},{8,11},{9,10},{10,... | collective-permute-start | bytes 589832 | tf_op jit(solution)/shard_map/ppermute | solution.py:360
  9.1 18.3 %collective-permute-start.5 = (bf16[3,4,64,128]{3,2,1,0:T(8,128)(2,1)}, bf16[3,4,64,128]{3,2,1,0:T(8,128)(2,1)S(1)}, u32[]{:S(2)}, u32[]{:S(2)}) collective-permute-start(bf16[3,4,64,128]{3,2,1,0:T(8,128)(2,1)} %get-tuple-element.35), channel_id=1, source_target_pairs={{0,4},{1,5},{2,6},{3,7},{4,0},{5,1},{6,2},{7,3},{8,12},{9,13},{10,... | collective-permute-start | bytes 589832 | tf_op jit(solution)/shard_map/ppermute | solution.py:360
  12.1 28.3 %collective-permute-start.6 = (bf16[3,4,64,128]{3,2,1,0:T(8,128)(2,1)}, bf16[3,4,64,128]{3,2,1,0:T(8,128)(2,1)S(1)}, u32[]{:S(2)}, u32[]{:S(2)}) collective-permute-start(bf16[3,4,64,128]{3,2,1,0:T(8,128)(2,1)} %get-tuple-element.36), channel_id=1, source_target_pairs={{0,5},{1,4},{2,7},{3,6},{4,1},{5,0},{6,3},{7,2},{8,13},{9,12},{10,... | collective-permute-start | bytes 589832 | tf_op jit(solution)/shard_map/ppermute | solution.py:360
  13.3 27.1 %collective-permute-start.7 = (bf16[3,4,64,128]{3,2,1,0:T(8,128)(2,1)}, bf16[3,4,64,128]{3,2,1,0:T(8,128)(2,1)S(1)}, u32[]{:S(2)}, u32[]{:S(2)}) collective-permute-start(bf16[3,4,64,128]{3,2,1,0:T(8,128)(2,1)} %get-tuple-element.37), channel_id=1, source_target_pairs={{0,6},{1,7},{2,4},{3,5},{4,2},{5,3},{6,0},{7,1},{8,14},{9,15},{10,... | collective-permute-start | bytes 589832 | tf_op jit(solution)/shard_map/ppermute | solution.py:360
  23.2 17.2 %collective-permute-start.8 = (bf16[3,4,64,128]{3,2,1,0:T(8,128)(2,1)}, bf16[3,4,64,128]{3,2,1,0:T(8,128)(2,1)S(1)}, u32[]{:S(2)}, u32[]{:S(2)}) collective-permute-start(bf16[3,4,64,128]{3,2,1,0:T(8,128)(2,1)} %get-tuple-element.38), channel_id=1, source_target_pairs={{0,7},{1,6},{2,5},{3,4},{4,3},{5,2},{6,1},{7,0},{8,15},{9,14},{10,... | collective-permute-start | bytes 589832 | tf_op jit(solution)/shard_map/ppermute | solution.py:360
  24.9 27.0 %collective-permute-start = (bf16[2,256,128]{2,1,0:T(8,128)(2,1)}, bf16[2,256,128]{2,1,0:T(8,128)(2,1)S(1)}, u32[]{:S(2)}, u32[]{:S(2)}) collective-permute-start(bf16[2,256,128]{2,1,0:T(8,128)(2,1)} %get-tuple-element.30), channel_id=1, source_target_pairs={{0,1},{1,0},{2,3},{3,2},{4,5},{5,4},{6,7},{7,6},{8,9},{9,8},{10,11... | collective-permute-start | bytes 393224 | tf_op jit(solution)/shard_map/ppermute | solution.py:360
  27.4 29.3 %collective-permute-start.1 = (bf16[2,256,128]{2,1,0:T(8,128)(2,1)}, bf16[2,256,128]{2,1,0:T(8,128)(2,1)S(1)}, u32[]{:S(2)}, u32[]{:S(2)}) collective-permute-start(bf16[2,256,128]{2,1,0:T(8,128)(2,1)} %get-tuple-element.31), channel_id=1, source_target_pairs={{1,2},{3,4},{5,6},{2,1},{4,3},{6,5},{9,10},{11,12},{13,14},{10,9},... | collective-permute-start | bytes 393224 | tf_op jit(solution)/shard_map/ppermute | solution.py:435
  28.2 33.3 %copy-start = (bf16[2,4,256,128]{3,2,1,0:T(8,128)(2,1)S(1)}, bf16[2,4,256,128]{3,2,1,0:T(8,128)(2,1)}, u32[]{:S(2)}) copy-start(bf16[2,4,256,128]{3,2,1,0:T(8,128)(2,1)} %cot_ref.3) | copy-start | bytes 1572868
  42.5 23.6 %copy-start.5 = (f32[2048]{0:T(1024)S(1)}, f32[2048]{0:T(1024)}, u32[]{:S(2)}) copy-start(f32[2048]{0:T(1024)} %param.11) | copy-start | bytes 24580
  42.5 14.2 %collective-permute-start.9 = (bf16[4,64,128]{2,1,0:T(8,128)(2,1)S(1)}, bf16[4,64,128]{2,1,0:T(8,128)(2,1)S(1)}, u32[]{:S(2)}, u32[]{:S(2)}) collective-permute-start(bf16[4,64,128]{2,1,0:T(8,128)(2,1)S(1)} %get-tuple-element.40), channel_id=1, source_target_pairs={{0,1},{1,0},{2,3},{3,2},{4,5},{5,4},{6,7},{7,6},{8,9},{9,8},{10,11... | collective-permute-start | bytes 196616 | tf_op jit(solution)/shard_map/ppermute | solution.py:360
  42.6 16.4 %collective-permute-start.10 = (bf16[4,64,128]{2,1,0:T(8,128)(2,1)S(1)}, bf16[4,64,128]{2,1,0:T(8,128)(2,1)S(1)}, u32[]{:S(2)}, u32[]{:S(2)}) collective-permute-start(bf16[4,64,128]{2,1,0:T(8,128)(2,1)S(1)} %get-tuple-element.41), channel_id=1, source_target_pairs={{0,2},{1,3},{2,0},{3,1},{4,6},{5,7},{6,4},{7,5},{8,10},{9,11},{10,... | collective-permute-start | bytes 196616 | tf_op jit(solution)/shard_map/ppermute | solution.py:360
  51.9 9.8 %collective-permute-start.11 = (bf16[4,64,128]{2,1,0:T(8,128)(2,1)S(1)}, bf16[4,64,128]{2,1,0:T(8,128)(2,1)S(1)}, u32[]{:S(2)}, u32[]{:S(2)}) collective-permute-start(bf16[4,64,128]{2,1,0:T(8,128)(2,1)S(1)} %get-tuple-element.42), channel_id=1, source_target_pairs={{0,3},{1,2},{2,1},{3,0},{4,7},{5,6},{6,5},{7,4},{8,11},{9,10},{10,... | collective-permute-start | bytes 196616 | tf_op jit(solution)/shard_map/ppermute | solution.py:360
  51.9 9.8 %collective-permute-start.12 = (bf16[4,64,128]{2,1,0:T(8,128)(2,1)S(1)}, bf16[4,64,128]{2,1,0:T(8,128)(2,1)S(1)}, u32[]{:S(2)}, u32[]{:S(2)}) collective-permute-start(bf16[4,64,128]{2,1,0:T(8,128)(2,1)S(1)} %get-tuple-element.43), channel_id=1, source_target_pairs={{0,4},{1,5},{2,6},{3,7},{4,0},{5,1},{6,2},{7,3},{8,12},{9,13},{10,... | collective-permute-start | bytes 196616 | tf_op jit(solution)/shard_map/ppermute | solution.py:360
  56.7 7.4 %collective-permute-start.13 = (bf16[4,64,128]{2,1,0:T(8,128)(2,1)S(1)}, bf16[4,64,128]{2,1,0:T(8,128)(2,1)S(1)}, u32[]{:S(2)}, u32[]{:S(2)}) collective-permute-start(bf16[4,64,128]{2,1,0:T(8,128)(2,1)S(1)} %get-tuple-element.44), channel_id=1, source_target_pairs={{0,5},{1,4},{2,7},{3,6},{4,1},{5,0},{6,3},{7,2},{8,13},{9,12},{10,... | collective-permute-start | bytes 196616 | tf_op jit(solution)/shard_map/ppermute | solution.py:360
  56.7 7.4 %collective-permute-start.14 = (bf16[4,64,128]{2,1,0:T(8,128)(2,1)S(1)}, bf16[4,64,128]{2,1,0:T(8,128)(2,1)S(1)}, u32[]{:S(2)}, u32[]{:S(2)}) collective-permute-start(bf16[4,64,128]{2,1,0:T(8,128)(2,1)S(1)} %get-tuple-element.45), channel_id=1, source_target_pairs={{0,6},{1,7},{2,4},{3,5},{4,2},{5,3},{6,0},{7,1},{8,14},{9,15},{10,... | collective-permute-start | bytes 196616 | tf_op jit(solution)/shard_map/ppermute | solution.py:360
  59.0 7.1 %collective-permute-start.15 = (bf16[4,64,128]{2,1,0:T(8,128)(2,1)S(1)}, bf16[4,64,128]{2,1,0:T(8,128)(2,1)S(1)}, u32[]{:S(2)}, u32[]{:S(2)}) collective-permute-start(bf16[4,64,128]{2,1,0:T(8,128)(2,1)S(1)} %get-tuple-element.46), channel_id=1, source_target_pairs={{0,7},{1,6},{2,5},{3,4},{4,3},{5,2},{6,1},{7,0},{8,15},{9,14},{10,... | collective-permute-start | bytes 196616 | tf_op jit(solution)/shard_map/ppermute | solution.py:360
  61.7 22.8 %copy-start.4 = (bf16[9,128,128]{2,1,0:T(8,128)(2,1)S(1)}, bf16[9,128,128]{2,1,0:T(8,128)(2,1)}, u32[]{:S(2)}) copy-start(bf16[9,128,128]{2,1,0:T(8,128)(2,1)} %param.12) | copy-start | bytes 884740
  69.2 2.4 %collective-permute-start.18 = (f32[576,128]{1,0:T(8,128)S(1)}, f32[576,128]{1,0:T(8,128)S(1)}, u32[]{:S(2)}, u32[]{:S(2)}) collective-permute-start(f32[576,128]{1,0:T(8,128)S(1)} %get-tuple-element.52), channel_id=1, source_target_pairs={{0,8},{8,0},{16,24},{24,16},{1,9},{9,1},{17,25},{25,17},{2,10},{10... | collective-permute-start | bytes 884744 | tf_op jit(solution)/shard_map/ppermute | solution.py:382
  69.3 15.3 %collective-permute-start.16 = (bf16[2,256,128]{2,1,0:T(8,128)(2,1)S(1)}, bf16[2,256,128]{2,1,0:T(8,128)(2,1)S(1)}, u32[]{:S(2)}, u32[]{:S(2)}) collective-permute-start(bf16[2,256,128]{2,1,0:T(8,128)(2,1)S(1)} %get-tuple-element.48), channel_id=1, source_target_pairs={{0,1},{1,0},{2,3},{3,2},{4,5},{5,4},{6,7},{7,6},{8,9},{9,8},{10,11... | collective-permute-start | bytes 393224 | tf_op jit(solution)/shard_map/ppermute | solution.py:360
  70.7 13.9 %collective-permute-start.17 = (bf16[2,256,128]{2,1,0:T(8,128)(2,1)S(1)}, bf16[2,256,128]{2,1,0:T(8,128)(2,1)S(1)}, u32[]{:S(2)}, u32[]{:S(2)}) collective-permute-start(bf16[2,256,128]{2,1,0:T(8,128)(2,1)S(1)} %get-tuple-element.49), channel_id=1, source_target_pairs={{1,2},{3,4},{5,6},{2,1},{4,3},{6,5},{9,10},{11,12},{13,14},{10,9},... | collective-permute-start | bytes 393224 | tf_op jit(solution)/shard_map/ppermute | solution.py:497
  71.6 6.3 %collective-permute-start.19 = (bf16[144,128]{1,0:T(8,128)(2,1)S(1)}, bf16[144,128]{1,0:T(8,128)(2,1)S(1)}, u32[]{:S(2)}, u32[]{:S(2)}) collective-permute-start(bf16[144,128]{1,0:T(8,128)(2,1)S(1)} %get-tuple-element.54), channel_id=1, source_target_pairs={{0,1},{1,0},{2,3},{3,2},{4,5},{5,4},{6,7},{7,6},{8,9},{9,8},{10,11... | collective-permute-start | bytes 110600 | tf_op jit(solution)/shard_map/ppermute | solution.py:378
  73.7 4.1 %collective-permute-start.20 = (bf16[144,128]{1,0:T(8,128)(2,1)S(1)}, bf16[144,128]{1,0:T(8,128)(2,1)S(1)}, u32[]{:S(2)}, u32[]{:S(2)}) collective-permute-start(bf16[144,128]{1,0:T(8,128)(2,1)S(1)} %get-tuple-element.55), channel_id=1, source_target_pairs={{0,16},{1,17},{2,18},{3,19},{4,20},{5,21},{6,22},{7,23},{8,24},{9,... | collective-permute-start | bytes 110600 | tf_op jit(solution)/shard_map/ppermute | solution.py:378
  75.2 4.9 %collective-permute-start.21 = (bf16[144,128]{1,0:T(8,128)(2,1)S(1)}, bf16[144,128]{1,0:T(8,128)(2,1)S(1)}, u32[]{:S(2)}, u32[]{:S(2)}) collective-permute-start(bf16[144,128]{1,0:T(8,128)(2,1)S(1)} %get-tuple-element.56), channel_id=1, source_target_pairs={{0,17},{1,16},{2,19},{3,18},{4,21},{5,20},{6,23},{7,22},{8,25},{9,... | collective-permute-start | bytes 110600 | tf_op jit(solution)/shard_map/ppermute | solution.py:378
  80.1 6.7 %collective-permute-start.24 = (bf16[144,128]{1,0:T(8,128)(2,1)S(1)}, bf16[144,128]{1,0:T(8,128)(2,1)S(1)}, u32[]{:S(2)}, u32[]{:S(2)}) collective-permute-start(bf16[144,128]{1,0:T(8,128)(2,1)S(1)} %sum_chips.1.refs_0_), channel_id=1, source_target_pairs={{0,6},{1,7},{2,4},{3,5},{4,2},{5,3},{6,0},{7,1},{8,14},{9,15},{10,... | collective-permute-start | bytes 110600 | tf_op jit(solution)/shard_map/ppermute | solution.py:360
  82.9 5.0 %collective-permute-start.23 = (bf16[144,128]{1,0:T(8,128)(2,1)S(1)}, bf16[144,128]{1,0:T(8,128)(2,1)S(1)}, u32[]{:S(2)}, u32[]{:S(2)}) collective-permute-start(bf16[144,128]{1,0:T(8,128)(2,1)S(1)} %sum_chips.1.refs_0_), channel_id=1, source_target_pairs={{0,4},{1,5},{2,6},{3,7},{4,0},{5,1},{6,2},{7,3},{8,12},{9,13},{10,... | collective-permute-start | bytes 110600 | tf_op jit(solution)/shard_map/ppermute | solution.py:360
  83.4 4.5 %collective-permute-start.22 = (bf16[144,128]{1,0:T(8,128)(2,1)S(1)}, bf16[144,128]{1,0:T(8,128)(2,1)S(1)}, u32[]{:S(2)}, u32[]{:S(2)}) collective-permute-start(bf16[144,128]{1,0:T(8,128)(2,1)S(1)} %sum_chips.1.refs_0_), channel_id=1, source_target_pairs={{0,2},{1,3},{2,0},{3,1},{4,6},{5,7},{6,4},{7,5},{8,10},{9,11},{10,... | collective-permute-start | bytes 110600 | tf_op jit(solution)/shard_map/ppermute | solution.py:360
  88.0 4.9 %collective-permute-start.27 = (bf16[144,128]{1,0:T(8,128)(2,1)S(1)}, bf16[144,128]{1,0:T(8,128)(2,1)S(1)}, u32[]{:S(2)}, u32[]{:S(2)}) collective-permute-start(bf16[144,128]{1,0:T(8,128)(2,1)S(1)} %sum_planes.1.refs_0_), channel_id=1, source_target_pairs={{0,17},{1,16},{2,19},{3,18},{4,21},{5,20},{6,23},{7,22},{8,25},{9,... | collective-permute-start | bytes 110600 | tf_op jit(solution)/shard_map/ppermute | solution.py:378
  89.3 4.0 %collective-permute-start.26 = (bf16[144,128]{1,0:T(8,128)(2,1)S(1)}, bf16[144,128]{1,0:T(8,128)(2,1)S(1)}, u32[]{:S(2)}, u32[]{:S(2)}) collective-permute-start(bf16[144,128]{1,0:T(8,128)(2,1)S(1)} %sum_planes.1.refs_0_), channel_id=1, source_target_pairs={{0,16},{1,17},{2,18},{3,19},{4,20},{5,21},{6,22},{7,23},{8,24},{9,... | collective-permute-start | bytes 110600 | tf_op jit(solution)/shard_map/ppermute | solution.py:378
  90.5 4.0 %collective-permute-start.25 = (bf16[144,128]{1,0:T(8,128)(2,1)S(1)}, bf16[144,128]{1,0:T(8,128)(2,1)S(1)}, u32[]{:S(2)}, u32[]{:S(2)}) collective-permute-start(bf16[144,128]{1,0:T(8,128)(2,1)S(1)} %sum_planes.1.refs_0_), channel_id=1, source_target_pairs={{0,1},{1,0},{2,3},{3,2},{4,5},{5,4},{6,7},{7,6},{8,9},{9,8},{10,11... | collective-permute-start | bytes 110600 | tf_op jit(solution)/shard_map/ppermute | solution.py:378
  94.5 1.4 %collective-permute-start.28 = (bf16[576,128]{1,0:T(8,128)(2,1)S(1)}, bf16[576,128]{1,0:T(8,128)(2,1)S(1)}, u32[]{:S(2)}, u32[]{:S(2)}) collective-permute-start(bf16[576,128]{1,0:T(8,128)(2,1)S(1)} %join_chips.1.own_ref), channel_id=1, source_target_pairs={{0,8},{8,0},{16,24},{24,16},{1,9},{9,1},{17,25},{25,17},{2,10},{10... | collective-permute-start | bytes 442376 | tf_op jit(solution)/shard_map/ppermute | solution.py:382

commit v12 on v11

--- a/solution.py
+++ b/solution.py
@@ -34,93 +34,67 @@
     )
 
 
-def unpack_items(held, which, regions, per_device, owner):
-    width = held.shape[3] // HEADS
-    aligned = per_device % regions == 0
-    items = []
-    for place in range(per_device):
-        if aligned and place % regions:
-            region = place % regions
+def columns_of(index, distance, regions, per_device, width):
+    owner = lax.bitwise_xor(index, distance)
+    span = max(1, per_device // regions) * width
+    start = lax.div(owner * per_device, regions) * width
+    return owner, pl.ds(pl.multiple_of(start, width), span)
+
+
+def take_items(held, owner, regions, per_device, width, out_ref):
+    for head in range(held.shape[2] // width):
+        block = held[:, :, head * width : (head + 1) * width].astype(jnp.float32)
+        if per_device % regions:
+            value = block[:, 0, :]
+            for other in range(1, regions):
+                value = jnp.where(lax.rem(owner, regions) == other, block[:, other, :], value)
+            out_ref[head] = value.astype(jnp.bfloat16)
         else:
-            item = owner * per_device + place
-            head = lax.div(item, regions)
-            region = 0 if aligned else lax.rem(item, regions)
-            start = pl.multiple_of(head * width, width)
-            block = held[which, :, :, pl.ds(start, width)].astype(jnp.float32)
-        value = block[:, 0, :]
-        for other in range(1, regions):
-            if aligned:
-                value = block[:, other, :] if region == other else value
-            else:
-                value = jnp.where(region == other, block[:, other, :], value)
-        items.append(value.astype(jnp.bfloat16))
-    return items
-
-
-def pack_kernel(
-    regions, per_device, index_ref, query_ref, key_ref, value_ref, cot_ref, *refs
-):
-    held, ready, edges, sems = refs[-4:]
-    edge_refs = refs[-6:-4]
-    out_refs = refs[:-6]
-    rows = cot_ref.shape[1]
-    loads = [
-        pltpu.make_async_copy(ref, held.at[which], sems.at[which])
-        for which, ref in enumerate((query_ref, key_ref, value_ref))
-    ]
-    odd = lax.rem(index_ref[0], 2)
-    for edge, row in enumerate(((1 - odd) * (rows - 1), odd * (rows - 1))):
-        loads.append(pltpu.make_async_copy(cot_ref.at[:, row], edges.at[edge], sems.at[3 + edge]))
-    for load in loads:
-        load.start()
+            for region in range(regions):
+                out_ref[head * regions + region] = block[:, region, :].astype(jnp.bfloat16)
+
+
+def pack_kernel(distances, regions, per_device, index_ref, query_ref, key_ref, value_ref, *refs):
+    refs = refs[-len(distances) - 4 :]
+    held, ready, load_sems, store_sems = refs[-4:]
+    width = query_ref.shape[2] // HEADS
+    loads = []
+    for number, distance in enumerate(distances):
+        owner, columns = columns_of(index_ref[0], distance, regions, per_device, width)
+        for which, ref in enumerate((query_ref, key_ref, value_ref)):
+            load = pltpu.make_async_copy(
+                ref.at[:, :, columns], held.at[number, which], load_sems.at[3 * number + which]
+            )
+            load.start()
+            loads.append((number, which, owner, load))
     stores = []
-    for which in range(3):
-        loads[which].wait()
-        for number, ref in enumerate(out_refs):
-            owner = lax.bitwise_xor(index_ref[0], number + 1)
-            for place, value in enumerate(unpack_items(held, which, regions, per_device, owner)):
-                ready[number, which, place] = value
-            stores.append(
-                pltpu.make_async_copy(
-                    ready.at[number, which], ref.at[which], sems.at[7 + 3 * number + which]
-                )
-            )
-            stores[-1].start()
-        if which == 0:
-            for edge, ref in enumerate(edge_refs):
-                loads[3 + edge].wait()
-                stores.append(pltpu.make_async_copy(edges.at[edge], ref, sems.at[5 + edge]))
-                stores[-1].start()
+    for number, which, owner, load in loads:
+        load.wait()
+        take_items(
+            held.at[number, which], owner, regions, per_device, width, ready.at[number, which]
+        )
+        if which == 2:
+            store = pltpu.make_async_copy(ready.at[number], refs[number], store_sems.at[number])
+            store.start()
+            stores.append(store)
     for store in stores:
         store.wait()
 
 
-def own_kernel(regions, per_device, index_ref, query_ref, key_ref, value_ref, out_ref, held, sems):
-    tokens, width = out_ref.shape[2:]
-    span = max(1, per_device // regions) * width
-    index = index_ref[0]
-    start = lax.div(index * per_device, regions) * width
+def own_kernel(
+    regions, per_device, index_ref, query_ref, key_ref, value_ref, out_ref, held, sems
+):
+    width = out_ref.shape[3]
+    owner, columns = columns_of(index_ref[0], 0, regions, per_device, width)
     loads = []
     for which, ref in enumerate((query_ref, key_ref, value_ref)):
-        columns = pl.ds(pl.multiple_of(start, width), span)
         loads.append(
             pltpu.make_async_copy(ref.at[:, :, columns], held.at[which], sems.at[which])
         )
         loads[-1].start()
     for which, load in enumerate(loads):
         load.wait()
-        for head in range(span // width):
-            block = held[which, :, :, head * width : (head + 1) * width].astype(jnp.float32)
-            if per_device % regions:
-                value = block[:, 0, :]
-                for other in range(1, regions):
-                    value = jnp.where(lax.rem(index, regions) == other, block[:, other, :], value)
-                out_ref[which, head] = value.astype(jnp.bfloat16)
-            else:
-                for region in range(regions):
-                    out_ref[which, head * regions + region] = block[:, region, :].astype(
-                        jnp.bfloat16
-                    )
+        take_items(held.at[which], owner, regions, per_device, width, out_ref.at[which])
 
 
 def attend_kernel(block_rows, group, order, index_ref, lengths_ref, *refs):
@@ -403,36 +377,50 @@
     edge_shape = jax.ShapeDtypeStruct((regions, columns, width), jnp.bfloat16)
     chunk_shape = jax.ShapeDtypeStruct((3, per_device, tokens, width), jnp.bfloat16)
     index = seq_index.reshape(1)
-    *leaving, cot_near, cot_far = call(
-        functools.partial(pack_kernel, regions, per_device),
-        "pack",
-        [chunk_shape] * (seq_count - 1) + [edge_shape] * 2,
-        [SMEM()] + [HBM()] * 4,
-        out_specs=[HBM()] * (seq_count + 1),
-        scratch=[
-            pltpu.VMEM((3,) + query_rows.shape, jnp.bfloat16),
-            pltpu.VMEM((seq_count - 1,) + chunk_shape.shape, jnp.bfloat16),
-            pltpu.VMEM((2,) + edge_shape.shape, jnp.bfloat16),
-            pltpu.SemaphoreType.DMA((7 + 3 * (seq_count - 1),)),
-        ],
-        moved=6 * local_bytes,
-        grant=VMEM_WHOLE,
-    )(index, query_rows, key_rows, value_rows, cotangent)
+    odd = lax.bitwise_and(seq_index, 1) == 1
+    cot_far = jnp.where(odd, cotangent[:, PATCH - 1], cotangent[:, 0])
+    cot_far = lax.ppermute(cot_far, "seq", far_pairs)
+    half = seq_count // 2
+    early = [2, half, half + 1]
+    late = [distance for distance in range(1, seq_count) if distance not in early]
+    span = max(1, per_device // regions) * width
+
+    def pack(name, distances, *after):
+        return call(
+            functools.partial(pack_kernel, distances, regions, per_device),
+            name,
+            [chunk_shape] * len(distances),
+            [SMEM()] + [HBM()] * 3 + [ANY()] * len(after),
+            out_specs=[HBM()] * len(distances),
+            scratch=[
+                pltpu.VMEM((len(distances), 3, tokens, regions, span), jnp.bfloat16),
+                pltpu.VMEM((len(distances),) + chunk_shape.shape, jnp.bfloat16),
+                pltpu.SemaphoreType.DMA((3 * len(distances),)),
+                pltpu.SemaphoreType.DMA((len(distances),)),
+            ],
+            moved=4 * len(distances) * chunk_shape.size,
+            grant=VMEM_WHOLE,
+        )(index, query_rows, key_rows, value_rows, *after)
+
+    packed = {}
+    for distance, chunk in zip(early, pack("pack_early", early)):
+        packed[distance] = trade(chunk, distance)
+    for distance, chunk in zip(late, pack("pack_late", late, cot_far)):
+        packed[distance] = trade(chunk, distance)
     order = list(range(1, seq_count)) + [0]
-    packed = [trade(chunk, distance) for distance, chunk in zip(order, leaving)]
-    own = call(
+    packed[0] = call(
         functools.partial(own_kernel, regions, per_device),
         "own_chunk",
         chunk_shape,
         [SMEM()] + [HBM()] * 3,
         scratch=[
-            pltpu.VMEM((3, tokens, regions, max(1, per_device // regions) * width), jnp.bfloat16),
+            pltpu.VMEM((3, tokens, regions, span), jnp.bfloat16),
             pltpu.SemaphoreType.DMA((3,)),
         ],
         moved=12 * chunk_shape.size,
     )(index, query_rows, key_rows, value_rows)
+    cot_near = jnp.where(odd, cotangent[:, 0], cotangent[:, PATCH - 1])
     cot_near = trade(cot_near, 1)
-    cot_far = lax.ppermute(cot_far, "seq", far_pairs)
 
     items = seq_index * per_device + jnp.arange(per_device, dtype=jnp.int32)
     item_lengths = jnp.sum(
@@ -453,7 +441,7 @@
         flops=4 * per_device * capacity * capacity * width,
         moved=4 * local_bytes,
         exps=per_device * capacity * capacity,
-    )(index, item_lengths, *packed, own)
+    )(index, item_lengths, *[packed[distance] for distance in order])
     attended = [mixed[0]] + [trade(mixed[distance], distance) for distance in order[:-1]]
 
     turned = call(

time: 97.3 us -> 96.3 us (0.990)
  waiting for transfers between devices: 33.6 us -> 20.3 us
  starting transfers between devices: 49.4 us -> 59.4 us
  Pallas kernels: 12.8 us -> 14.7 us
    ppermute x19, waiting for transfers between devices: 24.4 us -> 11 us  [trade(): return lax.ppermute(values, 'seq', pairs)]
    ppermute x19, starting transfers between devices: 40.6 us -> 48.5 us  [trade(): return lax.ppermute(values, 'seq', pairs)]
    ppermute x6, starting transfers between devices: 7.2 us -> 9.24 us  [trade_chips(): return lax.ppermute(values, ('dp', 'seq'), pairs)]
    pallas_call x1 -> x2, Pallas kernels: 3.81 us -> 5.3 us  [pack(): call(functools.partial(pack_kernel, distances, regions, per_device), name...]
  transfers between devices with their start and end apart: 29 -> 29, of which waited for: 12 -> 13; matrix products, arithmetic and copies ran while one was open for 0% -> 0% of each run, Pallas kernels for 5% -> 8%
where the time goes in v12:
time: 96.3 us; the launch traced here: 96 us
  starting transfers between devices  59.4 us (62%)
  waiting for transfers between devices  20.3 us (21%)
  Pallas kernels  14.7 us (15%)
    ppermute x19, starting transfers between devices, trade(): return lax.ppermute(values, 'seq', pairs)  48.5 us
    ppermute x19, waiting for transfers between devices, trade(): return lax.ppermute(values, 'seq', pairs)  11 us
    ppermute x6, starting transfers between devices, trade_chips(): return lax.ppermute(values, ('dp', 'seq'), pairs)  9.24 us
    ppermute x6, waiting for transfers between devices, trade_chips(): return lax.ppermute(values, ('dp', 'seq'), pairs)  7.92 us
    pallas_call x2, Pallas kernels, pack(): call(functools.partial(pack_kernel, distances, regions, per_device), name...  5.3 us
    pallas_call x1, Pallas kernels, body(): call(norm_kernel, 'norm_and_gradient', [jax.ShapeDtypeStruct((regions, PA...  3.06 us
    pallas_call x1, Pallas kernels, body(): call(functools.partial(attend_kernel, block_rows, group, order), 'attend'...  2.49 us
    pallas_call x1, Pallas kernels, body(): call(decode_kernel, 'decode', [jax.ShapeDtypeStruct(cotangent.shape, jnp....  2.21 us
  transfers between devices with their start and end apart: 29, of which 13 were waited for; matrix products, arithmetic and copies ran while one was open for 0% of the time, Pallas kernels for 8%

profile of v12, /device:TPU:0, one launch (start us, length us, event | category | flops | bytes accessed | tf_op | source)
XLA Modules:
  0.0 96.0 jit_solution(10650454783833328837)
XLA Ops:
  0.7 0.0 copy-start
  0.7 0.0 copy-start.1
  0.7 0.0 copy-start.2
  0.7 2.6 %pack_early.1 = (bf16[3,4,64,128]{3,2,1,0:T(8,128)(2,1)}, bf16[3,4,64,128]{3,2,1,0:T(8,128)(2,1)}, bf16[3,4,64,128]{3,2,1,0:T(8,128)(2,1)}) custom-call(s32[1]{0:T(128)} %bitcast.index_ref, bf16[64,2,2048]{2,1,0:T(2,128)(2,1)} %query_ref.5, bf16[64,2,2048]{2,1,0:T(2,128)(2,1)} %key_ref.5, bf16[64,2,2048]{2,1,0:T(2,128)(2,1)} %value_ref.5), custom_call_target="tpu_custom_call" | custom-call | bytes 1179648 | tf_op jit(solution)/shard_map/pack_early/pallas_call | solution.py:389
  3.3 3.1 %collective-permute-start.3 = (bf16[3,4,64,128]{3,2,1,0:T(8,128)(2,1)}, bf16[3,4,64,128]{3,2,1,0:T(8,128)(2,1)S(1)}, u32[]{:S(2)}, u32[]{:S(2)}) collective-permute-start(bf16[3,4,64,128]{3,2,1,0:T(8,128)(2,1)} %get-tuple-element.29), channel_id=1, source_target_pairs={{0,2},{1,3},{2,0},{3,1},{4,6},{5,7},{6,4},{7,5},{8,10},{9,11},{10,... | collective-permute-start | bytes 589832 | tf_op jit(solution)/shard_map/ppermute | solution.py:334
  6.4 2.6 %collective-permute-start.5 = (bf16[3,4,64,128]{3,2,1,0:T(8,128)(2,1)}, bf16[3,4,64,128]{3,2,1,0:T(8,128)(2,1)S(1)}, u32[]{:S(2)}, u32[]{:S(2)}) collective-permute-start(bf16[3,4,64,128]{3,2,1,0:T(8,128)(2,1)} %get-tuple-element.31), channel_id=1, source_target_pairs={{0,4},{1,5},{2,6},{3,7},{4,0},{5,1},{6,2},{7,3},{8,12},{9,13},{10,... | collective-permute-start | bytes 589832 | tf_op jit(solution)/shard_map/ppermute | solution.py:334
  9.0 0.7 collective-permute-start.1
  9.7 2.7 %collective-permute-start.6 = (bf16[3,4,64,128]{3,2,1,0:T(8,128)(2,1)}, bf16[3,4,64,128]{3,2,1,0:T(8,128)(2,1)S(1)}, u32[]{:S(2)}, u32[]{:S(2)}) collective-permute-start(bf16[3,4,64,128]{3,2,1,0:T(8,128)(2,1)} %get-tuple-element.32), channel_id=1, source_target_pairs={{0,5},{1,4},{2,7},{3,6},{4,1},{5,0},{6,3},{7,2},{8,13},{9,12},{10,... | collective-permute-start | bytes 589832 | tf_op jit(solution)/shard_map/ppermute | solution.py:334
  12.3 0.7 copy-done.4
  13.0 2.7 %pack_late.1 = (bf16[3,4,64,128]{3,2,1,0:T(8,128)(2,1)}, bf16[3,4,64,128]{3,2,1,0:T(8,128)(2,1)}, bf16[3,4,64,128]{3,2,1,0:T(8,128)(2,1)}, bf16[3,4,64,128]{3,2,1,0:T(8,128)(2,1)}) custom-call(s32[1]{0:T(128)} %bitcast.index_ref, bf16[64,2,2048]{2,1,0:T(2,128)(2,1)} %query_ref.5, bf16[64,2,2048]{2,1,0:T(2,128)(2,1)} %key_ref.5, ...), custom_call_target="tpu_custom_call" | custom-call | bytes 1572864 | tf_op jit(solution)/shard_map/pack_late/pallas_call | solution.py:389
  15.7 8.2 %collective-permute-start.2 = (bf16[3,4,64,128]{3,2,1,0:T(8,128)(2,1)}, bf16[3,4,64,128]{3,2,1,0:T(8,128)(2,1)S(1)}, u32[]{:S(2)}, u32[]{:S(2)}) collective-permute-start(bf16[3,4,64,128]{3,2,1,0:T(8,128)(2,1)} %get-tuple-element.28), channel_id=1, source_target_pairs={{0,1},{1,0},{2,3},{3,2},{4,5},{5,4},{6,7},{7,6},{8,9},{9,8},{10,11... | collective-permute-start | bytes 589832 | tf_op jit(solution)/shard_map/ppermute | solution.py:334
  23.9 7.0 %collective-permute-start.4 = (bf16[3,4,64,128]{3,2,1,0:T(8,128)(2,1)}, bf16[3,4,64,128]{3,2,1,0:T(8,128)(2,1)S(1)}, u32[]{:S(2)}, u32[]{:S(2)}) collective-permute-start(bf16[3,4,64,128]{3,2,1,0:T(8,128)(2,1)} %get-tuple-element.30), channel_id=1, source_target_pairs={{0,3},{1,2},{2,1},{3,0},{4,7},{5,6},{6,5},{7,4},{8,11},{9,10},{10,... | collective-permute-start | bytes 589832 | tf_op jit(solution)/shard_map/ppermute | solution.py:334
  30.9 4.5 %collective-permute-start.7 = (bf16[3,4,64,128]{3,2,1,0:T(8,128)(2,1)}, bf16[3,4,64,128]{3,2,1,0:T(8,128)(2,1)S(1)}, u32[]{:S(2)}, u32[]{:S(2)}) collective-permute-start(bf16[3,4,64,128]{3,2,1,0:T(8,128)(2,1)} %get-tuple-element.33), channel_id=1, source_target_pairs={{0,6},{1,7},{2,4},{3,5},{4,2},{5,3},{6,0},{7,1},{8,14},{9,15},{10,... | collective-permute-start | bytes 589832 | tf_op jit(solution)/shard_map/ppermute | solution.py:334
  35.4 0.0 collective-permute-done.5.refs_3_
  35.4 0.7 collective-permute-start.8
  36.1 0.0 collective-permute-done.6.refs_4_
  36.1 0.9 collective-permute-start
  37.0 0.1 fusion.2.lengths_ref
  37.2 0.4 own_chunk.1.refs_7_
  37.6 1.0 %collective-permute-done.2.refs_0_ = bf16[3,4,64,128]{3,2,1,0:T(8,128)(2,1)S(1)} collective-permute-done((bf16[3,4,64,128]{3,2,1,0:T(8,128)(2,1)}, bf16[3,4,64,128]{3,2,1,0:T(8,128)(2,1)S(1)}, u32[]{:S(2)}, u32[]{:S(2)}) %collective-permute-start.2) | collective-permute-done | bytes 196640 | tf_op jit(solution)/shard_map/ppermute | solution.py:334
  38.6 0.0 collective-permute-done.4.refs_2_
  38.6 3.2 %collective-permute-done.7.refs_5_ = bf16[3,4,64,128]{3,2,1,0:T(8,128)(2,1)S(1)} collective-permute-done((bf16[3,4,64,128]{3,2,1,0:T(8,128)(2,1)}, bf16[3,4,64,128]{3,2,1,0:T(8,128)(2,1)S(1)}, u32[]{:S(2)}, u32[]{:S(2)}) %collective-permute-start.7) | collective-permute-done | bytes 196640 | tf_op jit(solution)/shard_map/ppermute | solution.py:334
  41.8 2.3 %collective-permute-done.8.refs_6_ = bf16[3,4,64,128]{3,2,1,0:T(8,128)(2,1)S(1)} collective-permute-done((bf16[3,4,64,128]{3,2,1,0:T(8,128)(2,1)}, bf16[3,4,64,128]{3,2,1,0:T(8,128)(2,1)S(1)}, u32[]{:S(2)}, u32[]{:S(2)}) %collective-permute-start.8) | collective-permute-done | bytes 196640 | tf_op jit(solution)/shard_map/ppermute | solution.py:334
  44.1 2.5 %attend.1 = (bf16[4,64,128]{2,1,0:T(8,128)(2,1)S(1)}, bf16[4,64,128]{2,1,0:T(8,128)(2,1)S(1)}, bf16[4,64,128]{2,1,0:T(8,128)(2,1)S(1)}, bf16[4,64,128]{2,1,0:T(8...) custom-call(s32[1]{0:T(128)} %bitcast.index_ref, ...), custom_call_target="tpu_custom_call" | custom-call | flops 536870912 | bytes 2097152 | tf_op jit(solution)/shard_map/attend/pallas_call | solution.py:436
  46.6 0.0 copy-start.7
  46.6 1.4 %collective-permute-start.9 = (bf16[4,64,128]{2,1,0:T(8,128)(2,1)S(1)}, bf16[4,64,128]{2,1,0:T(8,128)(2,1)S(1)}, u32[]{:S(2)}, u32[]{:S(2)}) collective-permute-start(bf16[4,64,128]{2,1,0:T(8,128)(2,1)S(1)} %get-tuple-element.36), channel_id=1, source_target_pairs={{0,1},{1,0},{2,3},{3,2},{4,5},{5,4},{6,7},{7,6},{8,9},{9,8},{10,11... | collective-permute-start | bytes 196616 | tf_op jit(solution)/shard_map/ppermute | solution.py:334
  48.0 2.9 %collective-permute-start.10 = (bf16[4,64,128]{2,1,0:T(8,128)(2,1)S(1)}, bf16[4,64,128]{2,1,0:T(8,128)(2,1)S(1)}, u32[]{:S(2)}, u32[]{:S(2)}) collective-permute-start(bf16[4,64,128]{2,1,0:T(8,128)(2,1)S(1)} %get-tuple-element.37), channel_id=1, source_target_pairs={{0,2},{1,3},{2,0},{3,1},{4,6},{5,7},{6,4},{7,5},{8,10},{9,11},{10,... | collective-permute-start | bytes 196616 | tf_op jit(solution)/shard_map/ppermute | solution.py:334
  50.8 0.0 collective-permute-start.11
  50.9 3.9 %collective-permute-start.12 = (bf16[4,64,128]{2,1,0:T(8,128)(2,1)S(1)}, bf16[4,64,128]{2,1,0:T(8,128)(2,1)S(1)}, u32[]{:S(2)}, u32[]{:S(2)}) collective-permute-start(bf16[4,64,128]{2,1,0:T(8,128)(2,1)S(1)} %get-tuple-element.39), channel_id=1, source_target_pairs={{0,4},{1,5},{2,6},{3,7},{4,0},{5,1},{6,2},{7,3},{8,12},{9,13},{10,... | collective-permute-start | bytes 196616 | tf_op jit(solution)/shard_map/ppermute | solution.py:334
  54.8 2.4 %collective-permute-start.14 = (bf16[4,64,128]{2,1,0:T(8,128)(2,1)S(1)}, bf16[4,64,128]{2,1,0:T(8,128)(2,1)S(1)}, u32[]{:S(2)}, u32[]{:S(2)}) collective-permute-start(bf16[4,64,128]{2,1,0:T(8,128)(2,1)S(1)} %get-tuple-element.41), channel_id=1, source_target_pairs={{0,6},{1,7},{2,4},{3,5},{4,2},{5,3},{6,0},{7,1},{8,14},{9,15},{10,... | collective-permute-start | bytes 196616 | tf_op jit(solution)/shard_map/ppermute | solution.py:334
  57.1 0.0 collective-permute-done.10.refs_2_
  57.1 2.4 %collective-permute-start.15 = (bf16[4,64,128]{2,1,0:T(8,128)(2,1)S(1)}, bf16[4,64,128]{2,1,0:T(8,128)(2,1)S(1)}, u32[]{:S(2)}, u32[]{:S(2)}) collective-permute-start(bf16[4,64,128]{2,1,0:T(8,128)(2,1)S(1)} %get-tuple-element.42), channel_id=1, source_target_pairs={{0,7},{1,6},{2,5},{3,4},{4,3},{5,2},{6,1},{7,0},{8,15},{9,14},{10,... | collective-permute-start | bytes 196616 | tf_op jit(solution)/shard_map/ppermute | solution.py:334
  59.5 0.3 turn_cotangent.1.turned_ref
  59.8 0.0 copy-start.6
  59.8 0.0 collective-permute-done.11.refs_3_
  59.8 1.2 %collective-permute-done.12.refs_4_ = bf16[4,64,128]{2,1,0:T(8,128)(2,1)S(1)} collective-permute-done((bf16[4,64,128]{2,1,0:T(8,128)(2,1)S(1)}, bf16[4,64,128]{2,1,0:T(8,128)(2,1)S(1)}, u32[]{:S(2)}, u32[]{:S(2)}) %collective-permute-start.12) | collective-permute-done | bytes 65568 | tf_op jit(solution)/shard_map/ppermute | solution.py:334
  61.0 1.6 %collective-permute-done.13.refs_5_ = bf16[4,64,128]{2,1,0:T(8,128)(2,1)S(1)} collective-permute-done((bf16[4,64,128]{2,1,0:T(8,128)(2,1)S(1)}, bf16[4,64,128]{2,1,0:T(8,128)(2,1)S(1)}, u32[]{:S(2)}, u32[]{:S(2)}) %collective-permute-start.13) | collective-permute-done | bytes 65568 | tf_op jit(solution)/shard_map/ppermute | solution.py:334
  62.6 0.0 collective-permute-done.14.refs_6_
  62.6 1.6 %collective-permute-done.15.refs_7_ = bf16[4,64,128]{2,1,0:T(8,128)(2,1)S(1)} collective-permute-done((bf16[4,64,128]{2,1,0:T(8,128)(2,1)S(1)}, bf16[4,64,128]{2,1,0:T(8,128)(2,1)S(1)}, u32[]{:S(2)}, u32[]{:S(2)}) %collective-permute-start.15) | collective-permute-done | bytes 65568 | tf_op jit(solution)/shard_map/ppermute | solution.py:334
  64.2 3.1 %norm_and_gradient.1 = (bf16[2,4,256,128]{3,2,1,0:T(8,128)(2,1)S(1)}, bf16[2,256,128]{2,1,0:T(8,128)(2,1)S(1)}, bf16[2,256,128]{2,1,0:T(8,128)(2,1)S(1)}, f32[576,128]{1,0:T(8,128)S(1)}, f32[576,128]{1,0:T(8,128)S(1)}) custom-call(s32[2]{0:T(128)S(1)} %copy-done.8, s32[1]{0:T(128)} %bitcast.index_ref, s32[1]{0:T(128)} %bitcast.1.core_ref, ...), custom_call_target="tpu_custom_call" | custom-call | flops 603979776 | bytes 2097152 | tf_op jit(solution)/shard_map/norm_and_gradient/pallas_call | solution.py:459
  67.3 0.1 collective-permute-start.18
  67.4 1.5 %collective-permute-start.16 = (bf16[2,256,128]{2,1,0:T(8,128)(2,1)S(1)}, bf16[2,256,128]{2,1,0:T(8,128)(2,1)S(1)}, u32[]{:S(2)}, u32[]{:S(2)}) collective-permute-start(bf16[2,256,128]{2,1,0:T(8,128)(2,1)S(1)} %get-tuple-element.44), channel_id=1, source_target_pairs={{0,1},{1,0},{2,3},{3,2},{4,5},{5,4},{6,7},{7,6},{8,9},{9,8},{10,11... | collective-permute-start | bytes 393224 | tf_op jit(solution)/shard_map/ppermute | solution.py:334
  68.9 0.8 collective-permute-start.17
  69.8 3.4 %collective-permute-start.19 = (bf16[144,128]{1,0:T(8,128)(2,1)S(1)}, bf16[144,128]{1,0:T(8,128)(2,1)S(1)}, u32[]{:S(2)}, u32[]{:S(2)}) collective-permute-start(bf16[144,128]{1,0:T(8,128)(2,1)S(1)} %get-tuple-element.50), channel_id=1, source_target_pairs={{0,1},{1,0},{2,3},{3,2},{4,5},{5,4},{6,7},{7,6},{8,9},{9,8},{10,11... | collective-permute-start | bytes 110600 | tf_op jit(solution)/shard_map/ppermute | solution.py:352
  73.2 2.3 %collective-permute-start.20 = (bf16[144,128]{1,0:T(8,128)(2,1)S(1)}, bf16[144,128]{1,0:T(8,128)(2,1)S(1)}, u32[]{:S(2)}, u32[]{:S(2)}) collective-permute-start(bf16[144,128]{1,0:T(8,128)(2,1)S(1)} %get-tuple-element.51), channel_id=1, source_target_pairs={{0,16},{1,17},{2,18},{3,19},{4,20},{5,21},{6,22},{7,23},{8,24},{9,... | collective-permute-start | bytes 110600 | tf_op jit(solution)/shard_map/ppermute | solution.py:352
  75.5 0.0 collective-permute-start.21
  75.5 0.7 collective-permute-done.19.refs_1_
  76.2 1.2 %collective-permute-done.20.refs_2_ = bf16[144,128]{1,0:T(8,128)(2,1)S(1)} collective-permute-done((bf16[144,128]{1,0:T(8,128)(2,1)S(1)}, bf16[144,128]{1,0:T(8,128)(2,1)S(1)}, u32[]{:S(2)}, u32[]{:S(2)}) %collective-permute-start.20) | collective-permute-done | bytes 36896 | tf_op jit(solution)/shard_map/ppermute | solution.py:352
  77.4 2.9 %collective-permute-done.21.refs_3_ = bf16[144,128]{1,0:T(8,128)(2,1)S(1)} collective-permute-done((bf16[144,128]{1,0:T(8,128)(2,1)S(1)}, bf16[144,128]{1,0:T(8,128)(2,1)S(1)}, u32[]{:S(2)}, u32[]{:S(2)}) %collective-permute-start.21) | collective-permute-done | bytes 36896 | tf_op jit(solution)/shard_map/ppermute | solution.py:352
  80.4 0.9 collective-permute-start.24
  81.3 1.7 %collective-permute-start.23 = (bf16[144,128]{1,0:T(8,128)(2,1)S(1)}, bf16[144,128]{1,0:T(8,128)(2,1)S(1)}, u32[]{:S(2)}, u32[]{:S(2)}) collective-permute-start(bf16[144,128]{1,0:T(8,128)(2,1)S(1)} %sum_chips.1.refs_0_), channel_id=1, source_target_pairs={{0,4},{1,5},{2,6},{3,7},{4,0},{5,1},{6,2},{7,3},{8,12},{9,13},{10,... | collective-permute-start | bytes 110600 | tf_op jit(solution)/shard_map/ppermute | solution.py:334
  83.0 1.8 %collective-permute-start.22 = (bf16[144,128]{1,0:T(8,128)(2,1)S(1)}, bf16[144,128]{1,0:T(8,128)(2,1)S(1)}, u32[]{:S(2)}, u32[]{:S(2)}) collective-permute-start(bf16[144,128]{1,0:T(8,128)(2,1)S(1)} %sum_chips.1.refs_0_), channel_id=1, source_target_pairs={{0,2},{1,3},{2,0},{3,1},{4,6},{5,7},{6,4},{7,5},{8,10},{9,11},{10,... | collective-permute-start | bytes 110600 | tf_op jit(solution)/shard_map/ppermute | solution.py:334
  84.8 0.0 collective-permute-done.17.far_ref
  84.8 2.2 %decode.1 = (bf16[2,4,256,128]{3,2,1,0:T(8,128)(2,1)}, f32[8,128]{1,0:T(8,128)S(1)}) custom-call(s32[1]{0:T(128)} %bitcast.index_ref, bf16[2,4,256,128]{3,2,1,0:T(8,128)(2,1)S(1)} %get-tuple-element.43.image_ref, bf16[2,256,128]{2,1,0:T(8,128)(2,1)S(1)} %collective-permute-done.16.near_ref, bf16[2,256,128]{2,1,0:T(8,128)(2,1)S(1)} %collective-permute-done.17.far_ref, ...), custom_call_target="tpu_custom_call" | custom-call | flops 603979776 | bytes 1048576 | tf_op jit(solution)/shard_map/decode/pallas_call | solution.py:497
  87.0 0.0 collective-permute-done.22.refs_1_
  87.1 0.8 collective-permute-start.27
  87.9 1.9 %collective-permute-start.26 = (bf16[144,128]{1,0:T(8,128)(2,1)S(1)}, bf16[144,128]{1,0:T(8,128)(2,1)S(1)}, u32[]{:S(2)}, u32[]{:S(2)}) collective-permute-start(bf16[144,128]{1,0:T(8,128)(2,1)S(1)} %sum_planes.1.refs_0_), channel_id=1, source_target_pairs={{0,16},{1,17},{2,18},{3,19},{4,20},{5,21},{6,22},{7,23},{8,24},{9,... | collective-permute-start | bytes 110600 | tf_op jit(solution)/shard_map/ppermute | solution.py:352
  89.8 0.9 collective-permute-start.25
  90.7 1.5 %collective-permute-done.27.refs_3_ = bf16[144,128]{1,0:T(8,128)(2,1)S(1)} collective-permute-done((bf16[144,128]{1,0:T(8,128)(2,1)S(1)}, bf16[144,128]{1,0:T(8,128)(2,1)S(1)}, u32[]{:S(2)}, u32[]{:S(2)}) %collective-permute-start.27) | collective-permute-done | bytes 36896 | tf_op jit(solution)/shard_map/ppermute | solution.py:352
  92.1 0.1 collective-permute-done.26.refs_2_
  92.2 1.5 %collective-permute-done.25.refs_1_ = bf16[144,128]{1,0:T(8,128)(2,1)S(1)} collective-permute-done((bf16[144,128]{1,0:T(8,128)(2,1)S(1)}, bf16[144,128]{1,0:T(8,128)(2,1)S(1)}, u32[]{:S(2)}, u32[]{:S(2)}) %collective-permute-start.25) | collective-permute-done | bytes 36896 | tf_op jit(solution)/shard_map/ppermute | solution.py:352
  93.7 0.1 collective-permute-start.28
  93.8 1.4 %collective-permute-done.28.other_ref = bf16[576,128]{1,0:T(8,128)(2,1)S(1)} collective-permute-done((bf16[576,128]{1,0:T(8,128)(2,1)S(1)}, bf16[576,128]{1,0:T(8,128)(2,1)S(1)}, u32[]{:S(2)}, u32[]{:S(2)}) %collective-permute-start.28) | collective-permute-done | bytes 147488 | tf_op jit(solution)/shard_map/ppermute | solution.py:356
  95.2 0.9 spread_sums.1
  (27 shorter events, 0.2 us)
Async XLA Ops:
  0.6 8.3 %copy-start.3 = (bf16[2,4,256,128]{3,2,1,0:T(8,128)(2,1)S(1)}, bf16[2,4,256,128]{3,2,1,0:T(8,128)(2,1)}, u32[]{:S(2)}) copy-start(bf16[2,4,256,128]{3,2,1,0:T(8,128)(2,1)} %cot_ref.1) | copy-start | bytes 1572868
  0.6 36.4 %copy-start.8 = (s32[2]{0:T(128)S(1)}, s32[2]{0:T(128)}, u32[]{:S(2)}) copy-start(s32[2]{0:T(128)} %lengths_ref.1) | copy-start | bytes 28
  0.7 36.5 %copy-start = (bf16[64,2,2048]{2,1,0:T(2,128)(2,1)S(1)}, bf16[64,2,2048]{2,1,0:T(2,128)(2,1)}, u32[]{:S(2)}) copy-start(bf16[64,2,2048]{2,1,0:T(2,128)(2,1)} %query_ref.5) | copy-start | bytes 1572868
  0.7 36.5 %copy-start.1 = (bf16[64,2,2048]{2,1,0:T(2,128)(2,1)S(1)}, bf16[64,2,2048]{2,1,0:T(2,128)(2,1)}, u32[]{:S(2)}) copy-start(bf16[64,2,2048]{2,1,0:T(2,128)(2,1)} %key_ref.5) | copy-start | bytes 1572868
  0.7 36.5 %copy-start.2 = (bf16[64,2,2048]{2,1,0:T(2,128)(2,1)S(1)}, bf16[64,2,2048]{2,1,0:T(2,128)(2,1)}, u32[]{:S(2)}) copy-start(bf16[64,2,2048]{2,1,0:T(2,128)(2,1)} %value_ref.5) | copy-start | bytes 1572868
  3.3 27.6 %collective-permute-start.3 = (bf16[3,4,64,128]{3,2,1,0:T(8,128)(2,1)}, bf16[3,4,64,128]{3,2,1,0:T(8,128)(2,1)S(1)}, u32[]{:S(2)}, u32[]{:S(2)}) collective-permute-start(bf16[3,4,64,128]{3,2,1,0:T(8,128)(2,1)} %get-tuple-element.29), channel_id=1, source_target_pairs={{0,2},{1,3},{2,0},{3,1},{4,6},{5,7},{6,4},{7,5},{8,10},{9,11},{10,... | collective-permute-start | bytes 589832 | tf_op jit(solution)/shard_map/ppermute | solution.py:334
  6.4 29.1 %collective-permute-start.5 = (bf16[3,4,64,128]{3,2,1,0:T(8,128)(2,1)}, bf16[3,4,64,128]{3,2,1,0:T(8,128)(2,1)S(1)}, u32[]{:S(2)}, u32[]{:S(2)}) collective-permute-start(bf16[3,4,64,128]{3,2,1,0:T(8,128)(2,1)} %get-tuple-element.31), channel_id=1, source_target_pairs={{0,4},{1,5},{2,6},{3,7},{4,0},{5,1},{6,2},{7,3},{8,12},{9,13},{10,... | collective-permute-start | bytes 589832 | tf_op jit(solution)/shard_map/ppermute | solution.py:334
  9.0 3.3 %collective-permute-start.1 = (bf16[2,256,128]{2,1,0:T(8,128)(2,1)S(1)}, bf16[2,256,128]{2,1,0:T(8,128)(2,1)S(1)}, u32[]{:S(2)}, u32[]{:S(2)}) collective-permute-start(bf16[2,256,128]{2,1,0:T(8,128)(2,1)S(1)} %get-tuple-element.54), channel_id=1, source_target_pairs={{1,2},{3,4},{5,6},{2,1},{4,3},{6,5},{9,10},{11,12},{13,14},{10,9},... | collective-permute-start | bytes 393224 | tf_op jit(solution)/shard_map/ppermute | solution.py:382
  9.7 26.5 %collective-permute-start.6 = (bf16[3,4,64,128]{3,2,1,0:T(8,128)(2,1)}, bf16[3,4,64,128]{3,2,1,0:T(8,128)(2,1)S(1)}, u32[]{:S(2)}, u32[]{:S(2)}) collective-permute-start(bf16[3,4,64,128]{3,2,1,0:T(8,128)(2,1)} %get-tuple-element.32), channel_id=1, source_target_pairs={{0,5},{1,4},{2,7},{3,6},{4,1},{5,0},{6,3},{7,2},{8,13},{9,12},{10,... | collective-permute-start | bytes 589832 | tf_op jit(solution)/shard_map/ppermute | solution.py:334
  12.3 0.7 copy-start.4
  15.7 22.9 %collective-permute-start.2 = (bf16[3,4,64,128]{3,2,1,0:T(8,128)(2,1)}, bf16[3,4,64,128]{3,2,1,0:T(8,128)(2,1)S(1)}, u32[]{:S(2)}, u32[]{:S(2)}) collective-permute-start(bf16[3,4,64,128]{3,2,1,0:T(8,128)(2,1)} %get-tuple-element.28), channel_id=1, source_target_pairs={{0,1},{1,0},{2,3},{3,2},{4,5},{5,4},{6,7},{7,6},{8,9},{9,8},{10,11... | collective-permute-start | bytes 589832 | tf_op jit(solution)/shard_map/ppermute | solution.py:334
  23.9 14.7 %collective-permute-start.4 = (bf16[3,4,64,128]{3,2,1,0:T(8,128)(2,1)}, bf16[3,4,64,128]{3,2,1,0:T(8,128)(2,1)S(1)}, u32[]{:S(2)}, u32[]{:S(2)}) collective-permute-start(bf16[3,4,64,128]{3,2,1,0:T(8,128)(2,1)} %get-tuple-element.30), channel_id=1, source_target_pairs={{0,3},{1,2},{2,1},{3,0},{4,7},{5,6},{6,5},{7,4},{8,11},{9,10},{10,... | collective-permute-start | bytes 589832 | tf_op jit(solution)/shard_map/ppermute | solution.py:334
  30.9 10.9 %collective-permute-start.7 = (bf16[3,4,64,128]{3,2,1,0:T(8,128)(2,1)}, bf16[3,4,64,128]{3,2,1,0:T(8,128)(2,1)S(1)}, u32[]{:S(2)}, u32[]{:S(2)}) collective-permute-start(bf16[3,4,64,128]{3,2,1,0:T(8,128)(2,1)} %get-tuple-element.33), channel_id=1, source_target_pairs={{0,6},{1,7},{2,4},{3,5},{4,2},{5,3},{6,0},{7,1},{8,14},{9,15},{10,... | collective-permute-start | bytes 589832 | tf_op jit(solution)/shard_map/ppermute | solution.py:334
  35.4 8.7 %collective-permute-start.8 = (bf16[3,4,64,128]{3,2,1,0:T(8,128)(2,1)}, bf16[3,4,64,128]{3,2,1,0:T(8,128)(2,1)S(1)}, u32[]{:S(2)}, u32[]{:S(2)}) collective-permute-start(bf16[3,4,64,128]{3,2,1,0:T(8,128)(2,1)} %get-tuple-element.34), channel_id=1, source_target_pairs={{0,7},{1,6},{2,5},{3,4},{4,3},{5,2},{6,1},{7,0},{8,15},{9,14},{10,... | collective-permute-start | bytes 589832 | tf_op jit(solution)/shard_map/ppermute | solution.py:334
  36.1 18.6 %collective-permute-start = (bf16[2,256,128]{2,1,0:T(8,128)(2,1)S(1)}, bf16[2,256,128]{2,1,0:T(8,128)(2,1)S(1)}, u32[]{:S(2)}, u32[]{:S(2)}) collective-permute-start(bf16[2,256,128]{2,1,0:T(8,128)(2,1)S(1)} %get-tuple-element.55), channel_id=1, source_target_pairs={{0,1},{1,0},{2,3},{3,2},{4,5},{5,4},{6,7},{7,6},{8,9},{9,8},{10,11... | collective-permute-start | bytes 393224 | tf_op jit(solution)/shard_map/ppermute | solution.py:334
  37.1 22.4 %copy-start.5 = (bf16[2,256,128]{2,1,0:T(8,128)(2,1)S(1)}, bf16[2,256,128]{2,1,0:T(8,128)(2,1)}, u32[]{:S(2)}) copy-start(bf16[2,256,128]{2,1,0:T(8,128)(2,1)} %copy-done.4) | copy-start | bytes 393220
  46.6 17.6 %copy-start.7 = (f32[2048]{0:T(1024)S(1)}, f32[2048]{0:T(1024)}, u32[]{:S(2)}) copy-start(f32[2048]{0:T(1024)} %param.11) | copy-start | bytes 24580
  46.6 8.2 %collective-permute-start.9 = (bf16[4,64,128]{2,1,0:T(8,128)(2,1)S(1)}, bf16[4,64,128]{2,1,0:T(8,128)(2,1)S(1)}, u32[]{:S(2)}, u32[]{:S(2)}) collective-permute-start(bf16[4,64,128]{2,1,0:T(8,128)(2,1)S(1)} %get-tuple-element.36), channel_id=1, source_target_pairs={{0,1},{1,0},{2,3},{3,2},{4,5},{5,4},{6,7},{7,6},{8,9},{9,8},{10,11... | collective-permute-start | bytes 196616 | tf_op jit(solution)/shard_map/ppermute | solution.py:334
  48.0 9.2 %collective-permute-start.10 = (bf16[4,64,128]{2,1,0:T(8,128)(2,1)S(1)}, bf16[4,64,128]{2,1,0:T(8,128)(2,1)S(1)}, u32[]{:S(2)}, u32[]{:S(2)}) collective-permute-start(bf16[4,64,128]{2,1,0:T(8,128)(2,1)S(1)} %get-tuple-element.37), channel_id=1, source_target_pairs={{0,2},{1,3},{2,0},{3,1},{4,6},{5,7},{6,4},{7,5},{8,10},{9,11},{10,... | collective-permute-start | bytes 196616 | tf_op jit(solution)/shard_map/ppermute | solution.py:334
  50.8 8.9 %collective-permute-start.11 = (bf16[4,64,128]{2,1,0:T(8,128)(2,1)S(1)}, bf16[4,64,128]{2,1,0:T(8,128)(2,1)S(1)}, u32[]{:S(2)}, u32[]{:S(2)}) collective-permute-start(bf16[4,64,128]{2,1,0:T(8,128)(2,1)S(1)} %get-tuple-element.38), channel_id=1, source_target_pairs={{0,3},{1,2},{2,1},{3,0},{4,7},{5,6},{6,5},{7,4},{8,11},{9,10},{10,... | collective-permute-start | bytes 196616 | tf_op jit(solution)/shard_map/ppermute | solution.py:334
  50.9 10.1 %collective-permute-start.12 = (bf16[4,64,128]{2,1,0:T(8,128)(2,1)S(1)}, bf16[4,64,128]{2,1,0:T(8,128)(2,1)S(1)}, u32[]{:S(2)}, u32[]{:S(2)}) collective-permute-start(bf16[4,64,128]{2,1,0:T(8,128)(2,1)S(1)} %get-tuple-element.39), channel_id=1, source_target_pairs={{0,4},{1,5},{2,6},{3,7},{4,0},{5,1},{6,2},{7,3},{8,12},{9,13},{10,... | collective-permute-start | bytes 196616 | tf_op jit(solution)/shard_map/ppermute | solution.py:334
  54.8 7.8 %collective-permute-start.13 = (bf16[4,64,128]{2,1,0:T(8,128)(2,1)S(1)}, bf16[4,64,128]{2,1,0:T(8,128)(2,1)S(1)}, u32[]{:S(2)}, u32[]{:S(2)}) collective-permute-start(bf16[4,64,128]{2,1,0:T(8,128)(2,1)S(1)} %get-tuple-element.40), channel_id=1, source_target_pairs={{0,5},{1,4},{2,7},{3,6},{4,1},{5,0},{6,3},{7,2},{8,13},{9,12},{10,... | collective-permute-start | bytes 196616 | tf_op jit(solution)/shard_map/ppermute | solution.py:334
  54.8 7.8 %collective-permute-start.14 = (bf16[4,64,128]{2,1,0:T(8,128)(2,1)S(1)}, bf16[4,64,128]{2,1,0:T(8,128)(2,1)S(1)}, u32[]{:S(2)}, u32[]{:S(2)}) collective-permute-start(bf16[4,64,128]{2,1,0:T(8,128)(2,1)S(1)} %get-tuple-element.41), channel_id=1, source_target_pairs={{0,6},{1,7},{2,4},{3,5},{4,2},{5,3},{6,0},{7,1},{8,14},{9,15},{10,... | collective-permute-start | bytes 196616 | tf_op jit(solution)/shard_map/ppermute | solution.py:334
  57.1 7.1 %collective-permute-start.15 = (bf16[4,64,128]{2,1,0:T(8,128)(2,1)S(1)}, bf16[4,64,128]{2,1,0:T(8,128)(2,1)S(1)}, u32[]{:S(2)}, u32[]{:S(2)}) collective-permute-start(bf16[4,64,128]{2,1,0:T(8,128)(2,1)S(1)} %get-tuple-element.42), channel_id=1, source_target_pairs={{0,7},{1,6},{2,5},{3,4},{4,3},{5,2},{6,1},{7,0},{8,15},{9,14},{10,... | collective-permute-start | bytes 196616 | tf_op jit(solution)/shard_map/ppermute | solution.py:334
  59.8 25.1 %copy-start.6 = (bf16[9,128,128]{2,1,0:T(8,128)(2,1)S(1)}, bf16[9,128,128]{2,1,0:T(8,128)(2,1)}, u32[]{:S(2)}) copy-start(bf16[9,128,128]{2,1,0:T(8,128)(2,1)} %param.12) | copy-start | bytes 884740
  67.3 2.5 %collective-permute-start.18 = (f32[576,128]{1,0:T(8,128)S(1)}, f32[576,128]{1,0:T(8,128)S(1)}, u32[]{:S(2)}, u32[]{:S(2)}) collective-permute-start(f32[576,128]{1,0:T(8,128)S(1)} %get-tuple-element.48), channel_id=1, source_target_pairs={{0,8},{8,0},{16,24},{24,16},{1,9},{9,1},{17,25},{25,17},{2,10},{10... | collective-permute-start | bytes 884744 | tf_op jit(solution)/shard_map/ppermute | solution.py:356
  67.4 17.5 %collective-permute-start.16 = (bf16[2,256,128]{2,1,0:T(8,128)(2,1)S(1)}, bf16[2,256,128]{2,1,0:T(8,128)(2,1)S(1)}, u32[]{:S(2)}, u32[]{:S(2)}) collective-permute-start(bf16[2,256,128]{2,1,0:T(8,128)(2,1)S(1)} %get-tuple-element.44), channel_id=1, source_target_pairs={{0,1},{1,0},{2,3},{3,2},{4,5},{5,4},{6,7},{7,6},{8,9},{9,8},{10,11... | collective-permute-start | bytes 393224 | tf_op jit(solution)/shard_map/ppermute | solution.py:334
  68.9 15.9 %collective-permute-start.17 = (bf16[2,256,128]{2,1,0:T(8,128)(2,1)S(1)}, bf16[2,256,128]{2,1,0:T(8,128)(2,1)S(1)}, u32[]{:S(2)}, u32[]{:S(2)}) collective-permute-start(bf16[2,256,128]{2,1,0:T(8,128)(2,1)S(1)} %get-tuple-element.45), channel_id=1, source_target_pairs={{1,2},{3,4},{5,6},{2,1},{4,3},{6,5},{9,10},{11,12},{13,14},{10,9},... | collective-permute-start | bytes 393224 | tf_op jit(solution)/shard_map/ppermute | solution.py:485
  69.8 6.4 %collective-permute-start.19 = (bf16[144,128]{1,0:T(8,128)(2,1)S(1)}, bf16[144,128]{1,0:T(8,128)(2,1)S(1)}, u32[]{:S(2)}, u32[]{:S(2)}) collective-permute-start(bf16[144,128]{1,0:T(8,128)(2,1)S(1)} %get-tuple-element.50), channel_id=1, source_target_pairs={{0,1},{1,0},{2,3},{3,2},{4,5},{5,4},{6,7},{7,6},{8,9},{9,8},{10,11... | collective-permute-start | bytes 110600 | tf_op jit(solution)/shard_map/ppermute | solution.py:352
  73.2 4.2 %collective-permute-start.20 = (bf16[144,128]{1,0:T(8,128)(2,1)S(1)}, bf16[144,128]{1,0:T(8,128)(2,1)S(1)}, u32[]{:S(2)}, u32[]{:S(2)}) collective-permute-start(bf16[144,128]{1,0:T(8,128)(2,1)S(1)} %get-tuple-element.51), channel_id=1, source_target_pairs={{0,16},{1,17},{2,18},{3,19},{4,20},{5,21},{6,22},{7,23},{8,24},{9,... | collective-permute-start | bytes 110600 | tf_op jit(solution)/shard_map/ppermute | solution.py:352
  75.5 4.9 %collective-permute-start.21 = (bf16[144,128]{1,0:T(8,128)(2,1)S(1)}, bf16[144,128]{1,0:T(8,128)(2,1)S(1)}, u32[]{:S(2)}, u32[]{:S(2)}) collective-permute-start(bf16[144,128]{1,0:T(8,128)(2,1)S(1)} %get-tuple-element.52), channel_id=1, source_target_pairs={{0,17},{1,16},{2,19},{3,18},{4,21},{5,20},{6,23},{7,22},{8,25},{9,... | collective-permute-start | bytes 110600 | tf_op jit(solution)/shard_map/ppermute | solution.py:352
  80.4 6.7 %collective-permute-start.24 = (bf16[144,128]{1,0:T(8,128)(2,1)S(1)}, bf16[144,128]{1,0:T(8,128)(2,1)S(1)}, u32[]{:S(2)}, u32[]{:S(2)}) collective-permute-start(bf16[144,128]{1,0:T(8,128)(2,1)S(1)} %sum_chips.1.refs_0_), channel_id=1, source_target_pairs={{0,6},{1,7},{2,4},{3,5},{4,2},{5,3},{6,0},{7,1},{8,14},{9,15},{10,... | collective-permute-start | bytes 110600 | tf_op jit(solution)/shard_map/ppermute | solution.py:334
  81.3 5.7 %collective-permute-start.23 = (bf16[144,128]{1,0:T(8,128)(2,1)S(1)}, bf16[144,128]{1,0:T(8,128)(2,1)S(1)}, u32[]{:S(2)}, u32[]{:S(2)}) collective-permute-start(bf16[144,128]{1,0:T(8,128)(2,1)S(1)} %sum_chips.1.refs_0_), channel_id=1, source_target_pairs={{0,4},{1,5},{2,6},{3,7},{4,0},{5,1},{6,2},{7,3},{8,12},{9,13},{10,... | collective-permute-start | bytes 110600 | tf_op jit(solution)/shard_map/ppermute | solution.py:334
  83.0 4.1 %collective-permute-start.22 = (bf16[144,128]{1,0:T(8,128)(2,1)S(1)}, bf16[144,128]{1,0:T(8,128)(2,1)S(1)}, u32[]{:S(2)}, u32[]{:S(2)}) collective-permute-start(bf16[144,128]{1,0:T(8,128)(2,1)S(1)} %sum_chips.1.refs_0_), channel_id=1, source_target_pairs={{0,2},{1,3},{2,0},{3,1},{4,6},{5,7},{6,4},{7,5},{8,10},{9,11},{10,... | collective-permute-start | bytes 110600 | tf_op jit(solution)/shard_map/ppermute | solution.py:334
  87.1 5.0 %collective-permute-start.27 = (bf16[144,128]{1,0:T(8,128)(2,1)S(1)}, bf16[144,128]{1,0:T(8,128)(2,1)S(1)}, u32[]{:S(2)}, u32[]{:S(2)}) collective-permute-start(bf16[144,128]{1,0:T(8,128)(2,1)S(1)} %sum_planes.1.refs_0_), channel_id=1, source_target_pairs={{0,17},{1,16},{2,19},{3,18},{4,21},{5,20},{6,23},{7,22},{8,25},{9,... | collective-permute-start | bytes 110600 | tf_op jit(solution)/shard_map/ppermute | solution.py:352
  87.9 4.4 %collective-permute-start.26 = (bf16[144,128]{1,0:T(8,128)(2,1)S(1)}, bf16[144,128]{1,0:T(8,128)(2,1)S(1)}, u32[]{:S(2)}, u32[]{:S(2)}) collective-permute-start(bf16[144,128]{1,0:T(8,128)(2,1)S(1)} %sum_planes.1.refs_0_), channel_id=1, source_target_pairs={{0,16},{1,17},{2,18},{3,19},{4,20},{5,21},{6,22},{7,23},{8,24},{9,... | collective-permute-start | bytes 110600 | tf_op jit(solution)/shard_map/ppermute | solution.py:352
  89.8 4.0 %collective-permute-start.25 = (bf16[144,128]{1,0:T(8,128)(2,1)S(1)}, bf16[144,128]{1,0:T(8,128)(2,1)S(1)}, u32[]{:S(2)}, u32[]{:S(2)}) collective-permute-start(bf16[144,128]{1,0:T(8,128)(2,1)S(1)} %sum_planes.1.refs_0_), channel_id=1, source_target_pairs={{0,1},{1,0},{2,3},{3,2},{4,5},{5,4},{6,7},{7,6},{8,9},{9,8},{10,11... | collective-permute-start | bytes 110600 | tf_op jit(solution)/shard_map/ppermute | solution.py:352
  93.7 1.4 %collective-permute-start.28 = (bf16[576,128]{1,0:T(8,128)(2,1)S(1)}, bf16[576,128]{1,0:T(8,128)(2,1)S(1)}, u32[]{:S(2)}, u32[]{:S(2)}) collective-permute-start(bf16[576,128]{1,0:T(8,128)(2,1)S(1)} %join_chips.1.own_ref), channel_id=1, source_target_pairs={{0,8},{8,0},{16,24},{24,16},{1,9},{9,1},{17,25},{25,17},{2,10},{10... | collective-permute-start | bytes 442376 | tf_op jit(solution)/shard_map/ppermute | solution.py:356

commit v13 on v12

--- a/solution.py
+++ b/solution.py
@@ -381,8 +381,9 @@
     cot_far = jnp.where(odd, cotangent[:, PATCH - 1], cotangent[:, 0])
     cot_far = lax.ppermute(cot_far, "seq", far_pairs)
     half = seq_count // 2
-    early = [2, half, half + 1]
-    late = [distance for distance in range(1, seq_count) if distance not in early]
+    early = [half, half + 1]
+    near_by, far_off = (list(range(1, half)), list(range(half + 2, seq_count)))
+    late = far_off[:1] + near_by[:2] + far_off[1:] + near_by[2:]
     span = max(1, per_device // regions) * width
 
     def pack(name, distances, *after):
@@ -407,7 +408,7 @@
         packed[distance] = trade(chunk, distance)
     for distance, chunk in zip(late, pack("pack_late", late, cot_far)):
         packed[distance] = trade(chunk, distance)
-    order = list(range(1, seq_count)) + [0]
+    order = early + late + [0]
     packed[0] = call(
         functools.partial(own_kernel, regions, per_device),
         "own_chunk",
@@ -442,7 +443,7 @@
         moved=4 * local_bytes,
         exps=per_device * capacity * capacity,
     )(index, item_lengths, *[packed[distance] for distance in order])
-    attended = [mixed[0]] + [trade(mixed[distance], distance) for distance in order[:-1]]
+    attended = [mixed[0]] + [trade(mixed[distance], distance) for distance in range(1, seq_count)]
 
     turned = call(
         turn_kernel,

time: 96.3 us -> 98.5 us (1.023)
  waiting for transfers between devices: 20.3 us -> 36.2 us
  starting transfers between devices: 59.4 us -> 44.6 us
    ppermute x19, waiting for transfers between devices: 11 us -> 27.4 us  [trade(): return lax.ppermute(values, 'seq', pairs)]
    ppermute x19, starting transfers between devices: 48.5 us -> 32.6 us  [trade(): return lax.ppermute(values, 'seq', pairs)]
    ppermute x6, starting transfers between devices: 9.24 us -> 10.3 us  [trade_chips(): return lax.ppermute(values, ('dp', 'seq'), pairs)]
  transfers between devices with their start and end apart: 29 -> 29, of which waited for: 13 -> 14; matrix products, arithmetic and copies ran while one was open for 0% -> 0% of each run, Pallas kernels for 8% -> 11%
where the time goes in v13:
time: 98.5 us; the launch traced here: 98.2 us
  starting transfers between devices  44.6 us (45%)
  waiting for transfers between devices  36.2 us (37%)
  Pallas kernels  14.7 us (15%)
  other arithmetic  1.09 us (1%)
    ppermute x19, starting transfers between devices, trade(): return lax.ppermute(values, 'seq', pairs)  32.6 us
    ppermute x19, waiting for transfers between devices, trade(): return lax.ppermute(values, 'seq', pairs)  27.4 us
    ppermute x6, starting transfers between devices, trade_chips(): return lax.ppermute(values, ('dp', 'seq'), pairs)  10.3 us
    ppermute x6, waiting for transfers between devices, trade_chips(): return lax.ppermute(values, ('dp', 'seq'), pairs)  7.42 us
    pallas_call x2, Pallas kernels, pack(): call(functools.partial(pack_kernel, distances, regions, per_device), name...  5.27 us
    pallas_call x1, Pallas kernels, body(): call(norm_kernel, 'norm_and_gradient', [jax.ShapeDtypeStruct((regions, PA...  3.06 us
    pallas_call x1, Pallas kernels, body(): call(functools.partial(attend_kernel, block_rows, group, order), 'attend'...  2.48 us
    pallas_call x1, Pallas kernels, body(): call(decode_kernel, 'decode', [jax.ShapeDtypeStruct(cotangent.shape, jnp....  2.22 us
  transfers between devices with their start and end apart: 29, of which 14 were waited for; matrix products, arithmetic and copies ran while one was open for 0% of the time, Pallas kernels for 11%

profile of v13, /device:TPU:0, one launch (start us, length us, event | category | flops | bytes accessed | tf_op | source)
XLA Modules:
  0.0 98.2 jit_solution(10040653042916962530)
XLA Ops:
  0.6 1.0 %fusion.1 = (bf16[2,256,128]{2,1,0:T(8,128)(2,1)S(1)}, bf16[2,256,128]{2,1,0:T(8,128)(2,1)S(1)}) fusion(pred[]{:T(512)S(6)} %eq.18, bf16[2,4,256,128]{3,2,1,0:T(8,128)(2,1)} %cot_ref.1), kind=kLoop, calls=%fused_computation.3 | loop fusion | flops 131072 | bytes 524289 | tf_op jit(solution)/shard_map/jit(_where)/select_n | solution.py:381
  1.6 0.7 collective-permute-start.1
  2.3 0.0 copy-start.8
  2.3 0.0 copy-start
  2.3 0.0 copy-start.1
  2.3 0.0 copy-start.2
  2.4 2.2 %pack_early.1 = (bf16[3,4,64,128]{3,2,1,0:T(8,128)(2,1)}, bf16[3,4,64,128]{3,2,1,0:T(8,128)(2,1)}) custom-call(s32[1]{0:T(128)} %bitcast.index_ref, bf16[64,2,2048]{2,1,0:T(2,128)(2,1)} %query_ref.5, bf16[64,2,2048]{2,1,0:T(2,128)(2,1)} %key_ref.5, bf16[64,2,2048]{2,1,0:T(2,128)(2,1)} %value_ref.5), custom_call_target="tpu_custom_call" | custom-call | bytes 786432 | tf_op jit(solution)/shard_map/pack_early/pallas_call | solution.py:390
  4.6 6.7 %collective-permute-start.2 = (bf16[3,4,64,128]{3,2,1,0:T(8,128)(2,1)}, bf16[3,4,64,128]{3,2,1,0:T(8,128)(2,1)S(1)}, u32[]{:S(2)}, u32[]{:S(2)}) collective-permute-start(bf16[3,4,64,128]{3,2,1,0:T(8,128)(2,1)} %get-tuple-element.28), channel_id=1, source_target_pairs={{0,4},{1,5},{2,6},{3,7},{4,0},{5,1},{6,2},{7,3},{8,12},{9,13},{10,... | collective-permute-start | bytes 589832 | tf_op jit(solution)/shard_map/ppermute | solution.py:334
  11.3 1.4 %collective-permute-start.3 = (bf16[3,4,64,128]{3,2,1,0:T(8,128)(2,1)}, bf16[3,4,64,128]{3,2,1,0:T(8,128)(2,1)S(1)}, u32[]{:S(2)}, u32[]{:S(2)}) collective-permute-start(bf16[3,4,64,128]{3,2,1,0:T(8,128)(2,1)} %get-tuple-element.29), channel_id=1, source_target_pairs={{0,5},{1,4},{2,7},{3,6},{4,1},{5,0},{6,3},{7,2},{8,13},{9,12},{10,... | collective-permute-start | bytes 589832 | tf_op jit(solution)/shard_map/ppermute | solution.py:334
  12.8 0.0 collective-permute-done.1.far_ref.refs_0_
  12.8 0.7 copy-done.4
  13.4 3.0 %pack_late.1 = (bf16[3,4,64,128]{3,2,1,0:T(8,128)(2,1)}, bf16[3,4,64,128]{3,2,1,0:T(8,128)(2,1)}, bf16[3,4,64,128]{3,2,1,0:T(8,128)(2,1)}, bf16[3,4,64,128]{3,2,1,0:T(8,128)(2,1)}, bf16[3,4,64,128]{3,2,1,0:T(8,128)(2,1)}) custom-call(s32[1]{0:T(128)} %bitcast.index_ref, bf16[64,2,2048]{2,1,0:T(2,128)(2,1)} %query_ref.5, bf16[64,2,2048]{2,1,0:T(2,128)(2,1)} %key_ref.5, ...), custom_call_target="tpu_custom_call" | custom-call | bytes 1966080 | tf_op jit(solution)/shard_map/pack_late/pallas_call | solution.py:390
  16.5 4.1 %collective-permute-start.4 = (bf16[3,4,64,128]{3,2,1,0:T(8,128)(2,1)}, bf16[3,4,64,128]{3,2,1,0:T(8,128)(2,1)S(1)}, u32[]{:S(2)}, u32[]{:S(2)}) collective-permute-start(bf16[3,4,64,128]{3,2,1,0:T(8,128)(2,1)} %get-tuple-element.30), channel_id=1, source_target_pairs={{0,6},{1,7},{2,4},{3,5},{4,2},{5,3},{6,0},{7,1},{8,14},{9,15},{10,... | collective-permute-start | bytes 589832 | tf_op jit(solution)/shard_map/ppermute | solution.py:334
  20.5 0.0 collective-permute-start.5
  20.5 0.0 collective-permute-start.6
  20.5 9.5 %collective-permute-done.2.refs_0_ = bf16[3,4,64,128]{3,2,1,0:T(8,128)(2,1)S(1)} collective-permute-done((bf16[3,4,64,128]{3,2,1,0:T(8,128)(2,1)}, bf16[3,4,64,128]{3,2,1,0:T(8,128)(2,1)S(1)}, u32[]{:S(2)}, u32[]{:S(2)}) %collective-permute-start.2) | collective-permute-done | bytes 196640 | tf_op jit(solution)/shard_map/ppermute | solution.py:334
  30.0 2.5 %collective-permute-start.7 = (bf16[3,4,64,128]{3,2,1,0:T(8,128)(2,1)}, bf16[3,4,64,128]{3,2,1,0:T(8,128)(2,1)S(1)}, u32[]{:S(2)}, u32[]{:S(2)}) collective-permute-start(bf16[3,4,64,128]{3,2,1,0:T(8,128)(2,1)} %get-tuple-element.33), channel_id=1, source_target_pairs={{0,7},{1,6},{2,5},{3,4},{4,3},{5,2},{6,1},{7,0},{8,15},{9,14},{10,... | collective-permute-start | bytes 589832 | tf_op jit(solution)/shard_map/ppermute | solution.py:334
  32.5 7.1 %collective-permute-done.3.refs_1_ = bf16[3,4,64,128]{3,2,1,0:T(8,128)(2,1)S(1)} collective-permute-done((bf16[3,4,64,128]{3,2,1,0:T(8,128)(2,1)}, bf16[3,4,64,128]{3,2,1,0:T(8,128)(2,1)S(1)}, u32[]{:S(2)}, u32[]{:S(2)}) %collective-permute-start.3) | collective-permute-done | bytes 196640 | tf_op jit(solution)/shard_map/ppermute | solution.py:334
  39.6 0.0 collective-permute-start.8
  39.6 0.1 collective-permute-start
  39.7 0.1 fusion.2.lengths_ref
  39.8 0.0 copy-start.3
  39.8 0.4 own_chunk.1.refs_7_
  40.2 0.0 collective-permute-done.5.refs_3_
  40.2 1.6 %collective-permute-done.6.refs_4_ = bf16[3,4,64,128]{3,2,1,0:T(8,128)(2,1)S(1)} collective-permute-done((bf16[3,4,64,128]{3,2,1,0:T(8,128)(2,1)}, bf16[3,4,64,128]{3,2,1,0:T(8,128)(2,1)S(1)}, u32[]{:S(2)}, u32[]{:S(2)}) %collective-permute-start.6) | collective-permute-done | bytes 196640 | tf_op jit(solution)/shard_map/ppermute | solution.py:334
  41.8 0.0 collective-permute-done.7.refs_5_
  41.8 4.7 %collective-permute-done.8.refs_6_ = bf16[3,4,64,128]{3,2,1,0:T(8,128)(2,1)S(1)} collective-permute-done((bf16[3,4,64,128]{3,2,1,0:T(8,128)(2,1)}, bf16[3,4,64,128]{3,2,1,0:T(8,128)(2,1)S(1)}, u32[]{:S(2)}, u32[]{:S(2)}) %collective-permute-start.8) | collective-permute-done | bytes 196640 | tf_op jit(solution)/shard_map/ppermute | solution.py:334
  46.5 2.5 %attend.1 = (bf16[4,64,128]{2,1,0:T(8,128)(2,1)S(1)}, bf16[4,64,128]{2,1,0:T(8,128)(2,1)S(1)}, bf16[4,64,128]{2,1,0:T(8,128)(2,1)S(1)}, bf16[4,64,128]{2,1,0:T(8...) custom-call(s32[1]{0:T(128)} %bitcast.index_ref, ...), custom_call_target="tpu_custom_call" | custom-call | flops 536870912 | bytes 2097152 | tf_op jit(solution)/shard_map/attend/pallas_call | solution.py:437
  49.0 0.0 copy-start.7
  49.0 0.4 collective-permute-start.9
  49.3 3.4 %collective-permute-start.10 = (bf16[4,64,128]{2,1,0:T(8,128)(2,1)S(1)}, bf16[4,64,128]{2,1,0:T(8,128)(2,1)S(1)}, u32[]{:S(2)}, u32[]{:S(2)}) collective-permute-start(bf16[4,64,128]{2,1,0:T(8,128)(2,1)S(1)} %get-tuple-element.37), channel_id=1, source_target_pairs={{0,2},{1,3},{2,0},{3,1},{4,6},{5,7},{6,4},{7,5},{8,10},{9,11},{10,... | collective-permute-start | bytes 196616 | tf_op jit(solution)/shard_map/ppermute | solution.py:334
  52.7 0.2 collective-permute-start.11
  52.9 3.4 %collective-permute-start.12 = (bf16[4,64,128]{2,1,0:T(8,128)(2,1)S(1)}, bf16[4,64,128]{2,1,0:T(8,128)(2,1)S(1)}, u32[]{:S(2)}, u32[]{:S(2)}) collective-permute-start(bf16[4,64,128]{2,1,0:T(8,128)(2,1)S(1)} %get-tuple-element.39), channel_id=1, source_target_pairs={{0,4},{1,5},{2,6},{3,7},{4,0},{5,1},{6,2},{7,3},{8,12},{9,13},{10,... | collective-permute-start | bytes 196616 | tf_op jit(solution)/shard_map/ppermute | solution.py:334
  56.3 0.3 collective-permute-start.13
  56.5 2.2 %collective-permute-start.14 = (bf16[4,64,128]{2,1,0:T(8,128)(2,1)S(1)}, bf16[4,64,128]{2,1,0:T(8,128)(2,1)S(1)}, u32[]{:S(2)}, u32[]{:S(2)}) collective-permute-start(bf16[4,64,128]{2,1,0:T(8,128)(2,1)S(1)} %get-tuple-element.41), channel_id=1, source_target_pairs={{0,6},{1,7},{2,4},{3,5},{4,2},{5,3},{6,0},{7,1},{8,14},{9,15},{10,... | collective-permute-start | bytes 196616 | tf_op jit(solution)/shard_map/ppermute | solution.py:334
  58.8 2.3 %collective-permute-start.15 = (bf16[4,64,128]{2,1,0:T(8,128)(2,1)S(1)}, bf16[4,64,128]{2,1,0:T(8,128)(2,1)S(1)}, u32[]{:S(2)}, u32[]{:S(2)}) collective-permute-start(bf16[4,64,128]{2,1,0:T(8,128)(2,1)S(1)} %get-tuple-element.42), channel_id=1, source_target_pairs={{0,7},{1,6},{2,5},{3,4},{4,3},{5,2},{6,1},{7,0},{8,15},{9,14},{10,... | collective-permute-start | bytes 196616 | tf_op jit(solution)/shard_map/ppermute | solution.py:334
  61.0 0.3 turn_cotangent.1.turned_ref
  61.3 0.0 copy-start.6
  61.3 1.8 %collective-permute-done.12.refs_4_ = bf16[4,64,128]{2,1,0:T(8,128)(2,1)S(1)} collective-permute-done((bf16[4,64,128]{2,1,0:T(8,128)(2,1)S(1)}, bf16[4,64,128]{2,1,0:T(8,128)(2,1)S(1)}, u32[]{:S(2)}, u32[]{:S(2)}) %collective-permute-start.12) | collective-permute-done | bytes 65568 | tf_op jit(solution)/shard_map/ppermute | solution.py:334
  63.1 1.9 %collective-permute-done.13.refs_5_ = bf16[4,64,128]{2,1,0:T(8,128)(2,1)S(1)} collective-permute-done((bf16[4,64,128]{2,1,0:T(8,128)(2,1)S(1)}, bf16[4,64,128]{2,1,0:T(8,128)(2,1)S(1)}, u32[]{:S(2)}, u32[]{:S(2)}) %collective-permute-start.13) | collective-permute-done | bytes 65568 | tf_op jit(solution)/shard_map/ppermute | solution.py:334
  65.1 0.8 collective-permute-done.15.refs_7_
  65.8 3.1 %norm_and_gradient.1 = (bf16[2,4,256,128]{3,2,1,0:T(8,128)(2,1)S(1)}, bf16[2,256,128]{2,1,0:T(8,128)(2,1)S(1)}, bf16[2,256,128]{2,1,0:T(8,128)(2,1)S(1)}, f32[576,128]{1,0:T(8,128)S(1)}, f32[576,128]{1,0:T(8,128)S(1)}) custom-call(s32[2]{0:T(128)S(1)} %copy-done.8, s32[1]{0:T(128)} %bitcast.index_ref, s32[1]{0:T(128)} %bitcast.1.core_ref, ...), custom_call_target="tpu_custom_call" | custom-call | flops 603979776 | bytes 2097152 | tf_op jit(solution)/shard_map/norm_and_gradient/pallas_call | solution.py:460
  68.9 0.1 collective-permute-start.18
  69.0 1.4 %collective-permute-start.16 = (bf16[2,256,128]{2,1,0:T(8,128)(2,1)S(1)}, bf16[2,256,128]{2,1,0:T(8,128)(2,1)S(1)}, u32[]{:S(2)}, u32[]{:S(2)}) collective-permute-start(bf16[2,256,128]{2,1,0:T(8,128)(2,1)S(1)} %get-tuple-element.44), channel_id=1, source_target_pairs={{0,1},{1,0},{2,3},{3,2},{4,5},{5,4},{6,7},{7,6},{8,9},{9,8},{10,11... | collective-permute-start | bytes 393224 | tf_op jit(solution)/shard_map/ppermute | solution.py:334
  70.4 0.8 collective-permute-start.17
  71.3 5.3 %collective-permute-start.19 = (bf16[144,128]{1,0:T(8,128)(2,1)S(1)}, bf16[144,128]{1,0:T(8,128)(2,1)S(1)}, u32[]{:S(2)}, u32[]{:S(2)}) collective-permute-start(bf16[144,128]{1,0:T(8,128)(2,1)S(1)} %get-tuple-element.50), channel_id=1, source_target_pairs={{0,1},{1,0},{2,3},{3,2},{4,5},{5,4},{6,7},{7,6},{8,9},{9,8},{10,11... | collective-permute-start | bytes 110600 | tf_op jit(solution)/shard_map/ppermute | solution.py:352
  76.6 1.4 %collective-permute-start.20 = (bf16[144,128]{1,0:T(8,128)(2,1)S(1)}, bf16[144,128]{1,0:T(8,128)(2,1)S(1)}, u32[]{:S(2)}, u32[]{:S(2)}) collective-permute-start(bf16[144,128]{1,0:T(8,128)(2,1)S(1)} %get-tuple-element.51), channel_id=1, source_target_pairs={{0,16},{1,17},{2,18},{3,19},{4,20},{5,21},{6,22},{7,23},{8,24},{9,... | collective-permute-start | bytes 110600 | tf_op jit(solution)/shard_map/ppermute | solution.py:352
  78.0 0.1 collective-permute-start.21
  78.1 0.4 collective-permute-done.19.refs_1_
  78.5 2.0 %collective-permute-done.20.refs_2_ = bf16[144,128]{1,0:T(8,128)(2,1)S(1)} collective-permute-done((bf16[144,128]{1,0:T(8,128)(2,1)S(1)}, bf16[144,128]{1,0:T(8,128)(2,1)S(1)}, u32[]{:S(2)}, u32[]{:S(2)}) %collective-permute-start.20) | collective-permute-done | bytes 36896 | tf_op jit(solution)/shard_map/ppermute | solution.py:352
  80.5 2.3 %collective-permute-done.21.refs_3_ = bf16[144,128]{1,0:T(8,128)(2,1)S(1)} collective-permute-done((bf16[144,128]{1,0:T(8,128)(2,1)S(1)}, bf16[144,128]{1,0:T(8,128)(2,1)S(1)}, u32[]{:S(2)}, u32[]{:S(2)}) %collective-permute-start.21) | collective-permute-done | bytes 36896 | tf_op jit(solution)/shard_map/ppermute | solution.py:352
  82.9 0.7 collective-permute-start.24
  83.5 1.3 %collective-permute-start.23 = (bf16[144,128]{1,0:T(8,128)(2,1)S(1)}, bf16[144,128]{1,0:T(8,128)(2,1)S(1)}, u32[]{:S(2)}, u32[]{:S(2)}) collective-permute-start(bf16[144,128]{1,0:T(8,128)(2,1)S(1)} %sum_chips.1.refs_0_), channel_id=1, source_target_pairs={{0,4},{1,5},{2,6},{3,7},{4,0},{5,1},{6,2},{7,3},{8,12},{9,13},{10,... | collective-permute-start | bytes 110600 | tf_op jit(solution)/shard_map/ppermute | solution.py:334
  84.8 2.5 %collective-permute-start.22 = (bf16[144,128]{1,0:T(8,128)(2,1)S(1)}, bf16[144,128]{1,0:T(8,128)(2,1)S(1)}, u32[]{:S(2)}, u32[]{:S(2)}) collective-permute-start(bf16[144,128]{1,0:T(8,128)(2,1)S(1)} %sum_chips.1.refs_0_), channel_id=1, source_target_pairs={{0,2},{1,3},{2,0},{3,1},{4,6},{5,7},{6,4},{7,5},{8,10},{9,11},{10,... | collective-permute-start | bytes 110600 | tf_op jit(solution)/shard_map/ppermute | solution.py:334
  87.3 2.2 %decode.1 = (bf16[2,4,256,128]{3,2,1,0:T(8,128)(2,1)}, f32[8,128]{1,0:T(8,128)S(1)}) custom-call(s32[1]{0:T(128)} %bitcast.index_ref, bf16[2,4,256,128]{3,2,1,0:T(8,128)(2,1)S(1)} %get-tuple-element.43.image_ref, bf16[2,256,128]{2,1,0:T(8,128)(2,1)S(1)} %collective-permute-done.16.near_ref, bf16[2,256,128]{2,1,0:T(8,128)(2,1)S(1)} %collective-permute-done.17.far_ref, ...), custom_call_target="tpu_custom_call" | custom-call | flops 603979776 | bytes 1048576 | tf_op jit(solution)/shard_map/decode/pallas_call | solution.py:498
  89.6 1.0 %collective-permute-start.27 = (bf16[144,128]{1,0:T(8,128)(2,1)S(1)}, bf16[144,128]{1,0:T(8,128)(2,1)S(1)}, u32[]{:S(2)}, u32[]{:S(2)}) collective-permute-start(bf16[144,128]{1,0:T(8,128)(2,1)S(1)} %sum_planes.1.refs_0_), channel_id=1, source_target_pairs={{0,17},{1,16},{2,19},{3,18},{4,21},{5,20},{6,23},{7,22},{8,25},{9,... | collective-permute-start | bytes 110600 | tf_op jit(solution)/shard_map/ppermute | solution.py:352
  90.6 1.3 %collective-permute-start.26 = (bf16[144,128]{1,0:T(8,128)(2,1)S(1)}, bf16[144,128]{1,0:T(8,128)(2,1)S(1)}, u32[]{:S(2)}, u32[]{:S(2)}) collective-permute-start(bf16[144,128]{1,0:T(8,128)(2,1)S(1)} %sum_planes.1.refs_0_), channel_id=1, source_target_pairs={{0,16},{1,17},{2,18},{3,19},{4,20},{5,21},{6,22},{7,23},{8,24},{9,... | collective-permute-start | bytes 110600 | tf_op jit(solution)/shard_map/ppermute | solution.py:352
  91.9 1.2 %collective-permute-start.25 = (bf16[144,128]{1,0:T(8,128)(2,1)S(1)}, bf16[144,128]{1,0:T(8,128)(2,1)S(1)}, u32[]{:S(2)}, u32[]{:S(2)}) collective-permute-start(bf16[144,128]{1,0:T(8,128)(2,1)S(1)} %sum_planes.1.refs_0_), channel_id=1, source_target_pairs={{0,1},{1,0},{2,3},{3,2},{4,5},{5,4},{6,7},{7,6},{8,9},{9,8},{10,11... | collective-permute-start | bytes 110600 | tf_op jit(solution)/shard_map/ppermute | solution.py:352
  93.1 1.4 %collective-permute-done.27.refs_3_ = bf16[144,128]{1,0:T(8,128)(2,1)S(1)} collective-permute-done((bf16[144,128]{1,0:T(8,128)(2,1)S(1)}, bf16[144,128]{1,0:T(8,128)(2,1)S(1)}, u32[]{:S(2)}, u32[]{:S(2)}) %collective-permute-start.27) | collective-permute-done | bytes 36896 | tf_op jit(solution)/shard_map/ppermute | solution.py:352
  94.5 0.4 collective-permute-done.26.refs_2_
  94.9 1.0 collective-permute-done.25.refs_1_
  95.9 0.1 collective-permute-start.28
  96.0 1.4 %collective-permute-done.28.other_ref = bf16[576,128]{1,0:T(8,128)(2,1)S(1)} collective-permute-done((bf16[576,128]{1,0:T(8,128)(2,1)S(1)}, bf16[576,128]{1,0:T(8,128)(2,1)S(1)}, u32[]{:S(2)}, u32[]{:S(2)}) %collective-permute-start.28) | collective-permute-done | bytes 147488 | tf_op jit(solution)/shard_map/ppermute | solution.py:356
  97.3 0.9 spread_sums.1
  (27 shorter events, 0.2 us)
Async XLA Ops:
  1.6 11.1 %collective-permute-start.1 = (bf16[2,256,128]{2,1,0:T(8,128)(2,1)S(1)}, bf16[2,256,128]{2,1,0:T(8,128)(2,1)S(1)}, u32[]{:S(2)}, u32[]{:S(2)}) collective-permute-start(bf16[2,256,128]{2,1,0:T(8,128)(2,1)S(1)} %get-tuple-element.54), channel_id=1, source_target_pairs={{1,2},{3,4},{5,6},{2,1},{4,3},{6,5},{9,10},{11,12},{13,14},{10,9},... | collective-permute-start | bytes 393224 | tf_op jit(solution)/shard_map/ppermute | solution.py:382
  2.3 37.4 %copy-start.8 = (s32[2]{0:T(128)S(1)}, s32[2]{0:T(128)}, u32[]{:S(2)}) copy-start(s32[2]{0:T(128)} %lengths_ref.1) | copy-start | bytes 28
  2.3 37.5 %copy-start = (bf16[64,2,2048]{2,1,0:T(2,128)(2,1)S(1)}, bf16[64,2,2048]{2,1,0:T(2,128)(2,1)}, u32[]{:S(2)}) copy-start(bf16[64,2,2048]{2,1,0:T(2,128)(2,1)} %query_ref.5) | copy-start | bytes 1572868
  2.3 37.5 %copy-start.1 = (bf16[64,2,2048]{2,1,0:T(2,128)(2,1)S(1)}, bf16[64,2,2048]{2,1,0:T(2,128)(2,1)}, u32[]{:S(2)}) copy-start(bf16[64,2,2048]{2,1,0:T(2,128)(2,1)} %key_ref.5) | copy-start | bytes 1572868
  2.3 37.4 %copy-start.2 = (bf16[64,2,2048]{2,1,0:T(2,128)(2,1)S(1)}, bf16[64,2,2048]{2,1,0:T(2,128)(2,1)}, u32[]{:S(2)}) copy-start(bf16[64,2,2048]{2,1,0:T(2,128)(2,1)} %value_ref.5) | copy-start | bytes 1572868
  4.6 25.4 %collective-permute-start.2 = (bf16[3,4,64,128]{3,2,1,0:T(8,128)(2,1)}, bf16[3,4,64,128]{3,2,1,0:T(8,128)(2,1)S(1)}, u32[]{:S(2)}, u32[]{:S(2)}) collective-permute-start(bf16[3,4,64,128]{3,2,1,0:T(8,128)(2,1)} %get-tuple-element.28), channel_id=1, source_target_pairs={{0,4},{1,5},{2,6},{3,7},{4,0},{5,1},{6,2},{7,3},{8,12},{9,13},{10,... | collective-permute-start | bytes 589832 | tf_op jit(solution)/shard_map/ppermute | solution.py:334
  11.3 28.3 %collective-permute-start.3 = (bf16[3,4,64,128]{3,2,1,0:T(8,128)(2,1)}, bf16[3,4,64,128]{3,2,1,0:T(8,128)(2,1)S(1)}, u32[]{:S(2)}, u32[]{:S(2)}) collective-permute-start(bf16[3,4,64,128]{3,2,1,0:T(8,128)(2,1)} %get-tuple-element.29), channel_id=1, source_target_pairs={{0,5},{1,4},{2,7},{3,6},{4,1},{5,0},{6,3},{7,2},{8,13},{9,12},{10,... | collective-permute-start | bytes 589832 | tf_op jit(solution)/shard_map/ppermute | solution.py:334
  12.8 0.7 copy-start.4
  16.5 23.1 %collective-permute-start.4 = (bf16[3,4,64,128]{3,2,1,0:T(8,128)(2,1)}, bf16[3,4,64,128]{3,2,1,0:T(8,128)(2,1)S(1)}, u32[]{:S(2)}, u32[]{:S(2)}) collective-permute-start(bf16[3,4,64,128]{3,2,1,0:T(8,128)(2,1)} %get-tuple-element.30), channel_id=1, source_target_pairs={{0,6},{1,7},{2,4},{3,5},{4,2},{5,3},{6,0},{7,1},{8,14},{9,15},{10,... | collective-permute-start | bytes 589832 | tf_op jit(solution)/shard_map/ppermute | solution.py:334
  20.5 19.7 %collective-permute-start.5 = (bf16[3,4,64,128]{3,2,1,0:T(8,128)(2,1)}, bf16[3,4,64,128]{3,2,1,0:T(8,128)(2,1)S(1)}, u32[]{:S(2)}, u32[]{:S(2)}) collective-permute-start(bf16[3,4,64,128]{3,2,1,0:T(8,128)(2,1)} %get-tuple-element.31), channel_id=1, source_target_pairs={{0,1},{1,0},{2,3},{3,2},{4,5},{5,4},{6,7},{7,6},{8,9},{9,8},{10,11... | collective-permute-start | bytes 589832 | tf_op jit(solution)/shard_map/ppermute | solution.py:334
  20.5 21.3 %collective-permute-start.6 = (bf16[3,4,64,128]{3,2,1,0:T(8,128)(2,1)}, bf16[3,4,64,128]{3,2,1,0:T(8,128)(2,1)S(1)}, u32[]{:S(2)}, u32[]{:S(2)}) collective-permute-start(bf16[3,4,64,128]{3,2,1,0:T(8,128)(2,1)} %get-tuple-element.32), channel_id=1, source_target_pairs={{0,2},{1,3},{2,0},{3,1},{4,6},{5,7},{6,4},{7,5},{8,10},{9,11},{10,... | collective-permute-start | bytes 589832 | tf_op jit(solution)/shard_map/ppermute | solution.py:334
  30.0 11.8 %collective-permute-start.7 = (bf16[3,4,64,128]{3,2,1,0:T(8,128)(2,1)}, bf16[3,4,64,128]{3,2,1,0:T(8,128)(2,1)S(1)}, u32[]{:S(2)}, u32[]{:S(2)}) collective-permute-start(bf16[3,4,64,128]{3,2,1,0:T(8,128)(2,1)} %get-tuple-element.33), channel_id=1, source_target_pairs={{0,7},{1,6},{2,5},{3,4},{4,3},{5,2},{6,1},{7,0},{8,15},{9,14},{10,... | collective-permute-start | bytes 589832 | tf_op jit(solution)/shard_map/ppermute | solution.py:334
  39.6 6.9 %collective-permute-start.8 = (bf16[3,4,64,128]{3,2,1,0:T(8,128)(2,1)}, bf16[3,4,64,128]{3,2,1,0:T(8,128)(2,1)S(1)}, u32[]{:S(2)}, u32[]{:S(2)}) collective-permute-start(bf16[3,4,64,128]{3,2,1,0:T(8,128)(2,1)} %get-tuple-element.34), channel_id=1, source_target_pairs={{0,3},{1,2},{2,1},{3,0},{4,7},{5,6},{6,5},{7,4},{8,11},{9,10},{10,... | collective-permute-start | bytes 589832 | tf_op jit(solution)/shard_map/ppermute | solution.py:334
  39.6 16.7 %collective-permute-start = (bf16[2,256,128]{2,1,0:T(8,128)(2,1)S(1)}, bf16[2,256,128]{2,1,0:T(8,128)(2,1)S(1)}, u32[]{:S(2)}, u32[]{:S(2)}) collective-permute-start(bf16[2,256,128]{2,1,0:T(8,128)(2,1)S(1)} %get-tuple-element.55), channel_id=1, source_target_pairs={{0,1},{1,0},{2,3},{3,2},{4,5},{5,4},{6,7},{7,6},{8,9},{9,8},{10,11... | collective-permute-start | bytes 393224 | tf_op jit(solution)/shard_map/ppermute | solution.py:334
  39.8 21.2 %copy-start.3 = (bf16[2,4,256,128]{3,2,1,0:T(8,128)(2,1)S(1)}, bf16[2,4,256,128]{3,2,1,0:T(8,128)(2,1)}, u32[]{:S(2)}) copy-start(bf16[2,4,256,128]{3,2,1,0:T(8,128)(2,1)} %cot_ref.1) | copy-start | bytes 1572868
  39.8 21.2 %copy-start.5 = (bf16[2,256,128]{2,1,0:T(8,128)(2,1)S(1)}, bf16[2,256,128]{2,1,0:T(8,128)(2,1)}, u32[]{:S(2)}) copy-start(bf16[2,256,128]{2,1,0:T(8,128)(2,1)} %copy-done.4) | copy-start | bytes 393220
  49.0 16.9 %copy-start.7 = (f32[2048]{0:T(1024)S(1)}, f32[2048]{0:T(1024)}, u32[]{:S(2)}) copy-start(f32[2048]{0:T(1024)} %param.11) | copy-start | bytes 24580
  49.0 7.6 %collective-permute-start.9 = (bf16[4,64,128]{2,1,0:T(8,128)(2,1)S(1)}, bf16[4,64,128]{2,1,0:T(8,128)(2,1)S(1)}, u32[]{:S(2)}, u32[]{:S(2)}) collective-permute-start(bf16[4,64,128]{2,1,0:T(8,128)(2,1)S(1)} %get-tuple-element.36), channel_id=1, source_target_pairs={{0,1},{1,0},{2,3},{3,2},{4,5},{5,4},{6,7},{7,6},{8,9},{9,8},{10,11... | collective-permute-start | bytes 196616 | tf_op jit(solution)/shard_map/ppermute | solution.py:334
  49.3 9.4 %collective-permute-start.10 = (bf16[4,64,128]{2,1,0:T(8,128)(2,1)S(1)}, bf16[4,64,128]{2,1,0:T(8,128)(2,1)S(1)}, u32[]{:S(2)}, u32[]{:S(2)}) collective-permute-start(bf16[4,64,128]{2,1,0:T(8,128)(2,1)S(1)} %get-tuple-element.37), channel_id=1, source_target_pairs={{0,2},{1,3},{2,0},{3,1},{4,6},{5,7},{6,4},{7,5},{8,10},{9,11},{10,... | collective-permute-start | bytes 196616 | tf_op jit(solution)/shard_map/ppermute | solution.py:334
  52.7 8.6 %collective-permute-start.11 = (bf16[4,64,128]{2,1,0:T(8,128)(2,1)S(1)}, bf16[4,64,128]{2,1,0:T(8,128)(2,1)S(1)}, u32[]{:S(2)}, u32[]{:S(2)}) collective-permute-start(bf16[4,64,128]{2,1,0:T(8,128)(2,1)S(1)} %get-tuple-element.38), channel_id=1, source_target_pairs={{0,3},{1,2},{2,1},{3,0},{4,7},{5,6},{6,5},{7,4},{8,11},{9,10},{10,... | collective-permute-start | bytes 196616 | tf_op jit(solution)/shard_map/ppermute | solution.py:334
  52.9 10.2 %collective-permute-start.12 = (bf16[4,64,128]{2,1,0:T(8,128)(2,1)S(1)}, bf16[4,64,128]{2,1,0:T(8,128)(2,1)S(1)}, u32[]{:S(2)}, u32[]{:S(2)}) collective-permute-start(bf16[4,64,128]{2,1,0:T(8,128)(2,1)S(1)} %get-tuple-element.39), channel_id=1, source_target_pairs={{0,4},{1,5},{2,6},{3,7},{4,0},{5,1},{6,2},{7,3},{8,12},{9,13},{10,... | collective-permute-start | bytes 196616 | tf_op jit(solution)/shard_map/ppermute | solution.py:334
  56.3 8.8 %collective-permute-start.13 = (bf16[4,64,128]{2,1,0:T(8,128)(2,1)S(1)}, bf16[4,64,128]{2,1,0:T(8,128)(2,1)S(1)}, u32[]{:S(2)}, u32[]{:S(2)}) collective-permute-start(bf16[4,64,128]{2,1,0:T(8,128)(2,1)S(1)} %get-tuple-element.40), channel_id=1, source_target_pairs={{0,5},{1,4},{2,7},{3,6},{4,1},{5,0},{6,3},{7,2},{8,13},{9,12},{10,... | collective-permute-start | bytes 196616 | tf_op jit(solution)/shard_map/ppermute | solution.py:334
  56.5 8.5 %collective-permute-start.14 = (bf16[4,64,128]{2,1,0:T(8,128)(2,1)S(1)}, bf16[4,64,128]{2,1,0:T(8,128)(2,1)S(1)}, u32[]{:S(2)}, u32[]{:S(2)}) collective-permute-start(bf16[4,64,128]{2,1,0:T(8,128)(2,1)S(1)} %get-tuple-element.41), channel_id=1, source_target_pairs={{0,6},{1,7},{2,4},{3,5},{4,2},{5,3},{6,0},{7,1},{8,14},{9,15},{10,... | collective-permute-start | bytes 196616 | tf_op jit(solution)/shard_map/ppermute | solution.py:334
  58.8 7.1 %collective-permute-start.15 = (bf16[4,64,128]{2,1,0:T(8,128)(2,1)S(1)}, bf16[4,64,128]{2,1,0:T(8,128)(2,1)S(1)}, u32[]{:S(2)}, u32[]{:S(2)}) collective-permute-start(bf16[4,64,128]{2,1,0:T(8,128)(2,1)S(1)} %get-tuple-element.42), channel_id=1, source_target_pairs={{0,7},{1,6},{2,5},{3,4},{4,3},{5,2},{6,1},{7,0},{8,15},{9,14},{10,... | collective-permute-start | bytes 196616 | tf_op jit(solution)/shard_map/ppermute | solution.py:334
  61.3 26.0 %copy-start.6 = (bf16[9,128,128]{2,1,0:T(8,128)(2,1)S(1)}, bf16[9,128,128]{2,1,0:T(8,128)(2,1)}, u32[]{:S(2)}) copy-start(bf16[9,128,128]{2,1,0:T(8,128)(2,1)} %param.12) | copy-start | bytes 884740
  68.9 2.4 %collective-permute-start.18 = (f32[576,128]{1,0:T(8,128)S(1)}, f32[576,128]{1,0:T(8,128)S(1)}, u32[]{:S(2)}, u32[]{:S(2)}) collective-permute-start(f32[576,128]{1,0:T(8,128)S(1)} %get-tuple-element.48), channel_id=1, source_target_pairs={{0,8},{8,0},{16,24},{24,16},{1,9},{9,1},{17,25},{25,17},{2,10},{10... | collective-permute-start | bytes 884744 | tf_op jit(solution)/shard_map/ppermute | solution.py:356
  69.0 18.3 %collective-permute-start.16 = (bf16[2,256,128]{2,1,0:T(8,128)(2,1)S(1)}, bf16[2,256,128]{2,1,0:T(8,128)(2,1)S(1)}, u32[]{:S(2)}, u32[]{:S(2)}) collective-permute-start(bf16[2,256,128]{2,1,0:T(8,128)(2,1)S(1)} %get-tuple-element.44), channel_id=1, source_target_pairs={{0,1},{1,0},{2,3},{3,2},{4,5},{5,4},{6,7},{7,6},{8,9},{9,8},{10,11... | collective-permute-start | bytes 393224 | tf_op jit(solution)/shard_map/ppermute | solution.py:334
  70.4 16.9 %collective-permute-start.17 = (bf16[2,256,128]{2,1,0:T(8,128)(2,1)S(1)}, bf16[2,256,128]{2,1,0:T(8,128)(2,1)S(1)}, u32[]{:S(2)}, u32[]{:S(2)}) collective-permute-start(bf16[2,256,128]{2,1,0:T(8,128)(2,1)S(1)} %get-tuple-element.45), channel_id=1, source_target_pairs={{1,2},{3,4},{5,6},{2,1},{4,3},{6,5},{9,10},{11,12},{13,14},{10,9},... | collective-permute-start | bytes 393224 | tf_op jit(solution)/shard_map/ppermute | solution.py:486
  71.3 7.2 %collective-permute-start.19 = (bf16[144,128]{1,0:T(8,128)(2,1)S(1)}, bf16[144,128]{1,0:T(8,128)(2,1)S(1)}, u32[]{:S(2)}, u32[]{:S(2)}) collective-permute-start(bf16[144,128]{1,0:T(8,128)(2,1)S(1)} %get-tuple-element.50), channel_id=1, source_target_pairs={{0,1},{1,0},{2,3},{3,2},{4,5},{5,4},{6,7},{7,6},{8,9},{9,8},{10,11... | collective-permute-start | bytes 110600 | tf_op jit(solution)/shard_map/ppermute | solution.py:352
  76.6 4.0 %collective-permute-start.20 = (bf16[144,128]{1,0:T(8,128)(2,1)S(1)}, bf16[144,128]{1,0:T(8,128)(2,1)S(1)}, u32[]{:S(2)}, u32[]{:S(2)}) collective-permute-start(bf16[144,128]{1,0:T(8,128)(2,1)S(1)} %get-tuple-element.51), channel_id=1, source_target_pairs={{0,16},{1,17},{2,18},{3,19},{4,20},{5,21},{6,22},{7,23},{8,24},{9,... | collective-permute-start | bytes 110600 | tf_op jit(solution)/shard_map/ppermute | solution.py:352
  78.0 4.9 %collective-permute-start.21 = (bf16[144,128]{1,0:T(8,128)(2,1)S(1)}, bf16[144,128]{1,0:T(8,128)(2,1)S(1)}, u32[]{:S(2)}, u32[]{:S(2)}) collective-permute-start(bf16[144,128]{1,0:T(8,128)(2,1)S(1)} %get-tuple-element.52), channel_id=1, source_target_pairs={{0,17},{1,16},{2,19},{3,18},{4,21},{5,20},{6,23},{7,22},{8,25},{9,... | collective-permute-start | bytes 110600 | tf_op jit(solution)/shard_map/ppermute | solution.py:352
  82.9 6.7 %collective-permute-start.24 = (bf16[144,128]{1,0:T(8,128)(2,1)S(1)}, bf16[144,128]{1,0:T(8,128)(2,1)S(1)}, u32[]{:S(2)}, u32[]{:S(2)}) collective-permute-start(bf16[144,128]{1,0:T(8,128)(2,1)S(1)} %sum_chips.1.refs_0_), channel_id=1, source_target_pairs={{0,6},{1,7},{2,4},{3,5},{4,2},{5,3},{6,0},{7,1},{8,14},{9,15},{10,... | collective-permute-start | bytes 110600 | tf_op jit(solution)/shard_map/ppermute | solution.py:334
  83.5 6.0 %collective-permute-start.23 = (bf16[144,128]{1,0:T(8,128)(2,1)S(1)}, bf16[144,128]{1,0:T(8,128)(2,1)S(1)}, u32[]{:S(2)}, u32[]{:S(2)}) collective-permute-start(bf16[144,128]{1,0:T(8,128)(2,1)S(1)} %sum_chips.1.refs_0_), channel_id=1, source_target_pairs={{0,4},{1,5},{2,6},{3,7},{4,0},{5,1},{6,2},{7,3},{8,12},{9,13},{10,... | collective-permute-start | bytes 110600 | tf_op jit(solution)/shard_map/ppermute | solution.py:334
  84.8 4.7 %collective-permute-start.22 = (bf16[144,128]{1,0:T(8,128)(2,1)S(1)}, bf16[144,128]{1,0:T(8,128)(2,1)S(1)}, u32[]{:S(2)}, u32[]{:S(2)}) collective-permute-start(bf16[144,128]{1,0:T(8,128)(2,1)S(1)} %sum_chips.1.refs_0_), channel_id=1, source_target_pairs={{0,2},{1,3},{2,0},{3,1},{4,6},{5,7},{6,4},{7,5},{8,10},{9,11},{10,... | collective-permute-start | bytes 110600 | tf_op jit(solution)/shard_map/ppermute | solution.py:334
  89.6 5.0 %collective-permute-start.27 = (bf16[144,128]{1,0:T(8,128)(2,1)S(1)}, bf16[144,128]{1,0:T(8,128)(2,1)S(1)}, u32[]{:S(2)}, u32[]{:S(2)}) collective-permute-start(bf16[144,128]{1,0:T(8,128)(2,1)S(1)} %sum_planes.1.refs_0_), channel_id=1, source_target_pairs={{0,17},{1,16},{2,19},{3,18},{4,21},{5,20},{6,23},{7,22},{8,25},{9,... | collective-permute-start | bytes 110600 | tf_op jit(solution)/shard_map/ppermute | solution.py:352
  90.6 4.3 %collective-permute-start.26 = (bf16[144,128]{1,0:T(8,128)(2,1)S(1)}, bf16[144,128]{1,0:T(8,128)(2,1)S(1)}, u32[]{:S(2)}, u32[]{:S(2)}) collective-permute-start(bf16[144,128]{1,0:T(8,128)(2,1)S(1)} %sum_planes.1.refs_0_), channel_id=1, source_target_pairs={{0,16},{1,17},{2,18},{3,19},{4,20},{5,21},{6,22},{7,23},{8,24},{9,... | collective-permute-start | bytes 110600 | tf_op jit(solution)/shard_map/ppermute | solution.py:352
  91.9 4.0 %collective-permute-start.25 = (bf16[144,128]{1,0:T(8,128)(2,1)S(1)}, bf16[144,128]{1,0:T(8,128)(2,1)S(1)}, u32[]{:S(2)}, u32[]{:S(2)}) collective-permute-start(bf16[144,128]{1,0:T(8,128)(2,1)S(1)} %sum_planes.1.refs_0_), channel_id=1, source_target_pairs={{0,1},{1,0},{2,3},{3,2},{4,5},{5,4},{6,7},{7,6},{8,9},{9,8},{10,11... | collective-permute-start | bytes 110600 | tf_op jit(solution)/shard_map/ppermute | solution.py:352
  95.9 1.4 %collective-permute-start.28 = (bf16[576,128]{1,0:T(8,128)(2,1)S(1)}, bf16[576,128]{1,0:T(8,128)(2,1)S(1)}, u32[]{:S(2)}, u32[]{:S(2)}) collective-permute-start(bf16[576,128]{1,0:T(8,128)(2,1)S(1)} %join_chips.1.own_ref), channel_id=1, source_target_pairs={{0,8},{8,0},{16,24},{24,16},{1,9},{9,1},{17,25},{25,17},{2,10},{10... | collective-permute-start | bytes 442376 | tf_op jit(solution)/shard_map/ppermute | solution.py:356

commit v14 on v12

--- a/solution.py
+++ b/solution.py
@@ -55,7 +55,6 @@
 
 
 def pack_kernel(distances, regions, per_device, index_ref, query_ref, key_ref, value_ref, *refs):
-    refs = refs[-len(distances) - 4 :]
     held, ready, load_sems, store_sems = refs[-4:]
     width = query_ref.shape[2] // HEADS
     loads = []
@@ -82,8 +81,22 @@
 
 
 def own_kernel(
-    regions, per_device, index_ref, query_ref, key_ref, value_ref, out_ref, held, sems
+    regions,
+    per_device,
+    index_ref,
+    query_ref,
+    key_ref,
+    value_ref,
+    near_ref,
+    far_ref,
+    out_ref,
+    near_out_ref,
+    far_out_ref,
+    held,
+    sems,
 ):
+    near_out_ref[...] = near_ref[...]
+    far_out_ref[...] = far_ref[...]
     width = out_ref.shape[3]
     owner, columns = columns_of(index_ref[0], 0, regions, per_device, width)
     loads = []
@@ -312,12 +325,13 @@
         ref[...] = total[rows, :].astype(jnp.bfloat16)
 
 
-def sum_kernel(count, factor, *refs):
-    total = add_pairs([ref[...].astype(jnp.float32) for ref in refs[:count]])
+def sum_kernel(factor, *refs):
+    total = add_pairs([ref[...].astype(jnp.float32) for ref in refs[:-1]])
     refs[-1][...] = (total * factor).astype(jnp.bfloat16)
 
 
-def join_kernel(quad_ref, *refs):
+def join_kernel(quad_ref, done_ref, *refs):
+    del done_ref
     for distance, ref in enumerate(refs[:-1]):
         rows = rows_at(lax.bitwise_xor(quad_ref[0], distance), ref.shape[0])
         refs[-1][rows, :] = ref[...]
@@ -379,18 +393,18 @@
     index = seq_index.reshape(1)
     odd = lax.bitwise_and(seq_index, 1) == 1
     cot_far = jnp.where(odd, cotangent[:, PATCH - 1], cotangent[:, 0])
-    cot_far = lax.ppermute(cot_far, "seq", far_pairs)
+    cot_near = jnp.where(odd, cotangent[:, 0], cotangent[:, PATCH - 1])
     half = seq_count // 2
     early = [2, half, half + 1]
     late = [distance for distance in range(1, seq_count) if distance not in early]
     span = max(1, per_device // regions) * width
 
-    def pack(name, distances, *after):
+    def pack(name, distances):
         return call(
             functools.partial(pack_kernel, distances, regions, per_device),
             name,
             [chunk_shape] * len(distances),
-            [SMEM()] + [HBM()] * 3 + [ANY()] * len(after),
+            [SMEM()] + [HBM()] * 3,
             out_specs=[HBM()] * len(distances),
             scratch=[
                 pltpu.VMEM((len(distances), 3, tokens, regions, span), jnp.bfloat16),
@@ -400,27 +414,27 @@
             ],
             moved=4 * len(distances) * chunk_shape.size,
             grant=VMEM_WHOLE,
-        )(index, query_rows, key_rows, value_rows, *after)
+        )(index, query_rows, key_rows, value_rows)
 
     packed = {}
     for distance, chunk in zip(early, pack("pack_early", early)):
         packed[distance] = trade(chunk, distance)
-    for distance, chunk in zip(late, pack("pack_late", late, cot_far)):
+    for distance, chunk in zip(late, pack("pack_late", late)):
         packed[distance] = trade(chunk, distance)
     order = list(range(1, seq_count)) + [0]
-    packed[0] = call(
+    packed[0], cot_near, cot_far = call(
         functools.partial(own_kernel, regions, per_device),
         "own_chunk",
-        chunk_shape,
-        [SMEM()] + [HBM()] * 3,
+        [chunk_shape, edge_shape, edge_shape],
+        [SMEM()] + [HBM()] * 3 + [VMEM()] * 2,
         scratch=[
             pltpu.VMEM((3, tokens, regions, span), jnp.bfloat16),
             pltpu.SemaphoreType.DMA((3,)),
         ],
         moved=12 * chunk_shape.size,
-    )(index, query_rows, key_rows, value_rows)
-    cot_near = jnp.where(odd, cotangent[:, 0], cotangent[:, PATCH - 1])
+    )(index, query_rows, key_rows, value_rows, cot_near, cot_far)
     cot_near = trade(cot_near, 1)
+    cot_far = lax.ppermute(cot_far, "seq", far_pairs)
 
     items = seq_index * per_device + jnp.arange(per_device, dtype=jnp.int32)
     item_lengths = jnp.sum(
@@ -485,7 +499,7 @@
     far = lax.ppermute(far, "seq", far_pairs)
     distances = range(1, quad_size)
     plane_sum = call(
-        functools.partial(sum_kernel, quad_size, 1.0),
+        functools.partial(sum_kernel, 1.0),
         "sum_chips",
         chunk_shape,
         [VMEM()] * quad_size,
@@ -507,19 +521,19 @@
         moved=2 * local_bytes,
     )(index, image, near, far, conv_weight.reshape(3, 3 * width, width))
     total = call(
-        functools.partial(sum_kernel, len(plane_sums), 1.0 / math.sqrt(PATCH * columns)),
+        functools.partial(sum_kernel, 1.0 / math.sqrt(PATCH * columns)),
         "sum_planes",
         chunk_shape,
-        [VMEM()] * len(plane_sums) + [ANY()],
+        [VMEM()] * len(plane_sums),
         moved=chunk_moved,
-    )(*plane_sums, done)
+    )(*plane_sums)
     joined = call(
         join_kernel,
         "join_chips",
         jax.ShapeDtypeStruct((half_rows, width), jnp.bfloat16),
-        [SMEM()] + [VMEM()] * quad_size,
+        [SMEM(), ANY()] + [VMEM()] * quad_size,
         moved=quad_size * chunk_moved,
-    )(quad, total, *[trade_chips(total, distance, inner) for distance in distances])
+    )(quad, done, total, *[trade_chips(total, distance, inner) for distance in distances])
     weight_grad = call(
         spread_kernel,
         "spread_sums",

time: 96.3 us -> 94 us (0.976)
  starting transfers between devices: 59.4 us -> 48.7 us
  waiting for transfers between devices: 20.3 us -> 28.7 us
    ppermute x19, waiting for transfers between devices: 11 us -> 21.9 us  [trade(): return lax.ppermute(values, 'seq', pairs)]
    ppermute x19, starting transfers between devices: 48.5 us -> 39.7 us  [trade(): return lax.ppermute(values, 'seq', pairs)]
    ppermute x6, waiting for transfers between devices: 7.92 us -> 5.48 us  [trade_chips(): return lax.ppermute(values, ('dp', 'seq'), pairs)]
    ppermute x6, starting transfers between devices: 9.24 us -> 7.41 us  [trade_chips(): return lax.ppermute(values, ('dp', 'seq'), pairs)]
  transfers between devices with their start and end apart: 29 -> 29, of which waited for: 13 -> 11; matrix products, arithmetic and copies ran while one was open for 0% -> 0% of each run, Pallas kernels for 8% -> 9%
where the time goes in v14:
time: 94 us; the launch traced here: 93.6 us
  starting transfers between devices  48.7 us (52%)
  waiting for transfers between devices  28.7 us (31%)
  Pallas kernels  14.7 us (16%)
    ppermute x19, starting transfers between devices, trade(): return lax.ppermute(values, 'seq', pairs)  39.7 us
    ppermute x19, waiting for transfers between devices, trade(): return lax.ppermute(values, 'seq', pairs)  21.9 us
    ppermute x6, starting transfers between devices, trade_chips(): return lax.ppermute(values, ('dp', 'seq'), pairs)  7.41 us
    ppermute x6, waiting for transfers between devices, trade_chips(): return lax.ppermute(values, ('dp', 'seq'), pairs)  5.48 us
    pallas_call x2, Pallas kernels, pack(): call(functools.partial(pack_kernel, distances, regions, per_device), name...  5.3 us
    pallas_call x1, Pallas kernels, body(): call(norm_kernel, 'norm_and_gradient', [jax.ShapeDtypeStruct((regions, PA...  3.07 us
    pallas_call x1, Pallas kernels, body(): call(functools.partial(attend_kernel, block_rows, group, order), 'attend'...  2.49 us
    pallas_call x1, Pallas kernels, body(): call(decode_kernel, 'decode', [jax.ShapeDtypeStruct(cotangent.shape, jnp....  2.23 us
  transfers between devices with their start and end apart: 29, of which 11 were waited for; matrix products, arithmetic and copies ran while one was open for 0% of the time, Pallas kernels for 9%

profile of v14, /device:TPU:0, one launch (start us, length us, event | category | flops | bytes accessed | tf_op | source)
XLA Modules:
  0.0 93.6 jit_solution(14568295113474014757)
XLA Ops:
  0.6 0.0 copy-start
  0.7 0.0 copy-start.1
  0.7 0.0 copy-start.2
  0.7 2.6 %pack_early.1 = (bf16[3,4,64,128]{3,2,1,0:T(8,128)(2,1)}, bf16[3,4,64,128]{3,2,1,0:T(8,128)(2,1)}, bf16[3,4,64,128]{3,2,1,0:T(8,128)(2,1)}) custom-call(s32[1]{0:T(128)} %bitcast.index_ref, bf16[64,2,2048]{2,1,0:T(2,128)(2,1)} %query_ref.5, bf16[64,2,2048]{2,1,0:T(2,128)(2,1)} %key_ref.5, bf16[64,2,2048]{2,1,0:T(2,128)(2,1)} %value_ref.5), custom_call_target="tpu_custom_call" | custom-call | bytes 1179648 | tf_op jit(solution)/shard_map/pack_early/pallas_call | solution.py:403
  3.3 3.1 %collective-permute-start.3 = (bf16[3,4,64,128]{3,2,1,0:T(8,128)(2,1)}, bf16[3,4,64,128]{3,2,1,0:T(8,128)(2,1)S(1)}, u32[]{:S(2)}, u32[]{:S(2)}) collective-permute-start(bf16[3,4,64,128]{3,2,1,0:T(8,128)(2,1)} %get-tuple-element.34), channel_id=1, source_target_pairs={{0,2},{1,3},{2,0},{3,1},{4,6},{5,7},{6,4},{7,5},{8,10},{9,11},{10,... | collective-permute-start | bytes 589832 | tf_op jit(solution)/shard_map/ppermute | solution.py:348
  6.3 2.6 %collective-permute-start.5 = (bf16[3,4,64,128]{3,2,1,0:T(8,128)(2,1)}, bf16[3,4,64,128]{3,2,1,0:T(8,128)(2,1)S(1)}, u32[]{:S(2)}, u32[]{:S(2)}) collective-permute-start(bf16[3,4,64,128]{3,2,1,0:T(8,128)(2,1)} %get-tuple-element.36), channel_id=1, source_target_pairs={{0,4},{1,5},{2,6},{3,7},{4,0},{5,1},{6,2},{7,3},{8,12},{9,13},{10,... | collective-permute-start | bytes 589832 | tf_op jit(solution)/shard_map/ppermute | solution.py:348
  8.9 1.3 %collective-permute-start.6 = (bf16[3,4,64,128]{3,2,1,0:T(8,128)(2,1)}, bf16[3,4,64,128]{3,2,1,0:T(8,128)(2,1)S(1)}, u32[]{:S(2)}, u32[]{:S(2)}) collective-permute-start(bf16[3,4,64,128]{3,2,1,0:T(8,128)(2,1)} %get-tuple-element.37), channel_id=1, source_target_pairs={{0,5},{1,4},{2,7},{3,6},{4,1},{5,0},{6,3},{7,2},{8,13},{9,12},{10,... | collective-permute-start | bytes 589832 | tf_op jit(solution)/shard_map/ppermute | solution.py:348
  10.2 2.7 %pack_late.1 = (bf16[3,4,64,128]{3,2,1,0:T(8,128)(2,1)}, bf16[3,4,64,128]{3,2,1,0:T(8,128)(2,1)}, bf16[3,4,64,128]{3,2,1,0:T(8,128)(2,1)}, bf16[3,4,64,128]{3,2,1,0:T(8,128)(2,1)}) custom-call(s32[1]{0:T(128)} %bitcast.index_ref, bf16[64,2,2048]{2,1,0:T(2,128)(2,1)} %query_ref.5, bf16[64,2,2048]{2,1,0:T(2,128)(2,1)} %key_ref.5, bf16[64,2,2048]{2,1,0:T(2,128)(2,1)} %value_ref.5), custom_call_target="tpu_custom_call" | custom-call | bytes 1572864 | tf_op jit(solution)/shard_map/pack_late/pallas_call | solution.py:403
  13.0 0.0 copy-start.6
  13.0 0.6 collective-permute-start.2
  13.6 1.4 %collective-permute-start.4 = (bf16[3,4,64,128]{3,2,1,0:T(8,128)(2,1)}, bf16[3,4,64,128]{3,2,1,0:T(8,128)(2,1)S(1)}, u32[]{:S(2)}, u32[]{:S(2)}) collective-permute-start(bf16[3,4,64,128]{3,2,1,0:T(8,128)(2,1)} %get-tuple-element.35), channel_id=1, source_target_pairs={{0,3},{1,2},{2,1},{3,0},{4,7},{5,6},{6,5},{7,4},{8,11},{9,10},{10,... | collective-permute-start | bytes 589832 | tf_op jit(solution)/shard_map/ppermute | solution.py:348
  15.0 0.4 own_chunk.1
  15.4 0.1 collective-permute-done.3.refs_1_
  15.6 0.3 copy-done.8
  15.9 3.6 %collective-permute-start.7 = (bf16[3,4,64,128]{3,2,1,0:T(8,128)(2,1)S(1)}, bf16[3,4,64,128]{3,2,1,0:T(8,128)(2,1)S(1)}, u32[]{:S(2)}, u32[]{:S(2)}) collective-permute-start(bf16[3,4,64,128]{3,2,1,0:T(8,128)(2,1)S(1)} %copy-done.8), channel_id=1, source_target_pairs={{0,6},{1,7},{2,4},{3,5},{4,2},{5,3},{6,0},{7,1},{8,14},{9,15},{10,... | collective-permute-start | bytes 589832 | tf_op jit(solution)/shard_map/ppermute | solution.py:348
  19.5 3.9 %collective-permute-done.5.refs_3_ = bf16[3,4,64,128]{3,2,1,0:T(8,128)(2,1)S(1)} collective-permute-done((bf16[3,4,64,128]{3,2,1,0:T(8,128)(2,1)}, bf16[3,4,64,128]{3,2,1,0:T(8,128)(2,1)S(1)}, u32[]{:S(2)}, u32[]{:S(2)}) %collective-permute-start.5) | collective-permute-done | bytes 196640 | tf_op jit(solution)/shard_map/ppermute | solution.py:348
  23.4 3.7 %collective-permute-start.8 = (bf16[3,4,64,128]{3,2,1,0:T(8,128)(2,1)S(1)}, bf16[3,4,64,128]{3,2,1,0:T(8,128)(2,1)S(1)}, u32[]{:S(2)}, u32[]{:S(2)}) collective-permute-start(bf16[3,4,64,128]{3,2,1,0:T(8,128)(2,1)S(1)} %copy-done.7), channel_id=1, source_target_pairs={{0,7},{1,6},{2,5},{3,4},{4,3},{5,2},{6,1},{7,0},{8,15},{9,14},{10,... | collective-permute-start | bytes 589832 | tf_op jit(solution)/shard_map/ppermute | solution.py:348
  27.1 10.2 %collective-permute-done.6.refs_4_ = bf16[3,4,64,128]{3,2,1,0:T(8,128)(2,1)S(1)} collective-permute-done((bf16[3,4,64,128]{3,2,1,0:T(8,128)(2,1)}, bf16[3,4,64,128]{3,2,1,0:T(8,128)(2,1)S(1)}, u32[]{:S(2)}, u32[]{:S(2)}) %collective-permute-start.6) | collective-permute-done | bytes 196640 | tf_op jit(solution)/shard_map/ppermute | solution.py:348
  37.3 0.3 collective-permute-start
  37.6 0.7 collective-permute-start.1
  38.2 0.1 fusion.2.lengths_ref
  38.3 0.0 collective-permute-done.4.refs_2_
  38.3 0.0 collective-permute-done.7.refs_5_
  38.3 0.0 collective-permute-done.8.refs_6_
  38.3 2.5 %attend.1 = (bf16[4,64,128]{2,1,0:T(8,128)(2,1)S(1)}, bf16[4,64,128]{2,1,0:T(8,128)(2,1)S(1)}, bf16[4,64,128]{2,1,0:T(8,128)(2,1)S(1)}, bf16[4,64,128]{2,1,0:T(8...) custom-call(s32[1]{0:T(128)} %bitcast.index_ref, ...), custom_call_target="tpu_custom_call" | custom-call | flops 536870912 | bytes 2097152 | tf_op jit(solution)/shard_map/attend/pallas_call | solution.py:450
  40.8 0.0 copy-start.5
  40.8 3.1 %collective-permute-start.9 = (bf16[4,64,128]{2,1,0:T(8,128)(2,1)S(1)}, bf16[4,64,128]{2,1,0:T(8,128)(2,1)S(1)}, u32[]{:S(2)}, u32[]{:S(2)}) collective-permute-start(bf16[4,64,128]{2,1,0:T(8,128)(2,1)S(1)} %get-tuple-element.42), channel_id=1, source_target_pairs={{0,1},{1,0},{2,3},{3,2},{4,5},{5,4},{6,7},{7,6},{8,9},{9,8},{10,11... | collective-permute-start | bytes 196616 | tf_op jit(solution)/shard_map/ppermute | solution.py:348
  43.9 5.3 %collective-permute-start.10 = (bf16[4,64,128]{2,1,0:T(8,128)(2,1)S(1)}, bf16[4,64,128]{2,1,0:T(8,128)(2,1)S(1)}, u32[]{:S(2)}, u32[]{:S(2)}) collective-permute-start(bf16[4,64,128]{2,1,0:T(8,128)(2,1)S(1)} %get-tuple-element.43), channel_id=1, source_target_pairs={{0,2},{1,3},{2,0},{3,1},{4,6},{5,7},{6,4},{7,5},{8,10},{9,11},{10,... | collective-permute-start | bytes 196616 | tf_op jit(solution)/shard_map/ppermute | solution.py:348
  49.2 0.4 collective-permute-start.11
  49.7 0.0 collective-permute-done.near_ref
  49.7 3.7 %collective-permute-start.12 = (bf16[4,64,128]{2,1,0:T(8,128)(2,1)S(1)}, bf16[4,64,128]{2,1,0:T(8,128)(2,1)S(1)}, u32[]{:S(2)}, u32[]{:S(2)}) collective-permute-start(bf16[4,64,128]{2,1,0:T(8,128)(2,1)S(1)} %get-tuple-element.45), channel_id=1, source_target_pairs={{0,4},{1,5},{2,6},{3,7},{4,0},{5,1},{6,2},{7,3},{8,12},{9,13},{10,... | collective-permute-start | bytes 196616 | tf_op jit(solution)/shard_map/ppermute | solution.py:348
  53.4 0.0 collective-permute-done.9.refs_1_
  53.4 2.4 %collective-permute-start.14 = (bf16[4,64,128]{2,1,0:T(8,128)(2,1)S(1)}, bf16[4,64,128]{2,1,0:T(8,128)(2,1)S(1)}, u32[]{:S(2)}, u32[]{:S(2)}) collective-permute-start(bf16[4,64,128]{2,1,0:T(8,128)(2,1)S(1)} %get-tuple-element.47), channel_id=1, source_target_pairs={{0,6},{1,7},{2,4},{3,5},{4,2},{5,3},{6,0},{7,1},{8,14},{9,15},{10,... | collective-permute-start | bytes 196616 | tf_op jit(solution)/shard_map/ppermute | solution.py:348
  55.7 0.0 collective-permute-done.10.refs_2_
  55.7 2.4 %collective-permute-start.15 = (bf16[4,64,128]{2,1,0:T(8,128)(2,1)S(1)}, bf16[4,64,128]{2,1,0:T(8,128)(2,1)S(1)}, u32[]{:S(2)}, u32[]{:S(2)}) collective-permute-start(bf16[4,64,128]{2,1,0:T(8,128)(2,1)S(1)} %get-tuple-element.48), channel_id=1, source_target_pairs={{0,7},{1,6},{2,5},{3,4},{4,3},{5,2},{6,1},{7,0},{8,15},{9,14},{10,... | collective-permute-start | bytes 196616 | tf_op jit(solution)/shard_map/ppermute | solution.py:348
  58.2 0.3 turn_cotangent.1.turned_ref
  58.4 0.0 collective-permute-done.12.refs_4_
  58.5 2.5 %collective-permute-done.13.refs_5_ = bf16[4,64,128]{2,1,0:T(8,128)(2,1)S(1)} collective-permute-done((bf16[4,64,128]{2,1,0:T(8,128)(2,1)S(1)}, bf16[4,64,128]{2,1,0:T(8,128)(2,1)S(1)}, u32[]{:S(2)}, u32[]{:S(2)}) %collective-permute-start.13) | collective-permute-done | bytes 65568 | tf_op jit(solution)/shard_map/ppermute | solution.py:348
  61.0 0.0 collective-permute-done.14.refs_6_
  61.0 1.8 %collective-permute-done.15.refs_7_ = bf16[4,64,128]{2,1,0:T(8,128)(2,1)S(1)} collective-permute-done((bf16[4,64,128]{2,1,0:T(8,128)(2,1)S(1)}, bf16[4,64,128]{2,1,0:T(8,128)(2,1)S(1)}, u32[]{:S(2)}, u32[]{:S(2)}) %collective-permute-start.15) | collective-permute-done | bytes 65568 | tf_op jit(solution)/shard_map/ppermute | solution.py:348
  62.8 3.1 %norm_and_gradient.1 = (bf16[2,4,256,128]{3,2,1,0:T(8,128)(2,1)S(1)}, bf16[2,256,128]{2,1,0:T(8,128)(2,1)S(1)}, bf16[2,256,128]{2,1,0:T(8,128)(2,1)S(1)}, f32[576,128]{1,0:T(8,128)S(1)}, f32[576,128]{1,0:T(8,128)S(1)}) custom-call(s32[2]{0:T(128)S(1)} %copy-done.6, s32[1]{0:T(128)} %bitcast.index_ref, s32[1]{0:T(128)} %bitcast.1.core_ref, ...), custom_call_target="tpu_custom_call" | custom-call | flops 603979776 | bytes 2097152 | tf_op jit(solution)/shard_map/norm_and_gradient/pallas_call | solution.py:473
  65.9 0.1 collective-permute-start.18
  66.0 1.4 %collective-permute-start.16 = (bf16[2,256,128]{2,1,0:T(8,128)(2,1)S(1)}, bf16[2,256,128]{2,1,0:T(8,128)(2,1)S(1)}, u32[]{:S(2)}, u32[]{:S(2)}) collective-permute-start(bf16[2,256,128]{2,1,0:T(8,128)(2,1)S(1)} %get-tuple-element.50), channel_id=1, source_target_pairs={{0,1},{1,0},{2,3},{3,2},{4,5},{5,4},{6,7},{7,6},{8,9},{9,8},{10,11... | collective-permute-start | bytes 393224 | tf_op jit(solution)/shard_map/ppermute | solution.py:348
  67.4 0.8 collective-permute-start.17
  68.2 0.1 sum_cores.1
  68.3 2.3 %collective-permute-start.19 = (bf16[144,128]{1,0:T(8,128)(2,1)S(1)}, bf16[144,128]{1,0:T(8,128)(2,1)S(1)}, u32[]{:S(2)}, u32[]{:S(2)}) collective-permute-start(bf16[144,128]{1,0:T(8,128)(2,1)S(1)} %get-tuple-element.57), channel_id=1, source_target_pairs={{0,1},{1,0},{2,3},{3,2},{4,5},{5,4},{6,7},{7,6},{8,9},{9,8},{10,11... | collective-permute-start | bytes 110600 | tf_op jit(solution)/shard_map/ppermute | solution.py:366
  70.6 1.5 %collective-permute-start.20 = (bf16[144,128]{1,0:T(8,128)(2,1)S(1)}, bf16[144,128]{1,0:T(8,128)(2,1)S(1)}, u32[]{:S(2)}, u32[]{:S(2)}) collective-permute-start(bf16[144,128]{1,0:T(8,128)(2,1)S(1)} %get-tuple-element.58), channel_id=1, source_target_pairs={{0,16},{1,17},{2,18},{3,19},{4,20},{5,21},{6,22},{7,23},{8,24},{9,... | collective-permute-start | bytes 110600 | tf_op jit(solution)/shard_map/ppermute | solution.py:366
  72.1 0.1 collective-permute-start.21
  72.2 2.5 %collective-permute-done.19.refs_1_ = bf16[144,128]{1,0:T(8,128)(2,1)S(1)} collective-permute-done((bf16[144,128]{1,0:T(8,128)(2,1)S(1)}, bf16[144,128]{1,0:T(8,128)(2,1)S(1)}, u32[]{:S(2)}, u32[]{:S(2)}) %collective-permute-start.19) | collective-permute-done | bytes 36896 | tf_op jit(solution)/shard_map/ppermute | solution.py:366
  74.7 2.3 %collective-permute-done.21.refs_3_ = bf16[144,128]{1,0:T(8,128)(2,1)S(1)} collective-permute-done((bf16[144,128]{1,0:T(8,128)(2,1)S(1)}, bf16[144,128]{1,0:T(8,128)(2,1)S(1)}, u32[]{:S(2)}, u32[]{:S(2)}) %collective-permute-start.21) | collective-permute-done | bytes 36896 | tf_op jit(solution)/shard_map/ppermute | solution.py:366
  77.0 2.6 %collective-permute-start.24 = (bf16[144,128]{1,0:T(8,128)(2,1)S(1)}, bf16[144,128]{1,0:T(8,128)(2,1)S(1)}, u32[]{:S(2)}, u32[]{:S(2)}) collective-permute-start(bf16[144,128]{1,0:T(8,128)(2,1)S(1)} %sum_chips.1.refs_0_), channel_id=1, source_target_pairs={{0,6},{1,7},{2,4},{3,5},{4,2},{5,3},{6,0},{7,1},{8,14},{9,15},{10,... | collective-permute-start | bytes 110600 | tf_op jit(solution)/shard_map/ppermute | solution.py:348
  79.6 0.8 collective-permute-start.23
  80.4 1.0 %collective-permute-start.22 = (bf16[144,128]{1,0:T(8,128)(2,1)S(1)}, bf16[144,128]{1,0:T(8,128)(2,1)S(1)}, u32[]{:S(2)}, u32[]{:S(2)}) collective-permute-start(bf16[144,128]{1,0:T(8,128)(2,1)S(1)} %sum_chips.1.refs_0_), channel_id=1, source_target_pairs={{0,2},{1,3},{2,0},{3,1},{4,6},{5,7},{6,4},{7,5},{8,10},{9,11},{10,... | collective-permute-start | bytes 110600 | tf_op jit(solution)/shard_map/ppermute | solution.py:348
  81.4 1.4 %collective-permute-done.24.refs_3_ = bf16[144,128]{1,0:T(8,128)(2,1)S(1)} collective-permute-done((bf16[144,128]{1,0:T(8,128)(2,1)S(1)}, bf16[144,128]{1,0:T(8,128)(2,1)S(1)}, u32[]{:S(2)}, u32[]{:S(2)}) %collective-permute-start.24) | collective-permute-done | bytes 36896 | tf_op jit(solution)/shard_map/ppermute | solution.py:348
  82.8 1.9 %collective-permute-done.23.refs_2_ = bf16[144,128]{1,0:T(8,128)(2,1)S(1)} collective-permute-done((bf16[144,128]{1,0:T(8,128)(2,1)S(1)}, bf16[144,128]{1,0:T(8,128)(2,1)S(1)}, u32[]{:S(2)}, u32[]{:S(2)}) %collective-permute-start.23) | collective-permute-done | bytes 36896 | tf_op jit(solution)/shard_map/ppermute | solution.py:348
  84.7 0.0 collective-permute-done.22.refs_1_
  84.8 1.3 %collective-permute-start.27 = (bf16[144,128]{1,0:T(8,128)(2,1)S(1)}, bf16[144,128]{1,0:T(8,128)(2,1)S(1)}, u32[]{:S(2)}, u32[]{:S(2)}) collective-permute-start(bf16[144,128]{1,0:T(8,128)(2,1)S(1)} %sum_planes.1.refs_0_), channel_id=1, source_target_pairs={{0,17},{1,16},{2,19},{3,18},{4,21},{5,20},{6,23},{7,22},{8,25},{9,... | collective-permute-start | bytes 110600 | tf_op jit(solution)/shard_map/ppermute | solution.py:366
  86.1 1.2 %collective-permute-start.26 = (bf16[144,128]{1,0:T(8,128)(2,1)S(1)}, bf16[144,128]{1,0:T(8,128)(2,1)S(1)}, u32[]{:S(2)}, u32[]{:S(2)}) collective-permute-start(bf16[144,128]{1,0:T(8,128)(2,1)S(1)} %sum_planes.1.refs_0_), channel_id=1, source_target_pairs={{0,16},{1,17},{2,18},{3,19},{4,20},{5,21},{6,22},{7,23},{8,24},{9,... | collective-permute-start | bytes 110600 | tf_op jit(solution)/shard_map/ppermute | solution.py:366
  87.3 1.0 %collective-permute-start.25 = (bf16[144,128]{1,0:T(8,128)(2,1)S(1)}, bf16[144,128]{1,0:T(8,128)(2,1)S(1)}, u32[]{:S(2)}, u32[]{:S(2)}) collective-permute-start(bf16[144,128]{1,0:T(8,128)(2,1)S(1)} %sum_planes.1.refs_0_), channel_id=1, source_target_pairs={{0,1},{1,0},{2,3},{3,2},{4,5},{5,4},{6,7},{7,6},{8,9},{9,8},{10,11... | collective-permute-start | bytes 110600 | tf_op jit(solution)/shard_map/ppermute | solution.py:366
  88.3 2.2 %decode.1 = (bf16[2,4,256,128]{3,2,1,0:T(8,128)(2,1)}, f32[8,128]{1,0:T(8,128)S(1)}) custom-call(s32[1]{0:T(128)} %bitcast.index_ref, bf16[2,4,256,128]{3,2,1,0:T(8,128)(2,1)S(1)} %get-tuple-element.49.image_ref, bf16[2,256,128]{2,1,0:T(8,128)(2,1)S(1)} %collective-permute-done.16.near_ref, bf16[2,256,128]{2,1,0:T(8,128)(2,1)S(1)} %collective-permute-done.17.far_ref, ...), custom_call_target="tpu_custom_call" | custom-call | flops 603979776 | bytes 1048576 | tf_op jit(solution)/shard_map/decode/pallas_call | solution.py:511
  90.6 0.7 collective-permute-done.25.refs_1_
  91.3 0.1 collective-permute-start.28
  91.4 1.4 %collective-permute-done.28.other_ref = bf16[576,128]{1,0:T(8,128)(2,1)S(1)} collective-permute-done((bf16[576,128]{1,0:T(8,128)(2,1)S(1)}, bf16[576,128]{1,0:T(8,128)(2,1)S(1)}, u32[]{:S(2)}, u32[]{:S(2)}) %collective-permute-start.28) | collective-permute-done | bytes 147488 | tf_op jit(solution)/shard_map/ppermute | solution.py:370
  92.7 0.9 spread_sums.1
  (27 shorter events, 0.1 us)
Async XLA Ops:
  0.6 14.3 %copy-start.3 = (bf16[2,4,256,128]{3,2,1,0:T(8,128)(2,1)S(1)}, bf16[2,4,256,128]{3,2,1,0:T(8,128)(2,1)}, u32[]{:S(2)}) copy-start(bf16[2,4,256,128]{3,2,1,0:T(8,128)(2,1)} %cot_ref.1) | copy-start | bytes 1572868
  0.6 14.3 %copy-start = (bf16[64,2,2048]{2,1,0:T(2,128)(2,1)S(1)}, bf16[64,2,2048]{2,1,0:T(2,128)(2,1)}, u32[]{:S(2)}) copy-start(bf16[64,2,2048]{2,1,0:T(2,128)(2,1)} %query_ref.5) | copy-start | bytes 1572868
  0.7 14.3 %copy-start.1 = (bf16[64,2,2048]{2,1,0:T(2,128)(2,1)S(1)}, bf16[64,2,2048]{2,1,0:T(2,128)(2,1)}, u32[]{:S(2)}) copy-start(bf16[64,2,2048]{2,1,0:T(2,128)(2,1)} %key_ref.5) | copy-start | bytes 1572868
  0.7 14.3 %copy-start.2 = (bf16[64,2,2048]{2,1,0:T(2,128)(2,1)S(1)}, bf16[64,2,2048]{2,1,0:T(2,128)(2,1)}, u32[]{:S(2)}) copy-start(bf16[64,2,2048]{2,1,0:T(2,128)(2,1)} %value_ref.5) | copy-start | bytes 1572868
  3.3 12.3 %collective-permute-start.3 = (bf16[3,4,64,128]{3,2,1,0:T(8,128)(2,1)}, bf16[3,4,64,128]{3,2,1,0:T(8,128)(2,1)S(1)}, u32[]{:S(2)}, u32[]{:S(2)}) collective-permute-start(bf16[3,4,64,128]{3,2,1,0:T(8,128)(2,1)} %get-tuple-element.34), channel_id=1, source_target_pairs={{0,2},{1,3},{2,0},{3,1},{4,6},{5,7},{6,4},{7,5},{8,10},{9,11},{10,... | collective-permute-start | bytes 589832 | tf_op jit(solution)/shard_map/ppermute | solution.py:348
  6.3 17.1 %collective-permute-start.5 = (bf16[3,4,64,128]{3,2,1,0:T(8,128)(2,1)}, bf16[3,4,64,128]{3,2,1,0:T(8,128)(2,1)S(1)}, u32[]{:S(2)}, u32[]{:S(2)}) collective-permute-start(bf16[3,4,64,128]{3,2,1,0:T(8,128)(2,1)} %get-tuple-element.36), channel_id=1, source_target_pairs={{0,4},{1,5},{2,6},{3,7},{4,0},{5,1},{6,2},{7,3},{8,12},{9,13},{10,... | collective-permute-start | bytes 589832 | tf_op jit(solution)/shard_map/ppermute | solution.py:348
  8.9 28.3 %collective-permute-start.6 = (bf16[3,4,64,128]{3,2,1,0:T(8,128)(2,1)}, bf16[3,4,64,128]{3,2,1,0:T(8,128)(2,1)S(1)}, u32[]{:S(2)}, u32[]{:S(2)}) collective-permute-start(bf16[3,4,64,128]{3,2,1,0:T(8,128)(2,1)} %get-tuple-element.37), channel_id=1, source_target_pairs={{0,5},{1,4},{2,7},{3,6},{4,1},{5,0},{6,3},{7,2},{8,13},{9,12},{10,... | collective-permute-start | bytes 589832 | tf_op jit(solution)/shard_map/ppermute | solution.py:348
  12.9 10.5 %copy-start.7 = (bf16[3,4,64,128]{3,2,1,0:T(8,128)(2,1)S(1)}, bf16[3,4,64,128]{3,2,1,0:T(8,128)(2,1)}, u32[]{:S(2)}) copy-start(bf16[3,4,64,128]{3,2,1,0:T(8,128)(2,1)} %get-tuple-element.39) | copy-start | bytes 589828
  13.0 25.3 %copy-start.6 = (s32[2]{0:T(128)S(1)}, s32[2]{0:T(128)}, u32[]{:S(2)}) copy-start(s32[2]{0:T(128)} %lengths_ref.1) | copy-start | bytes 28
  13.0 24.6 %collective-permute-start.2 = (bf16[3,4,64,128]{3,2,1,0:T(8,128)(2,1)}, bf16[3,4,64,128]{3,2,1,0:T(8,128)(2,1)S(1)}, u32[]{:S(2)}, u32[]{:S(2)}) collective-permute-start(bf16[3,4,64,128]{3,2,1,0:T(8,128)(2,1)} %get-tuple-element.33), channel_id=1, source_target_pairs={{0,1},{1,0},{2,3},{3,2},{4,5},{5,4},{6,7},{7,6},{8,9},{9,8},{10,11... | collective-permute-start | bytes 589832 | tf_op jit(solution)/shard_map/ppermute | solution.py:348
  13.6 24.8 %collective-permute-start.4 = (bf16[3,4,64,128]{3,2,1,0:T(8,128)(2,1)}, bf16[3,4,64,128]{3,2,1,0:T(8,128)(2,1)S(1)}, u32[]{:S(2)}, u32[]{:S(2)}) collective-permute-start(bf16[3,4,64,128]{3,2,1,0:T(8,128)(2,1)} %get-tuple-element.35), channel_id=1, source_target_pairs={{0,3},{1,2},{2,1},{3,0},{4,7},{5,6},{6,5},{7,4},{8,11},{9,10},{10,... | collective-permute-start | bytes 589832 | tf_op jit(solution)/shard_map/ppermute | solution.py:348
  15.0 0.9 copy-start.8
  15.9 22.4 %collective-permute-start.7 = (bf16[3,4,64,128]{3,2,1,0:T(8,128)(2,1)S(1)}, bf16[3,4,64,128]{3,2,1,0:T(8,128)(2,1)S(1)}, u32[]{:S(2)}, u32[]{:S(2)}) collective-permute-start(bf16[3,4,64,128]{3,2,1,0:T(8,128)(2,1)S(1)} %copy-done.8), channel_id=1, source_target_pairs={{0,6},{1,7},{2,4},{3,5},{4,2},{5,3},{6,0},{7,1},{8,14},{9,15},{10,... | collective-permute-start | bytes 589832 | tf_op jit(solution)/shard_map/ppermute | solution.py:348
  23.4 14.9 %collective-permute-start.8 = (bf16[3,4,64,128]{3,2,1,0:T(8,128)(2,1)S(1)}, bf16[3,4,64,128]{3,2,1,0:T(8,128)(2,1)S(1)}, u32[]{:S(2)}, u32[]{:S(2)}) collective-permute-start(bf16[3,4,64,128]{3,2,1,0:T(8,128)(2,1)S(1)} %copy-done.7), channel_id=1, source_target_pairs={{0,7},{1,6},{2,5},{3,4},{4,3},{5,2},{6,1},{7,0},{8,15},{9,14},{10,... | collective-permute-start | bytes 589832 | tf_op jit(solution)/shard_map/ppermute | solution.py:348
  37.3 12.4 %collective-permute-start = (bf16[2,256,128]{2,1,0:T(8,128)(2,1)S(1)}, bf16[2,256,128]{2,1,0:T(8,128)(2,1)S(1)}, u32[]{:S(2)}, u32[]{:S(2)}) collective-permute-start(bf16[2,256,128]{2,1,0:T(8,128)(2,1)S(1)} %get-tuple-element.31), channel_id=1, source_target_pairs={{0,1},{1,0},{2,3},{3,2},{4,5},{5,4},{6,7},{7,6},{8,9},{9,8},{10,11... | collective-permute-start | bytes 393224 | tf_op jit(solution)/shard_map/ppermute | solution.py:348
  37.6 15.8 %collective-permute-start.1 = (bf16[2,256,128]{2,1,0:T(8,128)(2,1)S(1)}, bf16[2,256,128]{2,1,0:T(8,128)(2,1)S(1)}, u32[]{:S(2)}, u32[]{:S(2)}) collective-permute-start(bf16[2,256,128]{2,1,0:T(8,128)(2,1)S(1)} %get-tuple-element.32), channel_id=1, source_target_pairs={{1,2},{3,4},{5,6},{2,1},{4,3},{6,5},{9,10},{11,12},{13,14},{10,9},... | collective-permute-start | bytes 393224 | tf_op jit(solution)/shard_map/ppermute | solution.py:437
  40.8 22.0 %copy-start.5 = (f32[2048]{0:T(1024)S(1)}, f32[2048]{0:T(1024)}, u32[]{:S(2)}) copy-start(f32[2048]{0:T(1024)} %param.11) | copy-start | bytes 24580
  40.8 12.5 %collective-permute-start.9 = (bf16[4,64,128]{2,1,0:T(8,128)(2,1)S(1)}, bf16[4,64,128]{2,1,0:T(8,128)(2,1)S(1)}, u32[]{:S(2)}, u32[]{:S(2)}) collective-permute-start(bf16[4,64,128]{2,1,0:T(8,128)(2,1)S(1)} %get-tuple-element.42), channel_id=1, source_target_pairs={{0,1},{1,0},{2,3},{3,2},{4,5},{5,4},{6,7},{7,6},{8,9},{9,8},{10,11... | collective-permute-start | bytes 196616 | tf_op jit(solution)/shard_map/ppermute | solution.py:348
  43.9 11.8 %collective-permute-start.10 = (bf16[4,64,128]{2,1,0:T(8,128)(2,1)S(1)}, bf16[4,64,128]{2,1,0:T(8,128)(2,1)S(1)}, u32[]{:S(2)}, u32[]{:S(2)}) collective-permute-start(bf16[4,64,128]{2,1,0:T(8,128)(2,1)S(1)} %get-tuple-element.43), channel_id=1, source_target_pairs={{0,2},{1,3},{2,0},{3,1},{4,6},{5,7},{6,4},{7,5},{8,10},{9,11},{10,... | collective-permute-start | bytes 196616 | tf_op jit(solution)/shard_map/ppermute | solution.py:348
  49.2 9.2 %collective-permute-start.11 = (bf16[4,64,128]{2,1,0:T(8,128)(2,1)S(1)}, bf16[4,64,128]{2,1,0:T(8,128)(2,1)S(1)}, u32[]{:S(2)}, u32[]{:S(2)}) collective-permute-start(bf16[4,64,128]{2,1,0:T(8,128)(2,1)S(1)} %get-tuple-element.44), channel_id=1, source_target_pairs={{0,3},{1,2},{2,1},{3,0},{4,7},{5,6},{6,5},{7,4},{8,11},{9,10},{10,... | collective-permute-start | bytes 196616 | tf_op jit(solution)/shard_map/ppermute | solution.py:348
  49.7 8.8 %collective-permute-start.12 = (bf16[4,64,128]{2,1,0:T(8,128)(2,1)S(1)}, bf16[4,64,128]{2,1,0:T(8,128)(2,1)S(1)}, u32[]{:S(2)}, u32[]{:S(2)}) collective-permute-start(bf16[4,64,128]{2,1,0:T(8,128)(2,1)S(1)} %get-tuple-element.45), channel_id=1, source_target_pairs={{0,4},{1,5},{2,6},{3,7},{4,0},{5,1},{6,2},{7,3},{8,12},{9,13},{10,... | collective-permute-start | bytes 196616 | tf_op jit(solution)/shard_map/ppermute | solution.py:348
  53.4 7.7 %collective-permute-start.13 = (bf16[4,64,128]{2,1,0:T(8,128)(2,1)S(1)}, bf16[4,64,128]{2,1,0:T(8,128)(2,1)S(1)}, u32[]{:S(2)}, u32[]{:S(2)}) collective-permute-start(bf16[4,64,128]{2,1,0:T(8,128)(2,1)S(1)} %get-tuple-element.46), channel_id=1, source_target_pairs={{0,5},{1,4},{2,7},{3,6},{4,1},{5,0},{6,3},{7,2},{8,13},{9,12},{10,... | collective-permute-start | bytes 196616 | tf_op jit(solution)/shard_map/ppermute | solution.py:348
  53.4 7.6 %collective-permute-start.14 = (bf16[4,64,128]{2,1,0:T(8,128)(2,1)S(1)}, bf16[4,64,128]{2,1,0:T(8,128)(2,1)S(1)}, u32[]{:S(2)}, u32[]{:S(2)}) collective-permute-start(bf16[4,64,128]{2,1,0:T(8,128)(2,1)S(1)} %get-tuple-element.47), channel_id=1, source_target_pairs={{0,6},{1,7},{2,4},{3,5},{4,2},{5,3},{6,0},{7,1},{8,14},{9,15},{10,... | collective-permute-start | bytes 196616 | tf_op jit(solution)/shard_map/ppermute | solution.py:348
  55.7 7.1 %collective-permute-start.15 = (bf16[4,64,128]{2,1,0:T(8,128)(2,1)S(1)}, bf16[4,64,128]{2,1,0:T(8,128)(2,1)S(1)}, u32[]{:S(2)}, u32[]{:S(2)}) collective-permute-start(bf16[4,64,128]{2,1,0:T(8,128)(2,1)S(1)} %get-tuple-element.48), channel_id=1, source_target_pairs={{0,7},{1,6},{2,5},{3,4},{4,3},{5,2},{6,1},{7,0},{8,15},{9,14},{10,... | collective-permute-start | bytes 196616 | tf_op jit(solution)/shard_map/ppermute | solution.py:348
  62.8 25.5 %copy-start.4 = (bf16[9,128,128]{2,1,0:T(8,128)(2,1)S(1)}, bf16[9,128,128]{2,1,0:T(8,128)(2,1)}, u32[]{:S(2)}) copy-start(bf16[9,128,128]{2,1,0:T(8,128)(2,1)} %param.12) | copy-start | bytes 884740
  65.9 2.4 %collective-permute-start.18 = (f32[576,128]{1,0:T(8,128)S(1)}, f32[576,128]{1,0:T(8,128)S(1)}, u32[]{:S(2)}, u32[]{:S(2)}) collective-permute-start(f32[576,128]{1,0:T(8,128)S(1)} %get-tuple-element.55), channel_id=1, source_target_pairs={{0,8},{8,0},{16,24},{24,16},{1,9},{9,1},{17,25},{25,17},{2,10},{10... | collective-permute-start | bytes 884744 | tf_op jit(solution)/shard_map/ppermute | solution.py:370
  66.0 22.4 %collective-permute-start.16 = (bf16[2,256,128]{2,1,0:T(8,128)(2,1)S(1)}, bf16[2,256,128]{2,1,0:T(8,128)(2,1)S(1)}, u32[]{:S(2)}, u32[]{:S(2)}) collective-permute-start(bf16[2,256,128]{2,1,0:T(8,128)(2,1)S(1)} %get-tuple-element.50), channel_id=1, source_target_pairs={{0,1},{1,0},{2,3},{3,2},{4,5},{5,4},{6,7},{7,6},{8,9},{9,8},{10,11... | collective-permute-start | bytes 393224 | tf_op jit(solution)/shard_map/ppermute | solution.py:348
  67.4 21.0 %collective-permute-start.17 = (bf16[2,256,128]{2,1,0:T(8,128)(2,1)S(1)}, bf16[2,256,128]{2,1,0:T(8,128)(2,1)S(1)}, u32[]{:S(2)}, u32[]{:S(2)}) collective-permute-start(bf16[2,256,128]{2,1,0:T(8,128)(2,1)S(1)} %get-tuple-element.51), channel_id=1, source_target_pairs={{1,2},{3,4},{5,6},{2,1},{4,3},{6,5},{9,10},{11,12},{13,14},{10,9},... | collective-permute-start | bytes 393224 | tf_op jit(solution)/shard_map/ppermute | solution.py:499
  68.3 6.4 %collective-permute-start.19 = (bf16[144,128]{1,0:T(8,128)(2,1)S(1)}, bf16[144,128]{1,0:T(8,128)(2,1)S(1)}, u32[]{:S(2)}, u32[]{:S(2)}) collective-permute-start(bf16[144,128]{1,0:T(8,128)(2,1)S(1)} %get-tuple-element.57), channel_id=1, source_target_pairs={{0,1},{1,0},{2,3},{3,2},{4,5},{5,4},{6,7},{7,6},{8,9},{9,8},{10,11... | collective-permute-start | bytes 110600 | tf_op jit(solution)/shard_map/ppermute | solution.py:366
  70.6 4.0 %collective-permute-start.20 = (bf16[144,128]{1,0:T(8,128)(2,1)S(1)}, bf16[144,128]{1,0:T(8,128)(2,1)S(1)}, u32[]{:S(2)}, u32[]{:S(2)}) collective-permute-start(bf16[144,128]{1,0:T(8,128)(2,1)S(1)} %get-tuple-element.58), channel_id=1, source_target_pairs={{0,16},{1,17},{2,18},{3,19},{4,20},{5,21},{6,22},{7,23},{8,24},{9,... | collective-permute-start | bytes 110600 | tf_op jit(solution)/shard_map/ppermute | solution.py:366
  72.1 4.9 %collective-permute-start.21 = (bf16[144,128]{1,0:T(8,128)(2,1)S(1)}, bf16[144,128]{1,0:T(8,128)(2,1)S(1)}, u32[]{:S(2)}, u32[]{:S(2)}) collective-permute-start(bf16[144,128]{1,0:T(8,128)(2,1)S(1)} %get-tuple-element.59), channel_id=1, source_target_pairs={{0,17},{1,16},{2,19},{3,18},{4,21},{5,20},{6,23},{7,22},{8,25},{9,... | collective-permute-start | bytes 110600 | tf_op jit(solution)/shard_map/ppermute | solution.py:366
  77.0 5.9 %collective-permute-start.24 = (bf16[144,128]{1,0:T(8,128)(2,1)S(1)}, bf16[144,128]{1,0:T(8,128)(2,1)S(1)}, u32[]{:S(2)}, u32[]{:S(2)}) collective-permute-start(bf16[144,128]{1,0:T(8,128)(2,1)S(1)} %sum_chips.1.refs_0_), channel_id=1, source_target_pairs={{0,6},{1,7},{2,4},{3,5},{4,2},{5,3},{6,0},{7,1},{8,14},{9,15},{10,... | collective-permute-start | bytes 110600 | tf_op jit(solution)/shard_map/ppermute | solution.py:348
  79.6 5.1 %collective-permute-start.23 = (bf16[144,128]{1,0:T(8,128)(2,1)S(1)}, bf16[144,128]{1,0:T(8,128)(2,1)S(1)}, u32[]{:S(2)}, u32[]{:S(2)}) collective-permute-start(bf16[144,128]{1,0:T(8,128)(2,1)S(1)} %sum_chips.1.refs_0_), channel_id=1, source_target_pairs={{0,4},{1,5},{2,6},{3,7},{4,0},{5,1},{6,2},{7,3},{8,12},{9,13},{10,... | collective-permute-start | bytes 110600 | tf_op jit(solution)/shard_map/ppermute | solution.py:348
  80.4 4.4 %collective-permute-start.22 = (bf16[144,128]{1,0:T(8,128)(2,1)S(1)}, bf16[144,128]{1,0:T(8,128)(2,1)S(1)}, u32[]{:S(2)}, u32[]{:S(2)}) collective-permute-start(bf16[144,128]{1,0:T(8,128)(2,1)S(1)} %sum_chips.1.refs_0_), channel_id=1, source_target_pairs={{0,2},{1,3},{2,0},{3,1},{4,6},{5,7},{6,4},{7,5},{8,10},{9,11},{10,... | collective-permute-start | bytes 110600 | tf_op jit(solution)/shard_map/ppermute | solution.py:348
  84.8 5.8 %collective-permute-start.27 = (bf16[144,128]{1,0:T(8,128)(2,1)S(1)}, bf16[144,128]{1,0:T(8,128)(2,1)S(1)}, u32[]{:S(2)}, u32[]{:S(2)}) collective-permute-start(bf16[144,128]{1,0:T(8,128)(2,1)S(1)} %sum_planes.1.refs_0_), channel_id=1, source_target_pairs={{0,17},{1,16},{2,19},{3,18},{4,21},{5,20},{6,23},{7,22},{8,25},{9,... | collective-permute-start | bytes 110600 | tf_op jit(solution)/shard_map/ppermute | solution.py:366
  86.1 4.5 %collective-permute-start.26 = (bf16[144,128]{1,0:T(8,128)(2,1)S(1)}, bf16[144,128]{1,0:T(8,128)(2,1)S(1)}, u32[]{:S(2)}, u32[]{:S(2)}) collective-permute-start(bf16[144,128]{1,0:T(8,128)(2,1)S(1)} %sum_planes.1.refs_0_), channel_id=1, source_target_pairs={{0,16},{1,17},{2,18},{3,19},{4,20},{5,21},{6,22},{7,23},{8,24},{9,... | collective-permute-start | bytes 110600 | tf_op jit(solution)/shard_map/ppermute | solution.py:366
  87.3 4.0 %collective-permute-start.25 = (bf16[144,128]{1,0:T(8,128)(2,1)S(1)}, bf16[144,128]{1,0:T(8,128)(2,1)S(1)}, u32[]{:S(2)}, u32[]{:S(2)}) collective-permute-start(bf16[144,128]{1,0:T(8,128)(2,1)S(1)} %sum_planes.1.refs_0_), channel_id=1, source_target_pairs={{0,1},{1,0},{2,3},{3,2},{4,5},{5,4},{6,7},{7,6},{8,9},{9,8},{10,11... | collective-permute-start | bytes 110600 | tf_op jit(solution)/shard_map/ppermute | solution.py:366
  91.3 1.4 %collective-permute-start.28 = (bf16[576,128]{1,0:T(8,128)(2,1)S(1)}, bf16[576,128]{1,0:T(8,128)(2,1)S(1)}, u32[]{:S(2)}, u32[]{:S(2)}) collective-permute-start(bf16[576,128]{1,0:T(8,128)(2,1)S(1)} %join_chips.1.own_ref), channel_id=1, source_target_pairs={{0,8},{8,0},{16,24},{24,16},{1,9},{9,1},{17,25},{25,17},{2,10},{10... | collective-permute-start | bytes 442376 | tf_op jit(solution)/shard_map/ppermute | solution.py:370

commit v15 on v14

--- a/solution.py
+++ b/solution.py
@@ -317,6 +317,21 @@
     return terms[0]
 
 
+def hold_kernel(value_ref, after_ref, out_ref):
+    del after_ref
+    out_ref[...] = value_ref[...]
+
+
+def hold(value, after):
+    return call(
+        hold_kernel,
+        "hold",
+        jax.ShapeDtypeStruct(value.shape, value.dtype),
+        [VMEM(), ANY()],
+        moved=4 * value.size,
+    )(value, after)
+
+
 def sum_cores_kernel(quad_ref, keep_ref, other_ref, *refs):
     total = refs[-1]
     total[...] = keep_ref[...] + other_ref[...]
@@ -496,15 +511,16 @@
         moved=quad_size * chunk_moved,
     )(quad, keep, trade_cores(send))
     near = trade(near, 1)
-    far = lax.ppermute(far, "seq", far_pairs)
     distances = range(1, quad_size)
+    parts = [parts[0]] + [trade_chips(parts[distance], distance, inner) for distance in distances]
     plane_sum = call(
         functools.partial(sum_kernel, 1.0),
         "sum_chips",
         chunk_shape,
         [VMEM()] * quad_size,
         moved=chunk_moved,
-    )(parts[0], *[trade_chips(parts[distance], distance, inner) for distance in distances])
+    )(*parts)
+    far = lax.ppermute(hold(far, plane_sum), "seq", far_pairs)
     plane_sums = [plane_sum] + [
         trade(plane_sum, distance) for distance in range(inner, seq_count, inner)
     ]

time: 94 us -> 94.3 us (level)
  waiting for transfers between devices: 28.7 us -> 29.9 us
    ppermute x2, waiting for transfers between devices: 1.36 us -> 2.92 us  [trade_cores(): lax.ppermute(values, 'dp', [(i, i ^ 1) for i in range(lax.axis_size('dp'))])]
    ppermute x6, waiting for transfers between devices: 5.48 us -> 3.97 us  [trade_chips(): return lax.ppermute(values, ('dp', 'seq'), pairs)]
    ppermute x19, waiting for transfers between devices: 21.9 us -> 23.1 us  [trade(): return lax.ppermute(values, 'seq', pairs)]
  transfers between devices with their start and end apart: 29 -> 29, of which waited for: 11 -> 12; matrix products, arithmetic and copies ran while one was open for 0% -> 0% of each run, Pallas kernels for 9% -> 8%
where the time goes in v15:
time: 94.3 us
  starting transfers between devices  48.6 us (52%)
  waiting for transfers between devices  29.9 us (32%)
  Pallas kernels  14.3 us (15%)
    ppermute x19, starting transfers between devices, trade(): return lax.ppermute(values, 'seq', pairs)  40 us
    ppermute x19, waiting for transfers between devices, trade(): return lax.ppermute(values, 'seq', pairs)  23.1 us
    ppermute x6, starting transfers between devices, trade_chips(): return lax.ppermute(values, ('dp', 'seq'), pairs)  7.1 us
    pallas_call x2, Pallas kernels, pack(): call(functools.partial(pack_kernel, distances, regions, per_device), name...  5.3 us
    ppermute x6, waiting for transfers between devices, trade_chips(): return lax.ppermute(values, ('dp', 'seq'), pairs)  3.97 us
    pallas_call x1, Pallas kernels, body(): call(norm_kernel, 'norm_and_gradient', [jax.ShapeDtypeStruct((regions, PA...  3.06 us
    ppermute x2, waiting for transfers between devices, trade_cores(): lax.ppermute(values, 'dp', [(i, i ^ 1) for i in range(lax.axis_size('dp'))])  2.92 us
    pallas_call x1, Pallas kernels, body(): call(decode_kernel, 'decode', [jax.ShapeDtypeStruct(cotangent.shape, jnp....  2.23 us
  transfers between devices with their start and end apart: 29, of which 12 were waited for; matrix products, arithmetic and copies ran while one was open for 0% of the time, Pallas kernels for 8%

profile of v15, /device:TPU:0, one launch (start us, length us, event | category | flops | bytes accessed | tf_op | source)
XLA Modules:
  0.0 94.3 jit_solution(10041450535598019676)
XLA Ops:
  0.6 0.0 copy-start
  0.7 0.0 copy-start.1
  0.7 0.0 copy-start.2
  0.7 2.6 %pack_early.1 = (bf16[3,4,64,128]{3,2,1,0:T(8,128)(2,1)}, bf16[3,4,64,128]{3,2,1,0:T(8,128)(2,1)}, bf16[3,4,64,128]{3,2,1,0:T(8,128)(2,1)}) custom-call(s32[1]{0:T(128)} %bitcast.index_ref, bf16[64,2,2048]{2,1,0:T(2,128)(2,1)} %query_ref.5, bf16[64,2,2048]{2,1,0:T(2,128)(2,1)} %key_ref.5, bf16[64,2,2048]{2,1,0:T(2,128)(2,1)} %value_ref.5), custom_call_target="tpu_custom_call" | custom-call | bytes 1179648 | tf_op jit(solution)/shard_map/pack_early/pallas_call | solution.py:418
  3.3 3.1 %collective-permute-start.3 = (bf16[3,4,64,128]{3,2,1,0:T(8,128)(2,1)}, bf16[3,4,64,128]{3,2,1,0:T(8,128)(2,1)S(1)}, u32[]{:S(2)}, u32[]{:S(2)}) collective-permute-start(bf16[3,4,64,128]{3,2,1,0:T(8,128)(2,1)} %get-tuple-element.34), channel_id=1, source_target_pairs={{0,2},{1,3},{2,0},{3,1},{4,6},{5,7},{6,4},{7,5},{8,10},{9,11},{10,... | collective-permute-start | bytes 589832 | tf_op jit(solution)/shard_map/ppermute | solution.py:363
  6.3 2.6 %collective-permute-start.5 = (bf16[3,4,64,128]{3,2,1,0:T(8,128)(2,1)}, bf16[3,4,64,128]{3,2,1,0:T(8,128)(2,1)S(1)}, u32[]{:S(2)}, u32[]{:S(2)}) collective-permute-start(bf16[3,4,64,128]{3,2,1,0:T(8,128)(2,1)} %get-tuple-element.36), channel_id=1, source_target_pairs={{0,4},{1,5},{2,6},{3,7},{4,0},{5,1},{6,2},{7,3},{8,12},{9,13},{10,... | collective-permute-start | bytes 589832 | tf_op jit(solution)/shard_map/ppermute | solution.py:363
  8.9 1.3 %collective-permute-start.6 = (bf16[3,4,64,128]{3,2,1,0:T(8,128)(2,1)}, bf16[3,4,64,128]{3,2,1,0:T(8,128)(2,1)S(1)}, u32[]{:S(2)}, u32[]{:S(2)}) collective-permute-start(bf16[3,4,64,128]{3,2,1,0:T(8,128)(2,1)} %get-tuple-element.37), channel_id=1, source_target_pairs={{0,5},{1,4},{2,7},{3,6},{4,1},{5,0},{6,3},{7,2},{8,13},{9,12},{10,... | collective-permute-start | bytes 589832 | tf_op jit(solution)/shard_map/ppermute | solution.py:363
  10.2 2.7 %pack_late.1 = (bf16[3,4,64,128]{3,2,1,0:T(8,128)(2,1)}, bf16[3,4,64,128]{3,2,1,0:T(8,128)(2,1)}, bf16[3,4,64,128]{3,2,1,0:T(8,128)(2,1)}, bf16[3,4,64,128]{3,2,1,0:T(8,128)(2,1)}) custom-call(s32[1]{0:T(128)} %bitcast.index_ref, bf16[64,2,2048]{2,1,0:T(2,128)(2,1)} %query_ref.5, bf16[64,2,2048]{2,1,0:T(2,128)(2,1)} %key_ref.5, bf16[64,2,2048]{2,1,0:T(2,128)(2,1)} %value_ref.5), custom_call_target="tpu_custom_call" | custom-call | bytes 1572864 | tf_op jit(solution)/shard_map/pack_late/pallas_call | solution.py:418
  13.0 0.0 copy-start.6
  13.0 0.6 collective-permute-start.2
  13.6 1.4 %collective-permute-start.4 = (bf16[3,4,64,128]{3,2,1,0:T(8,128)(2,1)}, bf16[3,4,64,128]{3,2,1,0:T(8,128)(2,1)S(1)}, u32[]{:S(2)}, u32[]{:S(2)}) collective-permute-start(bf16[3,4,64,128]{3,2,1,0:T(8,128)(2,1)} %get-tuple-element.35), channel_id=1, source_target_pairs={{0,3},{1,2},{2,1},{3,0},{4,7},{5,6},{6,5},{7,4},{8,11},{9,10},{10,... | collective-permute-start | bytes 589832 | tf_op jit(solution)/shard_map/ppermute | solution.py:363
  15.0 0.4 own_chunk.1
  15.4 0.1 collective-permute-done.3.refs_1_
  15.6 0.3 copy-done.8
  15.9 3.6 %collective-permute-start.7 = (bf16[3,4,64,128]{3,2,1,0:T(8,128)(2,1)S(1)}, bf16[3,4,64,128]{3,2,1,0:T(8,128)(2,1)S(1)}, u32[]{:S(2)}, u32[]{:S(2)}) collective-permute-start(bf16[3,4,64,128]{3,2,1,0:T(8,128)(2,1)S(1)} %copy-done.8), channel_id=1, source_target_pairs={{0,6},{1,7},{2,4},{3,5},{4,2},{5,3},{6,0},{7,1},{8,14},{9,15},{10,... | collective-permute-start | bytes 589832 | tf_op jit(solution)/shard_map/ppermute | solution.py:363
  19.5 3.9 %collective-permute-done.5.refs_3_ = bf16[3,4,64,128]{3,2,1,0:T(8,128)(2,1)S(1)} collective-permute-done((bf16[3,4,64,128]{3,2,1,0:T(8,128)(2,1)}, bf16[3,4,64,128]{3,2,1,0:T(8,128)(2,1)S(1)}, u32[]{:S(2)}, u32[]{:S(2)}) %collective-permute-start.5) | collective-permute-done | bytes 196640 | tf_op jit(solution)/shard_map/ppermute | solution.py:363
  23.4 3.7 %collective-permute-start.8 = (bf16[3,4,64,128]{3,2,1,0:T(8,128)(2,1)S(1)}, bf16[3,4,64,128]{3,2,1,0:T(8,128)(2,1)S(1)}, u32[]{:S(2)}, u32[]{:S(2)}) collective-permute-start(bf16[3,4,64,128]{3,2,1,0:T(8,128)(2,1)S(1)} %copy-done.7), channel_id=1, source_target_pairs={{0,7},{1,6},{2,5},{3,4},{4,3},{5,2},{6,1},{7,0},{8,15},{9,14},{10,... | collective-permute-start | bytes 589832 | tf_op jit(solution)/shard_map/ppermute | solution.py:363
  27.1 10.2 %collective-permute-done.6.refs_4_ = bf16[3,4,64,128]{3,2,1,0:T(8,128)(2,1)S(1)} collective-permute-done((bf16[3,4,64,128]{3,2,1,0:T(8,128)(2,1)}, bf16[3,4,64,128]{3,2,1,0:T(8,128)(2,1)S(1)}, u32[]{:S(2)}, u32[]{:S(2)}) %collective-permute-start.6) | collective-permute-done | bytes 196640 | tf_op jit(solution)/shard_map/ppermute | solution.py:363
  37.3 0.3 collective-permute-start
  37.6 0.0 collective-permute-done.2.refs_0_
  37.6 0.7 collective-permute-start.1
  38.2 0.1 fusion.2.lengths_ref
  38.3 0.0 collective-permute-done.4.refs_2_
  38.3 0.0 collective-permute-done.7.refs_5_
  38.3 0.0 collective-permute-done.8.refs_6_
  38.3 2.1 %attend.1 = (bf16[4,64,128]{2,1,0:T(8,128)(2,1)S(1)}, bf16[4,64,128]{2,1,0:T(8,128)(2,1)S(1)}, bf16[4,64,128]{2,1,0:T(8,128)(2,1)S(1)}, bf16[4,64,128]{2,1,0:T(8...) custom-call(s32[1]{0:T(128)} %bitcast.index_ref, ...), custom_call_target="tpu_custom_call" | custom-call | flops 536870912 | bytes 2097152 | tf_op jit(solution)/shard_map/attend/pallas_call | solution.py:465
  40.4 0.0 copy-start.5
  40.5 3.1 %collective-permute-start.9 = (bf16[4,64,128]{2,1,0:T(8,128)(2,1)S(1)}, bf16[4,64,128]{2,1,0:T(8,128)(2,1)S(1)}, u32[]{:S(2)}, u32[]{:S(2)}) collective-permute-start(bf16[4,64,128]{2,1,0:T(8,128)(2,1)S(1)} %get-tuple-element.42), channel_id=1, source_target_pairs={{0,1},{1,0},{2,3},{3,2},{4,5},{5,4},{6,7},{7,6},{8,9},{9,8},{10,11... | collective-permute-start | bytes 196616 | tf_op jit(solution)/shard_map/ppermute | solution.py:363
  43.5 5.3 %collective-permute-start.10 = (bf16[4,64,128]{2,1,0:T(8,128)(2,1)S(1)}, bf16[4,64,128]{2,1,0:T(8,128)(2,1)S(1)}, u32[]{:S(2)}, u32[]{:S(2)}) collective-permute-start(bf16[4,64,128]{2,1,0:T(8,128)(2,1)S(1)} %get-tuple-element.43), channel_id=1, source_target_pairs={{0,2},{1,3},{2,0},{3,1},{4,6},{5,7},{6,4},{7,5},{8,10},{9,11},{10,... | collective-permute-start | bytes 196616 | tf_op jit(solution)/shard_map/ppermute | solution.py:363
  48.8 0.4 collective-permute-start.11
  49.3 0.0 collective-permute-done.near_ref
  49.3 3.7 %collective-permute-start.12 = (bf16[4,64,128]{2,1,0:T(8,128)(2,1)S(1)}, bf16[4,64,128]{2,1,0:T(8,128)(2,1)S(1)}, u32[]{:S(2)}, u32[]{:S(2)}) collective-permute-start(bf16[4,64,128]{2,1,0:T(8,128)(2,1)S(1)} %get-tuple-element.45), channel_id=1, source_target_pairs={{0,4},{1,5},{2,6},{3,7},{4,0},{5,1},{6,2},{7,3},{8,12},{9,13},{10,... | collective-permute-start | bytes 196616 | tf_op jit(solution)/shard_map/ppermute | solution.py:363
  53.0 0.0 collective-permute-done.1.far_ref
  53.0 0.0 collective-permute-start.13
  53.0 0.0 collective-permute-done.9.refs_1_
  53.0 2.4 %collective-permute-start.14 = (bf16[4,64,128]{2,1,0:T(8,128)(2,1)S(1)}, bf16[4,64,128]{2,1,0:T(8,128)(2,1)S(1)}, u32[]{:S(2)}, u32[]{:S(2)}) collective-permute-start(bf16[4,64,128]{2,1,0:T(8,128)(2,1)S(1)} %get-tuple-element.47), channel_id=1, source_target_pairs={{0,6},{1,7},{2,4},{3,5},{4,2},{5,3},{6,0},{7,1},{8,14},{9,15},{10,... | collective-permute-start | bytes 196616 | tf_op jit(solution)/shard_map/ppermute | solution.py:363
  55.3 2.4 %collective-permute-start.15 = (bf16[4,64,128]{2,1,0:T(8,128)(2,1)S(1)}, bf16[4,64,128]{2,1,0:T(8,128)(2,1)S(1)}, u32[]{:S(2)}, u32[]{:S(2)}) collective-permute-start(bf16[4,64,128]{2,1,0:T(8,128)(2,1)S(1)} %get-tuple-element.48), channel_id=1, source_target_pairs={{0,7},{1,6},{2,5},{3,4},{4,3},{5,2},{6,1},{7,0},{8,15},{9,14},{10,... | collective-permute-start | bytes 196616 | tf_op jit(solution)/shard_map/ppermute | solution.py:363
  57.8 0.3 turn_cotangent.1.turned_ref
  58.0 0.0 collective-permute-done.11.refs_3_
  58.0 0.0 collective-permute-done.12.refs_4_
  58.1 2.5 %collective-permute-done.13.refs_5_ = bf16[4,64,128]{2,1,0:T(8,128)(2,1)S(1)} collective-permute-done((bf16[4,64,128]{2,1,0:T(8,128)(2,1)S(1)}, bf16[4,64,128]{2,1,0:T(8,128)(2,1)S(1)}, u32[]{:S(2)}, u32[]{:S(2)}) %collective-permute-start.13) | collective-permute-done | bytes 65568 | tf_op jit(solution)/shard_map/ppermute | solution.py:363
  60.6 1.8 %collective-permute-done.15.refs_7_ = bf16[4,64,128]{2,1,0:T(8,128)(2,1)S(1)} collective-permute-done((bf16[4,64,128]{2,1,0:T(8,128)(2,1)S(1)}, bf16[4,64,128]{2,1,0:T(8,128)(2,1)S(1)}, u32[]{:S(2)}, u32[]{:S(2)}) %collective-permute-start.15) | collective-permute-done | bytes 65568 | tf_op jit(solution)/shard_map/ppermute | solution.py:363
  62.4 3.1 %norm_and_gradient.1 = (bf16[2,4,256,128]{3,2,1,0:T(8,128)(2,1)S(1)}, bf16[2,256,128]{2,1,0:T(8,128)(2,1)S(1)}, bf16[2,256,128]{2,1,0:T(8,128)(2,1)S(1)}, f32[576,128]{1,0:T(8,128)S(1)}, f32[576,128]{1,0:T(8,128)S(1)}) custom-call(s32[2]{0:T(128)S(1)} %copy-done.6, s32[1]{0:T(128)} %bitcast.index_ref, s32[1]{0:T(128)} %bitcast.1.core_ref, ...), custom_call_target="tpu_custom_call" | custom-call | flops 603979776 | bytes 2097152 | tf_op jit(solution)/shard_map/norm_and_gradient/pallas_call | solution.py:488
  65.5 0.1 collective-permute-start.17
  65.6 1.6 %collective-permute-done.17.other_ref = f32[576,128]{1,0:T(8,128)S(1)} collective-permute-done((f32[576,128]{1,0:T(8,128)S(1)}, f32[576,128]{1,0:T(8,128)S(1)}, u32[]{:S(2)}, u32[]{:S(2)}) %collective-permute-start.17) | collective-permute-done | bytes 294944 | tf_op jit(solution)/shard_map/ppermute | solution.py:385
  67.2 1.4 %collective-permute-start.18 = (bf16[144,128]{1,0:T(8,128)(2,1)S(1)}, bf16[144,128]{1,0:T(8,128)(2,1)S(1)}, u32[]{:S(2)}, u32[]{:S(2)}) collective-permute-start(bf16[144,128]{1,0:T(8,128)(2,1)S(1)} %get-tuple-element.55), channel_id=1, source_target_pairs={{0,1},{1,0},{2,3},{3,2},{4,5},{5,4},{6,7},{7,6},{8,9},{9,8},{10,11... | collective-permute-start | bytes 110600 | tf_op jit(solution)/shard_map/ppermute | solution.py:381
  68.6 1.9 %collective-permute-start.19 = (bf16[144,128]{1,0:T(8,128)(2,1)S(1)}, bf16[144,128]{1,0:T(8,128)(2,1)S(1)}, u32[]{:S(2)}, u32[]{:S(2)}) collective-permute-start(bf16[144,128]{1,0:T(8,128)(2,1)S(1)} %get-tuple-element.56), channel_id=1, source_target_pairs={{0,16},{1,17},{2,18},{3,19},{4,20},{5,21},{6,22},{7,23},{8,24},{9,... | collective-permute-start | bytes 110600 | tf_op jit(solution)/shard_map/ppermute | solution.py:381
  70.5 0.2 collective-permute-start.20
  70.7 1.4 %collective-permute-start.16 = (bf16[2,256,128]{2,1,0:T(8,128)(2,1)S(1)}, bf16[2,256,128]{2,1,0:T(8,128)(2,1)S(1)}, u32[]{:S(2)}, u32[]{:S(2)}) collective-permute-start(bf16[2,256,128]{2,1,0:T(8,128)(2,1)S(1)} %get-tuple-element.50), channel_id=1, source_target_pairs={{0,1},{1,0},{2,3},{3,2},{4,5},{5,4},{6,7},{7,6},{8,9},{9,8},{10,11... | collective-permute-start | bytes 393224 | tf_op jit(solution)/shard_map/ppermute | solution.py:363
  72.1 0.5 collective-permute-done.19.refs_2_
  72.6 3.2 %collective-permute-done.20.refs_3_ = bf16[144,128]{1,0:T(8,128)(2,1)S(1)} collective-permute-done((bf16[144,128]{1,0:T(8,128)(2,1)S(1)}, bf16[144,128]{1,0:T(8,128)(2,1)S(1)}, u32[]{:S(2)}, u32[]{:S(2)}) %collective-permute-start.20) | collective-permute-done | bytes 36896 | tf_op jit(solution)/shard_map/ppermute | solution.py:381
  75.8 0.7 collective-permute-start.21
  76.5 4.1 %collective-permute-start.24 = (bf16[144,128]{1,0:T(8,128)(2,1)S(1)}, bf16[144,128]{1,0:T(8,128)(2,1)S(1)}, u32[]{:S(2)}, u32[]{:S(2)}) collective-permute-start(bf16[144,128]{1,0:T(8,128)(2,1)S(1)} %sum_chips.1.after_ref.refs_0_), channel_id=1, source_target_pairs={{0,6},{1,7},{2,4},{3,5},{4,2},{5,3},{6,0},{7,1},{8,14},{9,15},{10,... | collective-permute-start | bytes 110600 | tf_op jit(solution)/shard_map/ppermute | solution.py:363
  80.6 0.8 collective-permute-start.23
  81.4 3.0 %collective-permute-done.24.refs_3_ = bf16[144,128]{1,0:T(8,128)(2,1)S(1)} collective-permute-done((bf16[144,128]{1,0:T(8,128)(2,1)S(1)}, bf16[144,128]{1,0:T(8,128)(2,1)S(1)}, u32[]{:S(2)}, u32[]{:S(2)}) %collective-permute-start.24) | collective-permute-done | bytes 36896 | tf_op jit(solution)/shard_map/ppermute | solution.py:363
  84.4 1.5 %collective-permute-done.23.refs_2_ = bf16[144,128]{1,0:T(8,128)(2,1)S(1)} collective-permute-done((bf16[144,128]{1,0:T(8,128)(2,1)S(1)}, bf16[144,128]{1,0:T(8,128)(2,1)S(1)}, u32[]{:S(2)}, u32[]{:S(2)}) %collective-permute-start.23) | collective-permute-done | bytes 36896 | tf_op jit(solution)/shard_map/ppermute | solution.py:363
  85.9 0.1 collective-permute-start.27
  86.0 2.0 %collective-permute-start.26 = (bf16[144,128]{1,0:T(8,128)(2,1)S(1)}, bf16[144,128]{1,0:T(8,128)(2,1)S(1)}, u32[]{:S(2)}, u32[]{:S(2)}) collective-permute-start(bf16[144,128]{1,0:T(8,128)(2,1)S(1)} %sum_planes.1.refs_0_), channel_id=1, source_target_pairs={{0,16},{1,17},{2,18},{3,19},{4,20},{5,21},{6,22},{7,23},{8,24},{9,... | collective-permute-start | bytes 110600 | tf_op jit(solution)/shard_map/ppermute | solution.py:381
  88.0 1.4 %collective-permute-start.25 = (bf16[144,128]{1,0:T(8,128)(2,1)S(1)}, bf16[144,128]{1,0:T(8,128)(2,1)S(1)}, u32[]{:S(2)}, u32[]{:S(2)}) collective-permute-start(bf16[144,128]{1,0:T(8,128)(2,1)S(1)} %sum_planes.1.refs_0_), channel_id=1, source_target_pairs={{0,1},{1,0},{2,3},{3,2},{4,5},{5,4},{6,7},{7,6},{8,9},{9,8},{10,11... | collective-permute-start | bytes 110600 | tf_op jit(solution)/shard_map/ppermute | solution.py:381
  89.5 2.2 %decode.1 = (bf16[2,4,256,128]{3,2,1,0:T(8,128)(2,1)}, f32[8,128]{1,0:T(8,128)S(1)}) custom-call(s32[1]{0:T(128)} %bitcast.index_ref, bf16[2,4,256,128]{3,2,1,0:T(8,128)(2,1)S(1)} %get-tuple-element.49.image_ref, bf16[2,256,128]{2,1,0:T(8,128)(2,1)S(1)} %collective-permute-done.16.near_ref, bf16[2,256,128]{2,1,0:T(8,128)(2,1)S(1)} %collective-permute-done.21.far_ref, ...), custom_call_target="tpu_custom_call" | custom-call | flops 603979776 | bytes 1048576 | tf_op jit(solution)/shard_map/decode/pallas_call | solution.py:527
  91.7 0.3 collective-permute-done.25.refs_1_
  92.0 0.1 collective-permute-start.28
  92.1 1.4 %collective-permute-done.28.other_ref = bf16[576,128]{1,0:T(8,128)(2,1)S(1)} collective-permute-done((bf16[576,128]{1,0:T(8,128)(2,1)S(1)}, bf16[576,128]{1,0:T(8,128)(2,1)S(1)}, u32[]{:S(2)}, u32[]{:S(2)}) %collective-permute-start.28) | collective-permute-done | bytes 147488 | tf_op jit(solution)/shard_map/ppermute | solution.py:385
  93.4 0.9 spread_sums.1
  (28 shorter events, 0.2 us)
Async XLA Ops:
  0.6 14.3 %copy-start.3 = (bf16[2,4,256,128]{3,2,1,0:T(8,128)(2,1)S(1)}, bf16[2,4,256,128]{3,2,1,0:T(8,128)(2,1)}, u32[]{:S(2)}) copy-start(bf16[2,4,256,128]{3,2,1,0:T(8,128)(2,1)} %cot_ref.1) | copy-start | bytes 1572868
  0.6 14.3 %copy-start = (bf16[64,2,2048]{2,1,0:T(2,128)(2,1)S(1)}, bf16[64,2,2048]{2,1,0:T(2,128)(2,1)}, u32[]{:S(2)}) copy-start(bf16[64,2,2048]{2,1,0:T(2,128)(2,1)} %query_ref.5) | copy-start | bytes 1572868
  0.7 14.3 %copy-start.1 = (bf16[64,2,2048]{2,1,0:T(2,128)(2,1)S(1)}, bf16[64,2,2048]{2,1,0:T(2,128)(2,1)}, u32[]{:S(2)}) copy-start(bf16[64,2,2048]{2,1,0:T(2,128)(2,1)} %key_ref.5) | copy-start | bytes 1572868
  0.7 14.3 %copy-start.2 = (bf16[64,2,2048]{2,1,0:T(2,128)(2,1)S(1)}, bf16[64,2,2048]{2,1,0:T(2,128)(2,1)}, u32[]{:S(2)}) copy-start(bf16[64,2,2048]{2,1,0:T(2,128)(2,1)} %value_ref.5) | copy-start | bytes 1572868
  3.3 12.3 %collective-permute-start.3 = (bf16[3,4,64,128]{3,2,1,0:T(8,128)(2,1)}, bf16[3,4,64,128]{3,2,1,0:T(8,128)(2,1)S(1)}, u32[]{:S(2)}, u32[]{:S(2)}) collective-permute-start(bf16[3,4,64,128]{3,2,1,0:T(8,128)(2,1)} %get-tuple-element.34), channel_id=1, source_target_pairs={{0,2},{1,3},{2,0},{3,1},{4,6},{5,7},{6,4},{7,5},{8,10},{9,11},{10,... | collective-permute-start | bytes 589832 | tf_op jit(solution)/shard_map/ppermute | solution.py:363
  6.3 17.1 %collective-permute-start.5 = (bf16[3,4,64,128]{3,2,1,0:T(8,128)(2,1)}, bf16[3,4,64,128]{3,2,1,0:T(8,128)(2,1)S(1)}, u32[]{:S(2)}, u32[]{:S(2)}) collective-permute-start(bf16[3,4,64,128]{3,2,1,0:T(8,128)(2,1)} %get-tuple-element.36), channel_id=1, source_target_pairs={{0,4},{1,5},{2,6},{3,7},{4,0},{5,1},{6,2},{7,3},{8,12},{9,13},{10,... | collective-permute-start | bytes 589832 | tf_op jit(solution)/shard_map/ppermute | solution.py:363
  8.9 28.3 %collective-permute-start.6 = (bf16[3,4,64,128]{3,2,1,0:T(8,128)(2,1)}, bf16[3,4,64,128]{3,2,1,0:T(8,128)(2,1)S(1)}, u32[]{:S(2)}, u32[]{:S(2)}) collective-permute-start(bf16[3,4,64,128]{3,2,1,0:T(8,128)(2,1)} %get-tuple-element.37), channel_id=1, source_target_pairs={{0,5},{1,4},{2,7},{3,6},{4,1},{5,0},{6,3},{7,2},{8,13},{9,12},{10,... | collective-permute-start | bytes 589832 | tf_op jit(solution)/shard_map/ppermute | solution.py:363
  12.9 10.5 %copy-start.7 = (bf16[3,4,64,128]{3,2,1,0:T(8,128)(2,1)S(1)}, bf16[3,4,64,128]{3,2,1,0:T(8,128)(2,1)}, u32[]{:S(2)}) copy-start(bf16[3,4,64,128]{3,2,1,0:T(8,128)(2,1)} %get-tuple-element.39) | copy-start | bytes 589828
  13.0 25.3 %copy-start.6 = (s32[2]{0:T(128)S(1)}, s32[2]{0:T(128)}, u32[]{:S(2)}) copy-start(s32[2]{0:T(128)} %lengths_ref.1) | copy-start | bytes 28
  13.0 24.6 %collective-permute-start.2 = (bf16[3,4,64,128]{3,2,1,0:T(8,128)(2,1)}, bf16[3,4,64,128]{3,2,1,0:T(8,128)(2,1)S(1)}, u32[]{:S(2)}, u32[]{:S(2)}) collective-permute-start(bf16[3,4,64,128]{3,2,1,0:T(8,128)(2,1)} %get-tuple-element.33), channel_id=1, source_target_pairs={{0,1},{1,0},{2,3},{3,2},{4,5},{5,4},{6,7},{7,6},{8,9},{9,8},{10,11... | collective-permute-start | bytes 589832 | tf_op jit(solution)/shard_map/ppermute | solution.py:363
  13.6 24.8 %collective-permute-start.4 = (bf16[3,4,64,128]{3,2,1,0:T(8,128)(2,1)}, bf16[3,4,64,128]{3,2,1,0:T(8,128)(2,1)S(1)}, u32[]{:S(2)}, u32[]{:S(2)}) collective-permute-start(bf16[3,4,64,128]{3,2,1,0:T(8,128)(2,1)} %get-tuple-element.35), channel_id=1, source_target_pairs={{0,3},{1,2},{2,1},{3,0},{4,7},{5,6},{6,5},{7,4},{8,11},{9,10},{10,... | collective-permute-start | bytes 589832 | tf_op jit(solution)/shard_map/ppermute | solution.py:363
  15.0 0.9 copy-start.8
  15.9 22.4 %collective-permute-start.7 = (bf16[3,4,64,128]{3,2,1,0:T(8,128)(2,1)S(1)}, bf16[3,4,64,128]{3,2,1,0:T(8,128)(2,1)S(1)}, u32[]{:S(2)}, u32[]{:S(2)}) collective-permute-start(bf16[3,4,64,128]{3,2,1,0:T(8,128)(2,1)S(1)} %copy-done.8), channel_id=1, source_target_pairs={{0,6},{1,7},{2,4},{3,5},{4,2},{5,3},{6,0},{7,1},{8,14},{9,15},{10,... | collective-permute-start | bytes 589832 | tf_op jit(solution)/shard_map/ppermute | solution.py:363
  23.4 14.9 %collective-permute-start.8 = (bf16[3,4,64,128]{3,2,1,0:T(8,128)(2,1)S(1)}, bf16[3,4,64,128]{3,2,1,0:T(8,128)(2,1)S(1)}, u32[]{:S(2)}, u32[]{:S(2)}) collective-permute-start(bf16[3,4,64,128]{3,2,1,0:T(8,128)(2,1)S(1)} %copy-done.7), channel_id=1, source_target_pairs={{0,7},{1,6},{2,5},{3,4},{4,3},{5,2},{6,1},{7,0},{8,15},{9,14},{10,... | collective-permute-start | bytes 589832 | tf_op jit(solution)/shard_map/ppermute | solution.py:363
  37.3 12.0 %collective-permute-start = (bf16[2,256,128]{2,1,0:T(8,128)(2,1)S(1)}, bf16[2,256,128]{2,1,0:T(8,128)(2,1)S(1)}, u32[]{:S(2)}, u32[]{:S(2)}) collective-permute-start(bf16[2,256,128]{2,1,0:T(8,128)(2,1)S(1)} %get-tuple-element.31), channel_id=1, source_target_pairs={{0,1},{1,0},{2,3},{3,2},{4,5},{5,4},{6,7},{7,6},{8,9},{9,8},{10,11... | collective-permute-start | bytes 393224 | tf_op jit(solution)/shard_map/ppermute | solution.py:363
  37.6 15.4 %collective-permute-start.1 = (bf16[2,256,128]{2,1,0:T(8,128)(2,1)S(1)}, bf16[2,256,128]{2,1,0:T(8,128)(2,1)S(1)}, u32[]{:S(2)}, u32[]{:S(2)}) collective-permute-start(bf16[2,256,128]{2,1,0:T(8,128)(2,1)S(1)} %get-tuple-element.32), channel_id=1, source_target_pairs={{1,2},{3,4},{5,6},{2,1},{4,3},{6,5},{9,10},{11,12},{13,14},{10,9},... | collective-permute-start | bytes 393224 | tf_op jit(solution)/shard_map/ppermute | solution.py:452
  40.4 22.0 %copy-start.5 = (f32[2048]{0:T(1024)S(1)}, f32[2048]{0:T(1024)}, u32[]{:S(2)}) copy-start(f32[2048]{0:T(1024)} %param.11) | copy-start | bytes 24580
  40.5 12.5 %collective-permute-start.9 = (bf16[4,64,128]{2,1,0:T(8,128)(2,1)S(1)}, bf16[4,64,128]{2,1,0:T(8,128)(2,1)S(1)}, u32[]{:S(2)}, u32[]{:S(2)}) collective-permute-start(bf16[4,64,128]{2,1,0:T(8,128)(2,1)S(1)} %get-tuple-element.42), channel_id=1, source_target_pairs={{0,1},{1,0},{2,3},{3,2},{4,5},{5,4},{6,7},{7,6},{8,9},{9,8},{10,11... | collective-permute-start | bytes 196616 | tf_op jit(solution)/shard_map/ppermute | solution.py:363
  43.5 11.8 %collective-permute-start.10 = (bf16[4,64,128]{2,1,0:T(8,128)(2,1)S(1)}, bf16[4,64,128]{2,1,0:T(8,128)(2,1)S(1)}, u32[]{:S(2)}, u32[]{:S(2)}) collective-permute-start(bf16[4,64,128]{2,1,0:T(8,128)(2,1)S(1)} %get-tuple-element.43), channel_id=1, source_target_pairs={{0,2},{1,3},{2,0},{3,1},{4,6},{5,7},{6,4},{7,5},{8,10},{9,11},{10,... | collective-permute-start | bytes 196616 | tf_op jit(solution)/shard_map/ppermute | solution.py:363
  48.8 9.2 %collective-permute-start.11 = (bf16[4,64,128]{2,1,0:T(8,128)(2,1)S(1)}, bf16[4,64,128]{2,1,0:T(8,128)(2,1)S(1)}, u32[]{:S(2)}, u32[]{:S(2)}) collective-permute-start(bf16[4,64,128]{2,1,0:T(8,128)(2,1)S(1)} %get-tuple-element.44), channel_id=1, source_target_pairs={{0,3},{1,2},{2,1},{3,0},{4,7},{5,6},{6,5},{7,4},{8,11},{9,10},{10,... | collective-permute-start | bytes 196616 | tf_op jit(solution)/shard_map/ppermute | solution.py:363
  49.3 8.8 %collective-permute-start.12 = (bf16[4,64,128]{2,1,0:T(8,128)(2,1)S(1)}, bf16[4,64,128]{2,1,0:T(8,128)(2,1)S(1)}, u32[]{:S(2)}, u32[]{:S(2)}) collective-permute-start(bf16[4,64,128]{2,1,0:T(8,128)(2,1)S(1)} %get-tuple-element.45), channel_id=1, source_target_pairs={{0,4},{1,5},{2,6},{3,7},{4,0},{5,1},{6,2},{7,3},{8,12},{9,13},{10,... | collective-permute-start | bytes 196616 | tf_op jit(solution)/shard_map/ppermute | solution.py:363
  53.0 7.7 %collective-permute-start.13 = (bf16[4,64,128]{2,1,0:T(8,128)(2,1)S(1)}, bf16[4,64,128]{2,1,0:T(8,128)(2,1)S(1)}, u32[]{:S(2)}, u32[]{:S(2)}) collective-permute-start(bf16[4,64,128]{2,1,0:T(8,128)(2,1)S(1)} %get-tuple-element.46), channel_id=1, source_target_pairs={{0,5},{1,4},{2,7},{3,6},{4,1},{5,0},{6,3},{7,2},{8,13},{9,12},{10,... | collective-permute-start | bytes 196616 | tf_op jit(solution)/shard_map/ppermute | solution.py:363
  53.0 7.7 %collective-permute-start.14 = (bf16[4,64,128]{2,1,0:T(8,128)(2,1)S(1)}, bf16[4,64,128]{2,1,0:T(8,128)(2,1)S(1)}, u32[]{:S(2)}, u32[]{:S(2)}) collective-permute-start(bf16[4,64,128]{2,1,0:T(8,128)(2,1)S(1)} %get-tuple-element.47), channel_id=1, source_target_pairs={{0,6},{1,7},{2,4},{3,5},{4,2},{5,3},{6,0},{7,1},{8,14},{9,15},{10,... | collective-permute-start | bytes 196616 | tf_op jit(solution)/shard_map/ppermute | solution.py:363
  55.3 7.1 %collective-permute-start.15 = (bf16[4,64,128]{2,1,0:T(8,128)(2,1)S(1)}, bf16[4,64,128]{2,1,0:T(8,128)(2,1)S(1)}, u32[]{:S(2)}, u32[]{:S(2)}) collective-permute-start(bf16[4,64,128]{2,1,0:T(8,128)(2,1)S(1)} %get-tuple-element.48), channel_id=1, source_target_pairs={{0,7},{1,6},{2,5},{3,4},{4,3},{5,2},{6,1},{7,0},{8,15},{9,14},{10,... | collective-permute-start | bytes 196616 | tf_op jit(solution)/shard_map/ppermute | solution.py:363
  62.4 27.0 %copy-start.4 = (bf16[9,128,128]{2,1,0:T(8,128)(2,1)S(1)}, bf16[9,128,128]{2,1,0:T(8,128)(2,1)}, u32[]{:S(2)}) copy-start(bf16[9,128,128]{2,1,0:T(8,128)(2,1)} %param.12) | copy-start | bytes 884740
  65.5 1.6 %collective-permute-start.17 = (f32[576,128]{1,0:T(8,128)S(1)}, f32[576,128]{1,0:T(8,128)S(1)}, u32[]{:S(2)}, u32[]{:S(2)}) collective-permute-start(f32[576,128]{1,0:T(8,128)S(1)} %get-tuple-element.53), channel_id=1, source_target_pairs={{0,8},{8,0},{16,24},{24,16},{1,9},{9,1},{17,25},{25,17},{2,10},{10... | collective-permute-start | bytes 884744 | tf_op jit(solution)/shard_map/ppermute | solution.py:385
  67.2 4.9 %collective-permute-start.18 = (bf16[144,128]{1,0:T(8,128)(2,1)S(1)}, bf16[144,128]{1,0:T(8,128)(2,1)S(1)}, u32[]{:S(2)}, u32[]{:S(2)}) collective-permute-start(bf16[144,128]{1,0:T(8,128)(2,1)S(1)} %get-tuple-element.55), channel_id=1, source_target_pairs={{0,1},{1,0},{2,3},{3,2},{4,5},{5,4},{6,7},{7,6},{8,9},{9,8},{10,11... | collective-permute-start | bytes 110600 | tf_op jit(solution)/shard_map/ppermute | solution.py:381
  68.6 4.0 %collective-permute-start.19 = (bf16[144,128]{1,0:T(8,128)(2,1)S(1)}, bf16[144,128]{1,0:T(8,128)(2,1)S(1)}, u32[]{:S(2)}, u32[]{:S(2)}) collective-permute-start(bf16[144,128]{1,0:T(8,128)(2,1)S(1)} %get-tuple-element.56), channel_id=1, source_target_pairs={{0,16},{1,17},{2,18},{3,19},{4,20},{5,21},{6,22},{7,23},{8,24},{9,... | collective-permute-start | bytes 110600 | tf_op jit(solution)/shard_map/ppermute | solution.py:381
  70.5 5.3 %collective-permute-start.20 = (bf16[144,128]{1,0:T(8,128)(2,1)S(1)}, bf16[144,128]{1,0:T(8,128)(2,1)S(1)}, u32[]{:S(2)}, u32[]{:S(2)}) collective-permute-start(bf16[144,128]{1,0:T(8,128)(2,1)S(1)} %get-tuple-element.57), channel_id=1, source_target_pairs={{0,17},{1,16},{2,19},{3,18},{4,21},{5,20},{6,23},{7,22},{8,25},{9,... | collective-permute-start | bytes 110600 | tf_op jit(solution)/shard_map/ppermute | solution.py:381
  70.7 18.7 %collective-permute-start.16 = (bf16[2,256,128]{2,1,0:T(8,128)(2,1)S(1)}, bf16[2,256,128]{2,1,0:T(8,128)(2,1)S(1)}, u32[]{:S(2)}, u32[]{:S(2)}) collective-permute-start(bf16[2,256,128]{2,1,0:T(8,128)(2,1)S(1)} %get-tuple-element.50), channel_id=1, source_target_pairs={{0,1},{1,0},{2,3},{3,2},{4,5},{5,4},{6,7},{7,6},{8,9},{9,8},{10,11... | collective-permute-start | bytes 393224 | tf_op jit(solution)/shard_map/ppermute | solution.py:363
  75.8 13.6 %collective-permute-start.21 = (bf16[2,256,128]{2,1,0:T(8,128)(2,1)S(1)}, bf16[2,256,128]{2,1,0:T(8,128)(2,1)S(1)}, u32[]{:S(2)}, u32[]{:S(2)}) collective-permute-start(bf16[2,256,128]{2,1,0:T(8,128)(2,1)S(1)} %hold.1), channel_id=1, source_target_pairs={{1,2},{3,4},{5,6},{2,1},{4,3},{6,5},{9,10},{11,12},{13,14},{10,9},... | collective-permute-start | bytes 393224 | tf_op jit(solution)/shard_map/ppermute | solution.py:523
  76.5 7.9 %collective-permute-start.24 = (bf16[144,128]{1,0:T(8,128)(2,1)S(1)}, bf16[144,128]{1,0:T(8,128)(2,1)S(1)}, u32[]{:S(2)}, u32[]{:S(2)}) collective-permute-start(bf16[144,128]{1,0:T(8,128)(2,1)S(1)} %sum_chips.1.after_ref.refs_0_), channel_id=1, source_target_pairs={{0,6},{1,7},{2,4},{3,5},{4,2},{5,3},{6,0},{7,1},{8,14},{9,15},{10,... | collective-permute-start | bytes 110600 | tf_op jit(solution)/shard_map/ppermute | solution.py:363
  80.6 5.2 %collective-permute-start.23 = (bf16[144,128]{1,0:T(8,128)(2,1)S(1)}, bf16[144,128]{1,0:T(8,128)(2,1)S(1)}, u32[]{:S(2)}, u32[]{:S(2)}) collective-permute-start(bf16[144,128]{1,0:T(8,128)(2,1)S(1)} %sum_chips.1.after_ref.refs_0_), channel_id=1, source_target_pairs={{0,4},{1,5},{2,6},{3,7},{4,0},{5,1},{6,2},{7,3},{8,12},{9,13},{10,... | collective-permute-start | bytes 110600 | tf_op jit(solution)/shard_map/ppermute | solution.py:363
  81.4 4.5 %collective-permute-start.22 = (bf16[144,128]{1,0:T(8,128)(2,1)S(1)}, bf16[144,128]{1,0:T(8,128)(2,1)S(1)}, u32[]{:S(2)}, u32[]{:S(2)}) collective-permute-start(bf16[144,128]{1,0:T(8,128)(2,1)S(1)} %sum_chips.1.after_ref.refs_0_), channel_id=1, source_target_pairs={{0,2},{1,3},{2,0},{3,1},{4,6},{5,7},{6,4},{7,5},{8,10},{9,11},{10,... | collective-permute-start | bytes 110600 | tf_op jit(solution)/shard_map/ppermute | solution.py:363
  85.9 5.8 %collective-permute-start.27 = (bf16[144,128]{1,0:T(8,128)(2,1)S(1)}, bf16[144,128]{1,0:T(8,128)(2,1)S(1)}, u32[]{:S(2)}, u32[]{:S(2)}) collective-permute-start(bf16[144,128]{1,0:T(8,128)(2,1)S(1)} %sum_planes.1.refs_0_), channel_id=1, source_target_pairs={{0,17},{1,16},{2,19},{3,18},{4,21},{5,20},{6,23},{7,22},{8,25},{9,... | collective-permute-start | bytes 110600 | tf_op jit(solution)/shard_map/ppermute | solution.py:381
  86.0 5.7 %collective-permute-start.26 = (bf16[144,128]{1,0:T(8,128)(2,1)S(1)}, bf16[144,128]{1,0:T(8,128)(2,1)S(1)}, u32[]{:S(2)}, u32[]{:S(2)}) collective-permute-start(bf16[144,128]{1,0:T(8,128)(2,1)S(1)} %sum_planes.1.refs_0_), channel_id=1, source_target_pairs={{0,16},{1,17},{2,18},{3,19},{4,20},{5,21},{6,22},{7,23},{8,24},{9,... | collective-permute-start | bytes 110600 | tf_op jit(solution)/shard_map/ppermute | solution.py:381
  88.0 4.0 %collective-permute-start.25 = (bf16[144,128]{1,0:T(8,128)(2,1)S(1)}, bf16[144,128]{1,0:T(8,128)(2,1)S(1)}, u32[]{:S(2)}, u32[]{:S(2)}) collective-permute-start(bf16[144,128]{1,0:T(8,128)(2,1)S(1)} %sum_planes.1.refs_0_), channel_id=1, source_target_pairs={{0,1},{1,0},{2,3},{3,2},{4,5},{5,4},{6,7},{7,6},{8,9},{9,8},{10,11... | collective-permute-start | bytes 110600 | tf_op jit(solution)/shard_map/ppermute | solution.py:381
  92.0 1.4 %collective-permute-start.28 = (bf16[576,128]{1,0:T(8,128)(2,1)S(1)}, bf16[576,128]{1,0:T(8,128)(2,1)S(1)}, u32[]{:S(2)}, u32[]{:S(2)}) collective-permute-start(bf16[576,128]{1,0:T(8,128)(2,1)S(1)} %join_chips.1.own_ref), channel_id=1, source_target_pairs={{0,8},{8,0},{16,24},{24,16},{1,9},{9,1},{17,25},{25,17},{2,10},{10... | collective-permute-start | bytes 442376 | tf_op jit(solution)/shard_map/ppermute | solution.py:385

commit v16 on v14

--- a/solution.py
+++ b/solution.py
@@ -224,9 +224,9 @@
                     out_ref[down * width : (down + 1) * width, start : start + columns] = turned
 
 
-def norm_kernel(lengths_ref, index_ref, core_ref, gain_ref, turned_ref, *refs):
+def norm_kernel(order, lengths_ref, index_ref, core_ref, gain_ref, turned_ref, *refs):
     image_ref, near_ref, far_ref, keep_ref, send_ref, attended, pixels, windows, grads = refs[-9:]
-    for distance, ref in enumerate(refs[:-9]):
+    for distance, ref in zip(order, refs):
         attended[lax.bitwise_xor(index_ref[0], distance)] = ref[...]
     heads = gain_ref.shape[0]
     regions = image_ref.shape[0]
@@ -456,7 +456,8 @@
         moved=4 * local_bytes,
         exps=per_device * capacity * capacity,
     )(index, item_lengths, *[packed[distance] for distance in order])
-    attended = [mixed[0]] + [trade(mixed[distance], distance) for distance in order[:-1]]
+    back = list(range(half, seq_count)) + list(range(2, half)) + [1]
+    attended = [trade(mixed[distance], distance) for distance in back] + [mixed[0]]
 
     turned = call(
         turn_kernel,
@@ -471,7 +472,7 @@
     conv_flops = 18 * pixel_rows * width * width
     chunk_moved = 8 * chunk_rows * width
     image, near, far, keep, send = call(
-        norm_kernel,
+        functools.partial(norm_kernel, back + [0]),
         "norm_and_gradient",
         [jax.ShapeDtypeStruct((regions, PATCH, columns, width), jnp.bfloat16)]
         + [edge_shape] * 2

time: 94 us -> 93.2 us (level)
    ppermute x19, starting transfers between devices: 39.7 us -> 38.6 us  [trade(): return lax.ppermute(values, 'seq', pairs)]
  transfers between devices with their start and end apart: 29 -> 29, of which waited for: 11 -> 14; matrix products, arithmetic and copies ran while one was open for 0% -> 0% of each run, Pallas kernels for 9% -> 8%
where the time goes in v16:
time: 93.2 us; the launch traced here: 93.1 us
  starting transfers between devices  48 us (52%)
  waiting for transfers between devices  29.4 us (32%)
  Pallas kernels  14.3 us (15%)
    ppermute x19, starting transfers between devices, trade(): return lax.ppermute(values, 'seq', pairs)  38.6 us
    ppermute x19, waiting for transfers between devices, trade(): return lax.ppermute(values, 'seq', pairs)  22.2 us
    ppermute x6, starting transfers between devices, trade_chips(): return lax.ppermute(values, ('dp', 'seq'), pairs)  7.78 us
    ppermute x6, waiting for transfers between devices, trade_chips(): return lax.ppermute(values, ('dp', 'seq'), pairs)  5.85 us
    pallas_call x2, Pallas kernels, pack(): call(functools.partial(pack_kernel, distances, regions, per_device), name...  5.3 us
    pallas_call x1, Pallas kernels, body(): call(functools.partial(norm_kernel, back + [0]), 'norm_and_gradient', [ja...  3.06 us
    pallas_call x1, Pallas kernels, body(): call(decode_kernel, 'decode', [jax.ShapeDtypeStruct(cotangent.shape, jnp....  2.23 us
    pallas_call x1, Pallas kernels, body(): call(functools.partial(attend_kernel, block_rows, group, order), 'attend'...  2.09 us
  transfers between devices with their start and end apart: 29, of which 14 were waited for; matrix products, arithmetic and copies ran while one was open for 0% of the time, Pallas kernels for 8%

profile of v16, /device:TPU:0, one launch (start us, length us, event | category | flops | bytes accessed | tf_op | source)
XLA Modules:
  0.0 93.1 jit_solution(10846784650102007549)
XLA Ops:
  0.6 0.0 copy-start
  0.7 0.0 copy-start.1
  0.7 0.0 copy-start.2
  0.7 2.6 %pack_early.1 = (bf16[3,4,64,128]{3,2,1,0:T(8,128)(2,1)}, bf16[3,4,64,128]{3,2,1,0:T(8,128)(2,1)}, bf16[3,4,64,128]{3,2,1,0:T(8,128)(2,1)}) custom-call(s32[1]{0:T(128)} %bitcast.index_ref, bf16[64,2,2048]{2,1,0:T(2,128)(2,1)} %query_ref.5, bf16[64,2,2048]{2,1,0:T(2,128)(2,1)} %key_ref.5, bf16[64,2,2048]{2,1,0:T(2,128)(2,1)} %value_ref.5), custom_call_target="tpu_custom_call" | custom-call | bytes 1179648 | tf_op jit(solution)/shard_map/pack_early/pallas_call | solution.py:403
  3.3 3.1 %collective-permute-start.3 = (bf16[3,4,64,128]{3,2,1,0:T(8,128)(2,1)}, bf16[3,4,64,128]{3,2,1,0:T(8,128)(2,1)S(1)}, u32[]{:S(2)}, u32[]{:S(2)}) collective-permute-start(bf16[3,4,64,128]{3,2,1,0:T(8,128)(2,1)} %get-tuple-element.34), channel_id=1, source_target_pairs={{0,2},{1,3},{2,0},{3,1},{4,6},{5,7},{6,4},{7,5},{8,10},{9,11},{10,... | collective-permute-start | bytes 589832 | tf_op jit(solution)/shard_map/ppermute | solution.py:348
  6.3 2.6 %collective-permute-start.5 = (bf16[3,4,64,128]{3,2,1,0:T(8,128)(2,1)}, bf16[3,4,64,128]{3,2,1,0:T(8,128)(2,1)S(1)}, u32[]{:S(2)}, u32[]{:S(2)}) collective-permute-start(bf16[3,4,64,128]{3,2,1,0:T(8,128)(2,1)} %get-tuple-element.36), channel_id=1, source_target_pairs={{0,4},{1,5},{2,6},{3,7},{4,0},{5,1},{6,2},{7,3},{8,12},{9,13},{10,... | collective-permute-start | bytes 589832 | tf_op jit(solution)/shard_map/ppermute | solution.py:348
  8.9 1.3 %collective-permute-start.6 = (bf16[3,4,64,128]{3,2,1,0:T(8,128)(2,1)}, bf16[3,4,64,128]{3,2,1,0:T(8,128)(2,1)S(1)}, u32[]{:S(2)}, u32[]{:S(2)}) collective-permute-start(bf16[3,4,64,128]{3,2,1,0:T(8,128)(2,1)} %get-tuple-element.37), channel_id=1, source_target_pairs={{0,5},{1,4},{2,7},{3,6},{4,1},{5,0},{6,3},{7,2},{8,13},{9,12},{10,... | collective-permute-start | bytes 589832 | tf_op jit(solution)/shard_map/ppermute | solution.py:348
  10.2 2.7 %pack_late.1 = (bf16[3,4,64,128]{3,2,1,0:T(8,128)(2,1)}, bf16[3,4,64,128]{3,2,1,0:T(8,128)(2,1)}, bf16[3,4,64,128]{3,2,1,0:T(8,128)(2,1)}, bf16[3,4,64,128]{3,2,1,0:T(8,128)(2,1)}) custom-call(s32[1]{0:T(128)} %bitcast.index_ref, bf16[64,2,2048]{2,1,0:T(2,128)(2,1)} %query_ref.5, bf16[64,2,2048]{2,1,0:T(2,128)(2,1)} %key_ref.5, bf16[64,2,2048]{2,1,0:T(2,128)(2,1)} %value_ref.5), custom_call_target="tpu_custom_call" | custom-call | bytes 1572864 | tf_op jit(solution)/shard_map/pack_late/pallas_call | solution.py:403
  13.0 0.0 copy-start.6
  13.0 0.6 collective-permute-start.2
  13.6 1.4 %collective-permute-start.4 = (bf16[3,4,64,128]{3,2,1,0:T(8,128)(2,1)}, bf16[3,4,64,128]{3,2,1,0:T(8,128)(2,1)S(1)}, u32[]{:S(2)}, u32[]{:S(2)}) collective-permute-start(bf16[3,4,64,128]{3,2,1,0:T(8,128)(2,1)} %get-tuple-element.35), channel_id=1, source_target_pairs={{0,3},{1,2},{2,1},{3,0},{4,7},{5,6},{6,5},{7,4},{8,11},{9,10},{10,... | collective-permute-start | bytes 589832 | tf_op jit(solution)/shard_map/ppermute | solution.py:348
  15.0 0.4 own_chunk.1
  15.4 0.1 collective-permute-done.3.refs_1_
  15.6 0.3 copy-done.8
  15.9 3.6 %collective-permute-start.7 = (bf16[3,4,64,128]{3,2,1,0:T(8,128)(2,1)S(1)}, bf16[3,4,64,128]{3,2,1,0:T(8,128)(2,1)S(1)}, u32[]{:S(2)}, u32[]{:S(2)}) collective-permute-start(bf16[3,4,64,128]{3,2,1,0:T(8,128)(2,1)S(1)} %copy-done.8), channel_id=1, source_target_pairs={{0,6},{1,7},{2,4},{3,5},{4,2},{5,3},{6,0},{7,1},{8,14},{9,15},{10,... | collective-permute-start | bytes 589832 | tf_op jit(solution)/shard_map/ppermute | solution.py:348
  19.5 3.9 %collective-permute-done.5.refs_3_ = bf16[3,4,64,128]{3,2,1,0:T(8,128)(2,1)S(1)} collective-permute-done((bf16[3,4,64,128]{3,2,1,0:T(8,128)(2,1)}, bf16[3,4,64,128]{3,2,1,0:T(8,128)(2,1)S(1)}, u32[]{:S(2)}, u32[]{:S(2)}) %collective-permute-start.5) | collective-permute-done | bytes 196640 | tf_op jit(solution)/shard_map/ppermute | solution.py:348
  23.4 3.7 %collective-permute-start.8 = (bf16[3,4,64,128]{3,2,1,0:T(8,128)(2,1)S(1)}, bf16[3,4,64,128]{3,2,1,0:T(8,128)(2,1)S(1)}, u32[]{:S(2)}, u32[]{:S(2)}) collective-permute-start(bf16[3,4,64,128]{3,2,1,0:T(8,128)(2,1)S(1)} %copy-done.7), channel_id=1, source_target_pairs={{0,7},{1,6},{2,5},{3,4},{4,3},{5,2},{6,1},{7,0},{8,15},{9,14},{10,... | collective-permute-start | bytes 589832 | tf_op jit(solution)/shard_map/ppermute | solution.py:348
  27.1 10.2 %collective-permute-done.6.refs_4_ = bf16[3,4,64,128]{3,2,1,0:T(8,128)(2,1)S(1)} collective-permute-done((bf16[3,4,64,128]{3,2,1,0:T(8,128)(2,1)}, bf16[3,4,64,128]{3,2,1,0:T(8,128)(2,1)S(1)}, u32[]{:S(2)}, u32[]{:S(2)}) %collective-permute-start.6) | collective-permute-done | bytes 196640 | tf_op jit(solution)/shard_map/ppermute | solution.py:348
  37.3 0.3 collective-permute-start
  37.6 0.0 collective-permute-done.2.refs_0_
  37.6 0.7 collective-permute-start.1
  38.2 0.1 fusion.2.lengths_ref
  38.3 0.0 collective-permute-done.4.refs_2_
  38.3 0.0 collective-permute-done.7.refs_5_
  38.3 0.0 collective-permute-done.8.refs_6_
  38.3 2.1 %attend.1 = (bf16[4,64,128]{2,1,0:T(8,128)(2,1)S(1)}, bf16[4,64,128]{2,1,0:T(8,128)(2,1)S(1)}, bf16[4,64,128]{2,1,0:T(8,128)(2,1)S(1)}, bf16[4,64,128]{2,1,0:T(8...) custom-call(s32[1]{0:T(128)} %bitcast.index_ref, ...), custom_call_target="tpu_custom_call" | custom-call | flops 536870912 | bytes 2097152 | tf_op jit(solution)/shard_map/attend/pallas_call | solution.py:450
  40.4 0.0 copy-start.5
  40.4 9.0 %collective-permute-start.9 = (bf16[4,64,128]{2,1,0:T(8,128)(2,1)S(1)}, bf16[4,64,128]{2,1,0:T(8,128)(2,1)S(1)}, u32[]{:S(2)}, u32[]{:S(2)}) collective-permute-start(bf16[4,64,128]{2,1,0:T(8,128)(2,1)S(1)} %get-tuple-element.41), channel_id=1, source_target_pairs={{0,4},{1,5},{2,6},{3,7},{4,0},{5,1},{6,2},{7,3},{8,12},{9,13},{10,... | collective-permute-start | bytes 196616 | tf_op jit(solution)/shard_map/ppermute | solution.py:348
  49.5 1.2 %collective-permute-start.11 = (bf16[4,64,128]{2,1,0:T(8,128)(2,1)S(1)}, bf16[4,64,128]{2,1,0:T(8,128)(2,1)S(1)}, u32[]{:S(2)}, u32[]{:S(2)}) collective-permute-start(bf16[4,64,128]{2,1,0:T(8,128)(2,1)S(1)} %get-tuple-element.43), channel_id=1, source_target_pairs={{0,6},{1,7},{2,4},{3,5},{4,2},{5,3},{6,0},{7,1},{8,14},{9,15},{10,... | collective-permute-start | bytes 196616 | tf_op jit(solution)/shard_map/ppermute | solution.py:348
  50.7 3.6 %collective-permute-start.12 = (bf16[4,64,128]{2,1,0:T(8,128)(2,1)S(1)}, bf16[4,64,128]{2,1,0:T(8,128)(2,1)S(1)}, u32[]{:S(2)}, u32[]{:S(2)}) collective-permute-start(bf16[4,64,128]{2,1,0:T(8,128)(2,1)S(1)} %get-tuple-element.44), channel_id=1, source_target_pairs={{0,7},{1,6},{2,5},{3,4},{4,3},{5,2},{6,1},{7,0},{8,15},{9,14},{10,... | collective-permute-start | bytes 196616 | tf_op jit(solution)/shard_map/ppermute | solution.py:348
  54.3 0.0 collective-permute-start.13
  54.3 1.3 %collective-permute-done.9.refs_0_ = bf16[4,64,128]{2,1,0:T(8,128)(2,1)S(1)} collective-permute-done((bf16[4,64,128]{2,1,0:T(8,128)(2,1)S(1)}, bf16[4,64,128]{2,1,0:T(8,128)(2,1)S(1)}, u32[]{:S(2)}, u32[]{:S(2)}) %collective-permute-start.9) | collective-permute-done | bytes 65568 | tf_op jit(solution)/shard_map/ppermute | solution.py:348
  55.6 0.6 collective-permute-start.14
  56.2 1.5 %collective-permute-done.10.refs_1_ = bf16[4,64,128]{2,1,0:T(8,128)(2,1)S(1)} collective-permute-done((bf16[4,64,128]{2,1,0:T(8,128)(2,1)S(1)}, bf16[4,64,128]{2,1,0:T(8,128)(2,1)S(1)}, u32[]{:S(2)}, u32[]{:S(2)}) %collective-permute-start.10) | collective-permute-done | bytes 65568 | tf_op jit(solution)/shard_map/ppermute | solution.py:348
  57.7 1.6 %collective-permute-start.15 = (bf16[4,64,128]{2,1,0:T(8,128)(2,1)S(1)}, bf16[4,64,128]{2,1,0:T(8,128)(2,1)S(1)}, u32[]{:S(2)}, u32[]{:S(2)}) collective-permute-start(bf16[4,64,128]{2,1,0:T(8,128)(2,1)S(1)} %get-tuple-element.47), channel_id=1, source_target_pairs={{0,1},{1,0},{2,3},{3,2},{4,5},{5,4},{6,7},{7,6},{8,9},{9,8},{10,11... | collective-permute-start | bytes 196616 | tf_op jit(solution)/shard_map/ppermute | solution.py:348
  59.3 0.3 turn_cotangent.1.turned_ref
  59.5 0.0 collective-permute-done.12.refs_3_
  59.5 0.0 collective-permute-done.13.refs_4_
  59.6 1.2 %collective-permute-done.14.refs_5_ = bf16[4,64,128]{2,1,0:T(8,128)(2,1)S(1)} collective-permute-done((bf16[4,64,128]{2,1,0:T(8,128)(2,1)S(1)}, bf16[4,64,128]{2,1,0:T(8,128)(2,1)S(1)}, u32[]{:S(2)}, u32[]{:S(2)}) %collective-permute-start.14) | collective-permute-done | bytes 65568 | tf_op jit(solution)/shard_map/ppermute | solution.py:348
  60.8 1.2 %collective-permute-done.15.refs_6_ = bf16[4,64,128]{2,1,0:T(8,128)(2,1)S(1)} collective-permute-done((bf16[4,64,128]{2,1,0:T(8,128)(2,1)S(1)}, bf16[4,64,128]{2,1,0:T(8,128)(2,1)S(1)}, u32[]{:S(2)}, u32[]{:S(2)}) %collective-permute-start.15) | collective-permute-done | bytes 65568 | tf_op jit(solution)/shard_map/ppermute | solution.py:348
  62.0 3.1 %norm_and_gradient.1 = (bf16[2,4,256,128]{3,2,1,0:T(8,128)(2,1)S(1)}, bf16[2,256,128]{2,1,0:T(8,128)(2,1)S(1)}, bf16[2,256,128]{2,1,0:T(8,128)(2,1)S(1)}, f32[576,128]{1,0:T(8,128)S(1)}, f32[576,128]{1,0:T(8,128)S(1)}) custom-call(s32[2]{0:T(128)S(1)} %copy-done.6, s32[1]{0:T(128)} %bitcast.index_ref, s32[1]{0:T(128)} %bitcast.1.core_ref, ...), custom_call_target="tpu_custom_call" | custom-call | flops 603979776 | bytes 2097152 | tf_op jit(solution)/shard_map/norm_and_gradient/pallas_call | solution.py:474
  65.0 0.1 collective-permute-start.18
  65.1 1.6 %collective-permute-start.16 = (bf16[2,256,128]{2,1,0:T(8,128)(2,1)S(1)}, bf16[2,256,128]{2,1,0:T(8,128)(2,1)S(1)}, u32[]{:S(2)}, u32[]{:S(2)}) collective-permute-start(bf16[2,256,128]{2,1,0:T(8,128)(2,1)S(1)} %get-tuple-element.50), channel_id=1, source_target_pairs={{0,1},{1,0},{2,3},{3,2},{4,5},{5,4},{6,7},{7,6},{8,9},{9,8},{10,11... | collective-permute-start | bytes 393224 | tf_op jit(solution)/shard_map/ppermute | solution.py:348
  66.7 0.8 collective-permute-start.17
  67.6 0.0 collective-permute-done.18.other_ref
  67.6 0.1 sum_cores.1
  67.7 2.6 %collective-permute-start.19 = (bf16[144,128]{1,0:T(8,128)(2,1)S(1)}, bf16[144,128]{1,0:T(8,128)(2,1)S(1)}, u32[]{:S(2)}, u32[]{:S(2)}) collective-permute-start(bf16[144,128]{1,0:T(8,128)(2,1)S(1)} %get-tuple-element.57), channel_id=1, source_target_pairs={{0,1},{1,0},{2,3},{3,2},{4,5},{5,4},{6,7},{7,6},{8,9},{9,8},{10,11... | collective-permute-start | bytes 110600 | tf_op jit(solution)/shard_map/ppermute | solution.py:366
  70.3 1.6 %collective-permute-start.20 = (bf16[144,128]{1,0:T(8,128)(2,1)S(1)}, bf16[144,128]{1,0:T(8,128)(2,1)S(1)}, u32[]{:S(2)}, u32[]{:S(2)}) collective-permute-start(bf16[144,128]{1,0:T(8,128)(2,1)S(1)} %get-tuple-element.58), channel_id=1, source_target_pairs={{0,16},{1,17},{2,18},{3,19},{4,20},{5,21},{6,22},{7,23},{8,24},{9,... | collective-permute-start | bytes 110600 | tf_op jit(solution)/shard_map/ppermute | solution.py:366
  71.9 2.1 %collective-permute-done.19.refs_1_ = bf16[144,128]{1,0:T(8,128)(2,1)S(1)} collective-permute-done((bf16[144,128]{1,0:T(8,128)(2,1)S(1)}, bf16[144,128]{1,0:T(8,128)(2,1)S(1)}, u32[]{:S(2)}, u32[]{:S(2)}) %collective-permute-start.19) | collective-permute-done | bytes 36896 | tf_op jit(solution)/shard_map/ppermute | solution.py:366
  74.0 0.3 collective-permute-done.20.refs_2_
  74.2 2.5 %collective-permute-done.21.refs_3_ = bf16[144,128]{1,0:T(8,128)(2,1)S(1)} collective-permute-done((bf16[144,128]{1,0:T(8,128)(2,1)S(1)}, bf16[144,128]{1,0:T(8,128)(2,1)S(1)}, u32[]{:S(2)}, u32[]{:S(2)}) %collective-permute-start.21) | collective-permute-done | bytes 36896 | tf_op jit(solution)/shard_map/ppermute | solution.py:366
  76.8 2.0 %collective-permute-start.24 = (bf16[144,128]{1,0:T(8,128)(2,1)S(1)}, bf16[144,128]{1,0:T(8,128)(2,1)S(1)}, u32[]{:S(2)}, u32[]{:S(2)}) collective-permute-start(bf16[144,128]{1,0:T(8,128)(2,1)S(1)} %sum_chips.1.refs_0_), channel_id=1, source_target_pairs={{0,6},{1,7},{2,4},{3,5},{4,2},{5,3},{6,0},{7,1},{8,14},{9,15},{10,... | collective-permute-start | bytes 110600 | tf_op jit(solution)/shard_map/ppermute | solution.py:348
  78.8 0.5 collective-permute-start.23
  79.2 2.0 %collective-permute-start.22 = (bf16[144,128]{1,0:T(8,128)(2,1)S(1)}, bf16[144,128]{1,0:T(8,128)(2,1)S(1)}, u32[]{:S(2)}, u32[]{:S(2)}) collective-permute-start(bf16[144,128]{1,0:T(8,128)(2,1)S(1)} %sum_chips.1.refs_0_), channel_id=1, source_target_pairs={{0,2},{1,3},{2,0},{3,1},{4,6},{5,7},{6,4},{7,5},{8,10},{9,11},{10,... | collective-permute-start | bytes 110600 | tf_op jit(solution)/shard_map/ppermute | solution.py:348
  81.2 1.4 %collective-permute-done.24.refs_3_ = bf16[144,128]{1,0:T(8,128)(2,1)S(1)} collective-permute-done((bf16[144,128]{1,0:T(8,128)(2,1)S(1)}, bf16[144,128]{1,0:T(8,128)(2,1)S(1)}, u32[]{:S(2)}, u32[]{:S(2)}) %collective-permute-start.24) | collective-permute-done | bytes 36896 | tf_op jit(solution)/shard_map/ppermute | solution.py:348
  82.6 1.4 %collective-permute-done.23.refs_2_ = bf16[144,128]{1,0:T(8,128)(2,1)S(1)} collective-permute-done((bf16[144,128]{1,0:T(8,128)(2,1)S(1)}, bf16[144,128]{1,0:T(8,128)(2,1)S(1)}, u32[]{:S(2)}, u32[]{:S(2)}) %collective-permute-start.23) | collective-permute-done | bytes 36896 | tf_op jit(solution)/shard_map/ppermute | solution.py:348
  84.0 1.0 %collective-permute-start.27 = (bf16[144,128]{1,0:T(8,128)(2,1)S(1)}, bf16[144,128]{1,0:T(8,128)(2,1)S(1)}, u32[]{:S(2)}, u32[]{:S(2)}) collective-permute-start(bf16[144,128]{1,0:T(8,128)(2,1)S(1)} %sum_planes.1.refs_0_), channel_id=1, source_target_pairs={{0,17},{1,16},{2,19},{3,18},{4,21},{5,20},{6,23},{7,22},{8,25},{9,... | collective-permute-start | bytes 110600 | tf_op jit(solution)/shard_map/ppermute | solution.py:366
  85.1 1.8 %collective-permute-start.26 = (bf16[144,128]{1,0:T(8,128)(2,1)S(1)}, bf16[144,128]{1,0:T(8,128)(2,1)S(1)}, u32[]{:S(2)}, u32[]{:S(2)}) collective-permute-start(bf16[144,128]{1,0:T(8,128)(2,1)S(1)} %sum_planes.1.refs_0_), channel_id=1, source_target_pairs={{0,16},{1,17},{2,18},{3,19},{4,20},{5,21},{6,22},{7,23},{8,24},{9,... | collective-permute-start | bytes 110600 | tf_op jit(solution)/shard_map/ppermute | solution.py:366
  86.9 0.7 collective-permute-start.25
  87.6 2.2 %decode.1 = (bf16[2,4,256,128]{3,2,1,0:T(8,128)(2,1)}, f32[8,128]{1,0:T(8,128)S(1)}) custom-call(s32[1]{0:T(128)} %bitcast.index_ref, bf16[2,4,256,128]{3,2,1,0:T(8,128)(2,1)S(1)} %get-tuple-element.49.image_ref, bf16[2,256,128]{2,1,0:T(8,128)(2,1)S(1)} %collective-permute-done.16.near_ref, bf16[2,256,128]{2,1,0:T(8,128)(2,1)S(1)} %collective-permute-done.17.far_ref, ...), custom_call_target="tpu_custom_call" | custom-call | flops 603979776 | bytes 1048576 | tf_op jit(solution)/shard_map/decode/pallas_call | solution.py:512
  89.8 1.0 %collective-permute-done.25.refs_1_ = bf16[144,128]{1,0:T(8,128)(2,1)S(1)} collective-permute-done((bf16[144,128]{1,0:T(8,128)(2,1)S(1)}, bf16[144,128]{1,0:T(8,128)(2,1)S(1)}, u32[]{:S(2)}, u32[]{:S(2)}) %collective-permute-start.25) | collective-permute-done | bytes 36896 | tf_op jit(solution)/shard_map/ppermute | solution.py:366
  90.9 0.1 collective-permute-start.28
  90.9 1.4 %collective-permute-done.28.other_ref = bf16[576,128]{1,0:T(8,128)(2,1)S(1)} collective-permute-done((bf16[576,128]{1,0:T(8,128)(2,1)S(1)}, bf16[576,128]{1,0:T(8,128)(2,1)S(1)}, u32[]{:S(2)}, u32[]{:S(2)}) %collective-permute-start.28) | collective-permute-done | bytes 147488 | tf_op jit(solution)/shard_map/ppermute | solution.py:370
  92.3 0.9 spread_sums.1
  (27 shorter events, 0.1 us)
Async XLA Ops:
  0.6 14.3 %copy-start.3 = (bf16[2,4,256,128]{3,2,1,0:T(8,128)(2,1)S(1)}, bf16[2,4,256,128]{3,2,1,0:T(8,128)(2,1)}, u32[]{:S(2)}) copy-start(bf16[2,4,256,128]{3,2,1,0:T(8,128)(2,1)} %cot_ref.1) | copy-start | bytes 1572868
  0.6 14.3 %copy-start = (bf16[64,2,2048]{2,1,0:T(2,128)(2,1)S(1)}, bf16[64,2,2048]{2,1,0:T(2,128)(2,1)}, u32[]{:S(2)}) copy-start(bf16[64,2,2048]{2,1,0:T(2,128)(2,1)} %query_ref.5) | copy-start | bytes 1572868
  0.7 14.3 %copy-start.1 = (bf16[64,2,2048]{2,1,0:T(2,128)(2,1)S(1)}, bf16[64,2,2048]{2,1,0:T(2,128)(2,1)}, u32[]{:S(2)}) copy-start(bf16[64,2,2048]{2,1,0:T(2,128)(2,1)} %key_ref.5) | copy-start | bytes 1572868
  0.7 14.3 %copy-start.2 = (bf16[64,2,2048]{2,1,0:T(2,128)(2,1)S(1)}, bf16[64,2,2048]{2,1,0:T(2,128)(2,1)}, u32[]{:S(2)}) copy-start(bf16[64,2,2048]{2,1,0:T(2,128)(2,1)} %value_ref.5) | copy-start | bytes 1572868
  3.3 12.3 %collective-permute-start.3 = (bf16[3,4,64,128]{3,2,1,0:T(8,128)(2,1)}, bf16[3,4,64,128]{3,2,1,0:T(8,128)(2,1)S(1)}, u32[]{:S(2)}, u32[]{:S(2)}) collective-permute-start(bf16[3,4,64,128]{3,2,1,0:T(8,128)(2,1)} %get-tuple-element.34), channel_id=1, source_target_pairs={{0,2},{1,3},{2,0},{3,1},{4,6},{5,7},{6,4},{7,5},{8,10},{9,11},{10,... | collective-permute-start | bytes 589832 | tf_op jit(solution)/shard_map/ppermute | solution.py:348
  6.3 17.1 %collective-permute-start.5 = (bf16[3,4,64,128]{3,2,1,0:T(8,128)(2,1)}, bf16[3,4,64,128]{3,2,1,0:T(8,128)(2,1)S(1)}, u32[]{:S(2)}, u32[]{:S(2)}) collective-permute-start(bf16[3,4,64,128]{3,2,1,0:T(8,128)(2,1)} %get-tuple-element.36), channel_id=1, source_target_pairs={{0,4},{1,5},{2,6},{3,7},{4,0},{5,1},{6,2},{7,3},{8,12},{9,13},{10,... | collective-permute-start | bytes 589832 | tf_op jit(solution)/shard_map/ppermute | solution.py:348
  8.9 28.3 %collective-permute-start.6 = (bf16[3,4,64,128]{3,2,1,0:T(8,128)(2,1)}, bf16[3,4,64,128]{3,2,1,0:T(8,128)(2,1)S(1)}, u32[]{:S(2)}, u32[]{:S(2)}) collective-permute-start(bf16[3,4,64,128]{3,2,1,0:T(8,128)(2,1)} %get-tuple-element.37), channel_id=1, source_target_pairs={{0,5},{1,4},{2,7},{3,6},{4,1},{5,0},{6,3},{7,2},{8,13},{9,12},{10,... | collective-permute-start | bytes 589832 | tf_op jit(solution)/shard_map/ppermute | solution.py:348
  12.9 10.5 %copy-start.7 = (bf16[3,4,64,128]{3,2,1,0:T(8,128)(2,1)S(1)}, bf16[3,4,64,128]{3,2,1,0:T(8,128)(2,1)}, u32[]{:S(2)}) copy-start(bf16[3,4,64,128]{3,2,1,0:T(8,128)(2,1)} %get-tuple-element.39) | copy-start | bytes 589828
  13.0 25.3 %copy-start.6 = (s32[2]{0:T(128)S(1)}, s32[2]{0:T(128)}, u32[]{:S(2)}) copy-start(s32[2]{0:T(128)} %lengths_ref.1) | copy-start | bytes 28
  13.0 24.6 %collective-permute-start.2 = (bf16[3,4,64,128]{3,2,1,0:T(8,128)(2,1)}, bf16[3,4,64,128]{3,2,1,0:T(8,128)(2,1)S(1)}, u32[]{:S(2)}, u32[]{:S(2)}) collective-permute-start(bf16[3,4,64,128]{3,2,1,0:T(8,128)(2,1)} %get-tuple-element.33), channel_id=1, source_target_pairs={{0,1},{1,0},{2,3},{3,2},{4,5},{5,4},{6,7},{7,6},{8,9},{9,8},{10,11... | collective-permute-start | bytes 589832 | tf_op jit(solution)/shard_map/ppermute | solution.py:348
  13.6 24.8 %collective-permute-start.4 = (bf16[3,4,64,128]{3,2,1,0:T(8,128)(2,1)}, bf16[3,4,64,128]{3,2,1,0:T(8,128)(2,1)S(1)}, u32[]{:S(2)}, u32[]{:S(2)}) collective-permute-start(bf16[3,4,64,128]{3,2,1,0:T(8,128)(2,1)} %get-tuple-element.35), channel_id=1, source_target_pairs={{0,3},{1,2},{2,1},{3,0},{4,7},{5,6},{6,5},{7,4},{8,11},{9,10},{10,... | collective-permute-start | bytes 589832 | tf_op jit(solution)/shard_map/ppermute | solution.py:348
  15.0 0.9 copy-start.8
  15.9 22.4 %collective-permute-start.7 = (bf16[3,4,64,128]{3,2,1,0:T(8,128)(2,1)S(1)}, bf16[3,4,64,128]{3,2,1,0:T(8,128)(2,1)S(1)}, u32[]{:S(2)}, u32[]{:S(2)}) collective-permute-start(bf16[3,4,64,128]{3,2,1,0:T(8,128)(2,1)S(1)} %copy-done.8), channel_id=1, source_target_pairs={{0,6},{1,7},{2,4},{3,5},{4,2},{5,3},{6,0},{7,1},{8,14},{9,15},{10,... | collective-permute-start | bytes 589832 | tf_op jit(solution)/shard_map/ppermute | solution.py:348
  23.4 14.9 %collective-permute-start.8 = (bf16[3,4,64,128]{3,2,1,0:T(8,128)(2,1)S(1)}, bf16[3,4,64,128]{3,2,1,0:T(8,128)(2,1)S(1)}, u32[]{:S(2)}, u32[]{:S(2)}) collective-permute-start(bf16[3,4,64,128]{3,2,1,0:T(8,128)(2,1)S(1)} %copy-done.7), channel_id=1, source_target_pairs={{0,7},{1,6},{2,5},{3,4},{4,3},{5,2},{6,1},{7,0},{8,15},{9,14},{10,... | collective-permute-start | bytes 589832 | tf_op jit(solution)/shard_map/ppermute | solution.py:348
  37.3 13.4 %collective-permute-start = (bf16[2,256,128]{2,1,0:T(8,128)(2,1)S(1)}, bf16[2,256,128]{2,1,0:T(8,128)(2,1)S(1)}, u32[]{:S(2)}, u32[]{:S(2)}) collective-permute-start(bf16[2,256,128]{2,1,0:T(8,128)(2,1)S(1)} %get-tuple-element.31), channel_id=1, source_target_pairs={{0,1},{1,0},{2,3},{3,2},{4,5},{5,4},{6,7},{7,6},{8,9},{9,8},{10,11... | collective-permute-start | bytes 393224 | tf_op jit(solution)/shard_map/ppermute | solution.py:348
  37.6 16.7 %collective-permute-start.1 = (bf16[2,256,128]{2,1,0:T(8,128)(2,1)S(1)}, bf16[2,256,128]{2,1,0:T(8,128)(2,1)S(1)}, u32[]{:S(2)}, u32[]{:S(2)}) collective-permute-start(bf16[2,256,128]{2,1,0:T(8,128)(2,1)S(1)} %get-tuple-element.32), channel_id=1, source_target_pairs={{1,2},{3,4},{5,6},{2,1},{4,3},{6,5},{9,10},{11,12},{13,14},{10,9},... | collective-permute-start | bytes 393224 | tf_op jit(solution)/shard_map/ppermute | solution.py:437
  40.4 21.5 %copy-start.5 = (f32[2048]{0:T(1024)S(1)}, f32[2048]{0:T(1024)}, u32[]{:S(2)}) copy-start(f32[2048]{0:T(1024)} %param.11) | copy-start | bytes 24580
  40.4 15.2 %collective-permute-start.9 = (bf16[4,64,128]{2,1,0:T(8,128)(2,1)S(1)}, bf16[4,64,128]{2,1,0:T(8,128)(2,1)S(1)}, u32[]{:S(2)}, u32[]{:S(2)}) collective-permute-start(bf16[4,64,128]{2,1,0:T(8,128)(2,1)S(1)} %get-tuple-element.41), channel_id=1, source_target_pairs={{0,4},{1,5},{2,6},{3,7},{4,0},{5,1},{6,2},{7,3},{8,12},{9,13},{10,... | collective-permute-start | bytes 196616 | tf_op jit(solution)/shard_map/ppermute | solution.py:348
  49.5 8.2 %collective-permute-start.10 = (bf16[4,64,128]{2,1,0:T(8,128)(2,1)S(1)}, bf16[4,64,128]{2,1,0:T(8,128)(2,1)S(1)}, u32[]{:S(2)}, u32[]{:S(2)}) collective-permute-start(bf16[4,64,128]{2,1,0:T(8,128)(2,1)S(1)} %get-tuple-element.42), channel_id=1, source_target_pairs={{0,5},{1,4},{2,7},{3,6},{4,1},{5,0},{6,3},{7,2},{8,13},{9,12},{10,... | collective-permute-start | bytes 196616 | tf_op jit(solution)/shard_map/ppermute | solution.py:348
  49.5 10.1 %collective-permute-start.11 = (bf16[4,64,128]{2,1,0:T(8,128)(2,1)S(1)}, bf16[4,64,128]{2,1,0:T(8,128)(2,1)S(1)}, u32[]{:S(2)}, u32[]{:S(2)}) collective-permute-start(bf16[4,64,128]{2,1,0:T(8,128)(2,1)S(1)} %get-tuple-element.43), channel_id=1, source_target_pairs={{0,6},{1,7},{2,4},{3,5},{4,2},{5,3},{6,0},{7,1},{8,14},{9,15},{10,... | collective-permute-start | bytes 196616 | tf_op jit(solution)/shard_map/ppermute | solution.py:348
  50.7 8.8 %collective-permute-start.12 = (bf16[4,64,128]{2,1,0:T(8,128)(2,1)S(1)}, bf16[4,64,128]{2,1,0:T(8,128)(2,1)S(1)}, u32[]{:S(2)}, u32[]{:S(2)}) collective-permute-start(bf16[4,64,128]{2,1,0:T(8,128)(2,1)S(1)} %get-tuple-element.44), channel_id=1, source_target_pairs={{0,7},{1,6},{2,5},{3,4},{4,3},{5,2},{6,1},{7,0},{8,15},{9,14},{10,... | collective-permute-start | bytes 196616 | tf_op jit(solution)/shard_map/ppermute | solution.py:348
  54.3 5.3 %collective-permute-start.13 = (bf16[4,64,128]{2,1,0:T(8,128)(2,1)S(1)}, bf16[4,64,128]{2,1,0:T(8,128)(2,1)S(1)}, u32[]{:S(2)}, u32[]{:S(2)}) collective-permute-start(bf16[4,64,128]{2,1,0:T(8,128)(2,1)S(1)} %get-tuple-element.45), channel_id=1, source_target_pairs={{0,2},{1,3},{2,0},{3,1},{4,6},{5,7},{6,4},{7,5},{8,10},{9,11},{10,... | collective-permute-start | bytes 196616 | tf_op jit(solution)/shard_map/ppermute | solution.py:348
  55.6 5.2 %collective-permute-start.14 = (bf16[4,64,128]{2,1,0:T(8,128)(2,1)S(1)}, bf16[4,64,128]{2,1,0:T(8,128)(2,1)S(1)}, u32[]{:S(2)}, u32[]{:S(2)}) collective-permute-start(bf16[4,64,128]{2,1,0:T(8,128)(2,1)S(1)} %get-tuple-element.46), channel_id=1, source_target_pairs={{0,3},{1,2},{2,1},{3,0},{4,7},{5,6},{6,5},{7,4},{8,11},{9,10},{10,... | collective-permute-start | bytes 196616 | tf_op jit(solution)/shard_map/ppermute | solution.py:348
  57.7 4.3 %collective-permute-start.15 = (bf16[4,64,128]{2,1,0:T(8,128)(2,1)S(1)}, bf16[4,64,128]{2,1,0:T(8,128)(2,1)S(1)}, u32[]{:S(2)}, u32[]{:S(2)}) collective-permute-start(bf16[4,64,128]{2,1,0:T(8,128)(2,1)S(1)} %get-tuple-element.47), channel_id=1, source_target_pairs={{0,1},{1,0},{2,3},{3,2},{4,5},{5,4},{6,7},{7,6},{8,9},{9,8},{10,11... | collective-permute-start | bytes 196616 | tf_op jit(solution)/shard_map/ppermute | solution.py:348
  62.0 25.6 %copy-start.4 = (bf16[9,128,128]{2,1,0:T(8,128)(2,1)S(1)}, bf16[9,128,128]{2,1,0:T(8,128)(2,1)}, u32[]{:S(2)}) copy-start(bf16[9,128,128]{2,1,0:T(8,128)(2,1)} %param.12) | copy-start | bytes 884740
  65.0 2.6 %collective-permute-start.18 = (f32[576,128]{1,0:T(8,128)S(1)}, f32[576,128]{1,0:T(8,128)S(1)}, u32[]{:S(2)}, u32[]{:S(2)}) collective-permute-start(f32[576,128]{1,0:T(8,128)S(1)} %get-tuple-element.55), channel_id=1, source_target_pairs={{0,8},{8,0},{16,24},{24,16},{1,9},{9,1},{17,25},{25,17},{2,10},{10... | collective-permute-start | bytes 884744 | tf_op jit(solution)/shard_map/ppermute | solution.py:370
  65.1 22.5 %collective-permute-start.16 = (bf16[2,256,128]{2,1,0:T(8,128)(2,1)S(1)}, bf16[2,256,128]{2,1,0:T(8,128)(2,1)S(1)}, u32[]{:S(2)}, u32[]{:S(2)}) collective-permute-start(bf16[2,256,128]{2,1,0:T(8,128)(2,1)S(1)} %get-tuple-element.50), channel_id=1, source_target_pairs={{0,1},{1,0},{2,3},{3,2},{4,5},{5,4},{6,7},{7,6},{8,9},{9,8},{10,11... | collective-permute-start | bytes 393224 | tf_op jit(solution)/shard_map/ppermute | solution.py:348
  66.7 20.9 %collective-permute-start.17 = (bf16[2,256,128]{2,1,0:T(8,128)(2,1)S(1)}, bf16[2,256,128]{2,1,0:T(8,128)(2,1)S(1)}, u32[]{:S(2)}, u32[]{:S(2)}) collective-permute-start(bf16[2,256,128]{2,1,0:T(8,128)(2,1)S(1)} %get-tuple-element.51), channel_id=1, source_target_pairs={{1,2},{3,4},{5,6},{2,1},{4,3},{6,5},{9,10},{11,12},{13,14},{10,9},... | collective-permute-start | bytes 393224 | tf_op jit(solution)/shard_map/ppermute | solution.py:500
  67.7 6.3 %collective-permute-start.19 = (bf16[144,128]{1,0:T(8,128)(2,1)S(1)}, bf16[144,128]{1,0:T(8,128)(2,1)S(1)}, u32[]{:S(2)}, u32[]{:S(2)}) collective-permute-start(bf16[144,128]{1,0:T(8,128)(2,1)S(1)} %get-tuple-element.57), channel_id=1, source_target_pairs={{0,1},{1,0},{2,3},{3,2},{4,5},{5,4},{6,7},{7,6},{8,9},{9,8},{10,11... | collective-permute-start | bytes 110600 | tf_op jit(solution)/shard_map/ppermute | solution.py:366
  70.3 4.0 %collective-permute-start.20 = (bf16[144,128]{1,0:T(8,128)(2,1)S(1)}, bf16[144,128]{1,0:T(8,128)(2,1)S(1)}, u32[]{:S(2)}, u32[]{:S(2)}) collective-permute-start(bf16[144,128]{1,0:T(8,128)(2,1)S(1)} %get-tuple-element.58), channel_id=1, source_target_pairs={{0,16},{1,17},{2,18},{3,19},{4,20},{5,21},{6,22},{7,23},{8,24},{9,... | collective-permute-start | bytes 110600 | tf_op jit(solution)/shard_map/ppermute | solution.py:366
  71.9 4.9 %collective-permute-start.21 = (bf16[144,128]{1,0:T(8,128)(2,1)S(1)}, bf16[144,128]{1,0:T(8,128)(2,1)S(1)}, u32[]{:S(2)}, u32[]{:S(2)}) collective-permute-start(bf16[144,128]{1,0:T(8,128)(2,1)S(1)} %get-tuple-element.59), channel_id=1, source_target_pairs={{0,17},{1,16},{2,19},{3,18},{4,21},{5,20},{6,23},{7,22},{8,25},{9,... | collective-permute-start | bytes 110600 | tf_op jit(solution)/shard_map/ppermute | solution.py:366
  76.8 5.8 %collective-permute-start.24 = (bf16[144,128]{1,0:T(8,128)(2,1)S(1)}, bf16[144,128]{1,0:T(8,128)(2,1)S(1)}, u32[]{:S(2)}, u32[]{:S(2)}) collective-permute-start(bf16[144,128]{1,0:T(8,128)(2,1)S(1)} %sum_chips.1.refs_0_), channel_id=1, source_target_pairs={{0,6},{1,7},{2,4},{3,5},{4,2},{5,3},{6,0},{7,1},{8,14},{9,15},{10,... | collective-permute-start | bytes 110600 | tf_op jit(solution)/shard_map/ppermute | solution.py:348
  78.8 5.3 %collective-permute-start.23 = (bf16[144,128]{1,0:T(8,128)(2,1)S(1)}, bf16[144,128]{1,0:T(8,128)(2,1)S(1)}, u32[]{:S(2)}, u32[]{:S(2)}) collective-permute-start(bf16[144,128]{1,0:T(8,128)(2,1)S(1)} %sum_chips.1.refs_0_), channel_id=1, source_target_pairs={{0,4},{1,5},{2,6},{3,7},{4,0},{5,1},{6,2},{7,3},{8,12},{9,13},{10,... | collective-permute-start | bytes 110600 | tf_op jit(solution)/shard_map/ppermute | solution.py:348
  79.2 4.8 %collective-permute-start.22 = (bf16[144,128]{1,0:T(8,128)(2,1)S(1)}, bf16[144,128]{1,0:T(8,128)(2,1)S(1)}, u32[]{:S(2)}, u32[]{:S(2)}) collective-permute-start(bf16[144,128]{1,0:T(8,128)(2,1)S(1)} %sum_chips.1.refs_0_), channel_id=1, source_target_pairs={{0,2},{1,3},{2,0},{3,1},{4,6},{5,7},{6,4},{7,5},{8,10},{9,11},{10,... | collective-permute-start | bytes 110600 | tf_op jit(solution)/shard_map/ppermute | solution.py:348
  84.0 5.8 %collective-permute-start.27 = (bf16[144,128]{1,0:T(8,128)(2,1)S(1)}, bf16[144,128]{1,0:T(8,128)(2,1)S(1)}, u32[]{:S(2)}, u32[]{:S(2)}) collective-permute-start(bf16[144,128]{1,0:T(8,128)(2,1)S(1)} %sum_planes.1.refs_0_), channel_id=1, source_target_pairs={{0,17},{1,16},{2,19},{3,18},{4,21},{5,20},{6,23},{7,22},{8,25},{9,... | collective-permute-start | bytes 110600 | tf_op jit(solution)/shard_map/ppermute | solution.py:366
  85.1 4.8 %collective-permute-start.26 = (bf16[144,128]{1,0:T(8,128)(2,1)S(1)}, bf16[144,128]{1,0:T(8,128)(2,1)S(1)}, u32[]{:S(2)}, u32[]{:S(2)}) collective-permute-start(bf16[144,128]{1,0:T(8,128)(2,1)S(1)} %sum_planes.1.refs_0_), channel_id=1, source_target_pairs={{0,16},{1,17},{2,18},{3,19},{4,20},{5,21},{6,22},{7,23},{8,24},{9,... | collective-permute-start | bytes 110600 | tf_op jit(solution)/shard_map/ppermute | solution.py:366
  86.9 4.0 %collective-permute-start.25 = (bf16[144,128]{1,0:T(8,128)(2,1)S(1)}, bf16[144,128]{1,0:T(8,128)(2,1)S(1)}, u32[]{:S(2)}, u32[]{:S(2)}) collective-permute-start(bf16[144,128]{1,0:T(8,128)(2,1)S(1)} %sum_planes.1.refs_0_), channel_id=1, source_target_pairs={{0,1},{1,0},{2,3},{3,2},{4,5},{5,4},{6,7},{7,6},{8,9},{9,8},{10,11... | collective-permute-start | bytes 110600 | tf_op jit(solution)/shard_map/ppermute | solution.py:366
  90.9 1.4 %collective-permute-start.28 = (bf16[576,128]{1,0:T(8,128)(2,1)S(1)}, bf16[576,128]{1,0:T(8,128)(2,1)S(1)}, u32[]{:S(2)}, u32[]{:S(2)}) collective-permute-start(bf16[576,128]{1,0:T(8,128)(2,1)S(1)} %join_chips.1.own_ref), channel_id=1, source_target_pairs={{0,8},{8,0},{16,24},{24,16},{1,9},{9,1},{17,25},{25,17},{2,10},{10... | collective-permute-start | bytes 442376 | tf_op jit(solution)/shard_map/ppermute | solution.py:370

commit v17 on v16

--- a/solution.py
+++ b/solution.py
@@ -317,6 +317,21 @@
     return terms[0]
 
 
+def hold_kernel(value_ref, after_ref, out_ref):
+    del after_ref
+    out_ref[...] = value_ref[...]
+
+
+def hold(value, after):
+    return call(
+        hold_kernel,
+        "hold",
+        jax.ShapeDtypeStruct(value.shape, value.dtype),
+        [VMEM(), ANY()],
+        moved=4 * value.size,
+    )(value, after)
+
+
 def sum_cores_kernel(quad_ref, keep_ref, other_ref, *refs):
     total = refs[-1]
     total[...] = keep_ref[...] + other_ref[...]
@@ -496,7 +511,6 @@
         scratch=[pltpu.VMEM((half_rows, width), jnp.float32)],
         moved=quad_size * chunk_moved,
     )(quad, keep, trade_cores(send))
-    near = trade(near, 1)
     far = lax.ppermute(far, "seq", far_pairs)
     distances = range(1, quad_size)
     plane_sum = call(
@@ -506,6 +520,7 @@
         [VMEM()] * quad_size,
         moved=chunk_moved,
     )(parts[0], *[trade_chips(parts[distance], distance, inner) for distance in distances])
+    near = trade(hold(near, plane_sum), 1)
     plane_sums = [plane_sum] + [
         trade(plane_sum, distance) for distance in range(inner, seq_count, inner)
     ]

time: 93.2 us -> 91.6 us (0.983)
  starting transfers between devices: 48 us -> 46 us
    ppermute x2, waiting for transfers between devices: 1.36 us -> 2.92 us  [trade_cores(): lax.ppermute(values, 'dp', [(i, i ^ 1) for i in range(lax.axis_size('dp'))])]
    ppermute x19, starting transfers between devices: 38.6 us -> 37.4 us  [trade(): return lax.ppermute(values, 'seq', pairs)]
  transfers between devices with their start and end apart: 29 -> 29, of which waited for: 14 -> 15; matrix products, arithmetic and copies ran while one was open for 0% -> 0% of each run, Pallas kernels for 8% -> 9%
where the time goes in v17:
time: 91.6 us; the launch traced here: 91.4 us
  starting transfers between devices  46 us (50%)
  waiting for transfers between devices  29.7 us (32%)
  Pallas kernels  14.3 us (16%)
    ppermute x19, starting transfers between devices, trade(): return lax.ppermute(values, 'seq', pairs)  37.4 us
    ppermute x19, waiting for transfers between devices, trade(): return lax.ppermute(values, 'seq', pairs)  21.7 us
    ppermute x6, starting transfers between devices, trade_chips(): return lax.ppermute(values, ('dp', 'seq'), pairs)  7.11 us
    pallas_call x2, Pallas kernels, pack(): call(functools.partial(pack_kernel, distances, regions, per_device), name...  5.3 us
    ppermute x6, waiting for transfers between devices, trade_chips(): return lax.ppermute(values, ('dp', 'seq'), pairs)  5 us
    pallas_call x1, Pallas kernels, body(): call(functools.partial(norm_kernel, back + [0]), 'norm_and_gradient', [ja...  3.06 us
    ppermute x2, waiting for transfers between devices, trade_cores(): lax.ppermute(values, 'dp', [(i, i ^ 1) for i in range(lax.axis_size('dp'))])  2.92 us
    pallas_call x1, Pallas kernels, body(): call(decode_kernel, 'decode', [jax.ShapeDtypeStruct(cotangent.shape, jnp....  2.22 us
  transfers between devices with their start and end apart: 29, of which 15 were waited for; matrix products, arithmetic and copies ran while one was open for 0% of the time, Pallas kernels for 9%

profile of v17, /device:TPU:0, one launch (start us, length us, event | category | flops | bytes accessed | tf_op | source)
XLA Modules:
  0.0 91.4 jit_solution(3161099348465395641)
XLA Ops:
  0.6 0.0 copy-start
  0.7 0.0 copy-start.1
  0.7 0.0 copy-start.2
  0.7 2.6 %pack_early.1 = (bf16[3,4,64,128]{3,2,1,0:T(8,128)(2,1)}, bf16[3,4,64,128]{3,2,1,0:T(8,128)(2,1)}, bf16[3,4,64,128]{3,2,1,0:T(8,128)(2,1)}) custom-call(s32[1]{0:T(128)} %bitcast.index_ref, bf16[64,2,2048]{2,1,0:T(2,128)(2,1)} %query_ref.5, bf16[64,2,2048]{2,1,0:T(2,128)(2,1)} %key_ref.5, bf16[64,2,2048]{2,1,0:T(2,128)(2,1)} %value_ref.5), custom_call_target="tpu_custom_call" | custom-call | bytes 1179648 | tf_op jit(solution)/shard_map/pack_early/pallas_call | solution.py:418
  3.3 3.1 %collective-permute-start.3 = (bf16[3,4,64,128]{3,2,1,0:T(8,128)(2,1)}, bf16[3,4,64,128]{3,2,1,0:T(8,128)(2,1)S(1)}, u32[]{:S(2)}, u32[]{:S(2)}) collective-permute-start(bf16[3,4,64,128]{3,2,1,0:T(8,128)(2,1)} %get-tuple-element.34), channel_id=1, source_target_pairs={{0,2},{1,3},{2,0},{3,1},{4,6},{5,7},{6,4},{7,5},{8,10},{9,11},{10,... | collective-permute-start | bytes 589832 | tf_op jit(solution)/shard_map/ppermute | solution.py:363
  6.3 2.6 %collective-permute-start.5 = (bf16[3,4,64,128]{3,2,1,0:T(8,128)(2,1)}, bf16[3,4,64,128]{3,2,1,0:T(8,128)(2,1)S(1)}, u32[]{:S(2)}, u32[]{:S(2)}) collective-permute-start(bf16[3,4,64,128]{3,2,1,0:T(8,128)(2,1)} %get-tuple-element.36), channel_id=1, source_target_pairs={{0,4},{1,5},{2,6},{3,7},{4,0},{5,1},{6,2},{7,3},{8,12},{9,13},{10,... | collective-permute-start | bytes 589832 | tf_op jit(solution)/shard_map/ppermute | solution.py:363
  8.9 1.3 %collective-permute-start.6 = (bf16[3,4,64,128]{3,2,1,0:T(8,128)(2,1)}, bf16[3,4,64,128]{3,2,1,0:T(8,128)(2,1)S(1)}, u32[]{:S(2)}, u32[]{:S(2)}) collective-permute-start(bf16[3,4,64,128]{3,2,1,0:T(8,128)(2,1)} %get-tuple-element.37), channel_id=1, source_target_pairs={{0,5},{1,4},{2,7},{3,6},{4,1},{5,0},{6,3},{7,2},{8,13},{9,12},{10,... | collective-permute-start | bytes 589832 | tf_op jit(solution)/shard_map/ppermute | solution.py:363
  10.2 2.7 %pack_late.1 = (bf16[3,4,64,128]{3,2,1,0:T(8,128)(2,1)}, bf16[3,4,64,128]{3,2,1,0:T(8,128)(2,1)}, bf16[3,4,64,128]{3,2,1,0:T(8,128)(2,1)}, bf16[3,4,64,128]{3,2,1,0:T(8,128)(2,1)}) custom-call(s32[1]{0:T(128)} %bitcast.index_ref, bf16[64,2,2048]{2,1,0:T(2,128)(2,1)} %query_ref.5, bf16[64,2,2048]{2,1,0:T(2,128)(2,1)} %key_ref.5, bf16[64,2,2048]{2,1,0:T(2,128)(2,1)} %value_ref.5), custom_call_target="tpu_custom_call" | custom-call | bytes 1572864 | tf_op jit(solution)/shard_map/pack_late/pallas_call | solution.py:418
  13.0 0.0 copy-start.6
  13.0 0.6 collective-permute-start.2
  13.6 1.4 %collective-permute-start.4 = (bf16[3,4,64,128]{3,2,1,0:T(8,128)(2,1)}, bf16[3,4,64,128]{3,2,1,0:T(8,128)(2,1)S(1)}, u32[]{:S(2)}, u32[]{:S(2)}) collective-permute-start(bf16[3,4,64,128]{3,2,1,0:T(8,128)(2,1)} %get-tuple-element.35), channel_id=1, source_target_pairs={{0,3},{1,2},{2,1},{3,0},{4,7},{5,6},{6,5},{7,4},{8,11},{9,10},{10,... | collective-permute-start | bytes 589832 | tf_op jit(solution)/shard_map/ppermute | solution.py:363
  15.0 0.4 own_chunk.1
  15.4 0.1 collective-permute-done.3.refs_1_
  15.6 0.3 copy-done.8
  15.9 3.6 %collective-permute-start.7 = (bf16[3,4,64,128]{3,2,1,0:T(8,128)(2,1)S(1)}, bf16[3,4,64,128]{3,2,1,0:T(8,128)(2,1)S(1)}, u32[]{:S(2)}, u32[]{:S(2)}) collective-permute-start(bf16[3,4,64,128]{3,2,1,0:T(8,128)(2,1)S(1)} %copy-done.8), channel_id=1, source_target_pairs={{0,6},{1,7},{2,4},{3,5},{4,2},{5,3},{6,0},{7,1},{8,14},{9,15},{10,... | collective-permute-start | bytes 589832 | tf_op jit(solution)/shard_map/ppermute | solution.py:363
  19.5 3.9 %collective-permute-done.5.refs_3_ = bf16[3,4,64,128]{3,2,1,0:T(8,128)(2,1)S(1)} collective-permute-done((bf16[3,4,64,128]{3,2,1,0:T(8,128)(2,1)}, bf16[3,4,64,128]{3,2,1,0:T(8,128)(2,1)S(1)}, u32[]{:S(2)}, u32[]{:S(2)}) %collective-permute-start.5) | collective-permute-done | bytes 196640 | tf_op jit(solution)/shard_map/ppermute | solution.py:363
  23.4 3.7 %collective-permute-start.8 = (bf16[3,4,64,128]{3,2,1,0:T(8,128)(2,1)S(1)}, bf16[3,4,64,128]{3,2,1,0:T(8,128)(2,1)S(1)}, u32[]{:S(2)}, u32[]{:S(2)}) collective-permute-start(bf16[3,4,64,128]{3,2,1,0:T(8,128)(2,1)S(1)} %copy-done.7), channel_id=1, source_target_pairs={{0,7},{1,6},{2,5},{3,4},{4,3},{5,2},{6,1},{7,0},{8,15},{9,14},{10,... | collective-permute-start | bytes 589832 | tf_op jit(solution)/shard_map/ppermute | solution.py:363
  27.1 10.2 %collective-permute-done.6.refs_4_ = bf16[3,4,64,128]{3,2,1,0:T(8,128)(2,1)S(1)} collective-permute-done((bf16[3,4,64,128]{3,2,1,0:T(8,128)(2,1)}, bf16[3,4,64,128]{3,2,1,0:T(8,128)(2,1)S(1)}, u32[]{:S(2)}, u32[]{:S(2)}) %collective-permute-start.6) | collective-permute-done | bytes 196640 | tf_op jit(solution)/shard_map/ppermute | solution.py:363
  37.3 0.3 collective-permute-start
  37.6 0.0 collective-permute-done.2.refs_0_
  37.6 0.7 collective-permute-start.1
  38.2 0.1 fusion.2.lengths_ref
  38.3 0.0 collective-permute-done.4.refs_2_
  38.3 0.0 collective-permute-done.7.refs_5_
  38.3 0.0 collective-permute-done.8.refs_6_
  38.3 2.1 %attend.1 = (bf16[4,64,128]{2,1,0:T(8,128)(2,1)S(1)}, bf16[4,64,128]{2,1,0:T(8,128)(2,1)S(1)}, bf16[4,64,128]{2,1,0:T(8,128)(2,1)S(1)}, bf16[4,64,128]{2,1,0:T(8...) custom-call(s32[1]{0:T(128)} %bitcast.index_ref, ...), custom_call_target="tpu_custom_call" | custom-call | flops 536870912 | bytes 2097152 | tf_op jit(solution)/shard_map/attend/pallas_call | solution.py:465
  40.4 0.0 copy-start.5
  40.5 9.0 %collective-permute-start.9 = (bf16[4,64,128]{2,1,0:T(8,128)(2,1)S(1)}, bf16[4,64,128]{2,1,0:T(8,128)(2,1)S(1)}, u32[]{:S(2)}, u32[]{:S(2)}) collective-permute-start(bf16[4,64,128]{2,1,0:T(8,128)(2,1)S(1)} %get-tuple-element.41), channel_id=1, source_target_pairs={{0,4},{1,5},{2,6},{3,7},{4,0},{5,1},{6,2},{7,3},{8,12},{9,13},{10,... | collective-permute-start | bytes 196616 | tf_op jit(solution)/shard_map/ppermute | solution.py:363
  49.5 1.2 %collective-permute-start.11 = (bf16[4,64,128]{2,1,0:T(8,128)(2,1)S(1)}, bf16[4,64,128]{2,1,0:T(8,128)(2,1)S(1)}, u32[]{:S(2)}, u32[]{:S(2)}) collective-permute-start(bf16[4,64,128]{2,1,0:T(8,128)(2,1)S(1)} %get-tuple-element.43), channel_id=1, source_target_pairs={{0,6},{1,7},{2,4},{3,5},{4,2},{5,3},{6,0},{7,1},{8,14},{9,15},{10,... | collective-permute-start | bytes 196616 | tf_op jit(solution)/shard_map/ppermute | solution.py:363
  50.7 0.0 collective-permute-done.near_ref
  50.7 3.6 %collective-permute-start.12 = (bf16[4,64,128]{2,1,0:T(8,128)(2,1)S(1)}, bf16[4,64,128]{2,1,0:T(8,128)(2,1)S(1)}, u32[]{:S(2)}, u32[]{:S(2)}) collective-permute-start(bf16[4,64,128]{2,1,0:T(8,128)(2,1)S(1)} %get-tuple-element.44), channel_id=1, source_target_pairs={{0,7},{1,6},{2,5},{3,4},{4,3},{5,2},{6,1},{7,0},{8,15},{9,14},{10,... | collective-permute-start | bytes 196616 | tf_op jit(solution)/shard_map/ppermute | solution.py:363
  54.3 0.0 collective-permute-start.13
  54.3 1.3 %collective-permute-done.9.refs_0_ = bf16[4,64,128]{2,1,0:T(8,128)(2,1)S(1)} collective-permute-done((bf16[4,64,128]{2,1,0:T(8,128)(2,1)S(1)}, bf16[4,64,128]{2,1,0:T(8,128)(2,1)S(1)}, u32[]{:S(2)}, u32[]{:S(2)}) %collective-permute-start.9) | collective-permute-done | bytes 65568 | tf_op jit(solution)/shard_map/ppermute | solution.py:363
  55.6 0.6 collective-permute-start.14
  56.2 1.5 %collective-permute-done.10.refs_1_ = bf16[4,64,128]{2,1,0:T(8,128)(2,1)S(1)} collective-permute-done((bf16[4,64,128]{2,1,0:T(8,128)(2,1)S(1)}, bf16[4,64,128]{2,1,0:T(8,128)(2,1)S(1)}, u32[]{:S(2)}, u32[]{:S(2)}) %collective-permute-start.10) | collective-permute-done | bytes 65568 | tf_op jit(solution)/shard_map/ppermute | solution.py:363
  57.7 1.6 %collective-permute-start.15 = (bf16[4,64,128]{2,1,0:T(8,128)(2,1)S(1)}, bf16[4,64,128]{2,1,0:T(8,128)(2,1)S(1)}, u32[]{:S(2)}, u32[]{:S(2)}) collective-permute-start(bf16[4,64,128]{2,1,0:T(8,128)(2,1)S(1)} %get-tuple-element.47), channel_id=1, source_target_pairs={{0,1},{1,0},{2,3},{3,2},{4,5},{5,4},{6,7},{7,6},{8,9},{9,8},{10,11... | collective-permute-start | bytes 196616 | tf_op jit(solution)/shard_map/ppermute | solution.py:363
  59.3 0.3 turn_cotangent.1.turned_ref
  59.5 0.0 collective-permute-done.11.refs_2_
  59.6 1.2 %collective-permute-done.14.refs_5_ = bf16[4,64,128]{2,1,0:T(8,128)(2,1)S(1)} collective-permute-done((bf16[4,64,128]{2,1,0:T(8,128)(2,1)S(1)}, bf16[4,64,128]{2,1,0:T(8,128)(2,1)S(1)}, u32[]{:S(2)}, u32[]{:S(2)}) %collective-permute-start.14) | collective-permute-done | bytes 65568 | tf_op jit(solution)/shard_map/ppermute | solution.py:363
  60.8 1.2 %collective-permute-done.15.refs_6_ = bf16[4,64,128]{2,1,0:T(8,128)(2,1)S(1)} collective-permute-done((bf16[4,64,128]{2,1,0:T(8,128)(2,1)S(1)}, bf16[4,64,128]{2,1,0:T(8,128)(2,1)S(1)}, u32[]{:S(2)}, u32[]{:S(2)}) %collective-permute-start.15) | collective-permute-done | bytes 65568 | tf_op jit(solution)/shard_map/ppermute | solution.py:363
  62.0 3.1 %norm_and_gradient.1 = (bf16[2,4,256,128]{3,2,1,0:T(8,128)(2,1)S(1)}, bf16[2,256,128]{2,1,0:T(8,128)(2,1)S(1)}, bf16[2,256,128]{2,1,0:T(8,128)(2,1)S(1)}, f32[576,128]{1,0:T(8,128)S(1)}, f32[576,128]{1,0:T(8,128)S(1)}) custom-call(s32[2]{0:T(128)S(1)} %copy-done.6, s32[1]{0:T(128)} %bitcast.index_ref, s32[1]{0:T(128)} %bitcast.1.core_ref, ...), custom_call_target="tpu_custom_call" | custom-call | flops 603979776 | bytes 2097152 | tf_op jit(solution)/shard_map/norm_and_gradient/pallas_call | solution.py:489
  65.0 0.1 collective-permute-start.16
  65.1 1.6 %collective-permute-done.16.other_ref = f32[576,128]{1,0:T(8,128)S(1)} collective-permute-done((f32[576,128]{1,0:T(8,128)S(1)}, f32[576,128]{1,0:T(8,128)S(1)}, u32[]{:S(2)}, u32[]{:S(2)}) %collective-permute-start.16) | collective-permute-done | bytes 294944 | tf_op jit(solution)/shard_map/ppermute | solution.py:385
  66.7 1.6 %collective-permute-start.17 = (bf16[144,128]{1,0:T(8,128)(2,1)S(1)}, bf16[144,128]{1,0:T(8,128)(2,1)S(1)}, u32[]{:S(2)}, u32[]{:S(2)}) collective-permute-start(bf16[144,128]{1,0:T(8,128)(2,1)S(1)} %get-tuple-element.54), channel_id=1, source_target_pairs={{0,1},{1,0},{2,3},{3,2},{4,5},{5,4},{6,7},{7,6},{8,9},{9,8},{10,11... | collective-permute-start | bytes 110600 | tf_op jit(solution)/shard_map/ppermute | solution.py:381
  68.4 1.5 %collective-permute-start.18 = (bf16[144,128]{1,0:T(8,128)(2,1)S(1)}, bf16[144,128]{1,0:T(8,128)(2,1)S(1)}, u32[]{:S(2)}, u32[]{:S(2)}) collective-permute-start(bf16[144,128]{1,0:T(8,128)(2,1)S(1)} %get-tuple-element.55), channel_id=1, source_target_pairs={{0,16},{1,17},{2,18},{3,19},{4,20},{5,21},{6,22},{7,23},{8,24},{9,... | collective-permute-start | bytes 110600 | tf_op jit(solution)/shard_map/ppermute | solution.py:381
  69.9 0.4 collective-permute-start.19
  70.3 0.7 collective-permute-start.21
  71.0 1.3 %collective-permute-done.18.refs_2_ = bf16[144,128]{1,0:T(8,128)(2,1)S(1)} collective-permute-done((bf16[144,128]{1,0:T(8,128)(2,1)S(1)}, bf16[144,128]{1,0:T(8,128)(2,1)S(1)}, u32[]{:S(2)}, u32[]{:S(2)}) %collective-permute-start.18) | collective-permute-done | bytes 36896 | tf_op jit(solution)/shard_map/ppermute | solution.py:381
  72.3 2.4 %collective-permute-done.19.refs_3_ = bf16[144,128]{1,0:T(8,128)(2,1)S(1)} collective-permute-done((bf16[144,128]{1,0:T(8,128)(2,1)S(1)}, bf16[144,128]{1,0:T(8,128)(2,1)S(1)}, u32[]{:S(2)}, u32[]{:S(2)}) %collective-permute-start.19) | collective-permute-done | bytes 36896 | tf_op jit(solution)/shard_map/ppermute | solution.py:381
  74.8 0.5 collective-permute-start.20
  75.3 1.4 %collective-permute-start.24 = (bf16[144,128]{1,0:T(8,128)(2,1)S(1)}, bf16[144,128]{1,0:T(8,128)(2,1)S(1)}, u32[]{:S(2)}, u32[]{:S(2)}) collective-permute-start(bf16[144,128]{1,0:T(8,128)(2,1)S(1)} %sum_chips.1.after_ref.refs_0_), channel_id=1, source_target_pairs={{0,6},{1,7},{2,4},{3,5},{4,2},{5,3},{6,0},{7,1},{8,14},{9,15},{10,... | collective-permute-start | bytes 110600 | tf_op jit(solution)/shard_map/ppermute | solution.py:363
  76.8 0.2 collective-permute-start.23
  76.9 2.8 %collective-permute-start.22 = (bf16[144,128]{1,0:T(8,128)(2,1)S(1)}, bf16[144,128]{1,0:T(8,128)(2,1)S(1)}, u32[]{:S(2)}, u32[]{:S(2)}) collective-permute-start(bf16[144,128]{1,0:T(8,128)(2,1)S(1)} %sum_chips.1.after_ref.refs_0_), channel_id=1, source_target_pairs={{0,2},{1,3},{2,0},{3,1},{4,6},{5,7},{6,4},{7,5},{8,10},{9,11},{10,... | collective-permute-start | bytes 110600 | tf_op jit(solution)/shard_map/ppermute | solution.py:363
  79.7 1.4 %collective-permute-done.24.refs_3_ = bf16[144,128]{1,0:T(8,128)(2,1)S(1)} collective-permute-done((bf16[144,128]{1,0:T(8,128)(2,1)S(1)}, bf16[144,128]{1,0:T(8,128)(2,1)S(1)}, u32[]{:S(2)}, u32[]{:S(2)}) %collective-permute-start.24) | collective-permute-done | bytes 36896 | tf_op jit(solution)/shard_map/ppermute | solution.py:363
  81.1 0.9 collective-permute-done.23.refs_2_
  82.0 0.1 collective-permute-done.22.refs_1_
  82.1 1.8 %collective-permute-start.27 = (bf16[144,128]{1,0:T(8,128)(2,1)S(1)}, bf16[144,128]{1,0:T(8,128)(2,1)S(1)}, u32[]{:S(2)}, u32[]{:S(2)}) collective-permute-start(bf16[144,128]{1,0:T(8,128)(2,1)S(1)} %sum_planes.1.refs_0_), channel_id=1, source_target_pairs={{0,17},{1,16},{2,19},{3,18},{4,21},{5,20},{6,23},{7,22},{8,25},{9,... | collective-permute-start | bytes 110600 | tf_op jit(solution)/shard_map/ppermute | solution.py:381
  83.9 1.3 %collective-permute-start.26 = (bf16[144,128]{1,0:T(8,128)(2,1)S(1)}, bf16[144,128]{1,0:T(8,128)(2,1)S(1)}, u32[]{:S(2)}, u32[]{:S(2)}) collective-permute-start(bf16[144,128]{1,0:T(8,128)(2,1)S(1)} %sum_planes.1.refs_0_), channel_id=1, source_target_pairs={{0,16},{1,17},{2,18},{3,19},{4,20},{5,21},{6,22},{7,23},{8,24},{9,... | collective-permute-start | bytes 110600 | tf_op jit(solution)/shard_map/ppermute | solution.py:381
  85.1 0.5 collective-permute-start.25
  85.6 2.2 %decode.1 = (bf16[2,4,256,128]{3,2,1,0:T(8,128)(2,1)}, f32[8,128]{1,0:T(8,128)S(1)}) custom-call(s32[1]{0:T(128)} %bitcast.index_ref, bf16[2,4,256,128]{3,2,1,0:T(8,128)(2,1)S(1)} %get-tuple-element.49.image_ref, bf16[2,256,128]{2,1,0:T(8,128)(2,1)S(1)} %collective-permute-done.20.near_ref, bf16[2,256,128]{2,1,0:T(8,128)(2,1)S(1)} %collective-permute-done.21.far_ref, ...), custom_call_target="tpu_custom_call" | custom-call | flops 603979776 | bytes 1048576 | tf_op jit(solution)/shard_map/decode/pallas_call | solution.py:527
  87.9 1.2 %collective-permute-done.25.refs_1_ = bf16[144,128]{1,0:T(8,128)(2,1)S(1)} collective-permute-done((bf16[144,128]{1,0:T(8,128)(2,1)S(1)}, bf16[144,128]{1,0:T(8,128)(2,1)S(1)}, u32[]{:S(2)}, u32[]{:S(2)}) %collective-permute-start.25) | collective-permute-done | bytes 36896 | tf_op jit(solution)/shard_map/ppermute | solution.py:381
  89.1 0.1 collective-permute-start.28
  89.2 1.4 %collective-permute-done.28.other_ref = bf16[576,128]{1,0:T(8,128)(2,1)S(1)} collective-permute-done((bf16[576,128]{1,0:T(8,128)(2,1)S(1)}, bf16[576,128]{1,0:T(8,128)(2,1)S(1)}, u32[]{:S(2)}, u32[]{:S(2)}) %collective-permute-start.28) | collective-permute-done | bytes 147488 | tf_op jit(solution)/shard_map/ppermute | solution.py:385
  90.6 0.9 spread_sums.1
  (28 shorter events, 0.2 us)
Async XLA Ops:
  0.6 14.3 %copy-start.3 = (bf16[2,4,256,128]{3,2,1,0:T(8,128)(2,1)S(1)}, bf16[2,4,256,128]{3,2,1,0:T(8,128)(2,1)}, u32[]{:S(2)}) copy-start(bf16[2,4,256,128]{3,2,1,0:T(8,128)(2,1)} %cot_ref.1) | copy-start | bytes 1572868
  0.6 14.3 %copy-start = (bf16[64,2,2048]{2,1,0:T(2,128)(2,1)S(1)}, bf16[64,2,2048]{2,1,0:T(2,128)(2,1)}, u32[]{:S(2)}) copy-start(bf16[64,2,2048]{2,1,0:T(2,128)(2,1)} %query_ref.5) | copy-start | bytes 1572868
  0.7 14.3 %copy-start.1 = (bf16[64,2,2048]{2,1,0:T(2,128)(2,1)S(1)}, bf16[64,2,2048]{2,1,0:T(2,128)(2,1)}, u32[]{:S(2)}) copy-start(bf16[64,2,2048]{2,1,0:T(2,128)(2,1)} %key_ref.5) | copy-start | bytes 1572868
  0.7 14.3 %copy-start.2 = (bf16[64,2,2048]{2,1,0:T(2,128)(2,1)S(1)}, bf16[64,2,2048]{2,1,0:T(2,128)(2,1)}, u32[]{:S(2)}) copy-start(bf16[64,2,2048]{2,1,0:T(2,128)(2,1)} %value_ref.5) | copy-start | bytes 1572868
  3.3 12.3 %collective-permute-start.3 = (bf16[3,4,64,128]{3,2,1,0:T(8,128)(2,1)}, bf16[3,4,64,128]{3,2,1,0:T(8,128)(2,1)S(1)}, u32[]{:S(2)}, u32[]{:S(2)}) collective-permute-start(bf16[3,4,64,128]{3,2,1,0:T(8,128)(2,1)} %get-tuple-element.34), channel_id=1, source_target_pairs={{0,2},{1,3},{2,0},{3,1},{4,6},{5,7},{6,4},{7,5},{8,10},{9,11},{10,... | collective-permute-start | bytes 589832 | tf_op jit(solution)/shard_map/ppermute | solution.py:363
  6.3 17.1 %collective-permute-start.5 = (bf16[3,4,64,128]{3,2,1,0:T(8,128)(2,1)}, bf16[3,4,64,128]{3,2,1,0:T(8,128)(2,1)S(1)}, u32[]{:S(2)}, u32[]{:S(2)}) collective-permute-start(bf16[3,4,64,128]{3,2,1,0:T(8,128)(2,1)} %get-tuple-element.36), channel_id=1, source_target_pairs={{0,4},{1,5},{2,6},{3,7},{4,0},{5,1},{6,2},{7,3},{8,12},{9,13},{10,... | collective-permute-start | bytes 589832 | tf_op jit(solution)/shard_map/ppermute | solution.py:363
  8.9 28.3 %collective-permute-start.6 = (bf16[3,4,64,128]{3,2,1,0:T(8,128)(2,1)}, bf16[3,4,64,128]{3,2,1,0:T(8,128)(2,1)S(1)}, u32[]{:S(2)}, u32[]{:S(2)}) collective-permute-start(bf16[3,4,64,128]{3,2,1,0:T(8,128)(2,1)} %get-tuple-element.37), channel_id=1, source_target_pairs={{0,5},{1,4},{2,7},{3,6},{4,1},{5,0},{6,3},{7,2},{8,13},{9,12},{10,... | collective-permute-start | bytes 589832 | tf_op jit(solution)/shard_map/ppermute | solution.py:363
  12.9 10.5 %copy-start.7 = (bf16[3,4,64,128]{3,2,1,0:T(8,128)(2,1)S(1)}, bf16[3,4,64,128]{3,2,1,0:T(8,128)(2,1)}, u32[]{:S(2)}) copy-start(bf16[3,4,64,128]{3,2,1,0:T(8,128)(2,1)} %get-tuple-element.39) | copy-start | bytes 589828
  13.0 25.3 %copy-start.6 = (s32[2]{0:T(128)S(1)}, s32[2]{0:T(128)}, u32[]{:S(2)}) copy-start(s32[2]{0:T(128)} %lengths_ref.1) | copy-start | bytes 28
  13.0 24.6 %collective-permute-start.2 = (bf16[3,4,64,128]{3,2,1,0:T(8,128)(2,1)}, bf16[3,4,64,128]{3,2,1,0:T(8,128)(2,1)S(1)}, u32[]{:S(2)}, u32[]{:S(2)}) collective-permute-start(bf16[3,4,64,128]{3,2,1,0:T(8,128)(2,1)} %get-tuple-element.33), channel_id=1, source_target_pairs={{0,1},{1,0},{2,3},{3,2},{4,5},{5,4},{6,7},{7,6},{8,9},{9,8},{10,11... | collective-permute-start | bytes 589832 | tf_op jit(solution)/shard_map/ppermute | solution.py:363
  13.6 24.8 %collective-permute-start.4 = (bf16[3,4,64,128]{3,2,1,0:T(8,128)(2,1)}, bf16[3,4,64,128]{3,2,1,0:T(8,128)(2,1)S(1)}, u32[]{:S(2)}, u32[]{:S(2)}) collective-permute-start(bf16[3,4,64,128]{3,2,1,0:T(8,128)(2,1)} %get-tuple-element.35), channel_id=1, source_target_pairs={{0,3},{1,2},{2,1},{3,0},{4,7},{5,6},{6,5},{7,4},{8,11},{9,10},{10,... | collective-permute-start | bytes 589832 | tf_op jit(solution)/shard_map/ppermute | solution.py:363
  15.0 0.9 %copy-start.8 = (bf16[3,4,64,128]{3,2,1,0:T(8,128)(2,1)S(1)}, bf16[3,4,64,128]{3,2,1,0:T(8,128)(2,1)}, u32[]{:S(2)}) copy-start(bf16[3,4,64,128]{3,2,1,0:T(8,128)(2,1)} %get-tuple-element.38) | copy-start | bytes 589828
  15.9 22.4 %collective-permute-start.7 = (bf16[3,4,64,128]{3,2,1,0:T(8,128)(2,1)S(1)}, bf16[3,4,64,128]{3,2,1,0:T(8,128)(2,1)S(1)}, u32[]{:S(2)}, u32[]{:S(2)}) collective-permute-start(bf16[3,4,64,128]{3,2,1,0:T(8,128)(2,1)S(1)} %copy-done.8), channel_id=1, source_target_pairs={{0,6},{1,7},{2,4},{3,5},{4,2},{5,3},{6,0},{7,1},{8,14},{9,15},{10,... | collective-permute-start | bytes 589832 | tf_op jit(solution)/shard_map/ppermute | solution.py:363
  23.4 14.9 %collective-permute-start.8 = (bf16[3,4,64,128]{3,2,1,0:T(8,128)(2,1)S(1)}, bf16[3,4,64,128]{3,2,1,0:T(8,128)(2,1)S(1)}, u32[]{:S(2)}, u32[]{:S(2)}) collective-permute-start(bf16[3,4,64,128]{3,2,1,0:T(8,128)(2,1)S(1)} %copy-done.7), channel_id=1, source_target_pairs={{0,7},{1,6},{2,5},{3,4},{4,3},{5,2},{6,1},{7,0},{8,15},{9,14},{10,... | collective-permute-start | bytes 589832 | tf_op jit(solution)/shard_map/ppermute | solution.py:363
  37.3 13.4 %collective-permute-start = (bf16[2,256,128]{2,1,0:T(8,128)(2,1)S(1)}, bf16[2,256,128]{2,1,0:T(8,128)(2,1)S(1)}, u32[]{:S(2)}, u32[]{:S(2)}) collective-permute-start(bf16[2,256,128]{2,1,0:T(8,128)(2,1)S(1)} %get-tuple-element.31), channel_id=1, source_target_pairs={{0,1},{1,0},{2,3},{3,2},{4,5},{5,4},{6,7},{7,6},{8,9},{9,8},{10,11... | collective-permute-start | bytes 393224 | tf_op jit(solution)/shard_map/ppermute | solution.py:363
  37.6 16.7 %collective-permute-start.1 = (bf16[2,256,128]{2,1,0:T(8,128)(2,1)S(1)}, bf16[2,256,128]{2,1,0:T(8,128)(2,1)S(1)}, u32[]{:S(2)}, u32[]{:S(2)}) collective-permute-start(bf16[2,256,128]{2,1,0:T(8,128)(2,1)S(1)} %get-tuple-element.32), channel_id=1, source_target_pairs={{1,2},{3,4},{5,6},{2,1},{4,3},{6,5},{9,10},{11,12},{13,14},{10,9},... | collective-permute-start | bytes 393224 | tf_op jit(solution)/shard_map/ppermute | solution.py:452
  40.4 21.5 %copy-start.5 = (f32[2048]{0:T(1024)S(1)}, f32[2048]{0:T(1024)}, u32[]{:S(2)}) copy-start(f32[2048]{0:T(1024)} %param.11) | copy-start | bytes 24580
  40.5 15.1 %collective-permute-start.9 = (bf16[4,64,128]{2,1,0:T(8,128)(2,1)S(1)}, bf16[4,64,128]{2,1,0:T(8,128)(2,1)S(1)}, u32[]{:S(2)}, u32[]{:S(2)}) collective-permute-start(bf16[4,64,128]{2,1,0:T(8,128)(2,1)S(1)} %get-tuple-element.41), channel_id=1, source_target_pairs={{0,4},{1,5},{2,6},{3,7},{4,0},{5,1},{6,2},{7,3},{8,12},{9,13},{10,... | collective-permute-start | bytes 196616 | tf_op jit(solution)/shard_map/ppermute | solution.py:363
  49.5 8.2 %collective-permute-start.10 = (bf16[4,64,128]{2,1,0:T(8,128)(2,1)S(1)}, bf16[4,64,128]{2,1,0:T(8,128)(2,1)S(1)}, u32[]{:S(2)}, u32[]{:S(2)}) collective-permute-start(bf16[4,64,128]{2,1,0:T(8,128)(2,1)S(1)} %get-tuple-element.42), channel_id=1, source_target_pairs={{0,5},{1,4},{2,7},{3,6},{4,1},{5,0},{6,3},{7,2},{8,13},{9,12},{10,... | collective-permute-start | bytes 196616 | tf_op jit(solution)/shard_map/ppermute | solution.py:363
  49.5 10.1 %collective-permute-start.11 = (bf16[4,64,128]{2,1,0:T(8,128)(2,1)S(1)}, bf16[4,64,128]{2,1,0:T(8,128)(2,1)S(1)}, u32[]{:S(2)}, u32[]{:S(2)}) collective-permute-start(bf16[4,64,128]{2,1,0:T(8,128)(2,1)S(1)} %get-tuple-element.43), channel_id=1, source_target_pairs={{0,6},{1,7},{2,4},{3,5},{4,2},{5,3},{6,0},{7,1},{8,14},{9,15},{10,... | collective-permute-start | bytes 196616 | tf_op jit(solution)/shard_map/ppermute | solution.py:363
  50.7 8.8 %collective-permute-start.12 = (bf16[4,64,128]{2,1,0:T(8,128)(2,1)S(1)}, bf16[4,64,128]{2,1,0:T(8,128)(2,1)S(1)}, u32[]{:S(2)}, u32[]{:S(2)}) collective-permute-start(bf16[4,64,128]{2,1,0:T(8,128)(2,1)S(1)} %get-tuple-element.44), channel_id=1, source_target_pairs={{0,7},{1,6},{2,5},{3,4},{4,3},{5,2},{6,1},{7,0},{8,15},{9,14},{10,... | collective-permute-start | bytes 196616 | tf_op jit(solution)/shard_map/ppermute | solution.py:363
  54.3 5.3 %collective-permute-start.13 = (bf16[4,64,128]{2,1,0:T(8,128)(2,1)S(1)}, bf16[4,64,128]{2,1,0:T(8,128)(2,1)S(1)}, u32[]{:S(2)}, u32[]{:S(2)}) collective-permute-start(bf16[4,64,128]{2,1,0:T(8,128)(2,1)S(1)} %get-tuple-element.45), channel_id=1, source_target_pairs={{0,2},{1,3},{2,0},{3,1},{4,6},{5,7},{6,4},{7,5},{8,10},{9,11},{10,... | collective-permute-start | bytes 196616 | tf_op jit(solution)/shard_map/ppermute | solution.py:363
  55.6 5.2 %collective-permute-start.14 = (bf16[4,64,128]{2,1,0:T(8,128)(2,1)S(1)}, bf16[4,64,128]{2,1,0:T(8,128)(2,1)S(1)}, u32[]{:S(2)}, u32[]{:S(2)}) collective-permute-start(bf16[4,64,128]{2,1,0:T(8,128)(2,1)S(1)} %get-tuple-element.46), channel_id=1, source_target_pairs={{0,3},{1,2},{2,1},{3,0},{4,7},{5,6},{6,5},{7,4},{8,11},{9,10},{10,... | collective-permute-start | bytes 196616 | tf_op jit(solution)/shard_map/ppermute | solution.py:363
  57.7 4.3 %collective-permute-start.15 = (bf16[4,64,128]{2,1,0:T(8,128)(2,1)S(1)}, bf16[4,64,128]{2,1,0:T(8,128)(2,1)S(1)}, u32[]{:S(2)}, u32[]{:S(2)}) collective-permute-start(bf16[4,64,128]{2,1,0:T(8,128)(2,1)S(1)} %get-tuple-element.47), channel_id=1, source_target_pairs={{0,1},{1,0},{2,3},{3,2},{4,5},{5,4},{6,7},{7,6},{8,9},{9,8},{10,11... | collective-permute-start | bytes 196616 | tf_op jit(solution)/shard_map/ppermute | solution.py:363
  62.0 23.7 %copy-start.4 = (bf16[9,128,128]{2,1,0:T(8,128)(2,1)S(1)}, bf16[9,128,128]{2,1,0:T(8,128)(2,1)}, u32[]{:S(2)}) copy-start(bf16[9,128,128]{2,1,0:T(8,128)(2,1)} %param.12) | copy-start | bytes 884740
  65.0 1.6 %collective-permute-start.16 = (f32[576,128]{1,0:T(8,128)S(1)}, f32[576,128]{1,0:T(8,128)S(1)}, u32[]{:S(2)}, u32[]{:S(2)}) collective-permute-start(f32[576,128]{1,0:T(8,128)S(1)} %get-tuple-element.52), channel_id=1, source_target_pairs={{0,8},{8,0},{16,24},{24,16},{1,9},{9,1},{17,25},{25,17},{2,10},{10... | collective-permute-start | bytes 884744 | tf_op jit(solution)/shard_map/ppermute | solution.py:385
  66.7 4.2 %collective-permute-start.17 = (bf16[144,128]{1,0:T(8,128)(2,1)S(1)}, bf16[144,128]{1,0:T(8,128)(2,1)S(1)}, u32[]{:S(2)}, u32[]{:S(2)}) collective-permute-start(bf16[144,128]{1,0:T(8,128)(2,1)S(1)} %get-tuple-element.54), channel_id=1, source_target_pairs={{0,1},{1,0},{2,3},{3,2},{4,5},{5,4},{6,7},{7,6},{8,9},{9,8},{10,11... | collective-permute-start | bytes 110600 | tf_op jit(solution)/shard_map/ppermute | solution.py:381
  68.4 4.0 %collective-permute-start.18 = (bf16[144,128]{1,0:T(8,128)(2,1)S(1)}, bf16[144,128]{1,0:T(8,128)(2,1)S(1)}, u32[]{:S(2)}, u32[]{:S(2)}) collective-permute-start(bf16[144,128]{1,0:T(8,128)(2,1)S(1)} %get-tuple-element.55), channel_id=1, source_target_pairs={{0,16},{1,17},{2,18},{3,19},{4,20},{5,21},{6,22},{7,23},{8,24},{9,... | collective-permute-start | bytes 110600 | tf_op jit(solution)/shard_map/ppermute | solution.py:381
  69.9 4.9 %collective-permute-start.19 = (bf16[144,128]{1,0:T(8,128)(2,1)S(1)}, bf16[144,128]{1,0:T(8,128)(2,1)S(1)}, u32[]{:S(2)}, u32[]{:S(2)}) collective-permute-start(bf16[144,128]{1,0:T(8,128)(2,1)S(1)} %get-tuple-element.56), channel_id=1, source_target_pairs={{0,17},{1,16},{2,19},{3,18},{4,21},{5,20},{6,23},{7,22},{8,25},{9,... | collective-permute-start | bytes 110600 | tf_op jit(solution)/shard_map/ppermute | solution.py:381
  70.3 15.3 %collective-permute-start.21 = (bf16[2,256,128]{2,1,0:T(8,128)(2,1)S(1)}, bf16[2,256,128]{2,1,0:T(8,128)(2,1)S(1)}, u32[]{:S(2)}, u32[]{:S(2)}) collective-permute-start(bf16[2,256,128]{2,1,0:T(8,128)(2,1)S(1)} %get-tuple-element.57), channel_id=1, source_target_pairs={{1,2},{3,4},{5,6},{2,1},{4,3},{6,5},{9,10},{11,12},{13,14},{10,9},... | collective-permute-start | bytes 393224 | tf_op jit(solution)/shard_map/ppermute | solution.py:514
  74.8 10.9 %collective-permute-start.20 = (bf16[2,256,128]{2,1,0:T(8,128)(2,1)S(1)}, bf16[2,256,128]{2,1,0:T(8,128)(2,1)S(1)}, u32[]{:S(2)}, u32[]{:S(2)}) collective-permute-start(bf16[2,256,128]{2,1,0:T(8,128)(2,1)S(1)} %hold.1), channel_id=1, source_target_pairs={{0,1},{1,0},{2,3},{3,2},{4,5},{5,4},{6,7},{7,6},{8,9},{9,8},{10,11... | collective-permute-start | bytes 393224 | tf_op jit(solution)/shard_map/ppermute | solution.py:363
  75.3 5.8 %collective-permute-start.24 = (bf16[144,128]{1,0:T(8,128)(2,1)S(1)}, bf16[144,128]{1,0:T(8,128)(2,1)S(1)}, u32[]{:S(2)}, u32[]{:S(2)}) collective-permute-start(bf16[144,128]{1,0:T(8,128)(2,1)S(1)} %sum_chips.1.after_ref.refs_0_), channel_id=1, source_target_pairs={{0,6},{1,7},{2,4},{3,5},{4,2},{5,3},{6,0},{7,1},{8,14},{9,15},{10,... | collective-permute-start | bytes 110600 | tf_op jit(solution)/shard_map/ppermute | solution.py:363
  76.8 5.2 %collective-permute-start.23 = (bf16[144,128]{1,0:T(8,128)(2,1)S(1)}, bf16[144,128]{1,0:T(8,128)(2,1)S(1)}, u32[]{:S(2)}, u32[]{:S(2)}) collective-permute-start(bf16[144,128]{1,0:T(8,128)(2,1)S(1)} %sum_chips.1.after_ref.refs_0_), channel_id=1, source_target_pairs={{0,4},{1,5},{2,6},{3,7},{4,0},{5,1},{6,2},{7,3},{8,12},{9,13},{10,... | collective-permute-start | bytes 110600 | tf_op jit(solution)/shard_map/ppermute | solution.py:363
  76.9 5.1 %collective-permute-start.22 = (bf16[144,128]{1,0:T(8,128)(2,1)S(1)}, bf16[144,128]{1,0:T(8,128)(2,1)S(1)}, u32[]{:S(2)}, u32[]{:S(2)}) collective-permute-start(bf16[144,128]{1,0:T(8,128)(2,1)S(1)} %sum_chips.1.after_ref.refs_0_), channel_id=1, source_target_pairs={{0,2},{1,3},{2,0},{3,1},{4,6},{5,7},{6,4},{7,5},{8,10},{9,11},{10,... | collective-permute-start | bytes 110600 | tf_op jit(solution)/shard_map/ppermute | solution.py:363
  82.1 5.8 %collective-permute-start.27 = (bf16[144,128]{1,0:T(8,128)(2,1)S(1)}, bf16[144,128]{1,0:T(8,128)(2,1)S(1)}, u32[]{:S(2)}, u32[]{:S(2)}) collective-permute-start(bf16[144,128]{1,0:T(8,128)(2,1)S(1)} %sum_planes.1.refs_0_), channel_id=1, source_target_pairs={{0,17},{1,16},{2,19},{3,18},{4,21},{5,20},{6,23},{7,22},{8,25},{9,... | collective-permute-start | bytes 110600 | tf_op jit(solution)/shard_map/ppermute | solution.py:381
  83.9 4.0 %collective-permute-start.26 = (bf16[144,128]{1,0:T(8,128)(2,1)S(1)}, bf16[144,128]{1,0:T(8,128)(2,1)S(1)}, u32[]{:S(2)}, u32[]{:S(2)}) collective-permute-start(bf16[144,128]{1,0:T(8,128)(2,1)S(1)} %sum_planes.1.refs_0_), channel_id=1, source_target_pairs={{0,16},{1,17},{2,18},{3,19},{4,20},{5,21},{6,22},{7,23},{8,24},{9,... | collective-permute-start | bytes 110600 | tf_op jit(solution)/shard_map/ppermute | solution.py:381
  85.1 4.0 %collective-permute-start.25 = (bf16[144,128]{1,0:T(8,128)(2,1)S(1)}, bf16[144,128]{1,0:T(8,128)(2,1)S(1)}, u32[]{:S(2)}, u32[]{:S(2)}) collective-permute-start(bf16[144,128]{1,0:T(8,128)(2,1)S(1)} %sum_planes.1.refs_0_), channel_id=1, source_target_pairs={{0,1},{1,0},{2,3},{3,2},{4,5},{5,4},{6,7},{7,6},{8,9},{9,8},{10,11... | collective-permute-start | bytes 110600 | tf_op jit(solution)/shard_map/ppermute | solution.py:381
  89.1 1.4 %collective-permute-start.28 = (bf16[576,128]{1,0:T(8,128)(2,1)S(1)}, bf16[576,128]{1,0:T(8,128)(2,1)S(1)}, u32[]{:S(2)}, u32[]{:S(2)}) collective-permute-start(bf16[576,128]{1,0:T(8,128)(2,1)S(1)} %join_chips.1.own_ref), channel_id=1, source_target_pairs={{0,8},{8,0},{16,24},{24,16},{1,9},{9,1},{17,25},{25,17},{2,10},{10... | collective-permute-start | bytes 442376 | tf_op jit(solution)/shard_map/ppermute | solution.py:385

commit v18 on v17

--- a/solution.py
+++ b/solution.py
@@ -511,7 +511,6 @@
         scratch=[pltpu.VMEM((half_rows, width), jnp.float32)],
         moved=quad_size * chunk_moved,
     )(quad, keep, trade_cores(send))
-    far = lax.ppermute(far, "seq", far_pairs)
     distances = range(1, quad_size)
     plane_sum = call(
         functools.partial(sum_kernel, 1.0),
@@ -524,6 +523,14 @@
     plane_sums = [plane_sum] + [
         trade(plane_sum, distance) for distance in range(inner, seq_count, inner)
     ]
+    total = call(
+        functools.partial(sum_kernel, 1.0 / math.sqrt(PATCH * columns)),
+        "sum_planes",
+        chunk_shape,
+        [VMEM()] * len(plane_sums),
+        moved=chunk_moved,
+    )(*plane_sums)
+    far = lax.ppermute(hold(far, total), "seq", far_pairs)
     decoded, done = call(
         decode_kernel,
         "decode",
@@ -536,13 +543,6 @@
         flops=conv_flops,
         moved=2 * local_bytes,
     )(index, image, near, far, conv_weight.reshape(3, 3 * width, width))
-    total = call(
-        functools.partial(sum_kernel, 1.0 / math.sqrt(PATCH * columns)),
-        "sum_planes",
-        chunk_shape,
-        [VMEM()] * len(plane_sums),
-        moved=chunk_moved,
-    )(*plane_sums)
     joined = call(
         join_kernel,
         "join_chips",

time: 91.6 us -> 94.9 us (1.036)
  starting transfers between devices: 46 us -> 48.4 us
  waiting for transfers between devices: 29.7 us -> 30.7 us
    ppermute x6, starting transfers between devices: 7.11 us -> 9.41 us  [trade_chips(): return lax.ppermute(values, ('dp', 'seq'), pairs)]
    ppermute x6, waiting for transfers between devices: 5 us -> 6.55 us  [trade_chips(): return lax.ppermute(values, ('dp', 'seq'), pairs)]
  transfers between devices with their start and end apart: 29 -> 29, of which waited for: 15 -> 16; matrix products, arithmetic and copies ran while one was open for 0% -> 0% of each run, Pallas kernels for 9% -> 8%
where the time goes in v18:
time: 94.9 us; the launch traced here: 94.8 us
  starting transfers between devices  48.4 us (51%)
  waiting for transfers between devices  30.7 us (32%)
  Pallas kernels  14.3 us (15%)
    ppermute x19, starting transfers between devices, trade(): return lax.ppermute(values, 'seq', pairs)  37.5 us
    ppermute x19, waiting for transfers between devices, trade(): return lax.ppermute(values, 'seq', pairs)  21.2 us
    ppermute x6, starting transfers between devices, trade_chips(): return lax.ppermute(values, ('dp', 'seq'), pairs)  9.41 us
    ppermute x6, waiting for transfers between devices, trade_chips(): return lax.ppermute(values, ('dp', 'seq'), pairs)  6.55 us
    pallas_call x2, Pallas kernels, pack(): call(functools.partial(pack_kernel, distances, regions, per_device), name...  5.3 us
    pallas_call x1, Pallas kernels, body(): call(functools.partial(norm_kernel, back + [0]), 'norm_and_gradient', [ja...  3.06 us
    ppermute x2, waiting for transfers between devices, trade_cores(): lax.ppermute(values, 'dp', [(i, i ^ 1) for i in range(lax.axis_size('dp'))])  2.92 us
    pallas_call x1, Pallas kernels, body(): call(decode_kernel, 'decode', [jax.ShapeDtypeStruct(cotangent.shape, jnp....  2.22 us
  transfers between devices with their start and end apart: 29, of which 16 were waited for; matrix products, arithmetic and copies ran while one was open for 0% of the time, Pallas kernels for 8%

profile of v18, /device:TPU:0, one launch (start us, length us, event | category | flops | bytes accessed | tf_op | source)
XLA Modules:
  0.0 94.8 jit_solution(14118575407205667830)
XLA Ops:
  0.6 0.0 copy-start
  0.7 0.0 copy-start.1
  0.7 0.0 copy-start.2
  0.7 2.6 %pack_early.1 = (bf16[3,4,64,128]{3,2,1,0:T(8,128)(2,1)}, bf16[3,4,64,128]{3,2,1,0:T(8,128)(2,1)}, bf16[3,4,64,128]{3,2,1,0:T(8,128)(2,1)}) custom-call(s32[1]{0:T(128)} %bitcast.index_ref, bf16[64,2,2048]{2,1,0:T(2,128)(2,1)} %query_ref.5, bf16[64,2,2048]{2,1,0:T(2,128)(2,1)} %key_ref.5, bf16[64,2,2048]{2,1,0:T(2,128)(2,1)} %value_ref.5), custom_call_target="tpu_custom_call" | custom-call | bytes 1179648 | tf_op jit(solution)/shard_map/pack_early/pallas_call | solution.py:418
  3.3 3.1 %collective-permute-start.3 = (bf16[3,4,64,128]{3,2,1,0:T(8,128)(2,1)}, bf16[3,4,64,128]{3,2,1,0:T(8,128)(2,1)S(1)}, u32[]{:S(2)}, u32[]{:S(2)}) collective-permute-start(bf16[3,4,64,128]{3,2,1,0:T(8,128)(2,1)} %get-tuple-element.34), channel_id=1, source_target_pairs={{0,2},{1,3},{2,0},{3,1},{4,6},{5,7},{6,4},{7,5},{8,10},{9,11},{10,... | collective-permute-start | bytes 589832 | tf_op jit(solution)/shard_map/ppermute | solution.py:363
  6.3 2.6 %collective-permute-start.5 = (bf16[3,4,64,128]{3,2,1,0:T(8,128)(2,1)}, bf16[3,4,64,128]{3,2,1,0:T(8,128)(2,1)S(1)}, u32[]{:S(2)}, u32[]{:S(2)}) collective-permute-start(bf16[3,4,64,128]{3,2,1,0:T(8,128)(2,1)} %get-tuple-element.36), channel_id=1, source_target_pairs={{0,4},{1,5},{2,6},{3,7},{4,0},{5,1},{6,2},{7,3},{8,12},{9,13},{10,... | collective-permute-start | bytes 589832 | tf_op jit(solution)/shard_map/ppermute | solution.py:363
  8.9 1.3 %collective-permute-start.6 = (bf16[3,4,64,128]{3,2,1,0:T(8,128)(2,1)}, bf16[3,4,64,128]{3,2,1,0:T(8,128)(2,1)S(1)}, u32[]{:S(2)}, u32[]{:S(2)}) collective-permute-start(bf16[3,4,64,128]{3,2,1,0:T(8,128)(2,1)} %get-tuple-element.37), channel_id=1, source_target_pairs={{0,5},{1,4},{2,7},{3,6},{4,1},{5,0},{6,3},{7,2},{8,13},{9,12},{10,... | collective-permute-start | bytes 589832 | tf_op jit(solution)/shard_map/ppermute | solution.py:363
  10.2 2.7 %pack_late.1 = (bf16[3,4,64,128]{3,2,1,0:T(8,128)(2,1)}, bf16[3,4,64,128]{3,2,1,0:T(8,128)(2,1)}, bf16[3,4,64,128]{3,2,1,0:T(8,128)(2,1)}, bf16[3,4,64,128]{3,2,1,0:T(8,128)(2,1)}) custom-call(s32[1]{0:T(128)} %bitcast.index_ref, bf16[64,2,2048]{2,1,0:T(2,128)(2,1)} %query_ref.5, bf16[64,2,2048]{2,1,0:T(2,128)(2,1)} %key_ref.5, bf16[64,2,2048]{2,1,0:T(2,128)(2,1)} %value_ref.5), custom_call_target="tpu_custom_call" | custom-call | bytes 1572864 | tf_op jit(solution)/shard_map/pack_late/pallas_call | solution.py:418
  13.0 0.0 copy-start.6
  13.0 0.6 collective-permute-start.2
  13.6 1.4 %collective-permute-start.4 = (bf16[3,4,64,128]{3,2,1,0:T(8,128)(2,1)}, bf16[3,4,64,128]{3,2,1,0:T(8,128)(2,1)S(1)}, u32[]{:S(2)}, u32[]{:S(2)}) collective-permute-start(bf16[3,4,64,128]{3,2,1,0:T(8,128)(2,1)} %get-tuple-element.35), channel_id=1, source_target_pairs={{0,3},{1,2},{2,1},{3,0},{4,7},{5,6},{6,5},{7,4},{8,11},{9,10},{10,... | collective-permute-start | bytes 589832 | tf_op jit(solution)/shard_map/ppermute | solution.py:363
  15.0 0.4 own_chunk.1
  15.4 0.1 collective-permute-done.3.refs_1_
  15.6 0.3 copy-done.8
  15.9 3.6 %collective-permute-start.7 = (bf16[3,4,64,128]{3,2,1,0:T(8,128)(2,1)S(1)}, bf16[3,4,64,128]{3,2,1,0:T(8,128)(2,1)S(1)}, u32[]{:S(2)}, u32[]{:S(2)}) collective-permute-start(bf16[3,4,64,128]{3,2,1,0:T(8,128)(2,1)S(1)} %copy-done.8), channel_id=1, source_target_pairs={{0,6},{1,7},{2,4},{3,5},{4,2},{5,3},{6,0},{7,1},{8,14},{9,15},{10,... | collective-permute-start | bytes 589832 | tf_op jit(solution)/shard_map/ppermute | solution.py:363
  19.5 3.9 %collective-permute-done.5.refs_3_ = bf16[3,4,64,128]{3,2,1,0:T(8,128)(2,1)S(1)} collective-permute-done((bf16[3,4,64,128]{3,2,1,0:T(8,128)(2,1)}, bf16[3,4,64,128]{3,2,1,0:T(8,128)(2,1)S(1)}, u32[]{:S(2)}, u32[]{:S(2)}) %collective-permute-start.5) | collective-permute-done | bytes 196640 | tf_op jit(solution)/shard_map/ppermute | solution.py:363
  23.4 3.7 %collective-permute-start.8 = (bf16[3,4,64,128]{3,2,1,0:T(8,128)(2,1)S(1)}, bf16[3,4,64,128]{3,2,1,0:T(8,128)(2,1)S(1)}, u32[]{:S(2)}, u32[]{:S(2)}) collective-permute-start(bf16[3,4,64,128]{3,2,1,0:T(8,128)(2,1)S(1)} %copy-done.7), channel_id=1, source_target_pairs={{0,7},{1,6},{2,5},{3,4},{4,3},{5,2},{6,1},{7,0},{8,15},{9,14},{10,... | collective-permute-start | bytes 589832 | tf_op jit(solution)/shard_map/ppermute | solution.py:363
  27.1 10.2 %collective-permute-done.6.refs_4_ = bf16[3,4,64,128]{3,2,1,0:T(8,128)(2,1)S(1)} collective-permute-done((bf16[3,4,64,128]{3,2,1,0:T(8,128)(2,1)}, bf16[3,4,64,128]{3,2,1,0:T(8,128)(2,1)S(1)}, u32[]{:S(2)}, u32[]{:S(2)}) %collective-permute-start.6) | collective-permute-done | bytes 196640 | tf_op jit(solution)/shard_map/ppermute | solution.py:363
  37.3 0.3 collective-permute-start
  37.6 0.0 collective-permute-done.2.refs_0_
  37.6 0.7 collective-permute-start.1
  38.2 0.1 fusion.2.lengths_ref
  38.3 0.0 collective-permute-done.4.refs_2_
  38.3 0.0 collective-permute-done.8.refs_6_
  38.3 2.1 %attend.1 = (bf16[4,64,128]{2,1,0:T(8,128)(2,1)S(1)}, bf16[4,64,128]{2,1,0:T(8,128)(2,1)S(1)}, bf16[4,64,128]{2,1,0:T(8,128)(2,1)S(1)}, bf16[4,64,128]{2,1,0:T(8...) custom-call(s32[1]{0:T(128)} %bitcast.index_ref, ...), custom_call_target="tpu_custom_call" | custom-call | flops 536870912 | bytes 2097152 | tf_op jit(solution)/shard_map/attend/pallas_call | solution.py:465
  40.4 0.0 copy-start.5
  40.5 9.0 %collective-permute-start.9 = (bf16[4,64,128]{2,1,0:T(8,128)(2,1)S(1)}, bf16[4,64,128]{2,1,0:T(8,128)(2,1)S(1)}, u32[]{:S(2)}, u32[]{:S(2)}) collective-permute-start(bf16[4,64,128]{2,1,0:T(8,128)(2,1)S(1)} %get-tuple-element.41), channel_id=1, source_target_pairs={{0,4},{1,5},{2,6},{3,7},{4,0},{5,1},{6,2},{7,3},{8,12},{9,13},{10,... | collective-permute-start | bytes 196616 | tf_op jit(solution)/shard_map/ppermute | solution.py:363
  49.5 0.0 collective-permute-start.10
  49.5 1.2 %collective-permute-start.11 = (bf16[4,64,128]{2,1,0:T(8,128)(2,1)S(1)}, bf16[4,64,128]{2,1,0:T(8,128)(2,1)S(1)}, u32[]{:S(2)}, u32[]{:S(2)}) collective-permute-start(bf16[4,64,128]{2,1,0:T(8,128)(2,1)S(1)} %get-tuple-element.43), channel_id=1, source_target_pairs={{0,6},{1,7},{2,4},{3,5},{4,2},{5,3},{6,0},{7,1},{8,14},{9,15},{10,... | collective-permute-start | bytes 196616 | tf_op jit(solution)/shard_map/ppermute | solution.py:363
  50.7 0.0 collective-permute-done.near_ref
  50.7 3.6 %collective-permute-start.12 = (bf16[4,64,128]{2,1,0:T(8,128)(2,1)S(1)}, bf16[4,64,128]{2,1,0:T(8,128)(2,1)S(1)}, u32[]{:S(2)}, u32[]{:S(2)}) collective-permute-start(bf16[4,64,128]{2,1,0:T(8,128)(2,1)S(1)} %get-tuple-element.44), channel_id=1, source_target_pairs={{0,7},{1,6},{2,5},{3,4},{4,3},{5,2},{6,1},{7,0},{8,15},{9,14},{10,... | collective-permute-start | bytes 196616 | tf_op jit(solution)/shard_map/ppermute | solution.py:363
  54.3 0.0 collective-permute-done.1.far_ref
  54.3 1.3 %collective-permute-done.9.refs_0_ = bf16[4,64,128]{2,1,0:T(8,128)(2,1)S(1)} collective-permute-done((bf16[4,64,128]{2,1,0:T(8,128)(2,1)S(1)}, bf16[4,64,128]{2,1,0:T(8,128)(2,1)S(1)}, u32[]{:S(2)}, u32[]{:S(2)}) %collective-permute-start.9) | collective-permute-done | bytes 65568 | tf_op jit(solution)/shard_map/ppermute | solution.py:363
  55.6 0.6 collective-permute-start.14
  56.2 1.5 %collective-permute-done.10.refs_1_ = bf16[4,64,128]{2,1,0:T(8,128)(2,1)S(1)} collective-permute-done((bf16[4,64,128]{2,1,0:T(8,128)(2,1)S(1)}, bf16[4,64,128]{2,1,0:T(8,128)(2,1)S(1)}, u32[]{:S(2)}, u32[]{:S(2)}) %collective-permute-start.10) | collective-permute-done | bytes 65568 | tf_op jit(solution)/shard_map/ppermute | solution.py:363
  57.7 1.6 %collective-permute-start.15 = (bf16[4,64,128]{2,1,0:T(8,128)(2,1)S(1)}, bf16[4,64,128]{2,1,0:T(8,128)(2,1)S(1)}, u32[]{:S(2)}, u32[]{:S(2)}) collective-permute-start(bf16[4,64,128]{2,1,0:T(8,128)(2,1)S(1)} %get-tuple-element.47), channel_id=1, source_target_pairs={{0,1},{1,0},{2,3},{3,2},{4,5},{5,4},{6,7},{7,6},{8,9},{9,8},{10,11... | collective-permute-start | bytes 196616 | tf_op jit(solution)/shard_map/ppermute | solution.py:363
  59.3 0.3 turn_cotangent.1.turned_ref
  59.5 0.0 collective-permute-done.11.refs_2_
  59.5 0.0 collective-permute-done.12.refs_3_
  59.6 1.2 %collective-permute-done.14.refs_5_ = bf16[4,64,128]{2,1,0:T(8,128)(2,1)S(1)} collective-permute-done((bf16[4,64,128]{2,1,0:T(8,128)(2,1)S(1)}, bf16[4,64,128]{2,1,0:T(8,128)(2,1)S(1)}, u32[]{:S(2)}, u32[]{:S(2)}) %collective-permute-start.14) | collective-permute-done | bytes 65568 | tf_op jit(solution)/shard_map/ppermute | solution.py:363
  60.8 1.2 %collective-permute-done.15.refs_6_ = bf16[4,64,128]{2,1,0:T(8,128)(2,1)S(1)} collective-permute-done((bf16[4,64,128]{2,1,0:T(8,128)(2,1)S(1)}, bf16[4,64,128]{2,1,0:T(8,128)(2,1)S(1)}, u32[]{:S(2)}, u32[]{:S(2)}) %collective-permute-start.15) | collective-permute-done | bytes 65568 | tf_op jit(solution)/shard_map/ppermute | solution.py:363
  62.0 3.1 %norm_and_gradient.1 = (bf16[2,4,256,128]{3,2,1,0:T(8,128)(2,1)S(1)}, bf16[2,256,128]{2,1,0:T(8,128)(2,1)S(1)}, bf16[2,256,128]{2,1,0:T(8,128)(2,1)S(1)}, f32[576,128]{1,0:T(8,128)S(1)}, f32[576,128]{1,0:T(8,128)S(1)}) custom-call(s32[2]{0:T(128)S(1)} %copy-done.6, s32[1]{0:T(128)} %bitcast.index_ref, s32[1]{0:T(128)} %bitcast.1.core_ref, ...), custom_call_target="tpu_custom_call" | custom-call | flops 603979776 | bytes 2097152 | tf_op jit(solution)/shard_map/norm_and_gradient/pallas_call | solution.py:489
  65.0 0.1 collective-permute-start.16
  65.1 1.6 %collective-permute-done.16.other_ref = f32[576,128]{1,0:T(8,128)S(1)} collective-permute-done((f32[576,128]{1,0:T(8,128)S(1)}, f32[576,128]{1,0:T(8,128)S(1)}, u32[]{:S(2)}, u32[]{:S(2)}) %collective-permute-start.16) | collective-permute-done | bytes 294944 | tf_op jit(solution)/shard_map/ppermute | solution.py:385
  66.7 1.6 %collective-permute-start.17 = (bf16[144,128]{1,0:T(8,128)(2,1)S(1)}, bf16[144,128]{1,0:T(8,128)(2,1)S(1)}, u32[]{:S(2)}, u32[]{:S(2)}) collective-permute-start(bf16[144,128]{1,0:T(8,128)(2,1)S(1)} %get-tuple-element.54), channel_id=1, source_target_pairs={{0,1},{1,0},{2,3},{3,2},{4,5},{5,4},{6,7},{7,6},{8,9},{9,8},{10,11... | collective-permute-start | bytes 110600 | tf_op jit(solution)/shard_map/ppermute | solution.py:381
  68.4 1.9 %collective-permute-start.18 = (bf16[144,128]{1,0:T(8,128)(2,1)S(1)}, bf16[144,128]{1,0:T(8,128)(2,1)S(1)}, u32[]{:S(2)}, u32[]{:S(2)}) collective-permute-start(bf16[144,128]{1,0:T(8,128)(2,1)S(1)} %get-tuple-element.55), channel_id=1, source_target_pairs={{0,16},{1,17},{2,18},{3,19},{4,20},{5,21},{6,22},{7,23},{8,24},{9,... | collective-permute-start | bytes 110600 | tf_op jit(solution)/shard_map/ppermute | solution.py:381
  70.3 0.0 collective-permute-start.19
  70.3 0.5 collective-permute-done.17.refs_1_
  70.8 1.6 %collective-permute-done.18.refs_2_ = bf16[144,128]{1,0:T(8,128)(2,1)S(1)} collective-permute-done((bf16[144,128]{1,0:T(8,128)(2,1)S(1)}, bf16[144,128]{1,0:T(8,128)(2,1)S(1)}, u32[]{:S(2)}, u32[]{:S(2)}) %collective-permute-start.18) | collective-permute-done | bytes 36896 | tf_op jit(solution)/shard_map/ppermute | solution.py:381
  72.3 2.8 %collective-permute-done.19.refs_3_ = bf16[144,128]{1,0:T(8,128)(2,1)S(1)} collective-permute-done((bf16[144,128]{1,0:T(8,128)(2,1)S(1)}, bf16[144,128]{1,0:T(8,128)(2,1)S(1)}, u32[]{:S(2)}, u32[]{:S(2)}) %collective-permute-start.19) | collective-permute-done | bytes 36896 | tf_op jit(solution)/shard_map/ppermute | solution.py:381
  75.2 1.5 %collective-permute-start.23 = (bf16[144,128]{1,0:T(8,128)(2,1)S(1)}, bf16[144,128]{1,0:T(8,128)(2,1)S(1)}, u32[]{:S(2)}, u32[]{:S(2)}) collective-permute-start(bf16[144,128]{1,0:T(8,128)(2,1)S(1)} %sum_chips.1.after_ref.refs_0_), channel_id=1, source_target_pairs={{0,6},{1,7},{2,4},{3,5},{4,2},{5,3},{6,0},{7,1},{8,14},{9,15},{10,... | collective-permute-start | bytes 110600 | tf_op jit(solution)/shard_map/ppermute | solution.py:363
  76.6 3.0 %collective-permute-start.21 = (bf16[144,128]{1,0:T(8,128)(2,1)S(1)}, bf16[144,128]{1,0:T(8,128)(2,1)S(1)}, u32[]{:S(2)}, u32[]{:S(2)}) collective-permute-start(bf16[144,128]{1,0:T(8,128)(2,1)S(1)} %sum_chips.1.after_ref.refs_0_), channel_id=1, source_target_pairs={{0,2},{1,3},{2,0},{3,1},{4,6},{5,7},{6,4},{7,5},{8,10},{9,11},{10,... | collective-permute-start | bytes 110600 | tf_op jit(solution)/shard_map/ppermute | solution.py:363
  79.6 0.5 collective-permute-start.20
  80.2 0.8 collective-permute-done.23.refs_3_
  81.0 0.9 collective-permute-done.22.refs_2_
  81.9 0.1 collective-permute-done.21.refs_1_
  82.0 0.7 collective-permute-start.24
  82.7 4.0 %collective-permute-start.27 = (bf16[144,128]{1,0:T(8,128)(2,1)S(1)}, bf16[144,128]{1,0:T(8,128)(2,1)S(1)}, u32[]{:S(2)}, u32[]{:S(2)}) collective-permute-start(bf16[144,128]{1,0:T(8,128)(2,1)S(1)} %sum_planes.1.after_ref.refs_0_), channel_id=1, source_target_pairs={{0,17},{1,16},{2,19},{3,18},{4,21},{5,20},{6,23},{7,22},{8,25},{9,... | collective-permute-start | bytes 110600 | tf_op jit(solution)/shard_map/ppermute | solution.py:381
  86.6 1.9 %collective-permute-start.26 = (bf16[144,128]{1,0:T(8,128)(2,1)S(1)}, bf16[144,128]{1,0:T(8,128)(2,1)S(1)}, u32[]{:S(2)}, u32[]{:S(2)}) collective-permute-start(bf16[144,128]{1,0:T(8,128)(2,1)S(1)} %sum_planes.1.after_ref.refs_0_), channel_id=1, source_target_pairs={{0,16},{1,17},{2,18},{3,19},{4,20},{5,21},{6,22},{7,23},{8,24},{9,... | collective-permute-start | bytes 110600 | tf_op jit(solution)/shard_map/ppermute | solution.py:381
  88.5 2.2 %decode.1 = (bf16[2,4,256,128]{3,2,1,0:T(8,128)(2,1)}, f32[8,128]{1,0:T(8,128)S(1)}) custom-call(s32[1]{0:T(128)} %bitcast.index_ref, bf16[2,4,256,128]{3,2,1,0:T(8,128)(2,1)S(1)} %get-tuple-element.49.image_ref, bf16[2,256,128]{2,1,0:T(8,128)(2,1)S(1)} %collective-permute-done.20.near_ref, bf16[2,256,128]{2,1,0:T(8,128)(2,1)S(1)} %collective-permute-done.24.far_ref, ...), custom_call_target="tpu_custom_call" | custom-call | flops 603979776 | bytes 1048576 | tf_op jit(solution)/shard_map/decode/pallas_call | solution.py:534
  90.8 1.7 %collective-permute-done.25.refs_1_ = bf16[144,128]{1,0:T(8,128)(2,1)S(1)} collective-permute-done((bf16[144,128]{1,0:T(8,128)(2,1)S(1)}, bf16[144,128]{1,0:T(8,128)(2,1)S(1)}, u32[]{:S(2)}, u32[]{:S(2)}) %collective-permute-start.25) | collective-permute-done | bytes 36896 | tf_op jit(solution)/shard_map/ppermute | solution.py:381
  92.5 0.1 collective-permute-start.28
  92.6 1.4 %collective-permute-done.28.other_ref = bf16[576,128]{1,0:T(8,128)(2,1)S(1)} collective-permute-done((bf16[576,128]{1,0:T(8,128)(2,1)S(1)}, bf16[576,128]{1,0:T(8,128)(2,1)S(1)}, u32[]{:S(2)}, u32[]{:S(2)}) %collective-permute-start.28) | collective-permute-done | bytes 147488 | tf_op jit(solution)/shard_map/ppermute | solution.py:385
  93.9 0.9 spread_sums.1
  (29 shorter events, 0.2 us)
Async XLA Ops:
  0.6 14.3 %copy-start.3 = (bf16[2,4,256,128]{3,2,1,0:T(8,128)(2,1)S(1)}, bf16[2,4,256,128]{3,2,1,0:T(8,128)(2,1)}, u32[]{:S(2)}) copy-start(bf16[2,4,256,128]{3,2,1,0:T(8,128)(2,1)} %cot_ref.1) | copy-start | bytes 1572868
  0.6 14.3 %copy-start = (bf16[64,2,2048]{2,1,0:T(2,128)(2,1)S(1)}, bf16[64,2,2048]{2,1,0:T(2,128)(2,1)}, u32[]{:S(2)}) copy-start(bf16[64,2,2048]{2,1,0:T(2,128)(2,1)} %query_ref.5) | copy-start | bytes 1572868
  0.7 14.3 %copy-start.1 = (bf16[64,2,2048]{2,1,0:T(2,128)(2,1)S(1)}, bf16[64,2,2048]{2,1,0:T(2,128)(2,1)}, u32[]{:S(2)}) copy-start(bf16[64,2,2048]{2,1,0:T(2,128)(2,1)} %key_ref.5) | copy-start | bytes 1572868
  0.7 14.3 %copy-start.2 = (bf16[64,2,2048]{2,1,0:T(2,128)(2,1)S(1)}, bf16[64,2,2048]{2,1,0:T(2,128)(2,1)}, u32[]{:S(2)}) copy-start(bf16[64,2,2048]{2,1,0:T(2,128)(2,1)} %value_ref.5) | copy-start | bytes 1572868
  3.3 12.3 %collective-permute-start.3 = (bf16[3,4,64,128]{3,2,1,0:T(8,128)(2,1)}, bf16[3,4,64,128]{3,2,1,0:T(8,128)(2,1)S(1)}, u32[]{:S(2)}, u32[]{:S(2)}) collective-permute-start(bf16[3,4,64,128]{3,2,1,0:T(8,128)(2,1)} %get-tuple-element.34), channel_id=1, source_target_pairs={{0,2},{1,3},{2,0},{3,1},{4,6},{5,7},{6,4},{7,5},{8,10},{9,11},{10,... | collective-permute-start | bytes 589832 | tf_op jit(solution)/shard_map/ppermute | solution.py:363
  6.3 17.1 %collective-permute-start.5 = (bf16[3,4,64,128]{3,2,1,0:T(8,128)(2,1)}, bf16[3,4,64,128]{3,2,1,0:T(8,128)(2,1)S(1)}, u32[]{:S(2)}, u32[]{:S(2)}) collective-permute-start(bf16[3,4,64,128]{3,2,1,0:T(8,128)(2,1)} %get-tuple-element.36), channel_id=1, source_target_pairs={{0,4},{1,5},{2,6},{3,7},{4,0},{5,1},{6,2},{7,3},{8,12},{9,13},{10,... | collective-permute-start | bytes 589832 | tf_op jit(solution)/shard_map/ppermute | solution.py:363
  8.9 28.3 %collective-permute-start.6 = (bf16[3,4,64,128]{3,2,1,0:T(8,128)(2,1)}, bf16[3,4,64,128]{3,2,1,0:T(8,128)(2,1)S(1)}, u32[]{:S(2)}, u32[]{:S(2)}) collective-permute-start(bf16[3,4,64,128]{3,2,1,0:T(8,128)(2,1)} %get-tuple-element.37), channel_id=1, source_target_pairs={{0,5},{1,4},{2,7},{3,6},{4,1},{5,0},{6,3},{7,2},{8,13},{9,12},{10,... | collective-permute-start | bytes 589832 | tf_op jit(solution)/shard_map/ppermute | solution.py:363
  12.9 10.5 %copy-start.7 = (bf16[3,4,64,128]{3,2,1,0:T(8,128)(2,1)S(1)}, bf16[3,4,64,128]{3,2,1,0:T(8,128)(2,1)}, u32[]{:S(2)}) copy-start(bf16[3,4,64,128]{3,2,1,0:T(8,128)(2,1)} %get-tuple-element.39) | copy-start | bytes 589828
  13.0 25.3 %copy-start.6 = (s32[2]{0:T(128)S(1)}, s32[2]{0:T(128)}, u32[]{:S(2)}) copy-start(s32[2]{0:T(128)} %lengths_ref.1) | copy-start | bytes 28
  13.0 24.6 %collective-permute-start.2 = (bf16[3,4,64,128]{3,2,1,0:T(8,128)(2,1)}, bf16[3,4,64,128]{3,2,1,0:T(8,128)(2,1)S(1)}, u32[]{:S(2)}, u32[]{:S(2)}) collective-permute-start(bf16[3,4,64,128]{3,2,1,0:T(8,128)(2,1)} %get-tuple-element.33), channel_id=1, source_target_pairs={{0,1},{1,0},{2,3},{3,2},{4,5},{5,4},{6,7},{7,6},{8,9},{9,8},{10,11... | collective-permute-start | bytes 589832 | tf_op jit(solution)/shard_map/ppermute | solution.py:363
  13.6 24.8 %collective-permute-start.4 = (bf16[3,4,64,128]{3,2,1,0:T(8,128)(2,1)}, bf16[3,4,64,128]{3,2,1,0:T(8,128)(2,1)S(1)}, u32[]{:S(2)}, u32[]{:S(2)}) collective-permute-start(bf16[3,4,64,128]{3,2,1,0:T(8,128)(2,1)} %get-tuple-element.35), channel_id=1, source_target_pairs={{0,3},{1,2},{2,1},{3,0},{4,7},{5,6},{6,5},{7,4},{8,11},{9,10},{10,... | collective-permute-start | bytes 589832 | tf_op jit(solution)/shard_map/ppermute | solution.py:363
  15.0 0.9 copy-start.8
  15.9 22.4 %collective-permute-start.7 = (bf16[3,4,64,128]{3,2,1,0:T(8,128)(2,1)S(1)}, bf16[3,4,64,128]{3,2,1,0:T(8,128)(2,1)S(1)}, u32[]{:S(2)}, u32[]{:S(2)}) collective-permute-start(bf16[3,4,64,128]{3,2,1,0:T(8,128)(2,1)S(1)} %copy-done.8), channel_id=1, source_target_pairs={{0,6},{1,7},{2,4},{3,5},{4,2},{5,3},{6,0},{7,1},{8,14},{9,15},{10,... | collective-permute-start | bytes 589832 | tf_op jit(solution)/shard_map/ppermute | solution.py:363
  23.4 14.9 %collective-permute-start.8 = (bf16[3,4,64,128]{3,2,1,0:T(8,128)(2,1)S(1)}, bf16[3,4,64,128]{3,2,1,0:T(8,128)(2,1)S(1)}, u32[]{:S(2)}, u32[]{:S(2)}) collective-permute-start(bf16[3,4,64,128]{3,2,1,0:T(8,128)(2,1)S(1)} %copy-done.7), channel_id=1, source_target_pairs={{0,7},{1,6},{2,5},{3,4},{4,3},{5,2},{6,1},{7,0},{8,15},{9,14},{10,... | collective-permute-start | bytes 589832 | tf_op jit(solution)/shard_map/ppermute | solution.py:363
  37.3 13.4 %collective-permute-start = (bf16[2,256,128]{2,1,0:T(8,128)(2,1)S(1)}, bf16[2,256,128]{2,1,0:T(8,128)(2,1)S(1)}, u32[]{:S(2)}, u32[]{:S(2)}) collective-permute-start(bf16[2,256,128]{2,1,0:T(8,128)(2,1)S(1)} %get-tuple-element.31), channel_id=1, source_target_pairs={{0,1},{1,0},{2,3},{3,2},{4,5},{5,4},{6,7},{7,6},{8,9},{9,8},{10,11... | collective-permute-start | bytes 393224 | tf_op jit(solution)/shard_map/ppermute | solution.py:363
  37.6 16.7 %collective-permute-start.1 = (bf16[2,256,128]{2,1,0:T(8,128)(2,1)S(1)}, bf16[2,256,128]{2,1,0:T(8,128)(2,1)S(1)}, u32[]{:S(2)}, u32[]{:S(2)}) collective-permute-start(bf16[2,256,128]{2,1,0:T(8,128)(2,1)S(1)} %get-tuple-element.32), channel_id=1, source_target_pairs={{1,2},{3,4},{5,6},{2,1},{4,3},{6,5},{9,10},{11,12},{13,14},{10,9},... | collective-permute-start | bytes 393224 | tf_op jit(solution)/shard_map/ppermute | solution.py:452
  40.4 21.5 %copy-start.5 = (f32[2048]{0:T(1024)S(1)}, f32[2048]{0:T(1024)}, u32[]{:S(2)}) copy-start(f32[2048]{0:T(1024)} %param.11) | copy-start | bytes 24580
  40.5 15.1 %collective-permute-start.9 = (bf16[4,64,128]{2,1,0:T(8,128)(2,1)S(1)}, bf16[4,64,128]{2,1,0:T(8,128)(2,1)S(1)}, u32[]{:S(2)}, u32[]{:S(2)}) collective-permute-start(bf16[4,64,128]{2,1,0:T(8,128)(2,1)S(1)} %get-tuple-element.41), channel_id=1, source_target_pairs={{0,4},{1,5},{2,6},{3,7},{4,0},{5,1},{6,2},{7,3},{8,12},{9,13},{10,... | collective-permute-start | bytes 196616 | tf_op jit(solution)/shard_map/ppermute | solution.py:363
  49.5 8.2 %collective-permute-start.10 = (bf16[4,64,128]{2,1,0:T(8,128)(2,1)S(1)}, bf16[4,64,128]{2,1,0:T(8,128)(2,1)S(1)}, u32[]{:S(2)}, u32[]{:S(2)}) collective-permute-start(bf16[4,64,128]{2,1,0:T(8,128)(2,1)S(1)} %get-tuple-element.42), channel_id=1, source_target_pairs={{0,5},{1,4},{2,7},{3,6},{4,1},{5,0},{6,3},{7,2},{8,13},{9,12},{10,... | collective-permute-start | bytes 196616 | tf_op jit(solution)/shard_map/ppermute | solution.py:363
  49.5 10.1 %collective-permute-start.11 = (bf16[4,64,128]{2,1,0:T(8,128)(2,1)S(1)}, bf16[4,64,128]{2,1,0:T(8,128)(2,1)S(1)}, u32[]{:S(2)}, u32[]{:S(2)}) collective-permute-start(bf16[4,64,128]{2,1,0:T(8,128)(2,1)S(1)} %get-tuple-element.43), channel_id=1, source_target_pairs={{0,6},{1,7},{2,4},{3,5},{4,2},{5,3},{6,0},{7,1},{8,14},{9,15},{10,... | collective-permute-start | bytes 196616 | tf_op jit(solution)/shard_map/ppermute | solution.py:363
  50.7 8.8 %collective-permute-start.12 = (bf16[4,64,128]{2,1,0:T(8,128)(2,1)S(1)}, bf16[4,64,128]{2,1,0:T(8,128)(2,1)S(1)}, u32[]{:S(2)}, u32[]{:S(2)}) collective-permute-start(bf16[4,64,128]{2,1,0:T(8,128)(2,1)S(1)} %get-tuple-element.44), channel_id=1, source_target_pairs={{0,7},{1,6},{2,5},{3,4},{4,3},{5,2},{6,1},{7,0},{8,15},{9,14},{10,... | collective-permute-start | bytes 196616 | tf_op jit(solution)/shard_map/ppermute | solution.py:363
  54.3 5.3 %collective-permute-start.13 = (bf16[4,64,128]{2,1,0:T(8,128)(2,1)S(1)}, bf16[4,64,128]{2,1,0:T(8,128)(2,1)S(1)}, u32[]{:S(2)}, u32[]{:S(2)}) collective-permute-start(bf16[4,64,128]{2,1,0:T(8,128)(2,1)S(1)} %get-tuple-element.45), channel_id=1, source_target_pairs={{0,2},{1,3},{2,0},{3,1},{4,6},{5,7},{6,4},{7,5},{8,10},{9,11},{10,... | collective-permute-start | bytes 196616 | tf_op jit(solution)/shard_map/ppermute | solution.py:363
  55.6 5.2 %collective-permute-start.14 = (bf16[4,64,128]{2,1,0:T(8,128)(2,1)S(1)}, bf16[4,64,128]{2,1,0:T(8,128)(2,1)S(1)}, u32[]{:S(2)}, u32[]{:S(2)}) collective-permute-start(bf16[4,64,128]{2,1,0:T(8,128)(2,1)S(1)} %get-tuple-element.46), channel_id=1, source_target_pairs={{0,3},{1,2},{2,1},{3,0},{4,7},{5,6},{6,5},{7,4},{8,11},{9,10},{10,... | collective-permute-start | bytes 196616 | tf_op jit(solution)/shard_map/ppermute | solution.py:363
  57.7 4.3 %collective-permute-start.15 = (bf16[4,64,128]{2,1,0:T(8,128)(2,1)S(1)}, bf16[4,64,128]{2,1,0:T(8,128)(2,1)S(1)}, u32[]{:S(2)}, u32[]{:S(2)}) collective-permute-start(bf16[4,64,128]{2,1,0:T(8,128)(2,1)S(1)} %get-tuple-element.47), channel_id=1, source_target_pairs={{0,1},{1,0},{2,3},{3,2},{4,5},{5,4},{6,7},{7,6},{8,9},{9,8},{10,11... | collective-permute-start | bytes 196616 | tf_op jit(solution)/shard_map/ppermute | solution.py:363
  62.0 26.6 %copy-start.4 = (bf16[9,128,128]{2,1,0:T(8,128)(2,1)S(1)}, bf16[9,128,128]{2,1,0:T(8,128)(2,1)}, u32[]{:S(2)}) copy-start(bf16[9,128,128]{2,1,0:T(8,128)(2,1)} %param.12) | copy-start | bytes 884740
  65.0 1.6 %collective-permute-start.16 = (f32[576,128]{1,0:T(8,128)S(1)}, f32[576,128]{1,0:T(8,128)S(1)}, u32[]{:S(2)}, u32[]{:S(2)}) collective-permute-start(f32[576,128]{1,0:T(8,128)S(1)} %get-tuple-element.52), channel_id=1, source_target_pairs={{0,8},{8,0},{16,24},{24,16},{1,9},{9,1},{17,25},{25,17},{2,10},{10... | collective-permute-start | bytes 884744 | tf_op jit(solution)/shard_map/ppermute | solution.py:385
  66.7 4.0 %collective-permute-start.17 = (bf16[144,128]{1,0:T(8,128)(2,1)S(1)}, bf16[144,128]{1,0:T(8,128)(2,1)S(1)}, u32[]{:S(2)}, u32[]{:S(2)}) collective-permute-start(bf16[144,128]{1,0:T(8,128)(2,1)S(1)} %get-tuple-element.54), channel_id=1, source_target_pairs={{0,1},{1,0},{2,3},{3,2},{4,5},{5,4},{6,7},{7,6},{8,9},{9,8},{10,11... | collective-permute-start | bytes 110600 | tf_op jit(solution)/shard_map/ppermute | solution.py:381
  68.4 4.0 %collective-permute-start.18 = (bf16[144,128]{1,0:T(8,128)(2,1)S(1)}, bf16[144,128]{1,0:T(8,128)(2,1)S(1)}, u32[]{:S(2)}, u32[]{:S(2)}) collective-permute-start(bf16[144,128]{1,0:T(8,128)(2,1)S(1)} %get-tuple-element.55), channel_id=1, source_target_pairs={{0,16},{1,17},{2,18},{3,19},{4,20},{5,21},{6,22},{7,23},{8,24},{9,... | collective-permute-start | bytes 110600 | tf_op jit(solution)/shard_map/ppermute | solution.py:381
  70.3 4.9 %collective-permute-start.19 = (bf16[144,128]{1,0:T(8,128)(2,1)S(1)}, bf16[144,128]{1,0:T(8,128)(2,1)S(1)}, u32[]{:S(2)}, u32[]{:S(2)}) collective-permute-start(bf16[144,128]{1,0:T(8,128)(2,1)S(1)} %get-tuple-element.56), channel_id=1, source_target_pairs={{0,17},{1,16},{2,19},{3,18},{4,21},{5,20},{6,23},{7,22},{8,25},{9,... | collective-permute-start | bytes 110600 | tf_op jit(solution)/shard_map/ppermute | solution.py:381
  75.2 5.8 %collective-permute-start.23 = (bf16[144,128]{1,0:T(8,128)(2,1)S(1)}, bf16[144,128]{1,0:T(8,128)(2,1)S(1)}, u32[]{:S(2)}, u32[]{:S(2)}) collective-permute-start(bf16[144,128]{1,0:T(8,128)(2,1)S(1)} %sum_chips.1.after_ref.refs_0_), channel_id=1, source_target_pairs={{0,6},{1,7},{2,4},{3,5},{4,2},{5,3},{6,0},{7,1},{8,14},{9,15},{10,... | collective-permute-start | bytes 110600 | tf_op jit(solution)/shard_map/ppermute | solution.py:363
  76.6 5.2 %collective-permute-start.22 = (bf16[144,128]{1,0:T(8,128)(2,1)S(1)}, bf16[144,128]{1,0:T(8,128)(2,1)S(1)}, u32[]{:S(2)}, u32[]{:S(2)}) collective-permute-start(bf16[144,128]{1,0:T(8,128)(2,1)S(1)} %sum_chips.1.after_ref.refs_0_), channel_id=1, source_target_pairs={{0,4},{1,5},{2,6},{3,7},{4,0},{5,1},{6,2},{7,3},{8,12},{9,13},{10,... | collective-permute-start | bytes 110600 | tf_op jit(solution)/shard_map/ppermute | solution.py:363
  76.6 5.3 %collective-permute-start.21 = (bf16[144,128]{1,0:T(8,128)(2,1)S(1)}, bf16[144,128]{1,0:T(8,128)(2,1)S(1)}, u32[]{:S(2)}, u32[]{:S(2)}) collective-permute-start(bf16[144,128]{1,0:T(8,128)(2,1)S(1)} %sum_chips.1.after_ref.refs_0_), channel_id=1, source_target_pairs={{0,2},{1,3},{2,0},{3,1},{4,6},{5,7},{6,4},{7,5},{8,10},{9,11},{10,... | collective-permute-start | bytes 110600 | tf_op jit(solution)/shard_map/ppermute | solution.py:363
  79.6 8.9 %collective-permute-start.20 = (bf16[2,256,128]{2,1,0:T(8,128)(2,1)S(1)}, bf16[2,256,128]{2,1,0:T(8,128)(2,1)S(1)}, u32[]{:S(2)}, u32[]{:S(2)}) collective-permute-start(bf16[2,256,128]{2,1,0:T(8,128)(2,1)S(1)} %hold.2), channel_id=1, source_target_pairs={{0,1},{1,0},{2,3},{3,2},{4,5},{5,4},{6,7},{7,6},{8,9},{9,8},{10,11... | collective-permute-start | bytes 393224 | tf_op jit(solution)/shard_map/ppermute | solution.py:363
  82.0 6.5 %collective-permute-start.24 = (bf16[2,256,128]{2,1,0:T(8,128)(2,1)S(1)}, bf16[2,256,128]{2,1,0:T(8,128)(2,1)S(1)}, u32[]{:S(2)}, u32[]{:S(2)}) collective-permute-start(bf16[2,256,128]{2,1,0:T(8,128)(2,1)S(1)} %hold.3), channel_id=1, source_target_pairs={{1,2},{3,4},{5,6},{2,1},{4,3},{6,5},{9,10},{11,12},{13,14},{10,9},... | collective-permute-start | bytes 393224 | tf_op jit(solution)/shard_map/ppermute | solution.py:533
  82.7 8.1 %collective-permute-start.27 = (bf16[144,128]{1,0:T(8,128)(2,1)S(1)}, bf16[144,128]{1,0:T(8,128)(2,1)S(1)}, u32[]{:S(2)}, u32[]{:S(2)}) collective-permute-start(bf16[144,128]{1,0:T(8,128)(2,1)S(1)} %sum_planes.1.after_ref.refs_0_), channel_id=1, source_target_pairs={{0,17},{1,16},{2,19},{3,18},{4,21},{5,20},{6,23},{7,22},{8,25},{9,... | collective-permute-start | bytes 110600 | tf_op jit(solution)/shard_map/ppermute | solution.py:381
  86.6 4.2 %collective-permute-start.26 = (bf16[144,128]{1,0:T(8,128)(2,1)S(1)}, bf16[144,128]{1,0:T(8,128)(2,1)S(1)}, u32[]{:S(2)}, u32[]{:S(2)}) collective-permute-start(bf16[144,128]{1,0:T(8,128)(2,1)S(1)} %sum_planes.1.after_ref.refs_0_), channel_id=1, source_target_pairs={{0,16},{1,17},{2,18},{3,19},{4,20},{5,21},{6,22},{7,23},{8,24},{9,... | collective-permute-start | bytes 110600 | tf_op jit(solution)/shard_map/ppermute | solution.py:381
  88.5 4.0 %collective-permute-start.25 = (bf16[144,128]{1,0:T(8,128)(2,1)S(1)}, bf16[144,128]{1,0:T(8,128)(2,1)S(1)}, u32[]{:S(2)}, u32[]{:S(2)}) collective-permute-start(bf16[144,128]{1,0:T(8,128)(2,1)S(1)} %sum_planes.1.after_ref.refs_0_), channel_id=1, source_target_pairs={{0,1},{1,0},{2,3},{3,2},{4,5},{5,4},{6,7},{7,6},{8,9},{9,8},{10,11... | collective-permute-start | bytes 110600 | tf_op jit(solution)/shard_map/ppermute | solution.py:381
  92.5 1.4 %collective-permute-start.28 = (bf16[576,128]{1,0:T(8,128)(2,1)S(1)}, bf16[576,128]{1,0:T(8,128)(2,1)S(1)}, u32[]{:S(2)}, u32[]{:S(2)}) collective-permute-start(bf16[576,128]{1,0:T(8,128)(2,1)S(1)} %join_chips.1.own_ref), channel_id=1, source_target_pairs={{0,8},{8,0},{16,24},{24,16},{1,9},{9,1},{17,25},{25,17},{2,10},{10... | collective-permute-start | bytes 442376 | tf_op jit(solution)/shard_map/ppermute | solution.py:385

commit v19 on v17

--- a/solution.py
+++ b/solution.py
@@ -283,8 +283,7 @@
     send_ref[...] = grads[rows_at(1 - core_ref[0], half), :]
 
 
-def decode_kernel(index_ref, image_ref, near_ref, far_ref, weight_ref, out_ref, done_ref, padded):
-    done_ref[...] = jnp.zeros(done_ref.shape, jnp.float32)
+def decode_kernel(index_ref, image_ref, near_ref, far_ref, weight_ref, out_ref, padded):
     regions, rows, columns, width = image_ref.shape
     padded[:RIM, :] = jnp.zeros((RIM, width), jnp.float32)
     padded[RIM + columns :, :] = jnp.zeros((RIM, width), jnp.float32)
@@ -345,8 +344,7 @@
     refs[-1][...] = (total * factor).astype(jnp.bfloat16)
 
 
-def join_kernel(quad_ref, done_ref, *refs):
-    del done_ref
+def join_kernel(quad_ref, *refs):
     for distance, ref in enumerate(refs[:-1]):
         rows = rows_at(lax.bitwise_xor(quad_ref[0], distance), ref.shape[0])
         refs[-1][rows, :] = ref[...]
@@ -511,7 +509,6 @@
         scratch=[pltpu.VMEM((half_rows, width), jnp.float32)],
         moved=quad_size * chunk_moved,
     )(quad, keep, trade_cores(send))
-    far = lax.ppermute(far, "seq", far_pairs)
     distances = range(1, quad_size)
     plane_sum = call(
         functools.partial(sum_kernel, 1.0),
@@ -521,16 +518,14 @@
         moved=chunk_moved,
     )(parts[0], *[trade_chips(parts[distance], distance, inner) for distance in distances])
     near = trade(hold(near, plane_sum), 1)
+    far = lax.ppermute(hold(far, plane_sum), "seq", far_pairs)
     plane_sums = [plane_sum] + [
         trade(plane_sum, distance) for distance in range(inner, seq_count, inner)
     ]
-    decoded, done = call(
+    decoded = call(
         decode_kernel,
         "decode",
-        [
-            jax.ShapeDtypeStruct(cotangent.shape, jnp.bfloat16),
-            jax.ShapeDtypeStruct((8, width), jnp.float32),
-        ],
+        jax.ShapeDtypeStruct(cotangent.shape, jnp.bfloat16),
         [SMEM()] + [VMEM()] * 4,
         scratch=[pltpu.VMEM((columns + 2 * RIM, width), jnp.float32)],
         flops=conv_flops,
@@ -547,9 +542,9 @@
         join_kernel,
         "join_chips",
         jax.ShapeDtypeStruct((half_rows, width), jnp.bfloat16),
-        [SMEM(), ANY()] + [VMEM()] * quad_size,
+        [SMEM()] + [VMEM()] * quad_size,
         moved=quad_size * chunk_moved,
-    )(quad, done, total, *[trade_chips(total, distance, inner) for distance in distances])
+    )(quad, total, *[trade_chips(total, distance, inner) for distance in distances])
     weight_grad = call(
         spread_kernel,
         "spread_sums",

time: 91.6 us -> 92.7 us (1.012)
    ppermute x6, waiting for transfers between devices: 5 us -> 8.49 us  [trade_chips(): return lax.ppermute(values, ('dp', 'seq'), pairs)]
    ppermute x19, waiting for transfers between devices: 21.7 us -> 20.1 us  [trade(): return lax.ppermute(values, 'seq', pairs)]
    ppermute x2, waiting for transfers between devices: 2.92 us -> 1.56 us  [trade_cores(): lax.ppermute(values, 'dp', [(i, i ^ 1) for i in range(lax.axis_size('dp'))])]
  transfers between devices with their start and end apart: 29 -> 29, of which waited for: 15 -> 16; matrix products, arithmetic and copies ran while one was open for 0% -> 0% of each run, Pallas kernels for 9% -> 8%
where the time goes in v19:
time: 92.7 us; the launch traced here: 92.4 us
  starting transfers between devices  46.4 us (50%)
  waiting for transfers between devices  30.2 us (33%)
  Pallas kernels  14.3 us (15%)
  between operations  0.94 us (1%)
    ppermute x19, starting transfers between devices, trade(): return lax.ppermute(values, 'seq', pairs)  37.9 us
    ppermute x19, waiting for transfers between devices, trade(): return lax.ppermute(values, 'seq', pairs)  20.1 us
    ppermute x6, waiting for transfers between devices, trade_chips(): return lax.ppermute(values, ('dp', 'seq'), pairs)  8.49 us
    ppermute x6, starting transfers between devices, trade_chips(): return lax.ppermute(values, ('dp', 'seq'), pairs)  7.11 us
    pallas_call x2, Pallas kernels, pack(): call(functools.partial(pack_kernel, distances, regions, per_device), name...  5.31 us
    pallas_call x1, Pallas kernels, body(): call(functools.partial(norm_kernel, back + [0]), 'norm_and_gradient', [ja...  3.07 us
    pallas_call x1, Pallas kernels, body(): call(decode_kernel, 'decode', jax.ShapeDtypeStruct(cotangent.shape, jnp.b...  2.22 us
    pallas_call x1, Pallas kernels, body(): call(functools.partial(attend_kernel, block_rows, group, order), 'attend'...  2.09 us
  transfers between devices with their start and end apart: 29, of which 16 were waited for; matrix products, arithmetic and copies ran while one was open for 0% of the time, Pallas kernels for 8%

profile of v19, /device:TPU:0, one launch (start us, length us, event | category | flops | bytes accessed | tf_op | source)
XLA Modules:
  0.0 92.4 jit_solution(2804964749478240353)
XLA Ops:
  0.6 0.0 copy-start
  0.7 0.0 copy-start.1
  0.7 0.0 copy-start.2
  0.7 2.6 %pack_early.1 = (bf16[3,4,64,128]{3,2,1,0:T(8,128)(2,1)}, bf16[3,4,64,128]{3,2,1,0:T(8,128)(2,1)}, bf16[3,4,64,128]{3,2,1,0:T(8,128)(2,1)}) custom-call(s32[1]{0:T(128)} %bitcast.index_ref, bf16[64,2,2048]{2,1,0:T(2,128)(2,1)} %query_ref.5, bf16[64,2,2048]{2,1,0:T(2,128)(2,1)} %key_ref.5, bf16[64,2,2048]{2,1,0:T(2,128)(2,1)} %value_ref.5), custom_call_target="tpu_custom_call" | custom-call | bytes 1179648 | tf_op jit(solution)/shard_map/pack_early/pallas_call | solution.py:416
  3.3 3.1 %collective-permute-start.3 = (bf16[3,4,64,128]{3,2,1,0:T(8,128)(2,1)}, bf16[3,4,64,128]{3,2,1,0:T(8,128)(2,1)S(1)}, u32[]{:S(2)}, u32[]{:S(2)}) collective-permute-start(bf16[3,4,64,128]{3,2,1,0:T(8,128)(2,1)} %get-tuple-element.32), channel_id=1, source_target_pairs={{0,2},{1,3},{2,0},{3,1},{4,6},{5,7},{6,4},{7,5},{8,10},{9,11},{10,... | collective-permute-start | bytes 589832 | tf_op jit(solution)/shard_map/ppermute | solution.py:361
  6.4 2.6 %collective-permute-start.5 = (bf16[3,4,64,128]{3,2,1,0:T(8,128)(2,1)}, bf16[3,4,64,128]{3,2,1,0:T(8,128)(2,1)S(1)}, u32[]{:S(2)}, u32[]{:S(2)}) collective-permute-start(bf16[3,4,64,128]{3,2,1,0:T(8,128)(2,1)} %get-tuple-element.34), channel_id=1, source_target_pairs={{0,4},{1,5},{2,6},{3,7},{4,0},{5,1},{6,2},{7,3},{8,12},{9,13},{10,... | collective-permute-start | bytes 589832 | tf_op jit(solution)/shard_map/ppermute | solution.py:361
  8.9 1.3 %collective-permute-start.6 = (bf16[3,4,64,128]{3,2,1,0:T(8,128)(2,1)}, bf16[3,4,64,128]{3,2,1,0:T(8,128)(2,1)S(1)}, u32[]{:S(2)}, u32[]{:S(2)}) collective-permute-start(bf16[3,4,64,128]{3,2,1,0:T(8,128)(2,1)} %get-tuple-element.35), channel_id=1, source_target_pairs={{0,5},{1,4},{2,7},{3,6},{4,1},{5,0},{6,3},{7,2},{8,13},{9,12},{10,... | collective-permute-start | bytes 589832 | tf_op jit(solution)/shard_map/ppermute | solution.py:361
  10.2 2.7 %pack_late.1 = (bf16[3,4,64,128]{3,2,1,0:T(8,128)(2,1)}, bf16[3,4,64,128]{3,2,1,0:T(8,128)(2,1)}, bf16[3,4,64,128]{3,2,1,0:T(8,128)(2,1)}, bf16[3,4,64,128]{3,2,1,0:T(8,128)(2,1)}) custom-call(s32[1]{0:T(128)} %bitcast.index_ref, bf16[64,2,2048]{2,1,0:T(2,128)(2,1)} %query_ref.5, bf16[64,2,2048]{2,1,0:T(2,128)(2,1)} %key_ref.5, bf16[64,2,2048]{2,1,0:T(2,128)(2,1)} %value_ref.5), custom_call_target="tpu_custom_call" | custom-call | bytes 1572864 | tf_op jit(solution)/shard_map/pack_late/pallas_call | solution.py:416
  13.0 0.0 copy-start.6
  13.0 0.6 collective-permute-start.2
  13.6 1.4 %collective-permute-start.4 = (bf16[3,4,64,128]{3,2,1,0:T(8,128)(2,1)}, bf16[3,4,64,128]{3,2,1,0:T(8,128)(2,1)S(1)}, u32[]{:S(2)}, u32[]{:S(2)}) collective-permute-start(bf16[3,4,64,128]{3,2,1,0:T(8,128)(2,1)} %get-tuple-element.33), channel_id=1, source_target_pairs={{0,3},{1,2},{2,1},{3,0},{4,7},{5,6},{6,5},{7,4},{8,11},{9,10},{10,... | collective-permute-start | bytes 589832 | tf_op jit(solution)/shard_map/ppermute | solution.py:361
  15.0 0.4 own_chunk.1
  15.4 0.1 collective-permute-done.3.refs_1_
  15.6 0.3 copy-done.8
  15.9 3.6 %collective-permute-start.7 = (bf16[3,4,64,128]{3,2,1,0:T(8,128)(2,1)S(1)}, bf16[3,4,64,128]{3,2,1,0:T(8,128)(2,1)S(1)}, u32[]{:S(2)}, u32[]{:S(2)}) collective-permute-start(bf16[3,4,64,128]{3,2,1,0:T(8,128)(2,1)S(1)} %copy-done.8), channel_id=1, source_target_pairs={{0,6},{1,7},{2,4},{3,5},{4,2},{5,3},{6,0},{7,1},{8,14},{9,15},{10,... | collective-permute-start | bytes 589832 | tf_op jit(solution)/shard_map/ppermute | solution.py:361
  19.5 3.9 %collective-permute-done.5.refs_3_ = bf16[3,4,64,128]{3,2,1,0:T(8,128)(2,1)S(1)} collective-permute-done((bf16[3,4,64,128]{3,2,1,0:T(8,128)(2,1)}, bf16[3,4,64,128]{3,2,1,0:T(8,128)(2,1)S(1)}, u32[]{:S(2)}, u32[]{:S(2)}) %collective-permute-start.5) | collective-permute-done | bytes 196640 | tf_op jit(solution)/shard_map/ppermute | solution.py:361
  23.4 3.7 %collective-permute-start.8 = (bf16[3,4,64,128]{3,2,1,0:T(8,128)(2,1)S(1)}, bf16[3,4,64,128]{3,2,1,0:T(8,128)(2,1)S(1)}, u32[]{:S(2)}, u32[]{:S(2)}) collective-permute-start(bf16[3,4,64,128]{3,2,1,0:T(8,128)(2,1)S(1)} %copy-done.7), channel_id=1, source_target_pairs={{0,7},{1,6},{2,5},{3,4},{4,3},{5,2},{6,1},{7,0},{8,15},{9,14},{10,... | collective-permute-start | bytes 589832 | tf_op jit(solution)/shard_map/ppermute | solution.py:361
  27.1 10.2 %collective-permute-done.6.refs_4_ = bf16[3,4,64,128]{3,2,1,0:T(8,128)(2,1)S(1)} collective-permute-done((bf16[3,4,64,128]{3,2,1,0:T(8,128)(2,1)}, bf16[3,4,64,128]{3,2,1,0:T(8,128)(2,1)S(1)}, u32[]{:S(2)}, u32[]{:S(2)}) %collective-permute-start.6) | collective-permute-done | bytes 196640 | tf_op jit(solution)/shard_map/ppermute | solution.py:361
  37.3 0.3 collective-permute-start
  37.6 0.0 collective-permute-done.2.refs_0_
  37.6 0.7 collective-permute-start.1
  38.2 0.1 fusion.2.lengths_ref
  38.3 0.0 collective-permute-done.4.refs_2_
  38.3 0.0 collective-permute-done.8.refs_6_
  38.3 2.1 %attend.1 = (bf16[4,64,128]{2,1,0:T(8,128)(2,1)S(1)}, bf16[4,64,128]{2,1,0:T(8,128)(2,1)S(1)}, bf16[4,64,128]{2,1,0:T(8,128)(2,1)S(1)}, bf16[4,64,128]{2,1,0:T(8...) custom-call(s32[1]{0:T(128)} %bitcast.index_ref, ...), custom_call_target="tpu_custom_call" | custom-call | flops 536870912 | bytes 2097152 | tf_op jit(solution)/shard_map/attend/pallas_call | solution.py:463
  40.4 0.0 copy-start.5
  40.5 9.0 %collective-permute-start.9 = (bf16[4,64,128]{2,1,0:T(8,128)(2,1)S(1)}, bf16[4,64,128]{2,1,0:T(8,128)(2,1)S(1)}, u32[]{:S(2)}, u32[]{:S(2)}) collective-permute-start(bf16[4,64,128]{2,1,0:T(8,128)(2,1)S(1)} %get-tuple-element.39), channel_id=1, source_target_pairs={{0,4},{1,5},{2,6},{3,7},{4,0},{5,1},{6,2},{7,3},{8,12},{9,13},{10,... | collective-permute-start | bytes 196616 | tf_op jit(solution)/shard_map/ppermute | solution.py:361
  49.5 0.0 collective-permute-start.10
  49.5 1.2 %collective-permute-start.11 = (bf16[4,64,128]{2,1,0:T(8,128)(2,1)S(1)}, bf16[4,64,128]{2,1,0:T(8,128)(2,1)S(1)}, u32[]{:S(2)}, u32[]{:S(2)}) collective-permute-start(bf16[4,64,128]{2,1,0:T(8,128)(2,1)S(1)} %get-tuple-element.41), channel_id=1, source_target_pairs={{0,6},{1,7},{2,4},{3,5},{4,2},{5,3},{6,0},{7,1},{8,14},{9,15},{10,... | collective-permute-start | bytes 196616 | tf_op jit(solution)/shard_map/ppermute | solution.py:361
  50.7 3.6 %collective-permute-start.12 = (bf16[4,64,128]{2,1,0:T(8,128)(2,1)S(1)}, bf16[4,64,128]{2,1,0:T(8,128)(2,1)S(1)}, u32[]{:S(2)}, u32[]{:S(2)}) collective-permute-start(bf16[4,64,128]{2,1,0:T(8,128)(2,1)S(1)} %get-tuple-element.42), channel_id=1, source_target_pairs={{0,7},{1,6},{2,5},{3,4},{4,3},{5,2},{6,1},{7,0},{8,15},{9,14},{10,... | collective-permute-start | bytes 196616 | tf_op jit(solution)/shard_map/ppermute | solution.py:361
  54.3 0.0 collective-permute-done.1.far_ref
  54.3 1.3 %collective-permute-done.9.refs_0_ = bf16[4,64,128]{2,1,0:T(8,128)(2,1)S(1)} collective-permute-done((bf16[4,64,128]{2,1,0:T(8,128)(2,1)S(1)}, bf16[4,64,128]{2,1,0:T(8,128)(2,1)S(1)}, u32[]{:S(2)}, u32[]{:S(2)}) %collective-permute-start.9) | collective-permute-done | bytes 65568 | tf_op jit(solution)/shard_map/ppermute | solution.py:361
  55.6 0.6 collective-permute-start.14
  56.2 1.5 %collective-permute-done.10.refs_1_ = bf16[4,64,128]{2,1,0:T(8,128)(2,1)S(1)} collective-permute-done((bf16[4,64,128]{2,1,0:T(8,128)(2,1)S(1)}, bf16[4,64,128]{2,1,0:T(8,128)(2,1)S(1)}, u32[]{:S(2)}, u32[]{:S(2)}) %collective-permute-start.10) | collective-permute-done | bytes 65568 | tf_op jit(solution)/shard_map/ppermute | solution.py:361
  57.7 1.6 %collective-permute-start.15 = (bf16[4,64,128]{2,1,0:T(8,128)(2,1)S(1)}, bf16[4,64,128]{2,1,0:T(8,128)(2,1)S(1)}, u32[]{:S(2)}, u32[]{:S(2)}) collective-permute-start(bf16[4,64,128]{2,1,0:T(8,128)(2,1)S(1)} %get-tuple-element.45), channel_id=1, source_target_pairs={{0,1},{1,0},{2,3},{3,2},{4,5},{5,4},{6,7},{7,6},{8,9},{9,8},{10,11... | collective-permute-start | bytes 196616 | tf_op jit(solution)/shard_map/ppermute | solution.py:361
  59.3 0.3 turn_cotangent.1.turned_ref
  59.5 0.0 collective-permute-done.11.refs_2_
  59.6 0.0 collective-permute-done.13.refs_4_
  59.6 1.2 %collective-permute-done.14.refs_5_ = bf16[4,64,128]{2,1,0:T(8,128)(2,1)S(1)} collective-permute-done((bf16[4,64,128]{2,1,0:T(8,128)(2,1)S(1)}, bf16[4,64,128]{2,1,0:T(8,128)(2,1)S(1)}, u32[]{:S(2)}, u32[]{:S(2)}) %collective-permute-start.14) | collective-permute-done | bytes 65568 | tf_op jit(solution)/shard_map/ppermute | solution.py:361
  60.8 1.2 %collective-permute-done.15.refs_6_ = bf16[4,64,128]{2,1,0:T(8,128)(2,1)S(1)} collective-permute-done((bf16[4,64,128]{2,1,0:T(8,128)(2,1)S(1)}, bf16[4,64,128]{2,1,0:T(8,128)(2,1)S(1)}, u32[]{:S(2)}, u32[]{:S(2)}) %collective-permute-start.15) | collective-permute-done | bytes 65568 | tf_op jit(solution)/shard_map/ppermute | solution.py:361
  62.0 3.1 %norm_and_gradient.1 = (bf16[2,4,256,128]{3,2,1,0:T(8,128)(2,1)S(1)}, bf16[2,256,128]{2,1,0:T(8,128)(2,1)S(1)}, bf16[2,256,128]{2,1,0:T(8,128)(2,1)S(1)}, f32[576,128]{1,0:T(8,128)S(1)}, f32[576,128]{1,0:T(8,128)S(1)}) custom-call(s32[2]{0:T(128)S(1)} %copy-done.6, s32[1]{0:T(128)} %bitcast.index_ref, s32[1]{0:T(128)} %bitcast.1.core_ref, ...), custom_call_target="tpu_custom_call" | custom-call | flops 603979776 | bytes 2097152 | tf_op jit(solution)/shard_map/norm_and_gradient/pallas_call | solution.py:487
  65.1 0.1 collective-permute-start.16
  65.1 1.6 %collective-permute-done.16.other_ref = f32[576,128]{1,0:T(8,128)S(1)} collective-permute-done((f32[576,128]{1,0:T(8,128)S(1)}, f32[576,128]{1,0:T(8,128)S(1)}, u32[]{:S(2)}, u32[]{:S(2)}) %collective-permute-start.16) | collective-permute-done | bytes 294944 | tf_op jit(solution)/shard_map/ppermute | solution.py:383
  66.8 1.6 %collective-permute-start.17 = (bf16[144,128]{1,0:T(8,128)(2,1)S(1)}, bf16[144,128]{1,0:T(8,128)(2,1)S(1)}, u32[]{:S(2)}, u32[]{:S(2)}) collective-permute-start(bf16[144,128]{1,0:T(8,128)(2,1)S(1)} %get-tuple-element.52), channel_id=1, source_target_pairs={{0,1},{1,0},{2,3},{3,2},{4,5},{5,4},{6,7},{7,6},{8,9},{9,8},{10,11... | collective-permute-start | bytes 110600 | tf_op jit(solution)/shard_map/ppermute | solution.py:379
  68.4 1.6 %collective-permute-start.18 = (bf16[144,128]{1,0:T(8,128)(2,1)S(1)}, bf16[144,128]{1,0:T(8,128)(2,1)S(1)}, u32[]{:S(2)}, u32[]{:S(2)}) collective-permute-start(bf16[144,128]{1,0:T(8,128)(2,1)S(1)} %get-tuple-element.53), channel_id=1, source_target_pairs={{0,16},{1,17},{2,18},{3,19},{4,20},{5,21},{6,22},{7,23},{8,24},{9,... | collective-permute-start | bytes 110600 | tf_op jit(solution)/shard_map/ppermute | solution.py:379
  70.0 0.3 collective-permute-start.19
  70.3 0.5 collective-permute-done.17.refs_1_
  70.8 1.5 %collective-permute-done.18.refs_2_ = bf16[144,128]{1,0:T(8,128)(2,1)S(1)} collective-permute-done((bf16[144,128]{1,0:T(8,128)(2,1)S(1)}, bf16[144,128]{1,0:T(8,128)(2,1)S(1)}, u32[]{:S(2)}, u32[]{:S(2)}) %collective-permute-start.18) | collective-permute-done | bytes 36896 | tf_op jit(solution)/shard_map/ppermute | solution.py:379
  72.3 2.5 %collective-permute-done.19.refs_3_ = bf16[144,128]{1,0:T(8,128)(2,1)S(1)} collective-permute-done((bf16[144,128]{1,0:T(8,128)(2,1)S(1)}, bf16[144,128]{1,0:T(8,128)(2,1)S(1)}, u32[]{:S(2)}, u32[]{:S(2)}) %collective-permute-start.19) | collective-permute-done | bytes 36896 | tf_op jit(solution)/shard_map/ppermute | solution.py:379
  74.9 1.7 %collective-permute-start.24 = (bf16[144,128]{1,0:T(8,128)(2,1)S(1)}, bf16[144,128]{1,0:T(8,128)(2,1)S(1)}, u32[]{:S(2)}, u32[]{:S(2)}) collective-permute-start(bf16[144,128]{1,0:T(8,128)(2,1)S(1)} %sum_chips.1.after_ref.refs_0_), channel_id=1, source_target_pairs={{0,6},{1,7},{2,4},{3,5},{4,2},{5,3},{6,0},{7,1},{8,14},{9,15},{10,... | collective-permute-start | bytes 110600 | tf_op jit(solution)/shard_map/ppermute | solution.py:361
  76.6 2.7 %collective-permute-start.22 = (bf16[144,128]{1,0:T(8,128)(2,1)S(1)}, bf16[144,128]{1,0:T(8,128)(2,1)S(1)}, u32[]{:S(2)}, u32[]{:S(2)}) collective-permute-start(bf16[144,128]{1,0:T(8,128)(2,1)S(1)} %sum_chips.1.after_ref.refs_0_), channel_id=1, source_target_pairs={{0,2},{1,3},{2,0},{3,1},{4,6},{5,7},{6,4},{7,5},{8,10},{9,11},{10,... | collective-permute-start | bytes 110600 | tf_op jit(solution)/shard_map/ppermute | solution.py:361
  79.4 0.9 collective-permute-start.20
  80.3 0.7 collective-permute-start.21
  80.9 0.7 collective-permute-done.23.refs_2_
  81.6 0.1 collective-permute-done.22.refs_1_
  81.7 1.6 %collective-permute-start.27 = (bf16[144,128]{1,0:T(8,128)(2,1)S(1)}, bf16[144,128]{1,0:T(8,128)(2,1)S(1)}, u32[]{:S(2)}, u32[]{:S(2)}) collective-permute-start(bf16[144,128]{1,0:T(8,128)(2,1)S(1)} %sum_planes.1.refs_0_), channel_id=1, source_target_pairs={{0,17},{1,16},{2,19},{3,18},{4,21},{5,20},{6,23},{7,22},{8,25},{9,... | collective-permute-start | bytes 110600 | tf_op jit(solution)/shard_map/ppermute | solution.py:379
  83.3 1.9 %collective-permute-start.26 = (bf16[144,128]{1,0:T(8,128)(2,1)S(1)}, bf16[144,128]{1,0:T(8,128)(2,1)S(1)}, u32[]{:S(2)}, u32[]{:S(2)}) collective-permute-start(bf16[144,128]{1,0:T(8,128)(2,1)S(1)} %sum_planes.1.refs_0_), channel_id=1, source_target_pairs={{0,16},{1,17},{2,18},{3,19},{4,20},{5,21},{6,22},{7,23},{8,24},{9,... | collective-permute-start | bytes 110600 | tf_op jit(solution)/shard_map/ppermute | solution.py:379
  85.2 0.0 collective-permute-start.25
  85.2 1.4 %collective-permute-done.27.refs_3_ = bf16[144,128]{1,0:T(8,128)(2,1)S(1)} collective-permute-done((bf16[144,128]{1,0:T(8,128)(2,1)S(1)}, bf16[144,128]{1,0:T(8,128)(2,1)S(1)}, u32[]{:S(2)}, u32[]{:S(2)}) %collective-permute-start.27) | collective-permute-done | bytes 36896 | tf_op jit(solution)/shard_map/ppermute | solution.py:379
  86.6 0.7 collective-permute-done.26.refs_2_
  87.3 1.9 %collective-permute-done.25.refs_1_ = bf16[144,128]{1,0:T(8,128)(2,1)S(1)} collective-permute-done((bf16[144,128]{1,0:T(8,128)(2,1)S(1)}, bf16[144,128]{1,0:T(8,128)(2,1)S(1)}, u32[]{:S(2)}, u32[]{:S(2)}) %collective-permute-start.25) | collective-permute-done | bytes 36896 | tf_op jit(solution)/shard_map/ppermute | solution.py:379
  89.2 0.1 collective-permute-start.28
  89.3 2.2 %decode.1 = bf16[2,4,256,128]{3,2,1,0:T(8,128)(2,1)} custom-call(s32[1]{0:T(128)} %bitcast.index_ref, bf16[2,4,256,128]{3,2,1,0:T(8,128)(2,1)S(1)} %get-tuple-element.47.image_ref, bf16[2,256,128]{2,1,0:T(8,128)(2,1)S(1)} %collective-permute-done.20.near_ref, bf16[2,256,128]{2,1,0:T(8,128)(2,1)S(1)} %collective-permute-done.21.far_ref, ...), custom_call_target="tpu_custom_call" | custom-call | flops 603979776 | bytes 1048576 | tf_op jit(solution)/shard_map/decode/pallas_call | solution.py:525
  91.5 0.9 spread_sums.1
  (29 shorter events, 0.2 us)
Async XLA Ops:
  0.6 14.3 %copy-start.3 = (bf16[2,4,256,128]{3,2,1,0:T(8,128)(2,1)S(1)}, bf16[2,4,256,128]{3,2,1,0:T(8,128)(2,1)}, u32[]{:S(2)}) copy-start(bf16[2,4,256,128]{3,2,1,0:T(8,128)(2,1)} %cot_ref.1) | copy-start | bytes 1572868
  0.6 14.3 %copy-start = (bf16[64,2,2048]{2,1,0:T(2,128)(2,1)S(1)}, bf16[64,2,2048]{2,1,0:T(2,128)(2,1)}, u32[]{:S(2)}) copy-start(bf16[64,2,2048]{2,1,0:T(2,128)(2,1)} %query_ref.5) | copy-start | bytes 1572868
  0.7 14.3 %copy-start.1 = (bf16[64,2,2048]{2,1,0:T(2,128)(2,1)S(1)}, bf16[64,2,2048]{2,1,0:T(2,128)(2,1)}, u32[]{:S(2)}) copy-start(bf16[64,2,2048]{2,1,0:T(2,128)(2,1)} %key_ref.5) | copy-start | bytes 1572868
  0.7 14.3 %copy-start.2 = (bf16[64,2,2048]{2,1,0:T(2,128)(2,1)S(1)}, bf16[64,2,2048]{2,1,0:T(2,128)(2,1)}, u32[]{:S(2)}) copy-start(bf16[64,2,2048]{2,1,0:T(2,128)(2,1)} %value_ref.5) | copy-start | bytes 1572868
  3.3 12.3 %collective-permute-start.3 = (bf16[3,4,64,128]{3,2,1,0:T(8,128)(2,1)}, bf16[3,4,64,128]{3,2,1,0:T(8,128)(2,1)S(1)}, u32[]{:S(2)}, u32[]{:S(2)}) collective-permute-start(bf16[3,4,64,128]{3,2,1,0:T(8,128)(2,1)} %get-tuple-element.32), channel_id=1, source_target_pairs={{0,2},{1,3},{2,0},{3,1},{4,6},{5,7},{6,4},{7,5},{8,10},{9,11},{10,... | collective-permute-start | bytes 589832 | tf_op jit(solution)/shard_map/ppermute | solution.py:361
  6.4 17.1 %collective-permute-start.5 = (bf16[3,4,64,128]{3,2,1,0:T(8,128)(2,1)}, bf16[3,4,64,128]{3,2,1,0:T(8,128)(2,1)S(1)}, u32[]{:S(2)}, u32[]{:S(2)}) collective-permute-start(bf16[3,4,64,128]{3,2,1,0:T(8,128)(2,1)} %get-tuple-element.34), channel_id=1, source_target_pairs={{0,4},{1,5},{2,6},{3,7},{4,0},{5,1},{6,2},{7,3},{8,12},{9,13},{10,... | collective-permute-start | bytes 589832 | tf_op jit(solution)/shard_map/ppermute | solution.py:361
  8.9 28.3 %collective-permute-start.6 = (bf16[3,4,64,128]{3,2,1,0:T(8,128)(2,1)}, bf16[3,4,64,128]{3,2,1,0:T(8,128)(2,1)S(1)}, u32[]{:S(2)}, u32[]{:S(2)}) collective-permute-start(bf16[3,4,64,128]{3,2,1,0:T(8,128)(2,1)} %get-tuple-element.35), channel_id=1, source_target_pairs={{0,5},{1,4},{2,7},{3,6},{4,1},{5,0},{6,3},{7,2},{8,13},{9,12},{10,... | collective-permute-start | bytes 589832 | tf_op jit(solution)/shard_map/ppermute | solution.py:361
  13.0 10.5 %copy-start.7 = (bf16[3,4,64,128]{3,2,1,0:T(8,128)(2,1)S(1)}, bf16[3,4,64,128]{3,2,1,0:T(8,128)(2,1)}, u32[]{:S(2)}) copy-start(bf16[3,4,64,128]{3,2,1,0:T(8,128)(2,1)} %get-tuple-element.37) | copy-start | bytes 589828
  13.0 25.3 %copy-start.6 = (s32[2]{0:T(128)S(1)}, s32[2]{0:T(128)}, u32[]{:S(2)}) copy-start(s32[2]{0:T(128)} %lengths_ref.1) | copy-start | bytes 28
  13.0 24.6 %collective-permute-start.2 = (bf16[3,4,64,128]{3,2,1,0:T(8,128)(2,1)}, bf16[3,4,64,128]{3,2,1,0:T(8,128)(2,1)S(1)}, u32[]{:S(2)}, u32[]{:S(2)}) collective-permute-start(bf16[3,4,64,128]{3,2,1,0:T(8,128)(2,1)} %get-tuple-element.31), channel_id=1, source_target_pairs={{0,1},{1,0},{2,3},{3,2},{4,5},{5,4},{6,7},{7,6},{8,9},{9,8},{10,11... | collective-permute-start | bytes 589832 | tf_op jit(solution)/shard_map/ppermute | solution.py:361
  13.6 24.8 %collective-permute-start.4 = (bf16[3,4,64,128]{3,2,1,0:T(8,128)(2,1)}, bf16[3,4,64,128]{3,2,1,0:T(8,128)(2,1)S(1)}, u32[]{:S(2)}, u32[]{:S(2)}) collective-permute-start(bf16[3,4,64,128]{3,2,1,0:T(8,128)(2,1)} %get-tuple-element.33), channel_id=1, source_target_pairs={{0,3},{1,2},{2,1},{3,0},{4,7},{5,6},{6,5},{7,4},{8,11},{9,10},{10,... | collective-permute-start | bytes 589832 | tf_op jit(solution)/shard_map/ppermute | solution.py:361
  15.0 0.9 %copy-start.8 = (bf16[3,4,64,128]{3,2,1,0:T(8,128)(2,1)S(1)}, bf16[3,4,64,128]{3,2,1,0:T(8,128)(2,1)}, u32[]{:S(2)}) copy-start(bf16[3,4,64,128]{3,2,1,0:T(8,128)(2,1)} %get-tuple-element.36) | copy-start | bytes 589828
  15.9 22.4 %collective-permute-start.7 = (bf16[3,4,64,128]{3,2,1,0:T(8,128)(2,1)S(1)}, bf16[3,4,64,128]{3,2,1,0:T(8,128)(2,1)S(1)}, u32[]{:S(2)}, u32[]{:S(2)}) collective-permute-start(bf16[3,4,64,128]{3,2,1,0:T(8,128)(2,1)S(1)} %copy-done.8), channel_id=1, source_target_pairs={{0,6},{1,7},{2,4},{3,5},{4,2},{5,3},{6,0},{7,1},{8,14},{9,15},{10,... | collective-permute-start | bytes 589832 | tf_op jit(solution)/shard_map/ppermute | solution.py:361
  23.4 14.9 %collective-permute-start.8 = (bf16[3,4,64,128]{3,2,1,0:T(8,128)(2,1)S(1)}, bf16[3,4,64,128]{3,2,1,0:T(8,128)(2,1)S(1)}, u32[]{:S(2)}, u32[]{:S(2)}) collective-permute-start(bf16[3,4,64,128]{3,2,1,0:T(8,128)(2,1)S(1)} %copy-done.7), channel_id=1, source_target_pairs={{0,7},{1,6},{2,5},{3,4},{4,3},{5,2},{6,1},{7,0},{8,15},{9,14},{10,... | collective-permute-start | bytes 589832 | tf_op jit(solution)/shard_map/ppermute | solution.py:361
  37.3 13.4 %collective-permute-start = (bf16[2,256,128]{2,1,0:T(8,128)(2,1)S(1)}, bf16[2,256,128]{2,1,0:T(8,128)(2,1)S(1)}, u32[]{:S(2)}, u32[]{:S(2)}) collective-permute-start(bf16[2,256,128]{2,1,0:T(8,128)(2,1)S(1)} %get-tuple-element.29), channel_id=1, source_target_pairs={{0,1},{1,0},{2,3},{3,2},{4,5},{5,4},{6,7},{7,6},{8,9},{9,8},{10,11... | collective-permute-start | bytes 393224 | tf_op jit(solution)/shard_map/ppermute | solution.py:361
  37.6 16.7 %collective-permute-start.1 = (bf16[2,256,128]{2,1,0:T(8,128)(2,1)S(1)}, bf16[2,256,128]{2,1,0:T(8,128)(2,1)S(1)}, u32[]{:S(2)}, u32[]{:S(2)}) collective-permute-start(bf16[2,256,128]{2,1,0:T(8,128)(2,1)S(1)} %get-tuple-element.30), channel_id=1, source_target_pairs={{1,2},{3,4},{5,6},{2,1},{4,3},{6,5},{9,10},{11,12},{13,14},{10,9},... | collective-permute-start | bytes 393224 | tf_op jit(solution)/shard_map/ppermute | solution.py:450
  40.4 21.5 %copy-start.5 = (f32[2048]{0:T(1024)S(1)}, f32[2048]{0:T(1024)}, u32[]{:S(2)}) copy-start(f32[2048]{0:T(1024)} %param.11) | copy-start | bytes 24580
  40.5 15.1 %collective-permute-start.9 = (bf16[4,64,128]{2,1,0:T(8,128)(2,1)S(1)}, bf16[4,64,128]{2,1,0:T(8,128)(2,1)S(1)}, u32[]{:S(2)}, u32[]{:S(2)}) collective-permute-start(bf16[4,64,128]{2,1,0:T(8,128)(2,1)S(1)} %get-tuple-element.39), channel_id=1, source_target_pairs={{0,4},{1,5},{2,6},{3,7},{4,0},{5,1},{6,2},{7,3},{8,12},{9,13},{10,... | collective-permute-start | bytes 196616 | tf_op jit(solution)/shard_map/ppermute | solution.py:361
  49.5 8.2 %collective-permute-start.10 = (bf16[4,64,128]{2,1,0:T(8,128)(2,1)S(1)}, bf16[4,64,128]{2,1,0:T(8,128)(2,1)S(1)}, u32[]{:S(2)}, u32[]{:S(2)}) collective-permute-start(bf16[4,64,128]{2,1,0:T(8,128)(2,1)S(1)} %get-tuple-element.40), channel_id=1, source_target_pairs={{0,5},{1,4},{2,7},{3,6},{4,1},{5,0},{6,3},{7,2},{8,13},{9,12},{10,... | collective-permute-start | bytes 196616 | tf_op jit(solution)/shard_map/ppermute | solution.py:361
  49.5 10.1 %collective-permute-start.11 = (bf16[4,64,128]{2,1,0:T(8,128)(2,1)S(1)}, bf16[4,64,128]{2,1,0:T(8,128)(2,1)S(1)}, u32[]{:S(2)}, u32[]{:S(2)}) collective-permute-start(bf16[4,64,128]{2,1,0:T(8,128)(2,1)S(1)} %get-tuple-element.41), channel_id=1, source_target_pairs={{0,6},{1,7},{2,4},{3,5},{4,2},{5,3},{6,0},{7,1},{8,14},{9,15},{10,... | collective-permute-start | bytes 196616 | tf_op jit(solution)/shard_map/ppermute | solution.py:361
  50.7 8.9 %collective-permute-start.12 = (bf16[4,64,128]{2,1,0:T(8,128)(2,1)S(1)}, bf16[4,64,128]{2,1,0:T(8,128)(2,1)S(1)}, u32[]{:S(2)}, u32[]{:S(2)}) collective-permute-start(bf16[4,64,128]{2,1,0:T(8,128)(2,1)S(1)} %get-tuple-element.42), channel_id=1, source_target_pairs={{0,7},{1,6},{2,5},{3,4},{4,3},{5,2},{6,1},{7,0},{8,15},{9,14},{10,... | collective-permute-start | bytes 196616 | tf_op jit(solution)/shard_map/ppermute | solution.py:361
  54.3 5.3 %collective-permute-start.13 = (bf16[4,64,128]{2,1,0:T(8,128)(2,1)S(1)}, bf16[4,64,128]{2,1,0:T(8,128)(2,1)S(1)}, u32[]{:S(2)}, u32[]{:S(2)}) collective-permute-start(bf16[4,64,128]{2,1,0:T(8,128)(2,1)S(1)} %get-tuple-element.43), channel_id=1, source_target_pairs={{0,2},{1,3},{2,0},{3,1},{4,6},{5,7},{6,4},{7,5},{8,10},{9,11},{10,... | collective-permute-start | bytes 196616 | tf_op jit(solution)/shard_map/ppermute | solution.py:361
  55.6 5.2 %collective-permute-start.14 = (bf16[4,64,128]{2,1,0:T(8,128)(2,1)S(1)}, bf16[4,64,128]{2,1,0:T(8,128)(2,1)S(1)}, u32[]{:S(2)}, u32[]{:S(2)}) collective-permute-start(bf16[4,64,128]{2,1,0:T(8,128)(2,1)S(1)} %get-tuple-element.44), channel_id=1, source_target_pairs={{0,3},{1,2},{2,1},{3,0},{4,7},{5,6},{6,5},{7,4},{8,11},{9,10},{10,... | collective-permute-start | bytes 196616 | tf_op jit(solution)/shard_map/ppermute | solution.py:361
  57.7 4.3 %collective-permute-start.15 = (bf16[4,64,128]{2,1,0:T(8,128)(2,1)S(1)}, bf16[4,64,128]{2,1,0:T(8,128)(2,1)S(1)}, u32[]{:S(2)}, u32[]{:S(2)}) collective-permute-start(bf16[4,64,128]{2,1,0:T(8,128)(2,1)S(1)} %get-tuple-element.45), channel_id=1, source_target_pairs={{0,1},{1,0},{2,3},{3,2},{4,5},{5,4},{6,7},{7,6},{8,9},{9,8},{10,11... | collective-permute-start | bytes 196616 | tf_op jit(solution)/shard_map/ppermute | solution.py:361
  62.0 27.3 %copy-start.4 = (bf16[9,128,128]{2,1,0:T(8,128)(2,1)S(1)}, bf16[9,128,128]{2,1,0:T(8,128)(2,1)}, u32[]{:S(2)}) copy-start(bf16[9,128,128]{2,1,0:T(8,128)(2,1)} %param.12) | copy-start | bytes 884740
  65.1 1.6 %collective-permute-start.16 = (f32[576,128]{1,0:T(8,128)S(1)}, f32[576,128]{1,0:T(8,128)S(1)}, u32[]{:S(2)}, u32[]{:S(2)}) collective-permute-start(f32[576,128]{1,0:T(8,128)S(1)} %get-tuple-element.50), channel_id=1, source_target_pairs={{0,8},{8,0},{16,24},{24,16},{1,9},{9,1},{17,25},{25,17},{2,10},{10... | collective-permute-start | bytes 884744 | tf_op jit(solution)/shard_map/ppermute | solution.py:383
  66.8 4.0 %collective-permute-start.17 = (bf16[144,128]{1,0:T(8,128)(2,1)S(1)}, bf16[144,128]{1,0:T(8,128)(2,1)S(1)}, u32[]{:S(2)}, u32[]{:S(2)}) collective-permute-start(bf16[144,128]{1,0:T(8,128)(2,1)S(1)} %get-tuple-element.52), channel_id=1, source_target_pairs={{0,1},{1,0},{2,3},{3,2},{4,5},{5,4},{6,7},{7,6},{8,9},{9,8},{10,11... | collective-permute-start | bytes 110600 | tf_op jit(solution)/shard_map/ppermute | solution.py:379
  68.4 4.0 %collective-permute-start.18 = (bf16[144,128]{1,0:T(8,128)(2,1)S(1)}, bf16[144,128]{1,0:T(8,128)(2,1)S(1)}, u32[]{:S(2)}, u32[]{:S(2)}) collective-permute-start(bf16[144,128]{1,0:T(8,128)(2,1)S(1)} %get-tuple-element.53), channel_id=1, source_target_pairs={{0,16},{1,17},{2,18},{3,19},{4,20},{5,21},{6,22},{7,23},{8,24},{9,... | collective-permute-start | bytes 110600 | tf_op jit(solution)/shard_map/ppermute | solution.py:379
  70.0 4.9 %collective-permute-start.19 = (bf16[144,128]{1,0:T(8,128)(2,1)S(1)}, bf16[144,128]{1,0:T(8,128)(2,1)S(1)}, u32[]{:S(2)}, u32[]{:S(2)}) collective-permute-start(bf16[144,128]{1,0:T(8,128)(2,1)S(1)} %get-tuple-element.54), channel_id=1, source_target_pairs={{0,17},{1,16},{2,19},{3,18},{4,21},{5,20},{6,23},{7,22},{8,25},{9,... | collective-permute-start | bytes 110600 | tf_op jit(solution)/shard_map/ppermute | solution.py:379
  74.9 6.1 %collective-permute-start.24 = (bf16[144,128]{1,0:T(8,128)(2,1)S(1)}, bf16[144,128]{1,0:T(8,128)(2,1)S(1)}, u32[]{:S(2)}, u32[]{:S(2)}) collective-permute-start(bf16[144,128]{1,0:T(8,128)(2,1)S(1)} %sum_chips.1.after_ref.refs_0_), channel_id=1, source_target_pairs={{0,6},{1,7},{2,4},{3,5},{4,2},{5,3},{6,0},{7,1},{8,14},{9,15},{10,... | collective-permute-start | bytes 110600 | tf_op jit(solution)/shard_map/ppermute | solution.py:361
  76.6 5.0 %collective-permute-start.23 = (bf16[144,128]{1,0:T(8,128)(2,1)S(1)}, bf16[144,128]{1,0:T(8,128)(2,1)S(1)}, u32[]{:S(2)}, u32[]{:S(2)}) collective-permute-start(bf16[144,128]{1,0:T(8,128)(2,1)S(1)} %sum_chips.1.after_ref.refs_0_), channel_id=1, source_target_pairs={{0,4},{1,5},{2,6},{3,7},{4,0},{5,1},{6,2},{7,3},{8,12},{9,13},{10,... | collective-permute-start | bytes 110600 | tf_op jit(solution)/shard_map/ppermute | solution.py:361
  76.6 5.1 %collective-permute-start.22 = (bf16[144,128]{1,0:T(8,128)(2,1)S(1)}, bf16[144,128]{1,0:T(8,128)(2,1)S(1)}, u32[]{:S(2)}, u32[]{:S(2)}) collective-permute-start(bf16[144,128]{1,0:T(8,128)(2,1)S(1)} %sum_chips.1.after_ref.refs_0_), channel_id=1, source_target_pairs={{0,2},{1,3},{2,0},{3,1},{4,6},{5,7},{6,4},{7,5},{8,10},{9,11},{10,... | collective-permute-start | bytes 110600 | tf_op jit(solution)/shard_map/ppermute | solution.py:361
  79.4 9.9 %collective-permute-start.20 = (bf16[2,256,128]{2,1,0:T(8,128)(2,1)S(1)}, bf16[2,256,128]{2,1,0:T(8,128)(2,1)S(1)}, u32[]{:S(2)}, u32[]{:S(2)}) collective-permute-start(bf16[2,256,128]{2,1,0:T(8,128)(2,1)S(1)} %hold.2), channel_id=1, source_target_pairs={{0,1},{1,0},{2,3},{3,2},{4,5},{5,4},{6,7},{7,6},{8,9},{9,8},{10,11... | collective-permute-start | bytes 393224 | tf_op jit(solution)/shard_map/ppermute | solution.py:361
  80.3 9.0 %collective-permute-start.21 = (bf16[2,256,128]{2,1,0:T(8,128)(2,1)S(1)}, bf16[2,256,128]{2,1,0:T(8,128)(2,1)S(1)}, u32[]{:S(2)}, u32[]{:S(2)}) collective-permute-start(bf16[2,256,128]{2,1,0:T(8,128)(2,1)S(1)} %hold.3), channel_id=1, source_target_pairs={{1,2},{3,4},{5,6},{2,1},{4,3},{6,5},{9,10},{11,12},{13,14},{10,9},... | collective-permute-start | bytes 393224 | tf_op jit(solution)/shard_map/ppermute | solution.py:521
  81.7 4.9 %collective-permute-start.27 = (bf16[144,128]{1,0:T(8,128)(2,1)S(1)}, bf16[144,128]{1,0:T(8,128)(2,1)S(1)}, u32[]{:S(2)}, u32[]{:S(2)}) collective-permute-start(bf16[144,128]{1,0:T(8,128)(2,1)S(1)} %sum_planes.1.refs_0_), channel_id=1, source_target_pairs={{0,17},{1,16},{2,19},{3,18},{4,21},{5,20},{6,23},{7,22},{8,25},{9,... | collective-permute-start | bytes 110600 | tf_op jit(solution)/shard_map/ppermute | solution.py:379
  83.3 4.0 %collective-permute-start.26 = (bf16[144,128]{1,0:T(8,128)(2,1)S(1)}, bf16[144,128]{1,0:T(8,128)(2,1)S(1)}, u32[]{:S(2)}, u32[]{:S(2)}) collective-permute-start(bf16[144,128]{1,0:T(8,128)(2,1)S(1)} %sum_planes.1.refs_0_), channel_id=1, source_target_pairs={{0,16},{1,17},{2,18},{3,19},{4,20},{5,21},{6,22},{7,23},{8,24},{9,... | collective-permute-start | bytes 110600 | tf_op jit(solution)/shard_map/ppermute | solution.py:379
  85.2 4.0 %collective-permute-start.25 = (bf16[144,128]{1,0:T(8,128)(2,1)S(1)}, bf16[144,128]{1,0:T(8,128)(2,1)S(1)}, u32[]{:S(2)}, u32[]{:S(2)}) collective-permute-start(bf16[144,128]{1,0:T(8,128)(2,1)S(1)} %sum_planes.1.refs_0_), channel_id=1, source_target_pairs={{0,1},{1,0},{2,3},{3,2},{4,5},{5,4},{6,7},{7,6},{8,9},{9,8},{10,11... | collective-permute-start | bytes 110600 | tf_op jit(solution)/shard_map/ppermute | solution.py:379
  89.2 2.3 %collective-permute-start.28 = (bf16[576,128]{1,0:T(8,128)(2,1)S(1)}, bf16[576,128]{1,0:T(8,128)(2,1)S(1)}, u32[]{:S(2)}, u32[]{:S(2)}) collective-permute-start(bf16[576,128]{1,0:T(8,128)(2,1)S(1)} %join_chips.1.own_ref), channel_id=1, source_target_pairs={{0,8},{8,0},{16,24},{24,16},{1,9},{9,1},{17,25},{25,17},{2,10},{10... | collective-permute-start | bytes 442376 | tf_op jit(solution)/shard_map/ppermute | solution.py:383

commit v20 on v19

--- a/solution.py
+++ b/solution.py
@@ -509,6 +509,7 @@
         scratch=[pltpu.VMEM((half_rows, width), jnp.float32)],
         moved=quad_size * chunk_moved,
     )(quad, keep, trade_cores(send))
+    far = lax.ppermute(far, "seq", far_pairs)
     distances = range(1, quad_size)
     plane_sum = call(
         functools.partial(sum_kernel, 1.0),
@@ -518,7 +519,6 @@
         moved=chunk_moved,
     )(parts[0], *[trade_chips(parts[distance], distance, inner) for distance in distances])
     near = trade(hold(near, plane_sum), 1)
-    far = lax.ppermute(hold(far, plane_sum), "seq", far_pairs)
     plane_sums = [plane_sum] + [
         trade(plane_sum, distance) for distance in range(inner, seq_count, inner)
     ]

time: 92.7 us -> 91.9 us (level)
  waiting for transfers between devices: 30.2 us -> 27.5 us
  starting transfers between devices: 46.4 us -> 48.3 us
    ppermute x6, waiting for transfers between devices: 8.49 us -> 6.57 us  [trade_chips(): return lax.ppermute(values, ('dp', 'seq'), pairs)]
    ppermute x19, starting transfers between devices: 37.9 us -> 39.7 us  [trade(): return lax.ppermute(values, 'seq', pairs)]
  transfers between devices with their start and end apart: 29 -> 29, of which waited for: 16 -> 13; matrix products, arithmetic and copies ran while one was open for 0% -> 0% of each run, Pallas kernels for 8% -> 8%
where the time goes in v20:
time: 91.9 us; the launch traced here: 91.6 us
  starting transfers between devices  48.3 us (53%)
  waiting for transfers between devices  27.5 us (30%)
  Pallas kernels  14.3 us (16%)
  between operations  0.94 us (1%)
    ppermute x19, starting transfers between devices, trade(): return lax.ppermute(values, 'seq', pairs)  39.7 us
    ppermute x19, waiting for transfers between devices, trade(): return lax.ppermute(values, 'seq', pairs)  19.4 us
    ppermute x6, starting transfers between devices, trade_chips(): return lax.ppermute(values, ('dp', 'seq'), pairs)  7.1 us
    ppermute x6, waiting for transfers between devices, trade_chips(): return lax.ppermute(values, ('dp', 'seq'), pairs)  6.57 us
    pallas_call x2, Pallas kernels, pack(): call(functools.partial(pack_kernel, distances, regions, per_device), name...  5.31 us
    pallas_call x1, Pallas kernels, body(): call(functools.partial(norm_kernel, back + [0]), 'norm_and_gradient', [ja...  3.07 us
    pallas_call x1, Pallas kernels, body(): call(decode_kernel, 'decode', jax.ShapeDtypeStruct(cotangent.shape, jnp.b...  2.22 us
    pallas_call x1, Pallas kernels, body(): call(functools.partial(attend_kernel, block_rows, group, order), 'attend'...  2.09 us
  transfers between devices with their start and end apart: 29, of which 13 were waited for; matrix products, arithmetic and copies ran while one was open for 0% of the time, Pallas kernels for 8%

profile of v20, /device:TPU:0, one launch (start us, length us, event | category | flops | bytes accessed | tf_op | source)
XLA Modules:
  0.0 91.6 jit_solution(15992604942396064275)
XLA Ops:
  0.6 0.0 copy-start
  0.7 0.0 copy-start.1
  0.7 0.0 copy-start.2
  0.7 2.6 %pack_early.1 = (bf16[3,4,64,128]{3,2,1,0:T(8,128)(2,1)}, bf16[3,4,64,128]{3,2,1,0:T(8,128)(2,1)}, bf16[3,4,64,128]{3,2,1,0:T(8,128)(2,1)}) custom-call(s32[1]{0:T(128)} %bitcast.index_ref, bf16[64,2,2048]{2,1,0:T(2,128)(2,1)} %query_ref.5, bf16[64,2,2048]{2,1,0:T(2,128)(2,1)} %key_ref.5, bf16[64,2,2048]{2,1,0:T(2,128)(2,1)} %value_ref.5), custom_call_target="tpu_custom_call" | custom-call | bytes 1179648 | tf_op jit(solution)/shard_map/pack_early/pallas_call | solution.py:416
  3.3 3.1 %collective-permute-start.3 = (bf16[3,4,64,128]{3,2,1,0:T(8,128)(2,1)}, bf16[3,4,64,128]{3,2,1,0:T(8,128)(2,1)S(1)}, u32[]{:S(2)}, u32[]{:S(2)}) collective-permute-start(bf16[3,4,64,128]{3,2,1,0:T(8,128)(2,1)} %get-tuple-element.32), channel_id=1, source_target_pairs={{0,2},{1,3},{2,0},{3,1},{4,6},{5,7},{6,4},{7,5},{8,10},{9,11},{10,... | collective-permute-start | bytes 589832 | tf_op jit(solution)/shard_map/ppermute | solution.py:361
  6.4 2.6 %collective-permute-start.5 = (bf16[3,4,64,128]{3,2,1,0:T(8,128)(2,1)}, bf16[3,4,64,128]{3,2,1,0:T(8,128)(2,1)S(1)}, u32[]{:S(2)}, u32[]{:S(2)}) collective-permute-start(bf16[3,4,64,128]{3,2,1,0:T(8,128)(2,1)} %get-tuple-element.34), channel_id=1, source_target_pairs={{0,4},{1,5},{2,6},{3,7},{4,0},{5,1},{6,2},{7,3},{8,12},{9,13},{10,... | collective-permute-start | bytes 589832 | tf_op jit(solution)/shard_map/ppermute | solution.py:361
  8.9 1.3 %collective-permute-start.6 = (bf16[3,4,64,128]{3,2,1,0:T(8,128)(2,1)}, bf16[3,4,64,128]{3,2,1,0:T(8,128)(2,1)S(1)}, u32[]{:S(2)}, u32[]{:S(2)}) collective-permute-start(bf16[3,4,64,128]{3,2,1,0:T(8,128)(2,1)} %get-tuple-element.35), channel_id=1, source_target_pairs={{0,5},{1,4},{2,7},{3,6},{4,1},{5,0},{6,3},{7,2},{8,13},{9,12},{10,... | collective-permute-start | bytes 589832 | tf_op jit(solution)/shard_map/ppermute | solution.py:361
  10.2 2.7 %pack_late.1 = (bf16[3,4,64,128]{3,2,1,0:T(8,128)(2,1)}, bf16[3,4,64,128]{3,2,1,0:T(8,128)(2,1)}, bf16[3,4,64,128]{3,2,1,0:T(8,128)(2,1)}, bf16[3,4,64,128]{3,2,1,0:T(8,128)(2,1)}) custom-call(s32[1]{0:T(128)} %bitcast.index_ref, bf16[64,2,2048]{2,1,0:T(2,128)(2,1)} %query_ref.5, bf16[64,2,2048]{2,1,0:T(2,128)(2,1)} %key_ref.5, bf16[64,2,2048]{2,1,0:T(2,128)(2,1)} %value_ref.5), custom_call_target="tpu_custom_call" | custom-call | bytes 1572864 | tf_op jit(solution)/shard_map/pack_late/pallas_call | solution.py:416
  13.0 0.0 copy-start.6
  13.0 0.6 collective-permute-start.2
  13.6 1.4 %collective-permute-start.4 = (bf16[3,4,64,128]{3,2,1,0:T(8,128)(2,1)}, bf16[3,4,64,128]{3,2,1,0:T(8,128)(2,1)S(1)}, u32[]{:S(2)}, u32[]{:S(2)}) collective-permute-start(bf16[3,4,64,128]{3,2,1,0:T(8,128)(2,1)} %get-tuple-element.33), channel_id=1, source_target_pairs={{0,3},{1,2},{2,1},{3,0},{4,7},{5,6},{6,5},{7,4},{8,11},{9,10},{10,... | collective-permute-start | bytes 589832 | tf_op jit(solution)/shard_map/ppermute | solution.py:361
  15.0 0.4 own_chunk.1
  15.4 0.1 collective-permute-done.3.refs_1_
  15.6 0.3 copy-done.8
  15.9 3.6 %collective-permute-start.7 = (bf16[3,4,64,128]{3,2,1,0:T(8,128)(2,1)S(1)}, bf16[3,4,64,128]{3,2,1,0:T(8,128)(2,1)S(1)}, u32[]{:S(2)}, u32[]{:S(2)}) collective-permute-start(bf16[3,4,64,128]{3,2,1,0:T(8,128)(2,1)S(1)} %copy-done.8), channel_id=1, source_target_pairs={{0,6},{1,7},{2,4},{3,5},{4,2},{5,3},{6,0},{7,1},{8,14},{9,15},{10,... | collective-permute-start | bytes 589832 | tf_op jit(solution)/shard_map/ppermute | solution.py:361
  19.5 3.9 %collective-permute-done.5.refs_3_ = bf16[3,4,64,128]{3,2,1,0:T(8,128)(2,1)S(1)} collective-permute-done((bf16[3,4,64,128]{3,2,1,0:T(8,128)(2,1)}, bf16[3,4,64,128]{3,2,1,0:T(8,128)(2,1)S(1)}, u32[]{:S(2)}, u32[]{:S(2)}) %collective-permute-start.5) | collective-permute-done | bytes 196640 | tf_op jit(solution)/shard_map/ppermute | solution.py:361
  23.4 3.7 %collective-permute-start.8 = (bf16[3,4,64,128]{3,2,1,0:T(8,128)(2,1)S(1)}, bf16[3,4,64,128]{3,2,1,0:T(8,128)(2,1)S(1)}, u32[]{:S(2)}, u32[]{:S(2)}) collective-permute-start(bf16[3,4,64,128]{3,2,1,0:T(8,128)(2,1)S(1)} %copy-done.7), channel_id=1, source_target_pairs={{0,7},{1,6},{2,5},{3,4},{4,3},{5,2},{6,1},{7,0},{8,15},{9,14},{10,... | collective-permute-start | bytes 589832 | tf_op jit(solution)/shard_map/ppermute | solution.py:361
  27.1 10.2 %collective-permute-done.6.refs_4_ = bf16[3,4,64,128]{3,2,1,0:T(8,128)(2,1)S(1)} collective-permute-done((bf16[3,4,64,128]{3,2,1,0:T(8,128)(2,1)}, bf16[3,4,64,128]{3,2,1,0:T(8,128)(2,1)S(1)}, u32[]{:S(2)}, u32[]{:S(2)}) %collective-permute-start.6) | collective-permute-done | bytes 196640 | tf_op jit(solution)/shard_map/ppermute | solution.py:361
  37.3 0.3 collective-permute-start
  37.6 0.0 collective-permute-done.2.refs_0_
  37.6 0.7 collective-permute-start.1
  38.2 0.1 fusion.2.lengths_ref
  38.3 0.0 collective-permute-done.4.refs_2_
  38.3 0.0 collective-permute-done.7.refs_5_
  38.3 0.0 collective-permute-done.8.refs_6_
  38.3 2.1 %attend.1 = (bf16[4,64,128]{2,1,0:T(8,128)(2,1)S(1)}, bf16[4,64,128]{2,1,0:T(8,128)(2,1)S(1)}, bf16[4,64,128]{2,1,0:T(8,128)(2,1)S(1)}, bf16[4,64,128]{2,1,0:T(8...) custom-call(s32[1]{0:T(128)} %bitcast.index_ref, ...), custom_call_target="tpu_custom_call" | custom-call | flops 536870912 | bytes 2097152 | tf_op jit(solution)/shard_map/attend/pallas_call | solution.py:463
  40.4 0.0 copy-start.5
  40.5 9.0 %collective-permute-start.9 = (bf16[4,64,128]{2,1,0:T(8,128)(2,1)S(1)}, bf16[4,64,128]{2,1,0:T(8,128)(2,1)S(1)}, u32[]{:S(2)}, u32[]{:S(2)}) collective-permute-start(bf16[4,64,128]{2,1,0:T(8,128)(2,1)S(1)} %get-tuple-element.39), channel_id=1, source_target_pairs={{0,4},{1,5},{2,6},{3,7},{4,0},{5,1},{6,2},{7,3},{8,12},{9,13},{10,... | collective-permute-start | bytes 196616 | tf_op jit(solution)/shard_map/ppermute | solution.py:361
  49.5 1.2 %collective-permute-start.11 = (bf16[4,64,128]{2,1,0:T(8,128)(2,1)S(1)}, bf16[4,64,128]{2,1,0:T(8,128)(2,1)S(1)}, u32[]{:S(2)}, u32[]{:S(2)}) collective-permute-start(bf16[4,64,128]{2,1,0:T(8,128)(2,1)S(1)} %get-tuple-element.41), channel_id=1, source_target_pairs={{0,6},{1,7},{2,4},{3,5},{4,2},{5,3},{6,0},{7,1},{8,14},{9,15},{10,... | collective-permute-start | bytes 196616 | tf_op jit(solution)/shard_map/ppermute | solution.py:361
  50.7 0.0 collective-permute-done.near_ref
  50.7 3.6 %collective-permute-start.12 = (bf16[4,64,128]{2,1,0:T(8,128)(2,1)S(1)}, bf16[4,64,128]{2,1,0:T(8,128)(2,1)S(1)}, u32[]{:S(2)}, u32[]{:S(2)}) collective-permute-start(bf16[4,64,128]{2,1,0:T(8,128)(2,1)S(1)} %get-tuple-element.42), channel_id=1, source_target_pairs={{0,7},{1,6},{2,5},{3,4},{4,3},{5,2},{6,1},{7,0},{8,15},{9,14},{10,... | collective-permute-start | bytes 196616 | tf_op jit(solution)/shard_map/ppermute | solution.py:361
  54.3 0.0 collective-permute-done.1.far_ref
  54.3 0.0 collective-permute-start.13
  54.3 1.3 %collective-permute-done.9.refs_0_ = bf16[4,64,128]{2,1,0:T(8,128)(2,1)S(1)} collective-permute-done((bf16[4,64,128]{2,1,0:T(8,128)(2,1)S(1)}, bf16[4,64,128]{2,1,0:T(8,128)(2,1)S(1)}, u32[]{:S(2)}, u32[]{:S(2)}) %collective-permute-start.9) | collective-permute-done | bytes 65568 | tf_op jit(solution)/shard_map/ppermute | solution.py:361
  55.6 0.6 collective-permute-start.14
  56.2 1.5 %collective-permute-done.10.refs_1_ = bf16[4,64,128]{2,1,0:T(8,128)(2,1)S(1)} collective-permute-done((bf16[4,64,128]{2,1,0:T(8,128)(2,1)S(1)}, bf16[4,64,128]{2,1,0:T(8,128)(2,1)S(1)}, u32[]{:S(2)}, u32[]{:S(2)}) %collective-permute-start.10) | collective-permute-done | bytes 65568 | tf_op jit(solution)/shard_map/ppermute | solution.py:361
  57.7 1.6 %collective-permute-start.15 = (bf16[4,64,128]{2,1,0:T(8,128)(2,1)S(1)}, bf16[4,64,128]{2,1,0:T(8,128)(2,1)S(1)}, u32[]{:S(2)}, u32[]{:S(2)}) collective-permute-start(bf16[4,64,128]{2,1,0:T(8,128)(2,1)S(1)} %get-tuple-element.45), channel_id=1, source_target_pairs={{0,1},{1,0},{2,3},{3,2},{4,5},{5,4},{6,7},{7,6},{8,9},{9,8},{10,11... | collective-permute-start | bytes 196616 | tf_op jit(solution)/shard_map/ppermute | solution.py:361
  59.3 0.3 turn_cotangent.1.turned_ref
  59.5 0.0 collective-permute-done.12.refs_3_
  59.6 0.0 collective-permute-done.13.refs_4_
  59.6 1.2 %collective-permute-done.14.refs_5_ = bf16[4,64,128]{2,1,0:T(8,128)(2,1)S(1)} collective-permute-done((bf16[4,64,128]{2,1,0:T(8,128)(2,1)S(1)}, bf16[4,64,128]{2,1,0:T(8,128)(2,1)S(1)}, u32[]{:S(2)}, u32[]{:S(2)}) %collective-permute-start.14) | collective-permute-done | bytes 65568 | tf_op jit(solution)/shard_map/ppermute | solution.py:361
  60.8 1.2 %collective-permute-done.15.refs_6_ = bf16[4,64,128]{2,1,0:T(8,128)(2,1)S(1)} collective-permute-done((bf16[4,64,128]{2,1,0:T(8,128)(2,1)S(1)}, bf16[4,64,128]{2,1,0:T(8,128)(2,1)S(1)}, u32[]{:S(2)}, u32[]{:S(2)}) %collective-permute-start.15) | collective-permute-done | bytes 65568 | tf_op jit(solution)/shard_map/ppermute | solution.py:361
  62.0 3.1 %norm_and_gradient.1 = (bf16[2,4,256,128]{3,2,1,0:T(8,128)(2,1)S(1)}, bf16[2,256,128]{2,1,0:T(8,128)(2,1)S(1)}, bf16[2,256,128]{2,1,0:T(8,128)(2,1)S(1)}, f32[576,128]{1,0:T(8,128)S(1)}, f32[576,128]{1,0:T(8,128)S(1)}) custom-call(s32[2]{0:T(128)S(1)} %copy-done.6, s32[1]{0:T(128)} %bitcast.index_ref, s32[1]{0:T(128)} %bitcast.1.core_ref, ...), custom_call_target="tpu_custom_call" | custom-call | flops 603979776 | bytes 2097152 | tf_op jit(solution)/shard_map/norm_and_gradient/pallas_call | solution.py:487
  65.1 0.1 collective-permute-start.16
  65.1 1.6 %collective-permute-done.16.other_ref = f32[576,128]{1,0:T(8,128)S(1)} collective-permute-done((f32[576,128]{1,0:T(8,128)S(1)}, f32[576,128]{1,0:T(8,128)S(1)}, u32[]{:S(2)}, u32[]{:S(2)}) %collective-permute-start.16) | collective-permute-done | bytes 294944 | tf_op jit(solution)/shard_map/ppermute | solution.py:383
  66.8 1.6 %collective-permute-start.17 = (bf16[144,128]{1,0:T(8,128)(2,1)S(1)}, bf16[144,128]{1,0:T(8,128)(2,1)S(1)}, u32[]{:S(2)}, u32[]{:S(2)}) collective-permute-start(bf16[144,128]{1,0:T(8,128)(2,1)S(1)} %get-tuple-element.52), channel_id=1, source_target_pairs={{0,1},{1,0},{2,3},{3,2},{4,5},{5,4},{6,7},{7,6},{8,9},{9,8},{10,11... | collective-permute-start | bytes 110600 | tf_op jit(solution)/shard_map/ppermute | solution.py:379
  68.4 1.7 %collective-permute-start.18 = (bf16[144,128]{1,0:T(8,128)(2,1)S(1)}, bf16[144,128]{1,0:T(8,128)(2,1)S(1)}, u32[]{:S(2)}, u32[]{:S(2)}) collective-permute-start(bf16[144,128]{1,0:T(8,128)(2,1)S(1)} %get-tuple-element.53), channel_id=1, source_target_pairs={{0,16},{1,17},{2,18},{3,19},{4,20},{5,21},{6,22},{7,23},{8,24},{9,... | collective-permute-start | bytes 110600 | tf_op jit(solution)/shard_map/ppermute | solution.py:379
  70.1 0.2 collective-permute-start.19
  70.3 0.5 collective-permute-done.17.refs_1_
  70.8 1.5 %collective-permute-done.18.refs_2_ = bf16[144,128]{1,0:T(8,128)(2,1)S(1)} collective-permute-done((bf16[144,128]{1,0:T(8,128)(2,1)S(1)}, bf16[144,128]{1,0:T(8,128)(2,1)S(1)}, u32[]{:S(2)}, u32[]{:S(2)}) %collective-permute-start.18) | collective-permute-done | bytes 36896 | tf_op jit(solution)/shard_map/ppermute | solution.py:379
  72.3 2.6 %collective-permute-done.19.refs_3_ = bf16[144,128]{1,0:T(8,128)(2,1)S(1)} collective-permute-done((bf16[144,128]{1,0:T(8,128)(2,1)S(1)}, bf16[144,128]{1,0:T(8,128)(2,1)S(1)}, u32[]{:S(2)}, u32[]{:S(2)}) %collective-permute-start.19) | collective-permute-done | bytes 36896 | tf_op jit(solution)/shard_map/ppermute | solution.py:379
  74.9 1.3 %collective-permute-start.24 = (bf16[144,128]{1,0:T(8,128)(2,1)S(1)}, bf16[144,128]{1,0:T(8,128)(2,1)S(1)}, u32[]{:S(2)}, u32[]{:S(2)}) collective-permute-start(bf16[144,128]{1,0:T(8,128)(2,1)S(1)} %sum_chips.1.after_ref.refs_0_), channel_id=1, source_target_pairs={{0,6},{1,7},{2,4},{3,5},{4,2},{5,3},{6,0},{7,1},{8,14},{9,15},{10,... | collective-permute-start | bytes 110600 | tf_op jit(solution)/shard_map/ppermute | solution.py:361
  76.3 0.0 collective-permute-start.23
  76.3 3.1 %collective-permute-start.22 = (bf16[144,128]{1,0:T(8,128)(2,1)S(1)}, bf16[144,128]{1,0:T(8,128)(2,1)S(1)}, u32[]{:S(2)}, u32[]{:S(2)}) collective-permute-start(bf16[144,128]{1,0:T(8,128)(2,1)S(1)} %sum_chips.1.after_ref.refs_0_), channel_id=1, source_target_pairs={{0,2},{1,3},{2,0},{3,1},{4,6},{5,7},{6,4},{7,5},{8,10},{9,11},{10,... | collective-permute-start | bytes 110600 | tf_op jit(solution)/shard_map/ppermute | solution.py:361
  79.4 0.7 collective-permute-start.21
  80.1 2.8 %collective-permute-start.20 = (bf16[2,256,128]{2,1,0:T(8,128)(2,1)S(1)}, bf16[2,256,128]{2,1,0:T(8,128)(2,1)S(1)}, u32[]{:S(2)}, u32[]{:S(2)}) collective-permute-start(bf16[2,256,128]{2,1,0:T(8,128)(2,1)S(1)} %hold.1), channel_id=1, source_target_pairs={{0,1},{1,0},{2,3},{3,2},{4,5},{5,4},{6,7},{7,6},{8,9},{9,8},{10,11... | collective-permute-start | bytes 393224 | tf_op jit(solution)/shard_map/ppermute | solution.py:361
  82.9 0.1 collective-permute-start.27
  83.0 1.5 %collective-permute-start.26 = (bf16[144,128]{1,0:T(8,128)(2,1)S(1)}, bf16[144,128]{1,0:T(8,128)(2,1)S(1)}, u32[]{:S(2)}, u32[]{:S(2)}) collective-permute-start(bf16[144,128]{1,0:T(8,128)(2,1)S(1)} %sum_planes.1.refs_0_), channel_id=1, source_target_pairs={{0,16},{1,17},{2,18},{3,19},{4,20},{5,21},{6,22},{7,23},{8,24},{9,... | collective-permute-start | bytes 110600 | tf_op jit(solution)/shard_map/ppermute | solution.py:379
  84.5 2.0 %collective-permute-start.25 = (bf16[144,128]{1,0:T(8,128)(2,1)S(1)}, bf16[144,128]{1,0:T(8,128)(2,1)S(1)}, u32[]{:S(2)}, u32[]{:S(2)}) collective-permute-start(bf16[144,128]{1,0:T(8,128)(2,1)S(1)} %sum_planes.1.refs_0_), channel_id=1, source_target_pairs={{0,1},{1,0},{2,3},{3,2},{4,5},{5,4},{6,7},{7,6},{8,9},{9,8},{10,11... | collective-permute-start | bytes 110600 | tf_op jit(solution)/shard_map/ppermute | solution.py:379
  86.5 1.4 %collective-permute-done.27.refs_3_ = bf16[144,128]{1,0:T(8,128)(2,1)S(1)} collective-permute-done((bf16[144,128]{1,0:T(8,128)(2,1)S(1)}, bf16[144,128]{1,0:T(8,128)(2,1)S(1)}, u32[]{:S(2)}, u32[]{:S(2)}) %collective-permute-start.27) | collective-permute-done | bytes 36896 | tf_op jit(solution)/shard_map/ppermute | solution.py:379
  87.8 0.6 collective-permute-done.25.refs_1_
  88.4 0.1 collective-permute-start.28
  88.5 2.2 %decode.1 = bf16[2,4,256,128]{3,2,1,0:T(8,128)(2,1)} custom-call(s32[1]{0:T(128)} %bitcast.index_ref, bf16[2,4,256,128]{3,2,1,0:T(8,128)(2,1)S(1)} %get-tuple-element.47.image_ref, bf16[2,256,128]{2,1,0:T(8,128)(2,1)S(1)} %collective-permute-done.20.near_ref, bf16[2,256,128]{2,1,0:T(8,128)(2,1)S(1)} %collective-permute-done.21.far_ref, ...), custom_call_target="tpu_custom_call" | custom-call | flops 603979776 | bytes 1048576 | tf_op jit(solution)/shard_map/decode/pallas_call | solution.py:525
  90.8 0.9 spread_sums.1
  (28 shorter events, 0.2 us)
Async XLA Ops:
  0.6 14.3 %copy-start.3 = (bf16[2,4,256,128]{3,2,1,0:T(8,128)(2,1)S(1)}, bf16[2,4,256,128]{3,2,1,0:T(8,128)(2,1)}, u32[]{:S(2)}) copy-start(bf16[2,4,256,128]{3,2,1,0:T(8,128)(2,1)} %cot_ref.1) | copy-start | bytes 1572868
  0.6 14.3 %copy-start = (bf16[64,2,2048]{2,1,0:T(2,128)(2,1)S(1)}, bf16[64,2,2048]{2,1,0:T(2,128)(2,1)}, u32[]{:S(2)}) copy-start(bf16[64,2,2048]{2,1,0:T(2,128)(2,1)} %query_ref.5) | copy-start | bytes 1572868
  0.7 14.3 %copy-start.1 = (bf16[64,2,2048]{2,1,0:T(2,128)(2,1)S(1)}, bf16[64,2,2048]{2,1,0:T(2,128)(2,1)}, u32[]{:S(2)}) copy-start(bf16[64,2,2048]{2,1,0:T(2,128)(2,1)} %key_ref.5) | copy-start | bytes 1572868
  0.7 14.3 %copy-start.2 = (bf16[64,2,2048]{2,1,0:T(2,128)(2,1)S(1)}, bf16[64,2,2048]{2,1,0:T(2,128)(2,1)}, u32[]{:S(2)}) copy-start(bf16[64,2,2048]{2,1,0:T(2,128)(2,1)} %value_ref.5) | copy-start | bytes 1572868
  3.3 12.3 %collective-permute-start.3 = (bf16[3,4,64,128]{3,2,1,0:T(8,128)(2,1)}, bf16[3,4,64,128]{3,2,1,0:T(8,128)(2,1)S(1)}, u32[]{:S(2)}, u32[]{:S(2)}) collective-permute-start(bf16[3,4,64,128]{3,2,1,0:T(8,128)(2,1)} %get-tuple-element.32), channel_id=1, source_target_pairs={{0,2},{1,3},{2,0},{3,1},{4,6},{5,7},{6,4},{7,5},{8,10},{9,11},{10,... | collective-permute-start | bytes 589832 | tf_op jit(solution)/shard_map/ppermute | solution.py:361
  6.4 17.1 %collective-permute-start.5 = (bf16[3,4,64,128]{3,2,1,0:T(8,128)(2,1)}, bf16[3,4,64,128]{3,2,1,0:T(8,128)(2,1)S(1)}, u32[]{:S(2)}, u32[]{:S(2)}) collective-permute-start(bf16[3,4,64,128]{3,2,1,0:T(8,128)(2,1)} %get-tuple-element.34), channel_id=1, source_target_pairs={{0,4},{1,5},{2,6},{3,7},{4,0},{5,1},{6,2},{7,3},{8,12},{9,13},{10,... | collective-permute-start | bytes 589832 | tf_op jit(solution)/shard_map/ppermute | solution.py:361
  8.9 28.3 %collective-permute-start.6 = (bf16[3,4,64,128]{3,2,1,0:T(8,128)(2,1)}, bf16[3,4,64,128]{3,2,1,0:T(8,128)(2,1)S(1)}, u32[]{:S(2)}, u32[]{:S(2)}) collective-permute-start(bf16[3,4,64,128]{3,2,1,0:T(8,128)(2,1)} %get-tuple-element.35), channel_id=1, source_target_pairs={{0,5},{1,4},{2,7},{3,6},{4,1},{5,0},{6,3},{7,2},{8,13},{9,12},{10,... | collective-permute-start | bytes 589832 | tf_op jit(solution)/shard_map/ppermute | solution.py:361
  13.0 10.5 %copy-start.7 = (bf16[3,4,64,128]{3,2,1,0:T(8,128)(2,1)S(1)}, bf16[3,4,64,128]{3,2,1,0:T(8,128)(2,1)}, u32[]{:S(2)}) copy-start(bf16[3,4,64,128]{3,2,1,0:T(8,128)(2,1)} %get-tuple-element.37) | copy-start | bytes 589828
  13.0 25.3 %copy-start.6 = (s32[2]{0:T(128)S(1)}, s32[2]{0:T(128)}, u32[]{:S(2)}) copy-start(s32[2]{0:T(128)} %lengths_ref.1) | copy-start | bytes 28
  13.0 24.6 %collective-permute-start.2 = (bf16[3,4,64,128]{3,2,1,0:T(8,128)(2,1)}, bf16[3,4,64,128]{3,2,1,0:T(8,128)(2,1)S(1)}, u32[]{:S(2)}, u32[]{:S(2)}) collective-permute-start(bf16[3,4,64,128]{3,2,1,0:T(8,128)(2,1)} %get-tuple-element.31), channel_id=1, source_target_pairs={{0,1},{1,0},{2,3},{3,2},{4,5},{5,4},{6,7},{7,6},{8,9},{9,8},{10,11... | collective-permute-start | bytes 589832 | tf_op jit(solution)/shard_map/ppermute | solution.py:361
  13.6 24.8 %collective-permute-start.4 = (bf16[3,4,64,128]{3,2,1,0:T(8,128)(2,1)}, bf16[3,4,64,128]{3,2,1,0:T(8,128)(2,1)S(1)}, u32[]{:S(2)}, u32[]{:S(2)}) collective-permute-start(bf16[3,4,64,128]{3,2,1,0:T(8,128)(2,1)} %get-tuple-element.33), channel_id=1, source_target_pairs={{0,3},{1,2},{2,1},{3,0},{4,7},{5,6},{6,5},{7,4},{8,11},{9,10},{10,... | collective-permute-start | bytes 589832 | tf_op jit(solution)/shard_map/ppermute | solution.py:361
  15.0 0.9 %copy-start.8 = (bf16[3,4,64,128]{3,2,1,0:T(8,128)(2,1)S(1)}, bf16[3,4,64,128]{3,2,1,0:T(8,128)(2,1)}, u32[]{:S(2)}) copy-start(bf16[3,4,64,128]{3,2,1,0:T(8,128)(2,1)} %get-tuple-element.36) | copy-start | bytes 589828
  15.9 22.4 %collective-permute-start.7 = (bf16[3,4,64,128]{3,2,1,0:T(8,128)(2,1)S(1)}, bf16[3,4,64,128]{3,2,1,0:T(8,128)(2,1)S(1)}, u32[]{:S(2)}, u32[]{:S(2)}) collective-permute-start(bf16[3,4,64,128]{3,2,1,0:T(8,128)(2,1)S(1)} %copy-done.8), channel_id=1, source_target_pairs={{0,6},{1,7},{2,4},{3,5},{4,2},{5,3},{6,0},{7,1},{8,14},{9,15},{10,... | collective-permute-start | bytes 589832 | tf_op jit(solution)/shard_map/ppermute | solution.py:361
  23.4 14.9 %collective-permute-start.8 = (bf16[3,4,64,128]{3,2,1,0:T(8,128)(2,1)S(1)}, bf16[3,4,64,128]{3,2,1,0:T(8,128)(2,1)S(1)}, u32[]{:S(2)}, u32[]{:S(2)}) collective-permute-start(bf16[3,4,64,128]{3,2,1,0:T(8,128)(2,1)S(1)} %copy-done.7), channel_id=1, source_target_pairs={{0,7},{1,6},{2,5},{3,4},{4,3},{5,2},{6,1},{7,0},{8,15},{9,14},{10,... | collective-permute-start | bytes 589832 | tf_op jit(solution)/shard_map/ppermute | solution.py:361
  37.3 13.4 %collective-permute-start = (bf16[2,256,128]{2,1,0:T(8,128)(2,1)S(1)}, bf16[2,256,128]{2,1,0:T(8,128)(2,1)S(1)}, u32[]{:S(2)}, u32[]{:S(2)}) collective-permute-start(bf16[2,256,128]{2,1,0:T(8,128)(2,1)S(1)} %get-tuple-element.29), channel_id=1, source_target_pairs={{0,1},{1,0},{2,3},{3,2},{4,5},{5,4},{6,7},{7,6},{8,9},{9,8},{10,11... | collective-permute-start | bytes 393224 | tf_op jit(solution)/shard_map/ppermute | solution.py:361
  37.6 16.7 %collective-permute-start.1 = (bf16[2,256,128]{2,1,0:T(8,128)(2,1)S(1)}, bf16[2,256,128]{2,1,0:T(8,128)(2,1)S(1)}, u32[]{:S(2)}, u32[]{:S(2)}) collective-permute-start(bf16[2,256,128]{2,1,0:T(8,128)(2,1)S(1)} %get-tuple-element.30), channel_id=1, source_target_pairs={{1,2},{3,4},{5,6},{2,1},{4,3},{6,5},{9,10},{11,12},{13,14},{10,9},... | collective-permute-start | bytes 393224 | tf_op jit(solution)/shard_map/ppermute | solution.py:450
  40.4 21.5 %copy-start.5 = (f32[2048]{0:T(1024)S(1)}, f32[2048]{0:T(1024)}, u32[]{:S(2)}) copy-start(f32[2048]{0:T(1024)} %param.11) | copy-start | bytes 24580
  40.5 15.1 %collective-permute-start.9 = (bf16[4,64,128]{2,1,0:T(8,128)(2,1)S(1)}, bf16[4,64,128]{2,1,0:T(8,128)(2,1)S(1)}, u32[]{:S(2)}, u32[]{:S(2)}) collective-permute-start(bf16[4,64,128]{2,1,0:T(8,128)(2,1)S(1)} %get-tuple-element.39), channel_id=1, source_target_pairs={{0,4},{1,5},{2,6},{3,7},{4,0},{5,1},{6,2},{7,3},{8,12},{9,13},{10,... | collective-permute-start | bytes 196616 | tf_op jit(solution)/shard_map/ppermute | solution.py:361
  49.5 8.2 %collective-permute-start.10 = (bf16[4,64,128]{2,1,0:T(8,128)(2,1)S(1)}, bf16[4,64,128]{2,1,0:T(8,128)(2,1)S(1)}, u32[]{:S(2)}, u32[]{:S(2)}) collective-permute-start(bf16[4,64,128]{2,1,0:T(8,128)(2,1)S(1)} %get-tuple-element.40), channel_id=1, source_target_pairs={{0,5},{1,4},{2,7},{3,6},{4,1},{5,0},{6,3},{7,2},{8,13},{9,12},{10,... | collective-permute-start | bytes 196616 | tf_op jit(solution)/shard_map/ppermute | solution.py:361
  49.5 10.1 %collective-permute-start.11 = (bf16[4,64,128]{2,1,0:T(8,128)(2,1)S(1)}, bf16[4,64,128]{2,1,0:T(8,128)(2,1)S(1)}, u32[]{:S(2)}, u32[]{:S(2)}) collective-permute-start(bf16[4,64,128]{2,1,0:T(8,128)(2,1)S(1)} %get-tuple-element.41), channel_id=1, source_target_pairs={{0,6},{1,7},{2,4},{3,5},{4,2},{5,3},{6,0},{7,1},{8,14},{9,15},{10,... | collective-permute-start | bytes 196616 | tf_op jit(solution)/shard_map/ppermute | solution.py:361
  50.7 8.9 %collective-permute-start.12 = (bf16[4,64,128]{2,1,0:T(8,128)(2,1)S(1)}, bf16[4,64,128]{2,1,0:T(8,128)(2,1)S(1)}, u32[]{:S(2)}, u32[]{:S(2)}) collective-permute-start(bf16[4,64,128]{2,1,0:T(8,128)(2,1)S(1)} %get-tuple-element.42), channel_id=1, source_target_pairs={{0,7},{1,6},{2,5},{3,4},{4,3},{5,2},{6,1},{7,0},{8,15},{9,14},{10,... | collective-permute-start | bytes 196616 | tf_op jit(solution)/shard_map/ppermute | solution.py:361
  54.3 5.3 %collective-permute-start.13 = (bf16[4,64,128]{2,1,0:T(8,128)(2,1)S(1)}, bf16[4,64,128]{2,1,0:T(8,128)(2,1)S(1)}, u32[]{:S(2)}, u32[]{:S(2)}) collective-permute-start(bf16[4,64,128]{2,1,0:T(8,128)(2,1)S(1)} %get-tuple-element.43), channel_id=1, source_target_pairs={{0,2},{1,3},{2,0},{3,1},{4,6},{5,7},{6,4},{7,5},{8,10},{9,11},{10,... | collective-permute-start | bytes 196616 | tf_op jit(solution)/shard_map/ppermute | solution.py:361
  55.6 5.2 %collective-permute-start.14 = (bf16[4,64,128]{2,1,0:T(8,128)(2,1)S(1)}, bf16[4,64,128]{2,1,0:T(8,128)(2,1)S(1)}, u32[]{:S(2)}, u32[]{:S(2)}) collective-permute-start(bf16[4,64,128]{2,1,0:T(8,128)(2,1)S(1)} %get-tuple-element.44), channel_id=1, source_target_pairs={{0,3},{1,2},{2,1},{3,0},{4,7},{5,6},{6,5},{7,4},{8,11},{9,10},{10,... | collective-permute-start | bytes 196616 | tf_op jit(solution)/shard_map/ppermute | solution.py:361
  57.7 4.3 %collective-permute-start.15 = (bf16[4,64,128]{2,1,0:T(8,128)(2,1)S(1)}, bf16[4,64,128]{2,1,0:T(8,128)(2,1)S(1)}, u32[]{:S(2)}, u32[]{:S(2)}) collective-permute-start(bf16[4,64,128]{2,1,0:T(8,128)(2,1)S(1)} %get-tuple-element.45), channel_id=1, source_target_pairs={{0,1},{1,0},{2,3},{3,2},{4,5},{5,4},{6,7},{7,6},{8,9},{9,8},{10,11... | collective-permute-start | bytes 196616 | tf_op jit(solution)/shard_map/ppermute | solution.py:361
  62.0 26.6 %copy-start.4 = (bf16[9,128,128]{2,1,0:T(8,128)(2,1)S(1)}, bf16[9,128,128]{2,1,0:T(8,128)(2,1)}, u32[]{:S(2)}) copy-start(bf16[9,128,128]{2,1,0:T(8,128)(2,1)} %param.12) | copy-start | bytes 884740
  65.1 1.6 %collective-permute-start.16 = (f32[576,128]{1,0:T(8,128)S(1)}, f32[576,128]{1,0:T(8,128)S(1)}, u32[]{:S(2)}, u32[]{:S(2)}) collective-permute-start(f32[576,128]{1,0:T(8,128)S(1)} %get-tuple-element.50), channel_id=1, source_target_pairs={{0,8},{8,0},{16,24},{24,16},{1,9},{9,1},{17,25},{25,17},{2,10},{10... | collective-permute-start | bytes 884744 | tf_op jit(solution)/shard_map/ppermute | solution.py:383
  66.8 4.0 %collective-permute-start.17 = (bf16[144,128]{1,0:T(8,128)(2,1)S(1)}, bf16[144,128]{1,0:T(8,128)(2,1)S(1)}, u32[]{:S(2)}, u32[]{:S(2)}) collective-permute-start(bf16[144,128]{1,0:T(8,128)(2,1)S(1)} %get-tuple-element.52), channel_id=1, source_target_pairs={{0,1},{1,0},{2,3},{3,2},{4,5},{5,4},{6,7},{7,6},{8,9},{9,8},{10,11... | collective-permute-start | bytes 110600 | tf_op jit(solution)/shard_map/ppermute | solution.py:379
  68.4 4.0 %collective-permute-start.18 = (bf16[144,128]{1,0:T(8,128)(2,1)S(1)}, bf16[144,128]{1,0:T(8,128)(2,1)S(1)}, u32[]{:S(2)}, u32[]{:S(2)}) collective-permute-start(bf16[144,128]{1,0:T(8,128)(2,1)S(1)} %get-tuple-element.53), channel_id=1, source_target_pairs={{0,16},{1,17},{2,18},{3,19},{4,20},{5,21},{6,22},{7,23},{8,24},{9,... | collective-permute-start | bytes 110600 | tf_op jit(solution)/shard_map/ppermute | solution.py:379
  70.1 4.9 %collective-permute-start.19 = (bf16[144,128]{1,0:T(8,128)(2,1)S(1)}, bf16[144,128]{1,0:T(8,128)(2,1)S(1)}, u32[]{:S(2)}, u32[]{:S(2)}) collective-permute-start(bf16[144,128]{1,0:T(8,128)(2,1)S(1)} %get-tuple-element.54), channel_id=1, source_target_pairs={{0,17},{1,16},{2,19},{3,18},{4,21},{5,20},{6,23},{7,22},{8,25},{9,... | collective-permute-start | bytes 110600 | tf_op jit(solution)/shard_map/ppermute | solution.py:379
  74.9 7.9 %collective-permute-start.24 = (bf16[144,128]{1,0:T(8,128)(2,1)S(1)}, bf16[144,128]{1,0:T(8,128)(2,1)S(1)}, u32[]{:S(2)}, u32[]{:S(2)}) collective-permute-start(bf16[144,128]{1,0:T(8,128)(2,1)S(1)} %sum_chips.1.after_ref.refs_0_), channel_id=1, source_target_pairs={{0,6},{1,7},{2,4},{3,5},{4,2},{5,3},{6,0},{7,1},{8,14},{9,15},{10,... | collective-permute-start | bytes 110600 | tf_op jit(solution)/shard_map/ppermute | solution.py:361
  76.3 6.6 %collective-permute-start.23 = (bf16[144,128]{1,0:T(8,128)(2,1)S(1)}, bf16[144,128]{1,0:T(8,128)(2,1)S(1)}, u32[]{:S(2)}, u32[]{:S(2)}) collective-permute-start(bf16[144,128]{1,0:T(8,128)(2,1)S(1)} %sum_chips.1.after_ref.refs_0_), channel_id=1, source_target_pairs={{0,4},{1,5},{2,6},{3,7},{4,0},{5,1},{6,2},{7,3},{8,12},{9,13},{10,... | collective-permute-start | bytes 110600 | tf_op jit(solution)/shard_map/ppermute | solution.py:361
  76.3 6.6 %collective-permute-start.22 = (bf16[144,128]{1,0:T(8,128)(2,1)S(1)}, bf16[144,128]{1,0:T(8,128)(2,1)S(1)}, u32[]{:S(2)}, u32[]{:S(2)}) collective-permute-start(bf16[144,128]{1,0:T(8,128)(2,1)S(1)} %sum_chips.1.after_ref.refs_0_), channel_id=1, source_target_pairs={{0,2},{1,3},{2,0},{3,1},{4,6},{5,7},{6,4},{7,5},{8,10},{9,11},{10,... | collective-permute-start | bytes 110600 | tf_op jit(solution)/shard_map/ppermute | solution.py:361
  79.4 9.1 %collective-permute-start.21 = (bf16[2,256,128]{2,1,0:T(8,128)(2,1)S(1)}, bf16[2,256,128]{2,1,0:T(8,128)(2,1)S(1)}, u32[]{:S(2)}, u32[]{:S(2)}) collective-permute-start(bf16[2,256,128]{2,1,0:T(8,128)(2,1)S(1)} %get-tuple-element.55), channel_id=1, source_target_pairs={{1,2},{3,4},{5,6},{2,1},{4,3},{6,5},{9,10},{11,12},{13,14},{10,9},... | collective-permute-start | bytes 393224 | tf_op jit(solution)/shard_map/ppermute | solution.py:512
  80.1 8.4 %collective-permute-start.20 = (bf16[2,256,128]{2,1,0:T(8,128)(2,1)S(1)}, bf16[2,256,128]{2,1,0:T(8,128)(2,1)S(1)}, u32[]{:S(2)}, u32[]{:S(2)}) collective-permute-start(bf16[2,256,128]{2,1,0:T(8,128)(2,1)S(1)} %hold.1), channel_id=1, source_target_pairs={{0,1},{1,0},{2,3},{3,2},{4,5},{5,4},{6,7},{7,6},{8,9},{9,8},{10,11... | collective-permute-start | bytes 393224 | tf_op jit(solution)/shard_map/ppermute | solution.py:361
  82.9 4.9 %collective-permute-start.27 = (bf16[144,128]{1,0:T(8,128)(2,1)S(1)}, bf16[144,128]{1,0:T(8,128)(2,1)S(1)}, u32[]{:S(2)}, u32[]{:S(2)}) collective-permute-start(bf16[144,128]{1,0:T(8,128)(2,1)S(1)} %sum_planes.1.refs_0_), channel_id=1, source_target_pairs={{0,17},{1,16},{2,19},{3,18},{4,21},{5,20},{6,23},{7,22},{8,25},{9,... | collective-permute-start | bytes 110600 | tf_op jit(solution)/shard_map/ppermute | solution.py:379
  83.0 4.8 %collective-permute-start.26 = (bf16[144,128]{1,0:T(8,128)(2,1)S(1)}, bf16[144,128]{1,0:T(8,128)(2,1)S(1)}, u32[]{:S(2)}, u32[]{:S(2)}) collective-permute-start(bf16[144,128]{1,0:T(8,128)(2,1)S(1)} %sum_planes.1.refs_0_), channel_id=1, source_target_pairs={{0,16},{1,17},{2,18},{3,19},{4,20},{5,21},{6,22},{7,23},{8,24},{9,... | collective-permute-start | bytes 110600 | tf_op jit(solution)/shard_map/ppermute | solution.py:379
  84.5 4.0 %collective-permute-start.25 = (bf16[144,128]{1,0:T(8,128)(2,1)S(1)}, bf16[144,128]{1,0:T(8,128)(2,1)S(1)}, u32[]{:S(2)}, u32[]{:S(2)}) collective-permute-start(bf16[144,128]{1,0:T(8,128)(2,1)S(1)} %sum_planes.1.refs_0_), channel_id=1, source_target_pairs={{0,1},{1,0},{2,3},{3,2},{4,5},{5,4},{6,7},{7,6},{8,9},{9,8},{10,11... | collective-permute-start | bytes 110600 | tf_op jit(solution)/shard_map/ppermute | solution.py:379
  88.4 2.3 %collective-permute-start.28 = (bf16[576,128]{1,0:T(8,128)(2,1)S(1)}, bf16[576,128]{1,0:T(8,128)(2,1)S(1)}, u32[]{:S(2)}, u32[]{:S(2)}) collective-permute-start(bf16[576,128]{1,0:T(8,128)(2,1)S(1)} %join_chips.1.own_ref), channel_id=1, source_target_pairs={{0,8},{8,0},{16,24},{24,16},{1,9},{9,1},{17,25},{25,17},{2,10},{10... | collective-permute-start | bytes 442376 | tf_op jit(solution)/shard_map/ppermute | solution.py:383

commit v21 on v17

--- a/solution.py
+++ b/solution.py
@@ -352,10 +352,17 @@
         refs[-1][rows, :] = ref[...]
 
 
-def spread_kernel(core_ref, own_ref, other_ref, out_ref):
+def spread_kernel(core_ref, own_ref, other_ref, out_ref, wide, sems):
     half = own_ref.shape[0]
-    out_ref[rows_at(core_ref[0], half), :] = own_ref[...].astype(jnp.float32)
-    out_ref[rows_at(1 - core_ref[0], half), :] = other_ref[...].astype(jnp.float32)
+    stores = []
+    for number, (place, ref) in enumerate(((core_ref[0], own_ref), (1 - core_ref[0], other_ref))):
+        wide[number] = ref[...].astype(jnp.float32)
+        stores.append(
+            pltpu.make_async_copy(wide.at[number], out_ref.at[rows_at(place, half)], sems.at[number])
+        )
+        stores[-1].start()
+    for store in stores:
+        store.wait()
 
 
 def trade(values, distance):
@@ -555,6 +562,11 @@
         "spread_sums",
         jax.ShapeDtypeStruct((2 * half_rows, width), jnp.float32),
         [SMEM()] + [VMEM()] * 2,
+        out_specs=HBM(),
+        scratch=[
+            pltpu.VMEM((2, half_rows, width), jnp.float32),
+            pltpu.SemaphoreType.DMA((2,)),
+        ],
         moved=2 * quad_size * chunk_moved,
     )(core, joined, trade_cores(joined))
     return (decoded, weight_grad[: 9 * width].reshape(conv_weight.shape))

time: 91.6 us -> 91.6 us (level)
  transfers between devices with their start and end apart: 29 -> 29, of which waited for: 15 -> 16; matrix products, arithmetic and copies ran while one was open for 0% -> 0% of each run, Pallas kernels for 9% -> 9%
where the time goes in v21:
time: 91.6 us; the launch traced here: 91.4 us
  starting transfers between devices  45.5 us (50%)
  waiting for transfers between devices  29.8 us (33%)
  Pallas kernels  14.7 us (16%)
    ppermute x19, starting transfers between devices, trade(): return lax.ppermute(values, 'seq', pairs)  36.9 us
    ppermute x19, waiting for transfers between devices, trade(): return lax.ppermute(values, 'seq', pairs)  22.2 us
    ppermute x6, starting transfers between devices, trade_chips(): return lax.ppermute(values, ('dp', 'seq'), pairs)  7.11 us
    pallas_call x2, Pallas kernels, pack(): call(functools.partial(pack_kernel, distances, regions, per_device), name...  5.3 us
    ppermute x6, waiting for transfers between devices, trade_chips(): return lax.ppermute(values, ('dp', 'seq'), pairs)  4.64 us
    pallas_call x1, Pallas kernels, body(): call(functools.partial(norm_kernel, back + [0]), 'norm_and_gradient', [ja...  3.06 us
    ppermute x2, waiting for transfers between devices, trade_cores(): lax.ppermute(values, 'dp', [(i, i ^ 1) for i in range(lax.axis_size('dp'))])  2.92 us
    pallas_call x1, Pallas kernels, body(): call(functools.partial(attend_kernel, block_rows, group, order), 'attend'...  2.49 us
  transfers between devices with their start and end apart: 29, of which 16 were waited for; matrix products, arithmetic and copies ran while one was open for 0% of the time, Pallas kernels for 9%

profile of v21, /device:TPU:0, one launch (start us, length us, event | category | flops | bytes accessed | tf_op | source)
XLA Modules:
  0.0 91.4 jit_solution(8563523893651173832)
XLA Ops:
  0.6 0.0 copy-start
  0.7 0.0 copy-start.1
  0.7 0.0 copy-start.2
  0.7 2.6 %pack_early.1 = (bf16[3,4,64,128]{3,2,1,0:T(8,128)(2,1)}, bf16[3,4,64,128]{3,2,1,0:T(8,128)(2,1)}, bf16[3,4,64,128]{3,2,1,0:T(8,128)(2,1)}) custom-call(s32[1]{0:T(128)} %bitcast.index_ref, bf16[64,2,2048]{2,1,0:T(2,128)(2,1)} %query_ref.5, bf16[64,2,2048]{2,1,0:T(2,128)(2,1)} %key_ref.5, bf16[64,2,2048]{2,1,0:T(2,128)(2,1)} %value_ref.5), custom_call_target="tpu_custom_call" | custom-call | bytes 1179648 | tf_op jit(solution)/shard_map/pack_early/pallas_call | solution.py:425
  3.3 3.1 %collective-permute-start.3 = (bf16[3,4,64,128]{3,2,1,0:T(8,128)(2,1)}, bf16[3,4,64,128]{3,2,1,0:T(8,128)(2,1)S(1)}, u32[]{:S(2)}, u32[]{:S(2)}) collective-permute-start(bf16[3,4,64,128]{3,2,1,0:T(8,128)(2,1)} %get-tuple-element.34), channel_id=1, source_target_pairs={{0,2},{1,3},{2,0},{3,1},{4,6},{5,7},{6,4},{7,5},{8,10},{9,11},{10,... | collective-permute-start | bytes 589832 | tf_op jit(solution)/shard_map/ppermute | solution.py:370
  6.3 2.6 %collective-permute-start.5 = (bf16[3,4,64,128]{3,2,1,0:T(8,128)(2,1)}, bf16[3,4,64,128]{3,2,1,0:T(8,128)(2,1)S(1)}, u32[]{:S(2)}, u32[]{:S(2)}) collective-permute-start(bf16[3,4,64,128]{3,2,1,0:T(8,128)(2,1)} %get-tuple-element.36), channel_id=1, source_target_pairs={{0,4},{1,5},{2,6},{3,7},{4,0},{5,1},{6,2},{7,3},{8,12},{9,13},{10,... | collective-permute-start | bytes 589832 | tf_op jit(solution)/shard_map/ppermute | solution.py:370
  8.9 1.3 %collective-permute-start.6 = (bf16[3,4,64,128]{3,2,1,0:T(8,128)(2,1)}, bf16[3,4,64,128]{3,2,1,0:T(8,128)(2,1)S(1)}, u32[]{:S(2)}, u32[]{:S(2)}) collective-permute-start(bf16[3,4,64,128]{3,2,1,0:T(8,128)(2,1)} %get-tuple-element.37), channel_id=1, source_target_pairs={{0,5},{1,4},{2,7},{3,6},{4,1},{5,0},{6,3},{7,2},{8,13},{9,12},{10,... | collective-permute-start | bytes 589832 | tf_op jit(solution)/shard_map/ppermute | solution.py:370
  10.2 2.7 %pack_late.1 = (bf16[3,4,64,128]{3,2,1,0:T(8,128)(2,1)}, bf16[3,4,64,128]{3,2,1,0:T(8,128)(2,1)}, bf16[3,4,64,128]{3,2,1,0:T(8,128)(2,1)}, bf16[3,4,64,128]{3,2,1,0:T(8,128)(2,1)}) custom-call(s32[1]{0:T(128)} %bitcast.index_ref, bf16[64,2,2048]{2,1,0:T(2,128)(2,1)} %query_ref.5, bf16[64,2,2048]{2,1,0:T(2,128)(2,1)} %key_ref.5, bf16[64,2,2048]{2,1,0:T(2,128)(2,1)} %value_ref.5), custom_call_target="tpu_custom_call" | custom-call | bytes 1572864 | tf_op jit(solution)/shard_map/pack_late/pallas_call | solution.py:425
  13.0 0.0 copy-start.6
  13.0 0.6 collective-permute-start.2
  13.6 1.4 %collective-permute-start.4 = (bf16[3,4,64,128]{3,2,1,0:T(8,128)(2,1)}, bf16[3,4,64,128]{3,2,1,0:T(8,128)(2,1)S(1)}, u32[]{:S(2)}, u32[]{:S(2)}) collective-permute-start(bf16[3,4,64,128]{3,2,1,0:T(8,128)(2,1)} %get-tuple-element.35), channel_id=1, source_target_pairs={{0,3},{1,2},{2,1},{3,0},{4,7},{5,6},{6,5},{7,4},{8,11},{9,10},{10,... | collective-permute-start | bytes 589832 | tf_op jit(solution)/shard_map/ppermute | solution.py:370
  15.0 0.4 own_chunk.1
  15.4 0.1 collective-permute-done.3.refs_1_
  15.6 0.3 copy-done.8
  15.9 3.6 %collective-permute-start.7 = (bf16[3,4,64,128]{3,2,1,0:T(8,128)(2,1)S(1)}, bf16[3,4,64,128]{3,2,1,0:T(8,128)(2,1)S(1)}, u32[]{:S(2)}, u32[]{:S(2)}) collective-permute-start(bf16[3,4,64,128]{3,2,1,0:T(8,128)(2,1)S(1)} %copy-done.8), channel_id=1, source_target_pairs={{0,6},{1,7},{2,4},{3,5},{4,2},{5,3},{6,0},{7,1},{8,14},{9,15},{10,... | collective-permute-start | bytes 589832 | tf_op jit(solution)/shard_map/ppermute | solution.py:370
  19.5 3.9 %collective-permute-done.5.refs_3_ = bf16[3,4,64,128]{3,2,1,0:T(8,128)(2,1)S(1)} collective-permute-done((bf16[3,4,64,128]{3,2,1,0:T(8,128)(2,1)}, bf16[3,4,64,128]{3,2,1,0:T(8,128)(2,1)S(1)}, u32[]{:S(2)}, u32[]{:S(2)}) %collective-permute-start.5) | collective-permute-done | bytes 196640 | tf_op jit(solution)/shard_map/ppermute | solution.py:370
  23.4 3.7 %collective-permute-start.8 = (bf16[3,4,64,128]{3,2,1,0:T(8,128)(2,1)S(1)}, bf16[3,4,64,128]{3,2,1,0:T(8,128)(2,1)S(1)}, u32[]{:S(2)}, u32[]{:S(2)}) collective-permute-start(bf16[3,4,64,128]{3,2,1,0:T(8,128)(2,1)S(1)} %copy-done.7), channel_id=1, source_target_pairs={{0,7},{1,6},{2,5},{3,4},{4,3},{5,2},{6,1},{7,0},{8,15},{9,14},{10,... | collective-permute-start | bytes 589832 | tf_op jit(solution)/shard_map/ppermute | solution.py:370
  27.1 10.2 %collective-permute-done.6.refs_4_ = bf16[3,4,64,128]{3,2,1,0:T(8,128)(2,1)S(1)} collective-permute-done((bf16[3,4,64,128]{3,2,1,0:T(8,128)(2,1)}, bf16[3,4,64,128]{3,2,1,0:T(8,128)(2,1)S(1)}, u32[]{:S(2)}, u32[]{:S(2)}) %collective-permute-start.6) | collective-permute-done | bytes 196640 | tf_op jit(solution)/shard_map/ppermute | solution.py:370
  37.3 0.3 collective-permute-start
  37.6 0.7 collective-permute-start.1
  38.2 0.1 fusion.2.lengths_ref
  38.3 0.0 collective-permute-done.4.refs_2_
  38.3 0.0 collective-permute-done.7.refs_5_
  38.3 0.0 collective-permute-done.8.refs_6_
  38.3 2.5 %attend.1 = (bf16[4,64,128]{2,1,0:T(8,128)(2,1)S(1)}, bf16[4,64,128]{2,1,0:T(8,128)(2,1)S(1)}, bf16[4,64,128]{2,1,0:T(8,128)(2,1)S(1)}, bf16[4,64,128]{2,1,0:T(8...) custom-call(s32[1]{0:T(128)} %bitcast.index_ref, ...), custom_call_target="tpu_custom_call" | custom-call | flops 536870912 | bytes 2097152 | tf_op jit(solution)/shard_map/attend/pallas_call | solution.py:472
  40.8 0.0 copy-start.5
  40.8 9.0 %collective-permute-start.9 = (bf16[4,64,128]{2,1,0:T(8,128)(2,1)S(1)}, bf16[4,64,128]{2,1,0:T(8,128)(2,1)S(1)}, u32[]{:S(2)}, u32[]{:S(2)}) collective-permute-start(bf16[4,64,128]{2,1,0:T(8,128)(2,1)S(1)} %get-tuple-element.41), channel_id=1, source_target_pairs={{0,4},{1,5},{2,6},{3,7},{4,0},{5,1},{6,2},{7,3},{8,12},{9,13},{10,... | collective-permute-start | bytes 196616 | tf_op jit(solution)/shard_map/ppermute | solution.py:370
  49.9 1.2 %collective-permute-start.11 = (bf16[4,64,128]{2,1,0:T(8,128)(2,1)S(1)}, bf16[4,64,128]{2,1,0:T(8,128)(2,1)S(1)}, u32[]{:S(2)}, u32[]{:S(2)}) collective-permute-start(bf16[4,64,128]{2,1,0:T(8,128)(2,1)S(1)} %get-tuple-element.43), channel_id=1, source_target_pairs={{0,6},{1,7},{2,4},{3,5},{4,2},{5,3},{6,0},{7,1},{8,14},{9,15},{10,... | collective-permute-start | bytes 196616 | tf_op jit(solution)/shard_map/ppermute | solution.py:370
  51.1 3.6 %collective-permute-start.12 = (bf16[4,64,128]{2,1,0:T(8,128)(2,1)S(1)}, bf16[4,64,128]{2,1,0:T(8,128)(2,1)S(1)}, u32[]{:S(2)}, u32[]{:S(2)}) collective-permute-start(bf16[4,64,128]{2,1,0:T(8,128)(2,1)S(1)} %get-tuple-element.44), channel_id=1, source_target_pairs={{0,7},{1,6},{2,5},{3,4},{4,3},{5,2},{6,1},{7,0},{8,15},{9,14},{10,... | collective-permute-start | bytes 196616 | tf_op jit(solution)/shard_map/ppermute | solution.py:370
  54.7 0.0 collective-permute-start.13
  54.7 0.3 collective-permute-done.9.refs_0_
  55.0 1.6 %collective-permute-start.14 = (bf16[4,64,128]{2,1,0:T(8,128)(2,1)S(1)}, bf16[4,64,128]{2,1,0:T(8,128)(2,1)S(1)}, u32[]{:S(2)}, u32[]{:S(2)}) collective-permute-start(bf16[4,64,128]{2,1,0:T(8,128)(2,1)S(1)} %get-tuple-element.46), channel_id=1, source_target_pairs={{0,3},{1,2},{2,1},{3,0},{4,7},{5,6},{6,5},{7,4},{8,11},{9,10},{10,... | collective-permute-start | bytes 196616 | tf_op jit(solution)/shard_map/ppermute | solution.py:370
  56.6 1.5 %collective-permute-done.10.refs_1_ = bf16[4,64,128]{2,1,0:T(8,128)(2,1)S(1)} collective-permute-done((bf16[4,64,128]{2,1,0:T(8,128)(2,1)S(1)}, bf16[4,64,128]{2,1,0:T(8,128)(2,1)S(1)}, u32[]{:S(2)}, u32[]{:S(2)}) %collective-permute-start.10) | collective-permute-done | bytes 65568 | tf_op jit(solution)/shard_map/ppermute | solution.py:370
  58.1 0.1 collective-permute-start.15
  58.2 0.3 turn_cotangent.1.turned_ref
  58.4 0.0 collective-permute-done.11.refs_2_
  58.5 0.5 collective-permute-done.13.refs_4_
  58.9 1.2 %collective-permute-done.14.refs_5_ = bf16[4,64,128]{2,1,0:T(8,128)(2,1)S(1)} collective-permute-done((bf16[4,64,128]{2,1,0:T(8,128)(2,1)S(1)}, bf16[4,64,128]{2,1,0:T(8,128)(2,1)S(1)}, u32[]{:S(2)}, u32[]{:S(2)}) %collective-permute-start.14) | collective-permute-done | bytes 65568 | tf_op jit(solution)/shard_map/ppermute | solution.py:370
  60.1 2.2 %collective-permute-done.15.refs_6_ = bf16[4,64,128]{2,1,0:T(8,128)(2,1)S(1)} collective-permute-done((bf16[4,64,128]{2,1,0:T(8,128)(2,1)S(1)}, bf16[4,64,128]{2,1,0:T(8,128)(2,1)S(1)}, u32[]{:S(2)}, u32[]{:S(2)}) %collective-permute-start.15) | collective-permute-done | bytes 65568 | tf_op jit(solution)/shard_map/ppermute | solution.py:370
  62.4 3.1 %norm_and_gradient.1 = (bf16[2,4,256,128]{3,2,1,0:T(8,128)(2,1)S(1)}, bf16[2,256,128]{2,1,0:T(8,128)(2,1)S(1)}, bf16[2,256,128]{2,1,0:T(8,128)(2,1)S(1)}, f32[576,128]{1,0:T(8,128)S(1)}, f32[576,128]{1,0:T(8,128)S(1)}) custom-call(s32[2]{0:T(128)S(1)} %copy-done.6, s32[1]{0:T(128)} %bitcast.index_ref, s32[1]{0:T(128)} %bitcast.1.core_ref, ...), custom_call_target="tpu_custom_call" | custom-call | flops 603979776 | bytes 2097152 | tf_op jit(solution)/shard_map/norm_and_gradient/pallas_call | solution.py:496
  65.4 0.1 collective-permute-start.16
  65.5 1.6 %collective-permute-done.16.other_ref = f32[576,128]{1,0:T(8,128)S(1)} collective-permute-done((f32[576,128]{1,0:T(8,128)S(1)}, f32[576,128]{1,0:T(8,128)S(1)}, u32[]{:S(2)}, u32[]{:S(2)}) %collective-permute-start.16) | collective-permute-done | bytes 294944 | tf_op jit(solution)/shard_map/ppermute | solution.py:392
  67.1 0.1 collective-permute-start.17
  67.3 2.6 %collective-permute-start.18 = (bf16[144,128]{1,0:T(8,128)(2,1)S(1)}, bf16[144,128]{1,0:T(8,128)(2,1)S(1)}, u32[]{:S(2)}, u32[]{:S(2)}) collective-permute-start(bf16[144,128]{1,0:T(8,128)(2,1)S(1)} %get-tuple-element.55), channel_id=1, source_target_pairs={{0,16},{1,17},{2,18},{3,19},{4,20},{5,21},{6,22},{7,23},{8,24},{9,... | collective-permute-start | bytes 110600 | tf_op jit(solution)/shard_map/ppermute | solution.py:388
  69.9 0.8 collective-permute-start.19
  70.7 0.7 collective-permute-start.21
  71.3 0.0 collective-permute-done.17.refs_1_
  71.4 0.5 collective-permute-done.18.refs_2_
  71.8 2.9 %collective-permute-done.19.refs_3_ = bf16[144,128]{1,0:T(8,128)(2,1)S(1)} collective-permute-done((bf16[144,128]{1,0:T(8,128)(2,1)S(1)}, bf16[144,128]{1,0:T(8,128)(2,1)S(1)}, u32[]{:S(2)}, u32[]{:S(2)}) %collective-permute-start.19) | collective-permute-done | bytes 36896 | tf_op jit(solution)/shard_map/ppermute | solution.py:388
  74.8 0.5 collective-permute-start.20
  75.3 1.4 %collective-permute-start.24 = (bf16[144,128]{1,0:T(8,128)(2,1)S(1)}, bf16[144,128]{1,0:T(8,128)(2,1)S(1)}, u32[]{:S(2)}, u32[]{:S(2)}) collective-permute-start(bf16[144,128]{1,0:T(8,128)(2,1)S(1)} %sum_chips.1.after_ref.refs_0_), channel_id=1, source_target_pairs={{0,6},{1,7},{2,4},{3,5},{4,2},{5,3},{6,0},{7,1},{8,14},{9,15},{10,... | collective-permute-start | bytes 110600 | tf_op jit(solution)/shard_map/ppermute | solution.py:370
  76.8 0.1 collective-permute-start.23
  76.8 2.9 %collective-permute-start.22 = (bf16[144,128]{1,0:T(8,128)(2,1)S(1)}, bf16[144,128]{1,0:T(8,128)(2,1)S(1)}, u32[]{:S(2)}, u32[]{:S(2)}) collective-permute-start(bf16[144,128]{1,0:T(8,128)(2,1)S(1)} %sum_chips.1.after_ref.refs_0_), channel_id=1, source_target_pairs={{0,2},{1,3},{2,0},{3,1},{4,6},{5,7},{6,4},{7,5},{8,10},{9,11},{10,... | collective-permute-start | bytes 110600 | tf_op jit(solution)/shard_map/ppermute | solution.py:370
  79.7 1.4 %collective-permute-done.24.refs_3_ = bf16[144,128]{1,0:T(8,128)(2,1)S(1)} collective-permute-done((bf16[144,128]{1,0:T(8,128)(2,1)S(1)}, bf16[144,128]{1,0:T(8,128)(2,1)S(1)}, u32[]{:S(2)}, u32[]{:S(2)}) %collective-permute-start.24) | collective-permute-done | bytes 36896 | tf_op jit(solution)/shard_map/ppermute | solution.py:370
  81.1 0.9 collective-permute-done.23.refs_2_
  82.0 0.1 collective-permute-done.22.refs_1_
  82.1 1.8 %collective-permute-start.27 = (bf16[144,128]{1,0:T(8,128)(2,1)S(1)}, bf16[144,128]{1,0:T(8,128)(2,1)S(1)}, u32[]{:S(2)}, u32[]{:S(2)}) collective-permute-start(bf16[144,128]{1,0:T(8,128)(2,1)S(1)} %sum_planes.1.refs_0_), channel_id=1, source_target_pairs={{0,17},{1,16},{2,19},{3,18},{4,21},{5,20},{6,23},{7,22},{8,25},{9,... | collective-permute-start | bytes 110600 | tf_op jit(solution)/shard_map/ppermute | solution.py:388
  83.9 1.3 %collective-permute-start.26 = (bf16[144,128]{1,0:T(8,128)(2,1)S(1)}, bf16[144,128]{1,0:T(8,128)(2,1)S(1)}, u32[]{:S(2)}, u32[]{:S(2)}) collective-permute-start(bf16[144,128]{1,0:T(8,128)(2,1)S(1)} %sum_planes.1.refs_0_), channel_id=1, source_target_pairs={{0,16},{1,17},{2,18},{3,19},{4,20},{5,21},{6,22},{7,23},{8,24},{9,... | collective-permute-start | bytes 110600 | tf_op jit(solution)/shard_map/ppermute | solution.py:388
  85.2 0.5 collective-permute-start.25
  85.6 2.2 %decode.1 = (bf16[2,4,256,128]{3,2,1,0:T(8,128)(2,1)}, f32[8,128]{1,0:T(8,128)S(1)}) custom-call(s32[1]{0:T(128)} %bitcast.index_ref, bf16[2,4,256,128]{3,2,1,0:T(8,128)(2,1)S(1)} %get-tuple-element.49.image_ref, bf16[2,256,128]{2,1,0:T(8,128)(2,1)S(1)} %collective-permute-done.20.near_ref, bf16[2,256,128]{2,1,0:T(8,128)(2,1)S(1)} %collective-permute-done.21.far_ref, ...), custom_call_target="tpu_custom_call" | custom-call | flops 603979776 | bytes 1048576 | tf_op jit(solution)/shard_map/decode/pallas_call | solution.py:534
  87.9 1.3 %collective-permute-done.25.refs_1_ = bf16[144,128]{1,0:T(8,128)(2,1)S(1)} collective-permute-done((bf16[144,128]{1,0:T(8,128)(2,1)S(1)}, bf16[144,128]{1,0:T(8,128)(2,1)S(1)}, u32[]{:S(2)}, u32[]{:S(2)}) %collective-permute-start.25) | collective-permute-done | bytes 36896 | tf_op jit(solution)/shard_map/ppermute | solution.py:388
  89.1 0.1 collective-permute-start.28
  89.2 1.4 %collective-permute-done.28.other_ref = bf16[576,128]{1,0:T(8,128)(2,1)S(1)} collective-permute-done((bf16[576,128]{1,0:T(8,128)(2,1)S(1)}, bf16[576,128]{1,0:T(8,128)(2,1)S(1)}, u32[]{:S(2)}, u32[]{:S(2)}) %collective-permute-start.28) | collective-permute-done | bytes 147488 | tf_op jit(solution)/shard_map/ppermute | solution.py:392
  90.6 0.8 spread_sums.1
  (28 shorter events, 0.2 us)
Async XLA Ops:
  0.6 14.3 %copy-start.3 = (bf16[2,4,256,128]{3,2,1,0:T(8,128)(2,1)S(1)}, bf16[2,4,256,128]{3,2,1,0:T(8,128)(2,1)}, u32[]{:S(2)}) copy-start(bf16[2,4,256,128]{3,2,1,0:T(8,128)(2,1)} %cot_ref.1) | copy-start | bytes 1572868
  0.6 14.3 %copy-start = (bf16[64,2,2048]{2,1,0:T(2,128)(2,1)S(1)}, bf16[64,2,2048]{2,1,0:T(2,128)(2,1)}, u32[]{:S(2)}) copy-start(bf16[64,2,2048]{2,1,0:T(2,128)(2,1)} %query_ref.5) | copy-start | bytes 1572868
  0.7 14.3 %copy-start.1 = (bf16[64,2,2048]{2,1,0:T(2,128)(2,1)S(1)}, bf16[64,2,2048]{2,1,0:T(2,128)(2,1)}, u32[]{:S(2)}) copy-start(bf16[64,2,2048]{2,1,0:T(2,128)(2,1)} %key_ref.5) | copy-start | bytes 1572868
  0.7 14.3 %copy-start.2 = (bf16[64,2,2048]{2,1,0:T(2,128)(2,1)S(1)}, bf16[64,2,2048]{2,1,0:T(2,128)(2,1)}, u32[]{:S(2)}) copy-start(bf16[64,2,2048]{2,1,0:T(2,128)(2,1)} %value_ref.5) | copy-start | bytes 1572868
  3.3 12.3 %collective-permute-start.3 = (bf16[3,4,64,128]{3,2,1,0:T(8,128)(2,1)}, bf16[3,4,64,128]{3,2,1,0:T(8,128)(2,1)S(1)}, u32[]{:S(2)}, u32[]{:S(2)}) collective-permute-start(bf16[3,4,64,128]{3,2,1,0:T(8,128)(2,1)} %get-tuple-element.34), channel_id=1, source_target_pairs={{0,2},{1,3},{2,0},{3,1},{4,6},{5,7},{6,4},{7,5},{8,10},{9,11},{10,... | collective-permute-start | bytes 589832 | tf_op jit(solution)/shard_map/ppermute | solution.py:370
  6.3 17.1 %collective-permute-start.5 = (bf16[3,4,64,128]{3,2,1,0:T(8,128)(2,1)}, bf16[3,4,64,128]{3,2,1,0:T(8,128)(2,1)S(1)}, u32[]{:S(2)}, u32[]{:S(2)}) collective-permute-start(bf16[3,4,64,128]{3,2,1,0:T(8,128)(2,1)} %get-tuple-element.36), channel_id=1, source_target_pairs={{0,4},{1,5},{2,6},{3,7},{4,0},{5,1},{6,2},{7,3},{8,12},{9,13},{10,... | collective-permute-start | bytes 589832 | tf_op jit(solution)/shard_map/ppermute | solution.py:370
  8.9 28.3 %collective-permute-start.6 = (bf16[3,4,64,128]{3,2,1,0:T(8,128)(2,1)}, bf16[3,4,64,128]{3,2,1,0:T(8,128)(2,1)S(1)}, u32[]{:S(2)}, u32[]{:S(2)}) collective-permute-start(bf16[3,4,64,128]{3,2,1,0:T(8,128)(2,1)} %get-tuple-element.37), channel_id=1, source_target_pairs={{0,5},{1,4},{2,7},{3,6},{4,1},{5,0},{6,3},{7,2},{8,13},{9,12},{10,... | collective-permute-start | bytes 589832 | tf_op jit(solution)/shard_map/ppermute | solution.py:370
  12.9 10.5 %copy-start.7 = (bf16[3,4,64,128]{3,2,1,0:T(8,128)(2,1)S(1)}, bf16[3,4,64,128]{3,2,1,0:T(8,128)(2,1)}, u32[]{:S(2)}) copy-start(bf16[3,4,64,128]{3,2,1,0:T(8,128)(2,1)} %get-tuple-element.39) | copy-start | bytes 589828
  13.0 25.3 %copy-start.6 = (s32[2]{0:T(128)S(1)}, s32[2]{0:T(128)}, u32[]{:S(2)}) copy-start(s32[2]{0:T(128)} %lengths_ref.1) | copy-start | bytes 28
  13.0 24.6 %collective-permute-start.2 = (bf16[3,4,64,128]{3,2,1,0:T(8,128)(2,1)}, bf16[3,4,64,128]{3,2,1,0:T(8,128)(2,1)S(1)}, u32[]{:S(2)}, u32[]{:S(2)}) collective-permute-start(bf16[3,4,64,128]{3,2,1,0:T(8,128)(2,1)} %get-tuple-element.33), channel_id=1, source_target_pairs={{0,1},{1,0},{2,3},{3,2},{4,5},{5,4},{6,7},{7,6},{8,9},{9,8},{10,11... | collective-permute-start | bytes 589832 | tf_op jit(solution)/shard_map/ppermute | solution.py:370
  13.6 24.8 %collective-permute-start.4 = (bf16[3,4,64,128]{3,2,1,0:T(8,128)(2,1)}, bf16[3,4,64,128]{3,2,1,0:T(8,128)(2,1)S(1)}, u32[]{:S(2)}, u32[]{:S(2)}) collective-permute-start(bf16[3,4,64,128]{3,2,1,0:T(8,128)(2,1)} %get-tuple-element.35), channel_id=1, source_target_pairs={{0,3},{1,2},{2,1},{3,0},{4,7},{5,6},{6,5},{7,4},{8,11},{9,10},{10,... | collective-permute-start | bytes 589832 | tf_op jit(solution)/shard_map/ppermute | solution.py:370
  15.0 0.9 %copy-start.8 = (bf16[3,4,64,128]{3,2,1,0:T(8,128)(2,1)S(1)}, bf16[3,4,64,128]{3,2,1,0:T(8,128)(2,1)}, u32[]{:S(2)}) copy-start(bf16[3,4,64,128]{3,2,1,0:T(8,128)(2,1)} %get-tuple-element.38) | copy-start | bytes 589828
  15.9 22.4 %collective-permute-start.7 = (bf16[3,4,64,128]{3,2,1,0:T(8,128)(2,1)S(1)}, bf16[3,4,64,128]{3,2,1,0:T(8,128)(2,1)S(1)}, u32[]{:S(2)}, u32[]{:S(2)}) collective-permute-start(bf16[3,4,64,128]{3,2,1,0:T(8,128)(2,1)S(1)} %copy-done.8), channel_id=1, source_target_pairs={{0,6},{1,7},{2,4},{3,5},{4,2},{5,3},{6,0},{7,1},{8,14},{9,15},{10,... | collective-permute-start | bytes 589832 | tf_op jit(solution)/shard_map/ppermute | solution.py:370
  23.4 14.9 %collective-permute-start.8 = (bf16[3,4,64,128]{3,2,1,0:T(8,128)(2,1)S(1)}, bf16[3,4,64,128]{3,2,1,0:T(8,128)(2,1)S(1)}, u32[]{:S(2)}, u32[]{:S(2)}) collective-permute-start(bf16[3,4,64,128]{3,2,1,0:T(8,128)(2,1)S(1)} %copy-done.7), channel_id=1, source_target_pairs={{0,7},{1,6},{2,5},{3,4},{4,3},{5,2},{6,1},{7,0},{8,15},{9,14},{10,... | collective-permute-start | bytes 589832 | tf_op jit(solution)/shard_map/ppermute | solution.py:370
  37.3 13.8 %collective-permute-start = (bf16[2,256,128]{2,1,0:T(8,128)(2,1)S(1)}, bf16[2,256,128]{2,1,0:T(8,128)(2,1)S(1)}, u32[]{:S(2)}, u32[]{:S(2)}) collective-permute-start(bf16[2,256,128]{2,1,0:T(8,128)(2,1)S(1)} %get-tuple-element.31), channel_id=1, source_target_pairs={{0,1},{1,0},{2,3},{3,2},{4,5},{5,4},{6,7},{7,6},{8,9},{9,8},{10,11... | collective-permute-start | bytes 393224 | tf_op jit(solution)/shard_map/ppermute | solution.py:370
  37.6 17.1 %collective-permute-start.1 = (bf16[2,256,128]{2,1,0:T(8,128)(2,1)S(1)}, bf16[2,256,128]{2,1,0:T(8,128)(2,1)S(1)}, u32[]{:S(2)}, u32[]{:S(2)}) collective-permute-start(bf16[2,256,128]{2,1,0:T(8,128)(2,1)S(1)} %get-tuple-element.32), channel_id=1, source_target_pairs={{1,2},{3,4},{5,6},{2,1},{4,3},{6,5},{9,10},{11,12},{13,14},{10,9},... | collective-permute-start | bytes 393224 | tf_op jit(solution)/shard_map/ppermute | solution.py:459
  40.8 21.5 %copy-start.5 = (f32[2048]{0:T(1024)S(1)}, f32[2048]{0:T(1024)}, u32[]{:S(2)}) copy-start(f32[2048]{0:T(1024)} %param.11) | copy-start | bytes 24580
  40.8 14.1 %collective-permute-start.9 = (bf16[4,64,128]{2,1,0:T(8,128)(2,1)S(1)}, bf16[4,64,128]{2,1,0:T(8,128)(2,1)S(1)}, u32[]{:S(2)}, u32[]{:S(2)}) collective-permute-start(bf16[4,64,128]{2,1,0:T(8,128)(2,1)S(1)} %get-tuple-element.41), channel_id=1, source_target_pairs={{0,4},{1,5},{2,6},{3,7},{4,0},{5,1},{6,2},{7,3},{8,12},{9,13},{10,... | collective-permute-start | bytes 196616 | tf_op jit(solution)/shard_map/ppermute | solution.py:370
  49.9 8.2 %collective-permute-start.10 = (bf16[4,64,128]{2,1,0:T(8,128)(2,1)S(1)}, bf16[4,64,128]{2,1,0:T(8,128)(2,1)S(1)}, u32[]{:S(2)}, u32[]{:S(2)}) collective-permute-start(bf16[4,64,128]{2,1,0:T(8,128)(2,1)S(1)} %get-tuple-element.42), channel_id=1, source_target_pairs={{0,5},{1,4},{2,7},{3,6},{4,1},{5,0},{6,3},{7,2},{8,13},{9,12},{10,... | collective-permute-start | bytes 196616 | tf_op jit(solution)/shard_map/ppermute | solution.py:370
  49.9 8.6 %collective-permute-start.11 = (bf16[4,64,128]{2,1,0:T(8,128)(2,1)S(1)}, bf16[4,64,128]{2,1,0:T(8,128)(2,1)S(1)}, u32[]{:S(2)}, u32[]{:S(2)}) collective-permute-start(bf16[4,64,128]{2,1,0:T(8,128)(2,1)S(1)} %get-tuple-element.43), channel_id=1, source_target_pairs={{0,6},{1,7},{2,4},{3,5},{4,2},{5,3},{6,0},{7,1},{8,14},{9,15},{10,... | collective-permute-start | bytes 196616 | tf_op jit(solution)/shard_map/ppermute | solution.py:370
  51.1 7.4 %collective-permute-start.12 = (bf16[4,64,128]{2,1,0:T(8,128)(2,1)S(1)}, bf16[4,64,128]{2,1,0:T(8,128)(2,1)S(1)}, u32[]{:S(2)}, u32[]{:S(2)}) collective-permute-start(bf16[4,64,128]{2,1,0:T(8,128)(2,1)S(1)} %get-tuple-element.44), channel_id=1, source_target_pairs={{0,7},{1,6},{2,5},{3,4},{4,3},{5,2},{6,1},{7,0},{8,15},{9,14},{10,... | collective-permute-start | bytes 196616 | tf_op jit(solution)/shard_map/ppermute | solution.py:370
  54.7 4.3 %collective-permute-start.13 = (bf16[4,64,128]{2,1,0:T(8,128)(2,1)S(1)}, bf16[4,64,128]{2,1,0:T(8,128)(2,1)S(1)}, u32[]{:S(2)}, u32[]{:S(2)}) collective-permute-start(bf16[4,64,128]{2,1,0:T(8,128)(2,1)S(1)} %get-tuple-element.45), channel_id=1, source_target_pairs={{0,2},{1,3},{2,0},{3,1},{4,6},{5,7},{6,4},{7,5},{8,10},{9,11},{10,... | collective-permute-start | bytes 196616 | tf_op jit(solution)/shard_map/ppermute | solution.py:370
  55.0 5.2 %collective-permute-start.14 = (bf16[4,64,128]{2,1,0:T(8,128)(2,1)S(1)}, bf16[4,64,128]{2,1,0:T(8,128)(2,1)S(1)}, u32[]{:S(2)}, u32[]{:S(2)}) collective-permute-start(bf16[4,64,128]{2,1,0:T(8,128)(2,1)S(1)} %get-tuple-element.46), channel_id=1, source_target_pairs={{0,3},{1,2},{2,1},{3,0},{4,7},{5,6},{6,5},{7,4},{8,11},{9,10},{10,... | collective-permute-start | bytes 196616 | tf_op jit(solution)/shard_map/ppermute | solution.py:370
  58.1 4.3 %collective-permute-start.15 = (bf16[4,64,128]{2,1,0:T(8,128)(2,1)S(1)}, bf16[4,64,128]{2,1,0:T(8,128)(2,1)S(1)}, u32[]{:S(2)}, u32[]{:S(2)}) collective-permute-start(bf16[4,64,128]{2,1,0:T(8,128)(2,1)S(1)} %get-tuple-element.47), channel_id=1, source_target_pairs={{0,1},{1,0},{2,3},{3,2},{4,5},{5,4},{6,7},{7,6},{8,9},{9,8},{10,11... | collective-permute-start | bytes 196616 | tf_op jit(solution)/shard_map/ppermute | solution.py:370
  62.4 23.3 %copy-start.4 = (bf16[9,128,128]{2,1,0:T(8,128)(2,1)S(1)}, bf16[9,128,128]{2,1,0:T(8,128)(2,1)}, u32[]{:S(2)}) copy-start(bf16[9,128,128]{2,1,0:T(8,128)(2,1)} %param.12) | copy-start | bytes 884740
  65.4 1.6 %collective-permute-start.16 = (f32[576,128]{1,0:T(8,128)S(1)}, f32[576,128]{1,0:T(8,128)S(1)}, u32[]{:S(2)}, u32[]{:S(2)}) collective-permute-start(f32[576,128]{1,0:T(8,128)S(1)} %get-tuple-element.52), channel_id=1, source_target_pairs={{0,8},{8,0},{16,24},{24,16},{1,9},{9,1},{17,25},{25,17},{2,10},{10... | collective-permute-start | bytes 884744 | tf_op jit(solution)/shard_map/ppermute | solution.py:392
  67.1 4.2 %collective-permute-start.17 = (bf16[144,128]{1,0:T(8,128)(2,1)S(1)}, bf16[144,128]{1,0:T(8,128)(2,1)S(1)}, u32[]{:S(2)}, u32[]{:S(2)}) collective-permute-start(bf16[144,128]{1,0:T(8,128)(2,1)S(1)} %get-tuple-element.54), channel_id=1, source_target_pairs={{0,1},{1,0},{2,3},{3,2},{4,5},{5,4},{6,7},{7,6},{8,9},{9,8},{10,11... | collective-permute-start | bytes 110600 | tf_op jit(solution)/shard_map/ppermute | solution.py:388
  67.3 4.6 %collective-permute-start.18 = (bf16[144,128]{1,0:T(8,128)(2,1)S(1)}, bf16[144,128]{1,0:T(8,128)(2,1)S(1)}, u32[]{:S(2)}, u32[]{:S(2)}) collective-permute-start(bf16[144,128]{1,0:T(8,128)(2,1)S(1)} %get-tuple-element.55), channel_id=1, source_target_pairs={{0,16},{1,17},{2,18},{3,19},{4,20},{5,21},{6,22},{7,23},{8,24},{9,... | collective-permute-start | bytes 110600 | tf_op jit(solution)/shard_map/ppermute | solution.py:388
  69.9 4.9 %collective-permute-start.19 = (bf16[144,128]{1,0:T(8,128)(2,1)S(1)}, bf16[144,128]{1,0:T(8,128)(2,1)S(1)}, u32[]{:S(2)}, u32[]{:S(2)}) collective-permute-start(bf16[144,128]{1,0:T(8,128)(2,1)S(1)} %get-tuple-element.56), channel_id=1, source_target_pairs={{0,17},{1,16},{2,19},{3,18},{4,21},{5,20},{6,23},{7,22},{8,25},{9,... | collective-permute-start | bytes 110600 | tf_op jit(solution)/shard_map/ppermute | solution.py:388
  70.7 14.9 %collective-permute-start.21 = (bf16[2,256,128]{2,1,0:T(8,128)(2,1)S(1)}, bf16[2,256,128]{2,1,0:T(8,128)(2,1)S(1)}, u32[]{:S(2)}, u32[]{:S(2)}) collective-permute-start(bf16[2,256,128]{2,1,0:T(8,128)(2,1)S(1)} %get-tuple-element.57), channel_id=1, source_target_pairs={{1,2},{3,4},{5,6},{2,1},{4,3},{6,5},{9,10},{11,12},{13,14},{10,9},... | collective-permute-start | bytes 393224 | tf_op jit(solution)/shard_map/ppermute | solution.py:521
  74.8 10.8 %collective-permute-start.20 = (bf16[2,256,128]{2,1,0:T(8,128)(2,1)S(1)}, bf16[2,256,128]{2,1,0:T(8,128)(2,1)S(1)}, u32[]{:S(2)}, u32[]{:S(2)}) collective-permute-start(bf16[2,256,128]{2,1,0:T(8,128)(2,1)S(1)} %hold.1), channel_id=1, source_target_pairs={{0,1},{1,0},{2,3},{3,2},{4,5},{5,4},{6,7},{7,6},{8,9},{9,8},{10,11... | collective-permute-start | bytes 393224 | tf_op jit(solution)/shard_map/ppermute | solution.py:370
  75.3 5.8 %collective-permute-start.24 = (bf16[144,128]{1,0:T(8,128)(2,1)S(1)}, bf16[144,128]{1,0:T(8,128)(2,1)S(1)}, u32[]{:S(2)}, u32[]{:S(2)}) collective-permute-start(bf16[144,128]{1,0:T(8,128)(2,1)S(1)} %sum_chips.1.after_ref.refs_0_), channel_id=1, source_target_pairs={{0,6},{1,7},{2,4},{3,5},{4,2},{5,3},{6,0},{7,1},{8,14},{9,15},{10,... | collective-permute-start | bytes 110600 | tf_op jit(solution)/shard_map/ppermute | solution.py:370
  76.8 5.2 %collective-permute-start.23 = (bf16[144,128]{1,0:T(8,128)(2,1)S(1)}, bf16[144,128]{1,0:T(8,128)(2,1)S(1)}, u32[]{:S(2)}, u32[]{:S(2)}) collective-permute-start(bf16[144,128]{1,0:T(8,128)(2,1)S(1)} %sum_chips.1.after_ref.refs_0_), channel_id=1, source_target_pairs={{0,4},{1,5},{2,6},{3,7},{4,0},{5,1},{6,2},{7,3},{8,12},{9,13},{10,... | collective-permute-start | bytes 110600 | tf_op jit(solution)/shard_map/ppermute | solution.py:370
  76.8 5.2 %collective-permute-start.22 = (bf16[144,128]{1,0:T(8,128)(2,1)S(1)}, bf16[144,128]{1,0:T(8,128)(2,1)S(1)}, u32[]{:S(2)}, u32[]{:S(2)}) collective-permute-start(bf16[144,128]{1,0:T(8,128)(2,1)S(1)} %sum_chips.1.after_ref.refs_0_), channel_id=1, source_target_pairs={{0,2},{1,3},{2,0},{3,1},{4,6},{5,7},{6,4},{7,5},{8,10},{9,11},{10,... | collective-permute-start | bytes 110600 | tf_op jit(solution)/shard_map/ppermute | solution.py:370
  82.1 5.8 %collective-permute-start.27 = (bf16[144,128]{1,0:T(8,128)(2,1)S(1)}, bf16[144,128]{1,0:T(8,128)(2,1)S(1)}, u32[]{:S(2)}, u32[]{:S(2)}) collective-permute-start(bf16[144,128]{1,0:T(8,128)(2,1)S(1)} %sum_planes.1.refs_0_), channel_id=1, source_target_pairs={{0,17},{1,16},{2,19},{3,18},{4,21},{5,20},{6,23},{7,22},{8,25},{9,... | collective-permute-start | bytes 110600 | tf_op jit(solution)/shard_map/ppermute | solution.py:388
  83.9 4.0 %collective-permute-start.26 = (bf16[144,128]{1,0:T(8,128)(2,1)S(1)}, bf16[144,128]{1,0:T(8,128)(2,1)S(1)}, u32[]{:S(2)}, u32[]{:S(2)}) collective-permute-start(bf16[144,128]{1,0:T(8,128)(2,1)S(1)} %sum_planes.1.refs_0_), channel_id=1, source_target_pairs={{0,16},{1,17},{2,18},{3,19},{4,20},{5,21},{6,22},{7,23},{8,24},{9,... | collective-permute-start | bytes 110600 | tf_op jit(solution)/shard_map/ppermute | solution.py:388
  85.2 4.0 %collective-permute-start.25 = (bf16[144,128]{1,0:T(8,128)(2,1)S(1)}, bf16[144,128]{1,0:T(8,128)(2,1)S(1)}, u32[]{:S(2)}, u32[]{:S(2)}) collective-permute-start(bf16[144,128]{1,0:T(8,128)(2,1)S(1)} %sum_planes.1.refs_0_), channel_id=1, source_target_pairs={{0,1},{1,0},{2,3},{3,2},{4,5},{5,4},{6,7},{7,6},{8,9},{9,8},{10,11... | collective-permute-start | bytes 110600 | tf_op jit(solution)/shard_map/ppermute | solution.py:388
  89.1 1.4 %collective-permute-start.28 = (bf16[576,128]{1,0:T(8,128)(2,1)S(1)}, bf16[576,128]{1,0:T(8,128)(2,1)S(1)}, u32[]{:S(2)}, u32[]{:S(2)}) collective-permute-start(bf16[576,128]{1,0:T(8,128)(2,1)S(1)} %join_chips.1.own_ref), channel_id=1, source_target_pairs={{0,8},{8,0},{16,24},{24,16},{1,9},{9,1},{17,25},{25,17},{2,10},{10... | collective-permute-start | bytes 442376 | tf_op jit(solution)/shard_map/ppermute | solution.py:392
